TPU v7x, 32 devices: a whole 2x2x4 slice. The times are simulated.
32 devices in a mesh: dp: 8 (over z, y), expert: 4 (over x, core).
Axes of the slice: x: 2, y: 2, z: 4, core: 2. Of those that a mesh axis runs over, the one named last changes fastest.
Arguments:
- tokens: bfloat16 [4096, 2048], P(('dp', 'expert')), may hold values from -6 to 6
- cotangent: bfloat16 [4096, 2048], P(('dp', 'expert')), may hold values from -6 to 6
- expert_ids: int32 [4096, 2], P(('dp', 'expert')), may hold values from 0 to 3, all different within a row; in each aligned block of 128 rows (0 to 127, 128 to 255, ...) at most 80 rows name the same one
- gate_probs: float32 [4096, 2], P(('dp', 'expert')), may hold values from 0.2 to 1
- gate_up_weight: bfloat16 [4, 2048, 1024], P('expert'), may hold values from -0.125 to 0.125
- down_weight: bfloat16 [4, 512, 2048], P('expert'), may hold values from -0.25 to 0.25
- down_residual: bfloat16 [8, 4, 512, 2048], P('dp', 'expert'), may hold values from -12 to 12
Outputs:
- token_grad: bfloat16 [4096, 2048], P(('dp', 'expert'))
- grad_gate_up: float32 [4, 2048, 1024], P('expert', 'dp')
- grad_down: float32 [4, 512, 2048], P('expert', 'dp')
Inputs may be any that keep to these rules, and one draw needn't show every extreme that they name: `expert_ids`: each token names 2 different experts. Among the tokens of one device no expert is named by more than 80 tokens, and in some device's tokens one expert is named by exactly 80.
All inputs are finite; a program needn't handle non-finite values.
Results may differ from a plain program's by a relative error of at most 0.0065.
Values may be sent and summed in bfloat16 or wider, within the bound.
No kernel may reach another device: no remote copies, remote signals or barrier semaphores. Data moves between devices by JAX's collectives and lax.ppermute only.
A program may use at most 128 MiB of HBM per device.

v0:
```python
import jax
import jax.numpy as jnp
from jax import lax
from jax.experimental import pallas as pl
from jax.experimental.pallas import tpu as pltpu
from jax.sharding import PartitionSpec as P

LANES = 128


def wide(values):
    return values.astype(jnp.float32)


def narrow(values):
    return values.astype(jnp.bfloat16)


def flip(values, axis, bit):
    return lax.ppermute(values, axis, [(i, i ^ bit) for i in range(lax.axis_size(axis))])


def take(values, axis, index):
    return lax.dynamic_index_in_dim(values, index, axis, keepdims=False)


def with_routes(cotangent, expert_ids, gate_probs, expert_count):
    lane = jnp.arange(LANES, dtype=jnp.int32)[None, :]
    route = jnp.zeros((expert_ids.shape[0], LANES), jnp.float32)
    for k in range(expert_ids.shape[1]):
        hit = (lane < 3 * expert_count) & (lane // 3 == expert_ids[:, k : k + 1])
        route = route + jnp.where(hit, gate_probs[:, k : k + 1], 0.0)
    high = lax.reduce_precision(route, 8, 7)
    middle = lax.reduce_precision(route - high, 8, 7)
    low = (route - high) - middle
    part = lane % 3
    coded = jnp.where(part == 0, high, jnp.where(part == 1, middle, low))
    return jnp.concatenate([cotangent, narrow(coded)], axis=1)


def expert_kernel(me, tok_a, tok_b, cot_a, cot_b, gate_up, down, hidden, scaled, back):
    width, units = gate_up.shape[0], down.shape[0]
    tile = units // 2
    lane = lax.broadcasted_iota(jnp.int32, (1, LANES), 1)
    for cot, at in ((cot_a, 0), (cot_b, cot_a.shape[0])):
        coded = wide(cot[:, width:])
        part = [
            jnp.sum(jnp.where(lane == 3 * me[0] + k, coded, 0.0), axis=1, keepdims=True)
            for k in range(3)
        ]
        weight = (part[0] + part[1]) + part[2]
        scaled[at : at + cot.shape[0], :] = narrow(wide(cot[:, :width]) * weight)
    rows = jnp.concatenate([tok_a[...], tok_b[...]], axis=0)
    grads = scaled[...]
    contract = (((1,), (1,)), ((), ()))
    for at in range(0, units, tile):
        gate = jnp.dot(rows, gate_up[:, at : at + tile], preferred_element_type=jnp.float32)
        up = jnp.dot(
            rows, gate_up[:, units + at : units + at + tile], preferred_element_type=jnp.float32
        )
        sig = jax.nn.sigmoid(gate)
        activated = gate * sig
        hidden[:, at : at + tile] = narrow(activated * up)
        back_hidden = lax.dot_general(
            grads, down[at : at + tile, :], contract, preferred_element_type=jnp.float32
        )
        slope = up * sig * (1.0 + gate * (1.0 - sig))
        back[:, at : at + tile] = narrow(back_hidden * slope)
        back[:, units + at : units + at + tile] = narrow(back_hidden * activated)


def expert_rows(me, tok_a, tok_b, cot_a, cot_b, gate_up, down):
    rows, width = 2 * tok_a.shape[0], tok_a.shape[1]
    units = down.shape[0]
    vmem = pl.BlockSpec(memory_space=pltpu.VMEM)
    return pl.pallas_call(
        expert_kernel,
        out_shape=(
            jax.ShapeDtypeStruct((rows, units), jnp.bfloat16),
            jax.ShapeDtypeStruct((rows, width), jnp.bfloat16),
            jax.ShapeDtypeStruct((rows, 2 * units), jnp.bfloat16),
        ),
        in_specs=[pl.BlockSpec(memory_space=pltpu.SMEM)] + [vmem] * 6,
        out_specs=(vmem, vmem, vmem),
        compiler_params=pltpu.CompilerParams(vmem_limit_bytes=24 << 20),
        cost_estimate=pl.CostEstimate(
            flops=6 * rows * width * units, bytes_accessed=12 << 20, transcendentals=rows * units
        ),
    )(me, tok_a, tok_b, cot_a, cot_b, gate_up, down)


def own_columns(values, group_count, parity):
    unit = values.shape[1] // group_count * 2
    blocks = [values[:, k * unit : (k + 1) * unit] for k in range(group_count // 2)]
    even, odd = jnp.concatenate(blocks[0::2], axis=1), jnp.concatenate(blocks[1::2], axis=1)
    return jnp.where(parity == 1, odd, even)


def on_device(
    tokens, cotangent, expert_ids, gate_probs, gate_up_weight, down_weight, down_residual
):
    tok_rows, model_width = tokens.shape
    expert_count = lax.axis_size("expert")
    group_count = lax.axis_size("dp")
    gate_up, down_matrix = gate_up_weight[0], down_weight[0]
    hidden_units = down_matrix.shape[0]
    me, group = lax.axis_index("expert"), lax.axis_index("dp")
    bit0, bit1, bit2 = group & 1, (group >> 1) & 1, (group >> 2) & 1
    high_count = group_count // 8

    tok_x, tok_c = flip(tokens, "expert", 2), flip(tokens, "expert", 1)
    carried = with_routes(cotangent, expert_ids, gate_probs, expert_count)
    cot_n, cot_c = flip(carried, "dp", 2), flip(carried, "expert", 1)
    tok_n, cot_x = flip(tokens, "dp", 2), flip(carried, "expert", 2)
    residual, tok_c = lax.optimization_barrier((down_residual, tok_c))
    residual = residual[0, 0].reshape(high_count, 2, 2, 2, -1, model_width)
    res_got = flip(take(residual, 3, 1 - bit0), "dp", 1)
    tok_d, cot_d = flip(tok_x, "dp", 2), flip(cot_n, "expert", 2)
    pairs = [(tokens, tok_c, carried, cot_c)] + [
        (tok, flip(tok, "expert", 1), cot, flip(cot, "expert", 1))
        for tok, cot in ((tok_x, cot_x), (tok_n, cot_n), (tok_d, cot_d))
    ]
    number = me.reshape(1).astype(jnp.int32)
    rows = [jnp.concatenate(pair[:2], axis=0) for pair in pairs]
    made = [expert_rows(number, *pair, gate_up, down_matrix) for pair in pairs]
    hidden, scaled, back = zip(*made)

    def terms(token_rows, hidden, scaled, back_both):
        contract = (((0,), (0,)), ((), ()))
        gate = lax.dot_general(
            own_columns(token_rows, group_count, bit1),
            back_both,
            contract,
            preferred_element_type=jnp.float32,
        )
        down = lax.dot_general(
            own_columns(hidden, group_count, bit1),
            scaled,
            contract,
            preferred_element_type=jnp.float32,
        )
        return gate, down

    joined = [jnp.concatenate(v[:3], axis=0) for v in (rows, hidden, scaled, back)]
    gate_early, down_early = terms(*joined)
    gate_late, down_late = terms(rows[3], hidden[3], scaled[3], back[3])
    gate_term = narrow(gate_early + gate_late).reshape(high_count, 2, 2, -1, 2 * hidden_units)
    down_term = narrow(down_early + down_late).reshape(high_count, 2, 2, -1, model_width)

    res_pair = wide(take(residual, 3, bit0)) + wide(res_got)
    res_send = narrow(take(res_pair, 2, 1 - bit1))
    res_send, _ = lax.optimization_barrier((res_send, cot_x))
    res_sum = take(res_pair, 2, bit1) + wide(flip(res_send, "dp", 2))

    def paired(term, side, after):
        mine = take(term, 1, side)
        sent, kept = take(mine, 1, 1 - bit0), take(mine, 1, bit0)
        if after is not None:
            sent, _ = lax.optimization_barrier((sent, after))
        got = flip(sent, "dp", 1)
        return wide(kept) + wide(got), got

    cut = gate_term.shape[3] // 2
    far_a, got_a = paired(gate_term[:, :, :, :cut], 1 - bit2, None)
    far_b, got_b = paired(gate_term[:, :, :, cut:], 1 - bit2, None)
    far_down, got_down = paired(down_term, 1 - bit2, got_a)
    far_down = far_down + take(res_sum, 1, 1 - bit2)
    crossed = [flip(narrow(piece), "dp", 4) for piece in (far_a, far_b, far_down)]
    near_gate, _ = paired(gate_term, bit2, got_b)
    near_down, _ = paired(down_term, bit2, got_down)
    gate_sum = near_gate + wide(jnp.concatenate(crossed[:2], axis=1))
    down_sum = near_down + take(res_sum, 1, bit2) + wide(crossed[2])
    bit = 8
    while bit < group_count:
        side = (group // bit) & 1
        halves = [v.reshape(-1, 2, *v.shape[1:]) for v in (gate_sum, down_sum)]
        gate_sum, down_sum = [
            take(v, 1, side) + wide(flip(narrow(take(v, 1, 1 - side)), "dp", bit)) for v in halves
        ]
        bit *= 2
    factor = 1.0 / group_count
    grad_gate_up, grad_down = gate_sum * factor, down_sum * factor

    back_group = jnp.concatenate(back[:2], axis=0)
    back_group, _ = lax.optimization_barrier((back_group, gate_term))
    token_part = narrow(jnp.dot(back_group, gate_up.T, preferred_element_type=jnp.float32))
    blocks = token_part.reshape(expert_count, tok_rows, model_width)
    core = flip(jnp.stack([blocks[1], blocks[3]]), "expert", 1)
    across = flip(narrow(wide(blocks[2]) + wide(core[1])), "expert", 2)
    token_grad = narrow(wide(blocks[0]) + wide(core[0]) + wide(across))
    return (token_grad, grad_gate_up, grad_down)


def solution(mesh):
    placed = (
        P(("dp", "expert"), None),
        P(("dp", "expert"), None),
        P(("dp", "expert"), None),
        P(("dp", "expert"), None),
        P("expert", None, None),
        P("expert", None, None),
        P("dp", "expert", None, None),
    )
    return jax.shard_map(
        on_device,
        mesh=mesh,
        in_specs=placed,
        out_specs=(P(("dp", "expert"), None), P("expert", "dp", None), P("expert", "dp", None)),
        check_vma=False,
    )
```

profile of v0, /device:TPU:0, one launch (start us, length us, event | category | flops | bytes accessed | tf_op | source)
XLA Modules:
  0.0 115.0 jit_solution(8794376102177010581)
XLA Ops:
  0.6 3.0 %collective-permute-start.2 = (bf16[128,2048]{1,0:T(8,128)(2,1)}, bf16[128,2048]{1,0:T(8,128)(2,1)S(1)}, u32[]{:S(2)}, u32[]{:S(2)}) collective-permute-start(bf16[128,2048]{1,0:T(8,128)(2,1)} %tok_a.1), channel_id=1, source_target_pairs={{0,2},{1,3},{2,0},{3,1},{4,6},{5,7},{6,4},{7,5},{8,10},{9,11},{10,... | collective-permute-start | bytes 1572872 | tf_op jit(solution)/shard_map/ppermute | solution.py:20
  5.3 1.1 pad_maximum_fusion.2.cot_a
  7.1 1.8 %collective-permute-start.8 = (bf16[128,2176]{1,0:T(8,128)(2,1)S(1)}, bf16[128,2176]{1,0:T(8,128)(2,1)S(1)}, u32[]{:S(2)}, u32[]{:S(2)}) collective-permute-start(bf16[128,2176]{1,0:T(8,128)(2,1)S(1)} %pad_maximum_fusion.2.cot_a), channel_id=1, source_target_pairs={{0,8},{4,12},{8,0},{12,4},{16,24},{20,28},{24,16},{28,20},{1,9},{5... | collective-permute-start | bytes 1671176 | tf_op jit(solution)/shard_map/ppermute | solution.py:20
  8.8 1.1 constant_dynamic-update-slice_fusion.5
  10.3 1.9 %constant_dynamic-slice_fusion.1 = (bf16[1,2,2,1,64,2048]{5,4,3,2,1,0:T(8,128)(2,1)S(1)}, bf16[1,2,2,1,64,2048]{5,4,3,2,1,0:T(8,128)(2,1)S(1)}) fusion(bf16[1,2,2,2,64,2048]{5,4,3,2,1,0:T(8,128)(2,1)} %bitcast.88, s32[]{:T(128)S(6)} %select_n.138, s32[]{:T(128)S(6)} %select_n.140), kind=kLoop, calls=%fused_computation.97 | loop fusion | bytes 4194312 | tf_op jit(solution)/shard_map/jit(dynamic_index_in_dim)/dynamic_slice | solution.py:24
  12.2 4.4 %collective-permute-done.2.tok_a = bf16[128,2048]{1,0:T(8,128)(2,1)S(1)} collective-permute-done((bf16[128,2048]{1,0:T(8,128)(2,1)}, bf16[128,2048]{1,0:T(8,128)(2,1)S(1)}, u32[]{:S(2)}, u32[]{:S(2)}) %collective-permute-start.2) | collective-permute-done | bytes 524320 | tf_op jit(solution)/shard_map/ppermute | solution.py:20
  16.8 16.3 %collective-permute-done.6.tok_a = bf16[128,2048]{1,0:T(8,128)(2,1)S(1)} collective-permute-done((bf16[128,2048]{1,0:T(8,128)(2,1)}, bf16[128,2048]{1,0:T(8,128)(2,1)S(1)}, u32[]{:S(2)}, u32[]{:S(2)}) %collective-permute-start.6) | collective-permute-done | bytes 524320 | tf_op jit(solution)/shard_map/ppermute | solution.py:20
  33.1 1.7 %collective-permute-start.10 = (bf16[128,2048]{1,0:T(8,128)(2,1)S(1)}, bf16[128,2048]{1,0:T(8,128)(2,1)S(1)}, u32[]{:S(2)}, u32[]{:S(2)}) collective-permute-start(bf16[128,2048]{1,0:T(8,128)(2,1)S(1)} %collective-permute-done.2.tok_a), channel_id=1, source_target_pairs={{0,8},{4,12},{8,0},{12,4},{16,24},{20,28},{24,16},{28,20},{1,9},{5... | collective-permute-start | bytes 1572872 | tf_op jit(solution)/shard_map/ppermute | solution.py:20
  34.9 1.9 %shard_map.94 = (bf16[256,512]{1,0:T(8,128)(2,1)S(1)}, bf16[256,2048]{1,0:T(8,128)(2,1)S(1)}, bf16[256,1024]{1,0:T(8,128)(2,1)S(1)}) custom-call(s32[1]{0:T(128)} %bitcast.me, bf16[128,2048]{1,0:T(8,128)(2,1)S(1)} %copy-done.2, bf16[128,2048]{1,0:T(8,128)(2,1)S(1)} %collective-permute-done.tok_b, bf16[128,2176]{1,0:T(8,128)(2,1)S(1)} %pad_maximum_fusion.2.cot_a, ...), custom_call_target="tpu_custom_call" | custom-call | flops 1610612736 | bytes 12582912 | tf_op jit(solution)/shard_map/pallas_call | solution.py:76
  36.9 1.6 %collective-permute-start.23 = (bf16[1,2,2,64,2048]{4,3,1,2,0:T(8,128)(2,1)S(1)}, bf16[1,2,2,64,2048]{4,3,1,2,0:T(8,128)(2,1)S(1)}, u32[]{:S(2)}, u32[]{:S(2)}) collective-permute-start(bf16[1,2,2,64,2048]{4,3,1,2,0:T(8,128)(2,1)S(1)} %bitcast.89), channel_id=1, source_target_pairs={{0,4},{4,0},{8,12},{12,8},{16,20},{20,16},{24,28},{28,24},{1,5},{5... | collective-permute-start | bytes 3145736 | tf_op jit(solution)/shard_map/ppermute | solution.py:20
  38.8 1.6 %collective-permute-start.12 = (bf16[128,2176]{1,0:T(8,128)(2,1)S(1)}, bf16[128,2176]{1,0:T(8,128)(2,1)S(1)}, u32[]{:S(2)}, u32[]{:S(2)}) collective-permute-start(bf16[128,2176]{1,0:T(8,128)(2,1)S(1)} %collective-permute-done.8.cot_a), channel_id=1, source_target_pairs={{0,2},{1,3},{2,0},{3,1},{4,6},{5,7},{6,4},{7,5},{8,10},{9,11},{10,... | collective-permute-start | bytes 1671176 | tf_op jit(solution)/shard_map/ppermute | solution.py:20
  40.4 6.1 %collective-permute-done.10.tok_a = bf16[128,2048]{1,0:T(8,128)(2,1)S(1)} collective-permute-done((bf16[128,2048]{1,0:T(8,128)(2,1)S(1)}, bf16[128,2048]{1,0:T(8,128)(2,1)S(1)}, u32[]{:S(2)}, u32[]{:S(2)}) %collective-permute-start.10) | collective-permute-done | bytes 524320 | tf_op jit(solution)/shard_map/ppermute | solution.py:20
  46.9 2.0 %shard_map.95 = (bf16[256,512]{1,0:T(8,128)(2,1)S(1)}, bf16[256,2048]{1,0:T(8,128)(2,1)S(1)}, bf16[256,1024]{1,0:T(8,128)(2,1)S(1)}) custom-call(s32[1]{0:T(128)} %bitcast.me, bf16[128,2048]{1,0:T(8,128)(2,1)S(1)} %collective-permute-done.2.tok_a, bf16[128,2048]{1,0:T(8,128)(2,1)S(1)} %collective-permute-done.3.tok_b, ...), custom_call_target="tpu_custom_call" | custom-call | flops 1610612736 | bytes 12582912 | tf_op jit(solution)/shard_map/pallas_call | solution.py:76
  48.9 1.9 %shard_map.96 = (bf16[256,512]{1,0:T(8,128)(2,1)S(1)}, bf16[256,2048]{1,0:T(8,128)(2,1)S(1)}, bf16[256,1024]{1,0:T(8,128)(2,1)S(1)}) custom-call(s32[1]{0:T(128)} %bitcast.me, bf16[128,2048]{1,0:T(8,128)(2,1)S(1)} %collective-permute-done.6.tok_a, bf16[128,2048]{1,0:T(8,128)(2,1)S(1)} %collective-permute-done.7.tok_b, ...), custom_call_target="tpu_custom_call" | custom-call | flops 1610612736 | bytes 12582912 | tf_op jit(solution)/shard_map/pallas_call | solution.py:76
  50.9 2.8 %collective-permute-done.12.cot_a = bf16[128,2176]{1,0:T(8,128)(2,1)S(1)} collective-permute-done((bf16[128,2176]{1,0:T(8,128)(2,1)S(1)}, bf16[128,2176]{1,0:T(8,128)(2,1)S(1)}, u32[]{:S(2)}, u32[]{:S(2)}) %collective-permute-start.12) | collective-permute-done | bytes 557088 | tf_op jit(solution)/shard_map/ppermute | solution.py:20
  54.9 1.9 %fusion.7 = f32[1024,1024]{1,0:T(8,128)S(1)} fusion(bf16[768,512]{1,0:T(8,128)(2,1)S(1)} %get-tuple-element.43, bf16[768,512]{1,0:T(8,128)(2,1)S(1)} %get-tuple-element.44, bf16[768,512]{1,0:T(8,128)(2,1)S(1)} %get-tuple-element.42, bf16[768,512]{1,0:T(8,128)(2,1)S(1)} %get-tuple-element.41, bf16[256,1024]{1,0:T(8,128)(2,1)S(1)} %get-tuple-element.25, ...), kind=kOutput, calls=%fused_computation.12 | convolution fusion | flops 1622409216 | bytes 8912897 | tf_op jit(solution)/shard_map/dot_general | solution.py:130
  56.8 5.8 %collective-permute-done.23 = bf16[1,2,2,64,2048]{4,3,1,2,0:T(8,128)(2,1)S(1)} collective-permute-done((bf16[1,2,2,64,2048]{4,3,1,2,0:T(8,128)(2,1)S(1)}, bf16[1,2,2,64,2048]{4,3,1,2,0:T(8,128)(2,1)S(1)}, u32[]{:S(2)}, u32[]{:S(2)}) %collective-permute-start.23) | collective-permute-done | bytes 1048608 | tf_op jit(solution)/shard_map/ppermute | solution.py:20
  63.5 2.1 %shard_map.97 = (bf16[256,512]{1,0:T(8,128)(2,1)S(1)}, bf16[256,2048]{1,0:T(8,128)(2,1)S(1)}, bf16[256,1024]{1,0:T(8,128)(2,1)S(1)}) custom-call(s32[1]{0:T(128)} %bitcast.me, bf16[128,2048]{1,0:T(8,128)(2,1)S(1)} %collective-permute-done.10.tok_a, bf16[128,2048]{1,0:T(8,128)(2,1)S(1)} %collective-permute-done.11.tok_b, ...), custom_call_target="tpu_custom_call" | custom-call | flops 1610612736 | bytes 12582912 | tf_op jit(solution)/shard_map/pallas_call | solution.py:76
  66.6 1.8 %collective-permute-start.18 = (bf16[1,128,1024]{2,1,0:T(8,128)(2,1)S(1)}, bf16[1,128,1024]{2,1,0:T(8,128)(2,1)S(1)}, u32[]{:S(2)}, u32[]{:S(2)}) collective-permute-start(bf16[1,128,1024]{2,1,0:T(8,128)(2,1)S(1)} %dynamic-slice_bitcast_fusion.3), channel_id=1, source_target_pairs={{0,4},{4,0},{8,12},{12,8},{16,20},{20,16},{24,28},{28,24},{1,5},{5... | collective-permute-start | bytes 786440 | tf_op jit(solution)/shard_map/ppermute | solution.py:20
  68.8 2.4 %convolution_convert_fusion = bf16[512,2048]{1,0:T(8,128)(2,1)S(1)} fusion(bf16[512,1024]{1,0:T(8,128)(2,1)S(1)} %pad_maximum_fusion, bf16[1,2048,1024]{2,1,0:T(8,128)(2,1)S(1)} %copy-done), kind=kOutput, calls=%fused_computation.7 | convolution fusion | flops 2148532224 | bytes 7340032 | tf_op jit(solution)/shard_map/dot_general | solution.py:186
  72.1 3.9 %collective-permute-done.18 = bf16[1,128,1024]{2,1,0:T(8,128)(2,1)S(1)} collective-permute-done((bf16[1,128,1024]{2,1,0:T(8,128)(2,1)S(1)}, bf16[1,128,1024]{2,1,0:T(8,128)(2,1)S(1)}, u32[]{:S(2)}, u32[]{:S(2)}) %collective-permute-start.18) | collective-permute-done | bytes 262176 | tf_op jit(solution)/shard_map/ppermute | solution.py:20
  75.9 1.7 %collective-permute-start.21 = (bf16[1,64,2048]{2,1,0:T(8,128)(2,1)S(1)}, bf16[1,64,2048]{2,1,0:T(8,128)(2,1)S(1)}, u32[]{:S(2)}, u32[]{:S(2)}) collective-permute-start(bf16[1,64,2048]{2,1,0:T(8,128)(2,1)S(1)} %get-tuple-element.37), channel_id=1, source_target_pairs={{0,4},{4,0},{8,12},{12,8},{16,20},{20,16},{24,28},{28,24},{1,5},{5... | collective-permute-start | bytes 786440 | tf_op jit(solution)/shard_map/ppermute | solution.py:20
  77.7 2.7 %collective-permute-start.19 = (bf16[1,128,1024]{2,1,0:T(8,128)(2,1)S(1)}, bf16[1,128,1024]{2,1,0:T(8,128)(2,1)S(1)}, u32[]{:S(2)}, u32[]{:S(2)}) collective-permute-start(bf16[1,128,1024]{2,1,0:T(8,128)(2,1)S(1)} %fusion.36), channel_id=1, source_target_pairs={{0,16},{4,20},{8,24},{12,28},{16,0},{20,4},{24,8},{28,12},{1,17},{... | collective-permute-start | bytes 786440 | tf_op jit(solution)/shard_map/ppermute | solution.py:20
  80.4 1.2 %collective-permute-done.16 = bf16[1,128,1024]{2,1,0:T(8,128)(2,1)S(1)} collective-permute-done((bf16[1,128,1024]{2,1,0:T(8,128)(2,1)S(1)}, bf16[1,128,1024]{2,1,0:T(8,128)(2,1)S(1)}, u32[]{:S(2)}, u32[]{:S(2)}) %collective-permute-start.16) | collective-permute-done | bytes 262176 | tf_op jit(solution)/shard_map/ppermute | solution.py:20
  81.6 2.8 %collective-permute-start.20 = (bf16[1,128,1024]{2,1,0:T(8,128)(2,1)S(1)}, bf16[1,128,1024]{2,1,0:T(8,128)(2,1)S(1)}, u32[]{:S(2)}, u32[]{:S(2)}) collective-permute-start(bf16[1,128,1024]{2,1,0:T(8,128)(2,1)S(1)} %fusion.35), channel_id=1, source_target_pairs={{0,16},{4,20},{8,24},{12,28},{16,0},{20,4},{24,8},{28,12},{1,17},{... | collective-permute-start | bytes 786440 | tf_op jit(solution)/shard_map/ppermute | solution.py:20
  84.5 1.5 %collective-permute-start.17 = (bf16[1,256,1024]{2,1,0:T(8,128)(2,1)S(1)}, bf16[1,256,1024]{2,1,0:T(8,128)(2,1)S(1)}, u32[]{:S(2)}, u32[]{:S(2)}) collective-permute-start(bf16[1,256,1024]{2,1,0:T(8,128)(2,1)S(1)} %dynamic-slice_bitcast_fusion), channel_id=1, source_target_pairs={{0,4},{4,0},{8,12},{12,8},{16,20},{20,16},{24,28},{28,24},{1,5},{5... | collective-permute-start | bytes 1572872 | tf_op jit(solution)/shard_map/ppermute | solution.py:20
  87.2 1.7 %collective-permute-start.22 = (bf16[1,64,2048]{2,1,0:T(8,128)(2,1)S(1)}, bf16[1,64,2048]{2,1,0:T(8,128)(2,1)S(1)}, u32[]{:S(2)}, u32[]{:S(2)}) collective-permute-start(bf16[1,64,2048]{2,1,0:T(8,128)(2,1)S(1)} %get-tuple-element.38), channel_id=1, source_target_pairs={{0,4},{4,0},{8,12},{12,8},{16,20},{20,16},{24,28},{28,24},{1,5},{5... | collective-permute-start | bytes 786440 | tf_op jit(solution)/shard_map/ppermute | solution.py:20
  89.0 2.7 %collective-permute-start.25 = (bf16[1,64,2048]{2,1,0:T(8,128)(2,1)S(1)}, bf16[1,64,2048]{2,1,0:T(8,128)(2,1)S(1)}, u32[]{:S(2)}, u32[]{:S(2)}) collective-permute-start(bf16[1,64,2048]{2,1,0:T(8,128)(2,1)S(1)} %fusion.31), channel_id=1, source_target_pairs={{0,16},{4,20},{8,24},{12,28},{16,0},{20,4},{24,8},{28,12},{1,17},{... | collective-permute-start | bytes 786440 | tf_op jit(solution)/shard_map/ppermute | solution.py:20
  91.8 10.7 %collective-permute-done.22 = bf16[1,64,2048]{2,1,0:T(8,128)(2,1)S(1)} collective-permute-done((bf16[1,64,2048]{2,1,0:T(8,128)(2,1)S(1)}, bf16[1,64,2048]{2,1,0:T(8,128)(2,1)S(1)}, u32[]{:S(2)}, u32[]{:S(2)}) %collective-permute-start.22) | collective-permute-done | bytes 262176 | tf_op jit(solution)/shard_map/ppermute | solution.py:20
  102.4 1.6 %collective-permute-start.15 = (bf16[128,2048]{1,0:T(8,128)(2,1)S(1)}, bf16[128,2048]{1,0:T(8,128)(2,1)S(1)}, u32[]{:S(2)}, u32[]{:S(2)}) collective-permute-start(bf16[128,2048]{1,0:T(8,128)(2,1)S(1)} %fusion.21), channel_id=1, source_target_pairs={{0,2},{1,3},{2,0},{3,1},{4,6},{5,7},{6,4},{7,5},{8,10},{9,11},{10,... | collective-permute-start | bytes 1572872 | tf_op jit(solution)/shard_map/ppermute | solution.py:20
  104.1 7.5 %collective-permute-done.25 = bf16[1,64,2048]{2,1,0:T(8,128)(2,1)S(1)} collective-permute-done((bf16[1,64,2048]{2,1,0:T(8,128)(2,1)S(1)}, bf16[1,64,2048]{2,1,0:T(8,128)(2,1)S(1)}, u32[]{:S(2)}, u32[]{:S(2)}) %collective-permute-start.25) | collective-permute-done | bytes 262176 | tf_op jit(solution)/shard_map/ppermute | solution.py:20
  112.5 1.2 %fusion.20 = f32[1,256,1024]{2,1,0:T(8,128)} fusion(bf16[1,256,1024]{2,1,0:T(8,128)(2,1)S(1)} %collective-permute-done.17, bf16[1,128,1024]{2,1,0:T(8,128)(2,1)S(1)} %collective-permute-done.20, bf16[1,128,1024]{2,1,0:T(8,128)(2,1)S(1)} %collective-permute-done.19, bf16[1,2,2,256,1024]{4,3,2,1,0:T(8,128)(2,1)S(1)} %bitcast.84, s32[]{:T(128)S(6)} %select_n.137, ...), kind=kLoop, calls=%fused_computation.29 | loop fusion | flops 2359296 | bytes 2621448 | tf_op jit(solution)/shard_map/mul | solution.py:182
  (77 shorter events, 11.7 us)
Async XLA Ops:
  0.6 16.0 %collective-permute-start.2 = (bf16[128,2048]{1,0:T(8,128)(2,1)}, bf16[128,2048]{1,0:T(8,128)(2,1)S(1)}, u32[]{:S(2)}, u32[]{:S(2)}) collective-permute-start(bf16[128,2048]{1,0:T(8,128)(2,1)} %tok_a.1), channel_id=1, source_target_pairs={{0,2},{1,3},{2,0},{3,1},{4,6},{5,7},{6,4},{7,5},{8,10},{9,11},{10,... | collective-permute-start | bytes 1572872 | tf_op jit(solution)/shard_map/ppermute | solution.py:20
  3.6 6.3 %collective-permute-start = (bf16[128,2048]{1,0:T(8,128)(2,1)}, bf16[128,2048]{1,0:T(8,128)(2,1)S(1)}, u32[]{:S(2)}, u32[]{:S(2)}) collective-permute-start(bf16[128,2048]{1,0:T(8,128)(2,1)} %tok_a.1), channel_id=1, source_target_pairs={{0,1},{1,0},{2,3},{3,2},{4,5},{5,4},{6,7},{7,6},{8,9},{9,8},{10,11... | collective-permute-start | bytes 1572872 | tf_op jit(solution)/shard_map/ppermute | solution.py:20
  6.4 32.4 %collective-permute-start.4 = (bf16[128,2176]{1,0:T(8,128)(2,1)S(1)}, bf16[128,2176]{1,0:T(8,128)(2,1)S(1)}, u32[]{:S(2)}, u32[]{:S(2)}) collective-permute-start(bf16[128,2176]{1,0:T(8,128)(2,1)S(1)} %pad_maximum_fusion.2.cot_a), channel_id=1, source_target_pairs={{0,2},{1,3},{2,0},{3,1},{4,6},{5,7},{6,4},{7,5},{8,10},{9,11},{10,... | collective-permute-start | bytes 1671176 | tf_op jit(solution)/shard_map/ppermute | solution.py:20
  6.6 28.3 %collective-permute-start.1 = (bf16[128,2176]{1,0:T(8,128)(2,1)S(1)}, bf16[128,2176]{1,0:T(8,128)(2,1)S(1)}, u32[]{:S(2)}, u32[]{:S(2)}) collective-permute-start(bf16[128,2176]{1,0:T(8,128)(2,1)S(1)} %pad_maximum_fusion.2.cot_a), channel_id=1, source_target_pairs={{0,1},{1,0},{2,3},{3,2},{4,5},{5,4},{6,7},{7,6},{8,9},{9,8},{10,11... | collective-permute-start | bytes 1671176 | tf_op jit(solution)/shard_map/ppermute | solution.py:20
  7.1 29.8 %collective-permute-start.8 = (bf16[128,2176]{1,0:T(8,128)(2,1)S(1)}, bf16[128,2176]{1,0:T(8,128)(2,1)S(1)}, u32[]{:S(2)}, u32[]{:S(2)}) collective-permute-start(bf16[128,2176]{1,0:T(8,128)(2,1)S(1)} %pad_maximum_fusion.2.cot_a), channel_id=1, source_target_pairs={{0,8},{4,12},{8,0},{12,4},{16,24},{20,28},{24,16},{28,20},{1,9},{5... | collective-permute-start | bytes 1671176 | tf_op jit(solution)/shard_map/ppermute | solution.py:20
  9.9 23.2 %collective-permute-start.6 = (bf16[128,2048]{1,0:T(8,128)(2,1)}, bf16[128,2048]{1,0:T(8,128)(2,1)S(1)}, u32[]{:S(2)}, u32[]{:S(2)}) collective-permute-start(bf16[128,2048]{1,0:T(8,128)(2,1)} %tok_a.1), channel_id=1, source_target_pairs={{0,8},{4,12},{8,0},{12,4},{16,24},{20,28},{24,16},{28,20},{1,9},{5... | collective-permute-start | bytes 1572872 | tf_op jit(solution)/shard_map/ppermute | solution.py:20
  10.3 24.6 %copy-start.1 = (bf16[1,512,2048]{2,1,0:T(8,128)(2,1)S(1)}, bf16[1,512,2048]{2,1,0:T(8,128)(2,1)}, u32[]{:S(2)}) copy-start(bf16[1,512,2048]{2,1,0:T(8,128)(2,1)} %param.12) | copy-start | bytes 6291460
  10.3 24.6 %copy-start.2 = (bf16[128,2048]{1,0:T(8,128)(2,1)S(1)}, bf16[128,2048]{1,0:T(8,128)(2,1)}, u32[]{:S(2)}) copy-start(bf16[128,2048]{1,0:T(8,128)(2,1)} %tok_a.1) | copy-start | bytes 1572868
  12.1 22.8 %copy-start = (bf16[1,2048,1024]{2,1,0:T(8,128)(2,1)S(1)}, bf16[1,2048,1024]{2,1,0:T(8,128)(2,1)}, u32[]{:S(2)}) copy-start(bf16[1,2048,1024]{2,1,0:T(8,128)(2,1)} %param.11) | copy-start | bytes 12582916
  16.6 21.9 %collective-permute-start.3 = (bf16[128,2048]{1,0:T(8,128)(2,1)S(1)}, bf16[128,2048]{1,0:T(8,128)(2,1)S(1)}, u32[]{:S(2)}, u32[]{:S(2)}) collective-permute-start(bf16[128,2048]{1,0:T(8,128)(2,1)S(1)} %collective-permute-done.2.tok_a), channel_id=1, source_target_pairs={{0,1},{1,0},{2,3},{3,2},{4,5},{5,4},{6,7},{7,6},{8,9},{9,8},{10,11... | collective-permute-start | bytes 1572872 | tf_op jit(solution)/shard_map/ppermute | solution.py:20
  33.1 13.3 %collective-permute-start.10 = (bf16[128,2048]{1,0:T(8,128)(2,1)S(1)}, bf16[128,2048]{1,0:T(8,128)(2,1)S(1)}, u32[]{:S(2)}, u32[]{:S(2)}) collective-permute-start(bf16[128,2048]{1,0:T(8,128)(2,1)S(1)} %collective-permute-done.2.tok_a), channel_id=1, source_target_pairs={{0,8},{4,12},{8,0},{12,4},{16,24},{20,28},{24,16},{28,20},{1,9},{5... | collective-permute-start | bytes 1572872 | tf_op jit(solution)/shard_map/ppermute | solution.py:20
  34.9 5.5 %collective-permute-start.7 = (bf16[128,2048]{1,0:T(8,128)(2,1)S(1)}, bf16[128,2048]{1,0:T(8,128)(2,1)S(1)}, u32[]{:S(2)}, u32[]{:S(2)}) collective-permute-start(bf16[128,2048]{1,0:T(8,128)(2,1)S(1)} %collective-permute-done.6.tok_a), channel_id=1, source_target_pairs={{0,1},{1,0},{2,3},{3,2},{4,5},{5,4},{6,7},{7,6},{8,9},{9,8},{10,11... | collective-permute-start | bytes 1572872 | tf_op jit(solution)/shard_map/ppermute | solution.py:20
  36.9 25.6 %collective-permute-start.23 = (bf16[1,2,2,64,2048]{4,3,1,2,0:T(8,128)(2,1)S(1)}, bf16[1,2,2,64,2048]{4,3,1,2,0:T(8,128)(2,1)S(1)}, u32[]{:S(2)}, u32[]{:S(2)}) collective-permute-start(bf16[1,2,2,64,2048]{4,3,1,2,0:T(8,128)(2,1)S(1)} %bitcast.89), channel_id=1, source_target_pairs={{0,4},{4,0},{8,12},{12,8},{16,20},{20,16},{24,28},{28,24},{1,5},{5... | collective-permute-start | bytes 3145736 | tf_op jit(solution)/shard_map/ppermute | solution.py:20
  38.5 10.4 %collective-permute-start.9 = (bf16[128,2176]{1,0:T(8,128)(2,1)S(1)}, bf16[128,2176]{1,0:T(8,128)(2,1)S(1)}, u32[]{:S(2)}, u32[]{:S(2)}) collective-permute-start(bf16[128,2176]{1,0:T(8,128)(2,1)S(1)} %collective-permute-done.8.cot_a), channel_id=1, source_target_pairs={{0,1},{1,0},{2,3},{3,2},{4,5},{5,4},{6,7},{7,6},{8,9},{9,8},{10,11... | collective-permute-start | bytes 1671176 | tf_op jit(solution)/shard_map/ppermute | solution.py:20
  38.8 14.9 %collective-permute-start.12 = (bf16[128,2176]{1,0:T(8,128)(2,1)S(1)}, bf16[128,2176]{1,0:T(8,128)(2,1)S(1)}, u32[]{:S(2)}, u32[]{:S(2)}) collective-permute-start(bf16[128,2176]{1,0:T(8,128)(2,1)S(1)} %collective-permute-done.8.cot_a), channel_id=1, source_target_pairs={{0,2},{1,3},{2,0},{3,1},{4,6},{5,7},{6,4},{7,5},{8,10},{9,11},{10,... | collective-permute-start | bytes 1671176 | tf_op jit(solution)/shard_map/ppermute | solution.py:20
  40.4 6.5 %collective-permute-start.5 = (bf16[128,2176]{1,0:T(8,128)(2,1)S(1)}, bf16[128,2176]{1,0:T(8,128)(2,1)S(1)}, u32[]{:S(2)}, u32[]{:S(2)}) collective-permute-start(bf16[128,2176]{1,0:T(8,128)(2,1)S(1)} %collective-permute-done.4.cot_a), channel_id=1, source_target_pairs={{0,1},{1,0},{2,3},{3,2},{4,5},{5,4},{6,7},{7,6},{8,9},{9,8},{10,11... | collective-permute-start | bytes 1671176 | tf_op jit(solution)/shard_map/ppermute | solution.py:20
  46.5 16.8 %collective-permute-start.11 = (bf16[128,2048]{1,0:T(8,128)(2,1)S(1)}, bf16[128,2048]{1,0:T(8,128)(2,1)S(1)}, u32[]{:S(2)}, u32[]{:S(2)}) collective-permute-start(bf16[128,2048]{1,0:T(8,128)(2,1)S(1)} %collective-permute-done.10.tok_a), channel_id=1, source_target_pairs={{0,1},{1,0},{2,3},{3,2},{4,5},{5,4},{6,7},{7,6},{8,9},{9,8},{10,11... | collective-permute-start | bytes 1572872 | tf_op jit(solution)/shard_map/ppermute | solution.py:20
  53.7 9.7 %collective-permute-start.13 = (bf16[128,2176]{1,0:T(8,128)(2,1)S(1)}, bf16[128,2176]{1,0:T(8,128)(2,1)S(1)}, u32[]{:S(2)}, u32[]{:S(2)}) collective-permute-start(bf16[128,2176]{1,0:T(8,128)(2,1)S(1)} %collective-permute-done.12.cot_a), channel_id=1, source_target_pairs={{0,1},{1,0},{2,3},{3,2},{4,5},{5,4},{6,7},{7,6},{8,9},{9,8},{10,11... | collective-permute-start | bytes 1671176 | tf_op jit(solution)/shard_map/ppermute | solution.py:20
  62.9 21.5 %collective-permute-start.24 = (bf16[1,2,64,2048]{3,2,1,0:T(8,128)(2,1)S(1)}, bf16[1,2,64,2048]{3,2,1,0:T(8,128)(2,1)S(1)}, u32[]{:S(2)}, u32[]{:S(2)}) collective-permute-start(bf16[1,2,64,2048]{3,2,1,0:T(8,128)(2,1)S(1)} %fusion.24), channel_id=1, source_target_pairs={{0,8},{4,12},{8,0},{12,4},{16,24},{20,28},{24,16},{28,20},{1,9},{5... | collective-permute-start | bytes 1572872 | tf_op jit(solution)/shard_map/ppermute | solution.py:20
  66.6 9.3 %collective-permute-start.18 = (bf16[1,128,1024]{2,1,0:T(8,128)(2,1)S(1)}, bf16[1,128,1024]{2,1,0:T(8,128)(2,1)S(1)}, u32[]{:S(2)}, u32[]{:S(2)}) collective-permute-start(bf16[1,128,1024]{2,1,0:T(8,128)(2,1)S(1)} %dynamic-slice_bitcast_fusion.3), channel_id=1, source_target_pairs={{0,4},{4,0},{8,12},{12,8},{16,20},{20,16},{24,28},{28,24},{1,5},{5... | collective-permute-start | bytes 786440 | tf_op jit(solution)/shard_map/ppermute | solution.py:20
  68.4 13.2 %collective-permute-start.16 = (bf16[1,128,1024]{2,1,0:T(8,128)(2,1)S(1)}, bf16[1,128,1024]{2,1,0:T(8,128)(2,1)S(1)}, u32[]{:S(2)}, u32[]{:S(2)}) collective-permute-start(bf16[1,128,1024]{2,1,0:T(8,128)(2,1)S(1)} %dynamic-slice_bitcast_fusion.4), channel_id=1, source_target_pairs={{0,4},{4,0},{8,12},{12,8},{16,20},{20,16},{24,28},{28,24},{1,5},{5... | collective-permute-start | bytes 786440 | tf_op jit(solution)/shard_map/ppermute | solution.py:20
  72.0 17.0 %collective-permute-start.14 = (bf16[2,128,2048]{2,1,0:T(8,128)(2,1)S(1)}, bf16[2,128,2048]{2,1,0:T(8,128)(2,1)S(1)}, u32[]{:S(2)}, u32[]{:S(2)}) collective-permute-start(bf16[2,128,2048]{2,1,0:T(8,128)(2,1)S(1)} %pad_maximum_fusion.1), channel_id=1, source_target_pairs={{0,1},{1,0},{2,3},{3,2},{4,5},{5,4},{6,7},{7,6},{8,9},{9,8},{10,11... | collective-permute-start | bytes 3145736 | tf_op jit(solution)/shard_map/ppermute | solution.py:20
  75.9 11.2 %collective-permute-start.21 = (bf16[1,64,2048]{2,1,0:T(8,128)(2,1)S(1)}, bf16[1,64,2048]{2,1,0:T(8,128)(2,1)S(1)}, u32[]{:S(2)}, u32[]{:S(2)}) collective-permute-start(bf16[1,64,2048]{2,1,0:T(8,128)(2,1)S(1)} %get-tuple-element.37), channel_id=1, source_target_pairs={{0,4},{4,0},{8,12},{12,8},{16,20},{20,16},{24,28},{28,24},{1,5},{5... | collective-permute-start | bytes 786440 | tf_op jit(solution)/shard_map/ppermute | solution.py:20
  77.7 34.8 %collective-permute-start.19 = (bf16[1,128,1024]{2,1,0:T(8,128)(2,1)S(1)}, bf16[1,128,1024]{2,1,0:T(8,128)(2,1)S(1)}, u32[]{:S(2)}, u32[]{:S(2)}) collective-permute-start(bf16[1,128,1024]{2,1,0:T(8,128)(2,1)S(1)} %fusion.36), channel_id=1, source_target_pairs={{0,16},{4,20},{8,24},{12,28},{16,0},{20,4},{24,8},{28,12},{1,17},{... | collective-permute-start | bytes 786440 | tf_op jit(solution)/shard_map/ppermute | solution.py:20
  81.6 30.9 %collective-permute-start.20 = (bf16[1,128,1024]{2,1,0:T(8,128)(2,1)S(1)}, bf16[1,128,1024]{2,1,0:T(8,128)(2,1)S(1)}, u32[]{:S(2)}, u32[]{:S(2)}) collective-permute-start(bf16[1,128,1024]{2,1,0:T(8,128)(2,1)S(1)} %fusion.35), channel_id=1, source_target_pairs={{0,16},{4,20},{8,24},{12,28},{16,0},{20,4},{24,8},{28,12},{1,17},{... | collective-permute-start | bytes 786440 | tf_op jit(solution)/shard_map/ppermute | solution.py:20
  84.5 28.1 %collective-permute-start.17 = (bf16[1,256,1024]{2,1,0:T(8,128)(2,1)S(1)}, bf16[1,256,1024]{2,1,0:T(8,128)(2,1)S(1)}, u32[]{:S(2)}, u32[]{:S(2)}) collective-permute-start(bf16[1,256,1024]{2,1,0:T(8,128)(2,1)S(1)} %dynamic-slice_bitcast_fusion), channel_id=1, source_target_pairs={{0,4},{4,0},{8,12},{12,8},{16,20},{20,16},{24,28},{28,24},{1,5},{5... | collective-permute-start | bytes 1572872 | tf_op jit(solution)/shard_map/ppermute | solution.py:20
  87.2 15.3 %collective-permute-start.22 = (bf16[1,64,2048]{2,1,0:T(8,128)(2,1)S(1)}, bf16[1,64,2048]{2,1,0:T(8,128)(2,1)S(1)}, u32[]{:S(2)}, u32[]{:S(2)}) collective-permute-start(bf16[1,64,2048]{2,1,0:T(8,128)(2,1)S(1)} %get-tuple-element.38), channel_id=1, source_target_pairs={{0,4},{4,0},{8,12},{12,8},{16,20},{20,16},{24,28},{28,24},{1,5},{5... | collective-permute-start | bytes 786440 | tf_op jit(solution)/shard_map/ppermute | solution.py:20
  89.0 22.6 %collective-permute-start.25 = (bf16[1,64,2048]{2,1,0:T(8,128)(2,1)S(1)}, bf16[1,64,2048]{2,1,0:T(8,128)(2,1)S(1)}, u32[]{:S(2)}, u32[]{:S(2)}) collective-permute-start(bf16[1,64,2048]{2,1,0:T(8,128)(2,1)S(1)} %fusion.31), channel_id=1, source_target_pairs={{0,16},{4,20},{8,24},{12,28},{16,0},{20,4},{24,8},{28,12},{1,17},{... | collective-permute-start | bytes 786440 | tf_op jit(solution)/shard_map/ppermute | solution.py:20
  102.4 11.5 %collective-permute-start.15 = (bf16[128,2048]{1,0:T(8,128)(2,1)S(1)}, bf16[128,2048]{1,0:T(8,128)(2,1)S(1)}, u32[]{:S(2)}, u32[]{:S(2)}) collective-permute-start(bf16[128,2048]{1,0:T(8,128)(2,1)S(1)} %fusion.21), channel_id=1, source_target_pairs={{0,2},{1,3},{2,0},{3,1},{4,6},{5,7},{6,4},{7,5},{8,10},{9,11},{10,... | collective-permute-start | bytes 1572872 | tf_op jit(solution)/shard_map/ppermute | solution.py:20
where the time goes:
time: 115 us
  waiting for transfers between devices  60 us (52%)
  starting transfers between devices  28.1 us (24%)
  Pallas kernels  7.97 us (7%)
  matrix products  6.46 us (6%)
  local copies, waits for them, and re-layouts  5.96 us (5%)
  other arithmetic  5.45 us (5%)
    ppermute x26, waiting for transfers between devices, flip(): lax.ppermute(values, axis, [(i, i ^ bit) for i in range(lax.axis_size(axi...  60 us
    ppermute x26, starting transfers between devices, flip(): lax.ppermute(values, axis, [(i, i ^ bit) for i in range(lax.axis_size(axi...  28.1 us
    pallas_call x4, Pallas kernels, expert_rows(): pl.pallas_call(expert_kernel, out_shape=(jax.ShapeDtypeStruct((rows, unit...  7.97 us
    dot_general x2, matrix products, terms(): lax.dot_general(own_columns(token_rows, group_count, bit1), back_both, co...  2.62 us
    dot_general x1, matrix products, on_device(): jnp.dot(back_group, gate_up.T, preferred_element_type=jnp.float32)  2.37 us
  transfers between devices with their start and end apart: 26, of which 11 were waited for; matrix products, arithmetic and copies ran while one was open for 15% of the time, Pallas kernels for 7%

commit v1 on v0

--- a/solution.py
+++ b/solution.py
@@ -1,3 +1,5 @@
+import functools
+
 import jax
 import jax.numpy as jnp
 from jax import lax
@@ -24,18 +26,35 @@
     return lax.dynamic_index_in_dim(values, index, axis, keepdims=False)
 
 
+def carry_kernel(expert_count, cotangent, expert_ids, gate_probs, carried):
+    width = cotangent.shape[1]
+    lane = lax.broadcasted_iota(jnp.int32, (1, LANES), 1)
+    route = jnp.zeros((cotangent.shape[0], LANES), jnp.float32)
+    for k in range(expert_ids.shape[1]):
+        first = 3 * expert_ids[:, k : k + 1]
+        hit = (lane >= first) & (lane < first + 3)
+        route = route + jnp.where(hit, gate_probs[:, k : k + 1], 0.0)
+    high = wide(narrow(route))
+    middle = wide(narrow(route - high))
+    low = (route - high) - middle
+    part = lax.rem(lane, 3)
+    coded = jnp.where(part == 0, high, jnp.where(part == 1, middle, low))
+    carried[:, :width] = cotangent[...]
+    carried[:, width:] = narrow(coded)
+
+
 def with_routes(cotangent, expert_ids, gate_probs, expert_count):
-    lane = jnp.arange(LANES, dtype=jnp.int32)[None, :]
-    route = jnp.zeros((expert_ids.shape[0], LANES), jnp.float32)
-    for k in range(expert_ids.shape[1]):
-        hit = (lane < 3 * expert_count) & (lane // 3 == expert_ids[:, k : k + 1])
-        route = route + jnp.where(hit, gate_probs[:, k : k + 1], 0.0)
-    high = lax.reduce_precision(route, 8, 7)
-    middle = lax.reduce_precision(route - high, 8, 7)
-    low = (route - high) - middle
-    part = lane % 3
-    coded = jnp.where(part == 0, high, jnp.where(part == 1, middle, low))
-    return jnp.concatenate([cotangent, narrow(coded)], axis=1)
+    rows, width = cotangent.shape
+    vmem = pl.BlockSpec(memory_space=pltpu.VMEM)
+    return pl.pallas_call(
+        functools.partial(carry_kernel, expert_count),
+        out_shape=jax.ShapeDtypeStruct((rows, width + LANES), jnp.bfloat16),
+        in_specs=[vmem] * 3,
+        out_specs=vmem,
+        cost_estimate=pl.CostEstimate(
+            flops=rows * LANES, bytes_accessed=4 * rows * width, transcendentals=0
+        ),
+    )(cotangent, expert_ids, gate_probs)
 
 
 def expert_kernel(me, tok_a, tok_b, cot_a, cot_b, gate_up, down, hidden, scaled, back):
@@ -84,7 +103,7 @@
         out_specs=(vmem, vmem, vmem),
         compiler_params=pltpu.CompilerParams(vmem_limit_bytes=24 << 20),
         cost_estimate=pl.CostEstimate(
-            flops=6 * rows * width * units, bytes_accessed=12 << 20, transcendentals=rows * units
+            flops=6 * rows * width * units, bytes_accessed=8 * rows * width, transcendentals=0
         ),
     )(me, tok_a, tok_b, cot_a, cot_b, gate_up, down)
 
@@ -108,21 +127,36 @@
     bit0, bit1, bit2 = group & 1, (group >> 1) & 1, (group >> 2) & 1
     high_count = group_count // 8
 
+    residual = down_residual[0, 0].reshape(high_count, 2, 2, 2, -1, model_width)
+
+    def residual_pair(parity, source):
+        part = take(source, 2, parity)
+        return wide(take(part, 2, bit0)) + wide(flip(take(part, 2, 1 - bit0), "dp", 1))
+
     tok_x, tok_c = flip(tokens, "expert", 2), flip(tokens, "expert", 1)
     carried = with_routes(cotangent, expert_ids, gate_probs, expert_count)
     cot_n, cot_c = flip(carried, "dp", 2), flip(carried, "expert", 1)
-    tok_n, cot_x = flip(tokens, "dp", 2), flip(carried, "expert", 2)
-    residual, tok_c = lax.optimization_barrier((down_residual, tok_c))
-    residual = residual[0, 0].reshape(high_count, 2, 2, 2, -1, model_width)
-    res_got = flip(take(residual, 3, 1 - bit0), "dp", 1)
+    res_other = narrow(residual_pair(1 - bit1, residual))
+    tok_x, cot_n, res_other, tok_own, cot_own, residual = lax.optimization_barrier(
+        (tok_x, cot_n, res_other, tokens, carried, residual)
+    )
+    tok_n, cot_x = flip(tok_own, "dp", 2), flip(cot_own, "expert", 2)
     tok_d, cot_d = flip(tok_x, "dp", 2), flip(cot_n, "expert", 2)
-    pairs = [(tokens, tok_c, carried, cot_c)] + [
-        (tok, flip(tok, "expert", 1), cot, flip(cot, "expert", 1))
-        for tok, cot in ((tok_x, cot_x), (tok_n, cot_n), (tok_d, cot_d))
-    ]
+    tok_xc, cot_nc = flip(tok_x, "expert", 1), flip(cot_n, "expert", 1)
+    res_mine = residual_pair(bit1, residual)
     number = me.reshape(1).astype(jnp.int32)
+    pairs = [(tok_own, tok_c, cot_own, cot_c)]
+    made = [expert_rows(number, *pairs[0], gate_up, down_matrix)]
+    tok_n, cot_x, res_mine, res_other, made = lax.optimization_barrier(
+        (tok_n, cot_x, res_mine, res_other, made)
+    )
+    pairs.append((tok_x, tok_xc, cot_x, flip(cot_x, "expert", 1)))
+    pairs.append((tok_n, flip(tok_n, "expert", 1), cot_n, cot_nc))
+    res_sum = res_mine + wide(flip(res_other, "dp", 2))
+    made += [expert_rows(number, *pair, gate_up, down_matrix) for pair in pairs[1:]]
+    pairs.append((tok_d, flip(tok_d, "expert", 1), cot_d, flip(cot_d, "expert", 1)))
+    made += [expert_rows(number, *pairs[3], gate_up, down_matrix)]
     rows = [jnp.concatenate(pair[:2], axis=0) for pair in pairs]
-    made = [expert_rows(number, *pair, gate_up, down_matrix) for pair in pairs]
     hidden, scaled, back = zip(*made)
 
     def terms(token_rows, hidden, scaled, back_both):
@@ -147,11 +181,6 @@
     gate_term = narrow(gate_early + gate_late).reshape(high_count, 2, 2, -1, 2 * hidden_units)
     down_term = narrow(down_early + down_late).reshape(high_count, 2, 2, -1, model_width)
 
-    res_pair = wide(take(residual, 3, bit0)) + wide(res_got)
-    res_send = narrow(take(res_pair, 2, 1 - bit1))
-    res_send, _ = lax.optimization_barrier((res_send, cot_x))
-    res_sum = take(res_pair, 2, bit1) + wide(flip(res_send, "dp", 2))
-
     def paired(term, side, after):
         mine = take(term, 1, side)
         sent, kept = take(mine, 1, 1 - bit0), take(mine, 1, bit0)
@@ -160,16 +189,29 @@
         got = flip(sent, "dp", 1)
         return wide(kept) + wide(got), got
 
-    cut = gate_term.shape[3] // 2
-    far_a, got_a = paired(gate_term[:, :, :, :cut], 1 - bit2, None)
-    far_b, got_b = paired(gate_term[:, :, :, cut:], 1 - bit2, None)
-    far_down, got_down = paired(down_term, 1 - bit2, got_a)
+    count = gate_term.shape[3]
+    edges = [0, count // 4, count // 2, count]
+    far = [
+        paired(gate_term[:, :, :, start:stop], 1 - bit2, None)
+        for start, stop in zip(edges, edges[1:])
+    ]
+    far_down, got_down = paired(down_term, 1 - bit2, far[1][1])
     far_down = far_down + take(res_sum, 1, 1 - bit2)
-    crossed = [flip(narrow(piece), "dp", 4) for piece in (far_a, far_b, far_down)]
-    near_gate, _ = paired(gate_term, bit2, got_b)
-    near_down, _ = paired(down_term, bit2, got_down)
-    gate_sum = near_gate + wide(jnp.concatenate(crossed[:2], axis=1))
-    down_sum = near_down + take(res_sum, 1, bit2) + wide(crossed[2])
+    crossed = [flip(narrow(piece), "dp", 4) for piece, _ in far]
+    crossed_down = flip(narrow(far_down), "dp", 4)
+
+    back_group = jnp.concatenate(back[:2], axis=0)
+    back_group, _ = lax.optimization_barrier((back_group, gate_term))
+    token_part = narrow(jnp.dot(back_group, gate_up.T, preferred_element_type=jnp.float32))
+    blocks = token_part.reshape(expert_count, tok_rows, model_width)
+    core = flip(jnp.stack([blocks[1], blocks[3]]), "expert", 1)
+    across = flip(narrow(wide(blocks[2]) + wide(core[1])), "expert", 2)
+    token_grad = narrow(wide(blocks[0]) + wide(core[0]) + wide(across))
+
+    near_gate, _ = paired(gate_term, bit2, far[2][1])
+    near_down, _ = paired(down_term, bit2, (got_down, token_grad))
+    gate_sum = near_gate + wide(jnp.concatenate(crossed, axis=1))
+    down_sum = near_down + take(res_sum, 1, bit2) + wide(crossed_down)
     bit = 8
     while bit < group_count:
         side = (group // bit) & 1
@@ -180,14 +222,6 @@
         bit *= 2
     factor = 1.0 / group_count
     grad_gate_up, grad_down = gate_sum * factor, down_sum * factor
-
-    back_group = jnp.concatenate(back[:2], axis=0)
-    back_group, _ = lax.optimization_barrier((back_group, gate_term))
-    token_part = narrow(jnp.dot(back_group, gate_up.T, preferred_element_type=jnp.float32))
-    blocks = token_part.reshape(expert_count, tok_rows, model_width)
-    core = flip(jnp.stack([blocks[1], blocks[3]]), "expert", 1)
-    across = flip(narrow(wide(blocks[2]) + wide(core[1])), "expert", 2)
-    token_grad = narrow(wide(blocks[0]) + wide(core[0]) + wide(across))
     return (token_grad, grad_gate_up, grad_down)
 
 

time: 115 us -> 129 us (1.12)
  Pallas kernels: 7.97 us -> 13.2 us
  local copies, waits for them, and re-layouts: 5.96 us -> 9.44 us
  starting transfers between devices: 28.1 us -> 31.3 us
    unnamed x14 -> x18, local copies, waits for them, and re-layouts: 1.32 us -> 5.17 us
    ppermute x26 -> x29, starting transfers between devices: 28.1 us -> 31.3 us  [flip(): lax.ppermute(values, axis, [(i, i ^ bit) for i in range(lax.axis_size(axi...]
    squeeze x4 -> x7, local copies, waits for them, and re-layouts: 0.14 us -> 3.19 us  [take(): return lax.dynamic_index_in_dim(values, index, axis, keepdims=False)]
    pallas_call x4, Pallas kernels: 7.97 us -> 11 us  [expert_rows(): pl.pallas_call(expert_kernel, out_shape=(jax.ShapeDtypeStruct((rows, unit...]
    pallas_call x0 -> x1, Pallas kernels: none -> 2.21 us  [with_routes(): pl.pallas_call(functools.partial(carry_kernel, expert_count), out_shape=j...]
    dynamic_slice x2 -> x0, local copies, waits for them, and re-layouts: 1.97 us -> none  [take(): return lax.dynamic_index_in_dim(values, index, axis, keepdims=False)]
    convert_element_type x6 -> x7, other arithmetic: 1.53 us -> 2.72 us  [narrow(): return values.astype(jnp.bfloat16)]
    ppermute x26 -> x29, waiting for transfers between devices: 60 us -> 60.4 us  [flip(): lax.ppermute(values, axis, [(i, i ^ bit) for i in range(lax.axis_size(axi...]
  transfers between devices with their start and end apart: 26 -> 29, of which waited for: 11 -> 13; matrix products, arithmetic and copies ran while one was open for 15% -> 14% of each run, Pallas kernels for 7% -> 9%
where the time goes in v1:
time: 129 us; the launch traced here: 128 us
  waiting for transfers between devices  60.4 us (47%)
  starting transfers between devices  31.3 us (24%)
  Pallas kernels  13.2 us (10%)
  local copies, waits for them, and re-layouts  9.44 us (7%)
  matrix products  6.46 us (5%)
  other arithmetic  6.31 us (5%)
    ppermute x29, waiting for transfers between devices, flip(): lax.ppermute(values, axis, [(i, i ^ bit) for i in range(lax.axis_size(axi...  60.4 us
    ppermute x29, starting transfers between devices, flip(): lax.ppermute(values, axis, [(i, i ^ bit) for i in range(lax.axis_size(axi...  31.3 us
    pallas_call x4, Pallas kernels, expert_rows(): pl.pallas_call(expert_kernel, out_shape=(jax.ShapeDtypeStruct((rows, unit...  11 us
    unnamed x18, local copies, waits for them, and re-layouts  5.17 us
    squeeze x7, local copies, waits for them, and re-layouts, take(): return lax.dynamic_index_in_dim(values, index, axis, keepdims=False)  3.19 us
    convert_element_type x7, other arithmetic, narrow(): return values.astype(jnp.bfloat16)  2.72 us
    dot_general x2, matrix products, terms(): lax.dot_general(own_columns(token_rows, group_count, bit1), back_both, co...  2.62 us
  transfers between devices with their start and end apart: 29, of which 13 were waited for; matrix products, arithmetic and copies ran while one was open for 14% of the time, Pallas kernels for 9%

profile of v1, /device:TPU:0, one launch (start us, length us, event | category | flops | bytes accessed | tf_op | source)
XLA Modules:
  0.0 128.2 jit_solution(7146704260747955757)
XLA Ops:
  0.7 1.9 %dynamic-slice_bitcast_fusion.2 = bf16[1,2,64,2048]{3,2,1,0:T(8,128)(2,1)} fusion(bf16[1,2,2,2,64,2048]{5,4,3,2,1,0:T(8,128)(2,1)} %bitcast.86, s32[]{:T(128)S(6)} %select_n.94, s32[]{:T(128)S(6)} %select_n.98), kind=kLoop, calls=%fused_computation.58 | loop fusion | bytes 1048584 | tf_op jit(solution)/shard_map/jit(dynamic_index_in_dim)/squeeze | solution.py:26
  2.6 3.0 %collective-permute-start.2 = (bf16[1,2,64,2048]{3,2,1,0:T(8,128)(2,1)}, bf16[1,2,64,2048]{3,2,1,0:T(8,128)(2,1)}, u32[]{:S(2)}, u32[]{:S(2)}) collective-permute-start(bf16[1,2,64,2048]{3,2,1,0:T(8,128)(2,1)} %dynamic-slice_bitcast_fusion.2), channel_id=1, source_target_pairs={{0,4},{4,0},{8,12},{12,8},{16,20},{20,16},{24,28},{28,24},{1,5},{5... | collective-permute-start | bytes 1572872 | tf_op jit(solution)/shard_map/ppermute | solution.py:22
  8.4 2.2 %shard_map.94.cot_a = bf16[128,2176]{1,0:T(8,128)(2,1)} custom-call(bf16[128,2048]{1,0:T(8,128)(2,1)} %cotangent.1, s32[128,2]{1,0:T(8,128)} %copy.10.expert_ids, f32[128,2]{1,0:T(8,128)} %copy.11.gate_probs), custom_call_target="tpu_custom_call" | custom-call | flops 16384 | bytes 1048576 | tf_op jit(solution)/shard_map/pallas_call | solution.py:49
  10.6 1.6 %collective-permute-start.1 = (bf16[128,2176]{1,0:T(8,128)(2,1)}, bf16[128,2176]{1,0:T(8,128)(2,1)}, u32[]{:S(2)}, u32[]{:S(2)}) collective-permute-start(bf16[128,2176]{1,0:T(8,128)(2,1)} %shard_map.94.cot_a), channel_id=1, source_target_pairs={{0,8},{4,12},{8,0},{12,4},{16,24},{20,28},{24,16},{28,20},{1,9},{5... | collective-permute-start | bytes 1671176 | tf_op jit(solution)/shard_map/ppermute | solution.py:22
  12.2 1.5 %collective-permute-start = (bf16[128,2048]{1,0:T(8,128)(2,1)}, bf16[128,2048]{1,0:T(8,128)(2,1)}, u32[]{:S(2)}, u32[]{:S(2)}) collective-permute-start(bf16[128,2048]{1,0:T(8,128)(2,1)} %tok_a), channel_id=1, source_target_pairs={{0,2},{1,3},{2,0},{3,1},{4,6},{5,7},{6,4},{7,5},{8,10},{9,11},{10,... | collective-permute-start | bytes 1572872 | tf_op jit(solution)/shard_map/ppermute | solution.py:22
  14.2 3.6 %collective-permute-done.2 = bf16[1,2,64,2048]{3,2,1,0:T(8,128)(2,1)} collective-permute-done((bf16[1,2,64,2048]{3,2,1,0:T(8,128)(2,1)}, bf16[1,2,64,2048]{3,2,1,0:T(8,128)(2,1)}, u32[]{:S(2)}, u32[]{:S(2)}) %collective-permute-start.2) | collective-permute-done | bytes 524320 | tf_op jit(solution)/shard_map/ppermute | solution.py:22
  19.1 6.5 %collective-permute-done.tok_a = bf16[128,2048]{1,0:T(8,128)(2,1)} collective-permute-done((bf16[128,2048]{1,0:T(8,128)(2,1)}, bf16[128,2048]{1,0:T(8,128)(2,1)}, u32[]{:S(2)}, u32[]{:S(2)}) %collective-permute-start) | collective-permute-done | bytes 524320 | tf_op jit(solution)/shard_map/ppermute | solution.py:22
  31.6 1.6 %collective-permute-start.4 = (bf16[128,2176]{1,0:T(8,128)(2,1)S(1)}, bf16[128,2176]{1,0:T(8,128)(2,1)S(1)}, u32[]{:S(2)}, u32[]{:S(2)}) collective-permute-start(bf16[128,2176]{1,0:T(8,128)(2,1)S(1)} %copy-done.2), channel_id=1, source_target_pairs={{0,2},{1,3},{2,0},{3,1},{4,6},{5,7},{6,4},{7,5},{8,10},{9,11},{10,... | collective-permute-start | bytes 1671176 | tf_op jit(solution)/shard_map/ppermute | solution.py:22
  33.1 3.1 %shard_map.95 = (bf16[256,512]{1,0:T(8,128)(2,1)S(1)}, bf16[256,2048]{1,0:T(8,128)(2,1)S(1)}, bf16[256,1024]{1,0:T(8,128)(2,1)S(1)}) custom-call(s32[1]{0:T(128)} %bitcast.5.me, bf16[128,2048]{1,0:T(8,128)(2,1)S(1)} %copy-done.3, bf16[128,2048]{1,0:T(8,128)(2,1)} %collective-permute-done.6.tok_b, bf16[128,2176]{1,0:T(8,128)(2,1)S(1)} %copy-done.2, ...), custom_call_target="tpu_custom_call" | custom-call | flops 1610612736 | bytes 4194304 | tf_op jit(solution)/shard_map/pallas_call | solution.py:95
  36.2 6.4 %collective-permute-done.5 = bf16[1,2,64,2048]{3,2,1,0:T(8,128)(2,1)S(1)} collective-permute-done((bf16[1,2,64,2048]{3,2,1,0:T(8,128)(2,1)S(1)}, bf16[1,2,64,2048]{3,2,1,0:T(8,128)(2,1)S(1)}, u32[]{:S(2)}, u32[]{:S(2)}) %collective-permute-start.5) | collective-permute-done | bytes 524320 | tf_op jit(solution)/shard_map/ppermute | solution.py:22
  43.8 1.6 %collective-permute-start.14 = (bf16[128,2176]{1,0:T(8,128)(2,1)}, bf16[128,2176]{1,0:T(8,128)(2,1)S(1)}, u32[]{:S(2)}, u32[]{:S(2)}) collective-permute-start(bf16[128,2176]{1,0:T(8,128)(2,1)} %collective-permute-done.1.cot_a), channel_id=1, source_target_pairs={{0,2},{1,3},{2,0},{3,1},{4,6},{5,7},{6,4},{7,5},{8,10},{9,11},{10,... | collective-permute-start | bytes 1671176 | tf_op jit(solution)/shard_map/ppermute | solution.py:22
  45.7 5.6 %collective-permute-done.3.tok_a = bf16[128,2048]{1,0:T(8,128)(2,1)S(1)} collective-permute-done((bf16[128,2048]{1,0:T(8,128)(2,1)S(1)}, bf16[128,2048]{1,0:T(8,128)(2,1)S(1)}, u32[]{:S(2)}, u32[]{:S(2)}) %collective-permute-start.3) | collective-permute-done | bytes 524320 | tf_op jit(solution)/shard_map/ppermute | solution.py:22
  52.0 7.2 %collective-permute-done.14.cot_a = bf16[128,2176]{1,0:T(8,128)(2,1)S(1)} collective-permute-done((bf16[128,2176]{1,0:T(8,128)(2,1)}, bf16[128,2176]{1,0:T(8,128)(2,1)S(1)}, u32[]{:S(2)}, u32[]{:S(2)}) %collective-permute-start.14) | collective-permute-done | bytes 557088 | tf_op jit(solution)/shard_map/ppermute | solution.py:22
  60.6 3.0 %shard_map.97 = (bf16[256,512]{1,0:T(8,128)(2,1)S(1)}, bf16[256,2048]{1,0:T(8,128)(2,1)S(1)}, bf16[256,1024]{1,0:T(8,128)(2,1)S(1)}) custom-call(s32[1]{0:T(128)} %bitcast.5.me, bf16[128,2048]{1,0:T(8,128)(2,1)S(1)} %collective-permute-done.3.tok_a, bf16[128,2048]{1,0:T(8,128)(2,1)S(1)} %collective-permute-done.10.tok_b, ...), custom_call_target="tpu_custom_call" | custom-call | flops 1610612736 | bytes 4194304 | tf_op jit(solution)/shard_map/pallas_call | solution.py:95
  63.6 9.1 %collective-permute-done.27 = bf16[1,2,64,2048]{3,2,1,0:T(8,128)(2,1)S(1)} collective-permute-done((bf16[1,2,64,2048]{3,2,1,0:T(8,128)(2,1)S(1)}, bf16[1,2,64,2048]{3,2,1,0:T(8,128)(2,1)S(1)}, u32[]{:S(2)}, u32[]{:S(2)}) %collective-permute-start.27) | collective-permute-done | bytes 524320 | tf_op jit(solution)/shard_map/ppermute | solution.py:22
  72.8 3.0 %shard_map.96 = (bf16[256,512]{1,0:T(8,128)(2,1)S(1)}, bf16[256,2048]{1,0:T(8,128)(2,1)S(1)}, bf16[256,1024]{1,0:T(8,128)(2,1)S(1)}) custom-call(s32[1]{0:T(128)} %bitcast.5.me, bf16[128,2048]{1,0:T(8,128)(2,1)} %collective-permute-done.tok_a, bf16[128,2048]{1,0:T(8,128)(2,1)S(1)} %collective-permute-done.8.tok_b, ...), custom_call_target="tpu_custom_call" | custom-call | flops 1610612736 | bytes 4194304 | tf_op jit(solution)/shard_map/pallas_call | solution.py:95
  75.9 1.9 %fusion.7 = f32[1024,1024]{1,0:T(8,128)S(1)} fusion(bf16[768,512]{1,0:T(8,128)(2,1)S(1)} %get-tuple-element.63, bf16[768,512]{1,0:T(8,128)(2,1)S(1)} %get-tuple-element.64, bf16[768,512]{1,0:T(8,128)(2,1)S(1)} %get-tuple-element.62, bf16[768,512]{1,0:T(8,128)(2,1)S(1)} %get-tuple-element.61, bf16[256,1024]{1,0:T(8,128)(2,1)S(1)} %get-tuple-element.45, ...), kind=kOutput, calls=%fused_computation.11 | convolution fusion | flops 1622409216 | bytes 8912897 | tf_op jit(solution)/shard_map/dot_general | solution.py:164
  77.8 1.9 %shard_map.98 = (bf16[256,512]{1,0:T(8,128)(2,1)S(1)}, bf16[256,2048]{1,0:T(8,128)(2,1)S(1)}, bf16[256,1024]{1,0:T(8,128)(2,1)S(1)}) custom-call(s32[1]{0:T(128)} %bitcast.5.me, bf16[128,2048]{1,0:T(8,128)(2,1)S(1)} %collective-permute-done.12.tok_a, bf16[128,2048]{1,0:T(8,128)(2,1)S(1)} %collective-permute-done.13.tok_b, ...), custom_call_target="tpu_custom_call" | custom-call | flops 1610612736 | bytes 4194304 | tf_op jit(solution)/shard_map/pallas_call | solution.py:95
  81.6 2.4 %convolution_convert_fusion = bf16[512,2048]{1,0:T(8,128)(2,1)S(1)} fusion(bf16[512,1024]{1,0:T(8,128)(2,1)S(1)} %pad_maximum_fusion, bf16[1,2048,1024]{2,1,0:T(8,128)(2,1)S(1)} %copy-done), kind=kOutput, calls=%fused_computation.7 | convolution fusion | flops 2148532224 | bytes 7340032 | tf_op jit(solution)/shard_map/dot_general | solution.py:205
  84.3 1.6 %collective-permute-start.20 = (bf16[1,64,1024]{2,1,0:T(8,128)(2,1)S(1)}, bf16[1,64,1024]{2,1,0:T(8,128)(2,1)S(1)}, u32[]{:S(2)}, u32[]{:S(2)}) collective-permute-start(bf16[1,64,1024]{2,1,0:T(8,128)(2,1)S(1)} %dynamic-slice_bitcast_fusion.7), channel_id=1, source_target_pairs={{0,4},{4,0},{8,12},{12,8},{16,20},{20,16},{24,28},{28,24},{1,5},{5... | collective-permute-start | bytes 393224 | tf_op jit(solution)/shard_map/ppermute | solution.py:22
  88.1 1.6 %collective-permute-start.25 = (bf16[1,64,2048]{2,1,0:T(8,128)(2,1)S(1)}, bf16[1,64,2048]{2,1,0:T(8,128)(2,1)S(1)}, u32[]{:S(2)}, u32[]{:S(2)}) collective-permute-start(bf16[1,64,2048]{2,1,0:T(8,128)(2,1)S(1)} %get-tuple-element.57), channel_id=1, source_target_pairs={{0,4},{4,0},{8,12},{12,8},{16,20},{20,16},{24,28},{28,24},{1,5},{5... | collective-permute-start | bytes 786440 | tf_op jit(solution)/shard_map/ppermute | solution.py:22
  90.8 2.6 %collective-permute-start.21 = (bf16[1,64,1024]{2,1,0:T(8,128)(2,1)S(1)}, bf16[1,64,1024]{2,1,0:T(8,128)(2,1)S(1)}, u32[]{:S(2)}, u32[]{:S(2)}) collective-permute-start(bf16[1,64,1024]{2,1,0:T(8,128)(2,1)S(1)} %fusion.44), channel_id=1, source_target_pairs={{0,16},{4,20},{8,24},{12,28},{16,0},{20,4},{24,8},{28,12},{1,17},{... | collective-permute-start | bytes 393224 | tf_op jit(solution)/shard_map/ppermute | solution.py:22
  94.0 1.6 %collective-permute-start.17 = (bf16[128,2048]{1,0:T(8,128)(2,1)S(1)}, bf16[128,2048]{1,0:T(8,128)(2,1)S(1)}, u32[]{:S(2)}, u32[]{:S(2)}) collective-permute-start(bf16[128,2048]{1,0:T(8,128)(2,1)S(1)} %fusion.21), channel_id=1, source_target_pairs={{0,2},{1,3},{2,0},{3,1},{4,6},{5,7},{6,4},{7,5},{8,10},{9,11},{10,... | collective-permute-start | bytes 1572872 | tf_op jit(solution)/shard_map/ppermute | solution.py:22
  96.4 2.6 %collective-permute-start.24 = (bf16[1,128,1024]{2,1,0:T(8,128)(2,1)S(1)}, bf16[1,128,1024]{2,1,0:T(8,128)(2,1)S(1)}, u32[]{:S(2)}, u32[]{:S(2)}) collective-permute-start(bf16[1,128,1024]{2,1,0:T(8,128)(2,1)S(1)} %fusion.35), channel_id=1, source_target_pairs={{0,16},{4,20},{8,24},{12,28},{16,0},{20,4},{24,8},{28,12},{1,17},{... | collective-permute-start | bytes 786440 | tf_op jit(solution)/shard_map/ppermute | solution.py:22
  99.1 2.5 %collective-permute-done.25 = bf16[1,64,2048]{2,1,0:T(8,128)(2,1)S(1)} collective-permute-done((bf16[1,64,2048]{2,1,0:T(8,128)(2,1)S(1)}, bf16[1,64,2048]{2,1,0:T(8,128)(2,1)S(1)}, u32[]{:S(2)}, u32[]{:S(2)}) %collective-permute-start.25) | collective-permute-done | bytes 262176 | tf_op jit(solution)/shard_map/ppermute | solution.py:22
  101.5 1.5 %collective-permute-start.19 = (bf16[1,256,1024]{2,1,0:T(8,128)(2,1)S(1)}, bf16[1,256,1024]{2,1,0:T(8,128)(2,1)S(1)}, u32[]{:S(2)}, u32[]{:S(2)}) collective-permute-start(bf16[1,256,1024]{2,1,0:T(8,128)(2,1)S(1)} %dynamic-slice_bitcast_fusion), channel_id=1, source_target_pairs={{0,4},{4,0},{8,12},{12,8},{16,20},{20,16},{24,28},{28,24},{1,5},{5... | collective-permute-start | bytes 1572872 | tf_op jit(solution)/shard_map/ppermute | solution.py:22
  103.2 3.5 %collective-permute-done.17 = bf16[128,2048]{1,0:T(8,128)(2,1)S(1)} collective-permute-done((bf16[128,2048]{1,0:T(8,128)(2,1)S(1)}, bf16[128,2048]{1,0:T(8,128)(2,1)S(1)}, u32[]{:S(2)}, u32[]{:S(2)}) %collective-permute-start.17) | collective-permute-done | bytes 524320 | tf_op jit(solution)/shard_map/ppermute | solution.py:22
  106.6 2.6 %collective-permute-start.28 = (bf16[1,64,2048]{2,1,0:T(8,128)(2,1)S(1)}, bf16[1,64,2048]{2,1,0:T(8,128)(2,1)S(1)}, u32[]{:S(2)}, u32[]{:S(2)}) collective-permute-start(bf16[1,64,2048]{2,1,0:T(8,128)(2,1)S(1)} %fusion.31), channel_id=1, source_target_pairs={{0,16},{4,20},{8,24},{12,28},{16,0},{20,4},{24,8},{28,12},{1,17},{... | collective-permute-start | bytes 786440 | tf_op jit(solution)/shard_map/ppermute | solution.py:22
  110.2 1.5 %collective-permute-start.26 = (bf16[1,64,2048]{2,1,0:T(8,128)(2,1)S(1)}, bf16[1,64,2048]{2,1,0:T(8,128)(2,1)S(1)}, u32[]{:S(2)}, u32[]{:S(2)}) collective-permute-start(bf16[1,64,2048]{2,1,0:T(8,128)(2,1)S(1)} %get-tuple-element.58), channel_id=1, source_target_pairs={{0,4},{4,0},{8,12},{12,8},{16,20},{20,16},{24,28},{28,24},{1,5},{5... | collective-permute-start | bytes 786440 | tf_op jit(solution)/shard_map/ppermute | solution.py:22
  111.8 4.9 %collective-permute-done.23 = bf16[1,64,1024]{2,1,0:T(8,128)(2,1)S(1)} collective-permute-done((bf16[1,64,1024]{2,1,0:T(8,128)(2,1)S(1)}, bf16[1,64,1024]{2,1,0:T(8,128)(2,1)S(1)}, u32[]{:S(2)}, u32[]{:S(2)}) %collective-permute-start.23) | collective-permute-done | bytes 131104 | tf_op jit(solution)/shard_map/ppermute | solution.py:22
  116.6 5.6 %collective-permute-done.24 = bf16[1,128,1024]{2,1,0:T(8,128)(2,1)S(1)} collective-permute-done((bf16[1,128,1024]{2,1,0:T(8,128)(2,1)S(1)}, bf16[1,128,1024]{2,1,0:T(8,128)(2,1)S(1)}, u32[]{:S(2)}, u32[]{:S(2)}) %collective-permute-start.24) | collective-permute-done | bytes 262176 | tf_op jit(solution)/shard_map/ppermute | solution.py:22
  123.5 3.8 %collective-permute-done.28 = bf16[1,64,2048]{2,1,0:T(8,128)(2,1)S(1)} collective-permute-done((bf16[1,64,2048]{2,1,0:T(8,128)(2,1)S(1)}, bf16[1,64,2048]{2,1,0:T(8,128)(2,1)S(1)}, u32[]{:S(2)}, u32[]{:S(2)}) %collective-permute-start.28) | collective-permute-done | bytes 262176 | tf_op jit(solution)/shard_map/ppermute | solution.py:22
  (84 shorter events, 24.3 us)
Async XLA Ops:
  0.6 26.0 %copy-start.3 = (bf16[128,2048]{1,0:T(8,128)(2,1)S(1)}, bf16[128,2048]{1,0:T(8,128)(2,1)}, u32[]{:S(2)}) copy-start(bf16[128,2048]{1,0:T(8,128)(2,1)} %tok_a) | copy-start | bytes 1572868
  2.6 15.2 %collective-permute-start.2 = (bf16[1,2,64,2048]{3,2,1,0:T(8,128)(2,1)}, bf16[1,2,64,2048]{3,2,1,0:T(8,128)(2,1)}, u32[]{:S(2)}, u32[]{:S(2)}) collective-permute-start(bf16[1,2,64,2048]{3,2,1,0:T(8,128)(2,1)} %dynamic-slice_bitcast_fusion.2), channel_id=1, source_target_pairs={{0,4},{4,0},{8,12},{12,8},{16,20},{20,16},{24,28},{28,24},{1,5},{5... | collective-permute-start | bytes 1572872 | tf_op jit(solution)/shard_map/ppermute | solution.py:22
  8.4 24.7 %copy-start.1 = (bf16[1,512,2048]{2,1,0:T(8,128)(2,1)S(1)}, bf16[1,512,2048]{2,1,0:T(8,128)(2,1)}, u32[]{:S(2)}) copy-start(bf16[1,512,2048]{2,1,0:T(8,128)(2,1)} %param.12) | copy-start | bytes 6291460
  10.6 20.9 %copy-start.2 = (bf16[128,2176]{1,0:T(8,128)(2,1)S(1)}, bf16[128,2176]{1,0:T(8,128)(2,1)}, u32[]{:S(2)}) copy-start(bf16[128,2176]{1,0:T(8,128)(2,1)} %shard_map.94.cot_a) | copy-start | bytes 1671172
  10.6 15.0 %collective-permute-start.1 = (bf16[128,2176]{1,0:T(8,128)(2,1)}, bf16[128,2176]{1,0:T(8,128)(2,1)}, u32[]{:S(2)}, u32[]{:S(2)}) collective-permute-start(bf16[128,2176]{1,0:T(8,128)(2,1)} %shard_map.94.cot_a), channel_id=1, source_target_pairs={{0,8},{4,12},{8,0},{12,4},{16,24},{20,28},{24,16},{28,20},{1,9},{5... | collective-permute-start | bytes 1671176 | tf_op jit(solution)/shard_map/ppermute | solution.py:22
  12.2 13.4 %collective-permute-start = (bf16[128,2048]{1,0:T(8,128)(2,1)}, bf16[128,2048]{1,0:T(8,128)(2,1)}, u32[]{:S(2)}, u32[]{:S(2)}) collective-permute-start(bf16[128,2048]{1,0:T(8,128)(2,1)} %tok_a), channel_id=1, source_target_pairs={{0,2},{1,3},{2,0},{3,1},{4,6},{5,7},{6,4},{7,5},{8,10},{9,11},{10,... | collective-permute-start | bytes 1572872 | tf_op jit(solution)/shard_map/ppermute | solution.py:22
  13.7 17.9 %collective-permute-start.7 = (bf16[128,2176]{1,0:T(8,128)(2,1)}, bf16[128,2176]{1,0:T(8,128)(2,1)}, u32[]{:S(2)}, u32[]{:S(2)}) collective-permute-start(bf16[128,2176]{1,0:T(8,128)(2,1)} %shard_map.94.cot_a), channel_id=1, source_target_pairs={{0,1},{1,0},{2,3},{3,2},{4,5},{5,4},{6,7},{7,6},{8,9},{9,8},{10,11... | collective-permute-start | bytes 1671176 | tf_op jit(solution)/shard_map/ppermute | solution.py:22
  13.7 15.1 %collective-permute-start.6 = (bf16[128,2048]{1,0:T(8,128)(2,1)}, bf16[128,2048]{1,0:T(8,128)(2,1)}, u32[]{:S(2)}, u32[]{:S(2)}) collective-permute-start(bf16[128,2048]{1,0:T(8,128)(2,1)} %tok_a), channel_id=1, source_target_pairs={{0,1},{1,0},{2,3},{3,2},{4,5},{5,4},{6,7},{7,6},{8,9},{9,8},{10,11... | collective-permute-start | bytes 1572872 | tf_op jit(solution)/shard_map/ppermute | solution.py:22
  25.6 19.8 %collective-permute-start.8 = (bf16[128,2048]{1,0:T(8,128)(2,1)}, bf16[128,2048]{1,0:T(8,128)(2,1)S(1)}, u32[]{:S(2)}, u32[]{:S(2)}) collective-permute-start(bf16[128,2048]{1,0:T(8,128)(2,1)} %collective-permute-done.tok_a), channel_id=1, source_target_pairs={{0,1},{1,0},{2,3},{3,2},{4,5},{5,4},{6,7},{7,6},{8,9},{9,8},{10,11... | collective-permute-start | bytes 1572872 | tf_op jit(solution)/shard_map/ppermute | solution.py:22
  25.6 18.2 %collective-permute-start.12 = (bf16[128,2048]{1,0:T(8,128)(2,1)}, bf16[128,2048]{1,0:T(8,128)(2,1)S(1)}, u32[]{:S(2)}, u32[]{:S(2)}) collective-permute-start(bf16[128,2048]{1,0:T(8,128)(2,1)} %collective-permute-done.tok_a), channel_id=1, source_target_pairs={{0,8},{4,12},{8,0},{12,4},{16,24},{20,28},{24,16},{28,20},{1,9},{5... | collective-permute-start | bytes 1572872 | tf_op jit(solution)/shard_map/ppermute | solution.py:22
  26.6 24.8 %collective-permute-start.3 = (bf16[128,2048]{1,0:T(8,128)(2,1)S(1)}, bf16[128,2048]{1,0:T(8,128)(2,1)S(1)}, u32[]{:S(2)}, u32[]{:S(2)}) collective-permute-start(bf16[128,2048]{1,0:T(8,128)(2,1)S(1)} %copy-done.3), channel_id=1, source_target_pairs={{0,8},{4,12},{8,0},{12,4},{16,24},{20,28},{24,16},{28,20},{1,9},{5... | collective-permute-start | bytes 1572872 | tf_op jit(solution)/shard_map/ppermute | solution.py:22
  28.8 13.8 %collective-permute-start.5 = (bf16[1,2,64,2048]{3,2,1,0:T(8,128)(2,1)S(1)}, bf16[1,2,64,2048]{3,2,1,0:T(8,128)(2,1)S(1)}, u32[]{:S(2)}, u32[]{:S(2)}) collective-permute-start(bf16[1,2,64,2048]{3,2,1,0:T(8,128)(2,1)S(1)} %dynamic-slice_bitcast_fusion.1), channel_id=1, source_target_pairs={{0,4},{4,0},{8,12},{12,8},{16,20},{20,16},{24,28},{28,24},{1,5},{5... | collective-permute-start | bytes 1572872 | tf_op jit(solution)/shard_map/ppermute | solution.py:22
  31.6 19.8 %collective-permute-start.4 = (bf16[128,2176]{1,0:T(8,128)(2,1)S(1)}, bf16[128,2176]{1,0:T(8,128)(2,1)S(1)}, u32[]{:S(2)}, u32[]{:S(2)}) collective-permute-start(bf16[128,2176]{1,0:T(8,128)(2,1)S(1)} %copy-done.2), channel_id=1, source_target_pairs={{0,2},{1,3},{2,0},{3,1},{4,6},{5,7},{6,4},{7,5},{8,10},{9,11},{10,... | collective-permute-start | bytes 1671176 | tf_op jit(solution)/shard_map/ppermute | solution.py:22
  42.6 18.0 %collective-permute-start.11 = (bf16[128,2176]{1,0:T(8,128)(2,1)}, bf16[128,2176]{1,0:T(8,128)(2,1)S(1)}, u32[]{:S(2)}, u32[]{:S(2)}) collective-permute-start(bf16[128,2176]{1,0:T(8,128)(2,1)} %collective-permute-done.1.cot_a), channel_id=1, source_target_pairs={{0,1},{1,0},{2,3},{3,2},{4,5},{5,4},{6,7},{7,6},{8,9},{9,8},{10,11... | collective-permute-start | bytes 1671176 | tf_op jit(solution)/shard_map/ppermute | solution.py:22
  43.8 15.3 %collective-permute-start.14 = (bf16[128,2176]{1,0:T(8,128)(2,1)}, bf16[128,2176]{1,0:T(8,128)(2,1)S(1)}, u32[]{:S(2)}, u32[]{:S(2)}) collective-permute-start(bf16[128,2176]{1,0:T(8,128)(2,1)} %collective-permute-done.1.cot_a), channel_id=1, source_target_pairs={{0,2},{1,3},{2,0},{3,1},{4,6},{5,7},{6,4},{7,5},{8,10},{9,11},{10,... | collective-permute-start | bytes 1671176 | tf_op jit(solution)/shard_map/ppermute | solution.py:22
  45.4 14.7 %collective-permute-start.13 = (bf16[128,2048]{1,0:T(8,128)(2,1)S(1)}, bf16[128,2048]{1,0:T(8,128)(2,1)S(1)}, u32[]{:S(2)}, u32[]{:S(2)}) collective-permute-start(bf16[128,2048]{1,0:T(8,128)(2,1)S(1)} %collective-permute-done.12.tok_a), channel_id=1, source_target_pairs={{0,1},{1,0},{2,3},{3,2},{4,5},{5,4},{6,7},{7,6},{8,9},{9,8},{10,11... | collective-permute-start | bytes 1572872 | tf_op jit(solution)/shard_map/ppermute | solution.py:22
  51.4 8.9 %collective-permute-start.10 = (bf16[128,2048]{1,0:T(8,128)(2,1)S(1)}, bf16[128,2048]{1,0:T(8,128)(2,1)S(1)}, u32[]{:S(2)}, u32[]{:S(2)}) collective-permute-start(bf16[128,2048]{1,0:T(8,128)(2,1)S(1)} %collective-permute-done.3.tok_a), channel_id=1, source_target_pairs={{0,1},{1,0},{2,3},{3,2},{4,5},{5,4},{6,7},{7,6},{8,9},{9,8},{10,11... | collective-permute-start | bytes 1572872 | tf_op jit(solution)/shard_map/ppermute | solution.py:22
  51.4 21.4 %collective-permute-start.9 = (bf16[128,2176]{1,0:T(8,128)(2,1)S(1)}, bf16[128,2176]{1,0:T(8,128)(2,1)S(1)}, u32[]{:S(2)}, u32[]{:S(2)}) collective-permute-start(bf16[128,2176]{1,0:T(8,128)(2,1)S(1)} %collective-permute-done.4.cot_a), channel_id=1, source_target_pairs={{0,1},{1,0},{2,3},{3,2},{4,5},{5,4},{6,7},{7,6},{8,9},{9,8},{10,11... | collective-permute-start | bytes 1671176 | tf_op jit(solution)/shard_map/ppermute | solution.py:22
  59.1 13.6 %collective-permute-start.27 = (bf16[1,2,64,2048]{3,2,1,0:T(8,128)(2,1)S(1)}, bf16[1,2,64,2048]{3,2,1,0:T(8,128)(2,1)S(1)}, u32[]{:S(2)}, u32[]{:S(2)}) collective-permute-start(bf16[1,2,64,2048]{3,2,1,0:T(8,128)(2,1)S(1)} %fusion.24), channel_id=1, source_target_pairs={{0,8},{4,12},{8,0},{12,4},{16,24},{20,28},{24,16},{28,20},{1,9},{5... | collective-permute-start | bytes 1572872 | tf_op jit(solution)/shard_map/ppermute | solution.py:22
  60.1 17.6 %collective-permute-start.15 = (bf16[128,2176]{1,0:T(8,128)(2,1)S(1)}, bf16[128,2176]{1,0:T(8,128)(2,1)S(1)}, u32[]{:S(2)}, u32[]{:S(2)}) collective-permute-start(bf16[128,2176]{1,0:T(8,128)(2,1)S(1)} %collective-permute-done.14.cot_a), channel_id=1, source_target_pairs={{0,1},{1,0},{2,3},{3,2},{4,5},{5,4},{6,7},{7,6},{8,9},{9,8},{10,11... | collective-permute-start | bytes 1671176 | tf_op jit(solution)/shard_map/ppermute | solution.py:22
  81.1 7.0 %collective-permute-start.22 = (bf16[1,64,1024]{2,1,0:T(8,128)(2,1)S(1)}, bf16[1,64,1024]{2,1,0:T(8,128)(2,1)S(1)}, u32[]{:S(2)}, u32[]{:S(2)}) collective-permute-start(bf16[1,64,1024]{2,1,0:T(8,128)(2,1)S(1)} %dynamic-slice_bitcast_fusion.6), channel_id=1, source_target_pairs={{0,4},{4,0},{8,12},{12,8},{16,20},{20,16},{24,28},{28,24},{1,5},{5... | collective-permute-start | bytes 393224 | tf_op jit(solution)/shard_map/ppermute | solution.py:22
  84.2 9.6 %collective-permute-start.16 = (bf16[2,128,2048]{2,1,0:T(8,128)(2,1)S(1)}, bf16[2,128,2048]{2,1,0:T(8,128)(2,1)S(1)}, u32[]{:S(2)}, u32[]{:S(2)}) collective-permute-start(bf16[2,128,2048]{2,1,0:T(8,128)(2,1)S(1)} %pad_maximum_fusion.1), channel_id=1, source_target_pairs={{0,1},{1,0},{2,3},{3,2},{4,5},{5,4},{6,7},{7,6},{8,9},{9,8},{10,11... | collective-permute-start | bytes 3145736 | tf_op jit(solution)/shard_map/ppermute | solution.py:22
  84.3 6.4 %collective-permute-start.20 = (bf16[1,64,1024]{2,1,0:T(8,128)(2,1)S(1)}, bf16[1,64,1024]{2,1,0:T(8,128)(2,1)S(1)}, u32[]{:S(2)}, u32[]{:S(2)}) collective-permute-start(bf16[1,64,1024]{2,1,0:T(8,128)(2,1)S(1)} %dynamic-slice_bitcast_fusion.7), channel_id=1, source_target_pairs={{0,4},{4,0},{8,12},{12,8},{16,20},{20,16},{24,28},{28,24},{1,5},{5... | collective-permute-start | bytes 393224 | tf_op jit(solution)/shard_map/ppermute | solution.py:22
  86.0 10.4 %collective-permute-start.18 = (bf16[1,128,1024]{2,1,0:T(8,128)(2,1)S(1)}, bf16[1,128,1024]{2,1,0:T(8,128)(2,1)S(1)}, u32[]{:S(2)}, u32[]{:S(2)}) collective-permute-start(bf16[1,128,1024]{2,1,0:T(8,128)(2,1)S(1)} %dynamic-slice_bitcast_fusion.5), channel_id=1, source_target_pairs={{0,4},{4,0},{8,12},{12,8},{16,20},{20,16},{24,28},{28,24},{1,5},{5... | collective-permute-start | bytes 786440 | tf_op jit(solution)/shard_map/ppermute | solution.py:22
  88.1 13.4 %collective-permute-start.25 = (bf16[1,64,2048]{2,1,0:T(8,128)(2,1)S(1)}, bf16[1,64,2048]{2,1,0:T(8,128)(2,1)S(1)}, u32[]{:S(2)}, u32[]{:S(2)}) collective-permute-start(bf16[1,64,2048]{2,1,0:T(8,128)(2,1)S(1)} %get-tuple-element.57), channel_id=1, source_target_pairs={{0,4},{4,0},{8,12},{12,8},{16,20},{20,16},{24,28},{28,24},{1,5},{5... | collective-permute-start | bytes 786440 | tf_op jit(solution)/shard_map/ppermute | solution.py:22
  90.8 19.5 %collective-permute-start.21 = (bf16[1,64,1024]{2,1,0:T(8,128)(2,1)S(1)}, bf16[1,64,1024]{2,1,0:T(8,128)(2,1)S(1)}, u32[]{:S(2)}, u32[]{:S(2)}) collective-permute-start(bf16[1,64,1024]{2,1,0:T(8,128)(2,1)S(1)} %fusion.44), channel_id=1, source_target_pairs={{0,16},{4,20},{8,24},{12,28},{16,0},{20,4},{24,8},{28,12},{1,17},{... | collective-permute-start | bytes 393224 | tf_op jit(solution)/shard_map/ppermute | solution.py:22
  93.4 23.2 %collective-permute-start.23 = (bf16[1,64,1024]{2,1,0:T(8,128)(2,1)S(1)}, bf16[1,64,1024]{2,1,0:T(8,128)(2,1)S(1)}, u32[]{:S(2)}, u32[]{:S(2)}) collective-permute-start(bf16[1,64,1024]{2,1,0:T(8,128)(2,1)S(1)} %fusion.43), channel_id=1, source_target_pairs={{0,16},{4,20},{8,24},{12,28},{16,0},{20,4},{24,8},{28,12},{1,17},{... | collective-permute-start | bytes 393224 | tf_op jit(solution)/shard_map/ppermute | solution.py:22
  94.0 12.6 %collective-permute-start.17 = (bf16[128,2048]{1,0:T(8,128)(2,1)S(1)}, bf16[128,2048]{1,0:T(8,128)(2,1)S(1)}, u32[]{:S(2)}, u32[]{:S(2)}) collective-permute-start(bf16[128,2048]{1,0:T(8,128)(2,1)S(1)} %fusion.21), channel_id=1, source_target_pairs={{0,2},{1,3},{2,0},{3,1},{4,6},{5,7},{6,4},{7,5},{8,10},{9,11},{10,... | collective-permute-start | bytes 1572872 | tf_op jit(solution)/shard_map/ppermute | solution.py:22
  96.4 25.9 %collective-permute-start.24 = (bf16[1,128,1024]{2,1,0:T(8,128)(2,1)S(1)}, bf16[1,128,1024]{2,1,0:T(8,128)(2,1)S(1)}, u32[]{:S(2)}, u32[]{:S(2)}) collective-permute-start(bf16[1,128,1024]{2,1,0:T(8,128)(2,1)S(1)} %fusion.35), channel_id=1, source_target_pairs={{0,16},{4,20},{8,24},{12,28},{16,0},{20,4},{24,8},{28,12},{1,17},{... | collective-permute-start | bytes 786440 | tf_op jit(solution)/shard_map/ppermute | solution.py:22
  101.5 20.7 %collective-permute-start.19 = (bf16[1,256,1024]{2,1,0:T(8,128)(2,1)S(1)}, bf16[1,256,1024]{2,1,0:T(8,128)(2,1)S(1)}, u32[]{:S(2)}, u32[]{:S(2)}) collective-permute-start(bf16[1,256,1024]{2,1,0:T(8,128)(2,1)S(1)} %dynamic-slice_bitcast_fusion), channel_id=1, source_target_pairs={{0,4},{4,0},{8,12},{12,8},{16,20},{20,16},{24,28},{28,24},{1,5},{5... | collective-permute-start | bytes 1572872 | tf_op jit(solution)/shard_map/ppermute | solution.py:22
  106.6 20.7 %collective-permute-start.28 = (bf16[1,64,2048]{2,1,0:T(8,128)(2,1)S(1)}, bf16[1,64,2048]{2,1,0:T(8,128)(2,1)S(1)}, u32[]{:S(2)}, u32[]{:S(2)}) collective-permute-start(bf16[1,64,2048]{2,1,0:T(8,128)(2,1)S(1)} %fusion.31), channel_id=1, source_target_pairs={{0,16},{4,20},{8,24},{12,28},{16,0},{20,4},{24,8},{28,12},{1,17},{... | collective-permute-start | bytes 786440 | tf_op jit(solution)/shard_map/ppermute | solution.py:22
  110.2 17.1 %collective-permute-start.26 = (bf16[1,64,2048]{2,1,0:T(8,128)(2,1)S(1)}, bf16[1,64,2048]{2,1,0:T(8,128)(2,1)S(1)}, u32[]{:S(2)}, u32[]{:S(2)}) collective-permute-start(bf16[1,64,2048]{2,1,0:T(8,128)(2,1)S(1)} %get-tuple-element.58), channel_id=1, source_target_pairs={{0,4},{4,0},{8,12},{12,8},{16,20},{20,16},{24,28},{28,24},{1,5},{5... | collective-permute-start | bytes 786440 | tf_op jit(solution)/shard_map/ppermute | solution.py:22
  (1 other events, 18.9 us)

commit v2 on v0

v2 whole, which is shorter than its diff:
```python
import functools

import jax
import jax.numpy as jnp
from jax import lax
from jax.experimental import pallas as pl
from jax.experimental.pallas import tpu as pltpu
from jax.sharding import PartitionSpec as P

LANES = 128


def wide(values):
    return values.astype(jnp.float32)


def narrow(values):
    return values.astype(jnp.bfloat16)


def flip(values, axis, bit):
    return lax.ppermute(values, axis, [(i, i ^ bit) for i in range(lax.axis_size(axis))])


def take(values, axis, index):
    return lax.dynamic_index_in_dim(values, index, axis, keepdims=False)


def with_routes(cotangent, expert_ids, gate_probs, expert_count):
    lane = jnp.arange(LANES, dtype=jnp.int32)[None, :]
    route = jnp.zeros((expert_ids.shape[0], LANES), jnp.float32)
    for k in range(expert_ids.shape[1]):
        hit = (lane < 3 * expert_count) & (lane // 3 == expert_ids[:, k : k + 1])
        route = route + jnp.where(hit, gate_probs[:, k : k + 1], 0.0)
    high = lax.reduce_precision(route, 8, 7)
    middle = lax.reduce_precision(route - high, 8, 7)
    low = (route - high) - middle
    part = lane % 3
    coded = jnp.where(part == 0, high, jnp.where(part == 1, middle, low))
    return jnp.concatenate([cotangent, narrow(coded)], axis=1)


def own_columns(values, group_count, parity):
    unit = values.shape[1] // group_count * 2
    blocks = [values[:, k * unit : (k + 1) * unit] for k in range(group_count // 2)]
    even, odd = jnp.concatenate(blocks[0::2], axis=1), jnp.concatenate(blocks[1::2], axis=1)
    return jnp.where(parity == 1, odd, even)


def expert_kernel(
    group_count, place, tok_a, tok_b, cot_a, cot_b, gate_up, down, tok_own, hid_own, scaled, back
):
    width, units = gate_up.shape[0], down.shape[0]
    tile = units // 2
    me, parity = place[0], place[1]
    lane = lax.broadcasted_iota(jnp.int32, (1, LANES), 1)
    for cot, at in ((cot_a, 0), (cot_b, cot_a.shape[0])):
        coded = wide(cot[:, width:])
        part = [
            jnp.sum(jnp.where(lane == 3 * me + k, coded, 0.0), axis=1, keepdims=True)
            for k in range(3)
        ]
        weight = (part[0] + part[1]) + part[2]
        scaled[at : at + cot.shape[0], :] = narrow(wide(cot[:, :width]) * weight)
    rows = jnp.concatenate([tok_a[...], tok_b[...]], axis=0)
    tok_own[...] = own_columns(rows, group_count, parity)
    grads = scaled[...]
    contract = (((1,), (1,)), ((), ()))
    hidden = []
    for at in range(0, units, tile):
        gate = jnp.dot(rows, gate_up[:, at : at + tile], preferred_element_type=jnp.float32)
        up = jnp.dot(
            rows, gate_up[:, units + at : units + at + tile], preferred_element_type=jnp.float32
        )
        sig = jax.nn.sigmoid(gate)
        activated = gate * sig
        hidden.append(narrow(activated * up))
        back_hidden = lax.dot_general(
            grads, down[at : at + tile, :], contract, preferred_element_type=jnp.float32
        )
        slope = up * sig * (1.0 + gate * (1.0 - sig))
        back[:, at : at + tile] = narrow(back_hidden * slope)
        back[:, units + at : units + at + tile] = narrow(back_hidden * activated)
    hid_own[...] = own_columns(jnp.concatenate(hidden, axis=1), group_count, parity)


def expert_rows(group_count, place, tok_a, tok_b, cot_a, cot_b, gate_up, down):
    rows, width = 2 * tok_a.shape[0], tok_a.shape[1]
    units = down.shape[0]
    vmem = pl.BlockSpec(memory_space=pltpu.VMEM)
    widths = (width // 2, units // 2, width, 2 * units)
    return pl.pallas_call(
        functools.partial(expert_kernel, group_count),
        out_shape=tuple(jax.ShapeDtypeStruct((rows, w), jnp.bfloat16) for w in widths),
        in_specs=[pl.BlockSpec(memory_space=pltpu.SMEM)] + [vmem] * 6,
        out_specs=(vmem,) * 4,
        compiler_params=pltpu.CompilerParams(vmem_limit_bytes=24 << 20),
        cost_estimate=pl.CostEstimate(flops=0, bytes_accessed=0, transcendentals=0),
    )(place, tok_a, tok_b, cot_a, cot_b, gate_up, down)


def on_device(
    tokens, cotangent, expert_ids, gate_probs, gate_up_weight, down_weight, down_residual
):
    tok_rows, model_width = tokens.shape
    expert_count = lax.axis_size("expert")
    group_count = lax.axis_size("dp")
    gate_up, down_matrix = gate_up_weight[0], down_weight[0]
    hidden_units = down_matrix.shape[0]
    me, group = lax.axis_index("expert"), lax.axis_index("dp")
    bit0, bit1, bit2 = group & 1, (group >> 1) & 1, (group >> 2) & 1
    high_count = group_count // 8

    tok_x, tok_n = flip(tokens, "expert", 2), flip(tokens, "dp", 2)
    tok_c = flip(tokens, "expert", 1)
    carried = with_routes(cotangent, expert_ids, gate_probs, expert_count)
    cot_x, cot_n = flip(carried, "expert", 2), flip(carried, "dp", 2)
    cot_c = flip(carried, "expert", 1)
    residual = down_residual[0, 0].reshape(high_count, 2, 2, 2, -1, model_width)
    res_got = flip(take(residual, 3, 1 - bit0), "dp", 1)
    tok_x, tok_n, tok_c, cot_x, cot_n, cot_c, res_got, tok_own, cot_own = lax.optimization_barrier(
        (tok_x, tok_n, tok_c, cot_x, cot_n, cot_c, res_got, tokens, carried)
    )
    tok_d, cot_d = flip(tok_x, "dp", 2), flip(cot_n, "expert", 2)
    place = jnp.stack([me, bit1]).astype(jnp.int32)

    def expert_on(tok, tok_other, cot, cot_other):
        return expert_rows(
            group_count, place, tok, tok_other, cot, cot_other, gate_up, down_matrix
        )

    def both_cores(tok, cot):
        return expert_on(tok, flip(tok, "expert", 1), cot, flip(cot, "expert", 1))

    made = [expert_on(tok_own, tok_c, cot_own, cot_c)]
    made += [both_cores(tok_x, cot_x), both_cores(tok_n, cot_n)]

    def terms(tok_cols, hid_cols, scaled, back):
        contract = (((0,), (0,)), ((), ()))
        gate = lax.dot_general(tok_cols, back, contract, preferred_element_type=jnp.float32)
        down = lax.dot_general(hid_cols, scaled, contract, preferred_element_type=jnp.float32)
        return gate, down

    early = [jnp.concatenate(v, axis=0) for v in zip(*made)]
    gate_early, down_early = terms(*early)
    tok_d, cot_d, gate_early, down_early = lax.optimization_barrier(
        (tok_d, cot_d, gate_early, down_early)
    )
    gate_late, down_late = terms(*both_cores(tok_d, cot_d))
    gate_term = narrow(gate_early + gate_late).reshape(high_count, 2, 2, -1, 2 * hidden_units)
    down_term = narrow(down_early + down_late).reshape(high_count, 2, 2, -1, model_width)

    res_pair = wide(take(residual, 3, bit0)) + wide(res_got)
    res_send = narrow(take(res_pair, 2, 1 - bit1))
    res_send, _ = lax.optimization_barrier((res_send, gate_term))
    res_sum = take(res_pair, 2, bit1) + wide(flip(res_send, "dp", 2))

    def paired(term, side, after):
        mine = take(term, 1, side)
        sent, kept = take(mine, 1, 1 - bit0), take(mine, 1, bit0)
        if after is not None:
            sent, _ = lax.optimization_barrier((sent, after))
        got = flip(sent, "dp", 1)
        return wide(kept) + wide(got), got

    count = gate_term.shape[3]
    edges = [0, count // 4, count // 2, count]
    far = [
        paired(gate_term[:, :, :, start:stop], 1 - bit2, None)
        for start, stop in zip(edges, edges[1:])
    ]
    far_down, got_down = paired(down_term, 1 - bit2, far[1][1])
    far_down = far_down + take(res_sum, 1, 1 - bit2)
    crossed = [flip(narrow(piece), "dp", 4) for piece, _ in far]
    crossed_down = flip(narrow(far_down), "dp", 4)

    back_group = jnp.concatenate([made[0][3], made[1][3]], axis=0)
    back_group, _ = lax.optimization_barrier((back_group, far[0][1]))
    token_part = narrow(jnp.dot(back_group, gate_up.T, preferred_element_type=jnp.float32))
    blocks = token_part.reshape(expert_count, tok_rows, model_width)
    core = flip(jnp.stack([blocks[1], blocks[3]]), "expert", 1)
    across = flip(narrow(wide(blocks[2]) + wide(core[1])), "expert", 2)
    token_grad = narrow(wide(blocks[0]) + wide(core[0]) + wide(across))

    near_gate, _ = paired(gate_term, bit2, far[2][1])
    near_down, _ = paired(down_term, bit2, (got_down, token_grad))
    gate_sum = near_gate + wide(jnp.concatenate(crossed, axis=1))
    down_sum = near_down + take(res_sum, 1, bit2) + wide(crossed_down)
    bit = 8
    while bit < group_count:
        side = (group // bit) & 1
        halves = [v.reshape(-1, 2, *v.shape[1:]) for v in (gate_sum, down_sum)]
        gate_sum, down_sum = [
            take(v, 1, side) + wide(flip(narrow(take(v, 1, 1 - side)), "dp", bit)) for v in halves
        ]
        bit *= 2
    factor = 1.0 / group_count
    grad_gate_up, grad_down = gate_sum * factor, down_sum * factor
    return (token_grad, grad_gate_up, grad_down)


def solution(mesh):
    placed = (
        P(("dp", "expert"), None),
        P(("dp", "expert"), None),
        P(("dp", "expert"), None),
        P(("dp", "expert"), None),
        P("expert", None, None),
        P("expert", None, None),
        P("dp", "expert", None, None),
    )
    return jax.shard_map(
        on_device,
        mesh=mesh,
        in_specs=placed,
        out_specs=(P(("dp", "expert"), None), P("expert", "dp", None), P("expert", "dp", None)),
        check_vma=False,
    )
```

time: 115 us -> 116 us (level)
  waiting for transfers between devices: 60 us -> 54.7 us
  local copies, waits for them, and re-layouts: 5.96 us -> 11.2 us
  Pallas kernels: 7.97 us -> 11.8 us
  starting transfers between devices: 28.1 us -> 24.9 us
    unnamed x14 -> x30, local copies, waits for them, and re-layouts: 1.32 us -> 7.95 us
    ppermute x26 -> x28, waiting for transfers between devices: 60 us -> 54.7 us  [flip(): lax.ppermute(values, axis, [(i, i ^ bit) for i in range(lax.axis_size(axi...]
    pallas_call x4, Pallas kernels: 7.97 us -> 11.8 us  [expert_rows(): pl.pallas_call(functools.partial(expert_kernel, group_count), out_shape=t...]
    ppermute x26 -> x28, starting transfers between devices: 28.1 us -> 24.9 us  [flip(): lax.ppermute(values, axis, [(i, i ^ bit) for i in range(lax.axis_size(axi...]
    convert_element_type x6 -> x9, other arithmetic: 1.53 us -> 3.16 us  [narrow(): return values.astype(jnp.bfloat16)]
  transfers between devices with their start and end apart: 26 -> 28, of which waited for: 11 -> 12; matrix products, arithmetic and copies ran while one was open for 15% -> 11% of each run, Pallas kernels for 7% -> 8%
where the time goes in v2:
time: 116 us
  waiting for transfers between devices  54.7 us (47%)
  starting transfers between devices  24.9 us (21%)
  Pallas kernels  11.8 us (10%)
  local copies, waits for them, and re-layouts  11.2 us (10%)
  matrix products  6.44 us (6%)
  other arithmetic  6.12 us (5%)
    ppermute x28, waiting for transfers between devices, flip(): lax.ppermute(values, axis, [(i, i ^ bit) for i in range(lax.axis_size(axi...  54.7 us
    ppermute x28, starting transfers between devices, flip(): lax.ppermute(values, axis, [(i, i ^ bit) for i in range(lax.axis_size(axi...  24.9 us
    pallas_call x4, Pallas kernels, expert_rows(): pl.pallas_call(functools.partial(expert_kernel, group_count), out_shape=t...  11.8 us
    unnamed x30, local copies, waits for them, and re-layouts  7.95 us
    convert_element_type x9, other arithmetic, narrow(): return values.astype(jnp.bfloat16)  3.16 us
    dynamic_slice x2, local copies, waits for them, and re-layouts, take(): return lax.dynamic_index_in_dim(values, index, axis, keepdims=False)  2.82 us
    dot_general x2, matrix products, terms(): lax.dot_general(tok_cols, back, contract, preferred_element_type=jnp.floa...  2.61 us
    dot_general x1, matrix products, on_device(): jnp.dot(back_group, gate_up.T, preferred_element_type=jnp.float32)  2.38 us
  transfers between devices with their start and end apart: 28, of which 12 were waited for; matrix products, arithmetic and copies ran while one was open for 11% of the time, Pallas kernels for 8%

profile of v2, /device:TPU:0, one launch (start us, length us, event | category | flops | bytes accessed | tf_op | source)
XLA Modules:
  0.0 116.1 jit_solution(10368784119195071969)
XLA Ops:
  0.6 3.0 %collective-permute-start = (bf16[128,2048]{1,0:T(8,128)(2,1)}, bf16[128,2048]{1,0:T(8,128)(2,1)}, u32[]{:S(2)}, u32[]{:S(2)}) collective-permute-start(bf16[128,2048]{1,0:T(8,128)(2,1)} %tok_a), channel_id=1, source_target_pairs={{0,2},{1,3},{2,0},{3,1},{4,6},{5,7},{6,4},{7,5},{8,10},{9,11},{10,... | collective-permute-start | bytes 1572872 | tf_op jit(solution)/shard_map/ppermute | solution.py:22
  3.6 1.6 %collective-permute-start.1 = (bf16[128,2048]{1,0:T(8,128)(2,1)}, bf16[128,2048]{1,0:T(8,128)(2,1)}, u32[]{:S(2)}, u32[]{:S(2)}) collective-permute-start(bf16[128,2048]{1,0:T(8,128)(2,1)} %tok_a), channel_id=1, source_target_pairs={{0,8},{4,12},{8,0},{12,4},{16,24},{20,28},{24,16},{28,20},{1,9},{5... | collective-permute-start | bytes 1572872 | tf_op jit(solution)/shard_map/ppermute | solution.py:22
  5.2 2.8 %constant_dynamic-slice_fusion = (bf16[1,2,2,1,64,2048]{5,4,3,2,1,0:T(8,128)(2,1)}, bf16[1,2,2,1,64,2048]{5,4,3,2,1,0:T(8,128)(2,1)S(1)}) fusion(bf16[1,2,2,2,64,2048]{5,4,3,2,1,0:T(8,128)(2,1)} %bitcast.97, s32[]{:T(128)S(6)} %select_n.111, s32[]{:T(128)S(6)} %select_n.105), kind=kLoop, calls=%fused_computation.69 | loop fusion | bytes 4194312 | tf_op jit(solution)/shard_map/jit(dynamic_index_in_dim)/dynamic_slice | solution.py:26
  8.0 1.6 %collective-permute-start.6 = (bf16[1,2,2,64,2048]{4,3,1,2,0:T(8,128)(2,1)S(1)}, bf16[1,2,2,64,2048]{4,3,1,2,0:T(8,128)(2,1)S(1)}, u32[]{:S(2)}, u32[]{:S(2)}) collective-permute-start(bf16[1,2,2,64,2048]{4,3,1,2,0:T(8,128)(2,1)S(1)} %bitcast.98), channel_id=1, source_target_pairs={{0,4},{4,0},{8,12},{12,8},{16,20},{20,16},{24,28},{28,24},{1,5},{5... | collective-permute-start | bytes 3145736 | tf_op jit(solution)/shard_map/ppermute | solution.py:22
  11.0 5.7 %collective-permute-done.tok_a = bf16[128,2048]{1,0:T(8,128)(2,1)} collective-permute-done((bf16[128,2048]{1,0:T(8,128)(2,1)}, bf16[128,2048]{1,0:T(8,128)(2,1)}, u32[]{:S(2)}, u32[]{:S(2)}) %collective-permute-start) | collective-permute-done | bytes 524320 | tf_op jit(solution)/shard_map/ppermute | solution.py:22
  16.7 2.1 %collective-permute-done.1.tok_a = bf16[128,2048]{1,0:T(8,128)(2,1)} collective-permute-done((bf16[128,2048]{1,0:T(8,128)(2,1)}, bf16[128,2048]{1,0:T(8,128)(2,1)}, u32[]{:S(2)}, u32[]{:S(2)}) %collective-permute-start.1) | collective-permute-done | bytes 524320 | tf_op jit(solution)/shard_map/ppermute | solution.py:22
  18.8 1.9 %collective-permute-done.2.tok_b = bf16[128,2048]{1,0:T(8,128)(2,1)S(1)} collective-permute-done((bf16[128,2048]{1,0:T(8,128)(2,1)S(1)}, bf16[128,2048]{1,0:T(8,128)(2,1)S(1)}, u32[]{:S(2)}, u32[]{:S(2)}) %collective-permute-start.2) | collective-permute-done | bytes 524320 | tf_op jit(solution)/shard_map/ppermute | solution.py:22
  21.5 6.3 %collective-permute-done.3.cot_a = bf16[128,2176]{1,0:T(8,128)(2,1)} collective-permute-done((bf16[128,2176]{1,0:T(8,128)(2,1)S(1)}, bf16[128,2176]{1,0:T(8,128)(2,1)}, u32[]{:S(2)}, u32[]{:S(2)}) %collective-permute-start.3) | collective-permute-done | bytes 557088 | tf_op jit(solution)/shard_map/ppermute | solution.py:22
  27.8 1.4 %collective-permute-done.4.cot_a = bf16[128,2176]{1,0:T(8,128)(2,1)S(1)} collective-permute-done((bf16[128,2176]{1,0:T(8,128)(2,1)S(1)}, bf16[128,2176]{1,0:T(8,128)(2,1)S(1)}, u32[]{:S(2)}, u32[]{:S(2)}) %collective-permute-start.4) | collective-permute-done | bytes 557088 | tf_op jit(solution)/shard_map/ppermute | solution.py:22
  30.0 2.5 %collective-permute-done.6 = bf16[1,2,2,64,2048]{4,3,1,2,0:T(8,128)(2,1)S(1)} collective-permute-done((bf16[1,2,2,64,2048]{4,3,1,2,0:T(8,128)(2,1)S(1)}, bf16[1,2,2,64,2048]{4,3,1,2,0:T(8,128)(2,1)S(1)}, u32[]{:S(2)}, u32[]{:S(2)}) %collective-permute-start.6) | collective-permute-done | bytes 1048608 | tf_op jit(solution)/shard_map/ppermute | solution.py:22
  35.1 2.2 %copy-done = bf16[1,2048,1024]{2,1,0:T(8,128)(2,1)S(1)} copy-done((bf16[1,2048,1024]{2,1,0:T(8,128)(2,1)S(1)}, bf16[1,2048,1024]{2,1,0:T(8,128)(2,1)}, u32[]{:S(2)}) %copy-start) | copy-done | bytes 4194328
  37.3 1.1 copy-done.4
  40.4 2.4 %shard_map.94 = (bf16[256,1024]{1,0:T(8,128)(2,1)S(1)}, bf16[256,256]{1,0:T(8,128)(2,1)S(1)}, bf16[256,2048]{1,0:T(8,128)(2,1)S(1)}, bf16[256,1024]{1,0:T(8,128)(2,1)S(1)}) custom-call(s32[2]{0:T(128)S(1)} %pad_add_fusion.place, bf16[128,2048]{1,0:T(8,128)(2,1)S(1)} %copy-done.6, bf16[128,2048]{1,0:T(8,128)(2,1)S(1)} %copy-done.8, ...), custom_call_target="tpu_custom_call" | custom-call | tf_op jit(solution)/shard_map/pallas_call | solution.py:92
  43.2 3.5 %shard_map.96 = (bf16[256,1024]{1,0:T(8,128)(2,1)S(1)}, bf16[256,256]{1,0:T(8,128)(2,1)S(1)}, bf16[256,2048]{1,0:T(8,128)(2,1)S(1)}, bf16[256,1024]{1,0:T(8,128)(2,1)S(1)}) custom-call(s32[2]{0:T(128)S(1)} %pad_add_fusion.place, bf16[128,2048]{1,0:T(8,128)(2,1)} %collective-permute-done.1.tok_a, bf16[128,2048]{1,0:T(8,128)(2,1)} %collective-permute-done.11.tok_b, ...), custom_call_target="tpu_custom_call" | custom-call | tf_op jit(solution)/shard_map/pallas_call | solution.py:92
  46.7 3.5 %shard_map.95 = (bf16[256,1024]{1,0:T(8,128)(2,1)S(1)}, bf16[256,256]{1,0:T(8,128)(2,1)S(1)}, bf16[256,2048]{1,0:T(8,128)(2,1)S(1)}, bf16[256,1024]{1,0:T(8,128)(2,1)S(1)}) custom-call(s32[2]{0:T(128)S(1)} %pad_add_fusion.place, bf16[128,2048]{1,0:T(8,128)(2,1)} %collective-permute-done.tok_a, bf16[128,2048]{1,0:T(8,128)(2,1)} %collective-permute-done.7.tok_b, ...), custom_call_target="tpu_custom_call" | custom-call | tf_op jit(solution)/shard_map/pallas_call | solution.py:92
  51.2 1.9 %fusion.6 = f32[1024,1024]{1,0:T(8,128)S(1)} fusion(bf16[256,1024]{1,0:T(8,128)(2,1)S(1)} %get-tuple-element.49, bf16[256,1024]{1,0:T(8,128)(2,1)S(1)} %get-tuple-element.47, bf16[256,1024]{1,0:T(8,128)(2,1)S(1)} %get-tuple-element.46, bf16[256,1024]{1,0:T(8,128)(2,1)S(1)} %get-tuple-element.50, bf16[256,1024]{1,0:T(8,128)(2,1)S(1)} %get-tuple-element.44, ...), kind=kOutput, calls=%fused_computation.10 | convolution fusion | flops 1620049920 | bytes 7340032 | tf_op jit(solution)/shard_map/dot_general | solution.py:140
  53.1 3.6 %collective-permute-done.9.tok_a = bf16[128,2048]{1,0:T(8,128)(2,1)S(1)} collective-permute-done((bf16[128,2048]{1,0:T(8,128)(2,1)}, bf16[128,2048]{1,0:T(8,128)(2,1)S(1)}, u32[]{:S(2)}, u32[]{:S(2)}) %collective-permute-start.9) | collective-permute-done | bytes 524320 | tf_op jit(solution)/shard_map/ppermute | solution.py:22
  57.7 1.7 %collective-permute-done.13.tok_b = bf16[128,2048]{1,0:T(8,128)(2,1)S(1)} collective-permute-done((bf16[128,2048]{1,0:T(8,128)(2,1)S(1)}, bf16[128,2048]{1,0:T(8,128)(2,1)S(1)}, u32[]{:S(2)}, u32[]{:S(2)}) %collective-permute-start.13) | collective-permute-done | bytes 524320 | tf_op jit(solution)/shard_map/ppermute | solution.py:22
  59.4 2.5 %shard_map.97 = (bf16[256,1024]{1,0:T(8,128)(2,1)S(1)}, bf16[256,256]{1,0:T(8,128)(2,1)S(1)}, bf16[256,2048]{1,0:T(8,128)(2,1)S(1)}, bf16[256,1024]{1,0:T(8,128)(2,1)S(1)}) custom-call(s32[2]{0:T(128)S(1)} %pad_add_fusion.place, bf16[128,2048]{1,0:T(8,128)(2,1)S(1)} %collective-permute-done.9.tok_a, bf16[128,2048]{1,0:T(8,128)(2,1)S(1)} %collective-permute-done.13.tok_b, ...), custom_call_target="tpu_custom_call" | custom-call | tf_op jit(solution)/shard_map/pallas_call | solution.py:92
  62.6 1.3 %add_convert_fusion = bf16[1024,1024]{1,0:T(8,128)(2,1)S(1)} fusion(f32[1024,1024]{1,0:T(8,128)S(1)} %fusion.6, f32[1024,1024]{1,0:T(8,128)S(1)} %fusion.41), kind=kLoop, calls=%fused_computation | loop fusion | flops 2097152 | bytes 10485760 | tf_op jit(solution)/shard_map/convert_element_type | solution.py:18
  64.1 1.6 %collective-permute-start.21 = (bf16[1,64,1024]{2,1,0:T(8,128)(2,1)S(1)}, bf16[1,64,1024]{2,1,0:T(8,128)(2,1)S(1)}, u32[]{:S(2)}, u32[]{:S(2)}) collective-permute-start(bf16[1,64,1024]{2,1,0:T(8,128)(2,1)S(1)} %dynamic-slice_bitcast_fusion.4), channel_id=1, source_target_pairs={{0,4},{4,0},{8,12},{12,8},{16,20},{20,16},{24,28},{28,24},{1,5},{5... | collective-permute-start | bytes 393224 | tf_op jit(solution)/shard_map/ppermute | solution.py:22
  66.6 1.7 %collective-permute-start.18 = (bf16[1,128,1024]{2,1,0:T(8,128)(2,1)S(1)}, bf16[1,128,1024]{2,1,0:T(8,128)(2,1)S(1)}, u32[]{:S(2)}, u32[]{:S(2)}) collective-permute-start(bf16[1,128,1024]{2,1,0:T(8,128)(2,1)S(1)} %dynamic-slice_bitcast_fusion.3), channel_id=1, source_target_pairs={{0,4},{4,0},{8,12},{12,8},{16,20},{20,16},{24,28},{28,24},{1,5},{5... | collective-permute-start | bytes 786440 | tf_op jit(solution)/shard_map/ppermute | solution.py:22
  69.1 4.2 %collective-permute-done.15 = bf16[1,64,1024]{2,1,0:T(8,128)(2,1)S(1)} collective-permute-done((bf16[1,64,1024]{2,1,0:T(8,128)(2,1)S(1)}, bf16[1,64,1024]{2,1,0:T(8,128)(2,1)S(1)}, u32[]{:S(2)}, u32[]{:S(2)}) %collective-permute-start.15) | collective-permute-done | bytes 131104 | tf_op jit(solution)/shard_map/ppermute | solution.py:22
  73.4 2.4 %convolution_convert_fusion = bf16[512,2048]{1,0:T(8,128)(2,1)S(1)} fusion(bf16[512,1024]{1,0:T(8,128)(2,1)S(1)} %pad_maximum_fusion, bf16[1,2048,1024]{2,1,0:T(8,128)(2,1)S(1)} %copy-done.1), kind=kOutput, calls=%fused_computation.7 | convolution fusion | flops 2148532224 | bytes 7340032 | tf_op jit(solution)/shard_map/dot_general | solution.py:179
  76.1 1.6 %collective-permute-start.24 = (bf16[1,64,2048]{2,1,0:T(8,128)(2,1)S(1)}, bf16[1,64,2048]{2,1,0:T(8,128)(2,1)S(1)}, u32[]{:S(2)}, u32[]{:S(2)}) collective-permute-start(bf16[1,64,2048]{2,1,0:T(8,128)(2,1)S(1)} %get-tuple-element.67), channel_id=1, source_target_pairs={{0,4},{4,0},{8,12},{12,8},{16,20},{20,16},{24,28},{28,24},{1,5},{5... | collective-permute-start | bytes 786440 | tf_op jit(solution)/shard_map/ppermute | solution.py:22
  77.7 2.7 %collective-permute-start.20 = (bf16[1,64,1024]{2,1,0:T(8,128)(2,1)S(1)}, bf16[1,64,1024]{2,1,0:T(8,128)(2,1)S(1)}, u32[]{:S(2)}, u32[]{:S(2)}) collective-permute-start(bf16[1,64,1024]{2,1,0:T(8,128)(2,1)S(1)} %fusion.35), channel_id=1, source_target_pairs={{0,16},{4,20},{8,24},{12,28},{16,0},{20,4},{24,8},{28,12},{1,17},{... | collective-permute-start | bytes 393224 | tf_op jit(solution)/shard_map/ppermute | solution.py:22
  80.9 2.7 %collective-permute-start.23 = (bf16[1,128,1024]{2,1,0:T(8,128)(2,1)S(1)}, bf16[1,128,1024]{2,1,0:T(8,128)(2,1)S(1)}, u32[]{:S(2)}, u32[]{:S(2)}) collective-permute-start(bf16[1,128,1024]{2,1,0:T(8,128)(2,1)S(1)} %fusion.28), channel_id=1, source_target_pairs={{0,16},{4,20},{8,24},{12,28},{16,0},{20,4},{24,8},{28,12},{1,17},{... | collective-permute-start | bytes 786440 | tf_op jit(solution)/shard_map/ppermute | solution.py:22
  83.8 1.6 %collective-permute-start.17 = (bf16[128,2048]{1,0:T(8,128)(2,1)S(1)}, bf16[128,2048]{1,0:T(8,128)(2,1)S(1)}, u32[]{:S(2)}, u32[]{:S(2)}) collective-permute-start(bf16[128,2048]{1,0:T(8,128)(2,1)S(1)} %fusion.19), channel_id=1, source_target_pairs={{0,2},{1,3},{2,0},{3,1},{4,6},{5,7},{6,4},{7,5},{8,10},{9,11},{10,... | collective-permute-start | bytes 1572872 | tf_op jit(solution)/shard_map/ppermute | solution.py:22
  86.5 10.5 %collective-permute-done.17 = bf16[128,2048]{1,0:T(8,128)(2,1)S(1)} collective-permute-done((bf16[128,2048]{1,0:T(8,128)(2,1)S(1)}, bf16[128,2048]{1,0:T(8,128)(2,1)S(1)}, u32[]{:S(2)}, u32[]{:S(2)}) %collective-permute-start.17) | collective-permute-done | bytes 524320 | tf_op jit(solution)/shard_map/ppermute | solution.py:22
  99.2 10.7 %collective-permute-done.23 = bf16[1,128,1024]{2,1,0:T(8,128)(2,1)S(1)} collective-permute-done((bf16[1,128,1024]{2,1,0:T(8,128)(2,1)S(1)}, bf16[1,128,1024]{2,1,0:T(8,128)(2,1)S(1)}, u32[]{:S(2)}, u32[]{:S(2)}) %collective-permute-start.23) | collective-permute-done | bytes 262176 | tf_op jit(solution)/shard_map/ppermute | solution.py:22
  109.9 1.2 %fusion.18 = f32[1,256,1024]{2,1,0:T(8,128)} fusion(bf16[1,256,1024]{2,1,0:T(8,128)(2,1)S(1)} %collective-permute-done.19, bf16[1,128,1024]{2,1,0:T(8,128)(2,1)S(1)} %collective-permute-done.23, bf16[1,64,1024]{2,1,0:T(8,128)(2,1)S(1)} %collective-permute-done.22, bf16[1,64,1024]{2,1,0:T(8,128)(2,1)S(1)} %collective-permute-done.20, ...), kind=kLoop, calls=%fused_computation.26 | loop fusion | flops 2883584 | bytes 2621448 | tf_op jit(solution)/shard_map/mul | solution.py:198
  111.1 4.1 %collective-permute-done.27 = bf16[1,64,2048]{2,1,0:T(8,128)(2,1)S(1)} collective-permute-done((bf16[1,64,2048]{2,1,0:T(8,128)(2,1)S(1)}, bf16[1,64,2048]{2,1,0:T(8,128)(2,1)S(1)}, u32[]{:S(2)}, u32[]{:S(2)}) %collective-permute-start.27) | collective-permute-done | bytes 262176 | tf_op jit(solution)/shard_map/ppermute | solution.py:22
  (96 shorter events, 17.9 us)
Async XLA Ops:
  0.6 16.1 %collective-permute-start = (bf16[128,2048]{1,0:T(8,128)(2,1)}, bf16[128,2048]{1,0:T(8,128)(2,1)}, u32[]{:S(2)}, u32[]{:S(2)}) collective-permute-start(bf16[128,2048]{1,0:T(8,128)(2,1)} %tok_a), channel_id=1, source_target_pairs={{0,2},{1,3},{2,0},{3,1},{4,6},{5,7},{6,4},{7,5},{8,10},{9,11},{10,... | collective-permute-start | bytes 1572872 | tf_op jit(solution)/shard_map/ppermute | solution.py:22
  3.6 15.2 %collective-permute-start.1 = (bf16[128,2048]{1,0:T(8,128)(2,1)}, bf16[128,2048]{1,0:T(8,128)(2,1)}, u32[]{:S(2)}, u32[]{:S(2)}) collective-permute-start(bf16[128,2048]{1,0:T(8,128)(2,1)} %tok_a), channel_id=1, source_target_pairs={{0,8},{4,12},{8,0},{12,4},{16,24},{20,28},{24,16},{28,20},{1,9},{5... | collective-permute-start | bytes 1572872 | tf_op jit(solution)/shard_map/ppermute | solution.py:22
  8.0 10.8 %copy-start.5 = (bf16[128,2048]{1,0:T(8,128)(2,1)S(1)}, bf16[128,2048]{1,0:T(8,128)(2,1)}, u32[]{:S(2)}) copy-start(bf16[128,2048]{1,0:T(8,128)(2,1)} %tok_a) | copy-start | bytes 1572868
  8.0 27.1 %copy-start.2 = (bf16[1,512,2048]{2,1,0:T(8,128)(2,1)S(1)}, bf16[1,512,2048]{2,1,0:T(8,128)(2,1)}, u32[]{:S(2)}) copy-start(bf16[1,512,2048]{2,1,0:T(8,128)(2,1)} %param.12) | copy-start | bytes 6291460
  8.0 24.4 %collective-permute-start.6 = (bf16[1,2,2,64,2048]{4,3,1,2,0:T(8,128)(2,1)S(1)}, bf16[1,2,2,64,2048]{4,3,1,2,0:T(8,128)(2,1)S(1)}, u32[]{:S(2)}, u32[]{:S(2)}) collective-permute-start(bf16[1,2,2,64,2048]{4,3,1,2,0:T(8,128)(2,1)S(1)} %bitcast.98), channel_id=1, source_target_pairs={{0,4},{4,0},{8,12},{12,8},{16,20},{20,16},{24,28},{28,24},{1,5},{5... | collective-permute-start | bytes 3145736 | tf_op jit(solution)/shard_map/ppermute | solution.py:22
  9.9 17.9 %collective-permute-start.3 = (bf16[128,2176]{1,0:T(8,128)(2,1)S(1)}, bf16[128,2176]{1,0:T(8,128)(2,1)}, u32[]{:S(2)}, u32[]{:S(2)}) collective-permute-start(bf16[128,2176]{1,0:T(8,128)(2,1)S(1)} %pad_maximum_fusion.2.cot_a), channel_id=1, source_target_pairs={{0,2},{1,3},{2,0},{3,1},{4,6},{5,7},{6,4},{7,5},{8,10},{9,11},{10,... | collective-permute-start | bytes 1671176 | tf_op jit(solution)/shard_map/ppermute | solution.py:22
  10.5 18.6 %collective-permute-start.4 = (bf16[128,2176]{1,0:T(8,128)(2,1)S(1)}, bf16[128,2176]{1,0:T(8,128)(2,1)S(1)}, u32[]{:S(2)}, u32[]{:S(2)}) collective-permute-start(bf16[128,2176]{1,0:T(8,128)(2,1)S(1)} %pad_maximum_fusion.2.cot_a), channel_id=1, source_target_pairs={{0,8},{4,12},{8,0},{12,4},{16,24},{20,28},{24,16},{28,20},{1,9},{5... | collective-permute-start | bytes 1671176 | tf_op jit(solution)/shard_map/ppermute | solution.py:22
  16.7 12.5 %collective-permute-start.5 = (bf16[128,2176]{1,0:T(8,128)(2,1)S(1)}, bf16[128,2176]{1,0:T(8,128)(2,1)S(1)}, u32[]{:S(2)}, u32[]{:S(2)}) collective-permute-start(bf16[128,2176]{1,0:T(8,128)(2,1)S(1)} %pad_maximum_fusion.2.cot_a), channel_id=1, source_target_pairs={{0,1},{1,0},{2,3},{3,2},{4,5},{5,4},{6,7},{7,6},{8,9},{9,8},{10,11... | collective-permute-start | bytes 1671176 | tf_op jit(solution)/shard_map/ppermute | solution.py:22
  18.8 1.9 %collective-permute-start.2 = (bf16[128,2048]{1,0:T(8,128)(2,1)S(1)}, bf16[128,2048]{1,0:T(8,128)(2,1)S(1)}, u32[]{:S(2)}, u32[]{:S(2)}) collective-permute-start(bf16[128,2048]{1,0:T(8,128)(2,1)S(1)} %copy-done.5), channel_id=1, source_target_pairs={{0,1},{1,0},{2,3},{3,2},{4,5},{5,4},{6,7},{7,6},{8,9},{9,8},{10,11... | collective-permute-start | bytes 1572872 | tf_op jit(solution)/shard_map/ppermute | solution.py:22
  33.5 9.8 %collective-permute-start.12 = (bf16[128,2176]{1,0:T(8,128)(2,1)S(1)}, bf16[128,2176]{1,0:T(8,128)(2,1)}, u32[]{:S(2)}, u32[]{:S(2)}) collective-permute-start(bf16[128,2176]{1,0:T(8,128)(2,1)S(1)} %collective-permute-done.4.cot_a), channel_id=1, source_target_pairs={{0,1},{1,0},{2,3},{3,2},{4,5},{5,4},{6,7},{7,6},{8,9},{9,8},{10,11... | collective-permute-start | bytes 1671176 | tf_op jit(solution)/shard_map/ppermute | solution.py:22
  33.5 13.3 %collective-permute-start.8 = (bf16[128,2176]{1,0:T(8,128)(2,1)}, bf16[128,2176]{1,0:T(8,128)(2,1)}, u32[]{:S(2)}, u32[]{:S(2)}) collective-permute-start(bf16[128,2176]{1,0:T(8,128)(2,1)} %collective-permute-done.3.cot_a), channel_id=1, source_target_pairs={{0,1},{1,0},{2,3},{3,2},{4,5},{5,4},{6,7},{7,6},{8,9},{9,8},{10,11... | collective-permute-start | bytes 1671176 | tf_op jit(solution)/shard_map/ppermute | solution.py:22
  34.0 8.9 %collective-permute-start.11 = (bf16[128,2048]{1,0:T(8,128)(2,1)}, bf16[128,2048]{1,0:T(8,128)(2,1)}, u32[]{:S(2)}, u32[]{:S(2)}) collective-permute-start(bf16[128,2048]{1,0:T(8,128)(2,1)} %collective-permute-done.1.tok_a), channel_id=1, source_target_pairs={{0,1},{1,0},{2,3},{3,2},{4,5},{5,4},{6,7},{7,6},{8,9},{9,8},{10,11... | collective-permute-start | bytes 1572872 | tf_op jit(solution)/shard_map/ppermute | solution.py:22
  34.0 12.7 %collective-permute-start.7 = (bf16[128,2048]{1,0:T(8,128)(2,1)}, bf16[128,2048]{1,0:T(8,128)(2,1)}, u32[]{:S(2)}, u32[]{:S(2)}) collective-permute-start(bf16[128,2048]{1,0:T(8,128)(2,1)} %collective-permute-done.tok_a), channel_id=1, source_target_pairs={{0,1},{1,0},{2,3},{3,2},{4,5},{5,4},{6,7},{7,6},{8,9},{9,8},{10,11... | collective-permute-start | bytes 1572872 | tf_op jit(solution)/shard_map/ppermute | solution.py:22
  34.5 22.2 %collective-permute-start.10 = (bf16[128,2176]{1,0:T(8,128)(2,1)S(1)}, bf16[128,2176]{1,0:T(8,128)(2,1)S(1)}, u32[]{:S(2)}, u32[]{:S(2)}) collective-permute-start(bf16[128,2176]{1,0:T(8,128)(2,1)S(1)} %collective-permute-done.4.cot_a), channel_id=1, source_target_pairs={{0,2},{1,3},{2,0},{3,1},{4,6},{5,7},{6,4},{7,5},{8,10},{9,11},{10,... | collective-permute-start | bytes 1671176 | tf_op jit(solution)/shard_map/ppermute | solution.py:22
  42.9 13.8 %collective-permute-start.9 = (bf16[128,2048]{1,0:T(8,128)(2,1)}, bf16[128,2048]{1,0:T(8,128)(2,1)S(1)}, u32[]{:S(2)}, u32[]{:S(2)}) collective-permute-start(bf16[128,2048]{1,0:T(8,128)(2,1)} %collective-permute-done.tok_a), channel_id=1, source_target_pairs={{0,8},{4,12},{8,0},{12,4},{16,24},{20,28},{24,16},{28,20},{1,9},{5... | collective-permute-start | bytes 1572872 | tf_op jit(solution)/shard_map/ppermute | solution.py:22
  51.2 6.0 %copy-start.9 = (bf16[1,2,2,1,64,2048]{5,4,3,2,1,0:T(8,128)(2,1)S(1)}, bf16[1,2,2,1,64,2048]{5,4,3,2,1,0:T(8,128)(2,1)}, u32[]{:S(2)}) copy-start(bf16[1,2,2,1,64,2048]{5,4,3,2,1,0:T(8,128)(2,1)} %get-tuple-element.71) | copy-start | bytes 3145732
  51.2 6.0 %copy-start.11 = (bf16[1,2,2,64,2048]{4,3,1,2,0:T(8,128)(2,1)S(1)}, bf16[1,2,2,64,2048]{4,3,1,2,0:T(8,128)(2,1)}, u32[]{:S(2)}) copy-start(bf16[1,2,2,64,2048]{4,3,1,2,0:T(8,128)(2,1)} %copy-done.10) | copy-start | bytes 3145732
  56.7 2.7 %collective-permute-start.14 = (bf16[128,2176]{1,0:T(8,128)(2,1)S(1)}, bf16[128,2176]{1,0:T(8,128)(2,1)S(1)}, u32[]{:S(2)}, u32[]{:S(2)}) collective-permute-start(bf16[128,2176]{1,0:T(8,128)(2,1)S(1)} %collective-permute-done.10.cot_a), channel_id=1, source_target_pairs={{0,1},{1,0},{2,3},{3,2},{4,5},{5,4},{6,7},{7,6},{8,9},{9,8},{10,11... | collective-permute-start | bytes 1671176 | tf_op jit(solution)/shard_map/ppermute | solution.py:22
  56.7 2.7 %collective-permute-start.13 = (bf16[128,2048]{1,0:T(8,128)(2,1)S(1)}, bf16[128,2048]{1,0:T(8,128)(2,1)S(1)}, u32[]{:S(2)}, u32[]{:S(2)}) collective-permute-start(bf16[128,2048]{1,0:T(8,128)(2,1)S(1)} %collective-permute-done.9.tok_a), channel_id=1, source_target_pairs={{0,1},{1,0},{2,3},{3,2},{4,5},{5,4},{6,7},{7,6},{8,9},{9,8},{10,11... | collective-permute-start | bytes 1572872 | tf_op jit(solution)/shard_map/ppermute | solution.py:22
  64.1 12.0 %collective-permute-start.21 = (bf16[1,64,1024]{2,1,0:T(8,128)(2,1)S(1)}, bf16[1,64,1024]{2,1,0:T(8,128)(2,1)S(1)}, u32[]{:S(2)}, u32[]{:S(2)}) collective-permute-start(bf16[1,64,1024]{2,1,0:T(8,128)(2,1)S(1)} %dynamic-slice_bitcast_fusion.4), channel_id=1, source_target_pairs={{0,4},{4,0},{8,12},{12,8},{16,20},{20,16},{24,28},{28,24},{1,5},{5... | collective-permute-start | bytes 393224 | tf_op jit(solution)/shard_map/ppermute | solution.py:22
  65.7 7.6 %collective-permute-start.15 = (bf16[1,64,1024]{2,1,0:T(8,128)(2,1)S(1)}, bf16[1,64,1024]{2,1,0:T(8,128)(2,1)S(1)}, u32[]{:S(2)}, u32[]{:S(2)}) collective-permute-start(bf16[1,64,1024]{2,1,0:T(8,128)(2,1)S(1)} %dynamic-slice_bitcast_fusion.5), channel_id=1, source_target_pairs={{0,4},{4,0},{8,12},{12,8},{16,20},{20,16},{24,28},{28,24},{1,5},{5... | collective-permute-start | bytes 393224 | tf_op jit(solution)/shard_map/ppermute | solution.py:22
  66.3 17.4 %collective-permute-start.26 = (bf16[1,2,64,2048]{3,2,1,0:T(8,128)(2,1)S(1)}, bf16[1,2,64,2048]{3,2,1,0:T(8,128)(2,1)S(1)}, u32[]{:S(2)}, u32[]{:S(2)}) collective-permute-start(bf16[1,2,64,2048]{3,2,1,0:T(8,128)(2,1)S(1)} %fusion.22), channel_id=1, source_target_pairs={{0,8},{4,12},{8,0},{12,4},{16,24},{20,28},{24,16},{28,20},{1,9},{5... | collective-permute-start | bytes 1572872 | tf_op jit(solution)/shard_map/ppermute | solution.py:22
  66.6 13.8 %collective-permute-start.18 = (bf16[1,128,1024]{2,1,0:T(8,128)(2,1)S(1)}, bf16[1,128,1024]{2,1,0:T(8,128)(2,1)S(1)}, u32[]{:S(2)}, u32[]{:S(2)}) collective-permute-start(bf16[1,128,1024]{2,1,0:T(8,128)(2,1)S(1)} %dynamic-slice_bitcast_fusion.3), channel_id=1, source_target_pairs={{0,4},{4,0},{8,12},{12,8},{16,20},{20,16},{24,28},{28,24},{1,5},{5... | collective-permute-start | bytes 786440 | tf_op jit(solution)/shard_map/ppermute | solution.py:22
  75.9 5.0 %collective-permute-start.16 = (bf16[2,128,2048]{2,1,0:T(8,128)(2,1)S(1)}, bf16[2,128,2048]{2,1,0:T(8,128)(2,1)S(1)}, u32[]{:S(2)}, u32[]{:S(2)}) collective-permute-start(bf16[2,128,2048]{2,1,0:T(8,128)(2,1)S(1)} %pad_maximum_fusion.1), channel_id=1, source_target_pairs={{0,1},{1,0},{2,3},{3,2},{4,5},{5,4},{6,7},{7,6},{8,9},{9,8},{10,11... | collective-permute-start | bytes 3145736 | tf_op jit(solution)/shard_map/ppermute | solution.py:22
  76.1 9.3 %collective-permute-start.24 = (bf16[1,64,2048]{2,1,0:T(8,128)(2,1)S(1)}, bf16[1,64,2048]{2,1,0:T(8,128)(2,1)S(1)}, u32[]{:S(2)}, u32[]{:S(2)}) collective-permute-start(bf16[1,64,2048]{2,1,0:T(8,128)(2,1)S(1)} %get-tuple-element.67), channel_id=1, source_target_pairs={{0,4},{4,0},{8,12},{12,8},{16,20},{20,16},{24,28},{28,24},{1,5},{5... | collective-permute-start | bytes 786440 | tf_op jit(solution)/shard_map/ppermute | solution.py:22
  77.7 20.6 %collective-permute-start.20 = (bf16[1,64,1024]{2,1,0:T(8,128)(2,1)S(1)}, bf16[1,64,1024]{2,1,0:T(8,128)(2,1)S(1)}, u32[]{:S(2)}, u32[]{:S(2)}) collective-permute-start(bf16[1,64,1024]{2,1,0:T(8,128)(2,1)S(1)} %fusion.35), channel_id=1, source_target_pairs={{0,16},{4,20},{8,24},{12,28},{16,0},{20,4},{24,8},{28,12},{1,17},{... | collective-permute-start | bytes 393224 | tf_op jit(solution)/shard_map/ppermute | solution.py:22
  80.5 18.7 %collective-permute-start.22 = (bf16[1,64,1024]{2,1,0:T(8,128)(2,1)S(1)}, bf16[1,64,1024]{2,1,0:T(8,128)(2,1)S(1)}, u32[]{:S(2)}, u32[]{:S(2)}) collective-permute-start(bf16[1,64,1024]{2,1,0:T(8,128)(2,1)S(1)} %fusion.34), channel_id=1, source_target_pairs={{0,16},{4,20},{8,24},{12,28},{16,0},{20,4},{24,8},{28,12},{1,17},{... | collective-permute-start | bytes 393224 | tf_op jit(solution)/shard_map/ppermute | solution.py:22
  80.9 28.9 %collective-permute-start.23 = (bf16[1,128,1024]{2,1,0:T(8,128)(2,1)S(1)}, bf16[1,128,1024]{2,1,0:T(8,128)(2,1)S(1)}, u32[]{:S(2)}, u32[]{:S(2)}) collective-permute-start(bf16[1,128,1024]{2,1,0:T(8,128)(2,1)S(1)} %fusion.28), channel_id=1, source_target_pairs={{0,16},{4,20},{8,24},{12,28},{16,0},{20,4},{24,8},{28,12},{1,17},{... | collective-permute-start | bytes 786440 | tf_op jit(solution)/shard_map/ppermute | solution.py:22
  83.8 13.2 %collective-permute-start.17 = (bf16[128,2048]{1,0:T(8,128)(2,1)S(1)}, bf16[128,2048]{1,0:T(8,128)(2,1)S(1)}, u32[]{:S(2)}, u32[]{:S(2)}) collective-permute-start(bf16[128,2048]{1,0:T(8,128)(2,1)S(1)} %fusion.19), channel_id=1, source_target_pairs={{0,2},{1,3},{2,0},{3,1},{4,6},{5,7},{6,4},{7,5},{8,10},{9,11},{10,... | collective-permute-start | bytes 1572872 | tf_op jit(solution)/shard_map/ppermute | solution.py:22
  85.5 24.4 %collective-permute-start.19 = (bf16[1,256,1024]{2,1,0:T(8,128)(2,1)S(1)}, bf16[1,256,1024]{2,1,0:T(8,128)(2,1)S(1)}, u32[]{:S(2)}, u32[]{:S(2)}) collective-permute-start(bf16[1,256,1024]{2,1,0:T(8,128)(2,1)S(1)} %dynamic-slice_bitcast_fusion), channel_id=1, source_target_pairs={{0,4},{4,0},{8,12},{12,8},{16,20},{20,16},{24,28},{28,24},{1,5},{5... | collective-permute-start | bytes 1572872 | tf_op jit(solution)/shard_map/ppermute | solution.py:22
  97.0 18.2 %collective-permute-start.27 = (bf16[1,64,2048]{2,1,0:T(8,128)(2,1)S(1)}, bf16[1,64,2048]{2,1,0:T(8,128)(2,1)S(1)}, u32[]{:S(2)}, u32[]{:S(2)}) collective-permute-start(bf16[1,64,2048]{2,1,0:T(8,128)(2,1)S(1)} %fusion.24), channel_id=1, source_target_pairs={{0,16},{4,20},{8,24},{12,28},{16,0},{20,4},{24,8},{28,12},{1,17},{... | collective-permute-start | bytes 786440 | tf_op jit(solution)/shard_map/ppermute | solution.py:22
  98.4 16.8 %collective-permute-start.25 = (bf16[1,64,2048]{2,1,0:T(8,128)(2,1)S(1)}, bf16[1,64,2048]{2,1,0:T(8,128)(2,1)S(1)}, u32[]{:S(2)}, u32[]{:S(2)}) collective-permute-start(bf16[1,64,2048]{2,1,0:T(8,128)(2,1)S(1)} %get-tuple-element.68), channel_id=1, source_target_pairs={{0,4},{4,0},{8,12},{12,8},{16,20},{20,16},{24,28},{28,24},{1,5},{5... | collective-permute-start | bytes 786440 | tf_op jit(solution)/shard_map/ppermute | solution.py:22
  (11 other events, 25.0 us)

commit v3 on v2

v3 whole, which is shorter than its diff:
```python
import functools

import jax
import jax.numpy as jnp
from jax import lax
from jax.experimental import pallas as pl
from jax.experimental.pallas import tpu as pltpu
from jax.sharding import PartitionSpec as P

LANES = 128


def wide(values):
    return values.astype(jnp.float32)


def narrow(values):
    return values.astype(jnp.bfloat16)


def flip(values, axis, bit):
    return lax.ppermute(values, axis, [(i, i ^ bit) for i in range(lax.axis_size(axis))])


def take(values, axis, index):
    return lax.dynamic_index_in_dim(values, index, axis, keepdims=False)


def with_routes(cotangent, expert_ids, gate_probs, expert_count):
    lane = jnp.arange(LANES, dtype=jnp.int32)[None, :]
    route = jnp.zeros((expert_ids.shape[0], LANES), jnp.float32)
    for k in range(expert_ids.shape[1]):
        hit = (lane < 3 * expert_count) & (lane // 3 == expert_ids[:, k : k + 1])
        route = route + jnp.where(hit, gate_probs[:, k : k + 1], 0.0)
    high = lax.reduce_precision(route, 8, 7)
    middle = lax.reduce_precision(route - high, 8, 7)
    low = (route - high) - middle
    part = lane % 3
    coded = jnp.where(part == 0, high, jnp.where(part == 1, middle, low))
    return jnp.concatenate([cotangent, narrow(coded)], axis=1)


def own_columns(values, group_count, parity):
    unit = values.shape[1] // group_count * 2
    blocks = [values[:, k * unit : (k + 1) * unit] for k in range(group_count // 2)]
    even, odd = jnp.concatenate(blocks[0::2], axis=1), jnp.concatenate(blocks[1::2], axis=1)
    return jnp.where(parity == 1, odd, even)


def expert_rows(place, group_count, toks, cots, gate_up, down, scaled, back):
    width, units = gate_up.shape[0], down.shape[0]
    tile = units // 2
    lane = lax.broadcasted_iota(jnp.int32, (1, LANES), 1)
    at = 0
    for cot in cots:
        coded = wide(cot[:, width:])
        part = [
            jnp.sum(jnp.where(lane == 3 * place[0] + k, coded, 0.0), axis=1, keepdims=True)
            for k in range(3)
        ]
        weight = (part[0] + part[1]) + part[2]
        scaled[at : at + cot.shape[0], :] = narrow(wide(cot[:, :width]) * weight)
        at += cot.shape[0]
    rows = jnp.concatenate([tok[...] for tok in toks], axis=0)
    grads = scaled[...]
    contract = (((1,), (1,)), ((), ()))
    hidden = []
    for at in range(0, units, tile):
        gate = jnp.dot(rows, gate_up[:, at : at + tile], preferred_element_type=jnp.float32)
        up = jnp.dot(
            rows, gate_up[:, units + at : units + at + tile], preferred_element_type=jnp.float32
        )
        sig = jax.nn.sigmoid(gate)
        activated = gate * sig
        hidden.append(narrow(activated * up))
        back_hidden = lax.dot_general(
            grads, down[at : at + tile, :], contract, preferred_element_type=jnp.float32
        )
        slope = up * sig * (1.0 + gate * (1.0 - sig))
        back[:, at : at + tile] = narrow(back_hidden * slope)
        back[:, units + at : units + at + tile] = narrow(back_hidden * activated)
    hid_cols = own_columns(jnp.concatenate(hidden, axis=1), group_count, place[1])
    return own_columns(rows, group_count, place[1]), hid_cols


ROWS = (((0,), (0,)), ((), ()))


def early_kernel(group_count, place, *refs):
    pairs, (gate_up, down, gate_sum, down_sum, back_group, scaled, back) = refs[:12], refs[12:]
    rows = scaled.shape[0]
    for k in range(3):
        tok_a, tok_b, cot_a, cot_b = pairs[4 * k : 4 * k + 4]
        here = back_group.at[k * rows : (k + 1) * rows, :] if k < 2 else back
        tok_cols, hid_cols = expert_rows(
            place, group_count, (tok_a, tok_b), (cot_a, cot_b), gate_up, down, scaled, here
        )
        gate = lax.dot_general(tok_cols, here[...], ROWS, preferred_element_type=jnp.float32)
        down_part = lax.dot_general(hid_cols, scaled[...], ROWS, preferred_element_type=jnp.float32)
        gate_sum[...] = gate if k == 0 else gate_sum[...] + gate
        down_sum[...] = down_part if k == 0 else down_sum[...] + down_part


def early_terms(group_count, place, pairs, gate_up, down):
    rows, width = 2 * pairs[0][0].shape[0], pairs[0][0].shape[1]
    units = down.shape[0]
    vmem = pl.BlockSpec(memory_space=pltpu.VMEM)
    return pl.pallas_call(
        functools.partial(early_kernel, group_count),
        out_shape=(
            jax.ShapeDtypeStruct((width // 2, 2 * units), jnp.float32),
            jax.ShapeDtypeStruct((units // 2, width), jnp.float32),
            jax.ShapeDtypeStruct((2 * rows, 2 * units), jnp.bfloat16),
        ),
        in_specs=[pl.BlockSpec(memory_space=pltpu.SMEM)] + [vmem] * 14,
        out_specs=(vmem,) * 3,
        scratch_shapes=[
            pltpu.VMEM((rows, width), jnp.bfloat16),
            pltpu.VMEM((rows, 2 * units), jnp.bfloat16),
        ],
        compiler_params=pltpu.CompilerParams(vmem_limit_bytes=30 << 20),
        cost_estimate=pl.CostEstimate(flops=0, bytes_accessed=0, transcendentals=0),
    )(place, *[v for pair in pairs for v in pair], gate_up, down)


def last_kernel(group_count, cuts, place, *refs):
    tok_a, tok_b, cot_a, cot_b, gate_up, down, gate_sum, hid_own, scaled = refs[:9]
    pieces, (back, total) = refs[9:-2], refs[-2:]
    tok_cols, hid_own[...] = expert_rows(
        place, group_count, (tok_a, tok_b), (cot_a, cot_b), gate_up, down, scaled, back
    )
    term = lax.dot_general(tok_cols, back[...], ROWS, preferred_element_type=jnp.float32)
    total[...] = gate_sum[...] + term
    bit0, bit2 = place[2], place[3]
    count = total.shape[0] // (group_count // 2)
    sides = ((1 - bit2, 1 - bit0), (1 - bit2, bit0), (bit2, 1 - bit0), (bit2, bit0))
    at = 0
    for (third, first), splits in zip(sides, (cuts, cuts, (0, count), (0, count))):
        for start, stop in zip(splits, splits[1:]):
            for high in range(group_count // 8):
                row = (high * 4 + third * 2 + first) * count + start
                row = pl.multiple_of(row, 8)
                pieces[at][high] = narrow(total[pl.ds(row, stop - start), :])
            at += 1


def last_terms(group_count, cuts, place, pair, gate_up, down, gate_sum):
    rows, width = 2 * pair[0].shape[0], pair[0].shape[1]
    units, high_count, count = down.shape[0], group_count // 8, cuts[-1]
    sizes = [b - a for a, b in zip(cuts, cuts[1:])] * 2 + [count] * 2
    vmem = pl.BlockSpec(memory_space=pltpu.VMEM)
    shapes = [(rows, units // 2), (rows, width)]
    shapes += [(high_count, size, 2 * units) for size in sizes]
    return pl.pallas_call(
        functools.partial(last_kernel, group_count, cuts),
        out_shape=tuple(jax.ShapeDtypeStruct(shape, jnp.bfloat16) for shape in shapes),
        in_specs=[pl.BlockSpec(memory_space=pltpu.SMEM)] + [vmem] * 7,
        out_specs=(vmem,) * len(shapes),
        scratch_shapes=[
            pltpu.VMEM((rows, 2 * units), jnp.bfloat16),
            pltpu.VMEM((width // 2, 2 * units), jnp.float32),
        ],
        compiler_params=pltpu.CompilerParams(vmem_limit_bytes=30 << 20),
        cost_estimate=pl.CostEstimate(flops=0, bytes_accessed=0, transcendentals=0),
    )(place, *pair, gate_up, down, gate_sum)


def on_device(
    tokens, cotangent, expert_ids, gate_probs, gate_up_weight, down_weight, down_residual
):
    tok_rows, model_width = tokens.shape
    expert_count = lax.axis_size("expert")
    group_count = lax.axis_size("dp")
    gate_up, down_matrix = gate_up_weight[0], down_weight[0]
    hidden_units = down_matrix.shape[0]
    me, group = lax.axis_index("expert"), lax.axis_index("dp")
    bit0, bit1, bit2 = group & 1, (group >> 1) & 1, (group >> 2) & 1
    high_count = group_count // 8

    residual = down_residual[0, 0].reshape(high_count, 2, 2, 2, -1, model_width)

    def residual_pair(source, parity):
        part = take(source, 2, parity)
        return take(part, 2, bit0), flip(take(part, 2, 1 - bit0), "dp", 1)

    tok_x, tok_n = flip(tokens, "expert", 2), flip(tokens, "dp", 2)
    tok_c = flip(tokens, "expert", 1)
    carried = with_routes(cotangent, expert_ids, gate_probs, expert_count)
    cot_x, cot_n = flip(carried, "expert", 2), flip(carried, "dp", 2)
    cot_c = flip(carried, "expert", 1)
    res_other = residual_pair(residual, 1 - bit1)
    tok_x, tok_n, tok_c, cot_x, cot_n, cot_c, tok_own, cot_own, res_other, residual = (
        lax.optimization_barrier(
            (tok_x, tok_n, tok_c, cot_x, cot_n, cot_c, tokens, carried, res_other, residual)
        )
    )
    tok_d, cot_d = flip(tok_x, "dp", 2), flip(cot_n, "expert", 2)
    res_mine = residual_pair(residual, bit1)
    place = jnp.stack([me, bit1, bit0, bit2]).astype(jnp.int32)

    def both_cores(tok, cot):
        return tok, flip(tok, "expert", 1), cot, flip(cot, "expert", 1)

    pairs = ((tok_own, tok_c, cot_own, cot_c), both_cores(tok_x, cot_x), both_cores(tok_n, cot_n))
    gate_sum, down_sum, back_group = early_terms(group_count, place, pairs, gate_up, down_matrix)
    tok_d, cot_d, gate_sum, down_sum, res_mine = lax.optimization_barrier(
        (tok_d, cot_d, gate_sum, down_sum, res_mine)
    )
    count = model_width // group_count
    first = max(count // 4, 16)
    cuts = (0, first, count // 2, count) if first < count // 2 else (0, first, count)
    hid_cols, scaled, *gate_pieces = last_terms(
        group_count, cuts, place, both_cores(tok_d, cot_d), gate_up, down_matrix, gate_sum
    )
    down_term = lax.dot_general(hid_cols, scaled, ROWS, preferred_element_type=jnp.float32)
    down_term = narrow(down_sum + down_term).reshape(high_count, 2, 2, -1, model_width)

    parts = len(cuts) - 1
    far_sent, far_kept = gate_pieces[:parts], gate_pieces[parts : 2 * parts]
    near_sent, near_kept = gate_pieces[2 * parts :]
    got = [flip(far_sent[0], "dp", 1)]
    second, down_term = lax.optimization_barrier((far_sent[1], down_term))
    got.append(flip(second, "dp", 1))
    for piece in far_sent[2:]:
        piece, _ = lax.optimization_barrier((piece, got[0]))
        got.append(flip(piece, "dp", 1))
    crossed = [
        flip(narrow(wide(kept) + wide(piece)), "dp", 4) for kept, piece in zip(far_kept, got)
    ]

    def down_side(third, side):
        return take(take(down_term, 1, third), 1, side)

    res_send = narrow(wide(res_other[0]) + wide(res_other[1]))
    res_send, _ = lax.optimization_barrier((res_send, got[0]))
    res_sum = wide(res_mine[0]) + wide(res_mine[1]) + wide(flip(res_send, "dp", 2))
    down_sent, _ = lax.optimization_barrier((down_side(1 - bit2, 1 - bit0), got[1]))
    got_down = flip(down_sent, "dp", 1)
    far_down = wide(down_side(1 - bit2, bit0)) + wide(got_down) + take(res_sum, 1, 1 - bit2)
    crossed_down = flip(narrow(far_down), "dp", 4)

    back_group, _ = lax.optimization_barrier((back_group, got[-1]))
    token_part = narrow(jnp.dot(back_group, gate_up.T, preferred_element_type=jnp.float32))
    blocks = token_part.reshape(expert_count, tok_rows, model_width)
    core = flip(jnp.stack([blocks[1], blocks[3]]), "expert", 1)
    across = flip(narrow(wide(blocks[2]) + wide(core[1])), "expert", 2)
    token_grad = narrow(wide(blocks[0]) + wide(core[0]) + wide(across))

    near_sent, _ = lax.optimization_barrier((near_sent, got[-1]))
    near_gate = wide(near_kept) + wide(flip(near_sent, "dp", 1))
    down_sent, _ = lax.optimization_barrier((down_side(bit2, 1 - bit0), got_down))
    near_down = wide(down_side(bit2, bit0)) + wide(flip(down_sent, "dp", 1))
    crossed, token_grad = lax.optimization_barrier((crossed, token_grad))
    gate_sum = near_gate + wide(jnp.concatenate(crossed, axis=1))
    down_sum = near_down + take(res_sum, 1, bit2) + wide(crossed_down)
    bit = 8
    while bit < group_count:
        side = (group // bit) & 1
        halves = [v.reshape(-1, 2, *v.shape[1:]) for v in (gate_sum, down_sum)]
        gate_sum, down_sum = [
            take(v, 1, side) + wide(flip(narrow(take(v, 1, 1 - side)), "dp", bit)) for v in halves
        ]
        bit *= 2
    factor = 1.0 / group_count
    grad_gate_up, grad_down = gate_sum * factor, down_sum * factor
    return (token_grad, grad_gate_up, grad_down)


def solution(mesh):
    placed = (
        P(("dp", "expert"), None),
        P(("dp", "expert"), None),
        P(("dp", "expert"), None),
        P(("dp", "expert"), None),
        P("expert", None, None),
        P("expert", None, None),
        P("dp", "expert", None, None),
    )
    return jax.shard_map(
        on_device,
        mesh=mesh,
        in_specs=placed,
        out_specs=(P(("dp", "expert"), None), P("expert", "dp", None), P("expert", "dp", None)),
        check_vma=False,
    )
```

time: 116 us -> 131 us (1.13)
  local copies, waits for them, and re-layouts: 11.2 us -> 21.1 us
  matrix products: 6.44 us -> 2.82 us
  starting transfers between devices: 24.9 us -> 27.8 us
  Pallas kernels: 11.8 us -> 14.1 us
  waiting for transfers between devices: 54.7 us -> 56.6 us
    unnamed x30 -> x38, local copies, waits for them, and re-layouts: 7.95 us -> 16.4 us
    squeeze x5 -> x3, local copies, waits for them, and re-layouts: 0.14 us -> 4.54 us  [take(): return lax.dynamic_index_in_dim(values, index, axis, keepdims=False)]
    dot_general x4 -> x1, matrix products: 4.06 us -> 0.46 us  [on_device(): lax.dot_general(hid_cols, scaled, ROWS, preferred_element_type=jnp.float32)]
    ppermute x28 -> x29, starting transfers between devices: 24.9 us -> 27.8 us  [flip(): lax.ppermute(values, axis, [(i, i ^ bit) for i in range(lax.axis_size(axi...]
    dynamic_slice x2 -> x0, local copies, waits for them, and re-layouts: 2.82 us -> none  [take(): return lax.dynamic_index_in_dim(values, index, axis, keepdims=False)]
    pallas_call x4 -> x2, Pallas kernels: 11.8 us -> 14.1 us  [the longest x1 10 us: early_terms(): pl.pallas_call(functools.partial(early_kernel, group_count), out_shape=(j...]
    ppermute x28 -> x29, waiting for transfers between devices: 54.7 us -> 56.6 us  [flip(): lax.ppermute(values, axis, [(i, i ^ bit) for i in range(lax.axis_size(axi...]
  transfers between devices with their start and end apart: 28 -> 29, of which waited for: 12 -> 10; matrix products, arithmetic and copies ran while one was open for 11% -> 8% of each run, Pallas kernels for 8% -> 8%
where the time goes in v3:
time: 131 us; the launch traced here: 130 us
  waiting for transfers between devices  56.6 us (43%)
  starting transfers between devices  27.8 us (21%)
  local copies, waits for them, and re-layouts  21.1 us (16%)
  Pallas kernels  14.1 us (11%)
  other arithmetic  6.81 us (5%)
  matrix products  2.82 us (2%)
    ppermute x29, waiting for transfers between devices, flip(): lax.ppermute(values, axis, [(i, i ^ bit) for i in range(lax.axis_size(axi...  56.6 us
    ppermute x29, starting transfers between devices, flip(): lax.ppermute(values, axis, [(i, i ^ bit) for i in range(lax.axis_size(axi...  27.8 us
    unnamed x38, local copies, waits for them, and re-layouts  16.4 us
    pallas_call x1, Pallas kernels, early_terms(): pl.pallas_call(functools.partial(early_kernel, group_count), out_shape=(j...  10 us
    squeeze x3, local copies, waits for them, and re-layouts, take(): return lax.dynamic_index_in_dim(values, index, axis, keepdims=False)  4.54 us
    pallas_call x1, Pallas kernels, last_terms(): pl.pallas_call(functools.partial(last_kernel, group_count, cuts), out_sha...  4.13 us
    convert_element_type x9, other arithmetic, narrow(): return values.astype(jnp.bfloat16)  3.16 us
  transfers between devices with their start and end apart: 29, of which 10 were waited for; matrix products, arithmetic and copies ran while one was open for 8% of the time, Pallas kernels for 8%

profile of v3, /device:TPU:0, one launch (start us, length us, event | category | flops | bytes accessed | tf_op | source)
XLA Modules:
  0.0 130.2 jit_solution(8076424572009679068)
XLA Ops:
  0.7 2.1 %dynamic-slice_bitcast_fusion.2 = (bf16[1,2,64,2048]{3,2,1,0:T(8,128)(2,1)S(1)}, bf16[1,2,64,2048]{3,2,1,0:T(8,128)(2,1)}) fusion(bf16[1,2,2,2,64,2048]{5,4,3,2,1,0:T(8,128)(2,1)} %bitcast.64, s32[]{:T(128)S(6)} %select_n.96, s32[]{:T(128)S(6)} %select_n.100, s32[]{:T(128)S(6)} %select_n.98), kind=kLoop, calls=%fused_computation.26 | loop fusion | bytes 2097164 | tf_op jit(solution)/shard_map/jit(dynamic_index_in_dim)/squeeze | solution.py:26
  2.8 3.0 %collective-permute-start.6 = (bf16[1,2,64,2048]{3,2,1,0:T(8,128)(2,1)S(1)}, bf16[1,2,64,2048]{3,2,1,0:T(8,128)(2,1)}, u32[]{:S(2)}, u32[]{:S(2)}) collective-permute-start(bf16[1,2,64,2048]{3,2,1,0:T(8,128)(2,1)S(1)} %get-tuple-element.91), channel_id=1, source_target_pairs={{0,4},{4,0},{8,12},{12,8},{16,20},{20,16},{24,28},{28,24},{1,5},{5... | collective-permute-start | bytes 1572872 | tf_op jit(solution)/shard_map/ppermute | solution.py:22
  5.8 1.5 %collective-permute-start = (bf16[128,2048]{1,0:T(8,128)(2,1)}, bf16[128,2048]{1,0:T(8,128)(2,1)}, u32[]{:S(2)}, u32[]{:S(2)}) collective-permute-start(bf16[128,2048]{1,0:T(8,128)(2,1)} %refs_0_), channel_id=1, source_target_pairs={{0,2},{1,3},{2,0},{3,1},{4,6},{5,7},{6,4},{7,5},{8,10},{9,11},{10,... | collective-permute-start | bytes 1572872 | tf_op jit(solution)/shard_map/ppermute | solution.py:22
  8.2 1.6 %collective-permute-start.4 = (bf16[128,2176]{1,0:T(8,128)(2,1)S(1)}, bf16[128,2176]{1,0:T(8,128)(2,1)S(1)}, u32[]{:S(2)}, u32[]{:S(2)}) collective-permute-start(bf16[128,2176]{1,0:T(8,128)(2,1)S(1)} %pad_maximum_fusion.1.refs_2_), channel_id=1, source_target_pairs={{0,8},{4,12},{8,0},{12,4},{16,24},{20,28},{24,16},{28,20},{1,9},{5... | collective-permute-start | bytes 1671176 | tf_op jit(solution)/shard_map/ppermute | solution.py:22
  9.8 8.1 %collective-permute-done.6 = bf16[1,2,64,2048]{3,2,1,0:T(8,128)(2,1)} collective-permute-done((bf16[1,2,64,2048]{3,2,1,0:T(8,128)(2,1)S(1)}, bf16[1,2,64,2048]{3,2,1,0:T(8,128)(2,1)}, u32[]{:S(2)}, u32[]{:S(2)}) %collective-permute-start.6) | collective-permute-done | bytes 524320 | tf_op jit(solution)/shard_map/ppermute | solution.py:22
  17.8 1.8 %collective-permute-start.1 = (bf16[128,2048]{1,0:T(8,128)(2,1)}, bf16[128,2048]{1,0:T(8,128)(2,1)}, u32[]{:S(2)}, u32[]{:S(2)}) collective-permute-start(bf16[128,2048]{1,0:T(8,128)(2,1)} %refs_0_), channel_id=1, source_target_pairs={{0,8},{4,12},{8,0},{12,4},{16,24},{20,28},{24,16},{28,20},{1,9},{5... | collective-permute-start | bytes 1572872 | tf_op jit(solution)/shard_map/ppermute | solution.py:22
  19.6 1.3 %collective-permute-done.refs_4_ = bf16[128,2048]{1,0:T(8,128)(2,1)} collective-permute-done((bf16[128,2048]{1,0:T(8,128)(2,1)}, bf16[128,2048]{1,0:T(8,128)(2,1)}, u32[]{:S(2)}, u32[]{:S(2)}) %collective-permute-start) | collective-permute-done | bytes 524320 | tf_op jit(solution)/shard_map/ppermute | solution.py:22
  21.0 12.1 %collective-permute-done.1.refs_8_ = bf16[128,2048]{1,0:T(8,128)(2,1)} collective-permute-done((bf16[128,2048]{1,0:T(8,128)(2,1)}, bf16[128,2048]{1,0:T(8,128)(2,1)}, u32[]{:S(2)}, u32[]{:S(2)}) %collective-permute-start.1) | collective-permute-done | bytes 524320 | tf_op jit(solution)/shard_map/ppermute | solution.py:22
  36.0 1.5 %collective-permute-start.8 = (bf16[128,2176]{1,0:T(8,128)(2,1)S(1)}, bf16[128,2176]{1,0:T(8,128)(2,1)}, u32[]{:S(2)}, u32[]{:S(2)}) collective-permute-start(bf16[128,2176]{1,0:T(8,128)(2,1)S(1)} %collective-permute-done.4.refs_10_), channel_id=1, source_target_pairs={{0,2},{1,3},{2,0},{3,1},{4,6},{5,7},{6,4},{7,5},{8,10},{9,11},{10,... | collective-permute-start | bytes 1671176 | tf_op jit(solution)/shard_map/ppermute | solution.py:22
  37.7 2.4 %dynamic-slice_bitcast_fusion = (bf16[1,2,64,2048]{3,2,1,0:T(8,128)(2,1)}, bf16[1,2,64,2048]{3,2,1,0:T(8,128)(2,1)}) fusion(bf16[1,2,2,2,64,2048]{5,4,3,2,1,0:T(8,128)(2,1)} %bitcast.65, s32[]{:T(128)S(6)} %select_n.102, s32[]{:T(128)S(6)} %select_n.100, s32[]{:T(128)S(6)} %select_n.98), kind=kLoop, calls=%fused_computation.24 | loop fusion | bytes 2097164 | tf_op jit(solution)/shard_map/jit(dynamic_index_in_dim)/squeeze | solution.py:26
  40.6 1.6 %collective-permute-start.7 = (bf16[128,2048]{1,0:T(8,128)(2,1)}, bf16[128,2048]{1,0:T(8,128)(2,1)}, u32[]{:S(2)}, u32[]{:S(2)}) collective-permute-start(bf16[128,2048]{1,0:T(8,128)(2,1)} %collective-permute-done.refs_4_), channel_id=1, source_target_pairs={{0,8},{4,12},{8,0},{12,4},{16,24},{20,28},{24,16},{28,20},{1,9},{5... | collective-permute-start | bytes 1572872 | tf_op jit(solution)/shard_map/ppermute | solution.py:22
  42.2 2.2 %copy-done = bf16[1,2048,1024]{2,1,0:T(8,128)(2,1)S(1)} copy-done((bf16[1,2048,1024]{2,1,0:T(8,128)(2,1)S(1)}, bf16[1,2048,1024]{2,1,0:T(8,128)(2,1)}, u32[]{:S(2)}) %copy-start) | copy-done | bytes 4194328
  47.6 10.0 %shard_map.94 = (f32[1024,1024]{1,0:T(8,128)S(1)}, f32[256,2048]{1,0:T(8,128)S(1)}, bf16[512,1024]{1,0:T(8,128)(2,1)S(1)}) custom-call(s32[4]{0:T(128)S(1)} %pad_add_fusion.place, bf16[128,2048]{1,0:T(8,128)(2,1)} %refs_0_, bf16[128,2048]{1,0:T(8,128)(2,1)S(1)} %copy-done.12, bf16[128,2176]{1,0:T(8,128)(2,1)S(1)} %pad_maximum_fusion.1.refs_2_, ...), custom_call_target="tpu_custom_call" | custom-call | tf_op jit(solution)/shard_map/pallas_call | solution.py:108
  57.6 2.0 %copy-done.3 = f32[1024,1024]{1,0:T(8,128)} copy-done((f32[1024,1024]{1,0:T(8,128)}, f32[1024,1024]{1,0:T(8,128)S(1)}, u32[]{:S(2)}) %copy-start.3) | copy-done | bytes 4194328
  59.6 1.4 %copy-done.5 = f32[256,2048]{1,0:T(8,128)} copy-done((f32[256,2048]{1,0:T(8,128)}, f32[256,2048]{1,0:T(8,128)S(1)}, u32[]{:S(2)}) %copy-start.5) | copy-done | bytes 2097176
  62.5 1.3 %add_convert_fusion.1 = bf16[1,2,64,2048]{3,2,1,0:T(8,128)(2,1)S(1)} fusion(bf16[1,2,64,2048]{3,2,1,0:T(8,128)(2,1)} %collective-permute-done.6, bf16[1,2,64,2048]{3,2,1,0:T(8,128)(2,1)} %get-tuple-element.84), kind=kLoop, calls=%fused_computation.9 | loop fusion | flops 1048576 | bytes 1572864 | tf_op jit(solution)/shard_map/convert_element_type | solution.py:18
  64.9 2.2 %copy-done.1 = bf16[1,2048,1024]{2,1,0:T(8,128)(2,1)S(1)} copy-done((bf16[1,2048,1024]{2,1,0:T(8,128)(2,1)S(1)}, bf16[1,2048,1024]{2,1,0:T(8,128)(2,1)}, u32[]{:S(2)}) %copy-start.1) | copy-done | bytes 4194328
  67.1 2.2 %copy-done.4 = f32[1024,1024]{1,0:T(8,128)S(1)} copy-done((f32[1024,1024]{1,0:T(8,128)S(1)}, f32[1024,1024]{1,0:T(8,128)}, u32[]{:S(2)}) %copy-start.4) | copy-done | bytes 4194328
  69.3 4.1 %shard_map.95 = (bf16[256,256]{1,0:T(8,128)(2,1)S(1)}, bf16[256,2048]{1,0:T(8,128)(2,1)S(1)}, bf16[1,64,1024]{2,1,0:T(8,128)(2,1)S(1)}, bf16[1,64,1024]{2,1,0:T(...) custom-call(s32[4]{0:T(128)S(1)} %pad_add_fusion.place, ...), custom_call_target="tpu_custom_call" | custom-call | tf_op jit(solution)/shard_map/pallas_call | solution.py:154
  73.4 1.6 %collective-permute-start.16 = (bf16[1,64,1024]{2,1,0:T(8,128)(2,1)S(1)}, bf16[1,64,1024]{2,1,0:T(8,128)(2,1)S(1)}, u32[]{:S(2)}, u32[]{:S(2)}) collective-permute-start(bf16[1,64,1024]{2,1,0:T(8,128)(2,1)S(1)} %get-tuple-element.60), channel_id=1, source_target_pairs={{0,4},{4,0},{8,12},{12,8},{16,20},{20,16},{24,28},{28,24},{1,5},{5... | collective-permute-start | bytes 393224 | tf_op jit(solution)/shard_map/ppermute | solution.py:22
  76.9 2.8 %collective-permute-done.16 = bf16[1,64,1024]{2,1,0:T(8,128)(2,1)S(1)} collective-permute-done((bf16[1,64,1024]{2,1,0:T(8,128)(2,1)S(1)}, bf16[1,64,1024]{2,1,0:T(8,128)(2,1)S(1)}, u32[]{:S(2)}, u32[]{:S(2)}) %collective-permute-start.16) | collective-permute-done | bytes 131104 | tf_op jit(solution)/shard_map/ppermute | solution.py:22
  79.7 1.6 %collective-permute-start.20 = (bf16[1,128,1024]{2,1,0:T(8,128)(2,1)S(1)}, bf16[1,128,1024]{2,1,0:T(8,128)(2,1)S(1)}, u32[]{:S(2)}, u32[]{:S(2)}) collective-permute-start(bf16[1,128,1024]{2,1,0:T(8,128)(2,1)S(1)} %get-tuple-element.69), channel_id=1, source_target_pairs={{0,4},{4,0},{8,12},{12,8},{16,20},{20,16},{24,28},{28,24},{1,5},{5... | collective-permute-start | bytes 786440 | tf_op jit(solution)/shard_map/ppermute | solution.py:22
  82.5 1.6 %collective-permute-start.25 = (bf16[1,64,2048]{2,1,0:T(8,128)(2,1)S(1)}, bf16[1,64,2048]{2,1,0:T(8,128)(2,1)S(1)}, u32[]{:S(2)}, u32[]{:S(2)}) collective-permute-start(bf16[1,64,2048]{2,1,0:T(8,128)(2,1)S(1)} %get-tuple-element.80), channel_id=1, source_target_pairs={{0,4},{4,0},{8,12},{12,8},{16,20},{20,16},{24,28},{28,24},{1,5},{5... | collective-permute-start | bytes 786440 | tf_op jit(solution)/shard_map/ppermute | solution.py:22
  84.6 2.6 %collective-permute-start.19 = (bf16[1,64,1024]{2,1,0:T(8,128)(2,1)S(1)}, bf16[1,64,1024]{2,1,0:T(8,128)(2,1)S(1)}, u32[]{:S(2)}, u32[]{:S(2)}) collective-permute-start(bf16[1,64,1024]{2,1,0:T(8,128)(2,1)S(1)} %add_convert_fusion.3), channel_id=1, source_target_pairs={{0,16},{4,20},{8,24},{12,28},{16,0},{20,4},{24,8},{28,12},{1,17},{... | collective-permute-start | bytes 393224 | tf_op jit(solution)/shard_map/ppermute | solution.py:22
  87.3 1.6 %collective-permute-done.20 = bf16[1,128,1024]{2,1,0:T(8,128)(2,1)S(1)} collective-permute-done((bf16[1,128,1024]{2,1,0:T(8,128)(2,1)S(1)}, bf16[1,128,1024]{2,1,0:T(8,128)(2,1)S(1)}, u32[]{:S(2)}, u32[]{:S(2)}) %collective-permute-start.20) | collective-permute-done | bytes 262176 | tf_op jit(solution)/shard_map/ppermute | solution.py:22
  88.9 2.4 %convolution_convert_fusion = bf16[512,2048]{1,0:T(8,128)(2,1)S(1)} fusion(bf16[512,1024]{1,0:T(8,128)(2,1)S(1)} %copy-done.14, bf16[1,2048,1024]{2,1,0:T(8,128)(2,1)S(1)} %copy-done.1), kind=kOutput, calls=%fused_computation | convolution fusion | flops 2148532224 | bytes 7340032 | tf_op jit(solution)/shard_map/dot_general | solution.py:243
  91.7 2.6 %collective-permute-start.17 = (bf16[1,64,1024]{2,1,0:T(8,128)(2,1)S(1)}, bf16[1,64,1024]{2,1,0:T(8,128)(2,1)S(1)}, u32[]{:S(2)}, u32[]{:S(2)}) collective-permute-start(bf16[1,64,1024]{2,1,0:T(8,128)(2,1)S(1)} %add_convert_fusion.4), channel_id=1, source_target_pairs={{0,16},{4,20},{8,24},{12,28},{16,0},{20,4},{24,8},{28,12},{1,17},{... | collective-permute-start | bytes 393224 | tf_op jit(solution)/shard_map/ppermute | solution.py:22
  94.3 1.7 %collective-permute-start.26 = (bf16[1,64,2048]{2,1,0:T(8,128)(2,1)S(1)}, bf16[1,64,2048]{2,1,0:T(8,128)(2,1)S(1)}, u32[]{:S(2)}, u32[]{:S(2)}) collective-permute-start(bf16[1,64,2048]{2,1,0:T(8,128)(2,1)S(1)} %get-tuple-element.81), channel_id=1, source_target_pairs={{0,4},{4,0},{8,12},{12,8},{16,20},{20,16},{24,28},{28,24},{1,5},{5... | collective-permute-start | bytes 786440 | tf_op jit(solution)/shard_map/ppermute | solution.py:22
  96.0 5.8 %collective-permute-done.27 = bf16[1,2,64,2048]{3,2,1,0:T(8,128)(2,1)S(1)} collective-permute-done((bf16[1,2,64,2048]{3,2,1,0:T(8,128)(2,1)S(1)}, bf16[1,2,64,2048]{3,2,1,0:T(8,128)(2,1)S(1)}, u32[]{:S(2)}, u32[]{:S(2)}) %collective-permute-start.27) | collective-permute-done | bytes 524320 | tf_op jit(solution)/shard_map/ppermute | solution.py:22
  101.8 1.3 convert_add_fusion.2
  104.4 10.8 %collective-permute-done.28 = bf16[1,64,2048]{2,1,0:T(8,128)(2,1)S(1)} collective-permute-done((bf16[1,64,2048]{2,1,0:T(8,128)(2,1)S(1)}, bf16[1,64,2048]{2,1,0:T(8,128)(2,1)S(1)}, u32[]{:S(2)}, u32[]{:S(2)}) %collective-permute-start.28) | collective-permute-done | bytes 262176 | tf_op jit(solution)/shard_map/ppermute | solution.py:22
  117.2 11.8 %collective-permute-done.21 = bf16[1,128,1024]{2,1,0:T(8,128)(2,1)S(1)} collective-permute-done((bf16[1,128,1024]{2,1,0:T(8,128)(2,1)S(1)}, bf16[1,128,1024]{2,1,0:T(8,128)(2,1)S(1)}, u32[]{:S(2)}, u32[]{:S(2)}) %collective-permute-start.21) | collective-permute-done | bytes 262176 | tf_op jit(solution)/shard_map/ppermute | solution.py:22
  (92 shorter events, 18.7 us)
Async XLA Ops:
  2.8 39.4 %copy-start.2 = (bf16[1,512,2048]{2,1,0:T(8,128)(2,1)S(1)}, bf16[1,512,2048]{2,1,0:T(8,128)(2,1)}, u32[]{:S(2)}) copy-start(bf16[1,512,2048]{2,1,0:T(8,128)(2,1)} %param.12) | copy-start | bytes 6291460
  2.8 15.0 %collective-permute-start.6 = (bf16[1,2,64,2048]{3,2,1,0:T(8,128)(2,1)S(1)}, bf16[1,2,64,2048]{3,2,1,0:T(8,128)(2,1)}, u32[]{:S(2)}, u32[]{:S(2)}) collective-permute-start(bf16[1,2,64,2048]{3,2,1,0:T(8,128)(2,1)S(1)} %get-tuple-element.91), channel_id=1, source_target_pairs={{0,4},{4,0},{8,12},{12,8},{16,20},{20,16},{24,28},{28,24},{1,5},{5... | collective-permute-start | bytes 1572872 | tf_op jit(solution)/shard_map/ppermute | solution.py:22
  5.8 15.2 %collective-permute-start = (bf16[128,2048]{1,0:T(8,128)(2,1)}, bf16[128,2048]{1,0:T(8,128)(2,1)}, u32[]{:S(2)}, u32[]{:S(2)}) collective-permute-start(bf16[128,2048]{1,0:T(8,128)(2,1)} %refs_0_), channel_id=1, source_target_pairs={{0,2},{1,3},{2,0},{3,1},{4,6},{5,7},{6,4},{7,5},{8,10},{9,11},{10,... | collective-permute-start | bytes 1572872 | tf_op jit(solution)/shard_map/ppermute | solution.py:22
  7.6 26.3 %collective-permute-start.3 = (bf16[128,2176]{1,0:T(8,128)(2,1)S(1)}, bf16[128,2176]{1,0:T(8,128)(2,1)S(1)}, u32[]{:S(2)}, u32[]{:S(2)}) collective-permute-start(bf16[128,2176]{1,0:T(8,128)(2,1)S(1)} %pad_maximum_fusion.1.refs_2_), channel_id=1, source_target_pairs={{0,2},{1,3},{2,0},{3,1},{4,6},{5,7},{6,4},{7,5},{8,10},{9,11},{10,... | collective-permute-start | bytes 1671176 | tf_op jit(solution)/shard_map/ppermute | solution.py:22
  8.2 25.7 %collective-permute-start.4 = (bf16[128,2176]{1,0:T(8,128)(2,1)S(1)}, bf16[128,2176]{1,0:T(8,128)(2,1)S(1)}, u32[]{:S(2)}, u32[]{:S(2)}) collective-permute-start(bf16[128,2176]{1,0:T(8,128)(2,1)S(1)} %pad_maximum_fusion.1.refs_2_), channel_id=1, source_target_pairs={{0,8},{4,12},{8,0},{12,4},{16,24},{20,28},{24,16},{28,20},{1,9},{5... | collective-permute-start | bytes 1671176 | tf_op jit(solution)/shard_map/ppermute | solution.py:22
  9.8 24.1 %collective-permute-start.5 = (bf16[128,2176]{1,0:T(8,128)(2,1)S(1)}, bf16[128,2176]{1,0:T(8,128)(2,1)S(1)}, u32[]{:S(2)}, u32[]{:S(2)}) collective-permute-start(bf16[128,2176]{1,0:T(8,128)(2,1)S(1)} %pad_maximum_fusion.1.refs_2_), channel_id=1, source_target_pairs={{0,1},{1,0},{2,3},{3,2},{4,5},{5,4},{6,7},{7,6},{8,9},{9,8},{10,11... | collective-permute-start | bytes 1671176 | tf_op jit(solution)/shard_map/ppermute | solution.py:22
  17.8 15.2 %collective-permute-start.1 = (bf16[128,2048]{1,0:T(8,128)(2,1)}, bf16[128,2048]{1,0:T(8,128)(2,1)}, u32[]{:S(2)}, u32[]{:S(2)}) collective-permute-start(bf16[128,2048]{1,0:T(8,128)(2,1)} %refs_0_), channel_id=1, source_target_pairs={{0,8},{4,12},{8,0},{12,4},{16,24},{20,28},{24,16},{28,20},{1,9},{5... | collective-permute-start | bytes 1572872 | tf_op jit(solution)/shard_map/ppermute | solution.py:22
  21.0 12.1 %collective-permute-start.2 = (bf16[128,2048]{1,0:T(8,128)(2,1)}, bf16[128,2048]{1,0:T(8,128)(2,1)S(1)}, u32[]{:S(2)}, u32[]{:S(2)}) collective-permute-start(bf16[128,2048]{1,0:T(8,128)(2,1)} %refs_0_), channel_id=1, source_target_pairs={{0,1},{1,0},{2,3},{3,2},{4,5},{5,4},{6,7},{7,6},{8,9},{9,8},{10,11... | collective-permute-start | bytes 1572872 | tf_op jit(solution)/shard_map/ppermute | solution.py:22
  35.5 4.6 %collective-permute-start.9 = (bf16[128,2048]{1,0:T(8,128)(2,1)}, bf16[128,2048]{1,0:T(8,128)(2,1)}, u32[]{:S(2)}, u32[]{:S(2)}) collective-permute-start(bf16[128,2048]{1,0:T(8,128)(2,1)} %collective-permute-done.refs_4_), channel_id=1, source_target_pairs={{0,1},{1,0},{2,3},{3,2},{4,5},{5,4},{6,7},{7,6},{8,9},{9,8},{10,11... | collective-permute-start | bytes 1572872 | tf_op jit(solution)/shard_map/ppermute | solution.py:22
  35.5 5.1 %collective-permute-start.11 = (bf16[128,2048]{1,0:T(8,128)(2,1)}, bf16[128,2048]{1,0:T(8,128)(2,1)}, u32[]{:S(2)}, u32[]{:S(2)}) collective-permute-start(bf16[128,2048]{1,0:T(8,128)(2,1)} %collective-permute-done.1.refs_8_), channel_id=1, source_target_pairs={{0,1},{1,0},{2,3},{3,2},{4,5},{5,4},{6,7},{7,6},{8,9},{9,8},{10,11... | collective-permute-start | bytes 1572872 | tf_op jit(solution)/shard_map/ppermute | solution.py:22
  36.0 6.2 %collective-permute-start.12 = (bf16[128,2176]{1,0:T(8,128)(2,1)S(1)}, bf16[128,2176]{1,0:T(8,128)(2,1)}, u32[]{:S(2)}, u32[]{:S(2)}) collective-permute-start(bf16[128,2176]{1,0:T(8,128)(2,1)S(1)} %collective-permute-done.4.refs_10_), channel_id=1, source_target_pairs={{0,1},{1,0},{2,3},{3,2},{4,5},{5,4},{6,7},{7,6},{8,9},{9,8},{10,11... | collective-permute-start | bytes 1671176 | tf_op jit(solution)/shard_map/ppermute | solution.py:22
  36.0 25.9 %collective-permute-start.8 = (bf16[128,2176]{1,0:T(8,128)(2,1)S(1)}, bf16[128,2176]{1,0:T(8,128)(2,1)}, u32[]{:S(2)}, u32[]{:S(2)}) collective-permute-start(bf16[128,2176]{1,0:T(8,128)(2,1)S(1)} %collective-permute-done.4.refs_10_), channel_id=1, source_target_pairs={{0,2},{1,3},{2,0},{3,1},{4,6},{5,7},{6,4},{7,5},{8,10},{9,11},{10,... | collective-permute-start | bytes 1671176 | tf_op jit(solution)/shard_map/ppermute | solution.py:22
  37.5 4.8 %collective-permute-start.10 = (bf16[128,2176]{1,0:T(8,128)(2,1)}, bf16[128,2176]{1,0:T(8,128)(2,1)}, u32[]{:S(2)}, u32[]{:S(2)}) collective-permute-start(bf16[128,2176]{1,0:T(8,128)(2,1)} %copy-done.7), channel_id=1, source_target_pairs={{0,1},{1,0},{2,3},{3,2},{4,5},{5,4},{6,7},{7,6},{8,9},{9,8},{10,11... | collective-permute-start | bytes 1671176 | tf_op jit(solution)/shard_map/ppermute | solution.py:22
  40.1 21.8 %collective-permute-start.13 = (bf16[1,2,64,2048]{3,2,1,0:T(8,128)(2,1)}, bf16[1,2,64,2048]{3,2,1,0:T(8,128)(2,1)}, u32[]{:S(2)}, u32[]{:S(2)}) collective-permute-start(bf16[1,2,64,2048]{3,2,1,0:T(8,128)(2,1)} %get-tuple-element.89), channel_id=1, source_target_pairs={{0,4},{4,0},{8,12},{12,8},{16,20},{20,16},{24,28},{28,24},{1,5},{5... | collective-permute-start | bytes 1572872 | tf_op jit(solution)/shard_map/ppermute | solution.py:22
  40.6 21.3 %collective-permute-start.7 = (bf16[128,2048]{1,0:T(8,128)(2,1)}, bf16[128,2048]{1,0:T(8,128)(2,1)}, u32[]{:S(2)}, u32[]{:S(2)}) collective-permute-start(bf16[128,2048]{1,0:T(8,128)(2,1)} %collective-permute-done.refs_4_), channel_id=1, source_target_pairs={{0,8},{4,12},{8,0},{12,4},{16,24},{20,28},{24,16},{28,20},{1,9},{5... | collective-permute-start | bytes 1572872 | tf_op jit(solution)/shard_map/ppermute | solution.py:22
  61.9 3.0 %collective-permute-start.15 = (bf16[128,2176]{1,0:T(8,128)(2,1)}, bf16[128,2176]{1,0:T(8,128)(2,1)S(1)}, u32[]{:S(2)}, u32[]{:S(2)}) collective-permute-start(bf16[128,2176]{1,0:T(8,128)(2,1)} %collective-permute-done.8.refs_2_), channel_id=1, source_target_pairs={{0,1},{1,0},{2,3},{3,2},{4,5},{5,4},{6,7},{7,6},{8,9},{9,8},{10,11... | collective-permute-start | bytes 1671176 | tf_op jit(solution)/shard_map/ppermute | solution.py:22
  62.0 2.9 %collective-permute-start.14 = (bf16[128,2048]{1,0:T(8,128)(2,1)}, bf16[128,2048]{1,0:T(8,128)(2,1)S(1)}, u32[]{:S(2)}, u32[]{:S(2)}) collective-permute-start(bf16[128,2048]{1,0:T(8,128)(2,1)} %collective-permute-done.7.refs_0_), channel_id=1, source_target_pairs={{0,1},{1,0},{2,3},{3,2},{4,5},{5,4},{6,7},{7,6},{8,9},{9,8},{10,11... | collective-permute-start | bytes 1572872 | tf_op jit(solution)/shard_map/ppermute | solution.py:22
  73.4 6.3 %collective-permute-start.16 = (bf16[1,64,1024]{2,1,0:T(8,128)(2,1)S(1)}, bf16[1,64,1024]{2,1,0:T(8,128)(2,1)S(1)}, u32[]{:S(2)}, u32[]{:S(2)}) collective-permute-start(bf16[1,64,1024]{2,1,0:T(8,128)(2,1)S(1)} %get-tuple-element.60), channel_id=1, source_target_pairs={{0,4},{4,0},{8,12},{12,8},{16,20},{20,16},{24,28},{28,24},{1,5},{5... | collective-permute-start | bytes 393224 | tf_op jit(solution)/shard_map/ppermute | solution.py:22
  75.5 13.5 %copy-start.14 = (bf16[512,1024]{1,0:T(8,128)(2,1)S(1)}, bf16[512,1024]{1,0:T(8,128)(2,1)}, u32[]{:S(2)}) copy-start(bf16[512,1024]{1,0:T(8,128)(2,1)} %copy-done.13) | copy-start | bytes 3145732
  75.8 6.7 %collective-permute-start.18 = (bf16[1,64,1024]{2,1,0:T(8,128)(2,1)S(1)}, bf16[1,64,1024]{2,1,0:T(8,128)(2,1)S(1)}, u32[]{:S(2)}, u32[]{:S(2)}) collective-permute-start(bf16[1,64,1024]{2,1,0:T(8,128)(2,1)S(1)} %get-tuple-element.66), channel_id=1, source_target_pairs={{0,4},{4,0},{8,12},{12,8},{16,20},{20,16},{24,28},{28,24},{1,5},{5... | collective-permute-start | bytes 393224 | tf_op jit(solution)/shard_map/ppermute | solution.py:22
  79.7 9.2 %collective-permute-start.20 = (bf16[1,128,1024]{2,1,0:T(8,128)(2,1)S(1)}, bf16[1,128,1024]{2,1,0:T(8,128)(2,1)S(1)}, u32[]{:S(2)}, u32[]{:S(2)}) collective-permute-start(bf16[1,128,1024]{2,1,0:T(8,128)(2,1)S(1)} %get-tuple-element.69), channel_id=1, source_target_pairs={{0,4},{4,0},{8,12},{12,8},{16,20},{20,16},{24,28},{28,24},{1,5},{5... | collective-permute-start | bytes 786440 | tf_op jit(solution)/shard_map/ppermute | solution.py:22
  82.5 11.8 %collective-permute-start.25 = (bf16[1,64,2048]{2,1,0:T(8,128)(2,1)S(1)}, bf16[1,64,2048]{2,1,0:T(8,128)(2,1)S(1)}, u32[]{:S(2)}, u32[]{:S(2)}) collective-permute-start(bf16[1,64,2048]{2,1,0:T(8,128)(2,1)S(1)} %get-tuple-element.80), channel_id=1, source_target_pairs={{0,4},{4,0},{8,12},{12,8},{16,20},{20,16},{24,28},{28,24},{1,5},{5... | collective-permute-start | bytes 786440 | tf_op jit(solution)/shard_map/ppermute | solution.py:22
  84.1 17.6 %collective-permute-start.27 = (bf16[1,2,64,2048]{3,2,1,0:T(8,128)(2,1)S(1)}, bf16[1,2,64,2048]{3,2,1,0:T(8,128)(2,1)S(1)}, u32[]{:S(2)}, u32[]{:S(2)}) collective-permute-start(bf16[1,2,64,2048]{3,2,1,0:T(8,128)(2,1)S(1)} %add_convert_fusion.1), channel_id=1, source_target_pairs={{0,8},{4,12},{8,0},{12,4},{16,24},{20,28},{24,16},{28,20},{1,9},{5... | collective-permute-start | bytes 1572872 | tf_op jit(solution)/shard_map/ppermute | solution.py:22
  84.6 32.5 %collective-permute-start.19 = (bf16[1,64,1024]{2,1,0:T(8,128)(2,1)S(1)}, bf16[1,64,1024]{2,1,0:T(8,128)(2,1)S(1)}, u32[]{:S(2)}, u32[]{:S(2)}) collective-permute-start(bf16[1,64,1024]{2,1,0:T(8,128)(2,1)S(1)} %add_convert_fusion.3), channel_id=1, source_target_pairs={{0,16},{4,20},{8,24},{12,28},{16,0},{20,4},{24,8},{28,12},{1,17},{... | collective-permute-start | bytes 393224 | tf_op jit(solution)/shard_map/ppermute | solution.py:22
  91.3 10.5 %copy-start.15 = (bf16[1,2,64,2048]{3,2,1,0:T(8,128)(2,1)S(1)}, bf16[1,2,64,2048]{3,2,1,0:T(8,128)(2,1)}, u32[]{:S(2)}) copy-start(bf16[1,2,64,2048]{3,2,1,0:T(8,128)(2,1)} %get-tuple-element.82) | copy-start | bytes 1572868
  91.5 11.7 %collective-permute-start.22 = (bf16[2,128,2048]{2,1,0:T(8,128)(2,1)S(1)}, bf16[2,128,2048]{2,1,0:T(8,128)(2,1)S(1)}, u32[]{:S(2)}, u32[]{:S(2)}) collective-permute-start(bf16[2,128,2048]{2,1,0:T(8,128)(2,1)S(1)} %pad_maximum_fusion), channel_id=1, source_target_pairs={{0,1},{1,0},{2,3},{3,2},{4,5},{5,4},{6,7},{7,6},{8,9},{9,8},{10,11... | collective-permute-start | bytes 3145736 | tf_op jit(solution)/shard_map/ppermute | solution.py:22
  91.7 25.5 %collective-permute-start.17 = (bf16[1,64,1024]{2,1,0:T(8,128)(2,1)S(1)}, bf16[1,64,1024]{2,1,0:T(8,128)(2,1)S(1)}, u32[]{:S(2)}, u32[]{:S(2)}) collective-permute-start(bf16[1,64,1024]{2,1,0:T(8,128)(2,1)S(1)} %add_convert_fusion.4), channel_id=1, source_target_pairs={{0,16},{4,20},{8,24},{12,28},{16,0},{20,4},{24,8},{28,12},{1,17},{... | collective-permute-start | bytes 393224 | tf_op jit(solution)/shard_map/ppermute | solution.py:22
  94.3 9.8 %collective-permute-start.26 = (bf16[1,64,2048]{2,1,0:T(8,128)(2,1)S(1)}, bf16[1,64,2048]{2,1,0:T(8,128)(2,1)S(1)}, u32[]{:S(2)}, u32[]{:S(2)}) collective-permute-start(bf16[1,64,2048]{2,1,0:T(8,128)(2,1)S(1)} %get-tuple-element.81), channel_id=1, source_target_pairs={{0,4},{4,0},{8,12},{12,8},{16,20},{20,16},{24,28},{28,24},{1,5},{5... | collective-permute-start | bytes 786440 | tf_op jit(solution)/shard_map/ppermute | solution.py:22
  103.1 12.1 %collective-permute-start.28 = (bf16[1,64,2048]{2,1,0:T(8,128)(2,1)S(1)}, bf16[1,64,2048]{2,1,0:T(8,128)(2,1)S(1)}, u32[]{:S(2)}, u32[]{:S(2)}) collective-permute-start(bf16[1,64,2048]{2,1,0:T(8,128)(2,1)S(1)} %fusion.4), channel_id=1, source_target_pairs={{0,16},{4,20},{8,24},{12,28},{16,0},{20,4},{24,8},{28,12},{1,17},{... | collective-permute-start | bytes 786440 | tf_op jit(solution)/shard_map/ppermute | solution.py:22
  103.4 12.8 %collective-permute-start.23 = (bf16[128,2048]{1,0:T(8,128)(2,1)S(1)}, bf16[128,2048]{1,0:T(8,128)(2,1)S(1)}, u32[]{:S(2)}, u32[]{:S(2)}) collective-permute-start(bf16[128,2048]{1,0:T(8,128)(2,1)S(1)} %fusion), channel_id=1, source_target_pairs={{0,2},{1,3},{2,0},{3,1},{4,6},{5,7},{6,4},{7,5},{8,10},{9,11},{10,... | collective-permute-start | bytes 1572872 | tf_op jit(solution)/shard_map/ppermute | solution.py:22
  104.1 24.9 %collective-permute-start.24 = (bf16[1,256,1024]{2,1,0:T(8,128)(2,1)S(1)}, bf16[1,256,1024]{2,1,0:T(8,128)(2,1)S(1)}, u32[]{:S(2)}, u32[]{:S(2)}) collective-permute-start(bf16[1,256,1024]{2,1,0:T(8,128)(2,1)S(1)} %get-tuple-element.75), channel_id=1, source_target_pairs={{0,4},{4,0},{8,12},{12,8},{16,20},{20,16},{24,28},{28,24},{1,5},{5... | collective-permute-start | bytes 1572872 | tf_op jit(solution)/shard_map/ppermute | solution.py:22
  115.2 13.8 %collective-permute-start.21 = (bf16[1,128,1024]{2,1,0:T(8,128)(2,1)S(1)}, bf16[1,128,1024]{2,1,0:T(8,128)(2,1)S(1)}, u32[]{:S(2)}, u32[]{:S(2)}) collective-permute-start(bf16[1,128,1024]{2,1,0:T(8,128)(2,1)S(1)} %add_convert_fusion.2), channel_id=1, source_target_pairs={{0,16},{4,20},{8,24},{12,28},{16,0},{20,4},{24,8},{28,12},{1,17},{... | collective-permute-start | bytes 786440 | tf_op jit(solution)/shard_map/ppermute | solution.py:22
  (16 other events, 38.8 us)

commit v4 on v3

v4 whole, which is shorter than its diff:
```python
import functools

import jax
import jax.numpy as jnp
from jax import lax
from jax.experimental import pallas as pl
from jax.experimental.pallas import tpu as pltpu
from jax.sharding import PartitionSpec as P

LANES = 128


def wide(values):
    return values.astype(jnp.float32)


def narrow(values):
    return values.astype(jnp.bfloat16)


def flip(values, axis, bit):
    return lax.ppermute(values, axis, [(i, i ^ bit) for i in range(lax.axis_size(axis))])


def take(values, axis, index):
    return lax.dynamic_index_in_dim(values, index, axis, keepdims=False)


def with_routes(cotangent, expert_ids, gate_probs, expert_count):
    lane = jnp.arange(LANES, dtype=jnp.int32)[None, :]
    route = jnp.zeros((expert_ids.shape[0], LANES), jnp.float32)
    for k in range(expert_ids.shape[1]):
        hit = (lane < 3 * expert_count) & (lane // 3 == expert_ids[:, k : k + 1])
        route = route + jnp.where(hit, gate_probs[:, k : k + 1], 0.0)
    high = lax.reduce_precision(route, 8, 7)
    middle = lax.reduce_precision(route - high, 8, 7)
    low = (route - high) - middle
    part = lane % 3
    coded = jnp.where(part == 0, high, jnp.where(part == 1, middle, low))
    return jnp.concatenate([cotangent, narrow(coded)], axis=1)


def own_columns(values, group_count, parity):
    unit = values.shape[1] // group_count * 2
    blocks = [values[:, k * unit : (k + 1) * unit] for k in range(group_count // 2)]
    even, odd = jnp.concatenate(blocks[0::2], axis=1), jnp.concatenate(blocks[1::2], axis=1)
    return jnp.where(parity == 1, odd, even)


def expert_rows(place, group_count, ready, tok, cot, gate_up, down, scaled, back):
    width, units = gate_up.shape[0], down.shape[0]
    tile = units // 2
    lane = lax.broadcasted_iota(jnp.int32, (1, LANES), 1)
    coded = wide(cot[:, width:])
    part = [
        jnp.sum(jnp.where(lane == 3 * place[0] + k, coded, 0.0), axis=1, keepdims=True)
        for k in range(3)
    ]
    weight = (part[0] + part[1]) + part[2]
    scaled[...] = narrow(wide(cot[:, :width]) * weight)
    contract = (((1,), (1,)), ((), ()))
    hidden = []
    for k in range(2):
        lower, upper = slice(k * tile, (k + 1) * tile), slice(units + k * tile, units + (k + 1) * tile)
        ready(3 * k)
        gate = jnp.dot(tok[...], gate_up[:, lower], preferred_element_type=jnp.float32)
        ready(3 * k + 1)
        up = jnp.dot(tok[...], gate_up[:, upper], preferred_element_type=jnp.float32)
        sig = jax.nn.sigmoid(gate)
        activated = gate * sig
        hidden.append(narrow(activated * up))
        ready(3 * k + 2)
        back_hidden = lax.dot_general(
            scaled[...], down[lower, :], contract, preferred_element_type=jnp.float32
        )
        slope = up * sig * (1.0 + gate * (1.0 - sig))
        back[:, lower] = narrow(back_hidden * slope)
        back[:, upper] = narrow(back_hidden * activated)
    hid_cols = own_columns(jnp.concatenate(hidden, axis=1), group_count, place[1])
    return own_columns(tok[...], group_count, place[1]), hid_cols


ROWS = (((0,), (0,)), ((), ()))
FREE = pl.CostEstimate(flops=0, bytes_accessed=0, transcendentals=0)
HERE = pl.BlockSpec(memory_space=pl.ANY)
VMEM = pl.BlockSpec(memory_space=pltpu.VMEM)
SMEM = pl.BlockSpec(memory_space=pltpu.SMEM)


def hold(values, awaited):
    return pl.pallas_call(
        lambda *refs: None,
        out_shape=tuple(jax.ShapeDtypeStruct(v.shape, v.dtype) for v in values),
        in_specs=[HERE] * (len(values) + len(awaited)),
        out_specs=(HERE,) * len(values),
        input_output_aliases={k: k for k in range(len(values))},
        cost_estimate=FREE,
    )(*values, *awaited)


def weight_tiles(gate_up, down, gate_up_here, down_here):
    units = down.shape[0]
    tile = units // 2
    moves = []
    for k in range(2):
        for start in (k * tile, units + k * tile):
            here = (slice(None), slice(start, start + tile))
            moves.append((gate_up.at[here], gate_up_here.at[here]))
        here = (slice(k * tile, (k + 1) * tile), slice(None))
        moves.append((down.at[here], down_here.at[here]))
    return moves


def begin(moves, sems):
    copies = [pltpu.make_async_copy(src, dst, sems.at[k]) for k, (src, dst) in enumerate(moves)]
    for copy in copies:
        copy.start()
    return copies


def rows_in(pairs, tok_here, cot_here):
    moves, at = [], 0
    for tok_a, tok_b, cot_a, cot_b in pairs:
        for tok, cot in ((tok_a, cot_a), (tok_b, cot_b)):
            here = slice(at, at + tok.shape[0])
            moves += [(cot, cot_here.at[here, :]), (tok, tok_here.at[here, :])]
            at += tok.shape[0]
    return moves


def early_kernel(group_count, place, *refs):
    ins, (gate_sum, down_sum, back_group), scratch = refs[:14], refs[14:17], refs[17:]
    tok_here, cot_here, gate_up, down, scaled, back, sems = scratch
    rows = scaled.shape[0]
    arriving = rows_in([ins[4 * k : 4 * k + 4] for k in range(3)], tok_here, cot_here)
    tiles = weight_tiles(ins[12], ins[13], gate_up, down)
    copies = begin(arriving[:4] + tiles + arriving[4:], sems)
    pair_copies = [copies[:4], copies[10:14], copies[14:]]
    tile_copies = copies[4:10]
    for k in range(3):
        for copy in pair_copies[k]:
            copy.wait()
        here = slice(k * rows, (k + 1) * rows)
        back_here = back_group.at[here, :] if k < 2 else back
        tok_cols, hid_cols = expert_rows(
            place,
            group_count,
            (lambda i: tile_copies[i].wait()) if k == 0 else (lambda i: None),
            tok_here.at[here, :],
            cot_here.at[here, :],
            gate_up,
            down,
            scaled,
            back_here,
        )
        gate = lax.dot_general(tok_cols, back_here[...], ROWS, preferred_element_type=jnp.float32)
        down_part = lax.dot_general(hid_cols, scaled[...], ROWS, preferred_element_type=jnp.float32)
        gate_sum[...] = gate if k == 0 else gate_sum[...] + gate
        down_sum[...] = down_part if k == 0 else down_sum[...] + down_part


def early_terms(group_count, place, pairs, gate_up, down):
    rows, width = 2 * pairs[0][0].shape[0], pairs[0][0].shape[1]
    units, carried = down.shape[0], pairs[0][2].shape[1]
    shapes = [(3 * rows, width), (3 * rows, carried), gate_up.shape, down.shape]
    shapes += [(rows, width), (rows, 2 * units)]
    return pl.pallas_call(
        functools.partial(early_kernel, group_count),
        out_shape=(
            jax.ShapeDtypeStruct((width // 2, 2 * units), jnp.float32),
            jax.ShapeDtypeStruct((units // 2, width), jnp.float32),
            jax.ShapeDtypeStruct((2 * rows, 2 * units), jnp.bfloat16),
        ),
        in_specs=[SMEM] + [HERE] * 14,
        out_specs=(VMEM,) * 3,
        scratch_shapes=[pltpu.VMEM(shape, jnp.bfloat16) for shape in shapes]
        + [pltpu.SemaphoreType.DMA((18,))],
        compiler_params=pltpu.CompilerParams(vmem_limit_bytes=40 << 20),
        cost_estimate=FREE,
    )(place, *[v for pair in pairs for v in pair], gate_up, down)


def last_kernel(group_count, cuts, place, *refs):
    pair, (gate_up_in, down_in, gate_sum, hid_own, scaled) = refs[:4], refs[4:9]
    pieces, (tok_here, cot_here, gate_up, down, back, total, sems) = refs[9:-7], refs[-7:]
    arriving = rows_in([pair], tok_here, cot_here)
    tiles = weight_tiles(gate_up_in, down_in, gate_up, down)
    copies = begin(arriving + tiles + [(gate_sum, total)], sems)
    for copy in copies[:4]:
        copy.wait()
    tok_cols, hid_own[...] = expert_rows(
        place,
        group_count,
        lambda i: copies[4 + i].wait(),
        tok_here,
        cot_here,
        gate_up,
        down,
        scaled,
        back,
    )
    term = lax.dot_general(tok_cols, back[...], ROWS, preferred_element_type=jnp.float32)
    copies[10].wait()
    total[...] = total[...] + term
    bit0, bit2 = place[2], place[3]
    count = total.shape[0] // (group_count // 2)
    sides = ((1 - bit2, 1 - bit0), (1 - bit2, bit0), (bit2, 1 - bit0), (bit2, bit0))
    at = 0
    for (third, first), splits in zip(sides, (cuts, cuts, (0, count), (0, count))):
        for start, stop in zip(splits, splits[1:]):
            for high in range(group_count // 8):
                row = (high * 4 + third * 2 + first) * count + start
                row = pl.multiple_of(row, 8)
                pieces[at][high] = narrow(total[pl.ds(row, stop - start), :])
            at += 1


def last_terms(group_count, cuts, place, pair, gate_up, down, gate_sum):
    rows, width = 2 * pair[0].shape[0], pair[0].shape[1]
    units, high_count, count = down.shape[0], group_count // 8, cuts[-1]
    sizes = [b - a for a, b in zip(cuts, cuts[1:])] * 2 + [count] * 2
    shapes = [(rows, units // 2), (rows, width)]
    shapes += [(high_count, size, 2 * units) for size in sizes]
    inner = [(rows, width), (rows, pair[2].shape[1]), gate_up.shape, down.shape]
    inner += [(rows, 2 * units)]
    return pl.pallas_call(
        functools.partial(last_kernel, group_count, cuts),
        out_shape=tuple(jax.ShapeDtypeStruct(shape, jnp.bfloat16) for shape in shapes),
        in_specs=[SMEM] + [HERE] * 7,
        out_specs=(VMEM,) * len(shapes),
        scratch_shapes=[pltpu.VMEM(shape, jnp.bfloat16) for shape in inner]
        + [pltpu.VMEM(gate_sum.shape, jnp.float32), pltpu.SemaphoreType.DMA((11,))],
        compiler_params=pltpu.CompilerParams(vmem_limit_bytes=40 << 20),
        cost_estimate=FREE,
    )(place, *pair, gate_up, down, gate_sum)


def on_device(
    tokens, cotangent, expert_ids, gate_probs, gate_up_weight, down_weight, down_residual
):
    tok_rows, model_width = tokens.shape
    expert_count = lax.axis_size("expert")
    group_count = lax.axis_size("dp")
    gate_up, down_matrix = gate_up_weight[0], down_weight[0]
    hidden_units = down_matrix.shape[0]
    me, group = lax.axis_index("expert"), lax.axis_index("dp")
    bit0, bit1, bit2 = group & 1, (group >> 1) & 1, (group >> 2) & 1
    high_count = group_count // 8

    place = jnp.stack([me, bit1, bit0, bit2]).astype(jnp.int32)
    tok_x, tok_n = flip(tokens, "expert", 2), flip(tokens, "dp", 2)
    tok_c = flip(tokens, "expert", 1)
    carried = with_routes(cotangent, expert_ids, gate_probs, expert_count)
    cot_x, cot_n = flip(carried, "expert", 2), flip(carried, "dp", 2)
    cot_c = flip(carried, "expert", 1)
    residual = down_residual[0, 0].reshape(high_count, 2, 2, 2, -1, model_width)
    res_got = flip(take(residual, 3, 1 - bit0), "dp", 1)
    tok_x, tok_n, cot_x, cot_n, res_got = hold(
        (tok_x, tok_n, cot_x, cot_n, res_got), (tok_c, cot_c)
    )
    tok_d, cot_d = flip(tok_x, "dp", 2), flip(cot_n, "expert", 2)

    def both_cores(tok, cot):
        return tok, flip(tok, "expert", 1), cot, flip(cot, "expert", 1)

    pairs = ((tokens, tok_c, carried, cot_c), both_cores(tok_x, cot_x), both_cores(tok_n, cot_n))
    gate_sum, down_sum, back_group = early_terms(group_count, place, pairs, gate_up, down_matrix)
    res_pair = wide(take(residual, 3, bit0)) + wide(res_got)
    res_send = narrow(take(res_pair, 2, 1 - bit1))
    tok_d, cot_d, res_send = hold((tok_d, cot_d, res_send), (back_group,))
    count = model_width // group_count
    first = max(count // 4, 16)
    cuts = (0, first, count // 2, count) if first < count // 2 else (0, first, count)
    hid_cols, scaled, *gate_pieces = last_terms(
        group_count, cuts, place, both_cores(tok_d, cot_d), gate_up, down_matrix, gate_sum
    )
    down_term = lax.dot_general(hid_cols, scaled, ROWS, preferred_element_type=jnp.float32)
    down_term = narrow(down_sum + down_term).reshape(high_count, 2, 2, -1, model_width)

    parts = len(cuts) - 1
    far_sent, far_kept = gate_pieces[:parts], gate_pieces[parts : 2 * parts]
    near_sent, near_kept = gate_pieces[2 * parts :]
    got = [flip(piece, "dp", 1) for piece in far_sent]
    crossed = [
        flip(narrow(wide(kept) + wide(piece)), "dp", 4) for kept, piece in zip(far_kept, got)
    ]

    def down_side(third, side):
        return take(take(down_term, 1, third), 1, side)

    res_sum = take(res_pair, 2, bit1) + wide(flip(res_send, "dp", 2))
    down_sent = down_side(1 - bit2, 1 - bit0)
    got_down = flip(down_sent, "dp", 1)
    far_down = wide(down_side(1 - bit2, bit0)) + wide(got_down) + take(res_sum, 1, 1 - bit2)
    crossed_down = flip(narrow(far_down), "dp", 4)

    token_part = narrow(jnp.dot(back_group, gate_up.T, preferred_element_type=jnp.float32))
    blocks = token_part.reshape(expert_count, tok_rows, model_width)
    core = flip(jnp.stack([blocks[1], blocks[3]]), "expert", 1)
    across = flip(narrow(wide(blocks[2]) + wide(core[1])), "expert", 2)
    token_grad = narrow(wide(blocks[0]) + wide(core[0]) + wide(across))

    (near_sent,) = hold((near_sent,), (across,))
    near_gate = wide(near_kept) + wide(flip(near_sent, "dp", 1))
    down_sent = down_side(bit2, 1 - bit0)
    near_down = wide(down_side(bit2, bit0)) + wide(flip(down_sent, "dp", 1))
    factor = 1.0 / group_count
    gate_sum = (near_gate + wide(jnp.concatenate(crossed, axis=1))) * factor
    down_sum = (near_down + take(res_sum, 1, bit2) + wide(crossed_down)) * factor
    bit = 8
    while bit < group_count:
        side = (group // bit) & 1
        halves = [v.reshape(-1, 2, *v.shape[1:]) for v in (gate_sum, down_sum)]
        gate_sum, down_sum = [
            take(v, 1, side) + wide(flip(narrow(take(v, 1, 1 - side)), "dp", bit)) for v in halves
        ]
        bit *= 2
    return (token_grad, gate_sum, down_sum)


def solution(mesh):
    placed = (
        P(("dp", "expert"), None),
        P(("dp", "expert"), None),
        P(("dp", "expert"), None),
        P(("dp", "expert"), None),
        P("expert", None, None),
        P("expert", None, None),
        P("dp", "expert", None, None),
    )
    return jax.shard_map(
        on_device,
        mesh=mesh,
        in_specs=placed,
        out_specs=(P(("dp", "expert"), None), P("expert", "dp", None), P("expert", "dp", None)),
        check_vma=False,
    )
```

time: 131 us -> 140 us (1.069)
  local copies, waits for them, and re-layouts: 21.1 us -> 9.52 us
  Pallas kernels: 14.1 us -> 22.9 us
  other arithmetic: 6.81 us -> 14.4 us
  waiting for transfers between devices: 56.6 us -> 60.9 us
    unnamed x38 -> x62, local copies, waits for them, and re-layouts: 16.4 us -> 3.94 us
    pallas_call x1, Pallas kernels: 10 us -> 15.3 us  [early_terms(): pl.pallas_call(functools.partial(early_kernel, group_count), out_shape=(j...]
    squeeze x3 -> x1, local copies, waits for them, and re-layouts: 4.54 us -> 0.05 us  [take(): return lax.dynamic_index_in_dim(values, index, axis, keepdims=False)]
    ppermute x29 -> x28, waiting for transfers between devices: 56.6 us -> 60.9 us  [flip(): lax.ppermute(values, axis, [(i, i ^ bit) for i in range(lax.axis_size(axi...]
    pallas_call x1, Pallas kernels: 4.13 us -> 7.63 us  [last_terms(): pl.pallas_call(functools.partial(last_kernel, group_count, cuts), out_sha...]
    convert_element_type x9 -> x8, other arithmetic: 3.16 us -> 6.62 us  [narrow(): return values.astype(jnp.bfloat16)]
    dynamic_slice x0 -> x1, local copies, waits for them, and re-layouts: none -> 3.23 us  [take(): return lax.dynamic_index_in_dim(values, index, axis, keepdims=False)]
    add x1 -> x2, other arithmetic: 1.25 us -> 3.4 us  [the longest x1 2.05 us: on_device(): res_pair = wide(take(residual, 3, bit0)) + wide(res_got)]
  transfers between devices with their start and end apart: 29 -> 28, of which waited for: 10 -> 9; matrix products, arithmetic and copies ran while one was open for 8% -> 16% of each run, Pallas kernels for 8% -> 16%
where the time goes in v4:
time: 140 us
  waiting for transfers between devices  60.9 us (44%)
  starting transfers between devices  27 us (19%)
  Pallas kernels  22.9 us (16%)
  other arithmetic  14.4 us (10%)
  local copies, waits for them, and re-layouts  9.52 us (7%)
  matrix products  4.2 us (3%)
    ppermute x28, waiting for transfers between devices, flip(): lax.ppermute(values, axis, [(i, i ^ bit) for i in range(lax.axis_size(axi...  60.9 us
    ppermute x28, starting transfers between devices, flip(): lax.ppermute(values, axis, [(i, i ^ bit) for i in range(lax.axis_size(axi...  27 us
    pallas_call x1, Pallas kernels, early_terms(): pl.pallas_call(functools.partial(early_kernel, group_count), out_shape=(j...  15.3 us
    pallas_call x1, Pallas kernels, last_terms(): pl.pallas_call(functools.partial(last_kernel, group_count, cuts), out_sha...  7.63 us
    convert_element_type x8, other arithmetic, narrow(): return values.astype(jnp.bfloat16)  6.62 us
    unnamed x62, local copies, waits for them, and re-layouts  3.94 us
    dot_general x1, matrix products, on_device(): jnp.dot(back_group, gate_up.T, preferred_element_type=jnp.float32)  3.74 us
    dynamic_slice x1, local copies, waits for them, and re-layouts, take(): return lax.dynamic_index_in_dim(values, index, axis, keepdims=False)  3.23 us
  transfers between devices with their start and end apart: 28, of which 9 were waited for; matrix products, arithmetic and copies ran while one was open for 16% of the time, Pallas kernels for 16%

profile of v4, /device:TPU:0, one launch (start us, length us, event | category | flops | bytes accessed | tf_op | source)
XLA Modules:
  0.0 140.0 jit_solution(14608730091836037303)
XLA Ops:
  1.1 2.6 %collective-permute-start.2 = (bf16[128,2048]{1,0:T(8,128)(2,1)}, bf16[128,2048]{1,0:T(8,128)(2,1)}, u32[]{:S(2)}, u32[]{:S(2)}) collective-permute-start(bf16[128,2048]{1,0:T(8,128)(2,1)} %refs_0_.1), channel_id=1, source_target_pairs={{0,2},{1,3},{2,0},{3,1},{4,6},{5,7},{6,4},{7,5},{8,10},{9,11},{10,... | collective-permute-start | bytes 1572872 | tf_op jit(solution)/shard_map/ppermute | solution.py:22
  3.7 3.2 %constant_dynamic-slice_fusion = (bf16[1,2,2,1,64,2048]{5,4,3,2,1,0:T(8,128)(2,1)}, bf16[1,2,2,64,2048]{4,3,2,1,0:T(8,128)(2,1)}) fusion(bf16[1,2,2,2,64,2048]{5,4,3,2,1,0:T(8,128)(2,1)} %bitcast.67, s32[]{:T(128)S(6)} %select_n.90, s32[]{:T(128)S(6)} %select_n.89), kind=kLoop, calls=%fused_computation.36 | loop fusion | bytes 4194312 | tf_op jit(solution)/shard_map/jit(dynamic_index_in_dim)/dynamic_slice | solution.py:26
  7.0 1.5 %collective-permute-start.6 = (bf16[1,2,2,64,2048]{4,3,2,1,0:T(8,128)(2,1)}, bf16[1,2,2,64,2048]{4,3,2,1,0:T(8,128)(2,1)}, u32[]{:S(2)}, u32[]{:S(2)}) collective-permute-start(bf16[1,2,2,64,2048]{4,3,2,1,0:T(8,128)(2,1)} %get-tuple-element.46), channel_id=1, source_target_pairs={{0,4},{4,0},{8,12},{12,8},{16,20},{20,16},{24,28},{28,24},{1,5},{5... | collective-permute-start | bytes 3145736 | tf_op jit(solution)/shard_map/ppermute | solution.py:22
  9.4 1.6 %collective-permute-start.5 = (bf16[128,2176]{1,0:T(8,128)(2,1)S(1)}, bf16[128,2176]{1,0:T(8,128)(2,1)S(1)}, u32[]{:S(2)}, u32[]{:S(2)}) collective-permute-start(bf16[128,2176]{1,0:T(8,128)(2,1)S(1)} %pad_maximum_fusion.1.refs_2_), channel_id=1, source_target_pairs={{0,8},{4,12},{8,0},{12,4},{16,24},{20,28},{24,16},{28,20},{1,9},{5... | collective-permute-start | bytes 1671176 | tf_op jit(solution)/shard_map/ppermute | solution.py:22
  11.0 5.8 %collective-permute-done.2.refs_0_ = bf16[128,2048]{1,0:T(8,128)(2,1)} collective-permute-done((bf16[128,2048]{1,0:T(8,128)(2,1)}, bf16[128,2048]{1,0:T(8,128)(2,1)}, u32[]{:S(2)}, u32[]{:S(2)}) %collective-permute-start.2) | collective-permute-done | bytes 524320 | tf_op jit(solution)/shard_map/ppermute | solution.py:22
  16.8 2.0 %collective-permute-start.3 = (bf16[128,2048]{1,0:T(8,128)(2,1)S(1)}, bf16[128,2048]{1,0:T(8,128)(2,1)}, u32[]{:S(2)}, u32[]{:S(2)}) collective-permute-start(bf16[128,2048]{1,0:T(8,128)(2,1)S(1)} %copy-done.18), channel_id=1, source_target_pairs={{0,8},{4,12},{8,0},{12,4},{16,24},{20,28},{24,16},{28,20},{1,9},{5... | collective-permute-start | bytes 1572872 | tf_op jit(solution)/shard_map/ppermute | solution.py:22
  18.9 16.6 %collective-permute-done.3.refs_1_ = bf16[128,2048]{1,0:T(8,128)(2,1)} collective-permute-done((bf16[128,2048]{1,0:T(8,128)(2,1)S(1)}, bf16[128,2048]{1,0:T(8,128)(2,1)}, u32[]{:S(2)}, u32[]{:S(2)}) %collective-permute-start.3) | collective-permute-done | bytes 524320 | tf_op jit(solution)/shard_map/ppermute | solution.py:22
  36.7 1.5 %collective-permute-start.14 = (bf16[128,2176]{1,0:T(8,128)(2,1)}, bf16[128,2176]{1,0:T(8,128)(2,1)S(1)}, u32[]{:S(2)}, u32[]{:S(2)}) collective-permute-start(bf16[128,2176]{1,0:T(8,128)(2,1)} %get-tuple-element.27.refs_10_), channel_id=1, source_target_pairs={{0,2},{1,3},{2,0},{3,1},{4,6},{5,7},{6,4},{7,5},{8,10},{9,11},{10,... | collective-permute-start | bytes 1671176 | tf_op jit(solution)/shard_map/ppermute | solution.py:22
  38.9 2.0 %convert_add_fusion = f32[1,2,2,64,2048]{4,3,1,2,0:T(8,128)S(1)} fusion(bf16[1,2,2,1,64,2048]{5,4,3,2,1,0:T(8,128)(2,1)} %get-tuple-element.45, bf16[1,2,2,64,2048]{4,3,2,1,0:T(8,128)(2,1)} %get-tuple-element.29), kind=kLoop, calls=%fused_computation.1 | loop fusion | flops 1572864 | bytes 4194304 | tf_op jit(solution)/shard_map/add | solution.py:268
  41.0 0.9 fusion.3.refs_2_
  42.0 1.6 %collective-permute-start.13 = (bf16[128,2048]{1,0:T(8,128)(2,1)}, bf16[128,2048]{1,0:T(8,128)(2,1)S(1)}, u32[]{:S(2)}, u32[]{:S(2)}) collective-permute-start(bf16[128,2048]{1,0:T(8,128)(2,1)} %get-tuple-element.24.refs_4_), channel_id=1, source_target_pairs={{0,8},{4,12},{8,0},{12,4},{16,24},{20,28},{24,16},{28,20},{1,9},{5... | collective-permute-start | bytes 1572872 | tf_op jit(solution)/shard_map/ppermute | solution.py:22
  43.6 15.3 %shard_map.95 = (f32[1024,1024]{1,0:T(8,128)}, f32[256,2048]{1,0:T(8,128)S(1)}, bf16[512,1024]{1,0:T(8,128)(2,1)S(1)}) custom-call(s32[4]{0:T(128)S(1)} %pad_add_fusion.place, bf16[128,2048]{1,0:T(8,128)(2,1)S(1)} %copy-done.19, bf16[128,2048]{1,0:T(8,128)(2,1)S(1)} %copy-done.16, bf16[128,2176]{1,0:T(8,128)(2,1)S(1)} %pad_maximum_fusion.1.refs_2_, ...), custom_call_target="tpu_custom_call" | custom-call | tf_op jit(solution)/shard_map/pallas_call | solution.py:167
  58.9 3.7 %convolution_convert_fusion = bf16[512,2048]{1,0:T(8,128)(2,1)} fusion(bf16[512,1024]{1,0:T(8,128)(2,1)S(1)} %get-tuple-element.28.refs_3_, bf16[1,2048,1024]{2,1,0:T(8,128)(2,1)S(1)} %copy-done), kind=kOutput, calls=%fused_computation | convolution fusion | flops 2148532224 | bytes 7340032 | tf_op jit(solution)/shard_map/dot_general | solution.py:297
  65.2 1.3 slice_bitcast_fusion.3
  66.8 12.0 %collective-permute-done.25 = bf16[1,2,64,2048]{3,2,1,0:T(8,128)(2,1)S(1)} collective-permute-done((bf16[1,2,64,2048]{3,2,1,0:T(8,128)(2,1)}, bf16[1,2,64,2048]{3,2,1,0:T(8,128)(2,1)S(1)}, u32[]{:S(2)}, u32[]{:S(2)}) %collective-permute-start.25) | collective-permute-done | bytes 524320 | tf_op jit(solution)/shard_map/ppermute | solution.py:22
  78.8 1.4 bitcast_add_fusion
  80.2 7.6 %shard_map.97 = (bf16[256,256]{1,0:T(8,128)(2,1)S(1)}, bf16[256,2048]{1,0:T(8,128)(2,1)S(1)}, bf16[1,64,1024]{2,1,0:T(8,128)(2,1)S(1)}, bf16[1,64,1024]{2,1,0:T(...) custom-call(s32[4]{0:T(128)S(1)} %pad_add_fusion.place, ...), custom_call_target="tpu_custom_call" | custom-call | tf_op jit(solution)/shard_map/pallas_call | solution.py:226
  90.1 0.9 collective-permute-start.26
  90.9 1.2 collective-permute-start.24
  92.1 0.8 collective-permute-start.20
  92.9 1.1 collective-permute-done.18
  95.2 2.6 %collective-permute-start.19 = (bf16[1,64,1024]{2,1,0:T(8,128)(2,1)}, bf16[1,64,1024]{2,1,0:T(8,128)(2,1)S(1)}, u32[]{:S(2)}, u32[]{:S(2)}) collective-permute-start(bf16[1,64,1024]{2,1,0:T(8,128)(2,1)} %add_convert_fusion.3), channel_id=1, source_target_pairs={{0,16},{4,20},{8,24},{12,28},{16,0},{20,4},{24,8},{28,12},{1,17},{... | collective-permute-start | bytes 393224 | tf_op jit(solution)/shard_map/ppermute | solution.py:22
  97.8 1.2 fusion
  100.9 7.1 %collective-permute-done.20 = bf16[1,64,1024]{2,1,0:T(8,128)(2,1)S(1)} collective-permute-done((bf16[1,64,1024]{2,1,0:T(8,128)(2,1)S(1)}, bf16[1,64,1024]{2,1,0:T(8,128)(2,1)S(1)}, u32[]{:S(2)}, u32[]{:S(2)}) %collective-permute-start.20) | collective-permute-done | bytes 131104 | tf_op jit(solution)/shard_map/ppermute | solution.py:22
  108.0 2.6 %collective-permute-start.27 = (bf16[1,64,2048]{2,1,0:T(8,128)(2,1)}, bf16[1,64,2048]{2,1,0:T(8,128)(2,1)}, u32[]{:S(2)}, u32[]{:S(2)}) collective-permute-start(bf16[1,64,2048]{2,1,0:T(8,128)(2,1)} %fusion.5), channel_id=1, source_target_pairs={{0,16},{4,20},{8,24},{12,28},{16,0},{20,4},{24,8},{28,12},{1,17},{... | collective-permute-start | bytes 786440 | tf_op jit(solution)/shard_map/ppermute | solution.py:22
  111.3 1.3 collective-permute-done.22
  112.6 2.6 %collective-permute-start.21 = (bf16[1,64,1024]{2,1,0:T(8,128)(2,1)}, bf16[1,64,1024]{2,1,0:T(8,128)(2,1)}, u32[]{:S(2)}, u32[]{:S(2)}) collective-permute-start(bf16[1,64,1024]{2,1,0:T(8,128)(2,1)} %add_convert_fusion.2), channel_id=1, source_target_pairs={{0,16},{4,20},{8,24},{12,28},{16,0},{20,4},{24,8},{28,12},{1,17},{... | collective-permute-start | bytes 393224 | tf_op jit(solution)/shard_map/ppermute | solution.py:22
  117.4 12.2 %collective-permute-done.27 = bf16[1,64,2048]{2,1,0:T(8,128)(2,1)} collective-permute-done((bf16[1,64,2048]{2,1,0:T(8,128)(2,1)}, bf16[1,64,2048]{2,1,0:T(8,128)(2,1)}, u32[]{:S(2)}, u32[]{:S(2)}) %collective-permute-start.27) | collective-permute-done | bytes 262176 | tf_op jit(solution)/shard_map/ppermute | solution.py:22
  129.6 1.9 %fusion.8 = f32[1,64,2048]{2,1,0:T(8,128)} fusion(bf16[1,64,2048]{2,1,0:T(8,128)(2,1)} %collective-permute-done.27, f32[1,2,64,2048]{3,2,1,0:T(8,128)S(1)} %copy-done.23, s32[]{:T(128)S(6)} %select_n.92, bf16[1,64,2048]{2,1,0:T(8,128)(2,1)} %collective-permute-done.24, bf16[1,2,2,64,2048]{4,3,2,1,0:T(8,128)(2,1)S(1)} %bitcast.66, s32[]{:T(128)S(6)} %select_n.93, ...), kind=kLoop, calls=%fused_computation.26 | loop fusion | flops 917504 | bytes 1835020 | tf_op jit(solution)/shard_map/mul | solution.py:309
  131.5 2.1 %fusion.2 = bf16[128,2048]{1,0:T(8,128)(2,1)} fusion(bf16[128,2048]{1,0:T(8,128)(2,1)S(1)} %copy-done.25, bf16[2,128,2048]{2,1,0:T(8,128)(2,1)S(1)} %copy-done.27, bf16[512,2048]{1,0:T(8,128)(2,1)} %convolution_convert_fusion), kind=kLoop, calls=%fused_computation.9 | loop fusion | flops 1572864 | bytes 2097152 | tf_op jit(solution)/shard_map/convert_element_type | solution.py:18
  133.6 4.2 %collective-permute-done.23 = bf16[1,128,1024]{2,1,0:T(8,128)(2,1)} collective-permute-done((bf16[1,128,1024]{2,1,0:T(8,128)(2,1)}, bf16[1,128,1024]{2,1,0:T(8,128)(2,1)}, u32[]{:S(2)}, u32[]{:S(2)}) %collective-permute-start.23) | collective-permute-done | bytes 262176 | tf_op jit(solution)/shard_map/ppermute | solution.py:22
  137.8 2.2 %add_multiply_fusion = f32[1,256,1024]{2,1,0:T(8,128)} fusion(bf16[1,256,1024]{2,1,0:T(8,128)(2,1)S(1)} %collective-permute-done.17, bf16[1,256,1024]{2,1,0:T(8,128)(2,1)S(1)} %get-tuple-element.33, bf16[1,128,1024]{2,1,0:T(8,128)(2,1)} %collective-permute-done.23, bf16[1,64,1024]{2,1,0:T(8,128)(2,1)} %collective-permute-done.21, ...), kind=kLoop, calls=%fused_computation.11 | loop fusion | flops 2883584 | bytes 2621440 | tf_op jit(solution)/shard_map/mul | solution.py:308
  (117 shorter events, 14.3 us)
Async XLA Ops:
  0.6 8.8 %collective-permute-start = (bf16[128,2048]{1,0:T(8,128)(2,1)}, bf16[128,2048]{1,0:T(8,128)(2,1)S(1)}, u32[]{:S(2)}, u32[]{:S(2)}) collective-permute-start(bf16[128,2048]{1,0:T(8,128)(2,1)} %refs_0_.1), channel_id=1, source_target_pairs={{0,1},{1,0},{2,3},{3,2},{4,5},{5,4},{6,7},{7,6},{8,9},{9,8},{10,11... | collective-permute-start | bytes 1572872 | tf_op jit(solution)/shard_map/ppermute | solution.py:22
  1.1 15.7 %collective-permute-start.2 = (bf16[128,2048]{1,0:T(8,128)(2,1)}, bf16[128,2048]{1,0:T(8,128)(2,1)}, u32[]{:S(2)}, u32[]{:S(2)}) collective-permute-start(bf16[128,2048]{1,0:T(8,128)(2,1)} %refs_0_.1), channel_id=1, source_target_pairs={{0,2},{1,3},{2,0},{3,1},{4,6},{5,7},{6,4},{7,5},{8,10},{9,11},{10,... | collective-permute-start | bytes 1572872 | tf_op jit(solution)/shard_map/ppermute | solution.py:22
  7.0 28.6 %collective-permute-start.6 = (bf16[1,2,2,64,2048]{4,3,2,1,0:T(8,128)(2,1)}, bf16[1,2,2,64,2048]{4,3,2,1,0:T(8,128)(2,1)}, u32[]{:S(2)}, u32[]{:S(2)}) collective-permute-start(bf16[1,2,2,64,2048]{4,3,2,1,0:T(8,128)(2,1)} %get-tuple-element.46), channel_id=1, source_target_pairs={{0,4},{4,0},{8,12},{12,8},{16,20},{20,16},{24,28},{28,24},{1,5},{5... | collective-permute-start | bytes 3145736 | tf_op jit(solution)/shard_map/ppermute | solution.py:22
  8.8 26.7 %collective-permute-start.1 = (bf16[128,2176]{1,0:T(8,128)(2,1)S(1)}, bf16[128,2176]{1,0:T(8,128)(2,1)S(1)}, u32[]{:S(2)}, u32[]{:S(2)}) collective-permute-start(bf16[128,2176]{1,0:T(8,128)(2,1)S(1)} %pad_maximum_fusion.1.refs_2_), channel_id=1, source_target_pairs={{0,1},{1,0},{2,3},{3,2},{4,5},{5,4},{6,7},{7,6},{8,9},{9,8},{10,11... | collective-permute-start | bytes 1671176 | tf_op jit(solution)/shard_map/ppermute | solution.py:22
  8.8 26.7 %collective-permute-start.4 = (bf16[128,2176]{1,0:T(8,128)(2,1)S(1)}, bf16[128,2176]{1,0:T(8,128)(2,1)S(1)}, u32[]{:S(2)}, u32[]{:S(2)}) collective-permute-start(bf16[128,2176]{1,0:T(8,128)(2,1)S(1)} %pad_maximum_fusion.1.refs_2_), channel_id=1, source_target_pairs={{0,2},{1,3},{2,0},{3,1},{4,6},{5,7},{6,4},{7,5},{8,10},{9,11},{10,... | collective-permute-start | bytes 1671176 | tf_op jit(solution)/shard_map/ppermute | solution.py:22
  9.4 26.1 %copy-start.15 = (bf16[128,2048]{1,0:T(8,128)(2,1)}, bf16[128,2048]{1,0:T(8,128)(2,1)S(1)}, u32[]{:S(2)}) copy-start(bf16[128,2048]{1,0:T(8,128)(2,1)S(1)} %collective-permute-done.refs_5_.refs_1_) | copy-start | bytes 1572868
  9.4 26.1 %collective-permute-start.5 = (bf16[128,2176]{1,0:T(8,128)(2,1)S(1)}, bf16[128,2176]{1,0:T(8,128)(2,1)S(1)}, u32[]{:S(2)}, u32[]{:S(2)}) collective-permute-start(bf16[128,2176]{1,0:T(8,128)(2,1)S(1)} %pad_maximum_fusion.1.refs_2_), channel_id=1, source_target_pairs={{0,8},{4,12},{8,0},{12,4},{16,24},{20,28},{24,16},{28,20},{1,9},{5... | collective-permute-start | bytes 1671176 | tf_op jit(solution)/shard_map/ppermute | solution.py:22
  16.8 18.7 %collective-permute-start.3 = (bf16[128,2048]{1,0:T(8,128)(2,1)S(1)}, bf16[128,2048]{1,0:T(8,128)(2,1)}, u32[]{:S(2)}, u32[]{:S(2)}) collective-permute-start(bf16[128,2048]{1,0:T(8,128)(2,1)S(1)} %copy-done.18), channel_id=1, source_target_pairs={{0,8},{4,12},{8,0},{12,4},{16,24},{20,28},{24,16},{28,20},{1,9},{5... | collective-permute-start | bytes 1572872 | tf_op jit(solution)/shard_map/ppermute | solution.py:22
  36.7 6.9 %collective-permute-start.10 = (bf16[128,2176]{1,0:T(8,128)(2,1)}, bf16[128,2176]{1,0:T(8,128)(2,1)S(1)}, u32[]{:S(2)}, u32[]{:S(2)}) collective-permute-start(bf16[128,2176]{1,0:T(8,128)(2,1)} %get-tuple-element.27.refs_10_), channel_id=1, source_target_pairs={{0,1},{1,0},{2,3},{3,2},{4,5},{5,4},{6,7},{7,6},{8,9},{9,8},{10,11... | collective-permute-start | bytes 1671176 | tf_op jit(solution)/shard_map/ppermute | solution.py:22
  36.7 26.8 %collective-permute-start.14 = (bf16[128,2176]{1,0:T(8,128)(2,1)}, bf16[128,2176]{1,0:T(8,128)(2,1)S(1)}, u32[]{:S(2)}, u32[]{:S(2)}) collective-permute-start(bf16[128,2176]{1,0:T(8,128)(2,1)} %get-tuple-element.27.refs_10_), channel_id=1, source_target_pairs={{0,2},{1,3},{2,0},{3,1},{4,6},{5,7},{6,4},{7,5},{8,10},{9,11},{10,... | collective-permute-start | bytes 1671176 | tf_op jit(solution)/shard_map/ppermute | solution.py:22
  38.2 3.8 %collective-permute-start.7 = (bf16[128,2048]{1,0:T(8,128)(2,1)}, bf16[128,2048]{1,0:T(8,128)(2,1)S(1)}, u32[]{:S(2)}, u32[]{:S(2)}) collective-permute-start(bf16[128,2048]{1,0:T(8,128)(2,1)} %get-tuple-element.24.refs_4_), channel_id=1, source_target_pairs={{0,1},{1,0},{2,3},{3,2},{4,5},{5,4},{6,7},{7,6},{8,9},{9,8},{10,11... | collective-permute-start | bytes 1572872 | tf_op jit(solution)/shard_map/ppermute | solution.py:22
  38.4 5.1 %collective-permute-start.8 = (bf16[128,2176]{1,0:T(8,128)(2,1)}, bf16[128,2176]{1,0:T(8,128)(2,1)S(1)}, u32[]{:S(2)}, u32[]{:S(2)}) collective-permute-start(bf16[128,2176]{1,0:T(8,128)(2,1)} %get-tuple-element.25.refs_6_), channel_id=1, source_target_pairs={{0,1},{1,0},{2,3},{3,2},{4,5},{5,4},{6,7},{7,6},{8,9},{9,8},{10,11... | collective-permute-start | bytes 1671176 | tf_op jit(solution)/shard_map/ppermute | solution.py:22
  38.7 4.9 %collective-permute-start.9 = (bf16[128,2048]{1,0:T(8,128)(2,1)}, bf16[128,2048]{1,0:T(8,128)(2,1)S(1)}, u32[]{:S(2)}, u32[]{:S(2)}) collective-permute-start(bf16[128,2048]{1,0:T(8,128)(2,1)} %get-tuple-element.26.refs_8_), channel_id=1, source_target_pairs={{0,1},{1,0},{2,3},{3,2},{4,5},{5,4},{6,7},{7,6},{8,9},{9,8},{10,11... | collective-permute-start | bytes 1572872 | tf_op jit(solution)/shard_map/ppermute | solution.py:22
  42.0 20.7 %collective-permute-start.13 = (bf16[128,2048]{1,0:T(8,128)(2,1)}, bf16[128,2048]{1,0:T(8,128)(2,1)S(1)}, u32[]{:S(2)}, u32[]{:S(2)}) collective-permute-start(bf16[128,2048]{1,0:T(8,128)(2,1)} %get-tuple-element.24.refs_4_), channel_id=1, source_target_pairs={{0,8},{4,12},{8,0},{12,4},{16,24},{20,28},{24,16},{28,20},{1,9},{5... | collective-permute-start | bytes 1572872 | tf_op jit(solution)/shard_map/ppermute | solution.py:22
  64.3 15.9 %collective-permute-start.16 = (bf16[128,2176]{1,0:T(8,128)(2,1)}, bf16[128,2176]{1,0:T(8,128)(2,1)S(1)}, u32[]{:S(2)}, u32[]{:S(2)}) collective-permute-start(bf16[128,2176]{1,0:T(8,128)(2,1)} %get-tuple-element.31.refs_2_), channel_id=1, source_target_pairs={{0,1},{1,0},{2,3},{3,2},{4,5},{5,4},{6,7},{7,6},{8,9},{9,8},{10,11... | collective-permute-start | bytes 1671176 | tf_op jit(solution)/shard_map/ppermute | solution.py:22
  64.3 15.9 %collective-permute-start.15 = (bf16[128,2048]{1,0:T(8,128)(2,1)}, bf16[128,2048]{1,0:T(8,128)(2,1)S(1)}, u32[]{:S(2)}, u32[]{:S(2)}) collective-permute-start(bf16[128,2048]{1,0:T(8,128)(2,1)} %get-tuple-element.30.refs_0_), channel_id=1, source_target_pairs={{0,1},{1,0},{2,3},{3,2},{4,5},{5,4},{6,7},{7,6},{8,9},{9,8},{10,11... | collective-permute-start | bytes 1572872 | tf_op jit(solution)/shard_map/ppermute | solution.py:22
  64.8 14.0 %collective-permute-start.25 = (bf16[1,2,64,2048]{3,2,1,0:T(8,128)(2,1)}, bf16[1,2,64,2048]{3,2,1,0:T(8,128)(2,1)S(1)}, u32[]{:S(2)}, u32[]{:S(2)}) collective-permute-start(bf16[1,2,64,2048]{3,2,1,0:T(8,128)(2,1)} %get-tuple-element.44), channel_id=1, source_target_pairs={{0,8},{4,12},{8,0},{12,4},{16,24},{20,28},{24,16},{28,20},{1,9},{5... | collective-permute-start | bytes 1572872 | tf_op jit(solution)/shard_map/ppermute | solution.py:22
  66.7 28.5 %collective-permute-start.11 = (bf16[2,128,2048]{2,1,0:T(8,128)(2,1)S(1)}, bf16[2,128,2048]{2,1,0:T(8,128)(2,1)S(1)}, u32[]{:S(2)}, u32[]{:S(2)}) collective-permute-start(bf16[2,128,2048]{2,1,0:T(8,128)(2,1)S(1)} %pad_maximum_fusion), channel_id=1, source_target_pairs={{0,1},{1,0},{2,3},{3,2},{4,5},{5,4},{6,7},{7,6},{8,9},{9,8},{10,11... | collective-permute-start | bytes 3145736 | tf_op jit(solution)/shard_map/ppermute | solution.py:22
  80.2 20.0 %copy-start.22 = (f32[1,2,64,2048]{3,2,1,0:T(8,128)}, f32[1,2,64,2048]{3,2,1,0:T(8,128)S(1)}, u32[]{:S(2)}) copy-start(f32[1,2,64,2048]{3,2,1,0:T(8,128)S(1)} %bitcast_add_fusion) | copy-start | bytes 3145732
  87.9 6.1 %collective-permute-start.18 = (bf16[1,64,1024]{2,1,0:T(8,128)(2,1)S(1)}, bf16[1,64,1024]{2,1,0:T(8,128)(2,1)S(1)}, u32[]{:S(2)}, u32[]{:S(2)}) collective-permute-start(bf16[1,64,1024]{2,1,0:T(8,128)(2,1)S(1)} %get-tuple-element.36), channel_id=1, source_target_pairs={{0,4},{4,0},{8,12},{12,8},{16,20},{20,16},{24,28},{28,24},{1,5},{5... | collective-permute-start | bytes 393224 | tf_op jit(solution)/shard_map/ppermute | solution.py:22
  90.1 9.6 %collective-permute-start.26 = (bf16[1,64,2048]{2,1,0:T(8,128)(2,1)S(1)}, bf16[1,64,2048]{2,1,0:T(8,128)(2,1)S(1)}, u32[]{:S(2)}, u32[]{:S(2)}) collective-permute-start(bf16[1,64,2048]{2,1,0:T(8,128)(2,1)S(1)} %get-tuple-element.50), channel_id=1, source_target_pairs={{0,4},{4,0},{8,12},{12,8},{16,20},{20,16},{24,28},{28,24},{1,5},{5... | collective-permute-start | bytes 786440 | tf_op jit(solution)/shard_map/ppermute | solution.py:22
  90.9 25.9 %collective-permute-start.24 = (bf16[1,64,2048]{2,1,0:T(8,128)(2,1)S(1)}, bf16[1,64,2048]{2,1,0:T(8,128)(2,1)}, u32[]{:S(2)}, u32[]{:S(2)}) collective-permute-start(bf16[1,64,2048]{2,1,0:T(8,128)(2,1)S(1)} %get-tuple-element.49), channel_id=1, source_target_pairs={{0,4},{4,0},{8,12},{12,8},{16,20},{20,16},{24,28},{28,24},{1,5},{5... | collective-permute-start | bytes 786440 | tf_op jit(solution)/shard_map/ppermute | solution.py:22
  92.1 15.9 %collective-permute-start.20 = (bf16[1,64,1024]{2,1,0:T(8,128)(2,1)S(1)}, bf16[1,64,1024]{2,1,0:T(8,128)(2,1)S(1)}, u32[]{:S(2)}, u32[]{:S(2)}) collective-permute-start(bf16[1,64,1024]{2,1,0:T(8,128)(2,1)S(1)} %get-tuple-element.38), channel_id=1, source_target_pairs={{0,4},{4,0},{8,12},{12,8},{16,20},{20,16},{24,28},{28,24},{1,5},{5... | collective-permute-start | bytes 393224 | tf_op jit(solution)/shard_map/ppermute | solution.py:22
  94.0 18.6 %collective-permute-start.22 = (bf16[1,128,1024]{2,1,0:T(8,128)(2,1)S(1)}, bf16[1,128,1024]{2,1,0:T(8,128)(2,1)S(1)}, u32[]{:S(2)}, u32[]{:S(2)}) collective-permute-start(bf16[1,128,1024]{2,1,0:T(8,128)(2,1)S(1)} %get-tuple-element.40), channel_id=1, source_target_pairs={{0,4},{4,0},{8,12},{12,8},{16,20},{20,16},{24,28},{28,24},{1,5},{5... | collective-permute-start | bytes 786440 | tf_op jit(solution)/shard_map/ppermute | solution.py:22
  95.2 20.8 %copy-start.26 = (bf16[2,128,2048]{2,1,0:T(8,128)(2,1)}, bf16[2,128,2048]{2,1,0:T(8,128)(2,1)S(1)}, u32[]{:S(2)}) copy-start(bf16[2,128,2048]{2,1,0:T(8,128)(2,1)S(1)} %collective-permute-done.11) | copy-start | bytes 3145732
  95.2 38.4 %collective-permute-start.19 = (bf16[1,64,1024]{2,1,0:T(8,128)(2,1)}, bf16[1,64,1024]{2,1,0:T(8,128)(2,1)S(1)}, u32[]{:S(2)}, u32[]{:S(2)}) collective-permute-start(bf16[1,64,1024]{2,1,0:T(8,128)(2,1)} %add_convert_fusion.3), channel_id=1, source_target_pairs={{0,16},{4,20},{8,24},{12,28},{16,0},{20,4},{24,8},{28,12},{1,17},{... | collective-permute-start | bytes 393224 | tf_op jit(solution)/shard_map/ppermute | solution.py:22
  99.6 16.4 %collective-permute-start.12 = (bf16[128,2048]{1,0:T(8,128)(2,1)S(1)}, bf16[128,2048]{1,0:T(8,128)(2,1)S(1)}, u32[]{:S(2)}, u32[]{:S(2)}) collective-permute-start(bf16[128,2048]{1,0:T(8,128)(2,1)S(1)} %fusion), channel_id=1, source_target_pairs={{0,2},{1,3},{2,0},{3,1},{4,6},{5,7},{6,4},{7,5},{8,10},{9,11},{10,... | collective-permute-start | bytes 1572872 | tf_op jit(solution)/shard_map/ppermute | solution.py:22
  100.9 28.6 %copy-start.23 = (f32[1,2,64,2048]{3,2,1,0:T(8,128)S(1)}, f32[1,2,64,2048]{3,2,1,0:T(8,128)}, u32[]{:S(2)}) copy-start(f32[1,2,64,2048]{3,2,1,0:T(8,128)} %copy-done.22) | copy-start | bytes 3145732
  108.0 21.5 %collective-permute-start.27 = (bf16[1,64,2048]{2,1,0:T(8,128)(2,1)}, bf16[1,64,2048]{2,1,0:T(8,128)(2,1)}, u32[]{:S(2)}, u32[]{:S(2)}) collective-permute-start(bf16[1,64,2048]{2,1,0:T(8,128)(2,1)} %fusion.5), channel_id=1, source_target_pairs={{0,16},{4,20},{8,24},{12,28},{16,0},{20,4},{24,8},{28,12},{1,17},{... | collective-permute-start | bytes 786440 | tf_op jit(solution)/shard_map/ppermute | solution.py:22
  112.6 21.0 %collective-permute-start.21 = (bf16[1,64,1024]{2,1,0:T(8,128)(2,1)}, bf16[1,64,1024]{2,1,0:T(8,128)(2,1)}, u32[]{:S(2)}, u32[]{:S(2)}) collective-permute-start(bf16[1,64,1024]{2,1,0:T(8,128)(2,1)} %add_convert_fusion.2), channel_id=1, source_target_pairs={{0,16},{4,20},{8,24},{12,28},{16,0},{20,4},{24,8},{28,12},{1,17},{... | collective-permute-start | bytes 393224 | tf_op jit(solution)/shard_map/ppermute | solution.py:22
  116.0 21.8 %collective-permute-start.23 = (bf16[1,128,1024]{2,1,0:T(8,128)(2,1)}, bf16[1,128,1024]{2,1,0:T(8,128)(2,1)}, u32[]{:S(2)}, u32[]{:S(2)}) collective-permute-start(bf16[1,128,1024]{2,1,0:T(8,128)(2,1)} %add_convert_fusion.1), channel_id=1, source_target_pairs={{0,16},{4,20},{8,24},{12,28},{16,0},{20,4},{24,8},{28,12},{1,17},{... | collective-permute-start | bytes 786440 | tf_op jit(solution)/shard_map/ppermute | solution.py:22
  116.8 21.0 %collective-permute-start.17 = (bf16[1,256,1024]{2,1,0:T(8,128)(2,1)}, bf16[1,256,1024]{2,1,0:T(8,128)(2,1)S(1)}, u32[]{:S(2)}, u32[]{:S(2)}) collective-permute-start(bf16[1,256,1024]{2,1,0:T(8,128)(2,1)} %shard_map.98), channel_id=1, source_target_pairs={{0,4},{4,0},{8,12},{12,8},{16,20},{20,16},{24,28},{28,24},{1,5},{5... | collective-permute-start | bytes 1572872 | tf_op jit(solution)/shard_map/ppermute | solution.py:22
  (27 other events, 177.4 us)

commit v5 on v2

--- a/solution.py
+++ b/solution.py
@@ -95,8 +95,50 @@
         in_specs=[pl.BlockSpec(memory_space=pltpu.SMEM)] + [vmem] * 6,
         out_specs=(vmem,) * 4,
         compiler_params=pltpu.CompilerParams(vmem_limit_bytes=24 << 20),
-        cost_estimate=pl.CostEstimate(flops=0, bytes_accessed=0, transcendentals=0),
+        cost_estimate=FREE,
     )(place, tok_a, tok_b, cot_a, cot_b, gate_up, down)
+
+
+ROWS = (((0,), (0,)), ((), ()))
+FREE = pl.CostEstimate(flops=0, bytes_accessed=0, transcendentals=0)
+
+
+def hold(values, awaited):
+    here = pl.BlockSpec(memory_space=pl.ANY)
+    return pl.pallas_call(
+        lambda *refs: None,
+        out_shape=tuple(jax.ShapeDtypeStruct(v.shape, v.dtype) for v in values),
+        in_specs=[here] * (len(values) + len(awaited)),
+        out_specs=(here,) * len(values),
+        input_output_aliases={k: k for k in range(len(values))},
+        cost_estimate=FREE,
+    )(*values, *awaited)
+
+
+def terms_kernel(*refs):
+    blocks, (gate_sum, down_sum) = refs[:-2], refs[-2:]
+    for at in range(0, len(blocks), 4):
+        tok_cols, hid_cols, scaled, back = [block[...] for block in blocks[at : at + 4]]
+        gate = lax.dot_general(tok_cols, back, ROWS, preferred_element_type=jnp.float32)
+        down = lax.dot_general(hid_cols, scaled, ROWS, preferred_element_type=jnp.float32)
+        gate_sum[...] = gate if at == 0 else gate_sum[...] + gate
+        down_sum[...] = down if at == 0 else down_sum[...] + down
+
+
+def early_terms(made):
+    tok_cols, hid_cols, scaled, back = made[0]
+    vmem = pl.BlockSpec(memory_space=pltpu.VMEM)
+    return pl.pallas_call(
+        terms_kernel,
+        out_shape=(
+            jax.ShapeDtypeStruct((tok_cols.shape[1], back.shape[1]), jnp.float32),
+            jax.ShapeDtypeStruct((hid_cols.shape[1], scaled.shape[1]), jnp.float32),
+        ),
+        in_specs=[vmem] * (4 * len(made)),
+        out_specs=(vmem, vmem),
+        compiler_params=pltpu.CompilerParams(vmem_limit_bytes=24 << 20),
+        cost_estimate=FREE,
+    )(*[v for block in made for v in block])
 
 
 def on_device(
@@ -118,10 +160,6 @@
     cot_c = flip(carried, "expert", 1)
     residual = down_residual[0, 0].reshape(high_count, 2, 2, 2, -1, model_width)
     res_got = flip(take(residual, 3, 1 - bit0), "dp", 1)
-    tok_x, tok_n, tok_c, cot_x, cot_n, cot_c, res_got, tok_own, cot_own = lax.optimization_barrier(
-        (tok_x, tok_n, tok_c, cot_x, cot_n, cot_c, res_got, tokens, carried)
-    )
-    tok_d, cot_d = flip(tok_x, "dp", 2), flip(cot_n, "expert", 2)
     place = jnp.stack([me, bit1]).astype(jnp.int32)
 
     def expert_on(tok, tok_other, cot, cot_other):
@@ -132,20 +170,20 @@
     def both_cores(tok, cot):
         return expert_on(tok, flip(tok, "expert", 1), cot, flip(cot, "expert", 1))
 
-    made = [expert_on(tok_own, tok_c, cot_own, cot_c)]
+    tok_x, tok_n, cot_x, cot_n, res_got, place = hold(
+        (tok_x, tok_n, cot_x, cot_n, res_got, place), (tok_c, cot_c)
+    )
+    tok_d, cot_d = flip(tok_x, "dp", 2), flip(cot_n, "expert", 2)
+    made = [expert_on(tokens, tok_c, carried, cot_c)]
     made += [both_cores(tok_x, cot_x), both_cores(tok_n, cot_n)]
+    gate_early, down_early = early_terms(made)
+    tok_d, cot_d, *back_group = hold((tok_d, cot_d, made[0][3], made[1][3]), (gate_early,))
 
     def terms(tok_cols, hid_cols, scaled, back):
-        contract = (((0,), (0,)), ((), ()))
-        gate = lax.dot_general(tok_cols, back, contract, preferred_element_type=jnp.float32)
-        down = lax.dot_general(hid_cols, scaled, contract, preferred_element_type=jnp.float32)
+        gate = lax.dot_general(tok_cols, back, ROWS, preferred_element_type=jnp.float32)
+        down = lax.dot_general(hid_cols, scaled, ROWS, preferred_element_type=jnp.float32)
         return gate, down
 
-    early = [jnp.concatenate(v, axis=0) for v in zip(*made)]
-    gate_early, down_early = terms(*early)
-    tok_d, cot_d, gate_early, down_early = lax.optimization_barrier(
-        (tok_d, cot_d, gate_early, down_early)
-    )
     gate_late, down_late = terms(*both_cores(tok_d, cot_d))
     gate_term = narrow(gate_early + gate_late).reshape(high_count, 2, 2, -1, 2 * hidden_units)
     down_term = narrow(down_early + down_late).reshape(high_count, 2, 2, -1, model_width)
@@ -174,13 +212,15 @@
     crossed = [flip(narrow(piece), "dp", 4) for piece, _ in far]
     crossed_down = flip(narrow(far_down), "dp", 4)
 
-    back_group = jnp.concatenate([made[0][3], made[1][3]], axis=0)
-    back_group, _ = lax.optimization_barrier((back_group, far[0][1]))
-    token_part = narrow(jnp.dot(back_group, gate_up.T, preferred_element_type=jnp.float32))
-    blocks = token_part.reshape(expert_count, tok_rows, model_width)
-    core = flip(jnp.stack([blocks[1], blocks[3]]), "expert", 1)
-    across = flip(narrow(wide(blocks[2]) + wide(core[1])), "expert", 2)
-    token_grad = narrow(wide(blocks[0]) + wide(core[0]) + wide(across))
+    def input_part(start):
+        rows = [back[start : start + tok_rows] for back in back_group]
+        part = jnp.dot(jnp.concatenate(rows), gate_up.T, preferred_element_type=jnp.float32)
+        return narrow(part)
+
+    core = flip(input_part(tok_rows), "expert", 1)
+    total = wide(input_part(0)) + wide(core)
+    across = flip(narrow(total[tok_rows:]), "expert", 2)
+    token_grad = narrow(total[:tok_rows] + wide(across))
 
     near_gate, _ = paired(gate_term, bit2, far[2][1])
     near_down, _ = paired(down_term, bit2, (got_down, token_grad))

time: 116 us -> 124 us (1.069)
  local copies, waits for them, and re-layouts: 11.2 us -> 16.5 us
  waiting for transfers between devices: 54.7 us -> 50.9 us
  Pallas kernels: 11.8 us -> 15.2 us
  starting transfers between devices: 24.9 us -> 27.1 us
    ppermute x28, waiting for transfers between devices: 54.7 us -> 50.9 us  [flip(): lax.ppermute(values, axis, [(i, i ^ bit) for i in range(lax.axis_size(axi...]
    dynamic_slice x2 -> x0, local copies, waits for them, and re-layouts: 2.82 us -> none  [take(): return lax.dynamic_index_in_dim(values, index, axis, keepdims=False)]
    unnamed x30 -> x52, local copies, waits for them, and re-layouts: 7.95 us -> 10.7 us
    pallas_call x0 -> x3, Pallas kernels: none -> 2.65 us  [the longest x1 2.65 us: early_terms(): pl.pallas_call(terms_kernel, out_shape=(jax.ShapeDtypeStruct((tok_cols.sh...]
    squeeze x5 -> x6, local copies, waits for them, and re-layouts: 0.14 us -> 2.45 us  [take(): return lax.dynamic_index_in_dim(values, index, axis, keepdims=False)]
    ppermute x28, starting transfers between devices: 24.9 us -> 27.1 us  [flip(): lax.ppermute(values, axis, [(i, i ^ bit) for i in range(lax.axis_size(axi...]
    slice x1 -> x3, local copies, waits for them, and re-layouts: 0.07 us -> 2.19 us  [the longest x2 2.13 us: input_part(): rows = [back[start:start + tok_rows] for back in back_group]]
    convert_element_type x9 -> x7, other arithmetic: 3.16 us -> 1.6 us  [narrow(): return values.astype(jnp.bfloat16)]
  transfers between devices with their start and end apart: 28 -> 28, of which waited for: 12 -> 8; matrix products, arithmetic and copies ran while one was open for 11% -> 14% of each run, Pallas kernels for 8% -> 12%
where the time goes in v5:
time: 124 us
  waiting for transfers between devices  50.9 us (41%)
  starting transfers between devices  27.1 us (22%)
  local copies, waits for them, and re-layouts  16.5 us (13%)
  Pallas kernels  15.2 us (12%)
  other arithmetic  6.91 us (6%)
  matrix products  6.13 us (5%)
    ppermute x28, waiting for transfers between devices, flip(): lax.ppermute(values, axis, [(i, i ^ bit) for i in range(lax.axis_size(axi...  50.9 us
    ppermute x28, starting transfers between devices, flip(): lax.ppermute(values, axis, [(i, i ^ bit) for i in range(lax.axis_size(axi...  27.1 us
    pallas_call x4, Pallas kernels, expert_rows(): pl.pallas_call(functools.partial(expert_kernel, group_count), out_shape=t...  12.5 us
    unnamed x52, local copies, waits for them, and re-layouts  10.7 us
    dot_general x2, matrix products, input_part(): jnp.dot(jnp.concatenate(rows), gate_up.T, preferred_element_type=jnp.floa...  4.93 us
    pallas_call x1, Pallas kernels, early_terms(): pl.pallas_call(terms_kernel, out_shape=(jax.ShapeDtypeStruct((tok_cols.sh...  2.65 us
  transfers between devices with their start and end apart: 28, of which 8 were waited for; matrix products, arithmetic and copies ran while one was open for 14% of the time, Pallas kernels for 12%

profile of v5, /device:TPU:0, one launch (start us, length us, event | category | flops | bytes accessed | tf_op | source)
XLA Modules:
  0.0 123.9 jit_solution(10706171432180184280)
XLA Ops:
  1.2 2.6 %collective-permute-start = (bf16[128,2048]{1,0:T(8,128)(2,1)}, bf16[128,2048]{1,0:T(8,128)(2,1)S(1)}, u32[]{:S(2)}, u32[]{:S(2)}) collective-permute-start(bf16[128,2048]{1,0:T(8,128)(2,1)} %tok_a.1), channel_id=1, source_target_pairs={{0,2},{1,3},{2,0},{3,1},{4,6},{5,7},{6,4},{7,5},{8,10},{9,11},{10,... | collective-permute-start | bytes 1572872 | tf_op jit(solution)/shard_map/ppermute | solution.py:22
  3.7 2.3 %dynamic-slice_bitcast_fusion = bf16[1,2,2,64,2048]{4,3,2,1,0:T(8,128)(2,1)} fusion(bf16[1,2,2,2,64,2048]{5,4,3,2,1,0:T(8,128)(2,1)} %bitcast.83, s32[]{:T(128)S(6)} %select_n.105), kind=kLoop, calls=%fused_computation.15 | loop fusion | bytes 2097156 | tf_op jit(solution)/shard_map/jit(dynamic_index_in_dim)/squeeze | solution.py:26
  6.0 1.5 %collective-permute-start.4 = (bf16[1,2,2,64,2048]{4,3,2,1,0:T(8,128)(2,1)}, bf16[1,2,2,64,2048]{4,3,2,1,0:T(8,128)(2,1)}, u32[]{:S(2)}, u32[]{:S(2)}) collective-permute-start(bf16[1,2,2,64,2048]{4,3,2,1,0:T(8,128)(2,1)} %dynamic-slice_bitcast_fusion), channel_id=1, source_target_pairs={{0,4},{4,0},{8,12},{12,8},{16,20},{20,16},{24,28},{28,24},{1,5},{5... | collective-permute-start | bytes 3145736 | tf_op jit(solution)/shard_map/ppermute | solution.py:22
  9.2 1.6 %collective-permute-start.3 = (bf16[128,2176]{1,0:T(8,128)(2,1)}, bf16[128,2176]{1,0:T(8,128)(2,1)}, u32[]{:S(2)}, u32[]{:S(2)}) collective-permute-start(bf16[128,2176]{1,0:T(8,128)(2,1)} %pad_maximum_fusion.cot_a), channel_id=1, source_target_pairs={{0,8},{4,12},{8,0},{12,4},{16,24},{20,28},{24,16},{28,20},{1,9},{5... | collective-permute-start | bytes 1671176 | tf_op jit(solution)/shard_map/ppermute | solution.py:22
  10.8 6.0 %collective-permute-done.refs_0_ = bf16[128,2048]{1,0:T(8,128)(2,1)S(1)} collective-permute-done((bf16[128,2048]{1,0:T(8,128)(2,1)}, bf16[128,2048]{1,0:T(8,128)(2,1)S(1)}, u32[]{:S(2)}, u32[]{:S(2)}) %collective-permute-start) | collective-permute-done | bytes 524320 | tf_op jit(solution)/shard_map/ppermute | solution.py:22
  16.7 2.0 %collective-permute-start.1 = (bf16[128,2048]{1,0:T(8,128)(2,1)}, bf16[128,2048]{1,0:T(8,128)(2,1)}, u32[]{:S(2)}, u32[]{:S(2)}) collective-permute-start(bf16[128,2048]{1,0:T(8,128)(2,1)} %tok_a.1), channel_id=1, source_target_pairs={{0,8},{4,12},{8,0},{12,4},{16,24},{20,28},{24,16},{28,20},{1,9},{5... | collective-permute-start | bytes 1572872 | tf_op jit(solution)/shard_map/ppermute | solution.py:22
  19.4 16.1 %collective-permute-done.1.refs_1_ = bf16[128,2048]{1,0:T(8,128)(2,1)} collective-permute-done((bf16[128,2048]{1,0:T(8,128)(2,1)}, bf16[128,2048]{1,0:T(8,128)(2,1)}, u32[]{:S(2)}, u32[]{:S(2)}) %collective-permute-start.1) | collective-permute-done | bytes 524320 | tf_op jit(solution)/shard_map/ppermute | solution.py:22
  36.8 1.5 %collective-permute-start.8 = (bf16[128,2176]{1,0:T(8,128)(2,1)}, bf16[128,2176]{1,0:T(8,128)(2,1)}, u32[]{:S(2)}, u32[]{:S(2)}) collective-permute-start(bf16[128,2176]{1,0:T(8,128)(2,1)} %get-tuple-element.36.cot_a), channel_id=1, source_target_pairs={{0,2},{1,3},{2,0},{3,1},{4,6},{5,7},{6,4},{7,5},{8,10},{9,11},{10,... | collective-permute-start | bytes 1671176 | tf_op jit(solution)/shard_map/ppermute | solution.py:22
  38.3 1.6 %collective-permute-start.7 = (bf16[128,2048]{1,0:T(8,128)(2,1)}, bf16[128,2048]{1,0:T(8,128)(2,1)S(1)}, u32[]{:S(2)}, u32[]{:S(2)}) collective-permute-start(bf16[128,2048]{1,0:T(8,128)(2,1)} %get-tuple-element.35.tok_a), channel_id=1, source_target_pairs={{0,8},{4,12},{8,0},{12,4},{16,24},{20,28},{24,16},{28,20},{1,9},{5... | collective-permute-start | bytes 1572872 | tf_op jit(solution)/shard_map/ppermute | solution.py:22
  39.9 2.2 %copy-done = bf16[1,2048,1024]{2,1,0:T(8,128)(2,1)S(1)} copy-done((bf16[1,2048,1024]{2,1,0:T(8,128)(2,1)S(1)}, bf16[1,2048,1024]{2,1,0:T(8,128)(2,1)}, u32[]{:S(2)}) %copy-start) | copy-done | bytes 4194328
  44.8 3.2 %shard_map.95 = (bf16[256,1024]{1,0:T(8,128)(2,1)S(1)}, bf16[256,256]{1,0:T(8,128)(2,1)S(1)}, bf16[256,2048]{1,0:T(8,128)(2,1)S(1)}, bf16[256,1024]{1,0:T(8,128)(2,1)S(1)}) custom-call(s32[2]{0:T(128)S(1)} %copy-done.17, bf16[128,2048]{1,0:T(8,128)(2,1)} %tok_a.1, bf16[128,2048]{1,0:T(8,128)(2,1)S(1)} %copy-done.10, ...), custom_call_target="tpu_custom_call" | custom-call | tf_op jit(solution)/shard_map/pallas_call | solution.py:92
  48.4 1.6 %convert_add_fusion = f32[1,2,2,64,2048]{4,3,2,1,0:T(8,128)S(1)} fusion(bf16[1,2,2,64,2048]{4,3,2,1,0:T(8,128)(2,1)} %get-tuple-element.65, bf16[1,2,2,2,64,2048]{5,4,3,2,1,0:T(8,128)(2,1)S(1)} %bitcast.84, s32[]{:T(128)S(6)} %select_n.108), kind=kLoop, calls=%fused_computation.4 | loop fusion | flops 1572864 | bytes 4194308 | tf_op jit(solution)/shard_map/add | solution.py:191
  51.5 3.1 %shard_map.97 = (bf16[256,1024]{1,0:T(8,128)(2,1)S(1)}, bf16[256,256]{1,0:T(8,128)(2,1)S(1)}, bf16[256,2048]{1,0:T(8,128)(2,1)S(1)}, bf16[256,1024]{1,0:T(8,128)(2,1)S(1)}) custom-call(s32[2]{0:T(128)S(1)} %copy-done.17, bf16[128,2048]{1,0:T(8,128)(2,1)} %get-tuple-element.47.tok_a, bf16[128,2048]{1,0:T(8,128)(2,1)S(1)} %collective-permute-done.11.tok_b, ...), custom_call_target="tpu_custom_call" | custom-call | tf_op jit(solution)/shard_map/pallas_call | solution.py:92
  54.7 2.9 %shard_map.96 = (bf16[256,1024]{1,0:T(8,128)(2,1)S(1)}, bf16[256,256]{1,0:T(8,128)(2,1)S(1)}, bf16[256,2048]{1,0:T(8,128)(2,1)S(1)}, bf16[256,1024]{1,0:T(8,128)(2,1)S(1)}) custom-call(s32[2]{0:T(128)S(1)} %copy-done.17, bf16[128,2048]{1,0:T(8,128)(2,1)S(1)} %copy-done.12, bf16[128,2048]{1,0:T(8,128)(2,1)S(1)} %collective-permute-done.9.tok_b, ...), custom_call_target="tpu_custom_call" | custom-call | tf_op jit(solution)/shard_map/pallas_call | solution.py:92
  57.6 2.7 %shard_map.98 = (f32[1024,1024]{1,0:T(8,128)S(1)}, f32[256,2048]{1,0:T(8,128)S(1)}) custom-call(bf16[256,1024]{1,0:T(8,128)(2,1)S(1)} %get-tuple-element.41.refs_0_, bf16[256,256]{1,0:T(8,128)(2,1)S(1)} %get-tuple-element.42.refs_1_, bf16[256,2048]{1,0:T(8,128)(2,1)S(1)} %get-tuple-element.43.refs_2_, ...), custom_call_target="tpu_custom_call" | custom-call | tf_op jit(solution)/shard_map/pallas_call | solution.py:131
  60.3 2.0 %copy-done.3 = f32[1024,1024]{1,0:T(8,128)} copy-done((f32[1024,1024]{1,0:T(8,128)}, f32[1024,1024]{1,0:T(8,128)S(1)}, u32[]{:S(2)}) %copy-start.3) | copy-done | bytes 4194328
  62.3 1.4 %copy-done.15 = f32[256,2048]{1,0:T(8,128)} copy-done((f32[256,2048]{1,0:T(8,128)}, f32[256,2048]{1,0:T(8,128)S(1)}, u32[]{:S(2)}) %copy-start.15) | copy-done | bytes 2097176
  66.0 1.1 fusion.28
  67.1 3.6 %convolution_convert_fusion = bf16[256,2048]{1,0:T(8,128)(2,1)S(1)} fusion(bf16[128,1024]{1,0:T(8,128)(2,1)S(1)} %get-tuple-element.74, bf16[128,1024]{1,0:T(8,128)(2,1)S(1)} %get-tuple-element.72, bf16[1,2048,1024]{2,1,0:T(8,128)(2,1)} %param.11), kind=kOutput, calls=%fused_computation.1 | convolution fusion | flops 1075314688 | bytes 5767168 | tf_op jit(solution)/shard_map/dot_general | solution.py:217
  71.2 3.3 %shard_map.100 = (bf16[256,1024]{1,0:T(8,128)(2,1)S(1)}, bf16[256,256]{1,0:T(8,128)(2,1)S(1)}, bf16[256,2048]{1,0:T(8,128)(2,1)S(1)}, bf16[256,1024]{1,0:T(8,128)(2,1)S(1)}) custom-call(s32[2]{0:T(128)S(1)} %copy-done.18, bf16[128,2048]{1,0:T(8,128)(2,1)S(1)} %copy-done.14, bf16[128,2048]{1,0:T(8,128)(2,1)S(1)} %collective-permute-done.15.tok_b, ...), custom_call_target="tpu_custom_call" | custom-call | tf_op jit(solution)/shard_map/pallas_call | solution.py:92
  76.7 1.3 %collective-permute-start.19 = (bf16[1,64,1024]{2,1,0:T(8,128)(2,1)S(1)}, bf16[1,64,1024]{2,1,0:T(8,128)(2,1)S(1)}, u32[]{:S(2)}, u32[]{:S(2)}) collective-permute-start(bf16[1,64,1024]{2,1,0:T(8,128)(2,1)S(1)} %dynamic-slice_bitcast_fusion.6), channel_id=1, source_target_pairs={{0,4},{4,0},{8,12},{12,8},{16,20},{20,16},{24,28},{28,24},{1,5},{5... | collective-permute-start | bytes 393224 | tf_op jit(solution)/shard_map/ppermute | solution.py:22
  79.8 2.0 %collective-permute-done.21 = bf16[1,64,1024]{2,1,0:T(8,128)(2,1)S(1)} collective-permute-done((bf16[1,64,1024]{2,1,0:T(8,128)(2,1)S(1)}, bf16[1,64,1024]{2,1,0:T(8,128)(2,1)S(1)}, u32[]{:S(2)}, u32[]{:S(2)}) %collective-permute-start.21) | collective-permute-done | bytes 131104 | tf_op jit(solution)/shard_map/ppermute | solution.py:22
  82.3 2.3 %collective-permute-done.19 = bf16[1,64,1024]{2,1,0:T(8,128)(2,1)S(1)} collective-permute-done((bf16[1,64,1024]{2,1,0:T(8,128)(2,1)S(1)}, bf16[1,64,1024]{2,1,0:T(8,128)(2,1)S(1)}, u32[]{:S(2)}, u32[]{:S(2)}) %collective-permute-start.19) | collective-permute-done | bytes 131104 | tf_op jit(solution)/shard_map/ppermute | solution.py:22
  84.7 2.7 %collective-permute-start.20 = (bf16[1,64,1024]{2,1,0:T(8,128)(2,1)S(1)}, bf16[1,64,1024]{2,1,0:T(8,128)(2,1)S(1)}, u32[]{:S(2)}, u32[]{:S(2)}) collective-permute-start(bf16[1,64,1024]{2,1,0:T(8,128)(2,1)S(1)} %fusion.20), channel_id=1, source_target_pairs={{0,16},{4,20},{8,24},{12,28},{16,0},{20,4},{24,8},{28,12},{1,17},{... | collective-permute-start | bytes 393224 | tf_op jit(solution)/shard_map/ppermute | solution.py:22
  87.4 2.9 %collective-permute-done.17 = bf16[1,128,1024]{2,1,0:T(8,128)(2,1)S(1)} collective-permute-done((bf16[1,128,1024]{2,1,0:T(8,128)(2,1)S(1)}, bf16[1,128,1024]{2,1,0:T(8,128)(2,1)S(1)}, u32[]{:S(2)}, u32[]{:S(2)}) %collective-permute-start.17) | collective-permute-done | bytes 262176 | tf_op jit(solution)/shard_map/ppermute | solution.py:22
  90.2 2.6 %collective-permute-start.22 = (bf16[1,64,1024]{2,1,0:T(8,128)(2,1)S(1)}, bf16[1,64,1024]{2,1,0:T(8,128)(2,1)S(1)}, u32[]{:S(2)}, u32[]{:S(2)}) collective-permute-start(bf16[1,64,1024]{2,1,0:T(8,128)(2,1)S(1)} %fusion.19), channel_id=1, source_target_pairs={{0,16},{4,20},{8,24},{12,28},{16,0},{20,4},{24,8},{28,12},{1,17},{... | collective-permute-start | bytes 393224 | tf_op jit(solution)/shard_map/ppermute | solution.py:22
  93.3 1.3 %convert_add_fusion.1 = f32[256,2048]{1,0:T(8,128)S(1)} fusion(bf16[256,2048]{1,0:T(8,128)(2,1)S(1)} %collective-permute-done.13, bf16[128,1024]{1,0:T(8,128)(2,1)S(1)} %get-tuple-element.73, bf16[128,1024]{1,0:T(8,128)(2,1)S(1)} %get-tuple-element.71, bf16[1,2048,1024]{2,1,0:T(8,128)(2,1)S(1)} %copy-done.1), kind=kOutput, calls=%fused_computation.6 | convolution fusion | flops 1076887552 | bytes 7864320 | tf_op jit(solution)/shard_map/dot_general | solution.py:217
  96.1 10.6 %collective-permute-done.14 = bf16[128,2048]{1,0:T(8,128)(2,1)S(1)} collective-permute-done((bf16[128,2048]{1,0:T(8,128)(2,1)S(1)}, bf16[128,2048]{1,0:T(8,128)(2,1)S(1)}, u32[]{:S(2)}, u32[]{:S(2)}) %collective-permute-start.14) | collective-permute-done | bytes 524320 | tf_op jit(solution)/shard_map/ppermute | solution.py:22
  106.7 2.6 %collective-permute-start.27 = (bf16[1,64,2048]{2,1,0:T(8,128)(2,1)S(1)}, bf16[1,64,2048]{2,1,0:T(8,128)(2,1)S(1)}, u32[]{:S(2)}, u32[]{:S(2)}) collective-permute-start(bf16[1,64,2048]{2,1,0:T(8,128)(2,1)S(1)} %fusion.14), channel_id=1, source_target_pairs={{0,16},{4,20},{8,24},{12,28},{16,0},{20,4},{24,8},{28,12},{1,17},{... | collective-permute-start | bytes 786440 | tf_op jit(solution)/shard_map/ppermute | solution.py:22
  110.7 7.0 %collective-permute-done.23 = bf16[1,128,1024]{2,1,0:T(8,128)(2,1)S(1)} collective-permute-done((bf16[1,128,1024]{2,1,0:T(8,128)(2,1)S(1)}, bf16[1,128,1024]{2,1,0:T(8,128)(2,1)S(1)}, u32[]{:S(2)}, u32[]{:S(2)}) %collective-permute-start.23) | collective-permute-done | bytes 262176 | tf_op jit(solution)/shard_map/ppermute | solution.py:22
  117.8 1.2 fusion.3
  119.0 3.9 %collective-permute-done.27 = bf16[1,64,2048]{2,1,0:T(8,128)(2,1)S(1)} collective-permute-done((bf16[1,64,2048]{2,1,0:T(8,128)(2,1)S(1)}, bf16[1,64,2048]{2,1,0:T(8,128)(2,1)S(1)}, u32[]{:S(2)}, u32[]{:S(2)}) %collective-permute-start.27) | collective-permute-done | bytes 262176 | tf_op jit(solution)/shard_map/ppermute | solution.py:22
  (117 shorter events, 20.2 us)
Async XLA Ops:
  0.7 7.1 %copy-start.22 = (bf16[128,2048]{1,0:T(8,128)(2,1)S(1)}, bf16[128,2048]{1,0:T(8,128)(2,1)}, u32[]{:S(2)}) copy-start(bf16[128,2048]{1,0:T(8,128)(2,1)} %param.8) | copy-start | bytes 1572868
  0.7 8.5 %collective-permute-start.5 = (bf16[128,2048]{1,0:T(8,128)(2,1)}, bf16[128,2048]{1,0:T(8,128)(2,1)S(1)}, u32[]{:S(2)}, u32[]{:S(2)}) collective-permute-start(bf16[128,2048]{1,0:T(8,128)(2,1)} %tok_a.1), channel_id=1, source_target_pairs={{0,1},{1,0},{2,3},{3,2},{4,5},{5,4},{6,7},{7,6},{8,9},{9,8},{10,11... | collective-permute-start | bytes 1572872 | tf_op jit(solution)/shard_map/ppermute | solution.py:22
  1.2 15.6 %collective-permute-start = (bf16[128,2048]{1,0:T(8,128)(2,1)}, bf16[128,2048]{1,0:T(8,128)(2,1)S(1)}, u32[]{:S(2)}, u32[]{:S(2)}) collective-permute-start(bf16[128,2048]{1,0:T(8,128)(2,1)} %tok_a.1), channel_id=1, source_target_pairs={{0,2},{1,3},{2,0},{3,1},{4,6},{5,7},{6,4},{7,5},{8,10},{9,11},{10,... | collective-permute-start | bytes 1572872 | tf_op jit(solution)/shard_map/ppermute | solution.py:22
  6.0 29.5 %collective-permute-start.4 = (bf16[1,2,2,64,2048]{4,3,2,1,0:T(8,128)(2,1)}, bf16[1,2,2,64,2048]{4,3,2,1,0:T(8,128)(2,1)}, u32[]{:S(2)}, u32[]{:S(2)}) collective-permute-start(bf16[1,2,2,64,2048]{4,3,2,1,0:T(8,128)(2,1)} %dynamic-slice_bitcast_fusion), channel_id=1, source_target_pairs={{0,4},{4,0},{8,12},{12,8},{16,20},{20,16},{24,28},{28,24},{1,5},{5... | collective-permute-start | bytes 3145736 | tf_op jit(solution)/shard_map/ppermute | solution.py:22
  8.7 26.9 %collective-permute-start.6 = (bf16[128,2176]{1,0:T(8,128)(2,1)}, bf16[128,2176]{1,0:T(8,128)(2,1)S(1)}, u32[]{:S(2)}, u32[]{:S(2)}) collective-permute-start(bf16[128,2176]{1,0:T(8,128)(2,1)} %pad_maximum_fusion.cot_a), channel_id=1, source_target_pairs={{0,1},{1,0},{2,3},{3,2},{4,5},{5,4},{6,7},{7,6},{8,9},{9,8},{10,11... | collective-permute-start | bytes 1671176 | tf_op jit(solution)/shard_map/ppermute | solution.py:22
  8.7 26.9 %collective-permute-start.2 = (bf16[128,2176]{1,0:T(8,128)(2,1)}, bf16[128,2176]{1,0:T(8,128)(2,1)}, u32[]{:S(2)}, u32[]{:S(2)}) collective-permute-start(bf16[128,2176]{1,0:T(8,128)(2,1)} %pad_maximum_fusion.cot_a), channel_id=1, source_target_pairs={{0,2},{1,3},{2,0},{3,1},{4,6},{5,7},{6,4},{7,5},{8,10},{9,11},{10,... | collective-permute-start | bytes 1671176 | tf_op jit(solution)/shard_map/ppermute | solution.py:22
  9.2 26.3 %copy-start.9 = (bf16[128,2048]{1,0:T(8,128)(2,1)}, bf16[128,2048]{1,0:T(8,128)(2,1)S(1)}, u32[]{:S(2)}) copy-start(bf16[128,2048]{1,0:T(8,128)(2,1)S(1)} %collective-permute-done.5.refs_6_.tok_b) | copy-start | bytes 1572868
  9.2 26.3 %collective-permute-start.3 = (bf16[128,2176]{1,0:T(8,128)(2,1)}, bf16[128,2176]{1,0:T(8,128)(2,1)}, u32[]{:S(2)}, u32[]{:S(2)}) collective-permute-start(bf16[128,2176]{1,0:T(8,128)(2,1)} %pad_maximum_fusion.cot_a), channel_id=1, source_target_pairs={{0,8},{4,12},{8,0},{12,4},{16,24},{20,28},{24,16},{28,20},{1,9},{5... | collective-permute-start | bytes 1671176 | tf_op jit(solution)/shard_map/ppermute | solution.py:22
  16.7 18.8 %collective-permute-start.1 = (bf16[128,2048]{1,0:T(8,128)(2,1)}, bf16[128,2048]{1,0:T(8,128)(2,1)}, u32[]{:S(2)}, u32[]{:S(2)}) collective-permute-start(bf16[128,2048]{1,0:T(8,128)(2,1)} %tok_a.1), channel_id=1, source_target_pairs={{0,8},{4,12},{8,0},{12,4},{16,24},{20,28},{24,16},{28,20},{1,9},{5... | collective-permute-start | bytes 1572872 | tf_op jit(solution)/shard_map/ppermute | solution.py:22
  19.4 20.5 %copy-start.2 = (bf16[1,512,2048]{2,1,0:T(8,128)(2,1)S(1)}, bf16[1,512,2048]{2,1,0:T(8,128)(2,1)}, u32[]{:S(2)}) copy-start(bf16[1,512,2048]{2,1,0:T(8,128)(2,1)} %param.12) | copy-start | bytes 6291460
  36.3 11.7 %collective-permute-start.11 = (bf16[128,2048]{1,0:T(8,128)(2,1)}, bf16[128,2048]{1,0:T(8,128)(2,1)S(1)}, u32[]{:S(2)}, u32[]{:S(2)}) collective-permute-start(bf16[128,2048]{1,0:T(8,128)(2,1)} %get-tuple-element.47.tok_a), channel_id=1, source_target_pairs={{0,1},{1,0},{2,3},{3,2},{4,5},{5,4},{6,7},{7,6},{8,9},{9,8},{10,11... | collective-permute-start | bytes 1572872 | tf_op jit(solution)/shard_map/ppermute | solution.py:22
  36.3 15.2 %collective-permute-start.12 = (bf16[128,2176]{1,0:T(8,128)(2,1)}, bf16[128,2176]{1,0:T(8,128)(2,1)S(1)}, u32[]{:S(2)}, u32[]{:S(2)}) collective-permute-start(bf16[128,2176]{1,0:T(8,128)(2,1)} %get-tuple-element.36.cot_a), channel_id=1, source_target_pairs={{0,1},{1,0},{2,3},{3,2},{4,5},{5,4},{6,7},{7,6},{8,9},{9,8},{10,11... | collective-permute-start | bytes 1671176 | tf_op jit(solution)/shard_map/ppermute | solution.py:22
  36.8 26.8 %collective-permute-start.8 = (bf16[128,2176]{1,0:T(8,128)(2,1)}, bf16[128,2176]{1,0:T(8,128)(2,1)}, u32[]{:S(2)}, u32[]{:S(2)}) collective-permute-start(bf16[128,2176]{1,0:T(8,128)(2,1)} %get-tuple-element.36.cot_a), channel_id=1, source_target_pairs={{0,2},{1,3},{2,0},{3,1},{4,6},{5,7},{6,4},{7,5},{8,10},{9,11},{10,... | collective-permute-start | bytes 1671176 | tf_op jit(solution)/shard_map/ppermute | solution.py:22
  38.3 16.3 %collective-permute-start.9 = (bf16[128,2048]{1,0:T(8,128)(2,1)}, bf16[128,2048]{1,0:T(8,128)(2,1)S(1)}, u32[]{:S(2)}, u32[]{:S(2)}) collective-permute-start(bf16[128,2048]{1,0:T(8,128)(2,1)} %get-tuple-element.35.tok_a), channel_id=1, source_target_pairs={{0,1},{1,0},{2,3},{3,2},{4,5},{5,4},{6,7},{7,6},{8,9},{9,8},{10,11... | collective-permute-start | bytes 1572872 | tf_op jit(solution)/shard_map/ppermute | solution.py:22
  38.3 25.3 %collective-permute-start.7 = (bf16[128,2048]{1,0:T(8,128)(2,1)}, bf16[128,2048]{1,0:T(8,128)(2,1)S(1)}, u32[]{:S(2)}, u32[]{:S(2)}) collective-permute-start(bf16[128,2048]{1,0:T(8,128)(2,1)} %get-tuple-element.35.tok_a), channel_id=1, source_target_pairs={{0,8},{4,12},{8,0},{12,4},{16,24},{20,28},{24,16},{28,20},{1,9},{5... | collective-permute-start | bytes 1572872 | tf_op jit(solution)/shard_map/ppermute | solution.py:22
  48.0 9.6 %copy-start.5 = (bf16[256,1024]{1,0:T(8,128)(2,1)}, bf16[256,1024]{1,0:T(8,128)(2,1)S(1)}, u32[]{:S(2)}) copy-start(bf16[256,1024]{1,0:T(8,128)(2,1)S(1)} %get-tuple-element.38.refs_3_.refs_2_) | copy-start | bytes 1572868
  48.1 6.6 %collective-permute-start.10 = (bf16[128,2176]{1,0:T(8,128)(2,1)}, bf16[128,2176]{1,0:T(8,128)(2,1)S(1)}, u32[]{:S(2)}, u32[]{:S(2)}) collective-permute-start(bf16[128,2176]{1,0:T(8,128)(2,1)} %get-tuple-element.39.cot_a), channel_id=1, source_target_pairs={{0,1},{1,0},{2,3},{3,2},{4,5},{5,4},{6,7},{7,6},{8,9},{9,8},{10,11... | collective-permute-start | bytes 1671176 | tf_op jit(solution)/shard_map/ppermute | solution.py:22
  64.5 6.7 %collective-permute-start.16 = (bf16[128,2176]{1,0:T(8,128)(2,1)}, bf16[128,2176]{1,0:T(8,128)(2,1)S(1)}, u32[]{:S(2)}, u32[]{:S(2)}) collective-permute-start(bf16[128,2176]{1,0:T(8,128)(2,1)} %get-tuple-element.56.cot_a), channel_id=1, source_target_pairs={{0,1},{1,0},{2,3},{3,2},{4,5},{5,4},{6,7},{7,6},{8,9},{9,8},{10,11... | collective-permute-start | bytes 1671176 | tf_op jit(solution)/shard_map/ppermute | solution.py:22
  64.8 6.4 %collective-permute-start.15 = (bf16[128,2048]{1,0:T(8,128)(2,1)}, bf16[128,2048]{1,0:T(8,128)(2,1)S(1)}, u32[]{:S(2)}, u32[]{:S(2)}) collective-permute-start(bf16[128,2048]{1,0:T(8,128)(2,1)} %get-tuple-element.55.tok_a), channel_id=1, source_target_pairs={{0,1},{1,0},{2,3},{3,2},{4,5},{5,4},{6,7},{7,6},{8,9},{9,8},{10,11... | collective-permute-start | bytes 1572872 | tf_op jit(solution)/shard_map/ppermute | solution.py:22
  70.8 22.1 %collective-permute-start.13 = (bf16[256,2048]{1,0:T(8,128)(2,1)S(1)}, bf16[256,2048]{1,0:T(8,128)(2,1)S(1)}, u32[]{:S(2)}, u32[]{:S(2)}) collective-permute-start(bf16[256,2048]{1,0:T(8,128)(2,1)S(1)} %convolution_convert_fusion), channel_id=1, source_target_pairs={{0,1},{1,0},{2,3},{3,2},{4,5},{5,4},{6,7},{7,6},{8,9},{9,8},{10,11... | collective-permute-start | bytes 3145736 | tf_op jit(solution)/shard_map/ppermute | solution.py:22
  75.4 6.4 %collective-permute-start.21 = (bf16[1,64,1024]{2,1,0:T(8,128)(2,1)S(1)}, bf16[1,64,1024]{2,1,0:T(8,128)(2,1)S(1)}, u32[]{:S(2)}, u32[]{:S(2)}) collective-permute-start(bf16[1,64,1024]{2,1,0:T(8,128)(2,1)S(1)} %dynamic-slice_bitcast_fusion.5), channel_id=1, source_target_pairs={{0,4},{4,0},{8,12},{12,8},{16,20},{20,16},{24,28},{28,24},{1,5},{5... | collective-permute-start | bytes 393224 | tf_op jit(solution)/shard_map/ppermute | solution.py:22
  76.3 18.4 %collective-permute-start.26 = (bf16[1,2,64,2048]{3,2,1,0:T(8,128)(2,1)S(1)}, bf16[1,2,64,2048]{3,2,1,0:T(8,128)(2,1)S(1)}, u32[]{:S(2)}, u32[]{:S(2)}) collective-permute-start(bf16[1,2,64,2048]{3,2,1,0:T(8,128)(2,1)S(1)} %copy-done.23), channel_id=1, source_target_pairs={{0,8},{4,12},{8,0},{12,4},{16,24},{20,28},{24,16},{28,20},{1,9},{5... | collective-permute-start | bytes 1572872 | tf_op jit(solution)/shard_map/ppermute | solution.py:22
  76.7 7.9 %collective-permute-start.19 = (bf16[1,64,1024]{2,1,0:T(8,128)(2,1)S(1)}, bf16[1,64,1024]{2,1,0:T(8,128)(2,1)S(1)}, u32[]{:S(2)}, u32[]{:S(2)}) collective-permute-start(bf16[1,64,1024]{2,1,0:T(8,128)(2,1)S(1)} %dynamic-slice_bitcast_fusion.6), channel_id=1, source_target_pairs={{0,4},{4,0},{8,12},{12,8},{16,20},{20,16},{24,28},{28,24},{1,5},{5... | collective-permute-start | bytes 393224 | tf_op jit(solution)/shard_map/ppermute | solution.py:22
  78.1 12.2 %collective-permute-start.17 = (bf16[1,128,1024]{2,1,0:T(8,128)(2,1)S(1)}, bf16[1,128,1024]{2,1,0:T(8,128)(2,1)S(1)}, u32[]{:S(2)}, u32[]{:S(2)}) collective-permute-start(bf16[1,128,1024]{2,1,0:T(8,128)(2,1)S(1)} %dynamic-slice_bitcast_fusion.4), channel_id=1, source_target_pairs={{0,4},{4,0},{8,12},{12,8},{16,20},{20,16},{24,28},{28,24},{1,5},{5... | collective-permute-start | bytes 786440 | tf_op jit(solution)/shard_map/ppermute | solution.py:22
  81.8 13.6 %collective-permute-start.24 = (bf16[1,64,2048]{2,1,0:T(8,128)(2,1)S(1)}, bf16[1,64,2048]{2,1,0:T(8,128)(2,1)S(1)}, u32[]{:S(2)}, u32[]{:S(2)}) collective-permute-start(bf16[1,64,2048]{2,1,0:T(8,128)(2,1)S(1)} %get-tuple-element.63), channel_id=1, source_target_pairs={{0,4},{4,0},{8,12},{12,8},{16,20},{20,16},{24,28},{28,24},{1,5},{5... | collective-permute-start | bytes 786440 | tf_op jit(solution)/shard_map/ppermute | solution.py:22
  84.7 25.5 %collective-permute-start.20 = (bf16[1,64,1024]{2,1,0:T(8,128)(2,1)S(1)}, bf16[1,64,1024]{2,1,0:T(8,128)(2,1)S(1)}, u32[]{:S(2)}, u32[]{:S(2)}) collective-permute-start(bf16[1,64,1024]{2,1,0:T(8,128)(2,1)S(1)} %fusion.20), channel_id=1, source_target_pairs={{0,16},{4,20},{8,24},{12,28},{16,0},{20,4},{24,8},{28,12},{1,17},{... | collective-permute-start | bytes 393224 | tf_op jit(solution)/shard_map/ppermute | solution.py:22
  90.2 20.5 %collective-permute-start.22 = (bf16[1,64,1024]{2,1,0:T(8,128)(2,1)S(1)}, bf16[1,64,1024]{2,1,0:T(8,128)(2,1)S(1)}, u32[]{:S(2)}, u32[]{:S(2)}) collective-permute-start(bf16[1,64,1024]{2,1,0:T(8,128)(2,1)S(1)} %fusion.19), channel_id=1, source_target_pairs={{0,16},{4,20},{8,24},{12,28},{16,0},{20,4},{24,8},{28,12},{1,17},{... | collective-permute-start | bytes 393224 | tf_op jit(solution)/shard_map/ppermute | solution.py:22
  92.9 24.9 %collective-permute-start.23 = (bf16[1,128,1024]{2,1,0:T(8,128)(2,1)S(1)}, bf16[1,128,1024]{2,1,0:T(8,128)(2,1)S(1)}, u32[]{:S(2)}, u32[]{:S(2)}) collective-permute-start(bf16[1,128,1024]{2,1,0:T(8,128)(2,1)S(1)} %fusion.18), channel_id=1, source_target_pairs={{0,16},{4,20},{8,24},{12,28},{16,0},{20,4},{24,8},{28,12},{1,17},{... | collective-permute-start | bytes 786440 | tf_op jit(solution)/shard_map/ppermute | solution.py:22
  94.7 12.0 %collective-permute-start.14 = (bf16[128,2048]{1,0:T(8,128)(2,1)S(1)}, bf16[128,2048]{1,0:T(8,128)(2,1)S(1)}, u32[]{:S(2)}, u32[]{:S(2)}) collective-permute-start(bf16[128,2048]{1,0:T(8,128)(2,1)S(1)} %slice.66), channel_id=1, source_target_pairs={{0,2},{1,3},{2,0},{3,1},{4,6},{5,7},{6,4},{7,5},{8,10},{9,11},{10,... | collective-permute-start | bytes 1572872 | tf_op jit(solution)/shard_map/ppermute | solution.py:22
  95.4 22.4 %collective-permute-start.18 = (bf16[1,256,1024]{2,1,0:T(8,128)(2,1)S(1)}, bf16[1,256,1024]{2,1,0:T(8,128)(2,1)S(1)}, u32[]{:S(2)}, u32[]{:S(2)}) collective-permute-start(bf16[1,256,1024]{2,1,0:T(8,128)(2,1)S(1)} %dynamic-slice_bitcast_fusion.1), channel_id=1, source_target_pairs={{0,4},{4,0},{8,12},{12,8},{16,20},{20,16},{24,28},{28,24},{1,5},{5... | collective-permute-start | bytes 1572872 | tf_op jit(solution)/shard_map/ppermute | solution.py:22
  106.7 16.2 %collective-permute-start.27 = (bf16[1,64,2048]{2,1,0:T(8,128)(2,1)S(1)}, bf16[1,64,2048]{2,1,0:T(8,128)(2,1)S(1)}, u32[]{:S(2)}, u32[]{:S(2)}) collective-permute-start(bf16[1,64,2048]{2,1,0:T(8,128)(2,1)S(1)} %fusion.14), channel_id=1, source_target_pairs={{0,16},{4,20},{8,24},{12,28},{16,0},{20,4},{24,8},{28,12},{1,17},{... | collective-permute-start | bytes 786440 | tf_op jit(solution)/shard_map/ppermute | solution.py:22
  110.2 12.7 %collective-permute-start.25 = (bf16[1,64,2048]{2,1,0:T(8,128)(2,1)S(1)}, bf16[1,64,2048]{2,1,0:T(8,128)(2,1)S(1)}, u32[]{:S(2)}, u32[]{:S(2)}) collective-permute-start(bf16[1,64,2048]{2,1,0:T(8,128)(2,1)S(1)} %get-tuple-element.64), channel_id=1, source_target_pairs={{0,4},{4,0},{8,12},{12,8},{16,20},{20,16},{24,28},{28,24},{1,5},{5... | collective-permute-start | bytes 786440 | tf_op jit(solution)/shard_map/ppermute | solution.py:22
  (22 other events, 59.2 us)

commit v6 on v5

v6 whole, which is shorter than its diff:
```python
import functools

import jax
import jax.numpy as jnp
from jax import lax
from jax.experimental import pallas as pl
from jax.experimental.pallas import tpu as pltpu
from jax.sharding import PartitionSpec as P

LANES = 128


def wide(values):
    return values.astype(jnp.float32)


def narrow(values):
    return values.astype(jnp.bfloat16)


def flip(values, axis, bit):
    return lax.ppermute(values, axis, [(i, i ^ bit) for i in range(lax.axis_size(axis))])


def take(values, axis, index):
    return lax.dynamic_index_in_dim(values, index, axis, keepdims=False)


def packed(tokens, cotangent, expert_ids, gate_probs, expert_count):
    lane = jnp.arange(LANES, dtype=jnp.int32)[None, :]
    route = jnp.zeros((expert_ids.shape[0], LANES), jnp.float32)
    for k in range(expert_ids.shape[1]):
        hit = (lane < 3 * expert_count) & (lane // 3 == expert_ids[:, k : k + 1])
        route = route + jnp.where(hit, gate_probs[:, k : k + 1], 0.0)
    high = lax.reduce_precision(route, 8, 7)
    middle = lax.reduce_precision(route - high, 8, 7)
    low = (route - high) - middle
    part = lane % 3
    coded = jnp.where(part == 0, high, jnp.where(part == 1, middle, low))
    return jnp.concatenate([tokens, cotangent, narrow(coded)], axis=1)


def own_columns(values, group_count, parity):
    unit = values.shape[1] // group_count * 2
    blocks = [values[:, k * unit : (k + 1) * unit] for k in range(group_count // 2)]
    even, odd = jnp.concatenate(blocks[0::2], axis=1), jnp.concatenate(blocks[1::2], axis=1)
    return jnp.where(parity == 1, odd, even)


def expert_kernel(group_count, place, *refs):
    blocks, (gate_up, down), made = refs[:-7], refs[-7:-5], refs[-5:]
    tok_own, hid_own, scaled, back_first, back_second = made
    width, units = gate_up.shape[0], down.shape[0]
    tile, split = units // 2, back_first.shape[0]
    me, parity = place[0], place[1]
    lane = lax.broadcasted_iota(jnp.int32, (1, LANES), 1)
    at = 0
    for block in blocks:
        coded = wide(block[:, 2 * width :])
        part = [
            jnp.sum(jnp.where(lane == 3 * me + k, coded, 0.0), axis=1, keepdims=True)
            for k in range(3)
        ]
        weight = (part[0] + part[1]) + part[2]
        here = slice(at, at + block.shape[0])
        scaled[here, :] = narrow(wide(block[:, width : 2 * width]) * weight)
        at += block.shape[0]
    rows = jnp.concatenate([block[:, :width] for block in blocks], axis=0)
    tok_own[...] = own_columns(rows, group_count, parity)
    grads = scaled[...]
    contract = (((1,), (1,)), ((), ()))
    hidden = []
    for at in range(0, units, tile):
        gate = jnp.dot(rows, gate_up[:, at : at + tile], preferred_element_type=jnp.float32)
        up = jnp.dot(
            rows, gate_up[:, units + at : units + at + tile], preferred_element_type=jnp.float32
        )
        sig = jax.nn.sigmoid(gate)
        activated = gate * sig
        hidden.append(narrow(activated * up))
        back_hidden = lax.dot_general(
            grads, down[at : at + tile, :], contract, preferred_element_type=jnp.float32
        )
        slope = up * sig * (1.0 + gate * (1.0 - sig))
        back_gate, back_up = narrow(back_hidden * slope), narrow(back_hidden * activated)
        for back, here in ((back_first, slice(0, split)), (back_second, slice(split, None))):
            back[:, at : at + tile] = back_gate[here]
            back[:, units + at : units + at + tile] = back_up[here]
    hid_own[...] = own_columns(jnp.concatenate(hidden, axis=1), group_count, parity)


def expert_rows(group_count, place, blocks, gate_up, down):
    rows, width = sum(block.shape[0] for block in blocks), gate_up.shape[0]
    units = down.shape[0]
    vmem = pl.BlockSpec(memory_space=pltpu.VMEM)
    shapes = [(rows, width // 2), (rows, units // 2), (rows, width)]
    shapes += [(rows // 2, 2 * units)] * 2
    return pl.pallas_call(
        functools.partial(expert_kernel, group_count),
        out_shape=tuple(jax.ShapeDtypeStruct(shape, jnp.bfloat16) for shape in shapes),
        in_specs=[pl.BlockSpec(memory_space=pltpu.SMEM)] + [vmem] * (len(blocks) + 2),
        out_specs=(vmem,) * 5,
        compiler_params=pltpu.CompilerParams(vmem_limit_bytes=24 << 20),
        cost_estimate=FREE,
    )(place, *blocks, gate_up, down)


ROWS = (((0,), (0,)), ((), ()))
FREE = pl.CostEstimate(flops=0, bytes_accessed=0, transcendentals=0)


def hold(values, awaited):
    here = pl.BlockSpec(memory_space=pl.ANY)
    return pl.pallas_call(
        lambda *refs: None,
        out_shape=tuple(jax.ShapeDtypeStruct(v.shape, v.dtype) for v in values),
        in_specs=[here] * (len(values) + len(awaited)),
        out_specs=(here,) * len(values),
        input_output_aliases={k: k for k in range(len(values))},
        cost_estimate=FREE,
    )(*values, *awaited)


def terms_kernel(*refs):
    blocks, (gate_sum, down_sum, sent, mark) = refs[:-4], refs[-4:]
    for k in range(len(blocks) // 5):
        tok_cols, hid_cols, scaled, *halves = [block[...] for block in blocks[5 * k : 5 * k + 5]]
        back = jnp.concatenate(halves, axis=0)
        gate = lax.dot_general(tok_cols, back, ROWS, preferred_element_type=jnp.float32)
        down = lax.dot_general(hid_cols, scaled, ROWS, preferred_element_type=jnp.float32)
        gate_sum[...] = gate if k == 0 else gate_sum[...] + gate
        down_sum[...] = down if k == 0 else down_sum[...] + down
        if k < 2:
            count = halves[1].shape[0]
            sent[k * count : (k + 1) * count, :] = halves[1]
    mark[...] = jnp.zeros_like(mark)


def early_terms(made):
    tok_cols, hid_cols, scaled, back, _ = made[0]
    vmem = pl.BlockSpec(memory_space=pltpu.VMEM)
    return pl.pallas_call(
        terms_kernel,
        out_shape=(
            jax.ShapeDtypeStruct((tok_cols.shape[1], back.shape[1]), jnp.float32),
            jax.ShapeDtypeStruct((hid_cols.shape[1], scaled.shape[1]), jnp.float32),
            jax.ShapeDtypeStruct((2 * back.shape[0], back.shape[1]), jnp.bfloat16),
            jax.ShapeDtypeStruct((8, LANES), jnp.float32),
        ),
        in_specs=[vmem] * (5 * len(made)),
        out_specs=(vmem,) * 4,
        compiler_params=pltpu.CompilerParams(vmem_limit_bytes=24 << 20),
        cost_estimate=FREE,
    )(*[v for block in made for v in block])


def on_device(
    tokens, cotangent, expert_ids, gate_probs, gate_up_weight, down_weight, down_residual
):
    tok_rows, model_width = tokens.shape
    expert_count = lax.axis_size("expert")
    group_count = lax.axis_size("dp")
    gate_up, down_matrix = gate_up_weight[0], down_weight[0]
    hidden_units = down_matrix.shape[0]
    me, group = lax.axis_index("expert"), lax.axis_index("dp")
    bit0, bit1, bit2 = group & 1, (group >> 1) & 1, (group >> 2) & 1
    high_count, half = group_count // 8, tok_rows // 2

    rows_own = packed(tokens, cotangent, expert_ids, gate_probs, expert_count)
    rows_c = flip(rows_own, "expert", 1)
    rows_x, rows_n = flip(rows_own, "expert", 2), flip(rows_own, "dp", 2)
    residual = down_residual[0, 0].reshape(high_count, 2, 2, 2, -1, model_width)
    res_got = flip(take(residual, 3, 1 - bit0), "dp", 1)
    place = jnp.stack([me, bit1]).astype(jnp.int32)

    def expert_on(*blocks):
        return expert_rows(group_count, place, blocks, gate_up, down_matrix)

    made = [expert_on(rows_own, rows_c)]
    rows_x, rows_n, res_got = hold((rows_x, rows_n, res_got), (made[0][1],))
    diagonal = [flip(rows_x[:half], "dp", 2), flip(rows_n[half:], "expert", 2)]
    made += [expert_on(rows, flip(rows, "expert", 1)) for rows in (rows_x, rows_n)]
    gate_early, down_early, back_sent, mark = early_terms(made)
    *diagonal, back_sent = hold((*diagonal, back_sent), (mark,))
    diagonal += [flip(rows, "expert", 1) for rows in diagonal]

    def terms(tok_cols, hid_cols, scaled, back):
        gate = lax.dot_general(tok_cols, back, ROWS, preferred_element_type=jnp.float32)
        down = lax.dot_general(hid_cols, scaled, ROWS, preferred_element_type=jnp.float32)
        return gate, down

    tok_late, hid_late, scaled_late, *back_late = expert_on(*diagonal)
    gate_late, down_late = terms(
        tok_late, hid_late, scaled_late, jnp.concatenate(back_late, axis=0)
    )
    gate_term = narrow(gate_early + gate_late).reshape(high_count, 2, 2, -1, 2 * hidden_units)
    down_term = narrow(down_early + down_late).reshape(high_count, 2, 2, -1, model_width)

    def side(term, third, first):
        return take(take(term, 1, third), 1, first)

    def pair_sum(kept, got):
        return wide(kept) + wide(got)

    count = gate_term.shape[3]
    first = max(count * 3 // 8, 16)
    edges = [0, first, count]
    far_sent, far_kept = [
        [side(gate_term[:, :, :, i:j], 1 - bit2, bit) for i, j in zip(edges, edges[1:])]
        for bit in (1 - bit0, bit0)
    ]
    far_got = [flip(piece, "dp", 1) for piece in far_sent]
    crossed = [
        flip(narrow(pair_sum(kept, got)), "dp", 4) for kept, got in zip(far_kept, far_got)
    ]
    res_pair = pair_sum(take(residual, 3, bit0), res_got)
    res_near = flip(narrow(take(res_pair, 2, 1 - bit1)), "dp", 2)
    res_near, near_sent = hold((res_near, side(gate_term, bit2, 1 - bit0)), (far_got[0],))
    res_sum = take(res_pair, 2, bit1) + wide(res_near)
    far_down = pair_sum(
        side(down_term, 1 - bit2, bit0), flip(side(down_term, 1 - bit2, 1 - bit0), "dp", 1)
    )
    crossed_down = flip(narrow(far_down + take(res_sum, 1, 1 - bit2)), "dp", 4)

    def input_part(back):
        return narrow(jnp.dot(back, gate_up.T, preferred_element_type=jnp.float32))

    core = flip(input_part(back_sent), "expert", 1)
    back_kept = jnp.concatenate([made[0][3], made[1][3]], axis=0)
    total = wide(input_part(back_kept)) + wide(core)
    across = flip(narrow(total[tok_rows:]), "expert", 2)
    token_grad = narrow(total[:tok_rows] + wide(across))

    near_gate = pair_sum(side(gate_term, bit2, bit0), flip(near_sent, "dp", 1))
    (near_sent,) = hold((side(down_term, bit2, 1 - bit0),), (across,))
    near_down = pair_sum(side(down_term, bit2, bit0), flip(near_sent, "dp", 1))
    gate_sum = near_gate + wide(jnp.concatenate(crossed, axis=1))
    down_sum = near_down + take(res_sum, 1, bit2) + wide(crossed_down)
    bit = 8
    while bit < group_count:
        mine = (group // bit) & 1
        halves = [v.reshape(-1, 2, *v.shape[1:]) for v in (gate_sum, down_sum)]
        gate_sum, down_sum = [
            take(v, 1, mine) + wide(flip(narrow(take(v, 1, 1 - mine)), "dp", bit)) for v in halves
        ]
        bit *= 2
    factor = 1.0 / group_count
    grad_gate_up, grad_down = gate_sum * factor, down_sum * factor
    return (token_grad, grad_gate_up, grad_down)


def solution(mesh):
    placed = (
        P(("dp", "expert"), None),
        P(("dp", "expert"), None),
        P(("dp", "expert"), None),
        P(("dp", "expert"), None),
        P("expert", None, None),
        P("expert", None, None),
        P("dp", "expert", None, None),
    )
    return jax.shard_map(
        on_device,
        mesh=mesh,
        in_specs=placed,
        out_specs=(P(("dp", "expert"), None), P("expert", "dp", None), P("expert", "dp", None)),
        check_vma=False,
    )
```

time: 124 us -> 138 us (1.11)
  other arithmetic: 6.91 us -> 17.8 us
  local copies, waits for them, and re-layouts: 16.5 us -> 26.2 us
  waiting for transfers between devices: 50.9 us -> 43.1 us
  matrix products: 6.13 us -> 9.72 us
  starting transfers between devices: 27.1 us -> 23.7 us
    ppermute x28 -> x21, waiting for transfers between devices: 50.9 us -> 43.1 us  [flip(): lax.ppermute(values, axis, [(i, i ^ bit) for i in range(lax.axis_size(axi...]
    convert_element_type x7, other arithmetic: 1.6 us -> 6.79 us  [narrow(): return values.astype(jnp.bfloat16)]
    unnamed x52 -> x64, local copies, waits for them, and re-layouts: 10.7 us -> 15.2 us
    dot_general x2, matrix products: 4.93 us -> 8.52 us  [input_part(): return narrow(jnp.dot(back, gate_up.T, preferred_element_type=jnp.float32))]
    ppermute x28 -> x21, starting transfers between devices: 27.1 us -> 23.7 us  [flip(): lax.ppermute(values, axis, [(i, i ^ bit) for i in range(lax.axis_size(axi...]
    dynamic_slice x0 -> x1, local copies, waits for them, and re-layouts: none -> 3.25 us  [take(): return lax.dynamic_index_in_dim(values, index, axis, keepdims=False)]
    add x2, other arithmetic: 1.67 us -> 4.59 us  [the longest x1 3.09 us: pair_sum(): return wide(kept) + wide(got)]
    mul x2, other arithmetic: 2.15 us -> 4.02 us  [on_device(): grad_gate_up, grad_down = (gate_sum * factor, down_sum * factor)]
  transfers between devices with their start and end apart: 28 -> 21, of which waited for: 8 -> 6; matrix products, arithmetic and copies ran while one was open for 14% -> 24% of each run, Pallas kernels for 12% -> 11%
where the time goes in v6:
time: 138 us; the launch traced here: 137 us
  waiting for transfers between devices  43.1 us (31%)
  local copies, waits for them, and re-layouts  26.2 us (19%)
  starting transfers between devices  23.7 us (17%)
  other arithmetic  17.8 us (13%)
  Pallas kernels  15.4 us (11%)
  matrix products  9.72 us (7%)
    ppermute x21, waiting for transfers between devices, flip(): lax.ppermute(values, axis, [(i, i ^ bit) for i in range(lax.axis_size(axi...  43.1 us
    ppermute x21, starting transfers between devices, flip(): lax.ppermute(values, axis, [(i, i ^ bit) for i in range(lax.axis_size(axi...  23.7 us
    unnamed x64, local copies, waits for them, and re-layouts  15.2 us
    pallas_call x4, Pallas kernels, expert_rows(): pl.pallas_call(functools.partial(expert_kernel, group_count), out_shape=t...  12.7 us
    dot_general x2, matrix products, input_part(): return narrow(jnp.dot(back, gate_up.T, preferred_element_type=jnp.float32))  8.52 us
    convert_element_type x7, other arithmetic, narrow(): return values.astype(jnp.bfloat16)  6.79 us
    mul x2, other arithmetic, on_device(): grad_gate_up, grad_down = (gate_sum * factor, down_sum * factor)  4.02 us
    dynamic_slice x1, local copies, waits for them, and re-layouts, take(): return lax.dynamic_index_in_dim(values, index, axis, keepdims=False)  3.25 us
  transfers between devices with their start and end apart: 21, of which 6 were waited for; matrix products, arithmetic and copies ran while one was open for 24% of the time, Pallas kernels for 11%

profile of v6, /device:TPU:0, one launch (start us, length us, event | category | flops | bytes accessed | tf_op | source)
XLA Modules:
  0.0 136.9 jit_solution(10144362408362386211)
XLA Ops:
  2.3 2.3 %pad_maximum_fusion.refs_0_ = bf16[128,4224]{1,0:T(8,128)(2,1)} fusion(bf16[128,128]{1,0:T(8,128)(2,1)S(1)} %fusion.20, bf16[128,2048]{1,0:T(8,128)(2,1)} %param.8, bf16[128,2048]{1,0:T(8,128)(2,1)} %param.7), kind=kLoop, calls=%fused_computation.7 | loop fusion | flops 3244032 | bytes 2162688 | tf_op jit(solution)/shard_map/concatenate | solution.py:40
  4.6 3.0 %collective-permute-start.2 = (bf16[128,4224]{1,0:T(8,128)(2,1)}, bf16[128,4224]{1,0:T(8,128)(2,1)S(1)}, u32[]{:S(2)}, u32[]{:S(2)}) collective-permute-start(bf16[128,4224]{1,0:T(8,128)(2,1)} %pad_maximum_fusion.refs_0_), channel_id=1, source_target_pairs={{0,8},{4,12},{8,0},{12,4},{16,24},{20,28},{24,16},{28,20},{1,9},{5... | collective-permute-start | bytes 3244040 | tf_op jit(solution)/shard_map/ppermute | solution.py:22
  7.6 1.5 %collective-permute-start.1 = (bf16[128,4224]{1,0:T(8,128)(2,1)}, bf16[128,4224]{1,0:T(8,128)(2,1)}, u32[]{:S(2)}, u32[]{:S(2)}) collective-permute-start(bf16[128,4224]{1,0:T(8,128)(2,1)} %pad_maximum_fusion.refs_0_), channel_id=1, source_target_pairs={{0,2},{1,3},{2,0},{3,1},{4,6},{5,7},{6,4},{7,5},{8,10},{9,11},{10,... | collective-permute-start | bytes 3244040 | tf_op jit(solution)/shard_map/ppermute | solution.py:22
  9.1 3.3 %constant_dynamic-slice_fusion = (bf16[1,2,2,1,64,2048]{5,4,3,2,1,0:T(8,128)(2,1)}, bf16[1,2,2,64,2048]{4,3,2,1,0:T(8,128)(2,1)}) fusion(bf16[1,2,2,2,64,2048]{5,4,3,2,1,0:T(8,128)(2,1)} %bitcast.78, s32[]{:T(128)S(6)} %select_n.110, s32[]{:T(128)S(6)} %select_n.107), kind=kLoop, calls=%fused_computation.46 | loop fusion | bytes 4194312 | tf_op jit(solution)/shard_map/jit(dynamic_index_in_dim)/dynamic_slice | solution.py:26
  12.4 1.5 %collective-permute-start.3 = (bf16[1,2,2,64,2048]{4,3,2,1,0:T(8,128)(2,1)}, bf16[1,2,2,64,2048]{4,3,2,1,0:T(8,128)(2,1)}, u32[]{:S(2)}, u32[]{:S(2)}) collective-permute-start(bf16[1,2,2,64,2048]{4,3,2,1,0:T(8,128)(2,1)} %get-tuple-element.68), channel_id=1, source_target_pairs={{0,4},{4,0},{8,12},{12,8},{16,20},{20,16},{24,28},{28,24},{1,5},{5... | collective-permute-start | bytes 3145736 | tf_op jit(solution)/shard_map/ppermute | solution.py:22
  14.0 2.2 %copy-done = bf16[1,2048,1024]{2,1,0:T(8,128)(2,1)S(1)} copy-done((bf16[1,2048,1024]{2,1,0:T(8,128)(2,1)S(1)}, bf16[1,2048,1024]{2,1,0:T(8,128)(2,1)}, u32[]{:S(2)}) %copy-start) | copy-done | bytes 4194328
  16.2 3.4 %shard_map.94 = (bf16[256,1024]{1,0:T(8,128)(2,1)S(1)}, bf16[256,256]{1,0:T(8,128)(2,1)S(1)}, bf16[256,2048]{1,0:T(8,128)(2,1)S(1)}, bf16[128,1024]{1,0:T(8,128)(2,1)S(1)}, bf16[128,1024]{1,0:T(8,128)(2,1)S(1)}) custom-call(s32[2]{0:T(128)S(1)} %pad_add_fusion.place, bf16[128,4224]{1,0:T(8,128)(2,1)} %pad_maximum_fusion.refs_0_, ...), custom_call_target="tpu_custom_call" | custom-call | tf_op jit(solution)/shard_map/pallas_call | solution.py:98
  22.8 15.5 %collective-permute-done.3.refs_2_ = bf16[1,2,2,64,2048]{4,3,2,1,0:T(8,128)(2,1)} collective-permute-done((bf16[1,2,2,64,2048]{4,3,2,1,0:T(8,128)(2,1)}, bf16[1,2,2,64,2048]{4,3,2,1,0:T(8,128)(2,1)}, u32[]{:S(2)}, u32[]{:S(2)}) %collective-permute-start.3) | collective-permute-done | bytes 1048608 | tf_op jit(solution)/shard_map/ppermute | solution.py:22
  42.9 3.1 %convert_add_fusion = f32[1,2,2,64,2048]{4,3,1,2,0:T(8,128)} fusion(bf16[1,2,2,1,64,2048]{5,4,3,2,1,0:T(8,128)(2,1)S(1)} %copy-done.26, bf16[1,2,2,64,2048]{4,3,2,1,0:T(8,128)(2,1)} %get-tuple-element.61), kind=kLoop, calls=%fused_computation.5 | loop fusion | flops 1572864 | bytes 4194304 | tf_op jit(solution)/shard_map/add | solution.py:203
  46.0 3.5 %shard_map.96 = (bf16[256,1024]{1,0:T(8,128)(2,1)S(1)}, bf16[256,256]{1,0:T(8,128)(2,1)S(1)}, bf16[256,2048]{1,0:T(8,128)(2,1)S(1)}, bf16[128,1024]{1,0:T(8,128)(2,1)S(1)}, bf16[128,1024]{1,0:T(8,128)(2,1)S(1)}) custom-call(s32[2]{0:T(128)S(1)} %pad_add_fusion.place, bf16[128,4224]{1,0:T(8,128)(2,1)} %get-tuple-element.37.refs_0_, ...), custom_call_target="tpu_custom_call" | custom-call | tf_op jit(solution)/shard_map/pallas_call | solution.py:98
  49.6 3.2 %shard_map.97 = (bf16[256,1024]{1,0:T(8,128)(2,1)S(1)}, bf16[256,256]{1,0:T(8,128)(2,1)S(1)}, bf16[256,2048]{1,0:T(8,128)(2,1)S(1)}, bf16[128,1024]{1,0:T(8,128)(2,1)S(1)}, bf16[128,1024]{1,0:T(8,128)(2,1)S(1)}) custom-call(s32[2]{0:T(128)S(1)} %pad_add_fusion.place, bf16[128,4224]{1,0:T(8,128)(2,1)S(1)} %copy-done.5, ...), custom_call_target="tpu_custom_call" | custom-call | tf_op jit(solution)/shard_map/pallas_call | solution.py:98
  52.9 2.7 %shard_map.98 = (f32[1024,1024]{1,0:T(8,128)S(1)}, f32[256,2048]{1,0:T(8,128)S(1)}, bf16[256,1024]{1,0:T(8,128)(2,1)S(1)}, f32[8,128]{1,0:T(8,128)S(1)}) custom-call(bf16[256,1024]{1,0:T(8,128)(2,1)S(1)} %copy-done.17, bf16[256,256]{1,0:T(8,128)(2,1)S(1)} %copy-done.20, bf16[256,2048]{1,0:T(8,128)(2,1)S(1)} %copy-done.15, ...), custom_call_target="tpu_custom_call" | custom-call | tf_op jit(solution)/shard_map/pallas_call | solution.py:142
  55.6 2.0 %copy-done.6 = f32[1024,1024]{1,0:T(8,128)} copy-done((f32[1024,1024]{1,0:T(8,128)}, f32[1024,1024]{1,0:T(8,128)S(1)}, u32[]{:S(2)}) %copy-start.6) | copy-done | bytes 4194328
  63.1 1.9 %collective-permute-start.12 = (bf16[1,2,64,2048]{3,2,1,0:T(8,128)(2,1)S(1)}, bf16[1,2,64,2048]{3,2,1,0:T(8,128)(2,1)}, u32[]{:S(2)}, u32[]{:S(2)}) collective-permute-start(bf16[1,2,64,2048]{3,2,1,0:T(8,128)(2,1)S(1)} %fusion.6), channel_id=1, source_target_pairs={{0,8},{4,12},{8,0},{12,4},{16,24},{20,28},{24,16},{28,20},{1,9},{5... | collective-permute-start | bytes 1572872 | tf_op jit(solution)/shard_map/ppermute | solution.py:22
  65.0 4.8 %convolution_convert_fusion = bf16[256,2048]{1,0:T(8,128)(2,1)} fusion(bf16[256,1024]{1,0:T(8,128)(2,1)} %get-tuple-element.54, bf16[1,2048,1024]{2,1,0:T(8,128)(2,1)} %param.11), kind=kOutput, calls=%fused_computation.1 | convolution fusion | flops 1074266112 | bytes 5767168 | tf_op jit(solution)/shard_map/dot_general | solution.py:226
  69.8 2.6 %shard_map.100 = (bf16[256,1024]{1,0:T(8,128)(2,1)S(1)}, bf16[256,256]{1,0:T(8,128)(2,1)S(1)}, bf16[256,2048]{1,0:T(8,128)(2,1)S(1)}, bf16[128,1024]{1,0:T(8,128)(2,1)S(1)}, bf16[128,1024]{1,0:T(8,128)(2,1)S(1)}) custom-call(s32[2]{0:T(128)S(1)} %pad_add_fusion.place, bf16[64,4224]{1,0:T(8,128)(2,1)S(1)} %copy-done.11, bf16[64,4224]{1,0:T(8,128)(2,1)S(1)} %copy-done.9, ...), custom_call_target="tpu_custom_call" | custom-call | tf_op jit(solution)/shard_map/pallas_call | solution.py:98
  76.3 1.6 %copy-done.13 = f32[256,2048]{1,0:T(8,128)S(1)} copy-done((f32[256,2048]{1,0:T(8,128)S(1)}, f32[256,2048]{1,0:T(8,128)}, u32[]{:S(2)}) %copy-start.13) | copy-done | bytes 2097176
  79.1 1.5 %collective-permute-start.19 = (bf16[1,64,2048]{2,1,0:T(8,128)(2,1)}, bf16[1,64,2048]{2,1,0:T(8,128)(2,1)}, u32[]{:S(2)}, u32[]{:S(2)}) collective-permute-start(bf16[1,64,2048]{2,1,0:T(8,128)(2,1)} %get-tuple-element.70), channel_id=1, source_target_pairs={{0,4},{4,0},{8,12},{12,8},{16,20},{20,16},{24,28},{28,24},{1,5},{5... | collective-permute-start | bytes 786440 | tf_op jit(solution)/shard_map/ppermute | solution.py:22
  82.0 1.5 %collective-permute-start.16 = (bf16[1,160,1024]{2,1,0:T(8,128)(2,1)}, bf16[1,160,1024]{2,1,0:T(8,128)(2,1)}, u32[]{:S(2)}, u32[]{:S(2)}) collective-permute-start(bf16[1,160,1024]{2,1,0:T(8,128)(2,1)} %dynamic-slice_bitcast_fusion.2), channel_id=1, source_target_pairs={{0,4},{4,0},{8,12},{12,8},{16,20},{20,16},{24,28},{28,24},{1,5},{5... | collective-permute-start | bytes 983048 | tf_op jit(solution)/shard_map/ppermute | solution.py:22
  84.3 8.3 %collective-permute-done.13.refs_2_ = bf16[1,96,1024]{2,1,0:T(8,128)(2,1)S(1)} collective-permute-done((bf16[1,96,1024]{2,1,0:T(8,128)(2,1)S(1)}, bf16[1,96,1024]{2,1,0:T(8,128)(2,1)S(1)}, u32[]{:S(2)}, u32[]{:S(2)}) %collective-permute-start.13) | collective-permute-done | bytes 196640 | tf_op jit(solution)/shard_map/ppermute | solution.py:22
  93.4 2.6 %collective-permute-start.15 = (bf16[1,96,1024]{2,1,0:T(8,128)(2,1)}, bf16[1,96,1024]{2,1,0:T(8,128)(2,1)}, u32[]{:S(2)}, u32[]{:S(2)}) collective-permute-start(bf16[1,96,1024]{2,1,0:T(8,128)(2,1)} %fusion.19), channel_id=1, source_target_pairs={{0,16},{4,20},{8,24},{12,28},{16,0},{20,4},{24,8},{28,12},{1,17},{... | collective-permute-start | bytes 589832 | tf_op jit(solution)/shard_map/ppermute | solution.py:22
  96.0 1.5 %collective-permute-start.14 = (bf16[1,256,1024]{2,1,0:T(8,128)(2,1)}, bf16[1,256,1024]{2,1,0:T(8,128)(2,1)S(1)}, u32[]{:S(2)}, u32[]{:S(2)}) collective-permute-start(bf16[1,256,1024]{2,1,0:T(8,128)(2,1)} %get-tuple-element.62), channel_id=1, source_target_pairs={{0,4},{4,0},{8,12},{12,8},{16,20},{20,16},{24,28},{28,24},{1,5},{5... | collective-permute-start | bytes 1572872 | tf_op jit(solution)/shard_map/ppermute | solution.py:22
  97.5 1.5 %bitcast_add_fusion = f32[1,2,64,2048]{3,2,1,0:T(8,128)S(1)} fusion(bf16[1,2,64,2048]{3,2,1,0:T(8,128)(2,1)} %get-tuple-element.66, f32[1,2,2,64,2048]{4,3,1,2,0:T(8,128)} %convert_add_fusion, s32[]{:T(128)S(6)} %select_n.116), kind=kLoop, calls=%fused_computation.15 | loop fusion | flops 524288 | bytes 2621444 | tf_op jit(solution)/shard_map/add | solution.py:219
  100.9 2.7 %collective-permute-start.17 = (bf16[1,160,1024]{2,1,0:T(8,128)(2,1)S(1)}, bf16[1,160,1024]{2,1,0:T(8,128)(2,1)S(1)}, u32[]{:S(2)}, u32[]{:S(2)}) collective-permute-start(bf16[1,160,1024]{2,1,0:T(8,128)(2,1)S(1)} %fusion.5), channel_id=1, source_target_pairs={{0,16},{4,20},{8,24},{12,28},{16,0},{20,4},{24,8},{28,12},{1,17},{... | collective-permute-start | bytes 983048 | tf_op jit(solution)/shard_map/ppermute | solution.py:22
  103.6 3.8 %fusion.1 = f32[256,2048]{1,0:T(8,128)S(1)} fusion(bf16[256,2048]{1,0:T(8,128)(2,1)} %collective-permute-done.8, bf16[128,1024]{1,0:T(8,128)(2,1)S(1)} %copy-done.22, bf16[128,1024]{1,0:T(8,128)(2,1)S(1)} %get-tuple-element.35.refs_3_, bf16[1,2048,1024]{2,1,0:T(8,128)(2,1)} %param.11), kind=kOutput, calls=%fused_computation.4 | convolution fusion | flops 1076887552 | bytes 7864320 | tf_op jit(solution)/shard_map/dot_general | solution.py:226
  107.5 1.6 %collective-permute-start.9 = (bf16[128,2048]{1,0:T(8,128)(2,1)S(1)}, bf16[128,2048]{1,0:T(8,128)(2,1)}, u32[]{:S(2)}, u32[]{:S(2)}) collective-permute-start(bf16[128,2048]{1,0:T(8,128)(2,1)S(1)} %slice.55), channel_id=1, source_target_pairs={{0,2},{1,3},{2,0},{3,1},{4,6},{5,7},{6,4},{7,5},{8,10},{9,11},{10,... | collective-permute-start | bytes 1572872 | tf_op jit(solution)/shard_map/ppermute | solution.py:22
  111.9 12.5 %collective-permute-done.17 = bf16[1,160,1024]{2,1,0:T(8,128)(2,1)S(1)} collective-permute-done((bf16[1,160,1024]{2,1,0:T(8,128)(2,1)S(1)}, bf16[1,160,1024]{2,1,0:T(8,128)(2,1)S(1)}, u32[]{:S(2)}, u32[]{:S(2)}) %collective-permute-start.17) | collective-permute-done | bytes 327712 | tf_op jit(solution)/shard_map/ppermute | solution.py:22
  124.4 2.1 %fusion.4 = f32[1,256,1024]{2,1,0:T(8,128)} fusion(bf16[1,256,1024]{2,1,0:T(8,128)(2,1)S(1)} %collective-permute-done.14, bf16[1,160,1024]{2,1,0:T(8,128)(2,1)S(1)} %collective-permute-done.17, bf16[1,96,1024]{2,1,0:T(8,128)(2,1)} %collective-permute-done.15, bf16[1,2,2,256,1024]{4,3,2,1,0:T(8,128)(2,1)S(1)} %bitcast.74, s32[]{:T(128)S(6)} %select_n.109, ...), kind=kLoop, calls=%fused_computation.14 | loop fusion | flops 2359296 | bytes 2621448 | tf_op jit(solution)/shard_map/mul | solution.py:248
  126.6 1.6 %collective-permute-start.18 = (bf16[1,64,2048]{2,1,0:T(8,128)(2,1)}, bf16[1,64,2048]{2,1,0:T(8,128)(2,1)S(1)}, u32[]{:S(2)}, u32[]{:S(2)}) collective-permute-start(bf16[1,64,2048]{2,1,0:T(8,128)(2,1)} %shard_map.102), channel_id=1, source_target_pairs={{0,4},{4,0},{8,12},{12,8},{16,20},{20,16},{24,28},{28,24},{1,5},{5... | collective-permute-start | bytes 786440 | tf_op jit(solution)/shard_map/ppermute | solution.py:22
  128.2 2.3 %fusion.2 = bf16[128,2048]{1,0:T(8,128)(2,1)} fusion(f32[256,2048]{1,0:T(8,128)} %copy-done.30, bf16[128,2048]{1,0:T(8,128)(2,1)} %collective-permute-done.9.refs_1_), kind=kLoop, calls=%fused_computation.10 | loop fusion | flops 786432 | bytes 2097152 | tf_op jit(solution)/shard_map/convert_element_type | solution.py:18
  130.5 4.5 %collective-permute-done.18 = bf16[1,64,2048]{2,1,0:T(8,128)(2,1)S(1)} collective-permute-done((bf16[1,64,2048]{2,1,0:T(8,128)(2,1)}, bf16[1,64,2048]{2,1,0:T(8,128)(2,1)S(1)}, u32[]{:S(2)}, u32[]{:S(2)}) %collective-permute-start.18) | collective-permute-done | bytes 262176 | tf_op jit(solution)/shard_map/ppermute | solution.py:22
  135.0 1.9 %fusion.18 = f32[1,64,2048]{2,1,0:T(8,128)} fusion(bf16[1,64,2048]{2,1,0:T(8,128)(2,1)} %collective-permute-done.20, f32[1,2,64,2048]{3,2,1,0:T(8,128)S(1)} %copy-done.28, s32[]{:T(128)S(6)} %select_n.108, bf16[1,64,2048]{2,1,0:T(8,128)(2,1)S(1)} %collective-permute-done.18, bf16[1,2,2,64,2048]{4,3,2,1,0:T(8,128)(2,1)S(1)} %bitcast.77, s32[]{:T(128)S(6)} %select_n.109, ...), kind=kLoop, calls=%fused_computation.34 | loop fusion | flops 917504 | bytes 1835020 | tf_op jit(solution)/shard_map/mul | solution.py:248
  (116 shorter events, 28.0 us)
Async XLA Ops:
  4.6 33.7 %collective-permute-start.2 = (bf16[128,4224]{1,0:T(8,128)(2,1)}, bf16[128,4224]{1,0:T(8,128)(2,1)S(1)}, u32[]{:S(2)}, u32[]{:S(2)}) collective-permute-start(bf16[128,4224]{1,0:T(8,128)(2,1)} %pad_maximum_fusion.refs_0_), channel_id=1, source_target_pairs={{0,8},{4,12},{8,0},{12,4},{16,24},{20,28},{24,16},{28,20},{1,9},{5... | collective-permute-start | bytes 3244040 | tf_op jit(solution)/shard_map/ppermute | solution.py:22
  7.6 30.6 %collective-permute-start.1 = (bf16[128,4224]{1,0:T(8,128)(2,1)}, bf16[128,4224]{1,0:T(8,128)(2,1)}, u32[]{:S(2)}, u32[]{:S(2)}) collective-permute-start(bf16[128,4224]{1,0:T(8,128)(2,1)} %pad_maximum_fusion.refs_0_), channel_id=1, source_target_pairs={{0,2},{1,3},{2,0},{3,1},{4,6},{5,7},{6,4},{7,5},{8,10},{9,11},{10,... | collective-permute-start | bytes 3244040 | tf_op jit(solution)/shard_map/ppermute | solution.py:22
  9.1 4.9 %collective-permute-start = (bf16[128,4224]{1,0:T(8,128)(2,1)}, bf16[128,4224]{1,0:T(8,128)(2,1)}, u32[]{:S(2)}, u32[]{:S(2)}) collective-permute-start(bf16[128,4224]{1,0:T(8,128)(2,1)} %pad_maximum_fusion.refs_0_), channel_id=1, source_target_pairs={{0,1},{1,0},{2,3},{3,2},{4,5},{5,4},{6,7},{7,6},{8,9},{9,8},{10,11... | collective-permute-start | bytes 3244040 | tf_op jit(solution)/shard_map/ppermute | solution.py:22
  9.1 4.9 %copy-start.3 = (bf16[1,512,2048]{2,1,0:T(8,128)(2,1)S(1)}, bf16[1,512,2048]{2,1,0:T(8,128)(2,1)}, u32[]{:S(2)}) copy-start(bf16[1,512,2048]{2,1,0:T(8,128)(2,1)} %param.12) | copy-start | bytes 6291460
  12.4 25.9 %collective-permute-start.3 = (bf16[1,2,2,64,2048]{4,3,2,1,0:T(8,128)(2,1)}, bf16[1,2,2,64,2048]{4,3,2,1,0:T(8,128)(2,1)}, u32[]{:S(2)}, u32[]{:S(2)}) collective-permute-start(bf16[1,2,2,64,2048]{4,3,2,1,0:T(8,128)(2,1)} %get-tuple-element.68), channel_id=1, source_target_pairs={{0,4},{4,0},{8,12},{12,8},{16,20},{20,16},{24,28},{28,24},{1,5},{5... | collective-permute-start | bytes 3145736 | tf_op jit(solution)/shard_map/ppermute | solution.py:22
  39.3 6.7 %collective-permute-start.4 = (bf16[128,4224]{1,0:T(8,128)(2,1)}, bf16[128,4224]{1,0:T(8,128)(2,1)}, u32[]{:S(2)}, u32[]{:S(2)}) collective-permute-start(bf16[128,4224]{1,0:T(8,128)(2,1)} %get-tuple-element.37.refs_0_), channel_id=1, source_target_pairs={{0,1},{1,0},{2,3},{3,2},{4,5},{5,4},{6,7},{7,6},{8,9},{9,8},{10,11... | collective-permute-start | bytes 3244040 | tf_op jit(solution)/shard_map/ppermute | solution.py:22
  39.3 10.3 %collective-permute-start.7 = (bf16[128,4224]{1,0:T(8,128)(2,1)}, bf16[128,4224]{1,0:T(8,128)(2,1)}, u32[]{:S(2)}, u32[]{:S(2)}) collective-permute-start(bf16[128,4224]{1,0:T(8,128)(2,1)} %get-tuple-element.39.refs_0_), channel_id=1, source_target_pairs={{0,1},{1,0},{2,3},{3,2},{4,5},{5,4},{6,7},{7,6},{8,9},{9,8},{10,11... | collective-permute-start | bytes 3244040 | tf_op jit(solution)/shard_map/ppermute | solution.py:22
  42.1 18.2 %collective-permute-start.6 = (bf16[64,4224]{1,0:T(8,128)(2,1)S(1)}, bf16[64,4224]{1,0:T(8,128)(2,1)S(1)}, u32[]{:S(2)}, u32[]{:S(2)}) collective-permute-start(bf16[64,4224]{1,0:T(8,128)(2,1)S(1)} %slice.38), channel_id=1, source_target_pairs={{0,2},{1,3},{2,0},{3,1},{4,6},{5,7},{6,4},{7,5},{8,10},{9,11},{10,... | collective-permute-start | bytes 1622024 | tf_op jit(solution)/shard_map/ppermute | solution.py:22
  42.7 17.6 %collective-permute-start.5 = (bf16[64,4224]{1,0:T(8,128)(2,1)S(1)}, bf16[64,4224]{1,0:T(8,128)(2,1)S(1)}, u32[]{:S(2)}, u32[]{:S(2)}) collective-permute-start(bf16[64,4224]{1,0:T(8,128)(2,1)S(1)} %slice.37), channel_id=1, source_target_pairs={{0,8},{4,12},{8,0},{12,4},{16,24},{20,28},{24,16},{28,20},{1,9},{5... | collective-permute-start | bytes 1622024 | tf_op jit(solution)/shard_map/ppermute | solution.py:22
  46.0 3.6 %copy-start.5 = (bf16[128,4224]{1,0:T(8,128)(2,1)S(1)}, bf16[128,4224]{1,0:T(8,128)(2,1)}, u32[]{:S(2)}) copy-start(bf16[128,4224]{1,0:T(8,128)(2,1)} %get-tuple-element.39.refs_0_) | copy-start | bytes 3244036
  49.5 3.3 %copy-start.21 = (bf16[128,1024]{1,0:T(8,128)(2,1)}, bf16[128,1024]{1,0:T(8,128)(2,1)S(1)}, u32[]{:S(2)}) copy-start(bf16[128,1024]{1,0:T(8,128)(2,1)S(1)} %get-tuple-element.38.refs_8_) | copy-start | bytes 786436
  61.3 8.4 %collective-permute-start.10 = (bf16[64,4224]{1,0:T(8,128)(2,1)}, bf16[64,4224]{1,0:T(8,128)(2,1)S(1)}, u32[]{:S(2)}, u32[]{:S(2)}) collective-permute-start(bf16[64,4224]{1,0:T(8,128)(2,1)} %get-tuple-element.56.refs_0_), channel_id=1, source_target_pairs={{0,1},{1,0},{2,3},{3,2},{4,5},{5,4},{6,7},{7,6},{8,9},{9,8},{10,11... | collective-permute-start | bytes 1622024 | tf_op jit(solution)/shard_map/ppermute | solution.py:22
  61.3 8.4 %collective-permute-start.11 = (bf16[64,4224]{1,0:T(8,128)(2,1)}, bf16[64,4224]{1,0:T(8,128)(2,1)S(1)}, u32[]{:S(2)}, u32[]{:S(2)}) collective-permute-start(bf16[64,4224]{1,0:T(8,128)(2,1)} %get-tuple-element.57.refs_1_), channel_id=1, source_target_pairs={{0,1},{1,0},{2,3},{3,2},{4,5},{5,4},{6,7},{7,6},{8,9},{9,8},{10,11... | collective-permute-start | bytes 1622024 | tf_op jit(solution)/shard_map/ppermute | solution.py:22
  63.1 32.9 %collective-permute-start.12 = (bf16[1,2,64,2048]{3,2,1,0:T(8,128)(2,1)S(1)}, bf16[1,2,64,2048]{3,2,1,0:T(8,128)(2,1)}, u32[]{:S(2)}, u32[]{:S(2)}) collective-permute-start(bf16[1,2,64,2048]{3,2,1,0:T(8,128)(2,1)S(1)} %fusion.6), channel_id=1, source_target_pairs={{0,8},{4,12},{8,0},{12,4},{16,24},{20,28},{24,16},{28,20},{1,9},{5... | collective-permute-start | bytes 1572872 | tf_op jit(solution)/shard_map/ppermute | solution.py:22
  65.0 4.8 %copy-start.2 = (bf16[1,2048,1024]{2,1,0:T(8,128)(2,1)S(1)}, bf16[1,2048,1024]{2,1,0:T(8,128)(2,1)}, u32[]{:S(2)}) copy-start(bf16[1,2048,1024]{2,1,0:T(8,128)(2,1)} %param.11) | copy-start | bytes 12582916
  65.0 4.8 %copy-start.9 = (bf16[64,4224]{1,0:T(8,128)(2,1)S(1)}, bf16[64,4224]{1,0:T(8,128)(2,1)}, u32[]{:S(2)}) copy-start(bf16[64,4224]{1,0:T(8,128)(2,1)} %get-tuple-element.57.refs_1_) | copy-start | bytes 1622020
  65.0 4.8 %copy-start.11 = (bf16[64,4224]{1,0:T(8,128)(2,1)S(1)}, bf16[64,4224]{1,0:T(8,128)(2,1)}, u32[]{:S(2)}) copy-start(bf16[64,4224]{1,0:T(8,128)(2,1)} %get-tuple-element.56.refs_0_) | copy-start | bytes 1622020
  69.7 33.9 %collective-permute-start.8 = (bf16[256,2048]{1,0:T(8,128)(2,1)}, bf16[256,2048]{1,0:T(8,128)(2,1)}, u32[]{:S(2)}, u32[]{:S(2)}) collective-permute-start(bf16[256,2048]{1,0:T(8,128)(2,1)} %convolution_convert_fusion), channel_id=1, source_target_pairs={{0,1},{1,0},{2,3},{3,2},{4,5},{5,4},{6,7},{7,6},{8,9},{9,8},{10,11... | collective-permute-start | bytes 3145736 | tf_op jit(solution)/shard_map/ppermute | solution.py:22
  75.8 5.4 %copy-start.29 = (bf16[1,2,2,160,1024]{4,3,2,1,0:T(8,128)(2,1)}, bf16[1,2,2,160,1024]{4,3,2,1,0:T(8,128)(2,1)S(1)}, u32[]{:S(2)}) copy-start(bf16[1,2,2,160,1024]{4,3,2,1,0:T(8,128)(2,1)S(1)} %slice.46) | copy-start | bytes 3932164
  79.1 29.9 %collective-permute-start.19 = (bf16[1,64,2048]{2,1,0:T(8,128)(2,1)}, bf16[1,64,2048]{2,1,0:T(8,128)(2,1)}, u32[]{:S(2)}, u32[]{:S(2)}) collective-permute-start(bf16[1,64,2048]{2,1,0:T(8,128)(2,1)} %get-tuple-element.70), channel_id=1, source_target_pairs={{0,4},{4,0},{8,12},{12,8},{16,20},{20,16},{24,28},{28,24},{1,5},{5... | collective-permute-start | bytes 786440 | tf_op jit(solution)/shard_map/ppermute | solution.py:22
  80.6 12.0 %collective-permute-start.13 = (bf16[1,96,1024]{2,1,0:T(8,128)(2,1)S(1)}, bf16[1,96,1024]{2,1,0:T(8,128)(2,1)S(1)}, u32[]{:S(2)}, u32[]{:S(2)}) collective-permute-start(bf16[1,96,1024]{2,1,0:T(8,128)(2,1)S(1)} %dynamic-slice_bitcast_fusion.5), channel_id=1, source_target_pairs={{0,4},{4,0},{8,12},{12,8},{16,20},{20,16},{24,28},{28,24},{1,5},{5... | collective-permute-start | bytes 589832 | tf_op jit(solution)/shard_map/ppermute | solution.py:22
  82.0 17.8 %collective-permute-start.16 = (bf16[1,160,1024]{2,1,0:T(8,128)(2,1)}, bf16[1,160,1024]{2,1,0:T(8,128)(2,1)}, u32[]{:S(2)}, u32[]{:S(2)}) collective-permute-start(bf16[1,160,1024]{2,1,0:T(8,128)(2,1)} %dynamic-slice_bitcast_fusion.2), channel_id=1, source_target_pairs={{0,4},{4,0},{8,12},{12,8},{16,20},{20,16},{24,28},{28,24},{1,5},{5... | collective-permute-start | bytes 983048 | tf_op jit(solution)/shard_map/ppermute | solution.py:22
  93.4 18.5 %collective-permute-start.15 = (bf16[1,96,1024]{2,1,0:T(8,128)(2,1)}, bf16[1,96,1024]{2,1,0:T(8,128)(2,1)}, u32[]{:S(2)}, u32[]{:S(2)}) collective-permute-start(bf16[1,96,1024]{2,1,0:T(8,128)(2,1)} %fusion.19), channel_id=1, source_target_pairs={{0,16},{4,20},{8,24},{12,28},{16,0},{20,4},{24,8},{28,12},{1,17},{... | collective-permute-start | bytes 589832 | tf_op jit(solution)/shard_map/ppermute | solution.py:22
  96.0 7.6 %copy-start.22 = (bf16[128,1024]{1,0:T(8,128)(2,1)S(1)}, bf16[128,1024]{1,0:T(8,128)(2,1)}, u32[]{:S(2)}) copy-start(bf16[128,1024]{1,0:T(8,128)(2,1)} %copy-done.21) | copy-start | bytes 786436
  96.0 28.5 %collective-permute-start.14 = (bf16[1,256,1024]{2,1,0:T(8,128)(2,1)}, bf16[1,256,1024]{2,1,0:T(8,128)(2,1)S(1)}, u32[]{:S(2)}, u32[]{:S(2)}) collective-permute-start(bf16[1,256,1024]{2,1,0:T(8,128)(2,1)} %get-tuple-element.62), channel_id=1, source_target_pairs={{0,4},{4,0},{8,12},{12,8},{16,20},{20,16},{24,28},{28,24},{1,5},{5... | collective-permute-start | bytes 1572872 | tf_op jit(solution)/shard_map/ppermute | solution.py:22
  99.0 10.0 %copy-start.27 = (f32[1,2,64,2048]{3,2,1,0:T(8,128)}, f32[1,2,64,2048]{3,2,1,0:T(8,128)S(1)}, u32[]{:S(2)}) copy-start(f32[1,2,64,2048]{3,2,1,0:T(8,128)S(1)} %bitcast_add_fusion) | copy-start | bytes 3145732
  100.9 23.5 %collective-permute-start.17 = (bf16[1,160,1024]{2,1,0:T(8,128)(2,1)S(1)}, bf16[1,160,1024]{2,1,0:T(8,128)(2,1)S(1)}, u32[]{:S(2)}, u32[]{:S(2)}) collective-permute-start(bf16[1,160,1024]{2,1,0:T(8,128)(2,1)S(1)} %fusion.5), channel_id=1, source_target_pairs={{0,16},{4,20},{8,24},{12,28},{16,0},{20,4},{24,8},{28,12},{1,17},{... | collective-permute-start | bytes 983048 | tf_op jit(solution)/shard_map/ppermute | solution.py:22
  107.4 19.2 %copy-start.30 = (f32[256,2048]{1,0:T(8,128)}, f32[256,2048]{1,0:T(8,128)S(1)}, u32[]{:S(2)}) copy-start(f32[256,2048]{1,0:T(8,128)S(1)} %fusion.1) | copy-start | bytes 6291460
  107.5 19.1 %collective-permute-start.9 = (bf16[128,2048]{1,0:T(8,128)(2,1)S(1)}, bf16[128,2048]{1,0:T(8,128)(2,1)}, u32[]{:S(2)}, u32[]{:S(2)}) collective-permute-start(bf16[128,2048]{1,0:T(8,128)(2,1)S(1)} %slice.55), channel_id=1, source_target_pairs={{0,2},{1,3},{2,0},{3,1},{4,6},{5,7},{6,4},{7,5},{8,10},{9,11},{10,... | collective-permute-start | bytes 1572872 | tf_op jit(solution)/shard_map/ppermute | solution.py:22
  110.1 20.4 %collective-permute-start.20 = (bf16[1,64,2048]{2,1,0:T(8,128)(2,1)S(1)}, bf16[1,64,2048]{2,1,0:T(8,128)(2,1)}, u32[]{:S(2)}, u32[]{:S(2)}) collective-permute-start(bf16[1,64,2048]{2,1,0:T(8,128)(2,1)S(1)} %fusion.15), channel_id=1, source_target_pairs={{0,16},{4,20},{8,24},{12,28},{16,0},{20,4},{24,8},{28,12},{1,17},{... | collective-permute-start | bytes 786440 | tf_op jit(solution)/shard_map/ppermute | solution.py:22
  126.6 8.4 %copy-start.28 = (f32[1,2,64,2048]{3,2,1,0:T(8,128)S(1)}, f32[1,2,64,2048]{3,2,1,0:T(8,128)}, u32[]{:S(2)}) copy-start(f32[1,2,64,2048]{3,2,1,0:T(8,128)} %copy-done.27) | copy-start | bytes 3145732
  126.6 8.4 %collective-permute-start.18 = (bf16[1,64,2048]{2,1,0:T(8,128)(2,1)}, bf16[1,64,2048]{2,1,0:T(8,128)(2,1)S(1)}, u32[]{:S(2)}, u32[]{:S(2)}) collective-permute-start(bf16[1,64,2048]{2,1,0:T(8,128)(2,1)} %shard_map.102), channel_id=1, source_target_pairs={{0,4},{4,0},{8,12},{12,8},{16,20},{20,16},{24,28},{28,24},{1,5},{5... | collective-permute-start | bytes 786440 | tf_op jit(solution)/shard_map/ppermute | solution.py:22
  (21 other events, 37.4 us)

commit v7 on v6

--- a/solution.py
+++ b/solution.py
@@ -8,6 +8,7 @@
 from jax.sharding import PartitionSpec as P
 
 LANES = 128
+FREE = pl.CostEstimate(flops=0, bytes_accessed=0, transcendentals=0)
 
 
 def wide(values):
@@ -26,18 +27,42 @@
     return lax.dynamic_index_in_dim(values, index, axis, keepdims=False)
 
 
+def pack_kernel(expert_count, tokens, cotangent, ids, probs, packed, coded, sems):
+    width = tokens.shape[1]
+    moves = [(tokens, packed.at[:, :width]), (cotangent, packed.at[:, width : 2 * width])]
+    copies = [pltpu.make_async_copy(src, dst, sems.at[k]) for k, (src, dst) in enumerate(moves)]
+    for copy in copies:
+        copy.start()
+    line = lax.broadcasted_iota(jnp.int32, (LANES, tokens.shape[0]), 0)
+    route = jnp.zeros(line.shape, jnp.float32)
+    for k in range(ids.shape[0]):
+        first = 3 * ids[k : k + 1, :]
+        hit = (line >= first) & (line < first + 3)
+        route = route + jnp.where(hit, probs[k : k + 1, :], 0.0)
+    high = wide(narrow(route))
+    middle = wide(narrow(route - high))
+    low = (route - high) - middle
+    part = lax.rem(line, 3)
+    lines = jnp.where(part == 0, high, jnp.where(part == 1, middle, low))
+    coded[...] = narrow(lines.T)
+    last = pltpu.make_async_copy(coded, packed.at[:, 2 * width :], sems.at[2])
+    last.start()
+    for copy in (*copies, last):
+        copy.wait()
+
+
 def packed(tokens, cotangent, expert_ids, gate_probs, expert_count):
-    lane = jnp.arange(LANES, dtype=jnp.int32)[None, :]
-    route = jnp.zeros((expert_ids.shape[0], LANES), jnp.float32)
-    for k in range(expert_ids.shape[1]):
-        hit = (lane < 3 * expert_count) & (lane // 3 == expert_ids[:, k : k + 1])
-        route = route + jnp.where(hit, gate_probs[:, k : k + 1], 0.0)
-    high = lax.reduce_precision(route, 8, 7)
-    middle = lax.reduce_precision(route - high, 8, 7)
-    low = (route - high) - middle
-    part = lane % 3
-    coded = jnp.where(part == 0, high, jnp.where(part == 1, middle, low))
-    return jnp.concatenate([tokens, cotangent, narrow(coded)], axis=1)
+    rows, width = tokens.shape
+    here, vmem = pl.BlockSpec(memory_space=pl.ANY), pl.BlockSpec(memory_space=pltpu.VMEM)
+    return pl.pallas_call(
+        functools.partial(pack_kernel, expert_count),
+        out_shape=jax.ShapeDtypeStruct((rows, 2 * width + LANES), jnp.bfloat16),
+        in_specs=[here, here, vmem, vmem],
+        out_specs=here,
+        scratch_shapes=[pltpu.VMEM((rows, LANES), jnp.bfloat16), pltpu.SemaphoreType.DMA((3,))],
+        compiler_params=pltpu.CompilerParams(vmem_limit_bytes=4 << 20),
+        cost_estimate=FREE,
+    )(tokens, cotangent, expert_ids.T, gate_probs.T)
 
 
 def own_columns(values, group_count, parity):
@@ -106,7 +131,6 @@
 
 
 ROWS = (((0,), (0,)), ((), ()))
-FREE = pl.CostEstimate(flops=0, bytes_accessed=0, transcendentals=0)
 
 
 def hold(values, awaited):
@@ -117,6 +141,7 @@
         in_specs=[here] * (len(values) + len(awaited)),
         out_specs=(here,) * len(values),
         input_output_aliases={k: k for k in range(len(values))},
+        compiler_params=pltpu.CompilerParams(vmem_limit_bytes=1 << 20),
         cost_estimate=FREE,
     )(*values, *awaited)
 
@@ -170,18 +195,29 @@
     rows_c = flip(rows_own, "expert", 1)
     rows_x, rows_n = flip(rows_own, "expert", 2), flip(rows_own, "dp", 2)
     residual = down_residual[0, 0].reshape(high_count, 2, 2, 2, -1, model_width)
-    res_got = flip(take(residual, 3, 1 - bit0), "dp", 1)
+
+
+    def residual_side(parity, first):
+        return take(take(residual, 2, parity), 2, first)
+
+    res_other = flip(residual_side(1 - bit1, 1 - bit0), "dp", 1)
+    res_mine = residual_side(bit1, 1 - bit0)
     place = jnp.stack([me, bit1]).astype(jnp.int32)
 
     def expert_on(*blocks):
         return expert_rows(group_count, place, blocks, gate_up, down_matrix)
 
     made = [expert_on(rows_own, rows_c)]
-    rows_x, rows_n, res_got = hold((rows_x, rows_n, res_got), (made[0][1],))
+    rows_x, rows_n, res_other, res_mine = hold(
+        (rows_x, rows_n, res_other, res_mine), (made[0][1],)
+    )
     diagonal = [flip(rows_x[:half], "dp", 2), flip(rows_n[half:], "expert", 2)]
     made += [expert_on(rows, flip(rows, "expert", 1)) for rows in (rows_x, rows_n)]
+    res_mine = flip(res_mine, "dp", 1)
     gate_early, down_early, back_sent, mark = early_terms(made)
-    *diagonal, back_sent = hold((*diagonal, back_sent), (mark,))
+    *diagonal, back_sent, res_other, res_mine = hold(
+        (*diagonal, back_sent, res_other, res_mine), (mark,)
+    )
     diagonal += [flip(rows, "expert", 1) for rows in diagonal]
 
     def terms(tok_cols, hid_cols, scaled, back):
@@ -213,13 +249,13 @@
     crossed = [
         flip(narrow(pair_sum(kept, got)), "dp", 4) for kept, got in zip(far_kept, far_got)
     ]
-    res_pair = pair_sum(take(residual, 3, bit0), res_got)
-    res_near = flip(narrow(take(res_pair, 2, 1 - bit1)), "dp", 2)
-    res_near, near_sent = hold((res_near, side(gate_term, bit2, 1 - bit0)), (far_got[0],))
-    res_sum = take(res_pair, 2, bit1) + wide(res_near)
-    far_down = pair_sum(
-        side(down_term, 1 - bit2, bit0), flip(side(down_term, 1 - bit2, 1 - bit0), "dp", 1)
-    )
+    res_near = flip(narrow(pair_sum(residual_side(1 - bit1, bit0), res_other)), "dp", 2)
+    res_near, down_sent = hold(
+        (res_near, side(down_term, 1 - bit2, 1 - bit0)), (far_got[0],)
+    )
+    (near_sent,) = hold((side(gate_term, bit2, 1 - bit0),), (far_got[1],))
+    res_sum = pair_sum(residual_side(bit1, bit0), res_mine) + wide(res_near)
+    far_down = pair_sum(side(down_term, 1 - bit2, bit0), flip(down_sent, "dp", 1))
     crossed_down = flip(narrow(far_down + take(res_sum, 1, 1 - bit2)), "dp", 4)
 
     def input_part(back):

time: 138 us -> 114 us (0.83)
  local copies, waits for them, and re-layouts: 26.2 us -> 13.2 us
  other arithmetic: 17.8 us -> 7.49 us
  matrix products: 9.72 us -> 3.98 us
  starting transfers between devices: 23.7 us -> 26.9 us
  Pallas kernels: 15.4 us -> 17.1 us
    unnamed x64 -> x34, local copies, waits for them, and re-layouts: 15.2 us -> 7.86 us
    dot_general x2, matrix products: 8.52 us -> 2.58 us  [input_part(): return narrow(jnp.dot(back, gate_up.T, preferred_element_type=jnp.float32))]
    add x2 -> x1, other arithmetic: 4.59 us -> 1.25 us  [on_device(): res_sum = pair_sum(residual_side(bit1, bit0), res_mine) + wide(res_near)]
    dynamic_slice x1 -> x0, local copies, waits for them, and re-layouts: 3.25 us -> none  [take(): return lax.dynamic_index_in_dim(values, index, axis, keepdims=False)]
    ppermute x21 -> x22, starting transfers between devices: 23.7 us -> 26.9 us  [flip(): lax.ppermute(values, axis, [(i, i ^ bit) for i in range(lax.axis_size(axi...]
    convert_element_type x7, other arithmetic: 6.79 us -> 4.01 us  [narrow(): return values.astype(jnp.bfloat16)]
    concatenate x1 -> x0, other arithmetic: 2.28 us -> none  [packed(): return jnp.concatenate([tokens, cotangent, narrow(coded)], axis=1)]
    mul x2, other arithmetic: 4.02 us -> 2.15 us  [on_device(): grad_gate_up, grad_down = (gate_sum * factor, down_sum * factor)]
  transfers between devices with their start and end apart: 21 -> 22, of which waited for: 6 -> 11; matrix products, arithmetic and copies ran while one was open for 24% -> 14% of each run, Pallas kernels for 11% -> 14%
where the time goes in v7:
time: 114 us; the launch traced here: 113 us
  waiting for transfers between devices  43.4 us (38%)
  starting transfers between devices  26.9 us (24%)
  Pallas kernels  17.1 us (15%)
  local copies, waits for them, and re-layouts  13.2 us (12%)
  other arithmetic  7.49 us (7%)
  matrix products  3.98 us (3%)
    ppermute x22, waiting for transfers between devices, flip(): lax.ppermute(values, axis, [(i, i ^ bit) for i in range(lax.axis_size(axi...  43.4 us
    ppermute x22, starting transfers between devices, flip(): lax.ppermute(values, axis, [(i, i ^ bit) for i in range(lax.axis_size(axi...  26.9 us
    pallas_call x4, Pallas kernels, expert_rows(): pl.pallas_call(functools.partial(expert_kernel, group_count), out_shape=t...  13.3 us
    unnamed x34, local copies, waits for them, and re-layouts  7.86 us
    convert_element_type x7, other arithmetic, narrow(): return values.astype(jnp.bfloat16)  4.01 us
    slice x2, local copies, waits for them, and re-layouts, on_device(): diagonal = [flip(rows_x[:half], 'dp', 2), flip(rows_n[half:], 'expert', 2)]  2.74 us
    pallas_call x1, Pallas kernels, early_terms(): pl.pallas_call(terms_kernel, out_shape=(jax.ShapeDtypeStruct((tok_cols.sh...  2.67 us
    dot_general x2, matrix products, input_part(): return narrow(jnp.dot(back, gate_up.T, preferred_element_type=jnp.float32))  2.58 us
  transfers between devices with their start and end apart: 22, of which 11 were waited for; matrix products, arithmetic and copies ran while one was open for 14% of the time, Pallas kernels for 14%

profile of v7, /device:TPU:0, one launch (start us, length us, event | category | flops | bytes accessed | tf_op | source)
XLA Modules:
  0.0 113.0 jit_solution(2416462991768203009)
XLA Ops:
  5.7 2.7 %collective-permute-start.2 = (bf16[128,4224]{1,0:T(8,128)(2,1)}, bf16[128,4224]{1,0:T(8,128)(2,1)S(1)}, u32[]{:S(2)}, u32[]{:S(2)}) collective-permute-start(bf16[128,4224]{1,0:T(8,128)(2,1)} %shard_map.94.refs_0_), channel_id=1, source_target_pairs={{0,8},{4,12},{8,0},{12,4},{16,24},{20,28},{24,16},{28,20},{1,9},{5... | collective-permute-start | bytes 3244040 | tf_op jit(solution)/shard_map/ppermute | solution.py:23
  8.3 1.5 %collective-permute-start.1 = (bf16[128,4224]{1,0:T(8,128)(2,1)}, bf16[128,4224]{1,0:T(8,128)(2,1)}, u32[]{:S(2)}, u32[]{:S(2)}) collective-permute-start(bf16[128,4224]{1,0:T(8,128)(2,1)} %shard_map.94.refs_0_), channel_id=1, source_target_pairs={{0,2},{1,3},{2,0},{3,1},{4,6},{5,7},{6,4},{7,5},{8,10},{9,11},{10,... | collective-permute-start | bytes 3244040 | tf_op jit(solution)/shard_map/ppermute | solution.py:23
  9.8 2.3 %dynamic-slice_bitcast_fusion.1 = (bf16[1,2,64,2048]{3,2,1,0:T(8,128)(2,1)}, bf16[1,2,64,2048]{3,2,1,0:T(8,128)(2,1)}) fusion(bf16[1,2,2,2,64,2048]{5,4,3,2,1,0:T(8,128)(2,1)} %bitcast.77, s32[]{:T(128)S(6)} %select_n.70, s32[]{:T(128)S(6)} %select_n.68, s32[]{:T(128)S(6)} %select_n.66), kind=kLoop, calls=%fused_computation.33 | loop fusion | bytes 2097164 | tf_op jit(solution)/shard_map/jit(dynamic_index_in_dim)/squeeze | solution.py:27
  12.1 1.5 %collective-permute-start.3 = (bf16[1,2,64,2048]{3,2,1,0:T(8,128)(2,1)}, bf16[1,2,64,2048]{3,2,1,0:T(8,128)(2,1)}, u32[]{:S(2)}, u32[]{:S(2)}) collective-permute-start(bf16[1,2,64,2048]{3,2,1,0:T(8,128)(2,1)} %get-tuple-element.74), channel_id=1, source_target_pairs={{0,4},{4,0},{8,12},{12,8},{16,20},{20,16},{24,28},{28,24},{1,5},{5... | collective-permute-start | bytes 1572872 | tf_op jit(solution)/shard_map/ppermute | solution.py:23
  13.7 2.2 %copy-done = bf16[1,2048,1024]{2,1,0:T(8,128)(2,1)S(1)} copy-done((bf16[1,2048,1024]{2,1,0:T(8,128)(2,1)S(1)}, bf16[1,2048,1024]{2,1,0:T(8,128)(2,1)}, u32[]{:S(2)}) %copy-start) | copy-done | bytes 4194328
  15.9 3.4 %shard_map.95 = (bf16[256,1024]{1,0:T(8,128)(2,1)S(1)}, bf16[256,256]{1,0:T(8,128)(2,1)S(1)}, bf16[256,2048]{1,0:T(8,128)(2,1)S(1)}, bf16[128,1024]{1,0:T(8,128)(2,1)S(1)}, bf16[128,1024]{1,0:T(8,128)(2,1)S(1)}) custom-call(s32[2]{0:T(128)S(1)} %pad_add_fusion.place, bf16[128,4224]{1,0:T(8,128)(2,1)} %shard_map.94.refs_0_, ...), custom_call_target="tpu_custom_call" | custom-call | tf_op jit(solution)/shard_map/pallas_call | solution.py:123
  19.3 6.8 %collective-permute-done.3.refs_2_ = bf16[1,2,64,2048]{3,2,1,0:T(8,128)(2,1)} collective-permute-done((bf16[1,2,64,2048]{3,2,1,0:T(8,128)(2,1)}, bf16[1,2,64,2048]{3,2,1,0:T(8,128)(2,1)}, u32[]{:S(2)}, u32[]{:S(2)}) %collective-permute-start.3) | collective-permute-done | bytes 524320 | tf_op jit(solution)/shard_map/ppermute | solution.py:23
  26.1 6.9 %collective-permute-done.2.refs_1_ = bf16[128,4224]{1,0:T(8,128)(2,1)S(1)} collective-permute-done((bf16[128,4224]{1,0:T(8,128)(2,1)}, bf16[128,4224]{1,0:T(8,128)(2,1)S(1)}, u32[]{:S(2)}, u32[]{:S(2)}) %collective-permute-start.2) | collective-permute-done | bytes 1081376 | tf_op jit(solution)/shard_map/ppermute | solution.py:23
  33.0 1.6 %collective-permute-done.1.refs_0_ = bf16[128,4224]{1,0:T(8,128)(2,1)} collective-permute-done((bf16[128,4224]{1,0:T(8,128)(2,1)}, bf16[128,4224]{1,0:T(8,128)(2,1)}, u32[]{:S(2)}, u32[]{:S(2)}) %collective-permute-start.1) | collective-permute-done | bytes 1081376 | tf_op jit(solution)/shard_map/ppermute | solution.py:23
  35.1 1.9 %slice.21 = bf16[64,4224]{1,0:T(8,128)(2,1)} slice(bf16[128,4224]{1,0:T(8,128)(2,1)} %get-tuple-element.40.refs_0_), slice={[0:64], [0:4224]} | slice | bytes 1081344 | tf_op jit(solution)/shard_map/slice | solution.py:214
  37.8 1.5 %collective-permute-start.6 = (bf16[64,4224]{1,0:T(8,128)(2,1)}, bf16[64,4224]{1,0:T(8,128)(2,1)}, u32[]{:S(2)}, u32[]{:S(2)}) collective-permute-start(bf16[64,4224]{1,0:T(8,128)(2,1)} %slice.22), channel_id=1, source_target_pairs={{0,2},{1,3},{2,0},{3,1},{4,6},{5,7},{6,4},{7,5},{8,10},{9,11},{10,... | collective-permute-start | bytes 1622024 | tf_op jit(solution)/shard_map/ppermute | solution.py:23
  39.8 1.5 %collective-permute-start.8 = (bf16[1,2,64,2048]{3,2,1,0:T(8,128)(2,1)}, bf16[1,2,64,2048]{3,2,1,0:T(8,128)(2,1)}, u32[]{:S(2)}, u32[]{:S(2)}) collective-permute-start(bf16[1,2,64,2048]{3,2,1,0:T(8,128)(2,1)} %get-tuple-element.57), channel_id=1, source_target_pairs={{0,4},{4,0},{8,12},{12,8},{16,20},{20,16},{24,28},{28,24},{1,5},{5... | collective-permute-start | bytes 1572872 | tf_op jit(solution)/shard_map/ppermute | solution.py:23
  41.3 2.2 %copy-done.1 = bf16[1,2048,1024]{2,1,0:T(8,128)(2,1)S(1)} copy-done((bf16[1,2048,1024]{2,1,0:T(8,128)(2,1)S(1)}, bf16[1,2048,1024]{2,1,0:T(8,128)(2,1)}, u32[]{:S(2)}) %copy-start.1) | copy-done | bytes 4194328
  43.5 3.4 %shard_map.97 = (bf16[256,1024]{1,0:T(8,128)(2,1)S(1)}, bf16[256,256]{1,0:T(8,128)(2,1)S(1)}, bf16[256,2048]{1,0:T(8,128)(2,1)S(1)}, bf16[128,1024]{1,0:T(8,128)(2,1)S(1)}, bf16[128,1024]{1,0:T(8,128)(2,1)S(1)}) custom-call(s32[2]{0:T(128)S(1)} %pad_add_fusion.place, bf16[128,4224]{1,0:T(8,128)(2,1)} %get-tuple-element.40.refs_0_, ...), custom_call_target="tpu_custom_call" | custom-call | tf_op jit(solution)/shard_map/pallas_call | solution.py:123
  47.0 3.3 %shard_map.98 = (bf16[256,1024]{1,0:T(8,128)(2,1)S(1)}, bf16[256,256]{1,0:T(8,128)(2,1)S(1)}, bf16[256,2048]{1,0:T(8,128)(2,1)S(1)}, bf16[128,1024]{1,0:T(8,128)(2,1)S(1)}, bf16[128,1024]{1,0:T(8,128)(2,1)S(1)}) custom-call(s32[2]{0:T(128)S(1)} %pad_add_fusion.place, bf16[128,4224]{1,0:T(8,128)(2,1)S(1)} %get-tuple-element.42.refs_0_, ...), custom_call_target="tpu_custom_call" | custom-call | tf_op jit(solution)/shard_map/pallas_call | solution.py:123
  50.3 2.7 %shard_map.99 = (f32[1024,1024]{1,0:T(8,128)S(1)}, f32[256,2048]{1,0:T(8,128)S(1)}, bf16[256,1024]{1,0:T(8,128)(2,1)S(1)}, f32[8,128]{1,0:T(8,128)S(1)}) custom-call(bf16[256,1024]{1,0:T(8,128)(2,1)S(1)} %copy-done.9, bf16[256,256]{1,0:T(8,128)(2,1)S(1)} %get-tuple-element.39.refs_4_.refs_1_, bf16[256,2048]{1,0:T(8,128)(2,1)S(1)} %copy-done.5, ...), custom_call_target="tpu_custom_call" | custom-call | tf_op jit(solution)/shard_map/pallas_call | solution.py:167
  54.1 1.4 %fusion.3 = bf16[1,2,64,2048]{3,2,1,0:T(8,128)(2,1)S(1)} fusion(bf16[1,2,64,2048]{3,2,1,0:T(8,128)(2,1)} %get-tuple-element.70, bf16[1,2,2,2,64,2048]{5,4,3,2,1,0:T(8,128)(2,1)S(1)} %bitcast.78, s32[]{:T(128)S(6)} %select_n.66, s32[]{:T(128)S(6)} %select_n.74), kind=kLoop, calls=%fused_computation.10 | loop fusion | flops 1048576 | bytes 1572872 | tf_op jit(solution)/shard_map/convert_element_type | solution.py:19
  55.5 1.6 %collective-permute-start.19 = (bf16[1,2,64,2048]{3,2,1,0:T(8,128)(2,1)S(1)}, bf16[1,2,64,2048]{3,2,1,0:T(8,128)(2,1)S(1)}, u32[]{:S(2)}, u32[]{:S(2)}) collective-permute-start(bf16[1,2,64,2048]{3,2,1,0:T(8,128)(2,1)S(1)} %fusion.3), channel_id=1, source_target_pairs={{0,8},{4,12},{8,0},{12,4},{16,24},{20,28},{24,16},{28,20},{1,9},{5... | collective-permute-start | bytes 1572872 | tf_op jit(solution)/shard_map/ppermute | solution.py:23
  58.5 3.2 %shard_map.101 = (bf16[256,1024]{1,0:T(8,128)(2,1)S(1)}, bf16[256,256]{1,0:T(8,128)(2,1)S(1)}, bf16[256,2048]{1,0:T(8,128)(2,1)S(1)}, bf16[128,1024]{1,0:T(8,128)(2,1)S(1)}, bf16[128,1024]{1,0:T(8,128)(2,1)S(1)}) custom-call(s32[2]{0:T(128)S(1)} %pad_add_fusion.place, bf16[64,4224]{1,0:T(8,128)(2,1)} %get-tuple-element.61.refs_0_, ...), custom_call_target="tpu_custom_call" | custom-call | tf_op jit(solution)/shard_map/pallas_call | solution.py:123
  63.9 1.6 %collective-permute-start.15 = (bf16[1,96,1024]{2,1,0:T(8,128)(2,1)S(1)}, bf16[1,96,1024]{2,1,0:T(8,128)(2,1)S(1)}, u32[]{:S(2)}, u32[]{:S(2)}) collective-permute-start(bf16[1,96,1024]{2,1,0:T(8,128)(2,1)S(1)} %dynamic-slice_bitcast_fusion.6), channel_id=1, source_target_pairs={{0,4},{4,0},{8,12},{12,8},{16,20},{20,16},{24,28},{28,24},{1,5},{5... | collective-permute-start | bytes 589832 | tf_op jit(solution)/shard_map/ppermute | solution.py:23
  67.0 4.7 %collective-permute-done.15.refs_2_ = bf16[1,96,1024]{2,1,0:T(8,128)(2,1)S(1)} collective-permute-done((bf16[1,96,1024]{2,1,0:T(8,128)(2,1)S(1)}, bf16[1,96,1024]{2,1,0:T(8,128)(2,1)S(1)}, u32[]{:S(2)}, u32[]{:S(2)}) %collective-permute-start.15) | collective-permute-done | bytes 196640 | tf_op jit(solution)/shard_map/ppermute | solution.py:23
  71.8 2.6 %collective-permute-start.16 = (bf16[1,96,1024]{2,1,0:T(8,128)(2,1)S(1)}, bf16[1,96,1024]{2,1,0:T(8,128)(2,1)S(1)}, u32[]{:S(2)}, u32[]{:S(2)}) collective-permute-start(bf16[1,96,1024]{2,1,0:T(8,128)(2,1)S(1)} %fusion.20), channel_id=1, source_target_pairs={{0,16},{4,20},{8,24},{12,28},{16,0},{20,4},{24,8},{28,12},{1,17},{... | collective-permute-start | bytes 589832 | tf_op jit(solution)/shard_map/ppermute | solution.py:23
  74.4 1.5 %collective-permute-start.20 = (bf16[1,64,2048]{2,1,0:T(8,128)(2,1)S(1)}, bf16[1,64,2048]{2,1,0:T(8,128)(2,1)S(1)}, u32[]{:S(2)}, u32[]{:S(2)}) collective-permute-start(bf16[1,64,2048]{2,1,0:T(8,128)(2,1)S(1)} %get-tuple-element.72), channel_id=1, source_target_pairs={{0,4},{4,0},{8,12},{12,8},{16,20},{20,16},{24,28},{28,24},{1,5},{5... | collective-permute-start | bytes 786440 | tf_op jit(solution)/shard_map/ppermute | solution.py:23
  77.2 1.5 %collective-permute-done.13.refs_1_ = bf16[1,160,1024]{2,1,0:T(8,128)(2,1)S(1)} collective-permute-done((bf16[1,160,1024]{2,1,0:T(8,128)(2,1)S(1)}, bf16[1,160,1024]{2,1,0:T(8,128)(2,1)S(1)}, u32[]{:S(2)}, u32[]{:S(2)}) %collective-permute-start.13) | collective-permute-done | bytes 327712 | tf_op jit(solution)/shard_map/ppermute | solution.py:23
  78.8 2.6 %collective-permute-start.17 = (bf16[1,160,1024]{2,1,0:T(8,128)(2,1)S(1)}, bf16[1,160,1024]{2,1,0:T(8,128)(2,1)S(1)}, u32[]{:S(2)}, u32[]{:S(2)}) collective-permute-start(bf16[1,160,1024]{2,1,0:T(8,128)(2,1)S(1)} %fusion.7), channel_id=1, source_target_pairs={{0,16},{4,20},{8,24},{12,28},{16,0},{20,4},{24,8},{28,12},{1,17},{... | collective-permute-start | bytes 983048 | tf_op jit(solution)/shard_map/ppermute | solution.py:23
  81.5 1.5 %collective-permute-start.14 = (bf16[1,256,1024]{2,1,0:T(8,128)(2,1)S(1)}, bf16[1,256,1024]{2,1,0:T(8,128)(2,1)S(1)}, u32[]{:S(2)}, u32[]{:S(2)}) collective-permute-start(bf16[1,256,1024]{2,1,0:T(8,128)(2,1)S(1)} %shard_map.102), channel_id=1, source_target_pairs={{0,4},{4,0},{8,12},{12,8},{16,20},{20,16},{24,28},{28,24},{1,5},{5... | collective-permute-start | bytes 1572872 | tf_op jit(solution)/shard_map/ppermute | solution.py:23
  85.1 2.0 %collective-permute-start.21 = (bf16[1,64,2048]{2,1,0:T(8,128)(2,1)S(1)}, bf16[1,64,2048]{2,1,0:T(8,128)(2,1)S(1)}, u32[]{:S(2)}, u32[]{:S(2)}) collective-permute-start(bf16[1,64,2048]{2,1,0:T(8,128)(2,1)S(1)} %fusion.16), channel_id=1, source_target_pairs={{0,16},{4,20},{8,24},{12,28},{16,0},{20,4},{24,8},{28,12},{1,17},{... | collective-permute-start | bytes 786440 | tf_op jit(solution)/shard_map/ppermute | solution.py:23
  87.1 8.6 %collective-permute-done.16 = bf16[1,96,1024]{2,1,0:T(8,128)(2,1)S(1)} collective-permute-done((bf16[1,96,1024]{2,1,0:T(8,128)(2,1)S(1)}, bf16[1,96,1024]{2,1,0:T(8,128)(2,1)S(1)}, u32[]{:S(2)}, u32[]{:S(2)}) %collective-permute-start.16) | collective-permute-done | bytes 196640 | tf_op jit(solution)/shard_map/ppermute | solution.py:23
  95.7 7.0 %collective-permute-done.17 = bf16[1,160,1024]{2,1,0:T(8,128)(2,1)S(1)} collective-permute-done((bf16[1,160,1024]{2,1,0:T(8,128)(2,1)S(1)}, bf16[1,160,1024]{2,1,0:T(8,128)(2,1)S(1)}, u32[]{:S(2)}, u32[]{:S(2)}) %collective-permute-start.17) | collective-permute-done | bytes 327712 | tf_op jit(solution)/shard_map/ppermute | solution.py:23
  104.0 1.5 %collective-permute-start.18 = (bf16[1,64,2048]{2,1,0:T(8,128)(2,1)S(1)}, bf16[1,64,2048]{2,1,0:T(8,128)(2,1)S(1)}, u32[]{:S(2)}, u32[]{:S(2)}) collective-permute-start(bf16[1,64,2048]{2,1,0:T(8,128)(2,1)S(1)} %shard_map.103), channel_id=1, source_target_pairs={{0,4},{4,0},{8,12},{12,8},{16,20},{20,16},{24,28},{28,24},{1,5},{5... | collective-permute-start | bytes 786440 | tf_op jit(solution)/shard_map/ppermute | solution.py:23
  106.4 1.9 %collective-permute-done.21 = bf16[1,64,2048]{2,1,0:T(8,128)(2,1)S(1)} collective-permute-done((bf16[1,64,2048]{2,1,0:T(8,128)(2,1)S(1)}, bf16[1,64,2048]{2,1,0:T(8,128)(2,1)S(1)}, u32[]{:S(2)}, u32[]{:S(2)}) %collective-permute-start.21) | collective-permute-done | bytes 262176 | tf_op jit(solution)/shard_map/ppermute | solution.py:23
  108.3 3.8 %collective-permute-done.18 = bf16[1,64,2048]{2,1,0:T(8,128)(2,1)S(1)} collective-permute-done((bf16[1,64,2048]{2,1,0:T(8,128)(2,1)S(1)}, bf16[1,64,2048]{2,1,0:T(8,128)(2,1)S(1)}, u32[]{:S(2)}, u32[]{:S(2)}) %collective-permute-start.18) | collective-permute-done | bytes 262176 | tf_op jit(solution)/shard_map/ppermute | solution.py:23
  (82 shorter events, 19.6 us)
Async XLA Ops:
  4.1 9.6 %copy-start.3 = (bf16[1,512,2048]{2,1,0:T(8,128)(2,1)S(1)}, bf16[1,512,2048]{2,1,0:T(8,128)(2,1)}, u32[]{:S(2)}) copy-start(bf16[1,512,2048]{2,1,0:T(8,128)(2,1)} %param.12) | copy-start | bytes 6291460
  5.1 8.5 %collective-permute-start = (bf16[128,4224]{1,0:T(8,128)(2,1)}, bf16[128,4224]{1,0:T(8,128)(2,1)}, u32[]{:S(2)}, u32[]{:S(2)}) collective-permute-start(bf16[128,4224]{1,0:T(8,128)(2,1)} %shard_map.94.refs_0_), channel_id=1, source_target_pairs={{0,1},{1,0},{2,3},{3,2},{4,5},{5,4},{6,7},{7,6},{8,9},{9,8},{10,11... | collective-permute-start | bytes 3244040 | tf_op jit(solution)/shard_map/ppermute | solution.py:23
  5.7 27.3 %collective-permute-start.2 = (bf16[128,4224]{1,0:T(8,128)(2,1)}, bf16[128,4224]{1,0:T(8,128)(2,1)S(1)}, u32[]{:S(2)}, u32[]{:S(2)}) collective-permute-start(bf16[128,4224]{1,0:T(8,128)(2,1)} %shard_map.94.refs_0_), channel_id=1, source_target_pairs={{0,8},{4,12},{8,0},{12,4},{16,24},{20,28},{24,16},{28,20},{1,9},{5... | collective-permute-start | bytes 3244040 | tf_op jit(solution)/shard_map/ppermute | solution.py:23
  8.3 26.2 %collective-permute-start.1 = (bf16[128,4224]{1,0:T(8,128)(2,1)}, bf16[128,4224]{1,0:T(8,128)(2,1)}, u32[]{:S(2)}, u32[]{:S(2)}) collective-permute-start(bf16[128,4224]{1,0:T(8,128)(2,1)} %shard_map.94.refs_0_), channel_id=1, source_target_pairs={{0,2},{1,3},{2,0},{3,1},{4,6},{5,7},{6,4},{7,5},{8,10},{9,11},{10,... | collective-permute-start | bytes 3244040 | tf_op jit(solution)/shard_map/ppermute | solution.py:23
  12.1 14.0 %collective-permute-start.3 = (bf16[1,2,64,2048]{3,2,1,0:T(8,128)(2,1)}, bf16[1,2,64,2048]{3,2,1,0:T(8,128)(2,1)}, u32[]{:S(2)}, u32[]{:S(2)}) collective-permute-start(bf16[1,2,64,2048]{3,2,1,0:T(8,128)(2,1)} %get-tuple-element.74), channel_id=1, source_target_pairs={{0,4},{4,0},{8,12},{12,8},{16,20},{20,16},{24,28},{28,24},{1,5},{5... | collective-permute-start | bytes 1572872 | tf_op jit(solution)/shard_map/ppermute | solution.py:23
  19.3 17.7 %copy-start.4 = (bf16[256,2048]{1,0:T(8,128)(2,1)}, bf16[256,2048]{1,0:T(8,128)(2,1)S(1)}, u32[]{:S(2)}) copy-start(bf16[256,2048]{1,0:T(8,128)(2,1)S(1)} %get-tuple-element.44.refs_2_) | copy-start | bytes 3145732
  19.3 17.7 %copy-start.8 = (bf16[256,1024]{1,0:T(8,128)(2,1)}, bf16[256,1024]{1,0:T(8,128)(2,1)S(1)}, u32[]{:S(2)}) copy-start(bf16[256,1024]{1,0:T(8,128)(2,1)S(1)} %get-tuple-element.43.refs_0_) | copy-start | bytes 1572868
  19.3 17.7 %copy-start.10 = (bf16[128,1024]{1,0:T(8,128)(2,1)}, bf16[128,1024]{1,0:T(8,128)(2,1)S(1)}, u32[]{:S(2)}) copy-start(bf16[128,1024]{1,0:T(8,128)(2,1)S(1)} %get-tuple-element.38.refs_3_) | copy-start | bytes 786436
  19.3 17.7 %copy-start.12 = (bf16[128,1024]{1,0:T(8,128)(2,1)}, bf16[128,1024]{1,0:T(8,128)(2,1)S(1)}, u32[]{:S(2)}) copy-start(bf16[128,1024]{1,0:T(8,128)(2,1)S(1)} %get-tuple-element.45.refs_4_) | copy-start | bytes 786436
  34.6 6.7 %collective-permute-start.4 = (bf16[128,4224]{1,0:T(8,128)(2,1)}, bf16[128,4224]{1,0:T(8,128)(2,1)}, u32[]{:S(2)}, u32[]{:S(2)}) collective-permute-start(bf16[128,4224]{1,0:T(8,128)(2,1)} %get-tuple-element.40.refs_0_), channel_id=1, source_target_pairs={{0,1},{1,0},{2,3},{3,2},{4,5},{5,4},{6,7},{7,6},{8,9},{9,8},{10,11... | collective-permute-start | bytes 3244040 | tf_op jit(solution)/shard_map/ppermute | solution.py:23
  34.6 12.4 %collective-permute-start.7 = (bf16[128,4224]{1,0:T(8,128)(2,1)S(1)}, bf16[128,4224]{1,0:T(8,128)(2,1)}, u32[]{:S(2)}, u32[]{:S(2)}) collective-permute-start(bf16[128,4224]{1,0:T(8,128)(2,1)S(1)} %get-tuple-element.42.refs_0_), channel_id=1, source_target_pairs={{0,1},{1,0},{2,3},{3,2},{4,5},{5,4},{6,7},{7,6},{8,9},{9,8},{10,11... | collective-permute-start | bytes 3244040 | tf_op jit(solution)/shard_map/ppermute | solution.py:23
  37.8 15.5 %collective-permute-start.6 = (bf16[64,4224]{1,0:T(8,128)(2,1)}, bf16[64,4224]{1,0:T(8,128)(2,1)}, u32[]{:S(2)}, u32[]{:S(2)}) collective-permute-start(bf16[64,4224]{1,0:T(8,128)(2,1)} %slice.22), channel_id=1, source_target_pairs={{0,2},{1,3},{2,0},{3,1},{4,6},{5,7},{6,4},{7,5},{8,10},{9,11},{10,... | collective-permute-start | bytes 1622024 | tf_op jit(solution)/shard_map/ppermute | solution.py:23
  39.3 14.2 %collective-permute-start.5 = (bf16[64,4224]{1,0:T(8,128)(2,1)}, bf16[64,4224]{1,0:T(8,128)(2,1)}, u32[]{:S(2)}, u32[]{:S(2)}) collective-permute-start(bf16[64,4224]{1,0:T(8,128)(2,1)} %slice.21), channel_id=1, source_target_pairs={{0,8},{4,12},{8,0},{12,4},{16,24},{20,28},{24,16},{28,20},{1,9},{5... | collective-permute-start | bytes 1622024 | tf_op jit(solution)/shard_map/ppermute | solution.py:23
  39.8 13.6 %collective-permute-start.8 = (bf16[1,2,64,2048]{3,2,1,0:T(8,128)(2,1)}, bf16[1,2,64,2048]{3,2,1,0:T(8,128)(2,1)}, u32[]{:S(2)}, u32[]{:S(2)}) collective-permute-start(bf16[1,2,64,2048]{3,2,1,0:T(8,128)(2,1)} %get-tuple-element.57), channel_id=1, source_target_pairs={{0,4},{4,0},{8,12},{12,8},{16,20},{20,16},{24,28},{28,24},{1,5},{5... | collective-permute-start | bytes 1572872 | tf_op jit(solution)/shard_map/ppermute | solution.py:23
  46.9 3.4 %copy-start.5 = (bf16[256,2048]{1,0:T(8,128)(2,1)S(1)}, bf16[256,2048]{1,0:T(8,128)(2,1)}, u32[]{:S(2)}) copy-start(bf16[256,2048]{1,0:T(8,128)(2,1)} %copy-done.4) | copy-start | bytes 3145732
  46.9 3.4 %copy-start.9 = (bf16[256,1024]{1,0:T(8,128)(2,1)S(1)}, bf16[256,1024]{1,0:T(8,128)(2,1)}, u32[]{:S(2)}) copy-start(bf16[256,1024]{1,0:T(8,128)(2,1)} %copy-done.8) | copy-start | bytes 1572868
  46.9 3.4 %copy-start.11 = (bf16[128,1024]{1,0:T(8,128)(2,1)S(1)}, bf16[128,1024]{1,0:T(8,128)(2,1)}, u32[]{:S(2)}) copy-start(bf16[128,1024]{1,0:T(8,128)(2,1)} %copy-done.10) | copy-start | bytes 786436
  50.3 3.7 %copy-start.16 = (bf16[1,1,512,2048]{3,2,1,0:T(8,128)(2,1)S(1)}, bf16[1,1,512,2048]{3,2,1,0:T(8,128)(2,1)}, u32[]{:S(2)}) copy-start(bf16[1,1,512,2048]{3,2,1,0:T(8,128)(2,1)} %param.13) | copy-start | bytes 6291460
  53.5 3.5 %copy-start.2 = (bf16[1,2048,1024]{2,1,0:T(8,128)(2,1)S(1)}, bf16[1,2048,1024]{2,1,0:T(8,128)(2,1)}, u32[]{:S(2)}) copy-start(bf16[1,2048,1024]{2,1,0:T(8,128)(2,1)} %param.11) | copy-start | bytes 12582916
  53.5 4.9 %collective-permute-start.11 = (bf16[64,4224]{1,0:T(8,128)(2,1)}, bf16[64,4224]{1,0:T(8,128)(2,1)S(1)}, u32[]{:S(2)}, u32[]{:S(2)}) collective-permute-start(bf16[64,4224]{1,0:T(8,128)(2,1)} %get-tuple-element.61.refs_0_), channel_id=1, source_target_pairs={{0,1},{1,0},{2,3},{3,2},{4,5},{5,4},{6,7},{7,6},{8,9},{9,8},{10,11... | collective-permute-start | bytes 1622024 | tf_op jit(solution)/shard_map/ppermute | solution.py:23
  53.5 4.9 %collective-permute-start.12 = (bf16[64,4224]{1,0:T(8,128)(2,1)}, bf16[64,4224]{1,0:T(8,128)(2,1)S(1)}, u32[]{:S(2)}, u32[]{:S(2)}) collective-permute-start(bf16[64,4224]{1,0:T(8,128)(2,1)} %get-tuple-element.62.refs_1_), channel_id=1, source_target_pairs={{0,1},{1,0},{2,3},{3,2},{4,5},{5,4},{6,7},{7,6},{8,9},{9,8},{10,11... | collective-permute-start | bytes 1622024 | tf_op jit(solution)/shard_map/ppermute | solution.py:23
  55.5 18.9 %collective-permute-start.19 = (bf16[1,2,64,2048]{3,2,1,0:T(8,128)(2,1)S(1)}, bf16[1,2,64,2048]{3,2,1,0:T(8,128)(2,1)S(1)}, u32[]{:S(2)}, u32[]{:S(2)}) collective-permute-start(bf16[1,2,64,2048]{3,2,1,0:T(8,128)(2,1)S(1)} %fusion.3), channel_id=1, source_target_pairs={{0,8},{4,12},{8,0},{12,4},{16,24},{20,28},{24,16},{28,20},{1,9},{5... | collective-permute-start | bytes 1572872 | tf_op jit(solution)/shard_map/ppermute | solution.py:23
  58.4 24.6 %collective-permute-start.9 = (bf16[256,2048]{1,0:T(8,128)(2,1)S(1)}, bf16[256,2048]{1,0:T(8,128)(2,1)S(1)}, u32[]{:S(2)}, u32[]{:S(2)}) collective-permute-start(bf16[256,2048]{1,0:T(8,128)(2,1)S(1)} %convolution_convert_fusion), channel_id=1, source_target_pairs={{0,1},{1,0},{2,3},{3,2},{4,5},{5,4},{6,7},{7,6},{8,9},{9,8},{10,11... | collective-permute-start | bytes 3145736 | tf_op jit(solution)/shard_map/ppermute | solution.py:23
  63.9 7.8 %collective-permute-start.15 = (bf16[1,96,1024]{2,1,0:T(8,128)(2,1)S(1)}, bf16[1,96,1024]{2,1,0:T(8,128)(2,1)S(1)}, u32[]{:S(2)}, u32[]{:S(2)}) collective-permute-start(bf16[1,96,1024]{2,1,0:T(8,128)(2,1)S(1)} %dynamic-slice_bitcast_fusion.6), channel_id=1, source_target_pairs={{0,4},{4,0},{8,12},{12,8},{16,20},{20,16},{24,28},{28,24},{1,5},{5... | collective-permute-start | bytes 589832 | tf_op jit(solution)/shard_map/ppermute | solution.py:23
  65.6 13.2 %collective-permute-start.13 = (bf16[1,160,1024]{2,1,0:T(8,128)(2,1)S(1)}, bf16[1,160,1024]{2,1,0:T(8,128)(2,1)S(1)}, u32[]{:S(2)}, u32[]{:S(2)}) collective-permute-start(bf16[1,160,1024]{2,1,0:T(8,128)(2,1)S(1)} %dynamic-slice_bitcast_fusion.3), channel_id=1, source_target_pairs={{0,4},{4,0},{8,12},{12,8},{16,20},{20,16},{24,28},{28,24},{1,5},{5... | collective-permute-start | bytes 983048 | tf_op jit(solution)/shard_map/ppermute | solution.py:23
  71.8 24.0 %collective-permute-start.16 = (bf16[1,96,1024]{2,1,0:T(8,128)(2,1)S(1)}, bf16[1,96,1024]{2,1,0:T(8,128)(2,1)S(1)}, u32[]{:S(2)}, u32[]{:S(2)}) collective-permute-start(bf16[1,96,1024]{2,1,0:T(8,128)(2,1)S(1)} %fusion.20), channel_id=1, source_target_pairs={{0,16},{4,20},{8,24},{12,28},{16,0},{20,4},{24,8},{28,12},{1,17},{... | collective-permute-start | bytes 589832 | tf_op jit(solution)/shard_map/ppermute | solution.py:23
  74.4 10.6 %collective-permute-start.20 = (bf16[1,64,2048]{2,1,0:T(8,128)(2,1)S(1)}, bf16[1,64,2048]{2,1,0:T(8,128)(2,1)S(1)}, u32[]{:S(2)}, u32[]{:S(2)}) collective-permute-start(bf16[1,64,2048]{2,1,0:T(8,128)(2,1)S(1)} %get-tuple-element.72), channel_id=1, source_target_pairs={{0,4},{4,0},{8,12},{12,8},{16,20},{20,16},{24,28},{28,24},{1,5},{5... | collective-permute-start | bytes 786440 | tf_op jit(solution)/shard_map/ppermute | solution.py:23
  78.8 23.9 %collective-permute-start.17 = (bf16[1,160,1024]{2,1,0:T(8,128)(2,1)S(1)}, bf16[1,160,1024]{2,1,0:T(8,128)(2,1)S(1)}, u32[]{:S(2)}, u32[]{:S(2)}) collective-permute-start(bf16[1,160,1024]{2,1,0:T(8,128)(2,1)S(1)} %fusion.7), channel_id=1, source_target_pairs={{0,16},{4,20},{8,24},{12,28},{16,0},{20,4},{24,8},{28,12},{1,17},{... | collective-permute-start | bytes 983048 | tf_op jit(solution)/shard_map/ppermute | solution.py:23
  81.5 21.3 %collective-permute-start.14 = (bf16[1,256,1024]{2,1,0:T(8,128)(2,1)S(1)}, bf16[1,256,1024]{2,1,0:T(8,128)(2,1)S(1)}, u32[]{:S(2)}, u32[]{:S(2)}) collective-permute-start(bf16[1,256,1024]{2,1,0:T(8,128)(2,1)S(1)} %shard_map.102), channel_id=1, source_target_pairs={{0,4},{4,0},{8,12},{12,8},{16,20},{20,16},{24,28},{28,24},{1,5},{5... | collective-permute-start | bytes 1572872 | tf_op jit(solution)/shard_map/ppermute | solution.py:23
  84.4 19.6 %collective-permute-start.10 = (bf16[128,2048]{1,0:T(8,128)(2,1)S(1)}, bf16[128,2048]{1,0:T(8,128)(2,1)S(1)}, u32[]{:S(2)}, u32[]{:S(2)}) collective-permute-start(bf16[128,2048]{1,0:T(8,128)(2,1)S(1)} %slice.35), channel_id=1, source_target_pairs={{0,2},{1,3},{2,0},{3,1},{4,6},{5,7},{6,4},{7,5},{8,10},{9,11},{10,... | collective-permute-start | bytes 1572872 | tf_op jit(solution)/shard_map/ppermute | solution.py:23
  85.1 23.2 %collective-permute-start.21 = (bf16[1,64,2048]{2,1,0:T(8,128)(2,1)S(1)}, bf16[1,64,2048]{2,1,0:T(8,128)(2,1)S(1)}, u32[]{:S(2)}, u32[]{:S(2)}) collective-permute-start(bf16[1,64,2048]{2,1,0:T(8,128)(2,1)S(1)} %fusion.16), channel_id=1, source_target_pairs={{0,16},{4,20},{8,24},{12,28},{16,0},{20,4},{24,8},{28,12},{1,17},{... | collective-permute-start | bytes 786440 | tf_op jit(solution)/shard_map/ppermute | solution.py:23
  104.0 8.1 %collective-permute-start.18 = (bf16[1,64,2048]{2,1,0:T(8,128)(2,1)S(1)}, bf16[1,64,2048]{2,1,0:T(8,128)(2,1)S(1)}, u32[]{:S(2)}, u32[]{:S(2)}) collective-permute-start(bf16[1,64,2048]{2,1,0:T(8,128)(2,1)S(1)} %shard_map.103), channel_id=1, source_target_pairs={{0,4},{4,0},{8,12},{12,8},{16,20},{20,16},{24,28},{28,24},{1,5},{5... | collective-permute-start | bytes 786440 | tf_op jit(solution)/shard_map/ppermute | solution.py:23
  (7 other events, 11.2 us)

commit v8 on v7

--- a/solution.py
+++ b/solution.py
@@ -8,6 +8,7 @@
 from jax.sharding import PartitionSpec as P
 
 LANES = 128
+HERE = pl.BlockSpec(memory_space=pl.ANY)
 FREE = pl.CostEstimate(flops=0, bytes_accessed=0, transcendentals=0)
 
 
@@ -27,12 +28,20 @@
     return lax.dynamic_index_in_dim(values, index, axis, keepdims=False)
 
 
-def pack_kernel(expert_count, tokens, cotangent, ids, probs, packed, coded, sems):
-    width = tokens.shape[1]
-    moves = [(tokens, packed.at[:, :width]), (cotangent, packed.at[:, width : 2 * width])]
+def begin(moves, sems):
     copies = [pltpu.make_async_copy(src, dst, sems.at[k]) for k, (src, dst) in enumerate(moves)]
     for copy in copies:
         copy.start()
+    return copies
+
+
+def pack_kernel(tokens, cotangent, ids_in, probs_in, packed, coded, ids, probs, sems):
+    width = tokens.shape[1]
+    small = begin([(ids_in, ids), (probs_in, probs)], sems)
+    moves = [(tokens, packed.at[:, :width]), (cotangent, packed.at[:, width : 2 * width])]
+    large = begin(moves, sems.at[2:4])
+    for copy in small:
+        copy.wait()
     line = lax.broadcasted_iota(jnp.int32, (LANES, tokens.shape[0]), 0)
     route = jnp.zeros(line.shape, jnp.float32)
     for k in range(ids.shape[0]):
@@ -45,22 +54,26 @@
     part = lax.rem(line, 3)
     lines = jnp.where(part == 0, high, jnp.where(part == 1, middle, low))
     coded[...] = narrow(lines.T)
-    last = pltpu.make_async_copy(coded, packed.at[:, 2 * width :], sems.at[2])
-    last.start()
-    for copy in (*copies, last):
+    last = begin([(coded, packed.at[:, 2 * width :])], sems.at[4:5])
+    for copy in (*large, *last):
         copy.wait()
 
 
-def packed(tokens, cotangent, expert_ids, gate_probs, expert_count):
+def packed(tokens, cotangent, expert_ids, gate_probs):
     rows, width = tokens.shape
-    here, vmem = pl.BlockSpec(memory_space=pl.ANY), pl.BlockSpec(memory_space=pltpu.VMEM)
+    top = expert_ids.shape[1]
     return pl.pallas_call(
-        functools.partial(pack_kernel, expert_count),
+        pack_kernel,
         out_shape=jax.ShapeDtypeStruct((rows, 2 * width + LANES), jnp.bfloat16),
-        in_specs=[here, here, vmem, vmem],
-        out_specs=here,
-        scratch_shapes=[pltpu.VMEM((rows, LANES), jnp.bfloat16), pltpu.SemaphoreType.DMA((3,))],
-        compiler_params=pltpu.CompilerParams(vmem_limit_bytes=4 << 20),
+        in_specs=[HERE] * 4,
+        out_specs=HERE,
+        scratch_shapes=[
+            pltpu.VMEM((rows, LANES), jnp.bfloat16),
+            pltpu.VMEM((top, rows), jnp.int32),
+            pltpu.VMEM((top, rows), jnp.float32),
+            pltpu.SemaphoreType.DMA((5,)),
+        ],
+        compiler_params=pltpu.CompilerParams(vmem_limit_bytes=48 << 20),
         cost_estimate=FREE,
     )(tokens, cotangent, expert_ids.T, gate_probs.T)
 
@@ -125,7 +138,7 @@
         out_shape=tuple(jax.ShapeDtypeStruct(shape, jnp.bfloat16) for shape in shapes),
         in_specs=[pl.BlockSpec(memory_space=pltpu.SMEM)] + [vmem] * (len(blocks) + 2),
         out_specs=(vmem,) * 5,
-        compiler_params=pltpu.CompilerParams(vmem_limit_bytes=24 << 20),
+        compiler_params=pltpu.CompilerParams(vmem_limit_bytes=18 << 20),
         cost_estimate=FREE,
     )(place, *blocks, gate_up, down)
 
@@ -133,14 +146,25 @@
 ROWS = (((0,), (0,)), ((), ()))
 
 
-def hold(values, awaited):
-    here = pl.BlockSpec(memory_space=pl.ANY)
+def hold_kernel(cuts, count, *refs):
+    values, cut_refs, sems = refs[:count], refs[-1 - len(cuts) : -1], refs[-1]
+    moves = [(values[k].at[rows, :], cut) for (k, rows), cut in zip(cuts, cut_refs)]
+    for copy in begin(moves, sems):
+        copy.wait()
+
+
+def hold(values, awaited, cuts=()):
+    like = [jax.ShapeDtypeStruct(v.shape, v.dtype) for v in values]
+    for k, rows in cuts:
+        shape = (rows.stop - rows.start, *values[k].shape[1:])
+        like.append(jax.ShapeDtypeStruct(shape, values[k].dtype))
     return pl.pallas_call(
-        lambda *refs: None,
-        out_shape=tuple(jax.ShapeDtypeStruct(v.shape, v.dtype) for v in values),
-        in_specs=[here] * (len(values) + len(awaited)),
-        out_specs=(here,) * len(values),
+        functools.partial(hold_kernel, cuts, len(values)),
+        out_shape=tuple(like),
+        in_specs=[HERE] * (len(values) + len(awaited)),
+        out_specs=(HERE,) * len(like),
         input_output_aliases={k: k for k in range(len(values))},
+        scratch_shapes=[pltpu.SemaphoreType.DMA((max(len(cuts), 1),))],
         compiler_params=pltpu.CompilerParams(vmem_limit_bytes=1 << 20),
         cost_estimate=FREE,
     )(*values, *awaited)
@@ -191,12 +215,15 @@
     bit0, bit1, bit2 = group & 1, (group >> 1) & 1, (group >> 2) & 1
     high_count, half = group_count // 8, tok_rows // 2
 
-    rows_own = packed(tokens, cotangent, expert_ids, gate_probs, expert_count)
+    rows_own = packed(tokens, cotangent, expert_ids, gate_probs)
     rows_c = flip(rows_own, "expert", 1)
     rows_x, rows_n = flip(rows_own, "expert", 2), flip(rows_own, "dp", 2)
     residual = down_residual[0, 0].reshape(high_count, 2, 2, 2, -1, model_width)
 
 
+    def pair_sum(kept, got):
+        return wide(kept) + wide(got)
+
     def residual_side(parity, first):
         return take(take(residual, 2, parity), 2, first)
 
@@ -208,15 +235,18 @@
         return expert_rows(group_count, place, blocks, gate_up, down_matrix)
 
     made = [expert_on(rows_own, rows_c)]
-    rows_x, rows_n, res_other, res_mine = hold(
-        (rows_x, rows_n, res_other, res_mine), (made[0][1],)
-    )
-    diagonal = [flip(rows_x[:half], "dp", 2), flip(rows_n[half:], "expert", 2)]
+    res_send = narrow(pair_sum(residual_side(1 - bit1, bit0), res_other))
+    rows_x, rows_n, res_send, res_mine, cut_x, cut_n = hold(
+        (rows_x, rows_n, res_send, res_mine),
+        (made[0][1],),
+        ((0, slice(0, half)), (1, slice(half, tok_rows))),
+    )
+    diagonal = [flip(cut_x, "dp", 2), flip(cut_n, "expert", 2)]
     made += [expert_on(rows, flip(rows, "expert", 1)) for rows in (rows_x, rows_n)]
     res_mine = flip(res_mine, "dp", 1)
     gate_early, down_early, back_sent, mark = early_terms(made)
-    *diagonal, back_sent, res_other, res_mine = hold(
-        (*diagonal, back_sent, res_other, res_mine), (mark,)
+    *diagonal, back_sent, res_send, res_mine = hold(
+        (*diagonal, back_sent, res_send, res_mine), (mark,)
     )
     diagonal += [flip(rows, "expert", 1) for rows in diagonal]
 
@@ -234,9 +264,6 @@
 
     def side(term, third, first):
         return take(take(term, 1, third), 1, first)
-
-    def pair_sum(kept, got):
-        return wide(kept) + wide(got)
 
     count = gate_term.shape[3]
     first = max(count * 3 // 8, 16)
@@ -249,7 +276,7 @@
     crossed = [
         flip(narrow(pair_sum(kept, got)), "dp", 4) for kept, got in zip(far_kept, far_got)
     ]
-    res_near = flip(narrow(pair_sum(residual_side(1 - bit1, bit0), res_other)), "dp", 2)
+    res_near = flip(res_send, "dp", 2)
     res_near, down_sent = hold(
         (res_near, side(down_term, 1 - bit2, 1 - bit0)), (far_got[0],)
     )
@@ -270,6 +297,7 @@
     near_gate = pair_sum(side(gate_term, bit2, bit0), flip(near_sent, "dp", 1))
     (near_sent,) = hold((side(down_term, bit2, 1 - bit0),), (across,))
     near_down = pair_sum(side(down_term, bit2, bit0), flip(near_sent, "dp", 1))
+    crossed[-1] = hold((crossed[-1],), (near_sent,))[0]
     gate_sum = near_gate + wide(jnp.concatenate(crossed, axis=1))
     down_sum = near_down + take(res_sum, 1, bit2) + wide(crossed_down)
     bit = 8

time: 114 us -> 113 us (level)
  matrix products: 3.98 us -> 6.47 us
  waiting for transfers between devices: 43.4 us -> 41.5 us
  starting transfers between devices: 26.9 us -> 25.3 us
    unnamed x34, local copies, waits for them, and re-layouts: 7.86 us -> 11.5 us
    slice x2 -> x0, local copies, waits for them, and re-layouts: 2.74 us -> none  [on_device(): diagonal = [flip(rows_x[:half], 'dp', 2), flip(rows_n[half:], 'expert', 2)]]
    dot_general x2, matrix products: 2.58 us -> 5.07 us  [input_part(): return narrow(jnp.dot(back, gate_up.T, preferred_element_type=jnp.float32))]
    ppermute x22, waiting for transfers between devices: 43.4 us -> 41.5 us  [flip(): lax.ppermute(values, axis, [(i, i ^ bit) for i in range(lax.axis_size(axi...]
    ppermute x22, starting transfers between devices: 26.9 us -> 25.3 us  [flip(): lax.ppermute(values, axis, [(i, i ^ bit) for i in range(lax.axis_size(axi...]
    pallas_call x6 -> x7, Pallas kernels: 1.06 us -> 2.32 us  [the longest x6 1.28 us: hold(): pl.pallas_call(functools.partial(hold_kernel, cuts, len(values)), out_sha...]
  transfers between devices with their start and end apart: 22 -> 22, of which waited for: 11 -> 9; matrix products, arithmetic and copies ran while one was open for 14% -> 13% of each run, Pallas kernels for 14% -> 14%
where the time goes in v8:
time: 113 us
  waiting for transfers between devices  41.5 us (37%)
  starting transfers between devices  25.3 us (22%)
  Pallas kernels  17.9 us (16%)
  local copies, waits for them, and re-layouts  13.1 us (12%)
  other arithmetic  7.38 us (7%)
  matrix products  6.47 us (6%)
    ppermute x22, waiting for transfers between devices, flip(): lax.ppermute(values, axis, [(i, i ^ bit) for i in range(lax.axis_size(axi...  41.5 us
    ppermute x22, starting transfers between devices, flip(): lax.ppermute(values, axis, [(i, i ^ bit) for i in range(lax.axis_size(axi...  25.3 us
    pallas_call x4, Pallas kernels, expert_rows(): pl.pallas_call(functools.partial(expert_kernel, group_count), out_shape=t...  12.9 us
    unnamed x34, local copies, waits for them, and re-layouts  11.5 us
    dot_general x2, matrix products, input_part(): return narrow(jnp.dot(back, gate_up.T, preferred_element_type=jnp.float32))  5.07 us
    convert_element_type x7, other arithmetic, narrow(): return values.astype(jnp.bfloat16)  3.9 us
    pallas_call x1, Pallas kernels, early_terms(): pl.pallas_call(terms_kernel, out_shape=(jax.ShapeDtypeStruct((tok_cols.sh...  2.71 us
  transfers between devices with their start and end apart: 22, of which 9 were waited for; matrix products, arithmetic and copies ran while one was open for 13% of the time, Pallas kernels for 14%

profile of v8, /device:TPU:0, one launch (start us, length us, event | category | flops | bytes accessed | tf_op | source)
XLA Modules:
  0.0 112.7 jit_solution(11553231865711342712)
XLA Ops:
  5.7 2.6 %collective-permute-start.1 = (bf16[128,4224]{1,0:T(8,128)(2,1)}, bf16[128,4224]{1,0:T(8,128)(2,1)}, u32[]{:S(2)}, u32[]{:S(2)}) collective-permute-start(bf16[128,4224]{1,0:T(8,128)(2,1)} %shard_map.94.refs_0_), channel_id=1, source_target_pairs={{0,2},{1,3},{2,0},{3,1},{4,6},{5,7},{6,4},{7,5},{8,10},{9,11},{10,... | collective-permute-start | bytes 3244040 | tf_op jit(solution)/shard_map/ppermute | solution.py:24
  8.2 1.6 %collective-permute-start.2 = (bf16[128,4224]{1,0:T(8,128)(2,1)}, bf16[128,4224]{1,0:T(8,128)(2,1)}, u32[]{:S(2)}, u32[]{:S(2)}) collective-permute-start(bf16[128,4224]{1,0:T(8,128)(2,1)} %shard_map.94.refs_0_), channel_id=1, source_target_pairs={{0,8},{4,12},{8,0},{12,4},{16,24},{20,28},{24,16},{28,20},{1,9},{5... | collective-permute-start | bytes 3244040 | tf_op jit(solution)/shard_map/ppermute | solution.py:24
  9.8 1.3 %dynamic-slice_bitcast_fusion.1 = (bf16[1,2,64,2048]{3,2,1,0:T(8,128)(2,1)S(1)}, bf16[1,2,64,2048]{3,2,1,0:T(8,128)(2,1)S(1)}) fusion(bf16[1,2,2,2,64,2048]{5,4,3,2,1,0:T(8,128)(2,1)} %bitcast.77, s32[]{:T(128)S(6)} %select_n.72, s32[]{:T(128)S(6)} %select_n.70, s32[]{:T(128)S(6)} %select_n.66), kind=kLoop, calls=%fused_computation.33 | loop fusion | bytes 2097164 | tf_op jit(solution)/shard_map/jit(dynamic_index_in_dim)/squeeze | solution.py:28
  11.1 1.6 %collective-permute-start.3 = (bf16[1,2,64,2048]{3,2,1,0:T(8,128)(2,1)S(1)}, bf16[1,2,64,2048]{3,2,1,0:T(8,128)(2,1)}, u32[]{:S(2)}, u32[]{:S(2)}) collective-permute-start(bf16[1,2,64,2048]{3,2,1,0:T(8,128)(2,1)S(1)} %get-tuple-element.78), channel_id=1, source_target_pairs={{0,4},{4,0},{8,12},{12,8},{16,20},{20,16},{24,28},{28,24},{1,5},{5... | collective-permute-start | bytes 1572872 | tf_op jit(solution)/shard_map/ppermute | solution.py:24
  12.7 12.2 %collective-permute-done.3 = bf16[1,2,64,2048]{3,2,1,0:T(8,128)(2,1)} collective-permute-done((bf16[1,2,64,2048]{3,2,1,0:T(8,128)(2,1)S(1)}, bf16[1,2,64,2048]{3,2,1,0:T(8,128)(2,1)}, u32[]{:S(2)}, u32[]{:S(2)}) %collective-permute-start.3) | collective-permute-done | bytes 524320 | tf_op jit(solution)/shard_map/ppermute | solution.py:24
  25.0 1.3 %fusion.6.refs_2_ = bf16[1,2,64,2048]{3,2,1,0:T(8,128)(2,1)S(1)} fusion(bf16[1,2,64,2048]{3,2,1,0:T(8,128)(2,1)} %collective-permute-done.3, bf16[1,2,2,2,64,2048]{5,4,3,2,1,0:T(8,128)(2,1)} %bitcast.78, s32[]{:T(128)S(6)} %select_n.66, s32[]{:T(128)S(6)} %select_n.68), kind=kLoop, calls=%fused_computation.15 | loop fusion | flops 1048576 | bytes 1572872 | tf_op jit(solution)/shard_map/convert_element_type | solution.py:20
  26.3 2.2 %copy-done = bf16[1,2048,1024]{2,1,0:T(8,128)(2,1)S(1)} copy-done((bf16[1,2048,1024]{2,1,0:T(8,128)(2,1)S(1)}, bf16[1,2048,1024]{2,1,0:T(8,128)(2,1)}, u32[]{:S(2)}) %copy-start) | copy-done | bytes 4194328
  28.5 3.4 %shard_map.95 = (bf16[256,1024]{1,0:T(8,128)(2,1)S(1)}, bf16[256,256]{1,0:T(8,128)(2,1)S(1)}, bf16[256,2048]{1,0:T(8,128)(2,1)S(1)}, bf16[128,1024]{1,0:T(8,128)(2,1)S(1)}, bf16[128,1024]{1,0:T(8,128)(2,1)S(1)}) custom-call(s32[2]{0:T(128)S(1)} %pad_add_fusion.place, bf16[128,4224]{1,0:T(8,128)(2,1)} %shard_map.94.refs_0_, ...), custom_call_target="tpu_custom_call" | custom-call | tf_op jit(solution)/shard_map/pallas_call | solution.py:136
  33.0 1.5 %collective-permute-done.2.refs_1_ = bf16[128,4224]{1,0:T(8,128)(2,1)} collective-permute-done((bf16[128,4224]{1,0:T(8,128)(2,1)}, bf16[128,4224]{1,0:T(8,128)(2,1)}, u32[]{:S(2)}, u32[]{:S(2)}) %collective-permute-start.2) | collective-permute-done | bytes 1081376 | tf_op jit(solution)/shard_map/ppermute | solution.py:24
  37.0 1.6 %collective-permute-start.5 = (bf16[64,4224]{1,0:T(8,128)(2,1)S(1)}, bf16[64,4224]{1,0:T(8,128)(2,1)S(1)}, u32[]{:S(2)}, u32[]{:S(2)}) collective-permute-start(bf16[64,4224]{1,0:T(8,128)(2,1)S(1)} %get-tuple-element.44), channel_id=1, source_target_pairs={{0,8},{4,12},{8,0},{12,4},{16,24},{20,28},{24,16},{28,20},{1,9},{5... | collective-permute-start | bytes 1622024 | tf_op jit(solution)/shard_map/ppermute | solution.py:24
  39.1 1.5 %collective-permute-start.8 = (bf16[1,2,64,2048]{3,2,1,0:T(8,128)(2,1)}, bf16[1,2,64,2048]{3,2,1,0:T(8,128)(2,1)S(1)}, u32[]{:S(2)}, u32[]{:S(2)}) collective-permute-start(bf16[1,2,64,2048]{3,2,1,0:T(8,128)(2,1)} %copy-done.9), channel_id=1, source_target_pairs={{0,4},{4,0},{8,12},{12,8},{16,20},{20,16},{24,28},{28,24},{1,5},{5... | collective-permute-start | bytes 1572872 | tf_op jit(solution)/shard_map/ppermute | solution.py:24
  40.7 3.1 %shard_map.98 = (bf16[256,1024]{1,0:T(8,128)(2,1)S(1)}, bf16[256,256]{1,0:T(8,128)(2,1)S(1)}, bf16[256,2048]{1,0:T(8,128)(2,1)S(1)}, bf16[128,1024]{1,0:T(8,128)(2,1)S(1)}, bf16[128,1024]{1,0:T(8,128)(2,1)S(1)}) custom-call(s32[2]{0:T(128)S(1)} %pad_add_fusion.place, bf16[128,4224]{1,0:T(8,128)(2,1)} %get-tuple-element.53.refs_0_, ...), custom_call_target="tpu_custom_call" | custom-call | tf_op jit(solution)/shard_map/pallas_call | solution.py:136
  43.8 3.1 %shard_map.97 = (bf16[256,1024]{1,0:T(8,128)(2,1)S(1)}, bf16[256,256]{1,0:T(8,128)(2,1)S(1)}, bf16[256,2048]{1,0:T(8,128)(2,1)S(1)}, bf16[128,1024]{1,0:T(8,128)(2,1)S(1)}, bf16[128,1024]{1,0:T(8,128)(2,1)S(1)}) custom-call(s32[2]{0:T(128)S(1)} %pad_add_fusion.place, bf16[128,4224]{1,0:T(8,128)(2,1)} %get-tuple-element.42.refs_0_, ...), custom_call_target="tpu_custom_call" | custom-call | tf_op jit(solution)/shard_map/pallas_call | solution.py:136
  46.9 2.7 %shard_map.99 = (f32[1024,1024]{1,0:T(8,128)S(1)}, f32[256,2048]{1,0:T(8,128)S(1)}, bf16[256,1024]{1,0:T(8,128)(2,1)S(1)}, f32[8,128]{1,0:T(8,128)S(1)}) custom-call(bf16[256,1024]{1,0:T(8,128)(2,1)S(1)} %get-tuple-element.46.refs_0_, bf16[256,256]{1,0:T(8,128)(2,1)S(1)} %get-tuple-element.41.refs_4_.refs_1_, ...), custom_call_target="tpu_custom_call" | custom-call | tf_op jit(solution)/shard_map/pallas_call | solution.py:191
  49.6 2.0 %copy-done.3 = f32[1024,1024]{1,0:T(8,128)} copy-done((f32[1024,1024]{1,0:T(8,128)}, f32[1024,1024]{1,0:T(8,128)S(1)}, u32[]{:S(2)}) %copy-start.3) | copy-done | bytes 4194328
  55.5 3.8 %convolution_convert_fusion = bf16[256,2048]{1,0:T(8,128)(2,1)S(1)} fusion(bf16[256,1024]{1,0:T(8,128)(2,1)} %copy-done.12, bf16[1,2048,1024]{2,1,0:T(8,128)(2,1)} %param.11), kind=kOutput, calls=%fused_computation.1 | convolution fusion | flops 1074266112 | bytes 5767168 | tf_op jit(solution)/shard_map/dot_general | solution.py:289
  59.4 3.3 %shard_map.101 = (bf16[256,1024]{1,0:T(8,128)(2,1)S(1)}, bf16[256,256]{1,0:T(8,128)(2,1)S(1)}, bf16[256,2048]{1,0:T(8,128)(2,1)S(1)}, bf16[128,1024]{1,0:T(8,128)(2,1)S(1)}, bf16[128,1024]{1,0:T(8,128)(2,1)S(1)}) custom-call(s32[2]{0:T(128)S(1)} %pad_add_fusion.place, bf16[64,4224]{1,0:T(8,128)(2,1)S(1)} %get-tuple-element.65.refs_0_, ...), custom_call_target="tpu_custom_call" | custom-call | tf_op jit(solution)/shard_map/pallas_call | solution.py:136
  63.7 1.2 %copy-done.4 = f32[1024,1024]{1,0:T(8,128)S(1)} copy-done((f32[1024,1024]{1,0:T(8,128)S(1)}, f32[1024,1024]{1,0:T(8,128)}, u32[]{:S(2)}) %copy-start.4) | copy-done | bytes 4194328
  66.2 1.5 %collective-permute-start.15 = (bf16[1,96,1024]{2,1,0:T(8,128)(2,1)S(1)}, bf16[1,96,1024]{2,1,0:T(8,128)(2,1)S(1)}, u32[]{:S(2)}, u32[]{:S(2)}) collective-permute-start(bf16[1,96,1024]{2,1,0:T(8,128)(2,1)S(1)} %dynamic-slice_bitcast_fusion.6), channel_id=1, source_target_pairs={{0,4},{4,0},{8,12},{12,8},{16,20},{20,16},{24,28},{28,24},{1,5},{5... | collective-permute-start | bytes 589832 | tf_op jit(solution)/shard_map/ppermute | solution.py:24
  69.3 4.7 %collective-permute-done.15.refs_2_ = bf16[1,96,1024]{2,1,0:T(8,128)(2,1)S(1)} collective-permute-done((bf16[1,96,1024]{2,1,0:T(8,128)(2,1)S(1)}, bf16[1,96,1024]{2,1,0:T(8,128)(2,1)S(1)}, u32[]{:S(2)}, u32[]{:S(2)}) %collective-permute-start.15) | collective-permute-done | bytes 196640 | tf_op jit(solution)/shard_map/ppermute | solution.py:24
  74.0 1.5 %collective-permute-start.20 = (bf16[1,64,2048]{2,1,0:T(8,128)(2,1)S(1)}, bf16[1,64,2048]{2,1,0:T(8,128)(2,1)S(1)}, u32[]{:S(2)}, u32[]{:S(2)}) collective-permute-start(bf16[1,64,2048]{2,1,0:T(8,128)(2,1)S(1)} %get-tuple-element.76), channel_id=1, source_target_pairs={{0,4},{4,0},{8,12},{12,8},{16,20},{20,16},{24,28},{28,24},{1,5},{5... | collective-permute-start | bytes 786440 | tf_op jit(solution)/shard_map/ppermute | solution.py:24
  75.6 2.7 %collective-permute-start.16 = (bf16[1,96,1024]{2,1,0:T(8,128)(2,1)S(1)}, bf16[1,96,1024]{2,1,0:T(8,128)(2,1)S(1)}, u32[]{:S(2)}, u32[]{:S(2)}) collective-permute-start(bf16[1,96,1024]{2,1,0:T(8,128)(2,1)S(1)} %fusion.20), channel_id=1, source_target_pairs={{0,16},{4,20},{8,24},{12,28},{16,0},{20,4},{24,8},{28,12},{1,17},{... | collective-permute-start | bytes 589832 | tf_op jit(solution)/shard_map/ppermute | solution.py:24
  78.2 1.2 %fusion.3 = f32[1,2,64,2048]{3,2,1,0:T(8,128)S(1)} fusion(bf16[1,2,64,2048]{3,2,1,0:T(8,128)(2,1)S(1)} %get-tuple-element.75, bf16[1,2,64,2048]{3,2,1,0:T(8,128)(2,1)S(1)} %copy-done.8, bf16[1,2,2,2,64,2048]{5,4,3,2,1,0:T(8,128)(2,1)} %bitcast.79, s32[]{:T(128)S(6)} %select_n.72, s32[]{:T(128)S(6)} %select_n.68), kind=kLoop, calls=%fused_computation.10 | loop fusion | flops 1310720 | bytes 2621448 | tf_op jit(solution)/shard_map/add | solution.py:284
  79.5 1.3 %fusion.1 = f32[256,2048]{1,0:T(8,128)S(1)} fusion(bf16[256,2048]{1,0:T(8,128)(2,1)S(1)} %collective-permute-done.9, bf16[128,1024]{1,0:T(8,128)(2,1)S(1)} %copy-done.14, bf16[128,1024]{1,0:T(8,128)(2,1)S(1)} %get-tuple-element.40.refs_3_, bf16[1,2048,1024]{2,1,0:T(8,128)(2,1)S(1)} %copy-done.1), kind=kOutput, calls=%fused_computation.4 | convolution fusion | flops 1076887552 | bytes 7864320 | tf_op jit(solution)/shard_map/dot_general | solution.py:289
  80.9 1.4 %collective-permute-start.10 = (bf16[128,2048]{1,0:T(8,128)(2,1)S(1)}, bf16[128,2048]{1,0:T(8,128)(2,1)S(1)}, u32[]{:S(2)}, u32[]{:S(2)}) collective-permute-start(bf16[128,2048]{1,0:T(8,128)(2,1)S(1)} %slice.27), channel_id=1, source_target_pairs={{0,2},{1,3},{2,0},{3,1},{4,6},{5,7},{6,4},{7,5},{8,10},{9,11},{10,... | collective-permute-start | bytes 1572872 | tf_op jit(solution)/shard_map/ppermute | solution.py:24
  82.4 1.4 %collective-permute-start.17 = (bf16[1,160,1024]{2,1,0:T(8,128)(2,1)S(1)}, bf16[1,160,1024]{2,1,0:T(8,128)(2,1)S(1)}, u32[]{:S(2)}, u32[]{:S(2)}) collective-permute-start(bf16[1,160,1024]{2,1,0:T(8,128)(2,1)S(1)} %fusion.7), channel_id=1, source_target_pairs={{0,16},{4,20},{8,24},{12,28},{16,0},{20,4},{24,8},{28,12},{1,17},{... | collective-permute-start | bytes 983048 | tf_op jit(solution)/shard_map/ppermute | solution.py:24
  83.8 1.5 %collective-permute-start.14 = (bf16[1,256,1024]{2,1,0:T(8,128)(2,1)S(1)}, bf16[1,256,1024]{2,1,0:T(8,128)(2,1)S(1)}, u32[]{:S(2)}, u32[]{:S(2)}) collective-permute-start(bf16[1,256,1024]{2,1,0:T(8,128)(2,1)S(1)} %shard_map.102), channel_id=1, source_target_pairs={{0,4},{4,0},{8,12},{12,8},{16,20},{20,16},{24,28},{28,24},{1,5},{5... | collective-permute-start | bytes 1572872 | tf_op jit(solution)/shard_map/ppermute | solution.py:24
  85.3 1.4 %collective-permute-done.20 = bf16[1,64,2048]{2,1,0:T(8,128)(2,1)S(1)} collective-permute-done((bf16[1,64,2048]{2,1,0:T(8,128)(2,1)S(1)}, bf16[1,64,2048]{2,1,0:T(8,128)(2,1)S(1)}, u32[]{:S(2)}, u32[]{:S(2)}) %collective-permute-start.20) | collective-permute-done | bytes 262176 | tf_op jit(solution)/shard_map/ppermute | solution.py:24
  86.7 2.7 %collective-permute-start.21 = (bf16[1,64,2048]{2,1,0:T(8,128)(2,1)S(1)}, bf16[1,64,2048]{2,1,0:T(8,128)(2,1)S(1)}, u32[]{:S(2)}, u32[]{:S(2)}) collective-permute-start(bf16[1,64,2048]{2,1,0:T(8,128)(2,1)S(1)} %fusion.16), channel_id=1, source_target_pairs={{0,16},{4,20},{8,24},{12,28},{16,0},{20,4},{24,8},{28,12},{1,17},{... | collective-permute-start | bytes 786440 | tf_op jit(solution)/shard_map/ppermute | solution.py:24
  89.4 4.1 %collective-permute-done.10.refs_1_ = bf16[128,2048]{1,0:T(8,128)(2,1)S(1)} collective-permute-done((bf16[128,2048]{1,0:T(8,128)(2,1)S(1)}, bf16[128,2048]{1,0:T(8,128)(2,1)S(1)}, u32[]{:S(2)}, u32[]{:S(2)}) %collective-permute-start.10) | collective-permute-done | bytes 524320 | tf_op jit(solution)/shard_map/ppermute | solution.py:24
  95.1 12.1 %collective-permute-done.17.refs_0_ = bf16[1,160,1024]{2,1,0:T(8,128)(2,1)S(1)} collective-permute-done((bf16[1,160,1024]{2,1,0:T(8,128)(2,1)S(1)}, bf16[1,160,1024]{2,1,0:T(8,128)(2,1)S(1)}, u32[]{:S(2)}, u32[]{:S(2)}) %collective-permute-start.17) | collective-permute-done | bytes 327712 | tf_op jit(solution)/shard_map/ppermute | solution.py:24
  108.5 3.3 %collective-permute-done.21 = bf16[1,64,2048]{2,1,0:T(8,128)(2,1)S(1)} collective-permute-done((bf16[1,64,2048]{2,1,0:T(8,128)(2,1)S(1)}, bf16[1,64,2048]{2,1,0:T(8,128)(2,1)S(1)}, u32[]{:S(2)}, u32[]{:S(2)}) %collective-permute-start.21) | collective-permute-done | bytes 262176 | tf_op jit(solution)/shard_map/ppermute | solution.py:24
  (81 shorter events, 21.1 us)
Async XLA Ops:
  5.1 21.2 %copy-start.2 = (bf16[1,512,2048]{2,1,0:T(8,128)(2,1)S(1)}, bf16[1,512,2048]{2,1,0:T(8,128)(2,1)}, u32[]{:S(2)}) copy-start(bf16[1,512,2048]{2,1,0:T(8,128)(2,1)} %param.12) | copy-start | bytes 6291460
  5.1 21.2 %collective-permute-start = (bf16[128,4224]{1,0:T(8,128)(2,1)}, bf16[128,4224]{1,0:T(8,128)(2,1)}, u32[]{:S(2)}, u32[]{:S(2)}) collective-permute-start(bf16[128,4224]{1,0:T(8,128)(2,1)} %shard_map.94.refs_0_), channel_id=1, source_target_pairs={{0,1},{1,0},{2,3},{3,2},{4,5},{5,4},{6,7},{7,6},{8,9},{9,8},{10,11... | collective-permute-start | bytes 3244040 | tf_op jit(solution)/shard_map/ppermute | solution.py:24
  5.7 27.3 %collective-permute-start.1 = (bf16[128,4224]{1,0:T(8,128)(2,1)}, bf16[128,4224]{1,0:T(8,128)(2,1)}, u32[]{:S(2)}, u32[]{:S(2)}) collective-permute-start(bf16[128,4224]{1,0:T(8,128)(2,1)} %shard_map.94.refs_0_), channel_id=1, source_target_pairs={{0,2},{1,3},{2,0},{3,1},{4,6},{5,7},{6,4},{7,5},{8,10},{9,11},{10,... | collective-permute-start | bytes 3244040 | tf_op jit(solution)/shard_map/ppermute | solution.py:24
  8.2 26.2 %collective-permute-start.2 = (bf16[128,4224]{1,0:T(8,128)(2,1)}, bf16[128,4224]{1,0:T(8,128)(2,1)}, u32[]{:S(2)}, u32[]{:S(2)}) collective-permute-start(bf16[128,4224]{1,0:T(8,128)(2,1)} %shard_map.94.refs_0_), channel_id=1, source_target_pairs={{0,8},{4,12},{8,0},{12,4},{16,24},{20,28},{24,16},{28,20},{1,9},{5... | collective-permute-start | bytes 3244040 | tf_op jit(solution)/shard_map/ppermute | solution.py:24
  11.1 13.9 %collective-permute-start.3 = (bf16[1,2,64,2048]{3,2,1,0:T(8,128)(2,1)S(1)}, bf16[1,2,64,2048]{3,2,1,0:T(8,128)(2,1)}, u32[]{:S(2)}, u32[]{:S(2)}) collective-permute-start(bf16[1,2,64,2048]{3,2,1,0:T(8,128)(2,1)S(1)} %get-tuple-element.78), channel_id=1, source_target_pairs={{0,4},{4,0},{8,12},{12,8},{16,20},{20,16},{24,28},{28,24},{1,5},{5... | collective-permute-start | bytes 1572872 | tf_op jit(solution)/shard_map/ppermute | solution.py:24
  26.3 2.2 %copy-start = (bf16[1,2048,1024]{2,1,0:T(8,128)(2,1)S(1)}, bf16[1,2048,1024]{2,1,0:T(8,128)(2,1)}, u32[]{:S(2)}) copy-start(bf16[1,2048,1024]{2,1,0:T(8,128)(2,1)} %param.11) | copy-start | bytes 12582916
  36.5 4.1 %collective-permute-start.7 = (bf16[128,4224]{1,0:T(8,128)(2,1)}, bf16[128,4224]{1,0:T(8,128)(2,1)S(1)}, u32[]{:S(2)}, u32[]{:S(2)}) collective-permute-start(bf16[128,4224]{1,0:T(8,128)(2,1)} %get-tuple-element.53.refs_0_), channel_id=1, source_target_pairs={{0,1},{1,0},{2,3},{3,2},{4,5},{5,4},{6,7},{7,6},{8,9},{9,8},{10,11... | collective-permute-start | bytes 3244040 | tf_op jit(solution)/shard_map/ppermute | solution.py:24
  36.5 7.2 %collective-permute-start.4 = (bf16[128,4224]{1,0:T(8,128)(2,1)}, bf16[128,4224]{1,0:T(8,128)(2,1)S(1)}, u32[]{:S(2)}, u32[]{:S(2)}) collective-permute-start(bf16[128,4224]{1,0:T(8,128)(2,1)} %get-tuple-element.42.refs_0_), channel_id=1, source_target_pairs={{0,1},{1,0},{2,3},{3,2},{4,5},{5,4},{6,7},{7,6},{8,9},{9,8},{10,11... | collective-permute-start | bytes 3244040 | tf_op jit(solution)/shard_map/ppermute | solution.py:24
  37.0 15.6 %collective-permute-start.5 = (bf16[64,4224]{1,0:T(8,128)(2,1)S(1)}, bf16[64,4224]{1,0:T(8,128)(2,1)S(1)}, u32[]{:S(2)}, u32[]{:S(2)}) collective-permute-start(bf16[64,4224]{1,0:T(8,128)(2,1)S(1)} %get-tuple-element.44), channel_id=1, source_target_pairs={{0,8},{4,12},{8,0},{12,4},{16,24},{20,28},{24,16},{28,20},{1,9},{5... | collective-permute-start | bytes 1622024 | tf_op jit(solution)/shard_map/ppermute | solution.py:24
  38.6 14.0 %collective-permute-start.6 = (bf16[64,4224]{1,0:T(8,128)(2,1)S(1)}, bf16[64,4224]{1,0:T(8,128)(2,1)}, u32[]{:S(2)}, u32[]{:S(2)}) collective-permute-start(bf16[64,4224]{1,0:T(8,128)(2,1)S(1)} %get-tuple-element.45), channel_id=1, source_target_pairs={{0,2},{1,3},{2,0},{3,1},{4,6},{5,7},{6,4},{7,5},{8,10},{9,11},{10,... | collective-permute-start | bytes 1622024 | tf_op jit(solution)/shard_map/ppermute | solution.py:24
  39.1 13.5 %collective-permute-start.8 = (bf16[1,2,64,2048]{3,2,1,0:T(8,128)(2,1)}, bf16[1,2,64,2048]{3,2,1,0:T(8,128)(2,1)S(1)}, u32[]{:S(2)}, u32[]{:S(2)}) collective-permute-start(bf16[1,2,64,2048]{3,2,1,0:T(8,128)(2,1)} %copy-done.9), channel_id=1, source_target_pairs={{0,4},{4,0},{8,12},{12,8},{16,20},{20,16},{24,28},{28,24},{1,5},{5... | collective-permute-start | bytes 1572872 | tf_op jit(solution)/shard_map/ppermute | solution.py:24
  46.9 2.7 %copy-start.13 = (bf16[128,1024]{1,0:T(8,128)(2,1)}, bf16[128,1024]{1,0:T(8,128)(2,1)S(1)}, u32[]{:S(2)}) copy-start(bf16[128,1024]{1,0:T(8,128)(2,1)S(1)} %get-tuple-element.43.refs_8_) | copy-start | bytes 786436
  49.6 2.0 %copy-start.3 = (f32[1024,1024]{1,0:T(8,128)}, f32[1024,1024]{1,0:T(8,128)S(1)}, u32[]{:S(2)}) copy-start(f32[1024,1024]{1,0:T(8,128)S(1)} %get-tuple-element.64) | copy-start | bytes 12582916
  51.6 1.4 %copy-start.5 = (f32[256,2048]{1,0:T(8,128)}, f32[256,2048]{1,0:T(8,128)S(1)}, u32[]{:S(2)}) copy-start(f32[256,2048]{1,0:T(8,128)S(1)} %get-tuple-element.70) | copy-start | bytes 6291460
  54.5 4.8 %collective-permute-start.11 = (bf16[64,4224]{1,0:T(8,128)(2,1)S(1)}, bf16[64,4224]{1,0:T(8,128)(2,1)}, u32[]{:S(2)}, u32[]{:S(2)}) collective-permute-start(bf16[64,4224]{1,0:T(8,128)(2,1)S(1)} %get-tuple-element.65.refs_0_), channel_id=1, source_target_pairs={{0,1},{1,0},{2,3},{3,2},{4,5},{5,4},{6,7},{7,6},{8,9},{9,8},{10,11... | collective-permute-start | bytes 1622024 | tf_op jit(solution)/shard_map/ppermute | solution.py:24
  54.5 4.8 %collective-permute-start.12 = (bf16[64,4224]{1,0:T(8,128)(2,1)}, bf16[64,4224]{1,0:T(8,128)(2,1)}, u32[]{:S(2)}, u32[]{:S(2)}) collective-permute-start(bf16[64,4224]{1,0:T(8,128)(2,1)} %get-tuple-element.66.refs_1_), channel_id=1, source_target_pairs={{0,1},{1,0},{2,3},{3,2},{4,5},{5,4},{6,7},{7,6},{8,9},{9,8},{10,11... | collective-permute-start | bytes 1622024 | tf_op jit(solution)/shard_map/ppermute | solution.py:24
  55.0 14.3 %collective-permute-start.19 = (bf16[1,2,64,2048]{3,2,1,0:T(8,128)(2,1)S(1)}, bf16[1,2,64,2048]{3,2,1,0:T(8,128)(2,1)S(1)}, u32[]{:S(2)}, u32[]{:S(2)}) collective-permute-start(bf16[1,2,64,2048]{3,2,1,0:T(8,128)(2,1)S(1)} %get-tuple-element.74), channel_id=1, source_target_pairs={{0,8},{4,12},{8,0},{12,4},{16,24},{20,28},{24,16},{28,20},{1,9},{5... | collective-permute-start | bytes 1572872 | tf_op jit(solution)/shard_map/ppermute | solution.py:24
  55.5 3.9 %copy-start.1 = (bf16[1,2048,1024]{2,1,0:T(8,128)(2,1)S(1)}, bf16[1,2048,1024]{2,1,0:T(8,128)(2,1)}, u32[]{:S(2)}) copy-start(bf16[1,2048,1024]{2,1,0:T(8,128)(2,1)} %param.11) | copy-start | bytes 12582916
  59.3 20.2 %collective-permute-start.9 = (bf16[256,2048]{1,0:T(8,128)(2,1)S(1)}, bf16[256,2048]{1,0:T(8,128)(2,1)S(1)}, u32[]{:S(2)}, u32[]{:S(2)}) collective-permute-start(bf16[256,2048]{1,0:T(8,128)(2,1)S(1)} %convolution_convert_fusion), channel_id=1, source_target_pairs={{0,1},{1,0},{2,3},{3,2},{4,5},{5,4},{6,7},{7,6},{8,9},{9,8},{10,11... | collective-permute-start | bytes 3145736 | tf_op jit(solution)/shard_map/ppermute | solution.py:24
  62.7 2.2 %copy-start.4 = (f32[1024,1024]{1,0:T(8,128)S(1)}, f32[1024,1024]{1,0:T(8,128)}, u32[]{:S(2)}) copy-start(f32[1024,1024]{1,0:T(8,128)} %copy-done.3) | copy-start | bytes 12582916
  66.2 2.7 %copy-start.6 = (f32[256,2048]{1,0:T(8,128)S(1)}, f32[256,2048]{1,0:T(8,128)}, u32[]{:S(2)}) copy-start(f32[256,2048]{1,0:T(8,128)} %copy-done.5) | copy-start | bytes 6291460
  66.2 7.8 %collective-permute-start.15 = (bf16[1,96,1024]{2,1,0:T(8,128)(2,1)S(1)}, bf16[1,96,1024]{2,1,0:T(8,128)(2,1)S(1)}, u32[]{:S(2)}, u32[]{:S(2)}) collective-permute-start(bf16[1,96,1024]{2,1,0:T(8,128)(2,1)S(1)} %dynamic-slice_bitcast_fusion.6), channel_id=1, source_target_pairs={{0,4},{4,0},{8,12},{12,8},{16,20},{20,16},{24,28},{28,24},{1,5},{5... | collective-permute-start | bytes 589832 | tf_op jit(solution)/shard_map/ppermute | solution.py:24
  67.7 14.5 %collective-permute-start.13 = (bf16[1,160,1024]{2,1,0:T(8,128)(2,1)S(1)}, bf16[1,160,1024]{2,1,0:T(8,128)(2,1)S(1)}, u32[]{:S(2)}, u32[]{:S(2)}) collective-permute-start(bf16[1,160,1024]{2,1,0:T(8,128)(2,1)S(1)} %dynamic-slice_bitcast_fusion.3), channel_id=1, source_target_pairs={{0,4},{4,0},{8,12},{12,8},{16,20},{20,16},{24,28},{28,24},{1,5},{5... | collective-permute-start | bytes 983048 | tf_op jit(solution)/shard_map/ppermute | solution.py:24
  69.2 9.0 %copy-start.8 = (bf16[1,2,64,2048]{3,2,1,0:T(8,128)(2,1)S(1)}, bf16[1,2,64,2048]{3,2,1,0:T(8,128)(2,1)}, u32[]{:S(2)}) copy-start(bf16[1,2,64,2048]{3,2,1,0:T(8,128)(2,1)} %copy-done.7) | copy-start | bytes 1572868
  74.0 5.5 %copy-start.14 = (bf16[128,1024]{1,0:T(8,128)(2,1)S(1)}, bf16[128,1024]{1,0:T(8,128)(2,1)}, u32[]{:S(2)}) copy-start(bf16[128,1024]{1,0:T(8,128)(2,1)} %copy-done.13) | copy-start | bytes 786436
  74.0 12.6 %collective-permute-start.20 = (bf16[1,64,2048]{2,1,0:T(8,128)(2,1)S(1)}, bf16[1,64,2048]{2,1,0:T(8,128)(2,1)S(1)}, u32[]{:S(2)}, u32[]{:S(2)}) collective-permute-start(bf16[1,64,2048]{2,1,0:T(8,128)(2,1)S(1)} %get-tuple-element.76), channel_id=1, source_target_pairs={{0,4},{4,0},{8,12},{12,8},{16,20},{20,16},{24,28},{28,24},{1,5},{5... | collective-permute-start | bytes 786440 | tf_op jit(solution)/shard_map/ppermute | solution.py:24
  75.6 31.7 %collective-permute-start.16 = (bf16[1,96,1024]{2,1,0:T(8,128)(2,1)S(1)}, bf16[1,96,1024]{2,1,0:T(8,128)(2,1)S(1)}, u32[]{:S(2)}, u32[]{:S(2)}) collective-permute-start(bf16[1,96,1024]{2,1,0:T(8,128)(2,1)S(1)} %fusion.20), channel_id=1, source_target_pairs={{0,16},{4,20},{8,24},{12,28},{16,0},{20,4},{24,8},{28,12},{1,17},{... | collective-permute-start | bytes 589832 | tf_op jit(solution)/shard_map/ppermute | solution.py:24
  80.9 12.6 %collective-permute-start.10 = (bf16[128,2048]{1,0:T(8,128)(2,1)S(1)}, bf16[128,2048]{1,0:T(8,128)(2,1)S(1)}, u32[]{:S(2)}, u32[]{:S(2)}) collective-permute-start(bf16[128,2048]{1,0:T(8,128)(2,1)S(1)} %slice.27), channel_id=1, source_target_pairs={{0,2},{1,3},{2,0},{3,1},{4,6},{5,7},{6,4},{7,5},{8,10},{9,11},{10,... | collective-permute-start | bytes 1572872 | tf_op jit(solution)/shard_map/ppermute | solution.py:24
  82.4 24.9 %collective-permute-start.17 = (bf16[1,160,1024]{2,1,0:T(8,128)(2,1)S(1)}, bf16[1,160,1024]{2,1,0:T(8,128)(2,1)S(1)}, u32[]{:S(2)}, u32[]{:S(2)}) collective-permute-start(bf16[1,160,1024]{2,1,0:T(8,128)(2,1)S(1)} %fusion.7), channel_id=1, source_target_pairs={{0,16},{4,20},{8,24},{12,28},{16,0},{20,4},{24,8},{28,12},{1,17},{... | collective-permute-start | bytes 983048 | tf_op jit(solution)/shard_map/ppermute | solution.py:24
  83.8 23.4 %collective-permute-start.14 = (bf16[1,256,1024]{2,1,0:T(8,128)(2,1)S(1)}, bf16[1,256,1024]{2,1,0:T(8,128)(2,1)S(1)}, u32[]{:S(2)}, u32[]{:S(2)}) collective-permute-start(bf16[1,256,1024]{2,1,0:T(8,128)(2,1)S(1)} %shard_map.102), channel_id=1, source_target_pairs={{0,4},{4,0},{8,12},{12,8},{16,20},{20,16},{24,28},{28,24},{1,5},{5... | collective-permute-start | bytes 1572872 | tf_op jit(solution)/shard_map/ppermute | solution.py:24
  86.7 25.1 %collective-permute-start.21 = (bf16[1,64,2048]{2,1,0:T(8,128)(2,1)S(1)}, bf16[1,64,2048]{2,1,0:T(8,128)(2,1)S(1)}, u32[]{:S(2)}, u32[]{:S(2)}) collective-permute-start(bf16[1,64,2048]{2,1,0:T(8,128)(2,1)S(1)} %fusion.16), channel_id=1, source_target_pairs={{0,16},{4,20},{8,24},{12,28},{16,0},{20,4},{24,8},{28,12},{1,17},{... | collective-permute-start | bytes 786440 | tf_op jit(solution)/shard_map/ppermute | solution.py:24
  93.5 18.3 %collective-permute-start.18 = (bf16[1,64,2048]{2,1,0:T(8,128)(2,1)S(1)}, bf16[1,64,2048]{2,1,0:T(8,128)(2,1)S(1)}, u32[]{:S(2)}, u32[]{:S(2)}) collective-permute-start(bf16[1,64,2048]{2,1,0:T(8,128)(2,1)S(1)} %shard_map.103.refs_1_), channel_id=1, source_target_pairs={{0,4},{4,0},{8,12},{12,8},{16,20},{20,16},{24,28},{28,24},{1,5},{5... | collective-permute-start | bytes 786440 | tf_op jit(solution)/shard_map/ppermute | solution.py:24
  (7 other events, 5.8 us)

commit v9 on v8

--- a/solution.py
+++ b/solution.py
@@ -65,15 +65,15 @@
     return pl.pallas_call(
         pack_kernel,
         out_shape=jax.ShapeDtypeStruct((rows, 2 * width + LANES), jnp.bfloat16),
-        in_specs=[HERE] * 4,
-        out_specs=HERE,
+        in_specs=[pl.BlockSpec(memory_space=pltpu.HBM)] * 4,
+        out_specs=pl.BlockSpec(memory_space=pltpu.HBM),
         scratch_shapes=[
             pltpu.VMEM((rows, LANES), jnp.bfloat16),
             pltpu.VMEM((top, rows), jnp.int32),
             pltpu.VMEM((top, rows), jnp.float32),
             pltpu.SemaphoreType.DMA((5,)),
         ],
-        compiler_params=pltpu.CompilerParams(vmem_limit_bytes=48 << 20),
+        compiler_params=pltpu.CompilerParams(vmem_limit_bytes=1 << 20),
         cost_estimate=FREE,
     )(tokens, cotangent, expert_ids.T, gate_probs.T)
 
@@ -138,7 +138,7 @@
         out_shape=tuple(jax.ShapeDtypeStruct(shape, jnp.bfloat16) for shape in shapes),
         in_specs=[pl.BlockSpec(memory_space=pltpu.SMEM)] + [vmem] * (len(blocks) + 2),
         out_specs=(vmem,) * 5,
-        compiler_params=pltpu.CompilerParams(vmem_limit_bytes=18 << 20),
+        compiler_params=pltpu.CompilerParams(vmem_limit_bytes=14 << 20),
         cost_estimate=FREE,
     )(place, *blocks, gate_up, down)
 
@@ -198,7 +198,7 @@
         ),
         in_specs=[vmem] * (5 * len(made)),
         out_specs=(vmem,) * 4,
-        compiler_params=pltpu.CompilerParams(vmem_limit_bytes=24 << 20),
+        compiler_params=pltpu.CompilerParams(vmem_limit_bytes=16 << 20),
         cost_estimate=FREE,
     )(*[v for block in made for v in block])
 

time: 113 us -> 113 us (level)
  no operation moved by 1% of the time
where the time goes in v9:
time: 113 us
  waiting for transfers between devices  41.5 us (37%)
  starting transfers between devices  25.3 us (22%)
  Pallas kernels  17.9 us (16%)
  local copies, waits for them, and re-layouts  13.1 us (12%)
  other arithmetic  7.38 us (7%)
  matrix products  6.46 us (6%)
    ppermute x22, waiting for transfers between devices, flip(): lax.ppermute(values, axis, [(i, i ^ bit) for i in range(lax.axis_size(axi...  41.5 us
    ppermute x22, starting transfers between devices, flip(): lax.ppermute(values, axis, [(i, i ^ bit) for i in range(lax.axis_size(axi...  25.3 us
    pallas_call x4, Pallas kernels, expert_rows(): pl.pallas_call(functools.partial(expert_kernel, group_count), out_shape=t...  12.9 us
    unnamed x34, local copies, waits for them, and re-layouts  11.5 us
    dot_general x2, matrix products, input_part(): return narrow(jnp.dot(back, gate_up.T, preferred_element_type=jnp.float32))  5.07 us
    convert_element_type x7, other arithmetic, narrow(): return values.astype(jnp.bfloat16)  3.9 us
    pallas_call x1, Pallas kernels, early_terms(): pl.pallas_call(terms_kernel, out_shape=(jax.ShapeDtypeStruct((tok_cols.sh...  2.66 us
  transfers between devices with their start and end apart: 22, of which 9 were waited for; matrix products, arithmetic and copies ran while one was open for 13% of the time, Pallas kernels for 14%

profile of v9, /device:TPU:0, one launch (start us, length us, event | category | flops | bytes accessed | tf_op | source)
XLA Modules:
  0.0 112.7 jit_solution(16169354469523440989)
XLA Ops:
  5.7 2.6 %collective-permute-start.1 = (bf16[128,4224]{1,0:T(8,128)(2,1)}, bf16[128,4224]{1,0:T(8,128)(2,1)}, u32[]{:S(2)}, u32[]{:S(2)}) collective-permute-start(bf16[128,4224]{1,0:T(8,128)(2,1)} %shard_map.94.refs_0_), channel_id=1, source_target_pairs={{0,2},{1,3},{2,0},{3,1},{4,6},{5,7},{6,4},{7,5},{8,10},{9,11},{10,... | collective-permute-start | bytes 3244040 | tf_op jit(solution)/shard_map/ppermute | solution.py:24
  8.2 1.6 %collective-permute-start.2 = (bf16[128,4224]{1,0:T(8,128)(2,1)}, bf16[128,4224]{1,0:T(8,128)(2,1)}, u32[]{:S(2)}, u32[]{:S(2)}) collective-permute-start(bf16[128,4224]{1,0:T(8,128)(2,1)} %shard_map.94.refs_0_), channel_id=1, source_target_pairs={{0,8},{4,12},{8,0},{12,4},{16,24},{20,28},{24,16},{28,20},{1,9},{5... | collective-permute-start | bytes 3244040 | tf_op jit(solution)/shard_map/ppermute | solution.py:24
  9.8 1.3 %dynamic-slice_bitcast_fusion.1 = (bf16[1,2,64,2048]{3,2,1,0:T(8,128)(2,1)S(1)}, bf16[1,2,64,2048]{3,2,1,0:T(8,128)(2,1)S(1)}) fusion(bf16[1,2,2,2,64,2048]{5,4,3,2,1,0:T(8,128)(2,1)} %bitcast.77, s32[]{:T(128)S(6)} %select_n.72, s32[]{:T(128)S(6)} %select_n.70, s32[]{:T(128)S(6)} %select_n.66), kind=kLoop, calls=%fused_computation.33 | loop fusion | bytes 2097164 | tf_op jit(solution)/shard_map/jit(dynamic_index_in_dim)/squeeze | solution.py:28
  11.1 1.6 %collective-permute-start.3 = (bf16[1,2,64,2048]{3,2,1,0:T(8,128)(2,1)S(1)}, bf16[1,2,64,2048]{3,2,1,0:T(8,128)(2,1)}, u32[]{:S(2)}, u32[]{:S(2)}) collective-permute-start(bf16[1,2,64,2048]{3,2,1,0:T(8,128)(2,1)S(1)} %get-tuple-element.78), channel_id=1, source_target_pairs={{0,4},{4,0},{8,12},{12,8},{16,20},{20,16},{24,28},{28,24},{1,5},{5... | collective-permute-start | bytes 1572872 | tf_op jit(solution)/shard_map/ppermute | solution.py:24
  12.7 12.2 %collective-permute-done.3 = bf16[1,2,64,2048]{3,2,1,0:T(8,128)(2,1)} collective-permute-done((bf16[1,2,64,2048]{3,2,1,0:T(8,128)(2,1)S(1)}, bf16[1,2,64,2048]{3,2,1,0:T(8,128)(2,1)}, u32[]{:S(2)}, u32[]{:S(2)}) %collective-permute-start.3) | collective-permute-done | bytes 524320 | tf_op jit(solution)/shard_map/ppermute | solution.py:24
  25.0 1.3 %fusion.6.refs_2_ = bf16[1,2,64,2048]{3,2,1,0:T(8,128)(2,1)S(1)} fusion(bf16[1,2,64,2048]{3,2,1,0:T(8,128)(2,1)} %collective-permute-done.3, bf16[1,2,2,2,64,2048]{5,4,3,2,1,0:T(8,128)(2,1)} %bitcast.78, s32[]{:T(128)S(6)} %select_n.66, s32[]{:T(128)S(6)} %select_n.68), kind=kLoop, calls=%fused_computation.15 | loop fusion | flops 1048576 | bytes 1572872 | tf_op jit(solution)/shard_map/convert_element_type | solution.py:20
  26.3 2.2 %copy-done = bf16[1,2048,1024]{2,1,0:T(8,128)(2,1)S(1)} copy-done((bf16[1,2048,1024]{2,1,0:T(8,128)(2,1)S(1)}, bf16[1,2048,1024]{2,1,0:T(8,128)(2,1)}, u32[]{:S(2)}) %copy-start) | copy-done | bytes 4194328
  28.5 3.4 %shard_map.95 = (bf16[256,1024]{1,0:T(8,128)(2,1)S(1)}, bf16[256,256]{1,0:T(8,128)(2,1)S(1)}, bf16[256,2048]{1,0:T(8,128)(2,1)S(1)}, bf16[128,1024]{1,0:T(8,128)(2,1)S(1)}, bf16[128,1024]{1,0:T(8,128)(2,1)S(1)}) custom-call(s32[2]{0:T(128)S(1)} %pad_add_fusion.place, bf16[128,4224]{1,0:T(8,128)(2,1)} %shard_map.94.refs_0_, ...), custom_call_target="tpu_custom_call" | custom-call | tf_op jit(solution)/shard_map/pallas_call | solution.py:136
  33.0 1.5 %collective-permute-done.2.refs_1_ = bf16[128,4224]{1,0:T(8,128)(2,1)} collective-permute-done((bf16[128,4224]{1,0:T(8,128)(2,1)}, bf16[128,4224]{1,0:T(8,128)(2,1)}, u32[]{:S(2)}, u32[]{:S(2)}) %collective-permute-start.2) | collective-permute-done | bytes 1081376 | tf_op jit(solution)/shard_map/ppermute | solution.py:24
  37.0 1.6 %collective-permute-start.5 = (bf16[64,4224]{1,0:T(8,128)(2,1)S(1)}, bf16[64,4224]{1,0:T(8,128)(2,1)S(1)}, u32[]{:S(2)}, u32[]{:S(2)}) collective-permute-start(bf16[64,4224]{1,0:T(8,128)(2,1)S(1)} %get-tuple-element.44), channel_id=1, source_target_pairs={{0,8},{4,12},{8,0},{12,4},{16,24},{20,28},{24,16},{28,20},{1,9},{5... | collective-permute-start | bytes 1622024 | tf_op jit(solution)/shard_map/ppermute | solution.py:24
  39.1 1.5 %collective-permute-start.8 = (bf16[1,2,64,2048]{3,2,1,0:T(8,128)(2,1)}, bf16[1,2,64,2048]{3,2,1,0:T(8,128)(2,1)S(1)}, u32[]{:S(2)}, u32[]{:S(2)}) collective-permute-start(bf16[1,2,64,2048]{3,2,1,0:T(8,128)(2,1)} %copy-done.9), channel_id=1, source_target_pairs={{0,4},{4,0},{8,12},{12,8},{16,20},{20,16},{24,28},{28,24},{1,5},{5... | collective-permute-start | bytes 1572872 | tf_op jit(solution)/shard_map/ppermute | solution.py:24
  40.7 3.1 %shard_map.98 = (bf16[256,1024]{1,0:T(8,128)(2,1)S(1)}, bf16[256,256]{1,0:T(8,128)(2,1)S(1)}, bf16[256,2048]{1,0:T(8,128)(2,1)S(1)}, bf16[128,1024]{1,0:T(8,128)(2,1)S(1)}, bf16[128,1024]{1,0:T(8,128)(2,1)S(1)}) custom-call(s32[2]{0:T(128)S(1)} %pad_add_fusion.place, bf16[128,4224]{1,0:T(8,128)(2,1)} %get-tuple-element.53.refs_0_, ...), custom_call_target="tpu_custom_call" | custom-call | tf_op jit(solution)/shard_map/pallas_call | solution.py:136
  43.8 3.1 %shard_map.97 = (bf16[256,1024]{1,0:T(8,128)(2,1)S(1)}, bf16[256,256]{1,0:T(8,128)(2,1)S(1)}, bf16[256,2048]{1,0:T(8,128)(2,1)S(1)}, bf16[128,1024]{1,0:T(8,128)(2,1)S(1)}, bf16[128,1024]{1,0:T(8,128)(2,1)S(1)}) custom-call(s32[2]{0:T(128)S(1)} %pad_add_fusion.place, bf16[128,4224]{1,0:T(8,128)(2,1)} %get-tuple-element.42.refs_0_, ...), custom_call_target="tpu_custom_call" | custom-call | tf_op jit(solution)/shard_map/pallas_call | solution.py:136
  46.9 2.7 %shard_map.99 = (f32[1024,1024]{1,0:T(8,128)S(1)}, f32[256,2048]{1,0:T(8,128)S(1)}, bf16[256,1024]{1,0:T(8,128)(2,1)S(1)}, f32[8,128]{1,0:T(8,128)S(1)}) custom-call(bf16[256,1024]{1,0:T(8,128)(2,1)S(1)} %get-tuple-element.46.refs_0_, bf16[256,256]{1,0:T(8,128)(2,1)S(1)} %get-tuple-element.41.refs_4_.refs_1_, ...), custom_call_target="tpu_custom_call" | custom-call | tf_op jit(solution)/shard_map/pallas_call | solution.py:191
  49.6 2.0 %copy-done.3 = f32[1024,1024]{1,0:T(8,128)} copy-done((f32[1024,1024]{1,0:T(8,128)}, f32[1024,1024]{1,0:T(8,128)S(1)}, u32[]{:S(2)}) %copy-start.3) | copy-done | bytes 4194328
  55.4 3.8 %convolution_convert_fusion = bf16[256,2048]{1,0:T(8,128)(2,1)S(1)} fusion(bf16[256,1024]{1,0:T(8,128)(2,1)} %copy-done.12, bf16[1,2048,1024]{2,1,0:T(8,128)(2,1)} %param.11), kind=kOutput, calls=%fused_computation.1 | convolution fusion | flops 1074266112 | bytes 5767168 | tf_op jit(solution)/shard_map/dot_general | solution.py:289
  59.3 3.3 %shard_map.101 = (bf16[256,1024]{1,0:T(8,128)(2,1)S(1)}, bf16[256,256]{1,0:T(8,128)(2,1)S(1)}, bf16[256,2048]{1,0:T(8,128)(2,1)S(1)}, bf16[128,1024]{1,0:T(8,128)(2,1)S(1)}, bf16[128,1024]{1,0:T(8,128)(2,1)S(1)}) custom-call(s32[2]{0:T(128)S(1)} %pad_add_fusion.place, bf16[64,4224]{1,0:T(8,128)(2,1)S(1)} %get-tuple-element.65.refs_0_, ...), custom_call_target="tpu_custom_call" | custom-call | tf_op jit(solution)/shard_map/pallas_call | solution.py:136
  63.6 1.2 %copy-done.4 = f32[1024,1024]{1,0:T(8,128)S(1)} copy-done((f32[1024,1024]{1,0:T(8,128)S(1)}, f32[1024,1024]{1,0:T(8,128)}, u32[]{:S(2)}) %copy-start.4) | copy-done | bytes 4194328
  66.2 1.5 %collective-permute-start.15 = (bf16[1,96,1024]{2,1,0:T(8,128)(2,1)S(1)}, bf16[1,96,1024]{2,1,0:T(8,128)(2,1)S(1)}, u32[]{:S(2)}, u32[]{:S(2)}) collective-permute-start(bf16[1,96,1024]{2,1,0:T(8,128)(2,1)S(1)} %dynamic-slice_bitcast_fusion.6), channel_id=1, source_target_pairs={{0,4},{4,0},{8,12},{12,8},{16,20},{20,16},{24,28},{28,24},{1,5},{5... | collective-permute-start | bytes 589832 | tf_op jit(solution)/shard_map/ppermute | solution.py:24
  69.3 4.7 %collective-permute-done.15.refs_2_ = bf16[1,96,1024]{2,1,0:T(8,128)(2,1)S(1)} collective-permute-done((bf16[1,96,1024]{2,1,0:T(8,128)(2,1)S(1)}, bf16[1,96,1024]{2,1,0:T(8,128)(2,1)S(1)}, u32[]{:S(2)}, u32[]{:S(2)}) %collective-permute-start.15) | collective-permute-done | bytes 196640 | tf_op jit(solution)/shard_map/ppermute | solution.py:24
  74.0 1.5 %collective-permute-start.20 = (bf16[1,64,2048]{2,1,0:T(8,128)(2,1)S(1)}, bf16[1,64,2048]{2,1,0:T(8,128)(2,1)S(1)}, u32[]{:S(2)}, u32[]{:S(2)}) collective-permute-start(bf16[1,64,2048]{2,1,0:T(8,128)(2,1)S(1)} %get-tuple-element.76), channel_id=1, source_target_pairs={{0,4},{4,0},{8,12},{12,8},{16,20},{20,16},{24,28},{28,24},{1,5},{5... | collective-permute-start | bytes 786440 | tf_op jit(solution)/shard_map/ppermute | solution.py:24
  75.5 2.6 %collective-permute-start.16 = (bf16[1,96,1024]{2,1,0:T(8,128)(2,1)S(1)}, bf16[1,96,1024]{2,1,0:T(8,128)(2,1)S(1)}, u32[]{:S(2)}, u32[]{:S(2)}) collective-permute-start(bf16[1,96,1024]{2,1,0:T(8,128)(2,1)S(1)} %fusion.20), channel_id=1, source_target_pairs={{0,16},{4,20},{8,24},{12,28},{16,0},{20,4},{24,8},{28,12},{1,17},{... | collective-permute-start | bytes 589832 | tf_op jit(solution)/shard_map/ppermute | solution.py:24
  78.2 1.2 %fusion.3 = f32[1,2,64,2048]{3,2,1,0:T(8,128)S(1)} fusion(bf16[1,2,64,2048]{3,2,1,0:T(8,128)(2,1)S(1)} %get-tuple-element.75, bf16[1,2,64,2048]{3,2,1,0:T(8,128)(2,1)S(1)} %copy-done.8, bf16[1,2,2,2,64,2048]{5,4,3,2,1,0:T(8,128)(2,1)} %bitcast.79, s32[]{:T(128)S(6)} %select_n.72, s32[]{:T(128)S(6)} %select_n.68), kind=kLoop, calls=%fused_computation.10 | loop fusion | flops 1310720 | bytes 2621448 | tf_op jit(solution)/shard_map/add | solution.py:284
  79.5 1.3 %fusion.1 = f32[256,2048]{1,0:T(8,128)S(1)} fusion(bf16[256,2048]{1,0:T(8,128)(2,1)S(1)} %collective-permute-done.9, bf16[128,1024]{1,0:T(8,128)(2,1)S(1)} %copy-done.14, bf16[128,1024]{1,0:T(8,128)(2,1)S(1)} %get-tuple-element.40.refs_3_, bf16[1,2048,1024]{2,1,0:T(8,128)(2,1)S(1)} %copy-done.1), kind=kOutput, calls=%fused_computation.4 | convolution fusion | flops 1076887552 | bytes 7864320 | tf_op jit(solution)/shard_map/dot_general | solution.py:289
  80.8 1.4 %collective-permute-start.10 = (bf16[128,2048]{1,0:T(8,128)(2,1)S(1)}, bf16[128,2048]{1,0:T(8,128)(2,1)S(1)}, u32[]{:S(2)}, u32[]{:S(2)}) collective-permute-start(bf16[128,2048]{1,0:T(8,128)(2,1)S(1)} %slice.27), channel_id=1, source_target_pairs={{0,2},{1,3},{2,0},{3,1},{4,6},{5,7},{6,4},{7,5},{8,10},{9,11},{10,... | collective-permute-start | bytes 1572872 | tf_op jit(solution)/shard_map/ppermute | solution.py:24
  82.4 1.4 %collective-permute-start.17 = (bf16[1,160,1024]{2,1,0:T(8,128)(2,1)S(1)}, bf16[1,160,1024]{2,1,0:T(8,128)(2,1)S(1)}, u32[]{:S(2)}, u32[]{:S(2)}) collective-permute-start(bf16[1,160,1024]{2,1,0:T(8,128)(2,1)S(1)} %fusion.7), channel_id=1, source_target_pairs={{0,16},{4,20},{8,24},{12,28},{16,0},{20,4},{24,8},{28,12},{1,17},{... | collective-permute-start | bytes 983048 | tf_op jit(solution)/shard_map/ppermute | solution.py:24
  83.7 1.5 %collective-permute-start.14 = (bf16[1,256,1024]{2,1,0:T(8,128)(2,1)S(1)}, bf16[1,256,1024]{2,1,0:T(8,128)(2,1)S(1)}, u32[]{:S(2)}, u32[]{:S(2)}) collective-permute-start(bf16[1,256,1024]{2,1,0:T(8,128)(2,1)S(1)} %shard_map.102), channel_id=1, source_target_pairs={{0,4},{4,0},{8,12},{12,8},{16,20},{20,16},{24,28},{28,24},{1,5},{5... | collective-permute-start | bytes 1572872 | tf_op jit(solution)/shard_map/ppermute | solution.py:24
  85.2 1.4 %collective-permute-done.20 = bf16[1,64,2048]{2,1,0:T(8,128)(2,1)S(1)} collective-permute-done((bf16[1,64,2048]{2,1,0:T(8,128)(2,1)S(1)}, bf16[1,64,2048]{2,1,0:T(8,128)(2,1)S(1)}, u32[]{:S(2)}, u32[]{:S(2)}) %collective-permute-start.20) | collective-permute-done | bytes 262176 | tf_op jit(solution)/shard_map/ppermute | solution.py:24
  86.7 2.7 %collective-permute-start.21 = (bf16[1,64,2048]{2,1,0:T(8,128)(2,1)S(1)}, bf16[1,64,2048]{2,1,0:T(8,128)(2,1)S(1)}, u32[]{:S(2)}, u32[]{:S(2)}) collective-permute-start(bf16[1,64,2048]{2,1,0:T(8,128)(2,1)S(1)} %fusion.16), channel_id=1, source_target_pairs={{0,16},{4,20},{8,24},{12,28},{16,0},{20,4},{24,8},{28,12},{1,17},{... | collective-permute-start | bytes 786440 | tf_op jit(solution)/shard_map/ppermute | solution.py:24
  89.3 4.1 %collective-permute-done.10.refs_1_ = bf16[128,2048]{1,0:T(8,128)(2,1)S(1)} collective-permute-done((bf16[128,2048]{1,0:T(8,128)(2,1)S(1)}, bf16[128,2048]{1,0:T(8,128)(2,1)S(1)}, u32[]{:S(2)}, u32[]{:S(2)}) %collective-permute-start.10) | collective-permute-done | bytes 524320 | tf_op jit(solution)/shard_map/ppermute | solution.py:24
  95.0 12.2 %collective-permute-done.17.refs_0_ = bf16[1,160,1024]{2,1,0:T(8,128)(2,1)S(1)} collective-permute-done((bf16[1,160,1024]{2,1,0:T(8,128)(2,1)S(1)}, bf16[1,160,1024]{2,1,0:T(8,128)(2,1)S(1)}, u32[]{:S(2)}, u32[]{:S(2)}) %collective-permute-start.17) | collective-permute-done | bytes 327712 | tf_op jit(solution)/shard_map/ppermute | solution.py:24
  108.5 3.3 %collective-permute-done.21 = bf16[1,64,2048]{2,1,0:T(8,128)(2,1)S(1)} collective-permute-done((bf16[1,64,2048]{2,1,0:T(8,128)(2,1)S(1)}, bf16[1,64,2048]{2,1,0:T(8,128)(2,1)S(1)}, u32[]{:S(2)}, u32[]{:S(2)}) %collective-permute-start.21) | collective-permute-done | bytes 262176 | tf_op jit(solution)/shard_map/ppermute | solution.py:24
  (81 shorter events, 21.1 us)
Async XLA Ops:
  5.1 21.2 %copy-start.2 = (bf16[1,512,2048]{2,1,0:T(8,128)(2,1)S(1)}, bf16[1,512,2048]{2,1,0:T(8,128)(2,1)}, u32[]{:S(2)}) copy-start(bf16[1,512,2048]{2,1,0:T(8,128)(2,1)} %param.12) | copy-start | bytes 6291460
  5.1 21.2 %collective-permute-start = (bf16[128,4224]{1,0:T(8,128)(2,1)}, bf16[128,4224]{1,0:T(8,128)(2,1)}, u32[]{:S(2)}, u32[]{:S(2)}) collective-permute-start(bf16[128,4224]{1,0:T(8,128)(2,1)} %shard_map.94.refs_0_), channel_id=1, source_target_pairs={{0,1},{1,0},{2,3},{3,2},{4,5},{5,4},{6,7},{7,6},{8,9},{9,8},{10,11... | collective-permute-start | bytes 3244040 | tf_op jit(solution)/shard_map/ppermute | solution.py:24
  5.7 27.3 %collective-permute-start.1 = (bf16[128,4224]{1,0:T(8,128)(2,1)}, bf16[128,4224]{1,0:T(8,128)(2,1)}, u32[]{:S(2)}, u32[]{:S(2)}) collective-permute-start(bf16[128,4224]{1,0:T(8,128)(2,1)} %shard_map.94.refs_0_), channel_id=1, source_target_pairs={{0,2},{1,3},{2,0},{3,1},{4,6},{5,7},{6,4},{7,5},{8,10},{9,11},{10,... | collective-permute-start | bytes 3244040 | tf_op jit(solution)/shard_map/ppermute | solution.py:24
  8.2 26.2 %collective-permute-start.2 = (bf16[128,4224]{1,0:T(8,128)(2,1)}, bf16[128,4224]{1,0:T(8,128)(2,1)}, u32[]{:S(2)}, u32[]{:S(2)}) collective-permute-start(bf16[128,4224]{1,0:T(8,128)(2,1)} %shard_map.94.refs_0_), channel_id=1, source_target_pairs={{0,8},{4,12},{8,0},{12,4},{16,24},{20,28},{24,16},{28,20},{1,9},{5... | collective-permute-start | bytes 3244040 | tf_op jit(solution)/shard_map/ppermute | solution.py:24
  11.1 13.9 %collective-permute-start.3 = (bf16[1,2,64,2048]{3,2,1,0:T(8,128)(2,1)S(1)}, bf16[1,2,64,2048]{3,2,1,0:T(8,128)(2,1)}, u32[]{:S(2)}, u32[]{:S(2)}) collective-permute-start(bf16[1,2,64,2048]{3,2,1,0:T(8,128)(2,1)S(1)} %get-tuple-element.78), channel_id=1, source_target_pairs={{0,4},{4,0},{8,12},{12,8},{16,20},{20,16},{24,28},{28,24},{1,5},{5... | collective-permute-start | bytes 1572872 | tf_op jit(solution)/shard_map/ppermute | solution.py:24
  26.3 2.2 %copy-start = (bf16[1,2048,1024]{2,1,0:T(8,128)(2,1)S(1)}, bf16[1,2048,1024]{2,1,0:T(8,128)(2,1)}, u32[]{:S(2)}) copy-start(bf16[1,2048,1024]{2,1,0:T(8,128)(2,1)} %param.11) | copy-start | bytes 12582916
  36.5 4.1 %collective-permute-start.7 = (bf16[128,4224]{1,0:T(8,128)(2,1)}, bf16[128,4224]{1,0:T(8,128)(2,1)S(1)}, u32[]{:S(2)}, u32[]{:S(2)}) collective-permute-start(bf16[128,4224]{1,0:T(8,128)(2,1)} %get-tuple-element.53.refs_0_), channel_id=1, source_target_pairs={{0,1},{1,0},{2,3},{3,2},{4,5},{5,4},{6,7},{7,6},{8,9},{9,8},{10,11... | collective-permute-start | bytes 3244040 | tf_op jit(solution)/shard_map/ppermute | solution.py:24
  36.5 7.2 %collective-permute-start.4 = (bf16[128,4224]{1,0:T(8,128)(2,1)}, bf16[128,4224]{1,0:T(8,128)(2,1)S(1)}, u32[]{:S(2)}, u32[]{:S(2)}) collective-permute-start(bf16[128,4224]{1,0:T(8,128)(2,1)} %get-tuple-element.42.refs_0_), channel_id=1, source_target_pairs={{0,1},{1,0},{2,3},{3,2},{4,5},{5,4},{6,7},{7,6},{8,9},{9,8},{10,11... | collective-permute-start | bytes 3244040 | tf_op jit(solution)/shard_map/ppermute | solution.py:24
  37.0 15.6 %collective-permute-start.5 = (bf16[64,4224]{1,0:T(8,128)(2,1)S(1)}, bf16[64,4224]{1,0:T(8,128)(2,1)S(1)}, u32[]{:S(2)}, u32[]{:S(2)}) collective-permute-start(bf16[64,4224]{1,0:T(8,128)(2,1)S(1)} %get-tuple-element.44), channel_id=1, source_target_pairs={{0,8},{4,12},{8,0},{12,4},{16,24},{20,28},{24,16},{28,20},{1,9},{5... | collective-permute-start | bytes 1622024 | tf_op jit(solution)/shard_map/ppermute | solution.py:24
  38.6 14.0 %collective-permute-start.6 = (bf16[64,4224]{1,0:T(8,128)(2,1)S(1)}, bf16[64,4224]{1,0:T(8,128)(2,1)}, u32[]{:S(2)}, u32[]{:S(2)}) collective-permute-start(bf16[64,4224]{1,0:T(8,128)(2,1)S(1)} %get-tuple-element.45), channel_id=1, source_target_pairs={{0,2},{1,3},{2,0},{3,1},{4,6},{5,7},{6,4},{7,5},{8,10},{9,11},{10,... | collective-permute-start | bytes 1622024 | tf_op jit(solution)/shard_map/ppermute | solution.py:24
  39.1 13.5 %collective-permute-start.8 = (bf16[1,2,64,2048]{3,2,1,0:T(8,128)(2,1)}, bf16[1,2,64,2048]{3,2,1,0:T(8,128)(2,1)S(1)}, u32[]{:S(2)}, u32[]{:S(2)}) collective-permute-start(bf16[1,2,64,2048]{3,2,1,0:T(8,128)(2,1)} %copy-done.9), channel_id=1, source_target_pairs={{0,4},{4,0},{8,12},{12,8},{16,20},{20,16},{24,28},{28,24},{1,5},{5... | collective-permute-start | bytes 1572872 | tf_op jit(solution)/shard_map/ppermute | solution.py:24
  46.9 2.7 %copy-start.13 = (bf16[128,1024]{1,0:T(8,128)(2,1)}, bf16[128,1024]{1,0:T(8,128)(2,1)S(1)}, u32[]{:S(2)}) copy-start(bf16[128,1024]{1,0:T(8,128)(2,1)S(1)} %get-tuple-element.43.refs_8_) | copy-start | bytes 786436
  49.5 2.0 %copy-start.3 = (f32[1024,1024]{1,0:T(8,128)}, f32[1024,1024]{1,0:T(8,128)S(1)}, u32[]{:S(2)}) copy-start(f32[1024,1024]{1,0:T(8,128)S(1)} %get-tuple-element.64) | copy-start | bytes 12582916
  51.5 1.4 %copy-start.5 = (f32[256,2048]{1,0:T(8,128)}, f32[256,2048]{1,0:T(8,128)S(1)}, u32[]{:S(2)}) copy-start(f32[256,2048]{1,0:T(8,128)S(1)} %get-tuple-element.70) | copy-start | bytes 6291460
  54.5 4.8 %collective-permute-start.11 = (bf16[64,4224]{1,0:T(8,128)(2,1)S(1)}, bf16[64,4224]{1,0:T(8,128)(2,1)}, u32[]{:S(2)}, u32[]{:S(2)}) collective-permute-start(bf16[64,4224]{1,0:T(8,128)(2,1)S(1)} %get-tuple-element.65.refs_0_), channel_id=1, source_target_pairs={{0,1},{1,0},{2,3},{3,2},{4,5},{5,4},{6,7},{7,6},{8,9},{9,8},{10,11... | collective-permute-start | bytes 1622024 | tf_op jit(solution)/shard_map/ppermute | solution.py:24
  54.5 4.8 %collective-permute-start.12 = (bf16[64,4224]{1,0:T(8,128)(2,1)}, bf16[64,4224]{1,0:T(8,128)(2,1)}, u32[]{:S(2)}, u32[]{:S(2)}) collective-permute-start(bf16[64,4224]{1,0:T(8,128)(2,1)} %get-tuple-element.66.refs_1_), channel_id=1, source_target_pairs={{0,1},{1,0},{2,3},{3,2},{4,5},{5,4},{6,7},{7,6},{8,9},{9,8},{10,11... | collective-permute-start | bytes 1622024 | tf_op jit(solution)/shard_map/ppermute | solution.py:24
  55.0 14.3 %collective-permute-start.19 = (bf16[1,2,64,2048]{3,2,1,0:T(8,128)(2,1)S(1)}, bf16[1,2,64,2048]{3,2,1,0:T(8,128)(2,1)S(1)}, u32[]{:S(2)}, u32[]{:S(2)}) collective-permute-start(bf16[1,2,64,2048]{3,2,1,0:T(8,128)(2,1)S(1)} %get-tuple-element.74), channel_id=1, source_target_pairs={{0,8},{4,12},{8,0},{12,4},{16,24},{20,28},{24,16},{28,20},{1,9},{5... | collective-permute-start | bytes 1572872 | tf_op jit(solution)/shard_map/ppermute | solution.py:24
  55.4 3.9 %copy-start.1 = (bf16[1,2048,1024]{2,1,0:T(8,128)(2,1)S(1)}, bf16[1,2048,1024]{2,1,0:T(8,128)(2,1)}, u32[]{:S(2)}) copy-start(bf16[1,2048,1024]{2,1,0:T(8,128)(2,1)} %param.11) | copy-start | bytes 12582916
  59.2 20.2 %collective-permute-start.9 = (bf16[256,2048]{1,0:T(8,128)(2,1)S(1)}, bf16[256,2048]{1,0:T(8,128)(2,1)S(1)}, u32[]{:S(2)}, u32[]{:S(2)}) collective-permute-start(bf16[256,2048]{1,0:T(8,128)(2,1)S(1)} %convolution_convert_fusion), channel_id=1, source_target_pairs={{0,1},{1,0},{2,3},{3,2},{4,5},{5,4},{6,7},{7,6},{8,9},{9,8},{10,11... | collective-permute-start | bytes 3145736 | tf_op jit(solution)/shard_map/ppermute | solution.py:24
  62.7 2.2 %copy-start.4 = (f32[1024,1024]{1,0:T(8,128)S(1)}, f32[1024,1024]{1,0:T(8,128)}, u32[]{:S(2)}) copy-start(f32[1024,1024]{1,0:T(8,128)} %copy-done.3) | copy-start | bytes 12582916
  66.1 2.7 %copy-start.6 = (f32[256,2048]{1,0:T(8,128)S(1)}, f32[256,2048]{1,0:T(8,128)}, u32[]{:S(2)}) copy-start(f32[256,2048]{1,0:T(8,128)} %copy-done.5) | copy-start | bytes 6291460
  66.2 7.8 %collective-permute-start.15 = (bf16[1,96,1024]{2,1,0:T(8,128)(2,1)S(1)}, bf16[1,96,1024]{2,1,0:T(8,128)(2,1)S(1)}, u32[]{:S(2)}, u32[]{:S(2)}) collective-permute-start(bf16[1,96,1024]{2,1,0:T(8,128)(2,1)S(1)} %dynamic-slice_bitcast_fusion.6), channel_id=1, source_target_pairs={{0,4},{4,0},{8,12},{12,8},{16,20},{20,16},{24,28},{28,24},{1,5},{5... | collective-permute-start | bytes 589832 | tf_op jit(solution)/shard_map/ppermute | solution.py:24
  67.7 14.6 %collective-permute-start.13 = (bf16[1,160,1024]{2,1,0:T(8,128)(2,1)S(1)}, bf16[1,160,1024]{2,1,0:T(8,128)(2,1)S(1)}, u32[]{:S(2)}, u32[]{:S(2)}) collective-permute-start(bf16[1,160,1024]{2,1,0:T(8,128)(2,1)S(1)} %dynamic-slice_bitcast_fusion.3), channel_id=1, source_target_pairs={{0,4},{4,0},{8,12},{12,8},{16,20},{20,16},{24,28},{28,24},{1,5},{5... | collective-permute-start | bytes 983048 | tf_op jit(solution)/shard_map/ppermute | solution.py:24
  69.2 9.0 %copy-start.8 = (bf16[1,2,64,2048]{3,2,1,0:T(8,128)(2,1)S(1)}, bf16[1,2,64,2048]{3,2,1,0:T(8,128)(2,1)}, u32[]{:S(2)}) copy-start(bf16[1,2,64,2048]{3,2,1,0:T(8,128)(2,1)} %copy-done.7) | copy-start | bytes 1572868
  74.0 5.5 %copy-start.14 = (bf16[128,1024]{1,0:T(8,128)(2,1)S(1)}, bf16[128,1024]{1,0:T(8,128)(2,1)}, u32[]{:S(2)}) copy-start(bf16[128,1024]{1,0:T(8,128)(2,1)} %copy-done.13) | copy-start | bytes 786436
  74.0 12.6 %collective-permute-start.20 = (bf16[1,64,2048]{2,1,0:T(8,128)(2,1)S(1)}, bf16[1,64,2048]{2,1,0:T(8,128)(2,1)S(1)}, u32[]{:S(2)}, u32[]{:S(2)}) collective-permute-start(bf16[1,64,2048]{2,1,0:T(8,128)(2,1)S(1)} %get-tuple-element.76), channel_id=1, source_target_pairs={{0,4},{4,0},{8,12},{12,8},{16,20},{20,16},{24,28},{28,24},{1,5},{5... | collective-permute-start | bytes 786440 | tf_op jit(solution)/shard_map/ppermute | solution.py:24
  75.5 31.7 %collective-permute-start.16 = (bf16[1,96,1024]{2,1,0:T(8,128)(2,1)S(1)}, bf16[1,96,1024]{2,1,0:T(8,128)(2,1)S(1)}, u32[]{:S(2)}, u32[]{:S(2)}) collective-permute-start(bf16[1,96,1024]{2,1,0:T(8,128)(2,1)S(1)} %fusion.20), channel_id=1, source_target_pairs={{0,16},{4,20},{8,24},{12,28},{16,0},{20,4},{24,8},{28,12},{1,17},{... | collective-permute-start | bytes 589832 | tf_op jit(solution)/shard_map/ppermute | solution.py:24
  80.8 12.6 %collective-permute-start.10 = (bf16[128,2048]{1,0:T(8,128)(2,1)S(1)}, bf16[128,2048]{1,0:T(8,128)(2,1)S(1)}, u32[]{:S(2)}, u32[]{:S(2)}) collective-permute-start(bf16[128,2048]{1,0:T(8,128)(2,1)S(1)} %slice.27), channel_id=1, source_target_pairs={{0,2},{1,3},{2,0},{3,1},{4,6},{5,7},{6,4},{7,5},{8,10},{9,11},{10,... | collective-permute-start | bytes 1572872 | tf_op jit(solution)/shard_map/ppermute | solution.py:24
  82.4 24.8 %collective-permute-start.17 = (bf16[1,160,1024]{2,1,0:T(8,128)(2,1)S(1)}, bf16[1,160,1024]{2,1,0:T(8,128)(2,1)S(1)}, u32[]{:S(2)}, u32[]{:S(2)}) collective-permute-start(bf16[1,160,1024]{2,1,0:T(8,128)(2,1)S(1)} %fusion.7), channel_id=1, source_target_pairs={{0,16},{4,20},{8,24},{12,28},{16,0},{20,4},{24,8},{28,12},{1,17},{... | collective-permute-start | bytes 983048 | tf_op jit(solution)/shard_map/ppermute | solution.py:24
  83.7 23.5 %collective-permute-start.14 = (bf16[1,256,1024]{2,1,0:T(8,128)(2,1)S(1)}, bf16[1,256,1024]{2,1,0:T(8,128)(2,1)S(1)}, u32[]{:S(2)}, u32[]{:S(2)}) collective-permute-start(bf16[1,256,1024]{2,1,0:T(8,128)(2,1)S(1)} %shard_map.102), channel_id=1, source_target_pairs={{0,4},{4,0},{8,12},{12,8},{16,20},{20,16},{24,28},{28,24},{1,5},{5... | collective-permute-start | bytes 1572872 | tf_op jit(solution)/shard_map/ppermute | solution.py:24
  86.7 25.1 %collective-permute-start.21 = (bf16[1,64,2048]{2,1,0:T(8,128)(2,1)S(1)}, bf16[1,64,2048]{2,1,0:T(8,128)(2,1)S(1)}, u32[]{:S(2)}, u32[]{:S(2)}) collective-permute-start(bf16[1,64,2048]{2,1,0:T(8,128)(2,1)S(1)} %fusion.16), channel_id=1, source_target_pairs={{0,16},{4,20},{8,24},{12,28},{16,0},{20,4},{24,8},{28,12},{1,17},{... | collective-permute-start | bytes 786440 | tf_op jit(solution)/shard_map/ppermute | solution.py:24
  93.5 18.3 %collective-permute-start.18 = (bf16[1,64,2048]{2,1,0:T(8,128)(2,1)S(1)}, bf16[1,64,2048]{2,1,0:T(8,128)(2,1)S(1)}, u32[]{:S(2)}, u32[]{:S(2)}) collective-permute-start(bf16[1,64,2048]{2,1,0:T(8,128)(2,1)S(1)} %shard_map.103.refs_1_), channel_id=1, source_target_pairs={{0,4},{4,0},{8,12},{12,8},{16,20},{20,16},{24,28},{28,24},{1,5},{5... | collective-permute-start | bytes 786440 | tf_op jit(solution)/shard_map/ppermute | solution.py:24
  (7 other events, 5.8 us)

commit v10 on v7

--- a/solution.py
+++ b/solution.py
@@ -197,6 +197,9 @@
     residual = down_residual[0, 0].reshape(high_count, 2, 2, 2, -1, model_width)
 
 
+    def pair_sum(kept, got):
+        return wide(kept) + wide(got)
+
     def residual_side(parity, first):
         return take(take(residual, 2, parity), 2, first)
 
@@ -208,16 +211,15 @@
         return expert_rows(group_count, place, blocks, gate_up, down_matrix)
 
     made = [expert_on(rows_own, rows_c)]
-    rows_x, rows_n, res_other, res_mine = hold(
-        (rows_x, rows_n, res_other, res_mine), (made[0][1],)
+    res_send = narrow(pair_sum(residual_side(1 - bit1, bit0), res_other))
+    rows_x, rows_n, res_send, res_mine = hold(
+        (rows_x, rows_n, res_send, res_mine), (made[0][1],)
     )
     diagonal = [flip(rows_x[:half], "dp", 2), flip(rows_n[half:], "expert", 2)]
     made += [expert_on(rows, flip(rows, "expert", 1)) for rows in (rows_x, rows_n)]
     res_mine = flip(res_mine, "dp", 1)
     gate_early, down_early, back_sent, mark = early_terms(made)
-    *diagonal, back_sent, res_other, res_mine = hold(
-        (*diagonal, back_sent, res_other, res_mine), (mark,)
-    )
+    *diagonal, res_send, res_mine = hold((*diagonal, res_send, res_mine), (mark,))
     diagonal += [flip(rows, "expert", 1) for rows in diagonal]
 
     def terms(tok_cols, hid_cols, scaled, back):
@@ -234,9 +236,6 @@
 
     def side(term, third, first):
         return take(take(term, 1, third), 1, first)
-
-    def pair_sum(kept, got):
-        return wide(kept) + wide(got)
 
     count = gate_term.shape[3]
     first = max(count * 3 // 8, 16)
@@ -249,7 +248,7 @@
     crossed = [
         flip(narrow(pair_sum(kept, got)), "dp", 4) for kept, got in zip(far_kept, far_got)
     ]
-    res_near = flip(narrow(pair_sum(residual_side(1 - bit1, bit0), res_other)), "dp", 2)
+    res_near = flip(res_send, "dp", 2)
     res_near, down_sent = hold(
         (res_near, side(down_term, 1 - bit2, 1 - bit0)), (far_got[0],)
     )
@@ -261,6 +260,7 @@
     def input_part(back):
         return narrow(jnp.dot(back, gate_up.T, preferred_element_type=jnp.float32))
 
+    (back_sent,) = hold((back_sent,), (far_sent[0],))
     core = flip(input_part(back_sent), "expert", 1)
     back_kept = jnp.concatenate([made[0][3], made[1][3]], axis=0)
     total = wide(input_part(back_kept)) + wide(core)
@@ -270,6 +270,7 @@
     near_gate = pair_sum(side(gate_term, bit2, bit0), flip(near_sent, "dp", 1))
     (near_sent,) = hold((side(down_term, bit2, 1 - bit0),), (across,))
     near_down = pair_sum(side(down_term, bit2, bit0), flip(near_sent, "dp", 1))
+    crossed[-1] = hold((crossed[-1],), (near_sent,))[0]
     gate_sum = near_gate + wide(jnp.concatenate(crossed, axis=1))
     down_sum = near_down + take(res_sum, 1, bit2) + wide(crossed_down)
     bit = 8

time: 114 us -> 110 us (0.965)
  waiting for transfers between devices: 43.4 us -> 36.2 us
  local copies, waits for them, and re-layouts: 13.2 us -> 19.3 us
  Pallas kernels: 17.1 us -> 15.9 us
    unnamed x34 -> x42, local copies, waits for them, and re-layouts: 7.86 us -> 15.3 us
    ppermute x22, waiting for transfers between devices: 43.4 us -> 36.2 us  [flip(): lax.ppermute(values, axis, [(i, i ^ bit) for i in range(lax.axis_size(axi...]
    slice x2, local copies, waits for them, and re-layouts: 2.74 us -> 1.38 us  [on_device(): diagonal = [flip(rows_x[:half], 'dp', 2), flip(rows_n[half:], 'expert', 2)]]
    pallas_call x4, Pallas kernels: 13.3 us -> 12.1 us  [expert_rows(): pl.pallas_call(functools.partial(expert_kernel, group_count), out_shape=t...]
  transfers between devices with their start and end apart: 22 -> 22, of which waited for: 11 -> 11; matrix products, arithmetic and copies ran while one was open for 14% -> 13% of each run, Pallas kernels for 14% -> 13%
where the time goes in v10:
time: 110 us
  waiting for transfers between devices  36.2 us (33%)
  starting transfers between devices  26.1 us (24%)
  local copies, waits for them, and re-layouts  19.3 us (18%)
  Pallas kernels  15.9 us (14%)
  other arithmetic  7.62 us (7%)
  matrix products  3.79 us (3%)
    ppermute x22, waiting for transfers between devices, flip(): lax.ppermute(values, axis, [(i, i ^ bit) for i in range(lax.axis_size(axi...  36.2 us
    ppermute x22, starting transfers between devices, flip(): lax.ppermute(values, axis, [(i, i ^ bit) for i in range(lax.axis_size(axi...  26.1 us
    unnamed x42, local copies, waits for them, and re-layouts  15.3 us
    pallas_call x4, Pallas kernels, expert_rows(): pl.pallas_call(functools.partial(expert_kernel, group_count), out_shape=t...  12.1 us
    convert_element_type x7, other arithmetic, narrow(): return values.astype(jnp.bfloat16)  4.12 us
    pallas_call x1, Pallas kernels, early_terms(): pl.pallas_call(terms_kernel, out_shape=(jax.ShapeDtypeStruct((tok_cols.sh...  2.7 us
    dot_general x2, matrix products, input_part(): return narrow(jnp.dot(back, gate_up.T, preferred_element_type=jnp.float32))  2.59 us
    squeeze x5, local copies, waits for them, and re-layouts, take(): return lax.dynamic_index_in_dim(values, index, axis, keepdims=False)  2.42 us
  transfers between devices with their start and end apart: 22, of which 11 were waited for; matrix products, arithmetic and copies ran while one was open for 13% of the time, Pallas kernels for 13%

profile of v10, /device:TPU:0, one launch (start us, length us, event | category | flops | bytes accessed | tf_op | source)
XLA Modules:
  0.0 109.9 jit_solution(12684744329034390548)
XLA Ops:
  5.2 3.1 %collective-permute-start.2 = (bf16[128,4224]{1,0:T(8,128)(2,1)}, bf16[128,4224]{1,0:T(8,128)(2,1)S(1)}, u32[]{:S(2)}, u32[]{:S(2)}) collective-permute-start(bf16[128,4224]{1,0:T(8,128)(2,1)} %shard_map.94.refs_0_), channel_id=1, source_target_pairs={{0,8},{4,12},{8,0},{12,4},{16,24},{20,28},{24,16},{28,20},{1,9},{5... | collective-permute-start | bytes 3244040 | tf_op jit(solution)/shard_map/ppermute | solution.py:23
  8.2 1.5 %collective-permute-start.1 = (bf16[128,4224]{1,0:T(8,128)(2,1)}, bf16[128,4224]{1,0:T(8,128)(2,1)}, u32[]{:S(2)}, u32[]{:S(2)}) collective-permute-start(bf16[128,4224]{1,0:T(8,128)(2,1)} %shard_map.94.refs_0_), channel_id=1, source_target_pairs={{0,2},{1,3},{2,0},{3,1},{4,6},{5,7},{6,4},{7,5},{8,10},{9,11},{10,... | collective-permute-start | bytes 3244040 | tf_op jit(solution)/shard_map/ppermute | solution.py:23
  9.7 2.3 %dynamic-slice_bitcast_fusion.1 = (bf16[1,2,64,2048]{3,2,1,0:T(8,128)(2,1)}, bf16[1,2,64,2048]{3,2,1,0:T(8,128)(2,1)}) fusion(bf16[1,2,2,2,64,2048]{5,4,3,2,1,0:T(8,128)(2,1)} %bitcast.77, s32[]{:T(128)S(6)} %select_n.72, s32[]{:T(128)S(6)} %select_n.70, s32[]{:T(128)S(6)} %select_n.66), kind=kLoop, calls=%fused_computation.33 | loop fusion | bytes 2097164 | tf_op jit(solution)/shard_map/jit(dynamic_index_in_dim)/squeeze | solution.py:27
  12.0 1.5 %collective-permute-start.3 = (bf16[1,2,64,2048]{3,2,1,0:T(8,128)(2,1)}, bf16[1,2,64,2048]{3,2,1,0:T(8,128)(2,1)}, u32[]{:S(2)}, u32[]{:S(2)}) collective-permute-start(bf16[1,2,64,2048]{3,2,1,0:T(8,128)(2,1)} %get-tuple-element.72), channel_id=1, source_target_pairs={{0,4},{4,0},{8,12},{12,8},{16,20},{20,16},{24,28},{28,24},{1,5},{5... | collective-permute-start | bytes 1572872 | tf_op jit(solution)/shard_map/ppermute | solution.py:23
  13.6 13.1 %collective-permute-done.3 = bf16[1,2,64,2048]{3,2,1,0:T(8,128)(2,1)} collective-permute-done((bf16[1,2,64,2048]{3,2,1,0:T(8,128)(2,1)}, bf16[1,2,64,2048]{3,2,1,0:T(8,128)(2,1)}, u32[]{:S(2)}, u32[]{:S(2)}) %collective-permute-start.3) | collective-permute-done | bytes 524320 | tf_op jit(solution)/shard_map/ppermute | solution.py:23
  26.7 1.3 %fusion.6.refs_2_ = bf16[1,2,64,2048]{3,2,1,0:T(8,128)(2,1)S(1)} fusion(bf16[1,2,64,2048]{3,2,1,0:T(8,128)(2,1)} %collective-permute-done.3, bf16[1,2,2,2,64,2048]{5,4,3,2,1,0:T(8,128)(2,1)} %bitcast.78, s32[]{:T(128)S(6)} %select_n.66, s32[]{:T(128)S(6)} %select_n.68), kind=kLoop, calls=%fused_computation.15 | loop fusion | flops 1048576 | bytes 1572872 | tf_op jit(solution)/shard_map/convert_element_type | solution.py:19
  28.0 2.2 %copy-done = bf16[1,2048,1024]{2,1,0:T(8,128)(2,1)S(1)} copy-done((bf16[1,2048,1024]{2,1,0:T(8,128)(2,1)S(1)}, bf16[1,2048,1024]{2,1,0:T(8,128)(2,1)}, u32[]{:S(2)}) %copy-start) | copy-done | bytes 4194328
  30.2 3.5 %shard_map.95 = (bf16[256,1024]{1,0:T(8,128)(2,1)S(1)}, bf16[256,256]{1,0:T(8,128)(2,1)S(1)}, bf16[256,2048]{1,0:T(8,128)(2,1)S(1)}, bf16[128,1024]{1,0:T(8,128)(2,1)S(1)}, bf16[128,1024]{1,0:T(8,128)(2,1)S(1)}) custom-call(s32[2]{0:T(128)S(1)} %pad_add_fusion.place, bf16[128,4224]{1,0:T(8,128)(2,1)} %shard_map.94.refs_0_, ...), custom_call_target="tpu_custom_call" | custom-call | tf_op jit(solution)/shard_map/pallas_call | solution.py:123
  34.4 1.3 %slice.21 = bf16[64,4224]{1,0:T(8,128)(2,1)S(1)} slice(bf16[128,4224]{1,0:T(8,128)(2,1)} %get-tuple-element.39.refs_0_), slice={[0:64], [0:4224]} | slice | bytes 1081344 | tf_op jit(solution)/shard_map/slice | solution.py:218
  35.8 1.6 %collective-permute-start.7 = (bf16[64,4224]{1,0:T(8,128)(2,1)S(1)}, bf16[64,4224]{1,0:T(8,128)(2,1)}, u32[]{:S(2)}, u32[]{:S(2)}) collective-permute-start(bf16[64,4224]{1,0:T(8,128)(2,1)S(1)} %slice.22), channel_id=1, source_target_pairs={{0,2},{1,3},{2,0},{3,1},{4,6},{5,7},{6,4},{7,5},{8,10},{9,11},{10,... | collective-permute-start | bytes 1622024 | tf_op jit(solution)/shard_map/ppermute | solution.py:23
  37.8 1.5 %collective-permute-start.8 = (bf16[1,2,64,2048]{3,2,1,0:T(8,128)(2,1)S(1)}, bf16[1,2,64,2048]{3,2,1,0:T(8,128)(2,1)S(1)}, u32[]{:S(2)}, u32[]{:S(2)}) collective-permute-start(bf16[1,2,64,2048]{3,2,1,0:T(8,128)(2,1)S(1)} %get-tuple-element.57), channel_id=1, source_target_pairs={{0,4},{4,0},{8,12},{12,8},{16,20},{20,16},{24,28},{28,24},{1,5},{5... | collective-permute-start | bytes 1572872 | tf_op jit(solution)/shard_map/ppermute | solution.py:23
  39.3 3.1 %shard_map.97 = (bf16[256,1024]{1,0:T(8,128)(2,1)S(1)}, bf16[256,256]{1,0:T(8,128)(2,1)S(1)}, bf16[256,2048]{1,0:T(8,128)(2,1)S(1)}, bf16[128,1024]{1,0:T(8,128)(2,1)S(1)}, bf16[128,1024]{1,0:T(8,128)(2,1)S(1)}) custom-call(s32[2]{0:T(128)S(1)} %pad_add_fusion.place, bf16[128,4224]{1,0:T(8,128)(2,1)} %get-tuple-element.39.refs_0_, ...), custom_call_target="tpu_custom_call" | custom-call | tf_op jit(solution)/shard_map/pallas_call | solution.py:123
  42.4 2.5 %shard_map.98 = (bf16[256,1024]{1,0:T(8,128)(2,1)S(1)}, bf16[256,256]{1,0:T(8,128)(2,1)S(1)}, bf16[256,2048]{1,0:T(8,128)(2,1)S(1)}, bf16[128,1024]{1,0:T(8,128)(2,1)S(1)}, bf16[128,1024]{1,0:T(8,128)(2,1)S(1)}) custom-call(s32[2]{0:T(128)S(1)} %pad_add_fusion.place, bf16[128,4224]{1,0:T(8,128)(2,1)S(1)} %get-tuple-element.48.refs_0_, ...), custom_call_target="tpu_custom_call" | custom-call | tf_op jit(solution)/shard_map/pallas_call | solution.py:123
  44.9 2.7 %shard_map.99 = (f32[1024,1024]{1,0:T(8,128)S(1)}, f32[256,2048]{1,0:T(8,128)S(1)}, bf16[256,1024]{1,0:T(8,128)(2,1)S(1)}, f32[8,128]{1,0:T(8,128)S(1)}) custom-call(bf16[256,1024]{1,0:T(8,128)(2,1)S(1)} %get-tuple-element.41.refs_0_, bf16[256,256]{1,0:T(8,128)(2,1)S(1)} %get-tuple-element.38.refs_4_.refs_1_, ...), custom_call_target="tpu_custom_call" | custom-call | tf_op jit(solution)/shard_map/pallas_call | solution.py:167
  47.6 2.0 %copy-done.6 = f32[1024,1024]{1,0:T(8,128)} copy-done((f32[1024,1024]{1,0:T(8,128)}, f32[1024,1024]{1,0:T(8,128)S(1)}, u32[]{:S(2)}) %copy-start.6) | copy-done | bytes 4194328
  53.8 1.6 %collective-permute-start.19 = (bf16[1,2,64,2048]{3,2,1,0:T(8,128)(2,1)}, bf16[1,2,64,2048]{3,2,1,0:T(8,128)(2,1)S(1)}, u32[]{:S(2)}, u32[]{:S(2)}) collective-permute-start(bf16[1,2,64,2048]{3,2,1,0:T(8,128)(2,1)} %copy-done.5), channel_id=1, source_target_pairs={{0,8},{4,12},{8,0},{12,4},{16,24},{20,28},{24,16},{28,20},{1,9},{5... | collective-permute-start | bytes 1572872 | tf_op jit(solution)/shard_map/ppermute | solution.py:23
  56.2 2.2 %copy-done.2 = bf16[1,2048,1024]{2,1,0:T(8,128)(2,1)S(1)} copy-done((bf16[1,2048,1024]{2,1,0:T(8,128)(2,1)S(1)}, bf16[1,2048,1024]{2,1,0:T(8,128)(2,1)}, u32[]{:S(2)}) %copy-start.2) | copy-done | bytes 4194328
  58.4 3.1 %shard_map.101 = (bf16[256,1024]{1,0:T(8,128)(2,1)S(1)}, bf16[256,256]{1,0:T(8,128)(2,1)S(1)}, bf16[256,2048]{1,0:T(8,128)(2,1)S(1)}, bf16[128,1024]{1,0:T(8,128)(2,1)S(1)}, bf16[128,1024]{1,0:T(8,128)(2,1)S(1)}) custom-call(s32[2]{0:T(128)S(1)} %pad_add_fusion.place, bf16[64,4224]{1,0:T(8,128)(2,1)} %get-tuple-element.59.refs_0_, ...), custom_call_target="tpu_custom_call" | custom-call | tf_op jit(solution)/shard_map/pallas_call | solution.py:123
  62.3 1.4 %copy-done.7 = f32[1024,1024]{1,0:T(8,128)S(1)} copy-done((f32[1024,1024]{1,0:T(8,128)S(1)}, f32[1024,1024]{1,0:T(8,128)}, u32[]{:S(2)}) %copy-start.7) | copy-done | bytes 4194328
  63.7 1.3 %add_convert_fusion = bf16[1024,1024]{1,0:T(8,128)(2,1)S(1)} fusion(f32[1024,1024]{1,0:T(8,128)S(1)} %copy-done.7, f32[1024,1024]{1,0:T(8,128)S(1)} %fusion.11), kind=kLoop, calls=%fused_computation | loop fusion | flops 2097152 | bytes 10485760 | tf_op jit(solution)/shard_map/convert_element_type | solution.py:19
  67.4 1.3 %convolution_convert_fusion = bf16[256,2048]{1,0:T(8,128)(2,1)S(1)} fusion(bf16[256,1024]{1,0:T(8,128)(2,1)S(1)} %shard_map.102, bf16[1,2048,1024]{2,1,0:T(8,128)(2,1)S(1)} %copy-done.3), kind=kOutput, calls=%fused_computation.1 | convolution fusion | flops 1074266112 | bytes 5767168 | tf_op jit(solution)/shard_map/dot_general | solution.py:261
  70.9 1.7 %collective-permute-done.15.refs_2_ = bf16[1,96,1024]{2,1,0:T(8,128)(2,1)S(1)} collective-permute-done((bf16[1,96,1024]{2,1,0:T(8,128)(2,1)S(1)}, bf16[1,96,1024]{2,1,0:T(8,128)(2,1)S(1)}, u32[]{:S(2)}, u32[]{:S(2)}) %collective-permute-start.15) | collective-permute-done | bytes 196640 | tf_op jit(solution)/shard_map/ppermute | solution.py:23
  72.7 2.7 %collective-permute-start.16 = (bf16[1,96,1024]{2,1,0:T(8,128)(2,1)S(1)}, bf16[1,96,1024]{2,1,0:T(8,128)(2,1)S(1)}, u32[]{:S(2)}, u32[]{:S(2)}) collective-permute-start(bf16[1,96,1024]{2,1,0:T(8,128)(2,1)S(1)} %fusion.20), channel_id=1, source_target_pairs={{0,16},{4,20},{8,24},{12,28},{16,0},{20,4},{24,8},{28,12},{1,17},{... | collective-permute-start | bytes 589832 | tf_op jit(solution)/shard_map/ppermute | solution.py:23
  76.3 1.2 %fusion.3 = f32[1,2,64,2048]{3,2,1,0:T(8,128)S(1)} fusion(bf16[1,2,64,2048]{3,2,1,0:T(8,128)(2,1)S(1)} %get-tuple-element.69, bf16[1,2,64,2048]{3,2,1,0:T(8,128)(2,1)S(1)} %copy-done.11, bf16[1,2,2,2,64,2048]{5,4,3,2,1,0:T(8,128)(2,1)} %bitcast.79, s32[]{:T(128)S(6)} %select_n.72, s32[]{:T(128)S(6)} %select_n.68), kind=kLoop, calls=%fused_computation.10 | loop fusion | flops 1310720 | bytes 2621448 | tf_op jit(solution)/shard_map/add | solution.py:256
  77.5 1.3 %fusion.1 = f32[256,2048]{1,0:T(8,128)S(1)} fusion(bf16[256,2048]{1,0:T(8,128)(2,1)S(1)} %collective-permute-done.11, bf16[128,1024]{1,0:T(8,128)(2,1)S(1)} %copy-done.18, bf16[128,1024]{1,0:T(8,128)(2,1)S(1)} %get-tuple-element.37.refs_3_, bf16[1,2048,1024]{2,1,0:T(8,128)(2,1)S(1)} %copy-done.3), kind=kOutput, calls=%fused_computation.4 | convolution fusion | flops 1076887552 | bytes 7864320 | tf_op jit(solution)/shard_map/dot_general | solution.py:261
  79.9 2.5 %collective-permute-start.17 = (bf16[1,160,1024]{2,1,0:T(8,128)(2,1)S(1)}, bf16[1,160,1024]{2,1,0:T(8,128)(2,1)S(1)}, u32[]{:S(2)}, u32[]{:S(2)}) collective-permute-start(bf16[1,160,1024]{2,1,0:T(8,128)(2,1)S(1)} %fusion.7), channel_id=1, source_target_pairs={{0,16},{4,20},{8,24},{12,28},{16,0},{20,4},{24,8},{28,12},{1,17},{... | collective-permute-start | bytes 983048 | tf_op jit(solution)/shard_map/ppermute | solution.py:23
  83.3 1.9 %collective-permute-done.20 = bf16[1,64,2048]{2,1,0:T(8,128)(2,1)S(1)} collective-permute-done((bf16[1,64,2048]{2,1,0:T(8,128)(2,1)S(1)}, bf16[1,64,2048]{2,1,0:T(8,128)(2,1)S(1)}, u32[]{:S(2)}, u32[]{:S(2)}) %collective-permute-start.20) | collective-permute-done | bytes 262176 | tf_op jit(solution)/shard_map/ppermute | solution.py:23
  85.3 2.7 %collective-permute-start.21 = (bf16[1,64,2048]{2,1,0:T(8,128)(2,1)S(1)}, bf16[1,64,2048]{2,1,0:T(8,128)(2,1)S(1)}, u32[]{:S(2)}, u32[]{:S(2)}) collective-permute-start(bf16[1,64,2048]{2,1,0:T(8,128)(2,1)S(1)} %fusion.16), channel_id=1, source_target_pairs={{0,16},{4,20},{8,24},{12,28},{16,0},{20,4},{24,8},{28,12},{1,17},{... | collective-permute-start | bytes 786440 | tf_op jit(solution)/shard_map/ppermute | solution.py:23
  88.0 3.3 %collective-permute-done.12.refs_1_ = bf16[128,2048]{1,0:T(8,128)(2,1)S(1)} collective-permute-done((bf16[128,2048]{1,0:T(8,128)(2,1)S(1)}, bf16[128,2048]{1,0:T(8,128)(2,1)S(1)}, u32[]{:S(2)}, u32[]{:S(2)}) %collective-permute-start.12) | collective-permute-done | bytes 524320 | tf_op jit(solution)/shard_map/ppermute | solution.py:23
  93.3 10.8 %collective-permute-done.17.refs_0_ = bf16[1,160,1024]{2,1,0:T(8,128)(2,1)S(1)} collective-permute-done((bf16[1,160,1024]{2,1,0:T(8,128)(2,1)S(1)}, bf16[1,160,1024]{2,1,0:T(8,128)(2,1)S(1)}, u32[]{:S(2)}, u32[]{:S(2)}) %collective-permute-start.17) | collective-permute-done | bytes 327712 | tf_op jit(solution)/shard_map/ppermute | solution.py:23
  104.1 1.2 %fusion.5 = f32[1,256,1024]{2,1,0:T(8,128)} fusion(bf16[1,256,1024]{2,1,0:T(8,128)(2,1)S(1)} %collective-permute-done.14, bf16[1,160,1024]{2,1,0:T(8,128)(2,1)S(1)} %shard_map.105, bf16[1,96,1024]{2,1,0:T(8,128)(2,1)S(1)} %collective-permute-done.16, bf16[1,2,2,256,1024]{4,3,2,1,0:T(8,128)(2,1)S(1)} %bitcast.73, s32[]{:T(128)S(6)} %select_n.76, s32[]{:T(128)S(6)} %select_n.68), kind=kLoop, calls=%fused_computation.13 | loop fusion | flops 2359296 | bytes 2621448 | tf_op jit(solution)/shard_map/mul | solution.py:285
  105.3 3.6 %collective-permute-done.21 = bf16[1,64,2048]{2,1,0:T(8,128)(2,1)S(1)} collective-permute-done((bf16[1,64,2048]{2,1,0:T(8,128)(2,1)S(1)}, bf16[1,64,2048]{2,1,0:T(8,128)(2,1)S(1)}, u32[]{:S(2)}, u32[]{:S(2)}) %collective-permute-start.21) | collective-permute-done | bytes 262176 | tf_op jit(solution)/shard_map/ppermute | solution.py:23
  (92 shorter events, 22.0 us)
Async XLA Ops:
  5.1 22.9 %copy-start.4 = (bf16[1,512,2048]{2,1,0:T(8,128)(2,1)S(1)}, bf16[1,512,2048]{2,1,0:T(8,128)(2,1)}, u32[]{:S(2)}) copy-start(bf16[1,512,2048]{2,1,0:T(8,128)(2,1)} %param.12) | copy-start | bytes 6291460
  5.2 28.5 %collective-permute-start.2 = (bf16[128,4224]{1,0:T(8,128)(2,1)}, bf16[128,4224]{1,0:T(8,128)(2,1)S(1)}, u32[]{:S(2)}, u32[]{:S(2)}) collective-permute-start(bf16[128,4224]{1,0:T(8,128)(2,1)} %shard_map.94.refs_0_), channel_id=1, source_target_pairs={{0,8},{4,12},{8,0},{12,4},{16,24},{20,28},{24,16},{28,20},{1,9},{5... | collective-permute-start | bytes 3244040 | tf_op jit(solution)/shard_map/ppermute | solution.py:23
  8.2 25.6 %collective-permute-start.1 = (bf16[128,4224]{1,0:T(8,128)(2,1)}, bf16[128,4224]{1,0:T(8,128)(2,1)}, u32[]{:S(2)}, u32[]{:S(2)}) collective-permute-start(bf16[128,4224]{1,0:T(8,128)(2,1)} %shard_map.94.refs_0_), channel_id=1, source_target_pairs={{0,2},{1,3},{2,0},{3,1},{4,6},{5,7},{6,4},{7,5},{8,10},{9,11},{10,... | collective-permute-start | bytes 3244040 | tf_op jit(solution)/shard_map/ppermute | solution.py:23
  9.7 18.3 %collective-permute-start = (bf16[128,4224]{1,0:T(8,128)(2,1)}, bf16[128,4224]{1,0:T(8,128)(2,1)}, u32[]{:S(2)}, u32[]{:S(2)}) collective-permute-start(bf16[128,4224]{1,0:T(8,128)(2,1)} %shard_map.94.refs_0_), channel_id=1, source_target_pairs={{0,1},{1,0},{2,3},{3,2},{4,5},{5,4},{6,7},{7,6},{8,9},{9,8},{10,11... | collective-permute-start | bytes 3244040 | tf_op jit(solution)/shard_map/ppermute | solution.py:23
  12.0 14.7 %collective-permute-start.3 = (bf16[1,2,64,2048]{3,2,1,0:T(8,128)(2,1)}, bf16[1,2,64,2048]{3,2,1,0:T(8,128)(2,1)}, u32[]{:S(2)}, u32[]{:S(2)}) collective-permute-start(bf16[1,2,64,2048]{3,2,1,0:T(8,128)(2,1)} %get-tuple-element.72), channel_id=1, source_target_pairs={{0,4},{4,0},{8,12},{12,8},{16,20},{20,16},{24,28},{28,24},{1,5},{5... | collective-permute-start | bytes 1572872 | tf_op jit(solution)/shard_map/ppermute | solution.py:23
  28.0 2.2 %copy-start = (bf16[1,2048,1024]{2,1,0:T(8,128)(2,1)S(1)}, bf16[1,2048,1024]{2,1,0:T(8,128)(2,1)}, u32[]{:S(2)}) copy-start(bf16[1,2048,1024]{2,1,0:T(8,128)(2,1)} %param.11) | copy-start | bytes 12582916
  30.2 3.7 %copy-start.12 = (bf16[1,2,64,2048]{3,2,1,0:T(8,128)(2,1)S(1)}, bf16[1,2,64,2048]{3,2,1,0:T(8,128)(2,1)}, u32[]{:S(2)}) copy-start(bf16[1,2,64,2048]{3,2,1,0:T(8,128)(2,1)} %get-tuple-element.71.refs_3_) | copy-start | bytes 1572868
  33.9 5.4 %copy-start.1 = (bf16[1,2048,1024]{2,1,0:T(8,128)(2,1)S(1)}, bf16[1,2048,1024]{2,1,0:T(8,128)(2,1)}, u32[]{:S(2)}) copy-start(bf16[1,2048,1024]{2,1,0:T(8,128)(2,1)} %param.11) | copy-start | bytes 12582916
  33.9 5.4 %collective-permute-start.4 = (bf16[128,4224]{1,0:T(8,128)(2,1)}, bf16[128,4224]{1,0:T(8,128)(2,1)S(1)}, u32[]{:S(2)}, u32[]{:S(2)}) collective-permute-start(bf16[128,4224]{1,0:T(8,128)(2,1)} %get-tuple-element.39.refs_0_), channel_id=1, source_target_pairs={{0,1},{1,0},{2,3},{3,2},{4,5},{5,4},{6,7},{7,6},{8,9},{9,8},{10,11... | collective-permute-start | bytes 3244040 | tf_op jit(solution)/shard_map/ppermute | solution.py:23
  33.9 8.5 %collective-permute-start.5 = (bf16[128,4224]{1,0:T(8,128)(2,1)S(1)}, bf16[128,4224]{1,0:T(8,128)(2,1)S(1)}, u32[]{:S(2)}, u32[]{:S(2)}) collective-permute-start(bf16[128,4224]{1,0:T(8,128)(2,1)S(1)} %get-tuple-element.48.refs_0_), channel_id=1, source_target_pairs={{0,1},{1,0},{2,3},{3,2},{4,5},{5,4},{6,7},{7,6},{8,9},{9,8},{10,11... | collective-permute-start | bytes 3244040 | tf_op jit(solution)/shard_map/ppermute | solution.py:23
  35.8 15.1 %collective-permute-start.7 = (bf16[64,4224]{1,0:T(8,128)(2,1)S(1)}, bf16[64,4224]{1,0:T(8,128)(2,1)}, u32[]{:S(2)}, u32[]{:S(2)}) collective-permute-start(bf16[64,4224]{1,0:T(8,128)(2,1)S(1)} %slice.22), channel_id=1, source_target_pairs={{0,2},{1,3},{2,0},{3,1},{4,6},{5,7},{6,4},{7,5},{8,10},{9,11},{10,... | collective-permute-start | bytes 1622024 | tf_op jit(solution)/shard_map/ppermute | solution.py:23
  37.3 13.8 %collective-permute-start.6 = (bf16[64,4224]{1,0:T(8,128)(2,1)S(1)}, bf16[64,4224]{1,0:T(8,128)(2,1)}, u32[]{:S(2)}, u32[]{:S(2)}) collective-permute-start(bf16[64,4224]{1,0:T(8,128)(2,1)S(1)} %slice.21), channel_id=1, source_target_pairs={{0,8},{4,12},{8,0},{12,4},{16,24},{20,28},{24,16},{28,20},{1,9},{5... | collective-permute-start | bytes 1622024 | tf_op jit(solution)/shard_map/ppermute | solution.py:23
  37.8 13.1 %collective-permute-start.8 = (bf16[1,2,64,2048]{3,2,1,0:T(8,128)(2,1)S(1)}, bf16[1,2,64,2048]{3,2,1,0:T(8,128)(2,1)S(1)}, u32[]{:S(2)}, u32[]{:S(2)}) collective-permute-start(bf16[1,2,64,2048]{3,2,1,0:T(8,128)(2,1)S(1)} %get-tuple-element.57), channel_id=1, source_target_pairs={{0,4},{4,0},{8,12},{12,8},{16,20},{20,16},{24,28},{28,24},{1,5},{5... | collective-permute-start | bytes 1572872 | tf_op jit(solution)/shard_map/ppermute | solution.py:23
  42.4 2.5 %copy-start.17 = (bf16[128,1024]{1,0:T(8,128)(2,1)}, bf16[128,1024]{1,0:T(8,128)(2,1)S(1)}, u32[]{:S(2)}) copy-start(bf16[128,1024]{1,0:T(8,128)(2,1)S(1)} %get-tuple-element.40.refs_8_) | copy-start | bytes 786436
  53.3 2.1 %collective-permute-start.9 = (bf16[64,4224]{1,0:T(8,128)(2,1)}, bf16[64,4224]{1,0:T(8,128)(2,1)S(1)}, u32[]{:S(2)}, u32[]{:S(2)}) collective-permute-start(bf16[64,4224]{1,0:T(8,128)(2,1)} %get-tuple-element.59.refs_0_), channel_id=1, source_target_pairs={{0,1},{1,0},{2,3},{3,2},{4,5},{5,4},{6,7},{7,6},{8,9},{9,8},{10,11... | collective-permute-start | bytes 1622024 | tf_op jit(solution)/shard_map/ppermute | solution.py:23
  53.3 2.9 %collective-permute-start.10 = (bf16[64,4224]{1,0:T(8,128)(2,1)}, bf16[64,4224]{1,0:T(8,128)(2,1)S(1)}, u32[]{:S(2)}, u32[]{:S(2)}) collective-permute-start(bf16[64,4224]{1,0:T(8,128)(2,1)} %get-tuple-element.60.refs_1_), channel_id=1, source_target_pairs={{0,1},{1,0},{2,3},{3,2},{4,5},{5,4},{6,7},{7,6},{8,9},{9,8},{10,11... | collective-permute-start | bytes 1622024 | tf_op jit(solution)/shard_map/ppermute | solution.py:23
  53.8 21.5 %collective-permute-start.19 = (bf16[1,2,64,2048]{3,2,1,0:T(8,128)(2,1)}, bf16[1,2,64,2048]{3,2,1,0:T(8,128)(2,1)S(1)}, u32[]{:S(2)}, u32[]{:S(2)}) collective-permute-start(bf16[1,2,64,2048]{3,2,1,0:T(8,128)(2,1)} %copy-done.5), channel_id=1, source_target_pairs={{0,8},{4,12},{8,0},{12,4},{16,24},{20,28},{24,16},{28,20},{1,9},{5... | collective-permute-start | bytes 1572872 | tf_op jit(solution)/shard_map/ppermute | solution.py:23
  56.2 2.2 %copy-start.2 = (bf16[1,2048,1024]{2,1,0:T(8,128)(2,1)S(1)}, bf16[1,2048,1024]{2,1,0:T(8,128)(2,1)}, u32[]{:S(2)}) copy-start(bf16[1,2048,1024]{2,1,0:T(8,128)(2,1)} %param.11) | copy-start | bytes 12582916
  61.5 2.2 %copy-start.7 = (f32[1024,1024]{1,0:T(8,128)S(1)}, f32[1024,1024]{1,0:T(8,128)}, u32[]{:S(2)}) copy-start(f32[1024,1024]{1,0:T(8,128)} %copy-done.6) | copy-start | bytes 12582916
  65.1 2.3 %copy-start.3 = (bf16[1,2048,1024]{2,1,0:T(8,128)(2,1)S(1)}, bf16[1,2048,1024]{2,1,0:T(8,128)(2,1)}, u32[]{:S(2)}) copy-start(bf16[1,2048,1024]{2,1,0:T(8,128)(2,1)} %param.11) | copy-start | bytes 12582916
  65.3 7.3 %collective-permute-start.15 = (bf16[1,96,1024]{2,1,0:T(8,128)(2,1)S(1)}, bf16[1,96,1024]{2,1,0:T(8,128)(2,1)S(1)}, u32[]{:S(2)}, u32[]{:S(2)}) collective-permute-start(bf16[1,96,1024]{2,1,0:T(8,128)(2,1)S(1)} %dynamic-slice_bitcast_fusion.6.refs_1_), channel_id=1, source_target_pairs={{0,4},{4,0},{8,12},{12,8},{16,20},{20,16},{24,28},{28,24},{1,5},{5... | collective-permute-start | bytes 589832 | tf_op jit(solution)/shard_map/ppermute | solution.py:23
  68.7 8.8 %collective-permute-start.11 = (bf16[256,2048]{1,0:T(8,128)(2,1)S(1)}, bf16[256,2048]{1,0:T(8,128)(2,1)S(1)}, u32[]{:S(2)}, u32[]{:S(2)}) collective-permute-start(bf16[256,2048]{1,0:T(8,128)(2,1)S(1)} %convolution_convert_fusion), channel_id=1, source_target_pairs={{0,1},{1,0},{2,3},{3,2},{4,5},{5,4},{6,7},{7,6},{8,9},{9,8},{10,11... | collective-permute-start | bytes 3145736 | tf_op jit(solution)/shard_map/ppermute | solution.py:23
  68.9 10.9 %collective-permute-start.13 = (bf16[1,160,1024]{2,1,0:T(8,128)(2,1)S(1)}, bf16[1,160,1024]{2,1,0:T(8,128)(2,1)S(1)}, u32[]{:S(2)}, u32[]{:S(2)}) collective-permute-start(bf16[1,160,1024]{2,1,0:T(8,128)(2,1)S(1)} %dynamic-slice_bitcast_fusion.3), channel_id=1, source_target_pairs={{0,4},{4,0},{8,12},{12,8},{16,20},{20,16},{24,28},{28,24},{1,5},{5... | collective-permute-start | bytes 983048 | tf_op jit(solution)/shard_map/ppermute | solution.py:23
  70.8 5.5 %copy-start.11 = (bf16[1,2,64,2048]{3,2,1,0:T(8,128)(2,1)S(1)}, bf16[1,2,64,2048]{3,2,1,0:T(8,128)(2,1)}, u32[]{:S(2)}) copy-start(bf16[1,2,64,2048]{3,2,1,0:T(8,128)(2,1)} %copy-done.10) | copy-start | bytes 1572868
  70.9 6.7 %copy-start.18 = (bf16[128,1024]{1,0:T(8,128)(2,1)S(1)}, bf16[128,1024]{1,0:T(8,128)(2,1)}, u32[]{:S(2)}) copy-start(bf16[128,1024]{1,0:T(8,128)(2,1)} %copy-done.17) | copy-start | bytes 786436
  72.7 31.4 %collective-permute-start.16 = (bf16[1,96,1024]{2,1,0:T(8,128)(2,1)S(1)}, bf16[1,96,1024]{2,1,0:T(8,128)(2,1)S(1)}, u32[]{:S(2)}, u32[]{:S(2)}) collective-permute-start(bf16[1,96,1024]{2,1,0:T(8,128)(2,1)S(1)} %fusion.20), channel_id=1, source_target_pairs={{0,16},{4,20},{8,24},{12,28},{16,0},{20,4},{24,8},{28,12},{1,17},{... | collective-permute-start | bytes 589832 | tf_op jit(solution)/shard_map/ppermute | solution.py:23
  75.3 9.9 %collective-permute-start.20 = (bf16[1,64,2048]{2,1,0:T(8,128)(2,1)S(1)}, bf16[1,64,2048]{2,1,0:T(8,128)(2,1)S(1)}, u32[]{:S(2)}, u32[]{:S(2)}) collective-permute-start(bf16[1,64,2048]{2,1,0:T(8,128)(2,1)S(1)} %get-tuple-element.70), channel_id=1, source_target_pairs={{0,4},{4,0},{8,12},{12,8},{16,20},{20,16},{24,28},{28,24},{1,5},{5... | collective-permute-start | bytes 786440 | tf_op jit(solution)/shard_map/ppermute | solution.py:23
  78.9 12.4 %collective-permute-start.12 = (bf16[128,2048]{1,0:T(8,128)(2,1)S(1)}, bf16[128,2048]{1,0:T(8,128)(2,1)S(1)}, u32[]{:S(2)}, u32[]{:S(2)}) collective-permute-start(bf16[128,2048]{1,0:T(8,128)(2,1)S(1)} %slice.35), channel_id=1, source_target_pairs={{0,2},{1,3},{2,0},{3,1},{4,6},{5,7},{6,4},{7,5},{8,10},{9,11},{10,... | collective-permute-start | bytes 1572872 | tf_op jit(solution)/shard_map/ppermute | solution.py:23
  79.9 24.2 %collective-permute-start.17 = (bf16[1,160,1024]{2,1,0:T(8,128)(2,1)S(1)}, bf16[1,160,1024]{2,1,0:T(8,128)(2,1)S(1)}, u32[]{:S(2)}, u32[]{:S(2)}) collective-permute-start(bf16[1,160,1024]{2,1,0:T(8,128)(2,1)S(1)} %fusion.7), channel_id=1, source_target_pairs={{0,16},{4,20},{8,24},{12,28},{16,0},{20,4},{24,8},{28,12},{1,17},{... | collective-permute-start | bytes 983048 | tf_op jit(solution)/shard_map/ppermute | solution.py:23
  82.4 21.7 %collective-permute-start.14 = (bf16[1,256,1024]{2,1,0:T(8,128)(2,1)S(1)}, bf16[1,256,1024]{2,1,0:T(8,128)(2,1)S(1)}, u32[]{:S(2)}, u32[]{:S(2)}) collective-permute-start(bf16[1,256,1024]{2,1,0:T(8,128)(2,1)S(1)} %shard_map.103), channel_id=1, source_target_pairs={{0,4},{4,0},{8,12},{12,8},{16,20},{20,16},{24,28},{28,24},{1,5},{5... | collective-permute-start | bytes 1572872 | tf_op jit(solution)/shard_map/ppermute | solution.py:23
  85.3 23.6 %collective-permute-start.21 = (bf16[1,64,2048]{2,1,0:T(8,128)(2,1)S(1)}, bf16[1,64,2048]{2,1,0:T(8,128)(2,1)S(1)}, u32[]{:S(2)}, u32[]{:S(2)}) collective-permute-start(bf16[1,64,2048]{2,1,0:T(8,128)(2,1)S(1)} %fusion.16), channel_id=1, source_target_pairs={{0,16},{4,20},{8,24},{12,28},{16,0},{20,4},{24,8},{28,12},{1,17},{... | collective-permute-start | bytes 786440 | tf_op jit(solution)/shard_map/ppermute | solution.py:23
  91.3 17.6 %collective-permute-start.18 = (bf16[1,64,2048]{2,1,0:T(8,128)(2,1)S(1)}, bf16[1,64,2048]{2,1,0:T(8,128)(2,1)S(1)}, u32[]{:S(2)}, u32[]{:S(2)}) collective-permute-start(bf16[1,64,2048]{2,1,0:T(8,128)(2,1)S(1)} %shard_map.104.refs_1_), channel_id=1, source_target_pairs={{0,4},{4,0},{8,12},{12,8},{16,20},{20,16},{24,28},{28,24},{1,5},{5... | collective-permute-start | bytes 786440 | tf_op jit(solution)/shard_map/ppermute | solution.py:23
  (11 other events, 12.2 us)

commit v11 on v10

--- a/solution.py
+++ b/solution.py
@@ -2,6 +2,7 @@
 
 import jax
 import jax.numpy as jnp
+import numpy as np
 from jax import lax
 from jax.experimental import pallas as pl
 from jax.experimental.pallas import tpu as pltpu
@@ -24,7 +25,10 @@
 
 
 def take(values, axis, index):
-    return lax.dynamic_index_in_dim(values, index, axis, keepdims=False)
+    starts = [np.uint32(0)] * values.ndim
+    starts[axis] = index
+    sizes = [1 if k == axis else size for k, size in enumerate(values.shape)]
+    return lax.squeeze(lax.dynamic_slice(values, starts, sizes), (axis,))
 
 
 def pack_kernel(expert_count, tokens, cotangent, ids, probs, packed, coded, sems):
@@ -188,10 +192,14 @@
     gate_up, down_matrix = gate_up_weight[0], down_weight[0]
     hidden_units = down_matrix.shape[0]
     me, group = lax.axis_index("expert"), lax.axis_index("dp")
-    bit0, bit1, bit2 = group & 1, (group >> 1) & 1, (group >> 2) & 1
+    bits = [lax.convert_element_type((group >> k) & 1, jnp.uint32) for k in range(3)]
+    bits += [1 - bit for bit in bits]
+    place = jnp.stack([me, (group >> 1) & 1]).astype(jnp.int32)
     high_count, half = group_count // 8, tok_rows // 2
 
     rows_own = packed(tokens, cotangent, expert_ids, gate_probs, expert_count)
+    rows_own, place, bits = lax.optimization_barrier((rows_own, place, bits))
+    bit0, bit1, bit2, not0, not1, not2 = bits
     rows_c = flip(rows_own, "expert", 1)
     rows_x, rows_n = flip(rows_own, "expert", 2), flip(rows_own, "dp", 2)
     residual = down_residual[0, 0].reshape(high_count, 2, 2, 2, -1, model_width)
@@ -203,15 +211,14 @@
     def residual_side(parity, first):
         return take(take(residual, 2, parity), 2, first)
 
-    res_other = flip(residual_side(1 - bit1, 1 - bit0), "dp", 1)
-    res_mine = residual_side(bit1, 1 - bit0)
-    place = jnp.stack([me, bit1]).astype(jnp.int32)
+    res_other = flip(residual_side(not1, not0), "dp", 1)
+    res_mine = residual_side(bit1, not0)
 
     def expert_on(*blocks):
         return expert_rows(group_count, place, blocks, gate_up, down_matrix)
 
     made = [expert_on(rows_own, rows_c)]
-    res_send = narrow(pair_sum(residual_side(1 - bit1, bit0), res_other))
+    res_send = narrow(pair_sum(residual_side(not1, bit0), res_other))
     rows_x, rows_n, res_send, res_mine = hold(
         (rows_x, rows_n, res_send, res_mine), (made[0][1],)
     )
@@ -241,8 +248,8 @@
     first = max(count * 3 // 8, 16)
     edges = [0, first, count]
     far_sent, far_kept = [
-        [side(gate_term[:, :, :, i:j], 1 - bit2, bit) for i, j in zip(edges, edges[1:])]
-        for bit in (1 - bit0, bit0)
+        [side(gate_term[:, :, :, i:j], not2, bit) for i, j in zip(edges, edges[1:])]
+        for bit in (not0, bit0)
     ]
     far_got = [flip(piece, "dp", 1) for piece in far_sent]
     crossed = [
@@ -250,12 +257,12 @@
     ]
     res_near = flip(res_send, "dp", 2)
     res_near, down_sent = hold(
-        (res_near, side(down_term, 1 - bit2, 1 - bit0)), (far_got[0],)
-    )
-    (near_sent,) = hold((side(gate_term, bit2, 1 - bit0),), (far_got[1],))
+        (res_near, side(down_term, not2, not0)), (far_got[0],)
+    )
+    (near_sent,) = hold((side(gate_term, bit2, not0),), (far_got[1],))
     res_sum = pair_sum(residual_side(bit1, bit0), res_mine) + wide(res_near)
-    far_down = pair_sum(side(down_term, 1 - bit2, bit0), flip(down_sent, "dp", 1))
-    crossed_down = flip(narrow(far_down + take(res_sum, 1, 1 - bit2)), "dp", 4)
+    far_down = pair_sum(side(down_term, not2, bit0), flip(down_sent, "dp", 1))
+    crossed_down = flip(narrow(far_down + take(res_sum, 1, not2)), "dp", 4)
 
     def input_part(back):
         return narrow(jnp.dot(back, gate_up.T, preferred_element_type=jnp.float32))
@@ -268,14 +275,14 @@
     token_grad = narrow(total[:tok_rows] + wide(across))
 
     near_gate = pair_sum(side(gate_term, bit2, bit0), flip(near_sent, "dp", 1))
-    (near_sent,) = hold((side(down_term, bit2, 1 - bit0),), (across,))
+    (near_sent,) = hold((side(down_term, bit2, not0),), (across,))
     near_down = pair_sum(side(down_term, bit2, bit0), flip(near_sent, "dp", 1))
     crossed[-1] = hold((crossed[-1],), (near_sent,))[0]
     gate_sum = near_gate + wide(jnp.concatenate(crossed, axis=1))
     down_sum = near_down + take(res_sum, 1, bit2) + wide(crossed_down)
     bit = 8
     while bit < group_count:
-        mine = (group // bit) & 1
+        mine = lax.convert_element_type((group // bit) & 1, jnp.uint32)
         halves = [v.reshape(-1, 2, *v.shape[1:]) for v in (gate_sum, down_sum)]
         gate_sum, down_sum = [
             take(v, 1, mine) + wide(flip(narrow(take(v, 1, 1 - mine)), "dp", bit)) for v in halves

time: 110 us -> 111 us (level)
  transfers between devices with their start and end apart: 22 -> 22, of which waited for: 11 -> 11; matrix products, arithmetic and copies ran while one was open for 13% -> 13% of each run, Pallas kernels for 13% -> 14%
where the time goes in v11:
time: 111 us; the launch traced here: 110 us
  waiting for transfers between devices  36.3 us (33%)
  starting transfers between devices  25.9 us (23%)
  local copies, waits for them, and re-layouts  19.4 us (17%)
  Pallas kernels  16.1 us (15%)
  other arithmetic  7.61 us (7%)
  matrix products  3.8 us (3%)
    ppermute x22, waiting for transfers between devices, flip(): lax.ppermute(values, axis, [(i, i ^ bit) for i in range(lax.axis_size(axi...  36.3 us
    ppermute x22, starting transfers between devices, flip(): lax.ppermute(values, axis, [(i, i ^ bit) for i in range(lax.axis_size(axi...  25.9 us
    unnamed x42, local copies, waits for them, and re-layouts  15.4 us
    pallas_call x4, Pallas kernels, expert_rows(): pl.pallas_call(functools.partial(expert_kernel, group_count), out_shape=t...  12.3 us
    convert_element_type x7, other arithmetic, narrow(): return values.astype(jnp.bfloat16)  4.11 us
    pallas_call x1, Pallas kernels, early_terms(): pl.pallas_call(terms_kernel, out_shape=(jax.ShapeDtypeStruct((tok_cols.sh...  2.7 us
    dot_general x2, matrix products, input_part(): return narrow(jnp.dot(back, gate_up.T, preferred_element_type=jnp.float32))  2.6 us
    squeeze x5, local copies, waits for them, and re-layouts, take(): return lax.squeeze(lax.dynamic_slice(values, starts, sizes), (axis,))  2.41 us
  transfers between devices with their start and end apart: 22, of which 11 were waited for; matrix products, arithmetic and copies ran while one was open for 13% of the time, Pallas kernels for 14%

profile of v11, /device:TPU:0, one launch (start us, length us, event | category | flops | bytes accessed | tf_op | source)
XLA Modules:
  0.0 110.1 jit_solution(9267682191125408938)
XLA Ops:
  5.2 3.1 %collective-permute-start.2 = (bf16[128,4224]{1,0:T(8,128)(2,1)}, bf16[128,4224]{1,0:T(8,128)(2,1)S(1)}, u32[]{:S(2)}, u32[]{:S(2)}) collective-permute-start(bf16[128,4224]{1,0:T(8,128)(2,1)} %shard_map.94.refs_0_), channel_id=1, source_target_pairs={{0,8},{4,12},{8,0},{12,4},{16,24},{20,28},{24,16},{28,20},{1,9},{5... | collective-permute-start | bytes 3244040 | tf_op jit(solution)/shard_map/ppermute | solution.py:24
  8.3 1.5 %collective-permute-start.1 = (bf16[128,4224]{1,0:T(8,128)(2,1)}, bf16[128,4224]{1,0:T(8,128)(2,1)}, u32[]{:S(2)}, u32[]{:S(2)}) collective-permute-start(bf16[128,4224]{1,0:T(8,128)(2,1)} %shard_map.94.refs_0_), channel_id=1, source_target_pairs={{0,2},{1,3},{2,0},{3,1},{4,6},{5,7},{6,4},{7,5},{8,10},{9,11},{10,... | collective-permute-start | bytes 3244040 | tf_op jit(solution)/shard_map/ppermute | solution.py:24
  9.8 2.3 %dynamic-slice_bitcast_fusion.1 = (bf16[1,2,64,2048]{3,2,1,0:T(8,128)(2,1)}, bf16[1,2,64,2048]{3,2,1,0:T(8,128)(2,1)}) fusion(bf16[1,2,2,2,64,2048]{5,4,3,2,1,0:T(8,128)(2,1)} %bitcast.77, u32[]{:T(128)S(6)} %optimization_barrier.37, u32[]{:T(128)S(6)} %optimization_barrier.36, u32[]{:T(128)S(6)} %optimization_barrier.34), kind=kLoop, calls=%fused_computation.33 | loop fusion | bytes 2097164 | tf_op jit(solution)/shard_map/squeeze | solution.py:31
  12.1 1.5 %collective-permute-start.3 = (bf16[1,2,64,2048]{3,2,1,0:T(8,128)(2,1)}, bf16[1,2,64,2048]{3,2,1,0:T(8,128)(2,1)}, u32[]{:S(2)}, u32[]{:S(2)}) collective-permute-start(bf16[1,2,64,2048]{3,2,1,0:T(8,128)(2,1)} %get-tuple-element.88), channel_id=1, source_target_pairs={{0,4},{4,0},{8,12},{12,8},{16,20},{20,16},{24,28},{28,24},{1,5},{5... | collective-permute-start | bytes 1572872 | tf_op jit(solution)/shard_map/ppermute | solution.py:24
  13.6 13.1 %collective-permute-done.3 = bf16[1,2,64,2048]{3,2,1,0:T(8,128)(2,1)} collective-permute-done((bf16[1,2,64,2048]{3,2,1,0:T(8,128)(2,1)}, bf16[1,2,64,2048]{3,2,1,0:T(8,128)(2,1)}, u32[]{:S(2)}, u32[]{:S(2)}) %collective-permute-start.3) | collective-permute-done | bytes 524320 | tf_op jit(solution)/shard_map/ppermute | solution.py:24
  26.8 1.3 %fusion.6.refs_2_ = bf16[1,2,64,2048]{3,2,1,0:T(8,128)(2,1)S(1)} fusion(bf16[1,2,64,2048]{3,2,1,0:T(8,128)(2,1)} %collective-permute-done.3, bf16[1,2,2,2,64,2048]{5,4,3,2,1,0:T(8,128)(2,1)} %bitcast.78, u32[]{:T(128)S(6)} %optimization_barrier.34, u32[]{:T(128)S(6)} %optimization_barrier.35), kind=kLoop, calls=%fused_computation.15 | loop fusion | flops 1048576 | bytes 1572872 | tf_op jit(solution)/shard_map/convert_element_type | solution.py:20
  28.1 2.2 %copy-done = bf16[1,2048,1024]{2,1,0:T(8,128)(2,1)S(1)} copy-done((bf16[1,2048,1024]{2,1,0:T(8,128)(2,1)S(1)}, bf16[1,2048,1024]{2,1,0:T(8,128)(2,1)}, u32[]{:S(2)}) %copy-start) | copy-done | bytes 4194328
  30.3 3.5 %shard_map.95 = (bf16[256,1024]{1,0:T(8,128)(2,1)S(1)}, bf16[256,256]{1,0:T(8,128)(2,1)S(1)}, bf16[256,2048]{1,0:T(8,128)(2,1)S(1)}, bf16[128,1024]{1,0:T(8,128)(2,1)S(1)}, bf16[128,1024]{1,0:T(8,128)(2,1)S(1)}) custom-call(s32[2]{0:T(128)S(1)} %pad_add_fusion.place, bf16[128,4224]{1,0:T(8,128)(2,1)} %shard_map.94.refs_0_, ...), custom_call_target="tpu_custom_call" | custom-call | tf_op jit(solution)/shard_map/pallas_call | solution.py:127
  34.5 1.3 %slice.21 = bf16[64,4224]{1,0:T(8,128)(2,1)S(1)} slice(bf16[128,4224]{1,0:T(8,128)(2,1)} %get-tuple-element.53.refs_0_), slice={[0:64], [0:4224]} | slice | bytes 1081344 | tf_op jit(solution)/shard_map/slice | solution.py:225
  35.9 1.6 %collective-permute-start.7 = (bf16[64,4224]{1,0:T(8,128)(2,1)S(1)}, bf16[64,4224]{1,0:T(8,128)(2,1)}, u32[]{:S(2)}, u32[]{:S(2)}) collective-permute-start(bf16[64,4224]{1,0:T(8,128)(2,1)S(1)} %slice.22), channel_id=1, source_target_pairs={{0,2},{1,3},{2,0},{3,1},{4,6},{5,7},{6,4},{7,5},{8,10},{9,11},{10,... | collective-permute-start | bytes 1622024 | tf_op jit(solution)/shard_map/ppermute | solution.py:24
  37.9 1.5 %collective-permute-start.8 = (bf16[1,2,64,2048]{3,2,1,0:T(8,128)(2,1)S(1)}, bf16[1,2,64,2048]{3,2,1,0:T(8,128)(2,1)S(1)}, u32[]{:S(2)}, u32[]{:S(2)}) collective-permute-start(bf16[1,2,64,2048]{3,2,1,0:T(8,128)(2,1)S(1)} %get-tuple-element.71), channel_id=1, source_target_pairs={{0,4},{4,0},{8,12},{12,8},{16,20},{20,16},{24,28},{28,24},{1,5},{5... | collective-permute-start | bytes 1572872 | tf_op jit(solution)/shard_map/ppermute | solution.py:24
  39.4 3.1 %shard_map.97 = (bf16[256,1024]{1,0:T(8,128)(2,1)S(1)}, bf16[256,256]{1,0:T(8,128)(2,1)S(1)}, bf16[256,2048]{1,0:T(8,128)(2,1)S(1)}, bf16[128,1024]{1,0:T(8,128)(2,1)S(1)}, bf16[128,1024]{1,0:T(8,128)(2,1)S(1)}) custom-call(s32[2]{0:T(128)S(1)} %pad_add_fusion.place, bf16[128,4224]{1,0:T(8,128)(2,1)} %get-tuple-element.53.refs_0_, ...), custom_call_target="tpu_custom_call" | custom-call | tf_op jit(solution)/shard_map/pallas_call | solution.py:127
  42.6 2.5 %shard_map.98 = (bf16[256,1024]{1,0:T(8,128)(2,1)S(1)}, bf16[256,256]{1,0:T(8,128)(2,1)S(1)}, bf16[256,2048]{1,0:T(8,128)(2,1)S(1)}, bf16[128,1024]{1,0:T(8,128)(2,1)S(1)}, bf16[128,1024]{1,0:T(8,128)(2,1)S(1)}) custom-call(s32[2]{0:T(128)S(1)} %pad_add_fusion.place, bf16[128,4224]{1,0:T(8,128)(2,1)S(1)} %get-tuple-element.62.refs_0_, ...), custom_call_target="tpu_custom_call" | custom-call | tf_op jit(solution)/shard_map/pallas_call | solution.py:127
  45.1 2.7 %shard_map.99 = (f32[1024,1024]{1,0:T(8,128)S(1)}, f32[256,2048]{1,0:T(8,128)S(1)}, bf16[256,1024]{1,0:T(8,128)(2,1)S(1)}, f32[8,128]{1,0:T(8,128)S(1)}) custom-call(bf16[256,1024]{1,0:T(8,128)(2,1)S(1)} %get-tuple-element.55.refs_0_, bf16[256,256]{1,0:T(8,128)(2,1)S(1)} %get-tuple-element.52.refs_4_.refs_1_, ...), custom_call_target="tpu_custom_call" | custom-call | tf_op jit(solution)/shard_map/pallas_call | solution.py:171
  47.8 2.0 %copy-done.6 = f32[1024,1024]{1,0:T(8,128)} copy-done((f32[1024,1024]{1,0:T(8,128)}, f32[1024,1024]{1,0:T(8,128)S(1)}, u32[]{:S(2)}) %copy-start.6) | copy-done | bytes 4194328
  54.0 1.6 %collective-permute-start.19 = (bf16[1,2,64,2048]{3,2,1,0:T(8,128)(2,1)}, bf16[1,2,64,2048]{3,2,1,0:T(8,128)(2,1)S(1)}, u32[]{:S(2)}, u32[]{:S(2)}) collective-permute-start(bf16[1,2,64,2048]{3,2,1,0:T(8,128)(2,1)} %copy-done.5), channel_id=1, source_target_pairs={{0,8},{4,12},{8,0},{12,4},{16,24},{20,28},{24,16},{28,20},{1,9},{5... | collective-permute-start | bytes 1572872 | tf_op jit(solution)/shard_map/ppermute | solution.py:24
  56.4 2.2 %copy-done.2 = bf16[1,2048,1024]{2,1,0:T(8,128)(2,1)S(1)} copy-done((bf16[1,2048,1024]{2,1,0:T(8,128)(2,1)S(1)}, bf16[1,2048,1024]{2,1,0:T(8,128)(2,1)}, u32[]{:S(2)}) %copy-start.2) | copy-done | bytes 4194328
  58.6 3.1 %shard_map.101 = (bf16[256,1024]{1,0:T(8,128)(2,1)S(1)}, bf16[256,256]{1,0:T(8,128)(2,1)S(1)}, bf16[256,2048]{1,0:T(8,128)(2,1)S(1)}, bf16[128,1024]{1,0:T(8,128)(2,1)S(1)}, bf16[128,1024]{1,0:T(8,128)(2,1)S(1)}) custom-call(s32[2]{0:T(128)S(1)} %pad_add_fusion.place, bf16[64,4224]{1,0:T(8,128)(2,1)} %get-tuple-element.73.refs_0_, ...), custom_call_target="tpu_custom_call" | custom-call | tf_op jit(solution)/shard_map/pallas_call | solution.py:127
  62.5 1.4 %copy-done.7 = f32[1024,1024]{1,0:T(8,128)S(1)} copy-done((f32[1024,1024]{1,0:T(8,128)S(1)}, f32[1024,1024]{1,0:T(8,128)}, u32[]{:S(2)}) %copy-start.7) | copy-done | bytes 4194328
  63.9 1.3 %add_convert_fusion = bf16[1024,1024]{1,0:T(8,128)(2,1)S(1)} fusion(f32[1024,1024]{1,0:T(8,128)S(1)} %copy-done.7, f32[1024,1024]{1,0:T(8,128)S(1)} %fusion.11), kind=kLoop, calls=%fused_computation | loop fusion | flops 2097152 | bytes 10485760 | tf_op jit(solution)/shard_map/convert_element_type | solution.py:20
  67.6 1.3 %convolution_convert_fusion = bf16[256,2048]{1,0:T(8,128)(2,1)S(1)} fusion(bf16[256,1024]{1,0:T(8,128)(2,1)S(1)} %shard_map.102, bf16[1,2048,1024]{2,1,0:T(8,128)(2,1)S(1)} %copy-done.3), kind=kOutput, calls=%fused_computation.1 | convolution fusion | flops 1074266112 | bytes 5767168 | tf_op jit(solution)/shard_map/dot_general | solution.py:268
  71.0 1.8 %collective-permute-done.15.refs_2_ = bf16[1,96,1024]{2,1,0:T(8,128)(2,1)S(1)} collective-permute-done((bf16[1,96,1024]{2,1,0:T(8,128)(2,1)S(1)}, bf16[1,96,1024]{2,1,0:T(8,128)(2,1)S(1)}, u32[]{:S(2)}, u32[]{:S(2)}) %collective-permute-start.15) | collective-permute-done | bytes 196640 | tf_op jit(solution)/shard_map/ppermute | solution.py:24
  72.9 2.7 %collective-permute-start.16 = (bf16[1,96,1024]{2,1,0:T(8,128)(2,1)S(1)}, bf16[1,96,1024]{2,1,0:T(8,128)(2,1)S(1)}, u32[]{:S(2)}, u32[]{:S(2)}) collective-permute-start(bf16[1,96,1024]{2,1,0:T(8,128)(2,1)S(1)} %fusion.20), channel_id=1, source_target_pairs={{0,16},{4,20},{8,24},{12,28},{16,0},{20,4},{24,8},{28,12},{1,17},{... | collective-permute-start | bytes 589832 | tf_op jit(solution)/shard_map/ppermute | solution.py:24
  76.4 1.2 %fusion.3 = f32[1,2,64,2048]{3,2,1,0:T(8,128)S(1)} fusion(bf16[1,2,64,2048]{3,2,1,0:T(8,128)(2,1)S(1)} %get-tuple-element.85, bf16[1,2,64,2048]{3,2,1,0:T(8,128)(2,1)S(1)} %copy-done.11, bf16[1,2,2,2,64,2048]{5,4,3,2,1,0:T(8,128)(2,1)} %bitcast.79, u32[]{:T(128)S(6)} %optimization_barrier.37, u32[]{:T(128)S(6)} %optimization_barrier.35), kind=kLoop, calls=%fused_computation.10 | loop fusion | flops 1310720 | bytes 2621448 | tf_op jit(solution)/shard_map/add | solution.py:263
  77.7 1.3 %fusion.1 = f32[256,2048]{1,0:T(8,128)S(1)} fusion(bf16[256,2048]{1,0:T(8,128)(2,1)S(1)} %collective-permute-done.11, bf16[128,1024]{1,0:T(8,128)(2,1)S(1)} %copy-done.18, bf16[128,1024]{1,0:T(8,128)(2,1)S(1)} %get-tuple-element.47.refs_3_, bf16[1,2048,1024]{2,1,0:T(8,128)(2,1)S(1)} %copy-done.3), kind=kOutput, calls=%fused_computation.4 | convolution fusion | flops 1076887552 | bytes 7864320 | tf_op jit(solution)/shard_map/dot_general | solution.py:268
  80.0 2.5 %collective-permute-start.17 = (bf16[1,160,1024]{2,1,0:T(8,128)(2,1)S(1)}, bf16[1,160,1024]{2,1,0:T(8,128)(2,1)S(1)}, u32[]{:S(2)}, u32[]{:S(2)}) collective-permute-start(bf16[1,160,1024]{2,1,0:T(8,128)(2,1)S(1)} %fusion.7), channel_id=1, source_target_pairs={{0,16},{4,20},{8,24},{12,28},{16,0},{20,4},{24,8},{28,12},{1,17},{... | collective-permute-start | bytes 983048 | tf_op jit(solution)/shard_map/ppermute | solution.py:24
  83.4 2.0 %collective-permute-done.20 = bf16[1,64,2048]{2,1,0:T(8,128)(2,1)S(1)} collective-permute-done((bf16[1,64,2048]{2,1,0:T(8,128)(2,1)S(1)}, bf16[1,64,2048]{2,1,0:T(8,128)(2,1)S(1)}, u32[]{:S(2)}, u32[]{:S(2)}) %collective-permute-start.20) | collective-permute-done | bytes 262176 | tf_op jit(solution)/shard_map/ppermute | solution.py:24
  85.5 2.7 %collective-permute-start.21 = (bf16[1,64,2048]{2,1,0:T(8,128)(2,1)S(1)}, bf16[1,64,2048]{2,1,0:T(8,128)(2,1)S(1)}, u32[]{:S(2)}, u32[]{:S(2)}) collective-permute-start(bf16[1,64,2048]{2,1,0:T(8,128)(2,1)S(1)} %fusion.16), channel_id=1, source_target_pairs={{0,16},{4,20},{8,24},{12,28},{16,0},{20,4},{24,8},{28,12},{1,17},{... | collective-permute-start | bytes 786440 | tf_op jit(solution)/shard_map/ppermute | solution.py:24
  88.2 3.2 %collective-permute-done.12.refs_1_ = bf16[128,2048]{1,0:T(8,128)(2,1)S(1)} collective-permute-done((bf16[128,2048]{1,0:T(8,128)(2,1)S(1)}, bf16[128,2048]{1,0:T(8,128)(2,1)S(1)}, u32[]{:S(2)}, u32[]{:S(2)}) %collective-permute-start.12) | collective-permute-done | bytes 524320 | tf_op jit(solution)/shard_map/ppermute | solution.py:24
  93.5 10.8 %collective-permute-done.17.refs_0_ = bf16[1,160,1024]{2,1,0:T(8,128)(2,1)S(1)} collective-permute-done((bf16[1,160,1024]{2,1,0:T(8,128)(2,1)S(1)}, bf16[1,160,1024]{2,1,0:T(8,128)(2,1)S(1)}, u32[]{:S(2)}, u32[]{:S(2)}) %collective-permute-start.17) | collective-permute-done | bytes 327712 | tf_op jit(solution)/shard_map/ppermute | solution.py:24
  104.3 1.2 %fusion.5 = f32[1,256,1024]{2,1,0:T(8,128)} fusion(bf16[1,256,1024]{2,1,0:T(8,128)(2,1)S(1)} %collective-permute-done.14, bf16[1,160,1024]{2,1,0:T(8,128)(2,1)S(1)} %shard_map.105, bf16[1,96,1024]{2,1,0:T(8,128)(2,1)S(1)} %collective-permute-done.16, bf16[1,2,2,256,1024]{4,3,2,1,0:T(8,128)(2,1)S(1)} %bitcast.73, u32[]{:T(128)S(6)} %optimization_barrier.39, ...), kind=kLoop, calls=%fused_computation.13 | loop fusion | flops 2359296 | bytes 2621448 | tf_op jit(solution)/shard_map/mul | solution.py:292
  105.5 3.6 %collective-permute-done.21 = bf16[1,64,2048]{2,1,0:T(8,128)(2,1)S(1)} collective-permute-done((bf16[1,64,2048]{2,1,0:T(8,128)(2,1)S(1)}, bf16[1,64,2048]{2,1,0:T(8,128)(2,1)S(1)}, u32[]{:S(2)}, u32[]{:S(2)}) %collective-permute-start.21) | collective-permute-done | bytes 262176 | tf_op jit(solution)/shard_map/ppermute | solution.py:24
  (92 shorter events, 21.9 us)
Async XLA Ops:
  5.2 22.9 %copy-start.4 = (bf16[1,512,2048]{2,1,0:T(8,128)(2,1)S(1)}, bf16[1,512,2048]{2,1,0:T(8,128)(2,1)}, u32[]{:S(2)}) copy-start(bf16[1,512,2048]{2,1,0:T(8,128)(2,1)} %param.12) | copy-start | bytes 6291460
  5.2 28.6 %collective-permute-start.2 = (bf16[128,4224]{1,0:T(8,128)(2,1)}, bf16[128,4224]{1,0:T(8,128)(2,1)S(1)}, u32[]{:S(2)}, u32[]{:S(2)}) collective-permute-start(bf16[128,4224]{1,0:T(8,128)(2,1)} %shard_map.94.refs_0_), channel_id=1, source_target_pairs={{0,8},{4,12},{8,0},{12,4},{16,24},{20,28},{24,16},{28,20},{1,9},{5... | collective-permute-start | bytes 3244040 | tf_op jit(solution)/shard_map/ppermute | solution.py:24
  8.3 25.6 %collective-permute-start.1 = (bf16[128,4224]{1,0:T(8,128)(2,1)}, bf16[128,4224]{1,0:T(8,128)(2,1)}, u32[]{:S(2)}, u32[]{:S(2)}) collective-permute-start(bf16[128,4224]{1,0:T(8,128)(2,1)} %shard_map.94.refs_0_), channel_id=1, source_target_pairs={{0,2},{1,3},{2,0},{3,1},{4,6},{5,7},{6,4},{7,5},{8,10},{9,11},{10,... | collective-permute-start | bytes 3244040 | tf_op jit(solution)/shard_map/ppermute | solution.py:24
  9.8 18.3 %collective-permute-start = (bf16[128,4224]{1,0:T(8,128)(2,1)}, bf16[128,4224]{1,0:T(8,128)(2,1)}, u32[]{:S(2)}, u32[]{:S(2)}) collective-permute-start(bf16[128,4224]{1,0:T(8,128)(2,1)} %shard_map.94.refs_0_), channel_id=1, source_target_pairs={{0,1},{1,0},{2,3},{3,2},{4,5},{5,4},{6,7},{7,6},{8,9},{9,8},{10,11... | collective-permute-start | bytes 3244040 | tf_op jit(solution)/shard_map/ppermute | solution.py:24
  12.1 14.7 %collective-permute-start.3 = (bf16[1,2,64,2048]{3,2,1,0:T(8,128)(2,1)}, bf16[1,2,64,2048]{3,2,1,0:T(8,128)(2,1)}, u32[]{:S(2)}, u32[]{:S(2)}) collective-permute-start(bf16[1,2,64,2048]{3,2,1,0:T(8,128)(2,1)} %get-tuple-element.88), channel_id=1, source_target_pairs={{0,4},{4,0},{8,12},{12,8},{16,20},{20,16},{24,28},{28,24},{1,5},{5... | collective-permute-start | bytes 1572872 | tf_op jit(solution)/shard_map/ppermute | solution.py:24
  28.1 2.2 %copy-start = (bf16[1,2048,1024]{2,1,0:T(8,128)(2,1)S(1)}, bf16[1,2048,1024]{2,1,0:T(8,128)(2,1)}, u32[]{:S(2)}) copy-start(bf16[1,2048,1024]{2,1,0:T(8,128)(2,1)} %param.11) | copy-start | bytes 12582916
  30.3 3.7 %copy-start.12 = (bf16[1,2,64,2048]{3,2,1,0:T(8,128)(2,1)S(1)}, bf16[1,2,64,2048]{3,2,1,0:T(8,128)(2,1)}, u32[]{:S(2)}) copy-start(bf16[1,2,64,2048]{3,2,1,0:T(8,128)(2,1)} %get-tuple-element.87.refs_3_) | copy-start | bytes 1572868
  34.0 5.4 %copy-start.1 = (bf16[1,2048,1024]{2,1,0:T(8,128)(2,1)S(1)}, bf16[1,2048,1024]{2,1,0:T(8,128)(2,1)}, u32[]{:S(2)}) copy-start(bf16[1,2048,1024]{2,1,0:T(8,128)(2,1)} %param.11) | copy-start | bytes 12582916
  34.0 5.4 %collective-permute-start.4 = (bf16[128,4224]{1,0:T(8,128)(2,1)}, bf16[128,4224]{1,0:T(8,128)(2,1)S(1)}, u32[]{:S(2)}, u32[]{:S(2)}) collective-permute-start(bf16[128,4224]{1,0:T(8,128)(2,1)} %get-tuple-element.53.refs_0_), channel_id=1, source_target_pairs={{0,1},{1,0},{2,3},{3,2},{4,5},{5,4},{6,7},{7,6},{8,9},{9,8},{10,11... | collective-permute-start | bytes 3244040 | tf_op jit(solution)/shard_map/ppermute | solution.py:24
  34.0 8.6 %collective-permute-start.5 = (bf16[128,4224]{1,0:T(8,128)(2,1)S(1)}, bf16[128,4224]{1,0:T(8,128)(2,1)S(1)}, u32[]{:S(2)}, u32[]{:S(2)}) collective-permute-start(bf16[128,4224]{1,0:T(8,128)(2,1)S(1)} %get-tuple-element.62.refs_0_), channel_id=1, source_target_pairs={{0,1},{1,0},{2,3},{3,2},{4,5},{5,4},{6,7},{7,6},{8,9},{9,8},{10,11... | collective-permute-start | bytes 3244040 | tf_op jit(solution)/shard_map/ppermute | solution.py:24
  35.9 15.1 %collective-permute-start.7 = (bf16[64,4224]{1,0:T(8,128)(2,1)S(1)}, bf16[64,4224]{1,0:T(8,128)(2,1)}, u32[]{:S(2)}, u32[]{:S(2)}) collective-permute-start(bf16[64,4224]{1,0:T(8,128)(2,1)S(1)} %slice.22), channel_id=1, source_target_pairs={{0,2},{1,3},{2,0},{3,1},{4,6},{5,7},{6,4},{7,5},{8,10},{9,11},{10,... | collective-permute-start | bytes 1622024 | tf_op jit(solution)/shard_map/ppermute | solution.py:24
  37.4 13.8 %collective-permute-start.6 = (bf16[64,4224]{1,0:T(8,128)(2,1)S(1)}, bf16[64,4224]{1,0:T(8,128)(2,1)}, u32[]{:S(2)}, u32[]{:S(2)}) collective-permute-start(bf16[64,4224]{1,0:T(8,128)(2,1)S(1)} %slice.21), channel_id=1, source_target_pairs={{0,8},{4,12},{8,0},{12,4},{16,24},{20,28},{24,16},{28,20},{1,9},{5... | collective-permute-start | bytes 1622024 | tf_op jit(solution)/shard_map/ppermute | solution.py:24
  37.9 13.1 %collective-permute-start.8 = (bf16[1,2,64,2048]{3,2,1,0:T(8,128)(2,1)S(1)}, bf16[1,2,64,2048]{3,2,1,0:T(8,128)(2,1)S(1)}, u32[]{:S(2)}, u32[]{:S(2)}) collective-permute-start(bf16[1,2,64,2048]{3,2,1,0:T(8,128)(2,1)S(1)} %get-tuple-element.71), channel_id=1, source_target_pairs={{0,4},{4,0},{8,12},{12,8},{16,20},{20,16},{24,28},{28,24},{1,5},{5... | collective-permute-start | bytes 1572872 | tf_op jit(solution)/shard_map/ppermute | solution.py:24
  42.6 2.5 %copy-start.17 = (bf16[128,1024]{1,0:T(8,128)(2,1)}, bf16[128,1024]{1,0:T(8,128)(2,1)S(1)}, u32[]{:S(2)}) copy-start(bf16[128,1024]{1,0:T(8,128)(2,1)S(1)} %get-tuple-element.54.refs_8_) | copy-start | bytes 786436
  53.5 2.1 %collective-permute-start.9 = (bf16[64,4224]{1,0:T(8,128)(2,1)}, bf16[64,4224]{1,0:T(8,128)(2,1)S(1)}, u32[]{:S(2)}, u32[]{:S(2)}) collective-permute-start(bf16[64,4224]{1,0:T(8,128)(2,1)} %get-tuple-element.73.refs_0_), channel_id=1, source_target_pairs={{0,1},{1,0},{2,3},{3,2},{4,5},{5,4},{6,7},{7,6},{8,9},{9,8},{10,11... | collective-permute-start | bytes 1622024 | tf_op jit(solution)/shard_map/ppermute | solution.py:24
  53.5 2.9 %collective-permute-start.10 = (bf16[64,4224]{1,0:T(8,128)(2,1)}, bf16[64,4224]{1,0:T(8,128)(2,1)S(1)}, u32[]{:S(2)}, u32[]{:S(2)}) collective-permute-start(bf16[64,4224]{1,0:T(8,128)(2,1)} %get-tuple-element.74.refs_1_), channel_id=1, source_target_pairs={{0,1},{1,0},{2,3},{3,2},{4,5},{5,4},{6,7},{7,6},{8,9},{9,8},{10,11... | collective-permute-start | bytes 1622024 | tf_op jit(solution)/shard_map/ppermute | solution.py:24
  54.0 21.5 %collective-permute-start.19 = (bf16[1,2,64,2048]{3,2,1,0:T(8,128)(2,1)}, bf16[1,2,64,2048]{3,2,1,0:T(8,128)(2,1)S(1)}, u32[]{:S(2)}, u32[]{:S(2)}) collective-permute-start(bf16[1,2,64,2048]{3,2,1,0:T(8,128)(2,1)} %copy-done.5), channel_id=1, source_target_pairs={{0,8},{4,12},{8,0},{12,4},{16,24},{20,28},{24,16},{28,20},{1,9},{5... | collective-permute-start | bytes 1572872 | tf_op jit(solution)/shard_map/ppermute | solution.py:24
  56.4 2.2 %copy-start.2 = (bf16[1,2048,1024]{2,1,0:T(8,128)(2,1)S(1)}, bf16[1,2048,1024]{2,1,0:T(8,128)(2,1)}, u32[]{:S(2)}) copy-start(bf16[1,2048,1024]{2,1,0:T(8,128)(2,1)} %param.11) | copy-start | bytes 12582916
  61.8 2.2 %copy-start.7 = (f32[1024,1024]{1,0:T(8,128)S(1)}, f32[1024,1024]{1,0:T(8,128)}, u32[]{:S(2)}) copy-start(f32[1024,1024]{1,0:T(8,128)} %copy-done.6) | copy-start | bytes 12582916
  65.3 2.3 %copy-start.3 = (bf16[1,2048,1024]{2,1,0:T(8,128)(2,1)S(1)}, bf16[1,2048,1024]{2,1,0:T(8,128)(2,1)}, u32[]{:S(2)}) copy-start(bf16[1,2048,1024]{2,1,0:T(8,128)(2,1)} %param.11) | copy-start | bytes 12582916
  65.5 7.3 %collective-permute-start.15 = (bf16[1,96,1024]{2,1,0:T(8,128)(2,1)S(1)}, bf16[1,96,1024]{2,1,0:T(8,128)(2,1)S(1)}, u32[]{:S(2)}, u32[]{:S(2)}) collective-permute-start(bf16[1,96,1024]{2,1,0:T(8,128)(2,1)S(1)} %dynamic-slice_bitcast_fusion.6.refs_1_), channel_id=1, source_target_pairs={{0,4},{4,0},{8,12},{12,8},{16,20},{20,16},{24,28},{28,24},{1,5},{5... | collective-permute-start | bytes 589832 | tf_op jit(solution)/shard_map/ppermute | solution.py:24
  68.9 8.7 %collective-permute-start.11 = (bf16[256,2048]{1,0:T(8,128)(2,1)S(1)}, bf16[256,2048]{1,0:T(8,128)(2,1)S(1)}, u32[]{:S(2)}, u32[]{:S(2)}) collective-permute-start(bf16[256,2048]{1,0:T(8,128)(2,1)S(1)} %convolution_convert_fusion), channel_id=1, source_target_pairs={{0,1},{1,0},{2,3},{3,2},{4,5},{5,4},{6,7},{7,6},{8,9},{9,8},{10,11... | collective-permute-start | bytes 3145736 | tf_op jit(solution)/shard_map/ppermute | solution.py:24
  69.2 10.8 %collective-permute-start.13 = (bf16[1,160,1024]{2,1,0:T(8,128)(2,1)S(1)}, bf16[1,160,1024]{2,1,0:T(8,128)(2,1)S(1)}, u32[]{:S(2)}, u32[]{:S(2)}) collective-permute-start(bf16[1,160,1024]{2,1,0:T(8,128)(2,1)S(1)} %dynamic-slice_bitcast_fusion.3), channel_id=1, source_target_pairs={{0,4},{4,0},{8,12},{12,8},{16,20},{20,16},{24,28},{28,24},{1,5},{5... | collective-permute-start | bytes 983048 | tf_op jit(solution)/shard_map/ppermute | solution.py:24
  70.9 5.5 %copy-start.11 = (bf16[1,2,64,2048]{3,2,1,0:T(8,128)(2,1)S(1)}, bf16[1,2,64,2048]{3,2,1,0:T(8,128)(2,1)}, u32[]{:S(2)}) copy-start(bf16[1,2,64,2048]{3,2,1,0:T(8,128)(2,1)} %copy-done.10) | copy-start | bytes 1572868
  71.0 6.7 %copy-start.18 = (bf16[128,1024]{1,0:T(8,128)(2,1)S(1)}, bf16[128,1024]{1,0:T(8,128)(2,1)}, u32[]{:S(2)}) copy-start(bf16[128,1024]{1,0:T(8,128)(2,1)} %copy-done.17) | copy-start | bytes 786436
  72.9 31.5 %collective-permute-start.16 = (bf16[1,96,1024]{2,1,0:T(8,128)(2,1)S(1)}, bf16[1,96,1024]{2,1,0:T(8,128)(2,1)S(1)}, u32[]{:S(2)}, u32[]{:S(2)}) collective-permute-start(bf16[1,96,1024]{2,1,0:T(8,128)(2,1)S(1)} %fusion.20), channel_id=1, source_target_pairs={{0,16},{4,20},{8,24},{12,28},{16,0},{20,4},{24,8},{28,12},{1,17},{... | collective-permute-start | bytes 589832 | tf_op jit(solution)/shard_map/ppermute | solution.py:24
  75.5 9.9 %collective-permute-start.20 = (bf16[1,64,2048]{2,1,0:T(8,128)(2,1)S(1)}, bf16[1,64,2048]{2,1,0:T(8,128)(2,1)S(1)}, u32[]{:S(2)}, u32[]{:S(2)}) collective-permute-start(bf16[1,64,2048]{2,1,0:T(8,128)(2,1)S(1)} %get-tuple-element.86), channel_id=1, source_target_pairs={{0,4},{4,0},{8,12},{12,8},{16,20},{20,16},{24,28},{28,24},{1,5},{5... | collective-permute-start | bytes 786440 | tf_op jit(solution)/shard_map/ppermute | solution.py:24
  79.1 12.4 %collective-permute-start.12 = (bf16[128,2048]{1,0:T(8,128)(2,1)S(1)}, bf16[128,2048]{1,0:T(8,128)(2,1)S(1)}, u32[]{:S(2)}, u32[]{:S(2)}) collective-permute-start(bf16[128,2048]{1,0:T(8,128)(2,1)S(1)} %slice.35), channel_id=1, source_target_pairs={{0,2},{1,3},{2,0},{3,1},{4,6},{5,7},{6,4},{7,5},{8,10},{9,11},{10,... | collective-permute-start | bytes 1572872 | tf_op jit(solution)/shard_map/ppermute | solution.py:24
  80.0 24.3 %collective-permute-start.17 = (bf16[1,160,1024]{2,1,0:T(8,128)(2,1)S(1)}, bf16[1,160,1024]{2,1,0:T(8,128)(2,1)S(1)}, u32[]{:S(2)}, u32[]{:S(2)}) collective-permute-start(bf16[1,160,1024]{2,1,0:T(8,128)(2,1)S(1)} %fusion.7), channel_id=1, source_target_pairs={{0,16},{4,20},{8,24},{12,28},{16,0},{20,4},{24,8},{28,12},{1,17},{... | collective-permute-start | bytes 983048 | tf_op jit(solution)/shard_map/ppermute | solution.py:24
  82.6 21.7 %collective-permute-start.14 = (bf16[1,256,1024]{2,1,0:T(8,128)(2,1)S(1)}, bf16[1,256,1024]{2,1,0:T(8,128)(2,1)S(1)}, u32[]{:S(2)}, u32[]{:S(2)}) collective-permute-start(bf16[1,256,1024]{2,1,0:T(8,128)(2,1)S(1)} %shard_map.103), channel_id=1, source_target_pairs={{0,4},{4,0},{8,12},{12,8},{16,20},{20,16},{24,28},{28,24},{1,5},{5... | collective-permute-start | bytes 1572872 | tf_op jit(solution)/shard_map/ppermute | solution.py:24
  85.5 23.6 %collective-permute-start.21 = (bf16[1,64,2048]{2,1,0:T(8,128)(2,1)S(1)}, bf16[1,64,2048]{2,1,0:T(8,128)(2,1)S(1)}, u32[]{:S(2)}, u32[]{:S(2)}) collective-permute-start(bf16[1,64,2048]{2,1,0:T(8,128)(2,1)S(1)} %fusion.16), channel_id=1, source_target_pairs={{0,16},{4,20},{8,24},{12,28},{16,0},{20,4},{24,8},{28,12},{1,17},{... | collective-permute-start | bytes 786440 | tf_op jit(solution)/shard_map/ppermute | solution.py:24
  91.4 17.7 %collective-permute-start.18 = (bf16[1,64,2048]{2,1,0:T(8,128)(2,1)S(1)}, bf16[1,64,2048]{2,1,0:T(8,128)(2,1)S(1)}, u32[]{:S(2)}, u32[]{:S(2)}) collective-permute-start(bf16[1,64,2048]{2,1,0:T(8,128)(2,1)S(1)} %shard_map.104.refs_1_), channel_id=1, source_target_pairs={{0,4},{4,0},{8,12},{12,8},{16,20},{20,16},{24,28},{28,24},{1,5},{5... | collective-permute-start | bytes 786440 | tf_op jit(solution)/shard_map/ppermute | solution.py:24
  (11 other events, 12.0 us)

commit v12 on v11

--- a/solution.py
+++ b/solution.py
@@ -209,7 +209,8 @@
         return wide(kept) + wide(got)
 
     def residual_side(parity, first):
-        return take(take(residual, 2, parity), 2, first)
+        part = take(take(residual, 3, first), 2, parity)
+        return jnp.stack([take(part, 1, third) for third in (not2, bit2)], axis=1)
 
     res_other = flip(residual_side(not1, not0), "dp", 1)
     res_mine = residual_side(bit1, not0)
@@ -262,7 +263,7 @@
     (near_sent,) = hold((side(gate_term, bit2, not0),), (far_got[1],))
     res_sum = pair_sum(residual_side(bit1, bit0), res_mine) + wide(res_near)
     far_down = pair_sum(side(down_term, not2, bit0), flip(down_sent, "dp", 1))
-    crossed_down = flip(narrow(far_down + take(res_sum, 1, not2)), "dp", 4)
+    crossed_down = flip(narrow(far_down + res_sum[:, 0]), "dp", 4)
 
     def input_part(back):
         return narrow(jnp.dot(back, gate_up.T, preferred_element_type=jnp.float32))
@@ -279,7 +280,7 @@
     near_down = pair_sum(side(down_term, bit2, bit0), flip(near_sent, "dp", 1))
     crossed[-1] = hold((crossed[-1],), (near_sent,))[0]
     gate_sum = near_gate + wide(jnp.concatenate(crossed, axis=1))
-    down_sum = near_down + take(res_sum, 1, bit2) + wide(crossed_down)
+    down_sum = near_down + res_sum[:, 1] + wide(crossed_down)
     bit = 8
     while bit < group_count:
         mine = lax.convert_element_type((group // bit) & 1, jnp.uint32)

time: 111 us -> 101 us (0.910)
  local copies, waits for them, and re-layouts: 19.4 us -> 5.68 us
  waiting for transfers between devices: 36.3 us -> 45 us
  Pallas kernels: 16.1 us -> 13.7 us
  other arithmetic: 7.61 us -> 5.42 us
    unnamed x42 -> x12, local copies, waits for them, and re-layouts: 15.4 us -> 3.45 us
    ppermute x22, waiting for transfers between devices: 36.3 us -> 45 us  [flip(): lax.ppermute(values, axis, [(i, i ^ bit) for i in range(lax.axis_size(axi...]
    squeeze x5 -> x4, local copies, waits for them, and re-layouts: 2.41 us -> 0.15 us  [take(): return lax.squeeze(lax.dynamic_slice(values, starts, sizes), (axis,))]
    another operation x0 -> x1, local copies, waits for them, and re-layouts: none -> 1.8 us  [residual_side(): return jnp.stack([take(part, 1, third) for third in (not2, bit2)], axis=1)]
    pallas_call x4, Pallas kernels: 12.3 us -> 10.7 us  [expert_rows(): pl.pallas_call(functools.partial(expert_kernel, group_count), out_shape=t...]
    slice x2, local copies, waits for them, and re-layouts: 1.38 us -> 0.08 us  [on_device(): diagonal = [flip(rows_x[:half], 'dp', 2), flip(rows_n[half:], 'expert', 2)]]
    convert_element_type x7, other arithmetic: 4.11 us -> 2.89 us  [narrow(): return values.astype(jnp.bfloat16)]
  transfers between devices with their start and end apart: 22 -> 22, of which waited for: 11 -> 12; matrix products, arithmetic and copies ran while one was open for 13% -> 10% of each run, Pallas kernels for 14% -> 13%
where the time goes in v12:
time: 101 us
  waiting for transfers between devices  45 us (45%)
  starting transfers between devices  26.5 us (26%)
  Pallas kernels  13.7 us (14%)
  local copies, waits for them, and re-layouts  5.68 us (6%)
  other arithmetic  5.42 us (5%)
  matrix products  3.78 us (4%)
    ppermute x22, waiting for transfers between devices, flip(): lax.ppermute(values, axis, [(i, i ^ bit) for i in range(lax.axis_size(axi...  45 us
    ppermute x22, starting transfers between devices, flip(): lax.ppermute(values, axis, [(i, i ^ bit) for i in range(lax.axis_size(axi...  26.5 us
    pallas_call x4, Pallas kernels, expert_rows(): pl.pallas_call(functools.partial(expert_kernel, group_count), out_shape=t...  10.7 us
    unnamed x12, local copies, waits for them, and re-layouts  3.45 us
    convert_element_type x7, other arithmetic, narrow(): return values.astype(jnp.bfloat16)  2.89 us
    pallas_call x1, Pallas kernels, early_terms(): pl.pallas_call(terms_kernel, out_shape=(jax.ShapeDtypeStruct((tok_cols.sh...  2.71 us
    dot_general x2, matrix products, input_part(): return narrow(jnp.dot(back, gate_up.T, preferred_element_type=jnp.float32))  2.58 us
    mul x2, other arithmetic, on_device(): grad_gate_up, grad_down = (gate_sum * factor, down_sum * factor)  2.15 us
  transfers between devices with their start and end apart: 22, of which 12 were waited for; matrix products, arithmetic and copies ran while one was open for 10% of the time, Pallas kernels for 13%

profile of v12, /device:TPU:0, one launch (start us, length us, event | category | flops | bytes accessed | tf_op | source)
XLA Modules:
  0.0 101.0 jit_solution(3094377984168190490)
XLA Ops:
  0.7 1.0 %copy-done.2 = bf16[128,2048]{1,0:T(8,128)(2,1)S(1)} copy-done((bf16[128,2048]{1,0:T(8,128)(2,1)S(1)}, bf16[128,2048]{1,0:T(8,128)(2,1)}, u32[]{:S(2)}) %copy-start.2) | copy-done | bytes 524312
  4.4 3.1 %collective-permute-start.2 = (bf16[128,4224]{1,0:T(8,128)(2,1)S(1)}, bf16[128,4224]{1,0:T(8,128)(2,1)S(1)}, u32[]{:S(2)}, u32[]{:S(2)}) collective-permute-start(bf16[128,4224]{1,0:T(8,128)(2,1)S(1)} %shard_map.94.refs_0_), channel_id=1, source_target_pairs={{0,8},{4,12},{8,0},{12,4},{16,24},{20,28},{24,16},{28,20},{1,9},{5... | collective-permute-start | bytes 3244040 | tf_op jit(solution)/shard_map/ppermute | solution.py:24
  7.5 1.5 %collective-permute-start.1 = (bf16[128,4224]{1,0:T(8,128)(2,1)S(1)}, bf16[128,4224]{1,0:T(8,128)(2,1)S(1)}, u32[]{:S(2)}, u32[]{:S(2)}) collective-permute-start(bf16[128,4224]{1,0:T(8,128)(2,1)S(1)} %shard_map.94.refs_0_), channel_id=1, source_target_pairs={{0,2},{1,3},{2,0},{3,1},{4,6},{5,7},{6,4},{7,5},{8,10},{9,11},{10,... | collective-permute-start | bytes 3244040 | tf_op jit(solution)/shard_map/ppermute | solution.py:24
  9.0 1.8 %dynamic-slice_bitcast_fusion.4 = (bf16[1,1,64,2048]{3,2,1,0:T(8,128)(2,1)S(1)}, bf16[1,1,64,2048]{3,2,1,0:T(8,128)(2,1)S(1)}, bf16[1,1,64,2048]{3,2,1,0:T(8,128...) fusion(bf16[1,2,2,2,64,2048]{5,4,3,2,1,0:T(8,128)(2,1)} %bitcas, ...), kind=kLoop, calls=%fused_computation.40 | loop fusion | bytes 4194328 | tf_op jit(solution)/shard_map/stack | solution.py:213
  10.9 1.6 %collective-permute-start.3 = (bf16[1,2,64,2048]{3,2,1,0:T(8,128)(2,1)S(1)}, bf16[1,2,64,2048]{3,2,1,0:T(8,128)(2,1)S(1)}, u32[]{:S(2)}, u32[]{:S(2)}) collective-permute-start(bf16[1,2,64,2048]{3,2,1,0:T(8,128)(2,1)S(1)} %pad_maximum_fusion), channel_id=1, source_target_pairs={{0,4},{4,0},{8,12},{12,8},{16,20},{20,16},{24,28},{28,24},{1,5},{5... | collective-permute-start | bytes 1572872 | tf_op jit(solution)/shard_map/ppermute | solution.py:24
  12.5 12.8 %collective-permute-done.3 = bf16[1,2,64,2048]{3,2,1,0:T(8,128)(2,1)S(1)} collective-permute-done((bf16[1,2,64,2048]{3,2,1,0:T(8,128)(2,1)S(1)}, bf16[1,2,64,2048]{3,2,1,0:T(8,128)(2,1)S(1)}, u32[]{:S(2)}, u32[]{:S(2)}) %collective-permute-start.3) | collective-permute-done | bytes 524320 | tf_op jit(solution)/shard_map/ppermute | solution.py:24
  25.5 3.2 %shard_map.95 = (bf16[256,1024]{1,0:T(8,128)(2,1)S(1)}, bf16[256,256]{1,0:T(8,128)(2,1)S(1)}, bf16[256,2048]{1,0:T(8,128)(2,1)S(1)}, bf16[128,1024]{1,0:T(8,128)(2,1)S(1)}, bf16[128,1024]{1,0:T(8,128)(2,1)S(1)}) custom-call(s32[2]{0:T(128)S(1)} %pad_add_fusion.place, bf16[128,4224]{1,0:T(8,128)(2,1)S(1)} %shard_map.94.refs_0_, ...), custom_call_target="tpu_custom_call" | custom-call | tf_op jit(solution)/shard_map/pallas_call | solution.py:127
  28.7 2.7 %collective-permute-done.2.refs_1_ = bf16[128,4224]{1,0:T(8,128)(2,1)S(1)} collective-permute-done((bf16[128,4224]{1,0:T(8,128)(2,1)S(1)}, bf16[128,4224]{1,0:T(8,128)(2,1)S(1)}, u32[]{:S(2)}, u32[]{:S(2)}) %collective-permute-start.2) | collective-permute-done | bytes 1081376 | tf_op jit(solution)/shard_map/ppermute | solution.py:24
  31.4 1.5 %collective-permute-done.1.refs_0_ = bf16[128,4224]{1,0:T(8,128)(2,1)S(1)} collective-permute-done((bf16[128,4224]{1,0:T(8,128)(2,1)S(1)}, bf16[128,4224]{1,0:T(8,128)(2,1)S(1)}, u32[]{:S(2)}, u32[]{:S(2)}) %collective-permute-start.1) | collective-permute-done | bytes 1081376 | tf_op jit(solution)/shard_map/ppermute | solution.py:24
  33.4 1.6 %collective-permute-start.7 = (bf16[64,4224]{1,0:T(8,128)(2,1)S(1)}, bf16[64,4224]{1,0:T(8,128)(2,1)S(1)}, u32[]{:S(2)}, u32[]{:S(2)}) collective-permute-start(bf16[64,4224]{1,0:T(8,128)(2,1)S(1)} %slice.28), channel_id=1, source_target_pairs={{0,2},{1,3},{2,0},{3,1},{4,6},{5,7},{6,4},{7,5},{8,10},{9,11},{10,... | collective-permute-start | bytes 1622024 | tf_op jit(solution)/shard_map/ppermute | solution.py:24
  35.4 1.5 %collective-permute-start.8 = (bf16[1,2,64,2048]{3,2,1,0:T(8,128)(2,1)S(1)}, bf16[1,2,64,2048]{3,2,1,0:T(8,128)(2,1)S(1)}, u32[]{:S(2)}, u32[]{:S(2)}) collective-permute-start(bf16[1,2,64,2048]{3,2,1,0:T(8,128)(2,1)S(1)} %get-tuple-element.73), channel_id=1, source_target_pairs={{0,4},{4,0},{8,12},{12,8},{16,20},{20,16},{24,28},{28,24},{1,5},{5... | collective-permute-start | bytes 1572872 | tf_op jit(solution)/shard_map/ppermute | solution.py:24
  37.0 2.5 %shard_map.97 = (bf16[256,1024]{1,0:T(8,128)(2,1)S(1)}, bf16[256,256]{1,0:T(8,128)(2,1)S(1)}, bf16[256,2048]{1,0:T(8,128)(2,1)S(1)}, bf16[128,1024]{1,0:T(8,128)(2,1)S(1)}, bf16[128,1024]{1,0:T(8,128)(2,1)S(1)}) custom-call(s32[2]{0:T(128)S(1)} %pad_add_fusion.place, bf16[128,4224]{1,0:T(8,128)(2,1)S(1)} %get-tuple-element.55.refs_0_, ...), custom_call_target="tpu_custom_call" | custom-call | tf_op jit(solution)/shard_map/pallas_call | solution.py:127
  39.5 2.5 %shard_map.98 = (bf16[256,1024]{1,0:T(8,128)(2,1)S(1)}, bf16[256,256]{1,0:T(8,128)(2,1)S(1)}, bf16[256,2048]{1,0:T(8,128)(2,1)S(1)}, bf16[128,1024]{1,0:T(8,128)(2,1)S(1)}, bf16[128,1024]{1,0:T(8,128)(2,1)S(1)}) custom-call(s32[2]{0:T(128)S(1)} %pad_add_fusion.place, bf16[128,4224]{1,0:T(8,128)(2,1)S(1)} %get-tuple-element.64.refs_0_, ...), custom_call_target="tpu_custom_call" | custom-call | tf_op jit(solution)/shard_map/pallas_call | solution.py:127
  42.0 2.7 %shard_map.99 = (f32[1024,1024]{1,0:T(8,128)S(1)}, f32[256,2048]{1,0:T(8,128)S(1)}, bf16[256,1024]{1,0:T(8,128)(2,1)S(1)}, f32[8,128]{1,0:T(8,128)S(1)}) custom-call(bf16[256,1024]{1,0:T(8,128)(2,1)S(1)} %get-tuple-element.57.refs_0_, bf16[256,256]{1,0:T(8,128)(2,1)S(1)} %get-tuple-element.54.refs_4_.refs_1_, ...), custom_call_target="tpu_custom_call" | custom-call | tf_op jit(solution)/shard_map/pallas_call | solution.py:171
  44.7 4.0 %collective-permute-done.8.refs_3_ = bf16[1,2,64,2048]{3,2,1,0:T(8,128)(2,1)S(1)} collective-permute-done((bf16[1,2,64,2048]{3,2,1,0:T(8,128)(2,1)S(1)}, bf16[1,2,64,2048]{3,2,1,0:T(8,128)(2,1)S(1)}, u32[]{:S(2)}, u32[]{:S(2)}) %collective-permute-start.8) | collective-permute-done | bytes 524320 | tf_op jit(solution)/shard_map/ppermute | solution.py:24
  49.4 1.5 %collective-permute-start.19 = (bf16[1,2,64,2048]{3,2,1,0:T(8,128)(2,1)S(1)}, bf16[1,2,64,2048]{3,2,1,0:T(8,128)(2,1)S(1)}, u32[]{:S(2)}, u32[]{:S(2)}) collective-permute-start(bf16[1,2,64,2048]{3,2,1,0:T(8,128)(2,1)S(1)} %get-tuple-element.84), channel_id=1, source_target_pairs={{0,8},{4,12},{8,0},{12,4},{16,24},{20,28},{24,16},{28,20},{1,9},{5... | collective-permute-start | bytes 1572872 | tf_op jit(solution)/shard_map/ppermute | solution.py:24
  51.6 2.5 %shard_map.101 = (bf16[256,1024]{1,0:T(8,128)(2,1)S(1)}, bf16[256,256]{1,0:T(8,128)(2,1)S(1)}, bf16[256,2048]{1,0:T(8,128)(2,1)S(1)}, bf16[128,1024]{1,0:T(8,128)(2,1)S(1)}, bf16[128,1024]{1,0:T(8,128)(2,1)S(1)}) custom-call(s32[2]{0:T(128)S(1)} %pad_add_fusion.place, bf16[64,4224]{1,0:T(8,128)(2,1)S(1)} %get-tuple-element.75.refs_0_, ...), custom_call_target="tpu_custom_call" | custom-call | tf_op jit(solution)/shard_map/pallas_call | solution.py:127
  54.9 1.3 %add_convert_fusion = bf16[1024,1024]{1,0:T(8,128)(2,1)S(1)} fusion(f32[1024,1024]{1,0:T(8,128)S(1)} %get-tuple-element.71, f32[1024,1024]{1,0:T(8,128)S(1)} %fusion.14), kind=kLoop, calls=%fused_computation | loop fusion | flops 2097152 | bytes 10485760 | tf_op jit(solution)/shard_map/convert_element_type | solution.py:20
  56.4 1.6 %collective-permute-start.15 = (bf16[1,96,1024]{2,1,0:T(8,128)(2,1)S(1)}, bf16[1,96,1024]{2,1,0:T(8,128)(2,1)S(1)}, u32[]{:S(2)}, u32[]{:S(2)}) collective-permute-start(bf16[1,96,1024]{2,1,0:T(8,128)(2,1)S(1)} %dynamic-slice_bitcast_fusion.12.refs_1_), channel_id=1, source_target_pairs={{0,4},{4,0},{8,12},{12,8},{16,20},{20,16},{24,28},{28,24},{1,5},{5... | collective-permute-start | bytes 589832 | tf_op jit(solution)/shard_map/ppermute | solution.py:24
  58.0 1.3 %convolution_convert_fusion = bf16[256,2048]{1,0:T(8,128)(2,1)S(1)} fusion(bf16[256,1024]{1,0:T(8,128)(2,1)S(1)} %shard_map.102, bf16[1,2048,1024]{2,1,0:T(8,128)(2,1)S(1)} %copy-done), kind=kOutput, calls=%fused_computation.1 | convolution fusion | flops 1074266112 | bytes 5767168 | tf_op jit(solution)/shard_map/dot_general | solution.py:269
  60.8 3.4 %collective-permute-done.15.refs_2_ = bf16[1,96,1024]{2,1,0:T(8,128)(2,1)S(1)} collective-permute-done((bf16[1,96,1024]{2,1,0:T(8,128)(2,1)S(1)}, bf16[1,96,1024]{2,1,0:T(8,128)(2,1)S(1)}, u32[]{:S(2)}, u32[]{:S(2)}) %collective-permute-start.15) | collective-permute-done | bytes 196640 | tf_op jit(solution)/shard_map/ppermute | solution.py:24
  64.3 2.7 %collective-permute-start.16 = (bf16[1,96,1024]{2,1,0:T(8,128)(2,1)S(1)}, bf16[1,96,1024]{2,1,0:T(8,128)(2,1)S(1)}, u32[]{:S(2)}, u32[]{:S(2)}) collective-permute-start(bf16[1,96,1024]{2,1,0:T(8,128)(2,1)S(1)} %fusion.18), channel_id=1, source_target_pairs={{0,16},{4,20},{8,24},{12,28},{16,0},{20,4},{24,8},{28,12},{1,17},{... | collective-permute-start | bytes 589832 | tf_op jit(solution)/shard_map/ppermute | solution.py:24
  67.0 1.5 %collective-permute-start.20 = (bf16[1,64,2048]{2,1,0:T(8,128)(2,1)S(1)}, bf16[1,64,2048]{2,1,0:T(8,128)(2,1)S(1)}, u32[]{:S(2)}, u32[]{:S(2)}) collective-permute-start(bf16[1,64,2048]{2,1,0:T(8,128)(2,1)S(1)} %get-tuple-element.86), channel_id=1, source_target_pairs={{0,4},{4,0},{8,12},{12,8},{16,20},{20,16},{24,28},{28,24},{1,5},{5... | collective-permute-start | bytes 786440 | tf_op jit(solution)/shard_map/ppermute | solution.py:24
  68.7 1.3 %fusion.1 = f32[256,2048]{1,0:T(8,128)S(1)} fusion(bf16[256,2048]{1,0:T(8,128)(2,1)S(1)} %collective-permute-done.11, bf16[128,1024]{1,0:T(8,128)(2,1)S(1)} %get-tuple-element.56.refs_8_, bf16[128,1024]{1,0:T(8,128)(2,1)S(1)} %get-tuple-element.47.refs_3_, bf16[1,2048,1024]{2,1,0:T(8,128)(2,1)S(1)} %copy-done), kind=kOutput, calls=%fused_computation.4 | convolution fusion | flops 1076887552 | bytes 7864320 | tf_op jit(solution)/shard_map/dot_general | solution.py:269
  71.4 2.7 %collective-permute-start.17 = (bf16[1,160,1024]{2,1,0:T(8,128)(2,1)S(1)}, bf16[1,160,1024]{2,1,0:T(8,128)(2,1)S(1)}, u32[]{:S(2)}, u32[]{:S(2)}) collective-permute-start(bf16[1,160,1024]{2,1,0:T(8,128)(2,1)S(1)} %fusion.5), channel_id=1, source_target_pairs={{0,16},{4,20},{8,24},{12,28},{16,0},{20,4},{24,8},{28,12},{1,17},{... | collective-permute-start | bytes 983048 | tf_op jit(solution)/shard_map/ppermute | solution.py:24
  74.0 1.5 %collective-permute-start.14 = (bf16[1,256,1024]{2,1,0:T(8,128)(2,1)S(1)}, bf16[1,256,1024]{2,1,0:T(8,128)(2,1)S(1)}, u32[]{:S(2)}, u32[]{:S(2)}) collective-permute-start(bf16[1,256,1024]{2,1,0:T(8,128)(2,1)S(1)} %shard_map.103), channel_id=1, source_target_pairs={{0,4},{4,0},{8,12},{12,8},{16,20},{20,16},{24,28},{28,24},{1,5},{5... | collective-permute-start | bytes 1572872 | tf_op jit(solution)/shard_map/ppermute | solution.py:24
  75.5 1.3 %collective-permute-done.20 = bf16[1,64,2048]{2,1,0:T(8,128)(2,1)S(1)} collective-permute-done((bf16[1,64,2048]{2,1,0:T(8,128)(2,1)S(1)}, bf16[1,64,2048]{2,1,0:T(8,128)(2,1)S(1)}, u32[]{:S(2)}, u32[]{:S(2)}) %collective-permute-start.20) | collective-permute-done | bytes 262176 | tf_op jit(solution)/shard_map/ppermute | solution.py:24
  77.0 2.7 %collective-permute-start.21 = (bf16[1,64,2048]{2,1,0:T(8,128)(2,1)S(1)}, bf16[1,64,2048]{2,1,0:T(8,128)(2,1)S(1)}, u32[]{:S(2)}, u32[]{:S(2)}) collective-permute-start(bf16[1,64,2048]{2,1,0:T(8,128)(2,1)S(1)} %fusion.7), channel_id=1, source_target_pairs={{0,16},{4,20},{8,24},{12,28},{16,0},{20,4},{24,8},{28,12},{1,17},{... | collective-permute-start | bytes 786440 | tf_op jit(solution)/shard_map/ppermute | solution.py:24
  79.6 2.2 %collective-permute-done.12.refs_1_ = bf16[128,2048]{1,0:T(8,128)(2,1)S(1)} collective-permute-done((bf16[128,2048]{1,0:T(8,128)(2,1)S(1)}, bf16[128,2048]{1,0:T(8,128)(2,1)S(1)}, u32[]{:S(2)}, u32[]{:S(2)}) %collective-permute-start.12) | collective-permute-done | bytes 524320 | tf_op jit(solution)/shard_map/ppermute | solution.py:24
  83.3 12.2 %collective-permute-done.17.refs_0_ = bf16[1,160,1024]{2,1,0:T(8,128)(2,1)S(1)} collective-permute-done((bf16[1,160,1024]{2,1,0:T(8,128)(2,1)S(1)}, bf16[1,160,1024]{2,1,0:T(8,128)(2,1)S(1)}, u32[]{:S(2)}, u32[]{:S(2)}) %collective-permute-start.17) | collective-permute-done | bytes 327712 | tf_op jit(solution)/shard_map/ppermute | solution.py:24
  95.5 1.2 %fusion.4 = f32[1,256,1024]{2,1,0:T(8,128)} fusion(bf16[1,256,1024]{2,1,0:T(8,128)(2,1)S(1)} %collective-permute-done.14, bf16[1,160,1024]{2,1,0:T(8,128)(2,1)S(1)} %shard_map.105, bf16[1,96,1024]{2,1,0:T(8,128)(2,1)S(1)} %collective-permute-done.16, bf16[1,2,2,256,1024]{4,3,2,1,0:T(8,128)(2,1)S(1)} %bitcast.85, u32[]{:T(128)S(6)} %optimization_barrier.37, ...), kind=kLoop, calls=%fused_computation.11 | loop fusion | flops 2359296 | bytes 2621448 | tf_op jit(solution)/shard_map/mul | solution.py:293
  96.7 3.3 %collective-permute-done.21 = bf16[1,64,2048]{2,1,0:T(8,128)(2,1)S(1)} collective-permute-done((bf16[1,64,2048]{2,1,0:T(8,128)(2,1)S(1)}, bf16[1,64,2048]{2,1,0:T(8,128)(2,1)S(1)}, u32[]{:S(2)}, u32[]{:S(2)}) %collective-permute-start.21) | collective-permute-done | bytes 262176 | tf_op jit(solution)/shard_map/ppermute | solution.py:24
  (64 shorter events, 11.9 us)
Async XLA Ops:
  0.7 1.0 %copy-start.2 = (bf16[128,2048]{1,0:T(8,128)(2,1)S(1)}, bf16[128,2048]{1,0:T(8,128)(2,1)}, u32[]{:S(2)}) copy-start(bf16[128,2048]{1,0:T(8,128)(2,1)} %tokens.1) | copy-start | bytes 1572868
  1.8 1.0 %copy-start.3 = (bf16[128,2048]{1,0:T(8,128)(2,1)S(1)}, bf16[128,2048]{1,0:T(8,128)(2,1)}, u32[]{:S(2)}) copy-start(bf16[128,2048]{1,0:T(8,128)(2,1)} %cotangent.1) | copy-start | bytes 1572868
  2.8 0.7 copy-start.4
  3.5 0.7 copy-start.5
  4.4 26.9 %collective-permute-start.2 = (bf16[128,4224]{1,0:T(8,128)(2,1)S(1)}, bf16[128,4224]{1,0:T(8,128)(2,1)S(1)}, u32[]{:S(2)}, u32[]{:S(2)}) collective-permute-start(bf16[128,4224]{1,0:T(8,128)(2,1)S(1)} %shard_map.94.refs_0_), channel_id=1, source_target_pairs={{0,8},{4,12},{8,0},{12,4},{16,24},{20,28},{24,16},{28,20},{1,9},{5... | collective-permute-start | bytes 3244040 | tf_op jit(solution)/shard_map/ppermute | solution.py:24
  7.5 25.3 %collective-permute-start.1 = (bf16[128,4224]{1,0:T(8,128)(2,1)S(1)}, bf16[128,4224]{1,0:T(8,128)(2,1)S(1)}, u32[]{:S(2)}, u32[]{:S(2)}) collective-permute-start(bf16[128,4224]{1,0:T(8,128)(2,1)S(1)} %shard_map.94.refs_0_), channel_id=1, source_target_pairs={{0,2},{1,3},{2,0},{3,1},{4,6},{5,7},{6,4},{7,5},{8,10},{9,11},{10,... | collective-permute-start | bytes 3244040 | tf_op jit(solution)/shard_map/ppermute | solution.py:24
  9.0 16.4 %collective-permute-start = (bf16[128,4224]{1,0:T(8,128)(2,1)S(1)}, bf16[128,4224]{1,0:T(8,128)(2,1)}, u32[]{:S(2)}, u32[]{:S(2)}) collective-permute-start(bf16[128,4224]{1,0:T(8,128)(2,1)S(1)} %shard_map.94.refs_0_), channel_id=1, source_target_pairs={{0,1},{1,0},{2,3},{3,2},{4,5},{5,4},{6,7},{7,6},{8,9},{9,8},{10,11... | collective-permute-start | bytes 3244040 | tf_op jit(solution)/shard_map/ppermute | solution.py:24
  9.0 16.4 %copy-start = (bf16[1,2048,1024]{2,1,0:T(8,128)(2,1)S(1)}, bf16[1,2048,1024]{2,1,0:T(8,128)(2,1)}, u32[]{:S(2)}) copy-start(bf16[1,2048,1024]{2,1,0:T(8,128)(2,1)} %param.11) | copy-start | bytes 12582916
  10.8 14.6 %copy-start.1 = (bf16[1,512,2048]{2,1,0:T(8,128)(2,1)S(1)}, bf16[1,512,2048]{2,1,0:T(8,128)(2,1)}, u32[]{:S(2)}) copy-start(bf16[1,512,2048]{2,1,0:T(8,128)(2,1)} %param.12) | copy-start | bytes 6291460
  10.9 14.4 %collective-permute-start.3 = (bf16[1,2,64,2048]{3,2,1,0:T(8,128)(2,1)S(1)}, bf16[1,2,64,2048]{3,2,1,0:T(8,128)(2,1)S(1)}, u32[]{:S(2)}, u32[]{:S(2)}) collective-permute-start(bf16[1,2,64,2048]{3,2,1,0:T(8,128)(2,1)S(1)} %pad_maximum_fusion), channel_id=1, source_target_pairs={{0,4},{4,0},{8,12},{12,8},{16,20},{20,16},{24,28},{28,24},{1,5},{5... | collective-permute-start | bytes 1572872 | tf_op jit(solution)/shard_map/ppermute | solution.py:24
  32.8 4.1 %collective-permute-start.4 = (bf16[128,4224]{1,0:T(8,128)(2,1)S(1)}, bf16[128,4224]{1,0:T(8,128)(2,1)S(1)}, u32[]{:S(2)}, u32[]{:S(2)}) collective-permute-start(bf16[128,4224]{1,0:T(8,128)(2,1)S(1)} %get-tuple-element.55.refs_0_), channel_id=1, source_target_pairs={{0,1},{1,0},{2,3},{3,2},{4,5},{5,4},{6,7},{7,6},{8,9},{9,8},{10,11... | collective-permute-start | bytes 3244040 | tf_op jit(solution)/shard_map/ppermute | solution.py:24
  32.8 6.6 %collective-permute-start.5 = (bf16[128,4224]{1,0:T(8,128)(2,1)S(1)}, bf16[128,4224]{1,0:T(8,128)(2,1)S(1)}, u32[]{:S(2)}, u32[]{:S(2)}) collective-permute-start(bf16[128,4224]{1,0:T(8,128)(2,1)S(1)} %get-tuple-element.64.refs_0_), channel_id=1, source_target_pairs={{0,1},{1,0},{2,3},{3,2},{4,5},{5,4},{6,7},{7,6},{8,9},{9,8},{10,11... | collective-permute-start | bytes 3244040 | tf_op jit(solution)/shard_map/ppermute | solution.py:24
  33.4 15.3 %collective-permute-start.7 = (bf16[64,4224]{1,0:T(8,128)(2,1)S(1)}, bf16[64,4224]{1,0:T(8,128)(2,1)S(1)}, u32[]{:S(2)}, u32[]{:S(2)}) collective-permute-start(bf16[64,4224]{1,0:T(8,128)(2,1)S(1)} %slice.28), channel_id=1, source_target_pairs={{0,2},{1,3},{2,0},{3,1},{4,6},{5,7},{6,4},{7,5},{8,10},{9,11},{10,... | collective-permute-start | bytes 1622024 | tf_op jit(solution)/shard_map/ppermute | solution.py:24
  35.0 13.9 %collective-permute-start.6 = (bf16[64,4224]{1,0:T(8,128)(2,1)S(1)}, bf16[64,4224]{1,0:T(8,128)(2,1)S(1)}, u32[]{:S(2)}, u32[]{:S(2)}) collective-permute-start(bf16[64,4224]{1,0:T(8,128)(2,1)S(1)} %slice.27), channel_id=1, source_target_pairs={{0,8},{4,12},{8,0},{12,4},{16,24},{20,28},{24,16},{28,20},{1,9},{5... | collective-permute-start | bytes 1622024 | tf_op jit(solution)/shard_map/ppermute | solution.py:24
  35.4 13.3 %collective-permute-start.8 = (bf16[1,2,64,2048]{3,2,1,0:T(8,128)(2,1)S(1)}, bf16[1,2,64,2048]{3,2,1,0:T(8,128)(2,1)S(1)}, u32[]{:S(2)}, u32[]{:S(2)}) collective-permute-start(bf16[1,2,64,2048]{3,2,1,0:T(8,128)(2,1)S(1)} %get-tuple-element.73), channel_id=1, source_target_pairs={{0,4},{4,0},{8,12},{12,8},{16,20},{20,16},{24,28},{28,24},{1,5},{5... | collective-permute-start | bytes 1572872 | tf_op jit(solution)/shard_map/ppermute | solution.py:24
  48.9 2.0 %collective-permute-start.9 = (bf16[64,4224]{1,0:T(8,128)(2,1)S(1)}, bf16[64,4224]{1,0:T(8,128)(2,1)S(1)}, u32[]{:S(2)}, u32[]{:S(2)}) collective-permute-start(bf16[64,4224]{1,0:T(8,128)(2,1)S(1)} %get-tuple-element.75.refs_0_), channel_id=1, source_target_pairs={{0,1},{1,0},{2,3},{3,2},{4,5},{5,4},{6,7},{7,6},{8,9},{9,8},{10,11... | collective-permute-start | bytes 1622024 | tf_op jit(solution)/shard_map/ppermute | solution.py:24
  48.9 2.7 %collective-permute-start.10 = (bf16[64,4224]{1,0:T(8,128)(2,1)S(1)}, bf16[64,4224]{1,0:T(8,128)(2,1)S(1)}, u32[]{:S(2)}, u32[]{:S(2)}) collective-permute-start(bf16[64,4224]{1,0:T(8,128)(2,1)S(1)} %get-tuple-element.76.refs_1_), channel_id=1, source_target_pairs={{0,1},{1,0},{2,3},{3,2},{4,5},{5,4},{6,7},{7,6},{8,9},{9,8},{10,11... | collective-permute-start | bytes 1622024 | tf_op jit(solution)/shard_map/ppermute | solution.py:24
  49.4 17.6 %collective-permute-start.19 = (bf16[1,2,64,2048]{3,2,1,0:T(8,128)(2,1)S(1)}, bf16[1,2,64,2048]{3,2,1,0:T(8,128)(2,1)S(1)}, u32[]{:S(2)}, u32[]{:S(2)}) collective-permute-start(bf16[1,2,64,2048]{3,2,1,0:T(8,128)(2,1)S(1)} %get-tuple-element.84), channel_id=1, source_target_pairs={{0,8},{4,12},{8,0},{12,4},{16,24},{20,28},{24,16},{28,20},{1,9},{5... | collective-permute-start | bytes 1572872 | tf_op jit(solution)/shard_map/ppermute | solution.py:24
  56.4 7.8 %collective-permute-start.15 = (bf16[1,96,1024]{2,1,0:T(8,128)(2,1)S(1)}, bf16[1,96,1024]{2,1,0:T(8,128)(2,1)S(1)}, u32[]{:S(2)}, u32[]{:S(2)}) collective-permute-start(bf16[1,96,1024]{2,1,0:T(8,128)(2,1)S(1)} %dynamic-slice_bitcast_fusion.12.refs_1_), channel_id=1, source_target_pairs={{0,4},{4,0},{8,12},{12,8},{16,20},{20,16},{24,28},{28,24},{1,5},{5... | collective-permute-start | bytes 589832 | tf_op jit(solution)/shard_map/ppermute | solution.py:24
  59.3 9.4 %collective-permute-start.11 = (bf16[256,2048]{1,0:T(8,128)(2,1)S(1)}, bf16[256,2048]{1,0:T(8,128)(2,1)S(1)}, u32[]{:S(2)}, u32[]{:S(2)}) collective-permute-start(bf16[256,2048]{1,0:T(8,128)(2,1)S(1)} %convolution_convert_fusion), channel_id=1, source_target_pairs={{0,1},{1,0},{2,3},{3,2},{4,5},{5,4},{6,7},{7,6},{8,9},{9,8},{10,11... | collective-permute-start | bytes 3145736 | tf_op jit(solution)/shard_map/ppermute | solution.py:24
  59.4 11.8 %collective-permute-start.13 = (bf16[1,160,1024]{2,1,0:T(8,128)(2,1)S(1)}, bf16[1,160,1024]{2,1,0:T(8,128)(2,1)S(1)}, u32[]{:S(2)}, u32[]{:S(2)}) collective-permute-start(bf16[1,160,1024]{2,1,0:T(8,128)(2,1)S(1)} %dynamic-slice_bitcast_fusion.1), channel_id=1, source_target_pairs={{0,4},{4,0},{8,12},{12,8},{16,20},{20,16},{24,28},{28,24},{1,5},{5... | collective-permute-start | bytes 983048 | tf_op jit(solution)/shard_map/ppermute | solution.py:24
  64.3 31.2 %collective-permute-start.16 = (bf16[1,96,1024]{2,1,0:T(8,128)(2,1)S(1)}, bf16[1,96,1024]{2,1,0:T(8,128)(2,1)S(1)}, u32[]{:S(2)}, u32[]{:S(2)}) collective-permute-start(bf16[1,96,1024]{2,1,0:T(8,128)(2,1)S(1)} %fusion.18), channel_id=1, source_target_pairs={{0,16},{4,20},{8,24},{12,28},{16,0},{20,4},{24,8},{28,12},{1,17},{... | collective-permute-start | bytes 589832 | tf_op jit(solution)/shard_map/ppermute | solution.py:24
  67.0 9.9 %collective-permute-start.20 = (bf16[1,64,2048]{2,1,0:T(8,128)(2,1)S(1)}, bf16[1,64,2048]{2,1,0:T(8,128)(2,1)S(1)}, u32[]{:S(2)}, u32[]{:S(2)}) collective-permute-start(bf16[1,64,2048]{2,1,0:T(8,128)(2,1)S(1)} %get-tuple-element.86), channel_id=1, source_target_pairs={{0,4},{4,0},{8,12},{12,8},{16,20},{20,16},{24,28},{28,24},{1,5},{5... | collective-permute-start | bytes 786440 | tf_op jit(solution)/shard_map/ppermute | solution.py:24
  70.1 11.8 %collective-permute-start.12 = (bf16[128,2048]{1,0:T(8,128)(2,1)S(1)}, bf16[128,2048]{1,0:T(8,128)(2,1)S(1)}, u32[]{:S(2)}, u32[]{:S(2)}) collective-permute-start(bf16[128,2048]{1,0:T(8,128)(2,1)S(1)} %slice.57), channel_id=1, source_target_pairs={{0,2},{1,3},{2,0},{3,1},{4,6},{5,7},{6,4},{7,5},{8,10},{9,11},{10,... | collective-permute-start | bytes 1572872 | tf_op jit(solution)/shard_map/ppermute | solution.py:24
  71.4 24.1 %collective-permute-start.17 = (bf16[1,160,1024]{2,1,0:T(8,128)(2,1)S(1)}, bf16[1,160,1024]{2,1,0:T(8,128)(2,1)S(1)}, u32[]{:S(2)}, u32[]{:S(2)}) collective-permute-start(bf16[1,160,1024]{2,1,0:T(8,128)(2,1)S(1)} %fusion.5), channel_id=1, source_target_pairs={{0,16},{4,20},{8,24},{12,28},{16,0},{20,4},{24,8},{28,12},{1,17},{... | collective-permute-start | bytes 983048 | tf_op jit(solution)/shard_map/ppermute | solution.py:24
  74.0 21.5 %collective-permute-start.14 = (bf16[1,256,1024]{2,1,0:T(8,128)(2,1)S(1)}, bf16[1,256,1024]{2,1,0:T(8,128)(2,1)S(1)}, u32[]{:S(2)}, u32[]{:S(2)}) collective-permute-start(bf16[1,256,1024]{2,1,0:T(8,128)(2,1)S(1)} %shard_map.103), channel_id=1, source_target_pairs={{0,4},{4,0},{8,12},{12,8},{16,20},{20,16},{24,28},{28,24},{1,5},{5... | collective-permute-start | bytes 1572872 | tf_op jit(solution)/shard_map/ppermute | solution.py:24
  77.0 23.1 %collective-permute-start.21 = (bf16[1,64,2048]{2,1,0:T(8,128)(2,1)S(1)}, bf16[1,64,2048]{2,1,0:T(8,128)(2,1)S(1)}, u32[]{:S(2)}, u32[]{:S(2)}) collective-permute-start(bf16[1,64,2048]{2,1,0:T(8,128)(2,1)S(1)} %fusion.7), channel_id=1, source_target_pairs={{0,16},{4,20},{8,24},{12,28},{16,0},{20,4},{24,8},{28,12},{1,17},{... | collective-permute-start | bytes 786440 | tf_op jit(solution)/shard_map/ppermute | solution.py:24
  81.9 18.2 %collective-permute-start.18 = (bf16[1,64,2048]{2,1,0:T(8,128)(2,1)S(1)}, bf16[1,64,2048]{2,1,0:T(8,128)(2,1)S(1)}, u32[]{:S(2)}, u32[]{:S(2)}) collective-permute-start(bf16[1,64,2048]{2,1,0:T(8,128)(2,1)S(1)} %shard_map.104.refs_1_), channel_id=1, source_target_pairs={{0,4},{4,0},{8,12},{12,8},{16,20},{20,16},{24,28},{28,24},{1,5},{5... | collective-permute-start | bytes 786440 | tf_op jit(solution)/shard_map/ppermute | solution.py:24

commit v13 on v12

--- a/solution.py
+++ b/solution.py
@@ -9,6 +9,7 @@
 from jax.sharding import PartitionSpec as P
 
 LANES = 128
+HERE = pl.BlockSpec(memory_space=pl.ANY)
 FREE = pl.CostEstimate(flops=0, bytes_accessed=0, transcendentals=0)
 
 
@@ -31,12 +32,20 @@
     return lax.squeeze(lax.dynamic_slice(values, starts, sizes), (axis,))
 
 
-def pack_kernel(expert_count, tokens, cotangent, ids, probs, packed, coded, sems):
-    width = tokens.shape[1]
-    moves = [(tokens, packed.at[:, :width]), (cotangent, packed.at[:, width : 2 * width])]
+def begin(moves, sems):
     copies = [pltpu.make_async_copy(src, dst, sems.at[k]) for k, (src, dst) in enumerate(moves)]
     for copy in copies:
         copy.start()
+    return copies
+
+
+def pack_kernel(tokens, cotangent, ids_in, probs_in, packed, coded, ids, probs, sems):
+    width = tokens.shape[1]
+    small = begin([(ids_in, ids), (probs_in, probs)], sems)
+    moves = [(tokens, packed.at[:, :width]), (cotangent, packed.at[:, width : 2 * width])]
+    large = begin(moves, sems.at[2:4])
+    for copy in small:
+        copy.wait()
     line = lax.broadcasted_iota(jnp.int32, (LANES, tokens.shape[0]), 0)
     route = jnp.zeros(line.shape, jnp.float32)
     for k in range(ids.shape[0]):
@@ -49,22 +58,25 @@
     part = lax.rem(line, 3)
     lines = jnp.where(part == 0, high, jnp.where(part == 1, middle, low))
     coded[...] = narrow(lines.T)
-    last = pltpu.make_async_copy(coded, packed.at[:, 2 * width :], sems.at[2])
-    last.start()
-    for copy in (*copies, last):
+    last = begin([(coded, packed.at[:, 2 * width :])], sems.at[4:5])
+    for copy in (*large, *last):
         copy.wait()
 
 
-def packed(tokens, cotangent, expert_ids, gate_probs, expert_count):
+def packed(tokens, cotangent, expert_ids, gate_probs):
     rows, width = tokens.shape
-    here, vmem = pl.BlockSpec(memory_space=pl.ANY), pl.BlockSpec(memory_space=pltpu.VMEM)
+    top = expert_ids.shape[1]
     return pl.pallas_call(
-        functools.partial(pack_kernel, expert_count),
+        pack_kernel,
         out_shape=jax.ShapeDtypeStruct((rows, 2 * width + LANES), jnp.bfloat16),
-        in_specs=[here, here, vmem, vmem],
-        out_specs=here,
-        scratch_shapes=[pltpu.VMEM((rows, LANES), jnp.bfloat16), pltpu.SemaphoreType.DMA((3,))],
-        compiler_params=pltpu.CompilerParams(vmem_limit_bytes=4 << 20),
+        in_specs=[HERE] * 4,
+        out_specs=HERE,
+        scratch_shapes=[
+            pltpu.VMEM((rows, LANES), jnp.bfloat16),
+            pltpu.VMEM((top, rows), jnp.int32),
+            pltpu.VMEM((top, rows), jnp.float32),
+            pltpu.SemaphoreType.DMA((5,)),
+        ],
         cost_estimate=FREE,
     )(tokens, cotangent, expert_ids.T, gate_probs.T)
 
@@ -197,7 +209,7 @@
     place = jnp.stack([me, (group >> 1) & 1]).astype(jnp.int32)
     high_count, half = group_count // 8, tok_rows // 2
 
-    rows_own = packed(tokens, cotangent, expert_ids, gate_probs, expert_count)
+    rows_own = packed(tokens, cotangent, expert_ids, gate_probs)
     rows_own, place, bits = lax.optimization_barrier((rows_own, place, bits))
     bit0, bit1, bit2, not0, not1, not2 = bits
     rows_c = flip(rows_own, "expert", 1)

time: 101 us -> 131 us (1.30)
  Pallas kernels: 13.7 us -> 45.6 us
  local copies, waits for them, and re-layouts: 5.68 us -> 2.25 us
    pallas_call x1, Pallas kernels: 0.25 us -> 32.9 us  [packed(): pl.pallas_call(pack_kernel, out_shape=jax.ShapeDtypeStruct((rows, 2 * wid...]
    unnamed x12 -> x6, local copies, waits for them, and re-layouts: 3.45 us -> 0.01 us
  transfers between devices with their start and end apart: 22 -> 22, of which waited for: 12 -> 12; matrix products, arithmetic and copies ran while one was open for 10% -> 8% of each run, Pallas kernels for 13% -> 10%
where the time goes in v13:
time: 131 us; the launch traced here: 130 us
  waiting for transfers between devices  45.9 us (35%)
  Pallas kernels  45.6 us (35%)
  starting transfers between devices  26.5 us (20%)
  other arithmetic  5.42 us (4%)
  matrix products  3.79 us (3%)
  local copies, waits for them, and re-layouts  2.25 us (2%)
    ppermute x22, waiting for transfers between devices, flip(): lax.ppermute(values, axis, [(i, i ^ bit) for i in range(lax.axis_size(axi...  45.9 us
    pallas_call x1, Pallas kernels, packed(): pl.pallas_call(pack_kernel, out_shape=jax.ShapeDtypeStruct((rows, 2 * wid...  32.9 us
    ppermute x22, starting transfers between devices, flip(): lax.ppermute(values, axis, [(i, i ^ bit) for i in range(lax.axis_size(axi...  26.5 us
    pallas_call x4, Pallas kernels, expert_rows(): pl.pallas_call(functools.partial(expert_kernel, group_count), out_shape=t...  10 us
    convert_element_type x7, other arithmetic, narrow(): return values.astype(jnp.bfloat16)  2.89 us
    pallas_call x1, Pallas kernels, early_terms(): pl.pallas_call(terms_kernel, out_shape=(jax.ShapeDtypeStruct((tok_cols.sh...  2.71 us
  transfers between devices with their start and end apart: 22, of which 12 were waited for; matrix products, arithmetic and copies ran while one was open for 8% of the time, Pallas kernels for 10%

profile of v13, /device:TPU:0, one launch (start us, length us, event | category | flops | bytes accessed | tf_op | source)
XLA Modules:
  0.0 130.4 jit_solution(13910066320383312795)
XLA Ops:
  0.7 32.9 %shard_map.94.refs_0_ = bf16[128,4224]{1,0:T(8,128)(2,1)} custom-call(bf16[128,2048]{1,0:T(8,128)(2,1)} %tokens.1, bf16[128,2048]{1,0:T(8,128)(2,1)} %cotangent.1, s32[2,128]{1,0:T(2,128)} %bitcast.88, f32[2,128]{1,0:T(2,128)} %bitcast.89), custom_call_target="tpu_custom_call" | custom-call | tf_op jit(solution)/shard_map/pallas_call | solution.py:69
  33.6 3.1 %collective-permute-start.2 = (bf16[128,4224]{1,0:T(8,128)(2,1)}, bf16[128,4224]{1,0:T(8,128)(2,1)S(1)}, u32[]{:S(2)}, u32[]{:S(2)}) collective-permute-start(bf16[128,4224]{1,0:T(8,128)(2,1)} %shard_map.94.refs_0_), channel_id=1, source_target_pairs={{0,8},{4,12},{8,0},{12,4},{16,24},{20,28},{24,16},{28,20},{1,9},{5... | collective-permute-start | bytes 3244040 | tf_op jit(solution)/shard_map/ppermute | solution.py:25
  36.7 1.5 %collective-permute-start.1 = (bf16[128,4224]{1,0:T(8,128)(2,1)}, bf16[128,4224]{1,0:T(8,128)(2,1)S(1)}, u32[]{:S(2)}, u32[]{:S(2)}) collective-permute-start(bf16[128,4224]{1,0:T(8,128)(2,1)} %shard_map.94.refs_0_), channel_id=1, source_target_pairs={{0,2},{1,3},{2,0},{3,1},{4,6},{5,7},{6,4},{7,5},{8,10},{9,11},{10,... | collective-permute-start | bytes 3244040 | tf_op jit(solution)/shard_map/ppermute | solution.py:25
  38.2 1.8 %dynamic-slice_bitcast_fusion.4 = (bf16[1,1,64,2048]{3,2,1,0:T(8,128)(2,1)S(1)}, bf16[1,1,64,2048]{3,2,1,0:T(8,128)(2,1)S(1)}, bf16[1,1,64,2048]{3,2,1,0:T(8,128...) fusion(bf16[1,2,2,2,64,2048]{5,4,3,2,1,0:T(8,128)(2,1)} %bitcas, ...), kind=kLoop, calls=%fused_computation.40 | loop fusion | bytes 4194328 | tf_op jit(solution)/shard_map/stack | solution.py:225
  40.1 1.6 %collective-permute-start.3 = (bf16[1,2,64,2048]{3,2,1,0:T(8,128)(2,1)S(1)}, bf16[1,2,64,2048]{3,2,1,0:T(8,128)(2,1)S(1)}, u32[]{:S(2)}, u32[]{:S(2)}) collective-permute-start(bf16[1,2,64,2048]{3,2,1,0:T(8,128)(2,1)S(1)} %pad_maximum_fusion), channel_id=1, source_target_pairs={{0,4},{4,0},{8,12},{12,8},{16,20},{20,16},{24,28},{28,24},{1,5},{5... | collective-permute-start | bytes 1572872 | tf_op jit(solution)/shard_map/ppermute | solution.py:25
  41.7 12.8 %collective-permute-done.3 = bf16[1,2,64,2048]{3,2,1,0:T(8,128)(2,1)S(1)} collective-permute-done((bf16[1,2,64,2048]{3,2,1,0:T(8,128)(2,1)S(1)}, bf16[1,2,64,2048]{3,2,1,0:T(8,128)(2,1)S(1)}, u32[]{:S(2)}, u32[]{:S(2)}) %collective-permute-start.3) | collective-permute-done | bytes 524320 | tf_op jit(solution)/shard_map/ppermute | solution.py:25
  54.7 2.5 %shard_map.95 = (bf16[256,1024]{1,0:T(8,128)(2,1)S(1)}, bf16[256,256]{1,0:T(8,128)(2,1)S(1)}, bf16[256,2048]{1,0:T(8,128)(2,1)S(1)}, bf16[128,1024]{1,0:T(8,128)(2,1)S(1)}, bf16[128,1024]{1,0:T(8,128)(2,1)S(1)}) custom-call(s32[2]{0:T(128)S(1)} %pad_add_fusion.place, bf16[128,4224]{1,0:T(8,128)(2,1)S(1)} %copy-done.2, ...), custom_call_target="tpu_custom_call" | custom-call | tf_op jit(solution)/shard_map/pallas_call | solution.py:139
  57.2 3.6 %collective-permute-done.2.refs_1_ = bf16[128,4224]{1,0:T(8,128)(2,1)S(1)} collective-permute-done((bf16[128,4224]{1,0:T(8,128)(2,1)}, bf16[128,4224]{1,0:T(8,128)(2,1)S(1)}, u32[]{:S(2)}, u32[]{:S(2)}) %collective-permute-start.2) | collective-permute-done | bytes 1081376 | tf_op jit(solution)/shard_map/ppermute | solution.py:25
  60.8 1.5 %collective-permute-done.1.refs_0_ = bf16[128,4224]{1,0:T(8,128)(2,1)S(1)} collective-permute-done((bf16[128,4224]{1,0:T(8,128)(2,1)}, bf16[128,4224]{1,0:T(8,128)(2,1)S(1)}, u32[]{:S(2)}, u32[]{:S(2)}) %collective-permute-start.1) | collective-permute-done | bytes 1081376 | tf_op jit(solution)/shard_map/ppermute | solution.py:25
  62.9 1.6 %collective-permute-start.7 = (bf16[64,4224]{1,0:T(8,128)(2,1)S(1)}, bf16[64,4224]{1,0:T(8,128)(2,1)S(1)}, u32[]{:S(2)}, u32[]{:S(2)}) collective-permute-start(bf16[64,4224]{1,0:T(8,128)(2,1)S(1)} %slice.28), channel_id=1, source_target_pairs={{0,2},{1,3},{2,0},{3,1},{4,6},{5,7},{6,4},{7,5},{8,10},{9,11},{10,... | collective-permute-start | bytes 1622024 | tf_op jit(solution)/shard_map/ppermute | solution.py:25
  64.9 1.5 %collective-permute-start.8 = (bf16[1,2,64,2048]{3,2,1,0:T(8,128)(2,1)S(1)}, bf16[1,2,64,2048]{3,2,1,0:T(8,128)(2,1)S(1)}, u32[]{:S(2)}, u32[]{:S(2)}) collective-permute-start(bf16[1,2,64,2048]{3,2,1,0:T(8,128)(2,1)S(1)} %get-tuple-element.73), channel_id=1, source_target_pairs={{0,4},{4,0},{8,12},{12,8},{16,20},{20,16},{24,28},{28,24},{1,5},{5... | collective-permute-start | bytes 1572872 | tf_op jit(solution)/shard_map/ppermute | solution.py:25
  66.4 2.5 %shard_map.97 = (bf16[256,1024]{1,0:T(8,128)(2,1)S(1)}, bf16[256,256]{1,0:T(8,128)(2,1)S(1)}, bf16[256,2048]{1,0:T(8,128)(2,1)S(1)}, bf16[128,1024]{1,0:T(8,128)(2,1)S(1)}, bf16[128,1024]{1,0:T(8,128)(2,1)S(1)}) custom-call(s32[2]{0:T(128)S(1)} %pad_add_fusion.place, bf16[128,4224]{1,0:T(8,128)(2,1)S(1)} %get-tuple-element.55.refs_0_, ...), custom_call_target="tpu_custom_call" | custom-call | tf_op jit(solution)/shard_map/pallas_call | solution.py:139
  68.9 2.5 %shard_map.98 = (bf16[256,1024]{1,0:T(8,128)(2,1)S(1)}, bf16[256,256]{1,0:T(8,128)(2,1)S(1)}, bf16[256,2048]{1,0:T(8,128)(2,1)S(1)}, bf16[128,1024]{1,0:T(8,128)(2,1)S(1)}, bf16[128,1024]{1,0:T(8,128)(2,1)S(1)}) custom-call(s32[2]{0:T(128)S(1)} %pad_add_fusion.place, bf16[128,4224]{1,0:T(8,128)(2,1)S(1)} %get-tuple-element.64.refs_0_, ...), custom_call_target="tpu_custom_call" | custom-call | tf_op jit(solution)/shard_map/pallas_call | solution.py:139
  71.4 2.7 %shard_map.99 = (f32[1024,1024]{1,0:T(8,128)S(1)}, f32[256,2048]{1,0:T(8,128)S(1)}, bf16[256,1024]{1,0:T(8,128)(2,1)S(1)}, f32[8,128]{1,0:T(8,128)S(1)}) custom-call(bf16[256,1024]{1,0:T(8,128)(2,1)S(1)} %get-tuple-element.57.refs_0_, bf16[256,256]{1,0:T(8,128)(2,1)S(1)} %get-tuple-element.54.refs_4_.refs_1_, ...), custom_call_target="tpu_custom_call" | custom-call | tf_op jit(solution)/shard_map/pallas_call | solution.py:183
  74.1 4.0 %collective-permute-done.8.refs_3_ = bf16[1,2,64,2048]{3,2,1,0:T(8,128)(2,1)S(1)} collective-permute-done((bf16[1,2,64,2048]{3,2,1,0:T(8,128)(2,1)S(1)}, bf16[1,2,64,2048]{3,2,1,0:T(8,128)(2,1)S(1)}, u32[]{:S(2)}, u32[]{:S(2)}) %collective-permute-start.8) | collective-permute-done | bytes 524320 | tf_op jit(solution)/shard_map/ppermute | solution.py:25
  78.8 1.5 %collective-permute-start.19 = (bf16[1,2,64,2048]{3,2,1,0:T(8,128)(2,1)S(1)}, bf16[1,2,64,2048]{3,2,1,0:T(8,128)(2,1)S(1)}, u32[]{:S(2)}, u32[]{:S(2)}) collective-permute-start(bf16[1,2,64,2048]{3,2,1,0:T(8,128)(2,1)S(1)} %get-tuple-element.84), channel_id=1, source_target_pairs={{0,8},{4,12},{8,0},{12,4},{16,24},{20,28},{24,16},{28,20},{1,9},{5... | collective-permute-start | bytes 1572872 | tf_op jit(solution)/shard_map/ppermute | solution.py:25
  81.0 2.5 %shard_map.101 = (bf16[256,1024]{1,0:T(8,128)(2,1)S(1)}, bf16[256,256]{1,0:T(8,128)(2,1)S(1)}, bf16[256,2048]{1,0:T(8,128)(2,1)S(1)}, bf16[128,1024]{1,0:T(8,128)(2,1)S(1)}, bf16[128,1024]{1,0:T(8,128)(2,1)S(1)}) custom-call(s32[2]{0:T(128)S(1)} %pad_add_fusion.place, bf16[64,4224]{1,0:T(8,128)(2,1)S(1)} %get-tuple-element.75.refs_0_, ...), custom_call_target="tpu_custom_call" | custom-call | tf_op jit(solution)/shard_map/pallas_call | solution.py:139
  84.3 1.3 %add_convert_fusion = bf16[1024,1024]{1,0:T(8,128)(2,1)S(1)} fusion(f32[1024,1024]{1,0:T(8,128)S(1)} %get-tuple-element.71, f32[1024,1024]{1,0:T(8,128)S(1)} %fusion.14), kind=kLoop, calls=%fused_computation | loop fusion | flops 2097152 | bytes 10485760 | tf_op jit(solution)/shard_map/convert_element_type | solution.py:21
  85.8 1.6 %collective-permute-start.15 = (bf16[1,96,1024]{2,1,0:T(8,128)(2,1)S(1)}, bf16[1,96,1024]{2,1,0:T(8,128)(2,1)S(1)}, u32[]{:S(2)}, u32[]{:S(2)}) collective-permute-start(bf16[1,96,1024]{2,1,0:T(8,128)(2,1)S(1)} %dynamic-slice_bitcast_fusion.12.refs_1_), channel_id=1, source_target_pairs={{0,4},{4,0},{8,12},{12,8},{16,20},{20,16},{24,28},{28,24},{1,5},{5... | collective-permute-start | bytes 589832 | tf_op jit(solution)/shard_map/ppermute | solution.py:25
  87.4 1.3 convolution_convert_fusion
  90.3 3.4 %collective-permute-done.15.refs_2_ = bf16[1,96,1024]{2,1,0:T(8,128)(2,1)S(1)} collective-permute-done((bf16[1,96,1024]{2,1,0:T(8,128)(2,1)S(1)}, bf16[1,96,1024]{2,1,0:T(8,128)(2,1)S(1)}, u32[]{:S(2)}, u32[]{:S(2)}) %collective-permute-start.15) | collective-permute-done | bytes 196640 | tf_op jit(solution)/shard_map/ppermute | solution.py:25
  93.7 2.6 %collective-permute-start.16 = (bf16[1,96,1024]{2,1,0:T(8,128)(2,1)S(1)}, bf16[1,96,1024]{2,1,0:T(8,128)(2,1)S(1)}, u32[]{:S(2)}, u32[]{:S(2)}) collective-permute-start(bf16[1,96,1024]{2,1,0:T(8,128)(2,1)S(1)} %fusion.18), channel_id=1, source_target_pairs={{0,16},{4,20},{8,24},{12,28},{16,0},{20,4},{24,8},{28,12},{1,17},{... | collective-permute-start | bytes 589832 | tf_op jit(solution)/shard_map/ppermute | solution.py:25
  96.4 1.5 %collective-permute-start.20 = (bf16[1,64,2048]{2,1,0:T(8,128)(2,1)S(1)}, bf16[1,64,2048]{2,1,0:T(8,128)(2,1)S(1)}, u32[]{:S(2)}, u32[]{:S(2)}) collective-permute-start(bf16[1,64,2048]{2,1,0:T(8,128)(2,1)S(1)} %get-tuple-element.86), channel_id=1, source_target_pairs={{0,4},{4,0},{8,12},{12,8},{16,20},{20,16},{24,28},{28,24},{1,5},{5... | collective-permute-start | bytes 786440 | tf_op jit(solution)/shard_map/ppermute | solution.py:25
  98.1 1.3 fusion.1
  100.8 2.6 %collective-permute-start.17 = (bf16[1,160,1024]{2,1,0:T(8,128)(2,1)S(1)}, bf16[1,160,1024]{2,1,0:T(8,128)(2,1)S(1)}, u32[]{:S(2)}, u32[]{:S(2)}) collective-permute-start(bf16[1,160,1024]{2,1,0:T(8,128)(2,1)S(1)} %fusion.5), channel_id=1, source_target_pairs={{0,16},{4,20},{8,24},{12,28},{16,0},{20,4},{24,8},{28,12},{1,17},{... | collective-permute-start | bytes 983048 | tf_op jit(solution)/shard_map/ppermute | solution.py:25
  103.4 1.5 %collective-permute-start.14 = (bf16[1,256,1024]{2,1,0:T(8,128)(2,1)S(1)}, bf16[1,256,1024]{2,1,0:T(8,128)(2,1)S(1)}, u32[]{:S(2)}, u32[]{:S(2)}) collective-permute-start(bf16[1,256,1024]{2,1,0:T(8,128)(2,1)S(1)} %shard_map.103), channel_id=1, source_target_pairs={{0,4},{4,0},{8,12},{12,8},{16,20},{20,16},{24,28},{28,24},{1,5},{5... | collective-permute-start | bytes 1572872 | tf_op jit(solution)/shard_map/ppermute | solution.py:25
  105.0 1.3 %collective-permute-done.20 = bf16[1,64,2048]{2,1,0:T(8,128)(2,1)S(1)} collective-permute-done((bf16[1,64,2048]{2,1,0:T(8,128)(2,1)S(1)}, bf16[1,64,2048]{2,1,0:T(8,128)(2,1)S(1)}, u32[]{:S(2)}, u32[]{:S(2)}) %collective-permute-start.20) | collective-permute-done | bytes 262176 | tf_op jit(solution)/shard_map/ppermute | solution.py:25
  106.4 2.6 %collective-permute-start.21 = (bf16[1,64,2048]{2,1,0:T(8,128)(2,1)S(1)}, bf16[1,64,2048]{2,1,0:T(8,128)(2,1)S(1)}, u32[]{:S(2)}, u32[]{:S(2)}) collective-permute-start(bf16[1,64,2048]{2,1,0:T(8,128)(2,1)S(1)} %fusion.7), channel_id=1, source_target_pairs={{0,16},{4,20},{8,24},{12,28},{16,0},{20,4},{24,8},{28,12},{1,17},{... | collective-permute-start | bytes 786440 | tf_op jit(solution)/shard_map/ppermute | solution.py:25
  109.1 2.2 %collective-permute-done.12.refs_1_ = bf16[128,2048]{1,0:T(8,128)(2,1)S(1)} collective-permute-done((bf16[128,2048]{1,0:T(8,128)(2,1)S(1)}, bf16[128,2048]{1,0:T(8,128)(2,1)S(1)}, u32[]{:S(2)}, u32[]{:S(2)}) %collective-permute-start.12) | collective-permute-done | bytes 524320 | tf_op jit(solution)/shard_map/ppermute | solution.py:25
  112.7 12.2 %collective-permute-done.17.refs_0_ = bf16[1,160,1024]{2,1,0:T(8,128)(2,1)S(1)} collective-permute-done((bf16[1,160,1024]{2,1,0:T(8,128)(2,1)S(1)}, bf16[1,160,1024]{2,1,0:T(8,128)(2,1)S(1)}, u32[]{:S(2)}, u32[]{:S(2)}) %collective-permute-start.17) | collective-permute-done | bytes 327712 | tf_op jit(solution)/shard_map/ppermute | solution.py:25
  124.9 1.2 fusion.4
  126.1 3.3 %collective-permute-done.21 = bf16[1,64,2048]{2,1,0:T(8,128)(2,1)S(1)} collective-permute-done((bf16[1,64,2048]{2,1,0:T(8,128)(2,1)S(1)}, bf16[1,64,2048]{2,1,0:T(8,128)(2,1)S(1)}, u32[]{:S(2)}, u32[]{:S(2)}) %collective-permute-start.21) | collective-permute-done | bytes 262176 | tf_op jit(solution)/shard_map/ppermute | solution.py:25
  (58 shorter events, 9.3 us)
Async XLA Ops:
  33.6 27.2 %collective-permute-start.2 = (bf16[128,4224]{1,0:T(8,128)(2,1)}, bf16[128,4224]{1,0:T(8,128)(2,1)S(1)}, u32[]{:S(2)}, u32[]{:S(2)}) collective-permute-start(bf16[128,4224]{1,0:T(8,128)(2,1)} %shard_map.94.refs_0_), channel_id=1, source_target_pairs={{0,8},{4,12},{8,0},{12,4},{16,24},{20,28},{24,16},{28,20},{1,9},{5... | collective-permute-start | bytes 3244040 | tf_op jit(solution)/shard_map/ppermute | solution.py:25
  36.7 25.5 %collective-permute-start.1 = (bf16[128,4224]{1,0:T(8,128)(2,1)}, bf16[128,4224]{1,0:T(8,128)(2,1)S(1)}, u32[]{:S(2)}, u32[]{:S(2)}) collective-permute-start(bf16[128,4224]{1,0:T(8,128)(2,1)} %shard_map.94.refs_0_), channel_id=1, source_target_pairs={{0,2},{1,3},{2,0},{3,1},{4,6},{5,7},{6,4},{7,5},{8,10},{9,11},{10,... | collective-permute-start | bytes 3244040 | tf_op jit(solution)/shard_map/ppermute | solution.py:25
  38.2 16.4 %collective-permute-start = (bf16[128,4224]{1,0:T(8,128)(2,1)}, bf16[128,4224]{1,0:T(8,128)(2,1)S(1)}, u32[]{:S(2)}, u32[]{:S(2)}) collective-permute-start(bf16[128,4224]{1,0:T(8,128)(2,1)} %shard_map.94.refs_0_), channel_id=1, source_target_pairs={{0,1},{1,0},{2,3},{3,2},{4,5},{5,4},{6,7},{7,6},{8,9},{9,8},{10,11... | collective-permute-start | bytes 3244040 | tf_op jit(solution)/shard_map/ppermute | solution.py:25
  38.2 16.4 %copy-start = (bf16[1,2048,1024]{2,1,0:T(8,128)(2,1)S(1)}, bf16[1,2048,1024]{2,1,0:T(8,128)(2,1)}, u32[]{:S(2)}) copy-start(bf16[1,2048,1024]{2,1,0:T(8,128)(2,1)} %param.11) | copy-start | bytes 12582916
  40.0 14.6 %copy-start.1 = (bf16[1,512,2048]{2,1,0:T(8,128)(2,1)S(1)}, bf16[1,512,2048]{2,1,0:T(8,128)(2,1)}, u32[]{:S(2)}) copy-start(bf16[1,512,2048]{2,1,0:T(8,128)(2,1)} %param.12) | copy-start | bytes 6291460
  40.0 14.6 %copy-start.2 = (bf16[128,4224]{1,0:T(8,128)(2,1)S(1)}, bf16[128,4224]{1,0:T(8,128)(2,1)}, u32[]{:S(2)}) copy-start(bf16[128,4224]{1,0:T(8,128)(2,1)} %shard_map.94.refs_0_) | copy-start | bytes 3244036
  40.1 14.4 %collective-permute-start.3 = (bf16[1,2,64,2048]{3,2,1,0:T(8,128)(2,1)S(1)}, bf16[1,2,64,2048]{3,2,1,0:T(8,128)(2,1)S(1)}, u32[]{:S(2)}, u32[]{:S(2)}) collective-permute-start(bf16[1,2,64,2048]{3,2,1,0:T(8,128)(2,1)S(1)} %pad_maximum_fusion), channel_id=1, source_target_pairs={{0,4},{4,0},{8,12},{12,8},{16,20},{20,16},{24,28},{28,24},{1,5},{5... | collective-permute-start | bytes 1572872 | tf_op jit(solution)/shard_map/ppermute | solution.py:25
  62.3 4.1 %collective-permute-start.4 = (bf16[128,4224]{1,0:T(8,128)(2,1)S(1)}, bf16[128,4224]{1,0:T(8,128)(2,1)S(1)}, u32[]{:S(2)}, u32[]{:S(2)}) collective-permute-start(bf16[128,4224]{1,0:T(8,128)(2,1)S(1)} %get-tuple-element.55.refs_0_), channel_id=1, source_target_pairs={{0,1},{1,0},{2,3},{3,2},{4,5},{5,4},{6,7},{7,6},{8,9},{9,8},{10,11... | collective-permute-start | bytes 3244040 | tf_op jit(solution)/shard_map/ppermute | solution.py:25
  62.3 6.6 %collective-permute-start.5 = (bf16[128,4224]{1,0:T(8,128)(2,1)S(1)}, bf16[128,4224]{1,0:T(8,128)(2,1)S(1)}, u32[]{:S(2)}, u32[]{:S(2)}) collective-permute-start(bf16[128,4224]{1,0:T(8,128)(2,1)S(1)} %get-tuple-element.64.refs_0_), channel_id=1, source_target_pairs={{0,1},{1,0},{2,3},{3,2},{4,5},{5,4},{6,7},{7,6},{8,9},{9,8},{10,11... | collective-permute-start | bytes 3244040 | tf_op jit(solution)/shard_map/ppermute | solution.py:25
  62.9 15.3 %collective-permute-start.7 = (bf16[64,4224]{1,0:T(8,128)(2,1)S(1)}, bf16[64,4224]{1,0:T(8,128)(2,1)S(1)}, u32[]{:S(2)}, u32[]{:S(2)}) collective-permute-start(bf16[64,4224]{1,0:T(8,128)(2,1)S(1)} %slice.28), channel_id=1, source_target_pairs={{0,2},{1,3},{2,0},{3,1},{4,6},{5,7},{6,4},{7,5},{8,10},{9,11},{10,... | collective-permute-start | bytes 1622024 | tf_op jit(solution)/shard_map/ppermute | solution.py:25
  64.4 13.9 %collective-permute-start.6 = (bf16[64,4224]{1,0:T(8,128)(2,1)S(1)}, bf16[64,4224]{1,0:T(8,128)(2,1)S(1)}, u32[]{:S(2)}, u32[]{:S(2)}) collective-permute-start(bf16[64,4224]{1,0:T(8,128)(2,1)S(1)} %slice.27), channel_id=1, source_target_pairs={{0,8},{4,12},{8,0},{12,4},{16,24},{20,28},{24,16},{28,20},{1,9},{5... | collective-permute-start | bytes 1622024 | tf_op jit(solution)/shard_map/ppermute | solution.py:25
  64.9 13.3 %collective-permute-start.8 = (bf16[1,2,64,2048]{3,2,1,0:T(8,128)(2,1)S(1)}, bf16[1,2,64,2048]{3,2,1,0:T(8,128)(2,1)S(1)}, u32[]{:S(2)}, u32[]{:S(2)}) collective-permute-start(bf16[1,2,64,2048]{3,2,1,0:T(8,128)(2,1)S(1)} %get-tuple-element.73), channel_id=1, source_target_pairs={{0,4},{4,0},{8,12},{12,8},{16,20},{20,16},{24,28},{28,24},{1,5},{5... | collective-permute-start | bytes 1572872 | tf_op jit(solution)/shard_map/ppermute | solution.py:25
  78.3 2.0 %collective-permute-start.9 = (bf16[64,4224]{1,0:T(8,128)(2,1)S(1)}, bf16[64,4224]{1,0:T(8,128)(2,1)S(1)}, u32[]{:S(2)}, u32[]{:S(2)}) collective-permute-start(bf16[64,4224]{1,0:T(8,128)(2,1)S(1)} %get-tuple-element.75.refs_0_), channel_id=1, source_target_pairs={{0,1},{1,0},{2,3},{3,2},{4,5},{5,4},{6,7},{7,6},{8,9},{9,8},{10,11... | collective-permute-start | bytes 1622024 | tf_op jit(solution)/shard_map/ppermute | solution.py:25
  78.3 2.7 %collective-permute-start.10 = (bf16[64,4224]{1,0:T(8,128)(2,1)S(1)}, bf16[64,4224]{1,0:T(8,128)(2,1)S(1)}, u32[]{:S(2)}, u32[]{:S(2)}) collective-permute-start(bf16[64,4224]{1,0:T(8,128)(2,1)S(1)} %get-tuple-element.76.refs_1_), channel_id=1, source_target_pairs={{0,1},{1,0},{2,3},{3,2},{4,5},{5,4},{6,7},{7,6},{8,9},{9,8},{10,11... | collective-permute-start | bytes 1622024 | tf_op jit(solution)/shard_map/ppermute | solution.py:25
  78.8 17.6 %collective-permute-start.19 = (bf16[1,2,64,2048]{3,2,1,0:T(8,128)(2,1)S(1)}, bf16[1,2,64,2048]{3,2,1,0:T(8,128)(2,1)S(1)}, u32[]{:S(2)}, u32[]{:S(2)}) collective-permute-start(bf16[1,2,64,2048]{3,2,1,0:T(8,128)(2,1)S(1)} %get-tuple-element.84), channel_id=1, source_target_pairs={{0,8},{4,12},{8,0},{12,4},{16,24},{20,28},{24,16},{28,20},{1,9},{5... | collective-permute-start | bytes 1572872 | tf_op jit(solution)/shard_map/ppermute | solution.py:25
  85.8 7.8 %collective-permute-start.15 = (bf16[1,96,1024]{2,1,0:T(8,128)(2,1)S(1)}, bf16[1,96,1024]{2,1,0:T(8,128)(2,1)S(1)}, u32[]{:S(2)}, u32[]{:S(2)}) collective-permute-start(bf16[1,96,1024]{2,1,0:T(8,128)(2,1)S(1)} %dynamic-slice_bitcast_fusion.12.refs_1_), channel_id=1, source_target_pairs={{0,4},{4,0},{8,12},{12,8},{16,20},{20,16},{24,28},{28,24},{1,5},{5... | collective-permute-start | bytes 589832 | tf_op jit(solution)/shard_map/ppermute | solution.py:25
  88.7 9.4 %collective-permute-start.11 = (bf16[256,2048]{1,0:T(8,128)(2,1)S(1)}, bf16[256,2048]{1,0:T(8,128)(2,1)S(1)}, u32[]{:S(2)}, u32[]{:S(2)}) collective-permute-start(bf16[256,2048]{1,0:T(8,128)(2,1)S(1)} %convolution_convert_fusion), channel_id=1, source_target_pairs={{0,1},{1,0},{2,3},{3,2},{4,5},{5,4},{6,7},{7,6},{8,9},{9,8},{10,11... | collective-permute-start | bytes 3145736 | tf_op jit(solution)/shard_map/ppermute | solution.py:25
  88.8 11.9 %collective-permute-start.13 = (bf16[1,160,1024]{2,1,0:T(8,128)(2,1)S(1)}, bf16[1,160,1024]{2,1,0:T(8,128)(2,1)S(1)}, u32[]{:S(2)}, u32[]{:S(2)}) collective-permute-start(bf16[1,160,1024]{2,1,0:T(8,128)(2,1)S(1)} %dynamic-slice_bitcast_fusion.1), channel_id=1, source_target_pairs={{0,4},{4,0},{8,12},{12,8},{16,20},{20,16},{24,28},{28,24},{1,5},{5... | collective-permute-start | bytes 983048 | tf_op jit(solution)/shard_map/ppermute | solution.py:25
  93.7 31.2 %collective-permute-start.16 = (bf16[1,96,1024]{2,1,0:T(8,128)(2,1)S(1)}, bf16[1,96,1024]{2,1,0:T(8,128)(2,1)S(1)}, u32[]{:S(2)}, u32[]{:S(2)}) collective-permute-start(bf16[1,96,1024]{2,1,0:T(8,128)(2,1)S(1)} %fusion.18), channel_id=1, source_target_pairs={{0,16},{4,20},{8,24},{12,28},{16,0},{20,4},{24,8},{28,12},{1,17},{... | collective-permute-start | bytes 589832 | tf_op jit(solution)/shard_map/ppermute | solution.py:25
  96.4 9.9 %collective-permute-start.20 = (bf16[1,64,2048]{2,1,0:T(8,128)(2,1)S(1)}, bf16[1,64,2048]{2,1,0:T(8,128)(2,1)S(1)}, u32[]{:S(2)}, u32[]{:S(2)}) collective-permute-start(bf16[1,64,2048]{2,1,0:T(8,128)(2,1)S(1)} %get-tuple-element.86), channel_id=1, source_target_pairs={{0,4},{4,0},{8,12},{12,8},{16,20},{20,16},{24,28},{28,24},{1,5},{5... | collective-permute-start | bytes 786440 | tf_op jit(solution)/shard_map/ppermute | solution.py:25
  99.5 11.8 %collective-permute-start.12 = (bf16[128,2048]{1,0:T(8,128)(2,1)S(1)}, bf16[128,2048]{1,0:T(8,128)(2,1)S(1)}, u32[]{:S(2)}, u32[]{:S(2)}) collective-permute-start(bf16[128,2048]{1,0:T(8,128)(2,1)S(1)} %slice.57), channel_id=1, source_target_pairs={{0,2},{1,3},{2,0},{3,1},{4,6},{5,7},{6,4},{7,5},{8,10},{9,11},{10,... | collective-permute-start | bytes 1572872 | tf_op jit(solution)/shard_map/ppermute | solution.py:25
  100.8 24.1 %collective-permute-start.17 = (bf16[1,160,1024]{2,1,0:T(8,128)(2,1)S(1)}, bf16[1,160,1024]{2,1,0:T(8,128)(2,1)S(1)}, u32[]{:S(2)}, u32[]{:S(2)}) collective-permute-start(bf16[1,160,1024]{2,1,0:T(8,128)(2,1)S(1)} %fusion.5), channel_id=1, source_target_pairs={{0,16},{4,20},{8,24},{12,28},{16,0},{20,4},{24,8},{28,12},{1,17},{... | collective-permute-start | bytes 983048 | tf_op jit(solution)/shard_map/ppermute | solution.py:25
  103.4 21.5 %collective-permute-start.14 = (bf16[1,256,1024]{2,1,0:T(8,128)(2,1)S(1)}, bf16[1,256,1024]{2,1,0:T(8,128)(2,1)S(1)}, u32[]{:S(2)}, u32[]{:S(2)}) collective-permute-start(bf16[1,256,1024]{2,1,0:T(8,128)(2,1)S(1)} %shard_map.103), channel_id=1, source_target_pairs={{0,4},{4,0},{8,12},{12,8},{16,20},{20,16},{24,28},{28,24},{1,5},{5... | collective-permute-start | bytes 1572872 | tf_op jit(solution)/shard_map/ppermute | solution.py:25
  106.4 23.1 %collective-permute-start.21 = (bf16[1,64,2048]{2,1,0:T(8,128)(2,1)S(1)}, bf16[1,64,2048]{2,1,0:T(8,128)(2,1)S(1)}, u32[]{:S(2)}, u32[]{:S(2)}) collective-permute-start(bf16[1,64,2048]{2,1,0:T(8,128)(2,1)S(1)} %fusion.7), channel_id=1, source_target_pairs={{0,16},{4,20},{8,24},{12,28},{16,0},{20,4},{24,8},{28,12},{1,17},{... | collective-permute-start | bytes 786440 | tf_op jit(solution)/shard_map/ppermute | solution.py:25
  111.3 18.2 %collective-permute-start.18 = (bf16[1,64,2048]{2,1,0:T(8,128)(2,1)S(1)}, bf16[1,64,2048]{2,1,0:T(8,128)(2,1)S(1)}, u32[]{:S(2)}, u32[]{:S(2)}) collective-permute-start(bf16[1,64,2048]{2,1,0:T(8,128)(2,1)S(1)} %shard_map.104.refs_1_), channel_id=1, source_target_pairs={{0,4},{4,0},{8,12},{12,8},{16,20},{20,16},{24,28},{28,24},{1,5},{5... | collective-permute-start | bytes 786440 | tf_op jit(solution)/shard_map/ppermute | solution.py:25

commit v14 on v13

--- a/solution.py
+++ b/solution.py
@@ -39,7 +39,7 @@
     return copies
 
 
-def pack_kernel(tokens, cotangent, ids_in, probs_in, packed, coded, ids, probs, sems):
+def pack_kernel(tokens, cotangent, ids_in, probs_in, packed, ids, probs, sems):
     width = tokens.shape[1]
     small = begin([(ids_in, ids), (probs_in, probs)], sems)
     moves = [(tokens, packed.at[:, :width]), (cotangent, packed.at[:, width : 2 * width])]
@@ -57,9 +57,8 @@
     low = (route - high) - middle
     part = lax.rem(line, 3)
     lines = jnp.where(part == 0, high, jnp.where(part == 1, middle, low))
-    coded[...] = narrow(lines.T)
-    last = begin([(coded, packed.at[:, 2 * width :])], sems.at[4:5])
-    for copy in (*large, *last):
+    packed[:, 2 * width :] = narrow(lines.T)
+    for copy in large:
         copy.wait()
 
 
@@ -70,12 +69,11 @@
         pack_kernel,
         out_shape=jax.ShapeDtypeStruct((rows, 2 * width + LANES), jnp.bfloat16),
         in_specs=[HERE] * 4,
-        out_specs=HERE,
+        out_specs=pl.BlockSpec(memory_space=pltpu.VMEM),
         scratch_shapes=[
-            pltpu.VMEM((rows, LANES), jnp.bfloat16),
             pltpu.VMEM((top, rows), jnp.int32),
             pltpu.VMEM((top, rows), jnp.float32),
-            pltpu.SemaphoreType.DMA((5,)),
+            pltpu.SemaphoreType.DMA((4,)),
         ],
         cost_estimate=FREE,
     )(tokens, cotangent, expert_ids.T, gate_probs.T)

time: 131 us -> 99.9 us (0.76)
  Pallas kernels: 45.6 us -> 15 us
    pallas_call x1, Pallas kernels: 32.9 us -> 2.25 us  [packed(): pl.pallas_call(pack_kernel, out_shape=jax.ShapeDtypeStruct((rows, 2 * wid...]
  transfers between devices with their start and end apart: 22 -> 22, of which waited for: 12 -> 12; matrix products, arithmetic and copies ran while one was open for 8% -> 10% of each run, Pallas kernels for 10% -> 13%
where the time goes in v14:
time: 99.9 us; the launch traced here: 99.7 us
  waiting for transfers between devices  45.9 us (46%)
  starting transfers between devices  26.5 us (27%)
  Pallas kernels  15 us (15%)
  other arithmetic  5.42 us (5%)
  matrix products  3.79 us (4%)
  local copies, waits for them, and re-layouts  2.25 us (2%)
    ppermute x22, waiting for transfers between devices, flip(): lax.ppermute(values, axis, [(i, i ^ bit) for i in range(lax.axis_size(axi...  45.9 us
    ppermute x22, starting transfers between devices, flip(): lax.ppermute(values, axis, [(i, i ^ bit) for i in range(lax.axis_size(axi...  26.5 us
    pallas_call x4, Pallas kernels, expert_rows(): pl.pallas_call(functools.partial(expert_kernel, group_count), out_shape=t...  9.99 us
    convert_element_type x7, other arithmetic, narrow(): return values.astype(jnp.bfloat16)  2.89 us
    pallas_call x1, Pallas kernels, early_terms(): pl.pallas_call(terms_kernel, out_shape=(jax.ShapeDtypeStruct((tok_cols.sh...  2.71 us
    dot_general x2, matrix products, input_part(): return narrow(jnp.dot(back, gate_up.T, preferred_element_type=jnp.float32))  2.58 us
    pallas_call x1, Pallas kernels, packed(): pl.pallas_call(pack_kernel, out_shape=jax.ShapeDtypeStruct((rows, 2 * wid...  2.25 us
    mul x2, other arithmetic, on_device(): grad_gate_up, grad_down = (gate_sum * factor, down_sum * factor)  2.15 us
  transfers between devices with their start and end apart: 22, of which 12 were waited for; matrix products, arithmetic and copies ran while one was open for 10% of the time, Pallas kernels for 13%

profile of v14, /device:TPU:0, one launch (start us, length us, event | category | flops | bytes accessed | tf_op | source)
XLA Modules:
  0.0 99.7 jit_solution(3590840620027838647)
XLA Ops:
  0.7 2.3 %shard_map.94.refs_0_ = bf16[128,4224]{1,0:T(8,128)(2,1)} custom-call(bf16[128,2048]{1,0:T(8,128)(2,1)} %tokens.1, bf16[128,2048]{1,0:T(8,128)(2,1)} %cotangent.1, s32[2,128]{1,0:T(2,128)} %bitcast.88, f32[2,128]{1,0:T(2,128)} %bitcast.89), custom_call_target="tpu_custom_call" | custom-call | tf_op jit(solution)/shard_map/pallas_call | solution.py:68
  3.0 3.1 %collective-permute-start.2 = (bf16[128,4224]{1,0:T(8,128)(2,1)}, bf16[128,4224]{1,0:T(8,128)(2,1)S(1)}, u32[]{:S(2)}, u32[]{:S(2)}) collective-permute-start(bf16[128,4224]{1,0:T(8,128)(2,1)} %shard_map.94.refs_0_), channel_id=1, source_target_pairs={{0,8},{4,12},{8,0},{12,4},{16,24},{20,28},{24,16},{28,20},{1,9},{5... | collective-permute-start | bytes 3244040 | tf_op jit(solution)/shard_map/ppermute | solution.py:25
  6.1 1.5 %collective-permute-start.1 = (bf16[128,4224]{1,0:T(8,128)(2,1)}, bf16[128,4224]{1,0:T(8,128)(2,1)S(1)}, u32[]{:S(2)}, u32[]{:S(2)}) collective-permute-start(bf16[128,4224]{1,0:T(8,128)(2,1)} %shard_map.94.refs_0_), channel_id=1, source_target_pairs={{0,2},{1,3},{2,0},{3,1},{4,6},{5,7},{6,4},{7,5},{8,10},{9,11},{10,... | collective-permute-start | bytes 3244040 | tf_op jit(solution)/shard_map/ppermute | solution.py:25
  7.6 1.8 %dynamic-slice_bitcast_fusion.4 = (bf16[1,1,64,2048]{3,2,1,0:T(8,128)(2,1)S(1)}, bf16[1,1,64,2048]{3,2,1,0:T(8,128)(2,1)S(1)}, bf16[1,1,64,2048]{3,2,1,0:T(8,128...) fusion(bf16[1,2,2,2,64,2048]{5,4,3,2,1,0:T(8,128)(2,1)} %bitcas, ...), kind=kLoop, calls=%fused_computation.40 | loop fusion | bytes 4194328 | tf_op jit(solution)/shard_map/stack | solution.py:223
  9.5 1.6 %collective-permute-start.3 = (bf16[1,2,64,2048]{3,2,1,0:T(8,128)(2,1)S(1)}, bf16[1,2,64,2048]{3,2,1,0:T(8,128)(2,1)S(1)}, u32[]{:S(2)}, u32[]{:S(2)}) collective-permute-start(bf16[1,2,64,2048]{3,2,1,0:T(8,128)(2,1)S(1)} %pad_maximum_fusion), channel_id=1, source_target_pairs={{0,4},{4,0},{8,12},{12,8},{16,20},{20,16},{24,28},{28,24},{1,5},{5... | collective-permute-start | bytes 1572872 | tf_op jit(solution)/shard_map/ppermute | solution.py:25
  11.1 12.8 %collective-permute-done.3 = bf16[1,2,64,2048]{3,2,1,0:T(8,128)(2,1)S(1)} collective-permute-done((bf16[1,2,64,2048]{3,2,1,0:T(8,128)(2,1)S(1)}, bf16[1,2,64,2048]{3,2,1,0:T(8,128)(2,1)S(1)}, u32[]{:S(2)}, u32[]{:S(2)}) %collective-permute-start.3) | collective-permute-done | bytes 524320 | tf_op jit(solution)/shard_map/ppermute | solution.py:25
  24.0 2.5 %shard_map.95 = (bf16[256,1024]{1,0:T(8,128)(2,1)S(1)}, bf16[256,256]{1,0:T(8,128)(2,1)S(1)}, bf16[256,2048]{1,0:T(8,128)(2,1)S(1)}, bf16[128,1024]{1,0:T(8,128)(2,1)S(1)}, bf16[128,1024]{1,0:T(8,128)(2,1)S(1)}) custom-call(s32[2]{0:T(128)S(1)} %pad_add_fusion.place, bf16[128,4224]{1,0:T(8,128)(2,1)S(1)} %copy-done.2, ...), custom_call_target="tpu_custom_call" | custom-call | tf_op jit(solution)/shard_map/pallas_call | solution.py:137
  26.5 3.6 %collective-permute-done.2.refs_1_ = bf16[128,4224]{1,0:T(8,128)(2,1)S(1)} collective-permute-done((bf16[128,4224]{1,0:T(8,128)(2,1)}, bf16[128,4224]{1,0:T(8,128)(2,1)S(1)}, u32[]{:S(2)}, u32[]{:S(2)}) %collective-permute-start.2) | collective-permute-done | bytes 1081376 | tf_op jit(solution)/shard_map/ppermute | solution.py:25
  30.1 1.5 %collective-permute-done.1.refs_0_ = bf16[128,4224]{1,0:T(8,128)(2,1)S(1)} collective-permute-done((bf16[128,4224]{1,0:T(8,128)(2,1)}, bf16[128,4224]{1,0:T(8,128)(2,1)S(1)}, u32[]{:S(2)}, u32[]{:S(2)}) %collective-permute-start.1) | collective-permute-done | bytes 1081376 | tf_op jit(solution)/shard_map/ppermute | solution.py:25
  32.2 1.6 %collective-permute-start.7 = (bf16[64,4224]{1,0:T(8,128)(2,1)S(1)}, bf16[64,4224]{1,0:T(8,128)(2,1)S(1)}, u32[]{:S(2)}, u32[]{:S(2)}) collective-permute-start(bf16[64,4224]{1,0:T(8,128)(2,1)S(1)} %slice.28), channel_id=1, source_target_pairs={{0,2},{1,3},{2,0},{3,1},{4,6},{5,7},{6,4},{7,5},{8,10},{9,11},{10,... | collective-permute-start | bytes 1622024 | tf_op jit(solution)/shard_map/ppermute | solution.py:25
  34.2 1.5 %collective-permute-start.8 = (bf16[1,2,64,2048]{3,2,1,0:T(8,128)(2,1)S(1)}, bf16[1,2,64,2048]{3,2,1,0:T(8,128)(2,1)S(1)}, u32[]{:S(2)}, u32[]{:S(2)}) collective-permute-start(bf16[1,2,64,2048]{3,2,1,0:T(8,128)(2,1)S(1)} %get-tuple-element.73), channel_id=1, source_target_pairs={{0,4},{4,0},{8,12},{12,8},{16,20},{20,16},{24,28},{28,24},{1,5},{5... | collective-permute-start | bytes 1572872 | tf_op jit(solution)/shard_map/ppermute | solution.py:25
  35.7 2.5 %shard_map.97 = (bf16[256,1024]{1,0:T(8,128)(2,1)S(1)}, bf16[256,256]{1,0:T(8,128)(2,1)S(1)}, bf16[256,2048]{1,0:T(8,128)(2,1)S(1)}, bf16[128,1024]{1,0:T(8,128)(2,1)S(1)}, bf16[128,1024]{1,0:T(8,128)(2,1)S(1)}) custom-call(s32[2]{0:T(128)S(1)} %pad_add_fusion.place, bf16[128,4224]{1,0:T(8,128)(2,1)S(1)} %get-tuple-element.55.refs_0_, ...), custom_call_target="tpu_custom_call" | custom-call | tf_op jit(solution)/shard_map/pallas_call | solution.py:137
  38.2 2.5 %shard_map.98 = (bf16[256,1024]{1,0:T(8,128)(2,1)S(1)}, bf16[256,256]{1,0:T(8,128)(2,1)S(1)}, bf16[256,2048]{1,0:T(8,128)(2,1)S(1)}, bf16[128,1024]{1,0:T(8,128)(2,1)S(1)}, bf16[128,1024]{1,0:T(8,128)(2,1)S(1)}) custom-call(s32[2]{0:T(128)S(1)} %pad_add_fusion.place, bf16[128,4224]{1,0:T(8,128)(2,1)S(1)} %get-tuple-element.64.refs_0_, ...), custom_call_target="tpu_custom_call" | custom-call | tf_op jit(solution)/shard_map/pallas_call | solution.py:137
  40.7 2.7 %shard_map.99 = (f32[1024,1024]{1,0:T(8,128)S(1)}, f32[256,2048]{1,0:T(8,128)S(1)}, bf16[256,1024]{1,0:T(8,128)(2,1)S(1)}, f32[8,128]{1,0:T(8,128)S(1)}) custom-call(bf16[256,1024]{1,0:T(8,128)(2,1)S(1)} %get-tuple-element.57.refs_0_, bf16[256,256]{1,0:T(8,128)(2,1)S(1)} %get-tuple-element.54.refs_4_.refs_1_, ...), custom_call_target="tpu_custom_call" | custom-call | tf_op jit(solution)/shard_map/pallas_call | solution.py:181
  43.5 4.0 %collective-permute-done.8.refs_3_ = bf16[1,2,64,2048]{3,2,1,0:T(8,128)(2,1)S(1)} collective-permute-done((bf16[1,2,64,2048]{3,2,1,0:T(8,128)(2,1)S(1)}, bf16[1,2,64,2048]{3,2,1,0:T(8,128)(2,1)S(1)}, u32[]{:S(2)}, u32[]{:S(2)}) %collective-permute-start.8) | collective-permute-done | bytes 524320 | tf_op jit(solution)/shard_map/ppermute | solution.py:25
  48.2 1.5 %collective-permute-start.19 = (bf16[1,2,64,2048]{3,2,1,0:T(8,128)(2,1)S(1)}, bf16[1,2,64,2048]{3,2,1,0:T(8,128)(2,1)S(1)}, u32[]{:S(2)}, u32[]{:S(2)}) collective-permute-start(bf16[1,2,64,2048]{3,2,1,0:T(8,128)(2,1)S(1)} %get-tuple-element.84), channel_id=1, source_target_pairs={{0,8},{4,12},{8,0},{12,4},{16,24},{20,28},{24,16},{28,20},{1,9},{5... | collective-permute-start | bytes 1572872 | tf_op jit(solution)/shard_map/ppermute | solution.py:25
  50.4 2.5 %shard_map.101 = (bf16[256,1024]{1,0:T(8,128)(2,1)S(1)}, bf16[256,256]{1,0:T(8,128)(2,1)S(1)}, bf16[256,2048]{1,0:T(8,128)(2,1)S(1)}, bf16[128,1024]{1,0:T(8,128)(2,1)S(1)}, bf16[128,1024]{1,0:T(8,128)(2,1)S(1)}) custom-call(s32[2]{0:T(128)S(1)} %pad_add_fusion.place, bf16[64,4224]{1,0:T(8,128)(2,1)S(1)} %get-tuple-element.75.refs_0_, ...), custom_call_target="tpu_custom_call" | custom-call | tf_op jit(solution)/shard_map/pallas_call | solution.py:137
  53.6 1.3 %add_convert_fusion = bf16[1024,1024]{1,0:T(8,128)(2,1)S(1)} fusion(f32[1024,1024]{1,0:T(8,128)S(1)} %get-tuple-element.71, f32[1024,1024]{1,0:T(8,128)S(1)} %fusion.14), kind=kLoop, calls=%fused_computation | loop fusion | flops 2097152 | bytes 10485760 | tf_op jit(solution)/shard_map/convert_element_type | solution.py:21
  55.2 1.6 %collective-permute-start.15 = (bf16[1,96,1024]{2,1,0:T(8,128)(2,1)S(1)}, bf16[1,96,1024]{2,1,0:T(8,128)(2,1)S(1)}, u32[]{:S(2)}, u32[]{:S(2)}) collective-permute-start(bf16[1,96,1024]{2,1,0:T(8,128)(2,1)S(1)} %dynamic-slice_bitcast_fusion.12.refs_1_), channel_id=1, source_target_pairs={{0,4},{4,0},{8,12},{12,8},{16,20},{20,16},{24,28},{28,24},{1,5},{5... | collective-permute-start | bytes 589832 | tf_op jit(solution)/shard_map/ppermute | solution.py:25
  56.8 1.3 %convolution_convert_fusion = bf16[256,2048]{1,0:T(8,128)(2,1)S(1)} fusion(bf16[256,1024]{1,0:T(8,128)(2,1)S(1)} %shard_map.102, bf16[1,2048,1024]{2,1,0:T(8,128)(2,1)S(1)} %copy-done), kind=kOutput, calls=%fused_computation.1 | convolution fusion | flops 1074266112 | bytes 5767168 | tf_op jit(solution)/shard_map/dot_general | solution.py:279
  59.6 3.4 %collective-permute-done.15.refs_2_ = bf16[1,96,1024]{2,1,0:T(8,128)(2,1)S(1)} collective-permute-done((bf16[1,96,1024]{2,1,0:T(8,128)(2,1)S(1)}, bf16[1,96,1024]{2,1,0:T(8,128)(2,1)S(1)}, u32[]{:S(2)}, u32[]{:S(2)}) %collective-permute-start.15) | collective-permute-done | bytes 196640 | tf_op jit(solution)/shard_map/ppermute | solution.py:25
  63.0 2.7 %collective-permute-start.16 = (bf16[1,96,1024]{2,1,0:T(8,128)(2,1)S(1)}, bf16[1,96,1024]{2,1,0:T(8,128)(2,1)S(1)}, u32[]{:S(2)}, u32[]{:S(2)}) collective-permute-start(bf16[1,96,1024]{2,1,0:T(8,128)(2,1)S(1)} %fusion.18), channel_id=1, source_target_pairs={{0,16},{4,20},{8,24},{12,28},{16,0},{20,4},{24,8},{28,12},{1,17},{... | collective-permute-start | bytes 589832 | tf_op jit(solution)/shard_map/ppermute | solution.py:25
  65.7 1.5 %collective-permute-start.20 = (bf16[1,64,2048]{2,1,0:T(8,128)(2,1)S(1)}, bf16[1,64,2048]{2,1,0:T(8,128)(2,1)S(1)}, u32[]{:S(2)}, u32[]{:S(2)}) collective-permute-start(bf16[1,64,2048]{2,1,0:T(8,128)(2,1)S(1)} %get-tuple-element.86), channel_id=1, source_target_pairs={{0,4},{4,0},{8,12},{12,8},{16,20},{20,16},{24,28},{28,24},{1,5},{5... | collective-permute-start | bytes 786440 | tf_op jit(solution)/shard_map/ppermute | solution.py:25
  67.5 1.3 %fusion.1 = f32[256,2048]{1,0:T(8,128)S(1)} fusion(bf16[256,2048]{1,0:T(8,128)(2,1)S(1)} %collective-permute-done.11, bf16[128,1024]{1,0:T(8,128)(2,1)S(1)} %get-tuple-element.56.refs_8_, bf16[128,1024]{1,0:T(8,128)(2,1)S(1)} %get-tuple-element.47.refs_3_, bf16[1,2048,1024]{2,1,0:T(8,128)(2,1)S(1)} %copy-done), kind=kOutput, calls=%fused_computation.4 | convolution fusion | flops 1076887552 | bytes 7864320 | tf_op jit(solution)/shard_map/dot_general | solution.py:279
  70.1 2.7 %collective-permute-start.17 = (bf16[1,160,1024]{2,1,0:T(8,128)(2,1)S(1)}, bf16[1,160,1024]{2,1,0:T(8,128)(2,1)S(1)}, u32[]{:S(2)}, u32[]{:S(2)}) collective-permute-start(bf16[1,160,1024]{2,1,0:T(8,128)(2,1)S(1)} %fusion.5), channel_id=1, source_target_pairs={{0,16},{4,20},{8,24},{12,28},{16,0},{20,4},{24,8},{28,12},{1,17},{... | collective-permute-start | bytes 983048 | tf_op jit(solution)/shard_map/ppermute | solution.py:25
  72.8 1.5 %collective-permute-start.14 = (bf16[1,256,1024]{2,1,0:T(8,128)(2,1)S(1)}, bf16[1,256,1024]{2,1,0:T(8,128)(2,1)S(1)}, u32[]{:S(2)}, u32[]{:S(2)}) collective-permute-start(bf16[1,256,1024]{2,1,0:T(8,128)(2,1)S(1)} %shard_map.103), channel_id=1, source_target_pairs={{0,4},{4,0},{8,12},{12,8},{16,20},{20,16},{24,28},{28,24},{1,5},{5... | collective-permute-start | bytes 1572872 | tf_op jit(solution)/shard_map/ppermute | solution.py:25
  74.3 1.3 %collective-permute-done.20 = bf16[1,64,2048]{2,1,0:T(8,128)(2,1)S(1)} collective-permute-done((bf16[1,64,2048]{2,1,0:T(8,128)(2,1)S(1)}, bf16[1,64,2048]{2,1,0:T(8,128)(2,1)S(1)}, u32[]{:S(2)}, u32[]{:S(2)}) %collective-permute-start.20) | collective-permute-done | bytes 262176 | tf_op jit(solution)/shard_map/ppermute | solution.py:25
  75.7 2.7 %collective-permute-start.21 = (bf16[1,64,2048]{2,1,0:T(8,128)(2,1)S(1)}, bf16[1,64,2048]{2,1,0:T(8,128)(2,1)S(1)}, u32[]{:S(2)}, u32[]{:S(2)}) collective-permute-start(bf16[1,64,2048]{2,1,0:T(8,128)(2,1)S(1)} %fusion.7), channel_id=1, source_target_pairs={{0,16},{4,20},{8,24},{12,28},{16,0},{20,4},{24,8},{28,12},{1,17},{... | collective-permute-start | bytes 786440 | tf_op jit(solution)/shard_map/ppermute | solution.py:25
  78.4 2.3 %collective-permute-done.12.refs_1_ = bf16[128,2048]{1,0:T(8,128)(2,1)S(1)} collective-permute-done((bf16[128,2048]{1,0:T(8,128)(2,1)S(1)}, bf16[128,2048]{1,0:T(8,128)(2,1)S(1)}, u32[]{:S(2)}, u32[]{:S(2)}) %collective-permute-start.12) | collective-permute-done | bytes 524320 | tf_op jit(solution)/shard_map/ppermute | solution.py:25
  82.0 12.2 %collective-permute-done.17.refs_0_ = bf16[1,160,1024]{2,1,0:T(8,128)(2,1)S(1)} collective-permute-done((bf16[1,160,1024]{2,1,0:T(8,128)(2,1)S(1)}, bf16[1,160,1024]{2,1,0:T(8,128)(2,1)S(1)}, u32[]{:S(2)}, u32[]{:S(2)}) %collective-permute-start.17) | collective-permute-done | bytes 327712 | tf_op jit(solution)/shard_map/ppermute | solution.py:25
  94.3 1.2 %fusion.4 = f32[1,256,1024]{2,1,0:T(8,128)} fusion(bf16[1,256,1024]{2,1,0:T(8,128)(2,1)S(1)} %collective-permute-done.14, bf16[1,160,1024]{2,1,0:T(8,128)(2,1)S(1)} %shard_map.105, bf16[1,96,1024]{2,1,0:T(8,128)(2,1)S(1)} %collective-permute-done.16, bf16[1,2,2,256,1024]{4,3,2,1,0:T(8,128)(2,1)S(1)} %bitcast.83, u32[]{:T(128)S(6)} %optimization_barrier.37, ...), kind=kLoop, calls=%fused_computation.11 | loop fusion | flops 2359296 | bytes 2621448 | tf_op jit(solution)/shard_map/mul | solution.py:303
  95.5 3.3 %collective-permute-done.21 = bf16[1,64,2048]{2,1,0:T(8,128)(2,1)S(1)} collective-permute-done((bf16[1,64,2048]{2,1,0:T(8,128)(2,1)S(1)}, bf16[1,64,2048]{2,1,0:T(8,128)(2,1)S(1)}, u32[]{:S(2)}, u32[]{:S(2)}) %collective-permute-start.21) | collective-permute-done | bytes 262176 | tf_op jit(solution)/shard_map/ppermute | solution.py:25
  (58 shorter events, 9.2 us)
Async XLA Ops:
  3.0 27.2 %collective-permute-start.2 = (bf16[128,4224]{1,0:T(8,128)(2,1)}, bf16[128,4224]{1,0:T(8,128)(2,1)S(1)}, u32[]{:S(2)}, u32[]{:S(2)}) collective-permute-start(bf16[128,4224]{1,0:T(8,128)(2,1)} %shard_map.94.refs_0_), channel_id=1, source_target_pairs={{0,8},{4,12},{8,0},{12,4},{16,24},{20,28},{24,16},{28,20},{1,9},{5... | collective-permute-start | bytes 3244040 | tf_op jit(solution)/shard_map/ppermute | solution.py:25
  6.1 25.5 %collective-permute-start.1 = (bf16[128,4224]{1,0:T(8,128)(2,1)}, bf16[128,4224]{1,0:T(8,128)(2,1)S(1)}, u32[]{:S(2)}, u32[]{:S(2)}) collective-permute-start(bf16[128,4224]{1,0:T(8,128)(2,1)} %shard_map.94.refs_0_), channel_id=1, source_target_pairs={{0,2},{1,3},{2,0},{3,1},{4,6},{5,7},{6,4},{7,5},{8,10},{9,11},{10,... | collective-permute-start | bytes 3244040 | tf_op jit(solution)/shard_map/ppermute | solution.py:25
  7.6 16.4 %collective-permute-start = (bf16[128,4224]{1,0:T(8,128)(2,1)}, bf16[128,4224]{1,0:T(8,128)(2,1)S(1)}, u32[]{:S(2)}, u32[]{:S(2)}) collective-permute-start(bf16[128,4224]{1,0:T(8,128)(2,1)} %shard_map.94.refs_0_), channel_id=1, source_target_pairs={{0,1},{1,0},{2,3},{3,2},{4,5},{5,4},{6,7},{7,6},{8,9},{9,8},{10,11... | collective-permute-start | bytes 3244040 | tf_op jit(solution)/shard_map/ppermute | solution.py:25
  7.6 16.4 %copy-start = (bf16[1,2048,1024]{2,1,0:T(8,128)(2,1)S(1)}, bf16[1,2048,1024]{2,1,0:T(8,128)(2,1)}, u32[]{:S(2)}) copy-start(bf16[1,2048,1024]{2,1,0:T(8,128)(2,1)} %param.11) | copy-start | bytes 12582916
  9.4 14.6 %copy-start.1 = (bf16[1,512,2048]{2,1,0:T(8,128)(2,1)S(1)}, bf16[1,512,2048]{2,1,0:T(8,128)(2,1)}, u32[]{:S(2)}) copy-start(bf16[1,512,2048]{2,1,0:T(8,128)(2,1)} %param.12) | copy-start | bytes 6291460
  9.4 14.6 %copy-start.2 = (bf16[128,4224]{1,0:T(8,128)(2,1)S(1)}, bf16[128,4224]{1,0:T(8,128)(2,1)}, u32[]{:S(2)}) copy-start(bf16[128,4224]{1,0:T(8,128)(2,1)} %shard_map.94.refs_0_) | copy-start | bytes 3244036
  9.5 14.4 %collective-permute-start.3 = (bf16[1,2,64,2048]{3,2,1,0:T(8,128)(2,1)S(1)}, bf16[1,2,64,2048]{3,2,1,0:T(8,128)(2,1)S(1)}, u32[]{:S(2)}, u32[]{:S(2)}) collective-permute-start(bf16[1,2,64,2048]{3,2,1,0:T(8,128)(2,1)S(1)} %pad_maximum_fusion), channel_id=1, source_target_pairs={{0,4},{4,0},{8,12},{12,8},{16,20},{20,16},{24,28},{28,24},{1,5},{5... | collective-permute-start | bytes 1572872 | tf_op jit(solution)/shard_map/ppermute | solution.py:25
  31.6 4.1 %collective-permute-start.4 = (bf16[128,4224]{1,0:T(8,128)(2,1)S(1)}, bf16[128,4224]{1,0:T(8,128)(2,1)S(1)}, u32[]{:S(2)}, u32[]{:S(2)}) collective-permute-start(bf16[128,4224]{1,0:T(8,128)(2,1)S(1)} %get-tuple-element.55.refs_0_), channel_id=1, source_target_pairs={{0,1},{1,0},{2,3},{3,2},{4,5},{5,4},{6,7},{7,6},{8,9},{9,8},{10,11... | collective-permute-start | bytes 3244040 | tf_op jit(solution)/shard_map/ppermute | solution.py:25
  31.6 6.6 %collective-permute-start.5 = (bf16[128,4224]{1,0:T(8,128)(2,1)S(1)}, bf16[128,4224]{1,0:T(8,128)(2,1)S(1)}, u32[]{:S(2)}, u32[]{:S(2)}) collective-permute-start(bf16[128,4224]{1,0:T(8,128)(2,1)S(1)} %get-tuple-element.64.refs_0_), channel_id=1, source_target_pairs={{0,1},{1,0},{2,3},{3,2},{4,5},{5,4},{6,7},{7,6},{8,9},{9,8},{10,11... | collective-permute-start | bytes 3244040 | tf_op jit(solution)/shard_map/ppermute | solution.py:25
  32.2 15.3 %collective-permute-start.7 = (bf16[64,4224]{1,0:T(8,128)(2,1)S(1)}, bf16[64,4224]{1,0:T(8,128)(2,1)S(1)}, u32[]{:S(2)}, u32[]{:S(2)}) collective-permute-start(bf16[64,4224]{1,0:T(8,128)(2,1)S(1)} %slice.28), channel_id=1, source_target_pairs={{0,2},{1,3},{2,0},{3,1},{4,6},{5,7},{6,4},{7,5},{8,10},{9,11},{10,... | collective-permute-start | bytes 1622024 | tf_op jit(solution)/shard_map/ppermute | solution.py:25
  33.8 13.9 %collective-permute-start.6 = (bf16[64,4224]{1,0:T(8,128)(2,1)S(1)}, bf16[64,4224]{1,0:T(8,128)(2,1)S(1)}, u32[]{:S(2)}, u32[]{:S(2)}) collective-permute-start(bf16[64,4224]{1,0:T(8,128)(2,1)S(1)} %slice.27), channel_id=1, source_target_pairs={{0,8},{4,12},{8,0},{12,4},{16,24},{20,28},{24,16},{28,20},{1,9},{5... | collective-permute-start | bytes 1622024 | tf_op jit(solution)/shard_map/ppermute | solution.py:25
  34.2 13.3 %collective-permute-start.8 = (bf16[1,2,64,2048]{3,2,1,0:T(8,128)(2,1)S(1)}, bf16[1,2,64,2048]{3,2,1,0:T(8,128)(2,1)S(1)}, u32[]{:S(2)}, u32[]{:S(2)}) collective-permute-start(bf16[1,2,64,2048]{3,2,1,0:T(8,128)(2,1)S(1)} %get-tuple-element.73), channel_id=1, source_target_pairs={{0,4},{4,0},{8,12},{12,8},{16,20},{20,16},{24,28},{28,24},{1,5},{5... | collective-permute-start | bytes 1572872 | tf_op jit(solution)/shard_map/ppermute | solution.py:25
  47.7 2.0 %collective-permute-start.9 = (bf16[64,4224]{1,0:T(8,128)(2,1)S(1)}, bf16[64,4224]{1,0:T(8,128)(2,1)S(1)}, u32[]{:S(2)}, u32[]{:S(2)}) collective-permute-start(bf16[64,4224]{1,0:T(8,128)(2,1)S(1)} %get-tuple-element.75.refs_0_), channel_id=1, source_target_pairs={{0,1},{1,0},{2,3},{3,2},{4,5},{5,4},{6,7},{7,6},{8,9},{9,8},{10,11... | collective-permute-start | bytes 1622024 | tf_op jit(solution)/shard_map/ppermute | solution.py:25
  47.7 2.7 %collective-permute-start.10 = (bf16[64,4224]{1,0:T(8,128)(2,1)S(1)}, bf16[64,4224]{1,0:T(8,128)(2,1)S(1)}, u32[]{:S(2)}, u32[]{:S(2)}) collective-permute-start(bf16[64,4224]{1,0:T(8,128)(2,1)S(1)} %get-tuple-element.76.refs_1_), channel_id=1, source_target_pairs={{0,1},{1,0},{2,3},{3,2},{4,5},{5,4},{6,7},{7,6},{8,9},{9,8},{10,11... | collective-permute-start | bytes 1622024 | tf_op jit(solution)/shard_map/ppermute | solution.py:25
  48.2 17.6 %collective-permute-start.19 = (bf16[1,2,64,2048]{3,2,1,0:T(8,128)(2,1)S(1)}, bf16[1,2,64,2048]{3,2,1,0:T(8,128)(2,1)S(1)}, u32[]{:S(2)}, u32[]{:S(2)}) collective-permute-start(bf16[1,2,64,2048]{3,2,1,0:T(8,128)(2,1)S(1)} %get-tuple-element.84), channel_id=1, source_target_pairs={{0,8},{4,12},{8,0},{12,4},{16,24},{20,28},{24,16},{28,20},{1,9},{5... | collective-permute-start | bytes 1572872 | tf_op jit(solution)/shard_map/ppermute | solution.py:25
  55.2 7.8 %collective-permute-start.15 = (bf16[1,96,1024]{2,1,0:T(8,128)(2,1)S(1)}, bf16[1,96,1024]{2,1,0:T(8,128)(2,1)S(1)}, u32[]{:S(2)}, u32[]{:S(2)}) collective-permute-start(bf16[1,96,1024]{2,1,0:T(8,128)(2,1)S(1)} %dynamic-slice_bitcast_fusion.12.refs_1_), channel_id=1, source_target_pairs={{0,4},{4,0},{8,12},{12,8},{16,20},{20,16},{24,28},{28,24},{1,5},{5... | collective-permute-start | bytes 589832 | tf_op jit(solution)/shard_map/ppermute | solution.py:25
  58.1 9.4 %collective-permute-start.11 = (bf16[256,2048]{1,0:T(8,128)(2,1)S(1)}, bf16[256,2048]{1,0:T(8,128)(2,1)S(1)}, u32[]{:S(2)}, u32[]{:S(2)}) collective-permute-start(bf16[256,2048]{1,0:T(8,128)(2,1)S(1)} %convolution_convert_fusion), channel_id=1, source_target_pairs={{0,1},{1,0},{2,3},{3,2},{4,5},{5,4},{6,7},{7,6},{8,9},{9,8},{10,11... | collective-permute-start | bytes 3145736 | tf_op jit(solution)/shard_map/ppermute | solution.py:25
  58.2 11.8 %collective-permute-start.13 = (bf16[1,160,1024]{2,1,0:T(8,128)(2,1)S(1)}, bf16[1,160,1024]{2,1,0:T(8,128)(2,1)S(1)}, u32[]{:S(2)}, u32[]{:S(2)}) collective-permute-start(bf16[1,160,1024]{2,1,0:T(8,128)(2,1)S(1)} %dynamic-slice_bitcast_fusion.1), channel_id=1, source_target_pairs={{0,4},{4,0},{8,12},{12,8},{16,20},{20,16},{24,28},{28,24},{1,5},{5... | collective-permute-start | bytes 983048 | tf_op jit(solution)/shard_map/ppermute | solution.py:25
  63.0 31.2 %collective-permute-start.16 = (bf16[1,96,1024]{2,1,0:T(8,128)(2,1)S(1)}, bf16[1,96,1024]{2,1,0:T(8,128)(2,1)S(1)}, u32[]{:S(2)}, u32[]{:S(2)}) collective-permute-start(bf16[1,96,1024]{2,1,0:T(8,128)(2,1)S(1)} %fusion.18), channel_id=1, source_target_pairs={{0,16},{4,20},{8,24},{12,28},{16,0},{20,4},{24,8},{28,12},{1,17},{... | collective-permute-start | bytes 589832 | tf_op jit(solution)/shard_map/ppermute | solution.py:25
  65.7 9.9 %collective-permute-start.20 = (bf16[1,64,2048]{2,1,0:T(8,128)(2,1)S(1)}, bf16[1,64,2048]{2,1,0:T(8,128)(2,1)S(1)}, u32[]{:S(2)}, u32[]{:S(2)}) collective-permute-start(bf16[1,64,2048]{2,1,0:T(8,128)(2,1)S(1)} %get-tuple-element.86), channel_id=1, source_target_pairs={{0,4},{4,0},{8,12},{12,8},{16,20},{20,16},{24,28},{28,24},{1,5},{5... | collective-permute-start | bytes 786440 | tf_op jit(solution)/shard_map/ppermute | solution.py:25
  68.8 11.8 %collective-permute-start.12 = (bf16[128,2048]{1,0:T(8,128)(2,1)S(1)}, bf16[128,2048]{1,0:T(8,128)(2,1)S(1)}, u32[]{:S(2)}, u32[]{:S(2)}) collective-permute-start(bf16[128,2048]{1,0:T(8,128)(2,1)S(1)} %slice.57), channel_id=1, source_target_pairs={{0,2},{1,3},{2,0},{3,1},{4,6},{5,7},{6,4},{7,5},{8,10},{9,11},{10,... | collective-permute-start | bytes 1572872 | tf_op jit(solution)/shard_map/ppermute | solution.py:25
  70.1 24.1 %collective-permute-start.17 = (bf16[1,160,1024]{2,1,0:T(8,128)(2,1)S(1)}, bf16[1,160,1024]{2,1,0:T(8,128)(2,1)S(1)}, u32[]{:S(2)}, u32[]{:S(2)}) collective-permute-start(bf16[1,160,1024]{2,1,0:T(8,128)(2,1)S(1)} %fusion.5), channel_id=1, source_target_pairs={{0,16},{4,20},{8,24},{12,28},{16,0},{20,4},{24,8},{28,12},{1,17},{... | collective-permute-start | bytes 983048 | tf_op jit(solution)/shard_map/ppermute | solution.py:25
  72.8 21.5 %collective-permute-start.14 = (bf16[1,256,1024]{2,1,0:T(8,128)(2,1)S(1)}, bf16[1,256,1024]{2,1,0:T(8,128)(2,1)S(1)}, u32[]{:S(2)}, u32[]{:S(2)}) collective-permute-start(bf16[1,256,1024]{2,1,0:T(8,128)(2,1)S(1)} %shard_map.103), channel_id=1, source_target_pairs={{0,4},{4,0},{8,12},{12,8},{16,20},{20,16},{24,28},{28,24},{1,5},{5... | collective-permute-start | bytes 1572872 | tf_op jit(solution)/shard_map/ppermute | solution.py:25
  75.7 23.1 %collective-permute-start.21 = (bf16[1,64,2048]{2,1,0:T(8,128)(2,1)S(1)}, bf16[1,64,2048]{2,1,0:T(8,128)(2,1)S(1)}, u32[]{:S(2)}, u32[]{:S(2)}) collective-permute-start(bf16[1,64,2048]{2,1,0:T(8,128)(2,1)S(1)} %fusion.7), channel_id=1, source_target_pairs={{0,16},{4,20},{8,24},{12,28},{16,0},{20,4},{24,8},{28,12},{1,17},{... | collective-permute-start | bytes 786440 | tf_op jit(solution)/shard_map/ppermute | solution.py:25
  80.7 18.2 %collective-permute-start.18 = (bf16[1,64,2048]{2,1,0:T(8,128)(2,1)S(1)}, bf16[1,64,2048]{2,1,0:T(8,128)(2,1)S(1)}, u32[]{:S(2)}, u32[]{:S(2)}) collective-permute-start(bf16[1,64,2048]{2,1,0:T(8,128)(2,1)S(1)} %shard_map.104.refs_1_), channel_id=1, source_target_pairs={{0,4},{4,0},{8,12},{12,8},{16,20},{20,16},{24,28},{28,24},{1,5},{5... | collective-permute-start | bytes 786440 | tf_op jit(solution)/shard_map/ppermute | solution.py:25

commit v15 on v14

--- a/solution.py
+++ b/solution.py
@@ -128,6 +128,34 @@
     hid_own[...] = own_columns(jnp.concatenate(hidden, axis=1), group_count, parity)
 
 
+def last_kernel(group_count, place, *refs):
+    *blocks, gate_up, down, early, tok_own, hid_own, scaled, first, second, piece = refs
+    made = (tok_own, hid_own, scaled, first, second)
+    expert_kernel(group_count, place, *blocks, gate_up, down, *made)
+    start, count = pl.multiple_of(place[2], LANES), piece.shape[1]
+    back = jnp.concatenate([first[...], second[...]], axis=0)
+    late = lax.dot_general(
+        tok_own[:, pl.ds(start, LANES)], back, ROWS, preferred_element_type=jnp.float32
+    )
+    piece[0] = narrow(early[pl.ds(start, count), :] + late[:count])
+
+
+def last_rows(group_count, place, blocks, gate_up, down, early, count):
+    rows, width = sum(block.shape[0] for block in blocks), gate_up.shape[0]
+    units = down.shape[0]
+    vmem = pl.BlockSpec(memory_space=pltpu.VMEM)
+    shapes = [(rows, width // 2), (rows, units // 2), (rows, width)]
+    shapes += [(rows // 2, 2 * units)] * 2 + [(1, count, 2 * units)]
+    return pl.pallas_call(
+        functools.partial(last_kernel, group_count),
+        out_shape=tuple(jax.ShapeDtypeStruct(shape, jnp.bfloat16) for shape in shapes),
+        in_specs=[pl.BlockSpec(memory_space=pltpu.SMEM)] + [vmem] * (len(blocks) + 3),
+        out_specs=(vmem,) * 6,
+        compiler_params=pltpu.CompilerParams(vmem_limit_bytes=24 << 20),
+        cost_estimate=FREE,
+    )(place, *blocks, gate_up, down, early)
+
+
 def expert_rows(group_count, place, blocks, gate_up, down):
     rows, width = sum(block.shape[0] for block in blocks), gate_up.shape[0]
     units = down.shape[0]
@@ -204,7 +232,10 @@
     me, group = lax.axis_index("expert"), lax.axis_index("dp")
     bits = [lax.convert_element_type((group >> k) & 1, jnp.uint32) for k in range(3)]
     bits += [1 - bit for bit in bits]
-    place = jnp.stack([me, (group >> 1) & 1]).astype(jnp.int32)
+    count = model_width // group_count
+    first = max(count * 3 // 8, 16)
+    far_at = (2 * (1 - ((group >> 2) & 1)) + (1 - (group & 1))) * count
+    place = jnp.stack([me, (group >> 1) & 1, far_at]).astype(jnp.int32)
     high_count, half = group_count // 8, tok_rows // 2
 
     rows_own = packed(tokens, cotangent, expert_ids, gate_probs)
@@ -245,7 +276,13 @@
         down = lax.dot_general(hid_cols, scaled, ROWS, preferred_element_type=jnp.float32)
         return gate, down
 
-    tok_late, hid_late, scaled_late, *back_late = expert_on(*diagonal)
+    direct = high_count == 1 and count % LANES == 0 and first <= LANES
+    if direct:
+        tok_late, hid_late, scaled_late, *back_late, first_piece = last_rows(
+            group_count, place, diagonal, gate_up, down_matrix, gate_early, first
+        )
+    else:
+        tok_late, hid_late, scaled_late, *back_late = expert_on(*diagonal)
     gate_late, down_late = terms(
         tok_late, hid_late, scaled_late, jnp.concatenate(back_late, axis=0)
     )
@@ -255,13 +292,13 @@
     def side(term, third, first):
         return take(take(term, 1, third), 1, first)
 
-    count = gate_term.shape[3]
-    first = max(count * 3 // 8, 16)
     edges = [0, first, count]
     far_sent, far_kept = [
         [side(gate_term[:, :, :, i:j], not2, bit) for i, j in zip(edges, edges[1:])]
         for bit in (not0, bit0)
     ]
+    if direct:
+        far_sent[0] = first_piece
     far_got = [flip(piece, "dp", 1) for piece in far_sent]
     crossed = [
         flip(narrow(pair_sum(kept, got)), "dp", 4) for kept, got in zip(far_kept, far_got)
@@ -278,7 +315,7 @@
     def input_part(back):
         return narrow(jnp.dot(back, gate_up.T, preferred_element_type=jnp.float32))
 
-    (back_sent,) = hold((back_sent,), (far_sent[0],))
+    (back_sent,) = hold((back_sent,), (far_sent[1],))
     core = flip(input_part(back_sent), "expert", 1)
     back_kept = jnp.concatenate([made[0][3], made[1][3]], axis=0)
     total = wide(input_part(back_kept)) + wide(core)

time: 99.9 us -> 98.7 us (0.988)
  other arithmetic: 5.42 us -> 4.11 us
    pallas_call x4 -> x3, Pallas kernels: 9.99 us -> 7.34 us  [expert_rows(): pl.pallas_call(functools.partial(expert_kernel, group_count), out_shape=t...]
    pallas_call x0 -> x1, Pallas kernels: none -> 2.59 us  [last_rows(): pl.pallas_call(functools.partial(last_kernel, group_count), out_shape=tup...]
    convert_element_type x7 -> x6, other arithmetic: 2.89 us -> 1.57 us  [narrow(): return values.astype(jnp.bfloat16)]
  transfers between devices with their start and end apart: 22 -> 22, of which waited for: 12 -> 12; matrix products, arithmetic and copies ran while one was open for 10% -> 9% of each run, Pallas kernels for 13% -> 13%
where the time goes in v15:
time: 98.7 us; the launch traced here: 98.5 us
  waiting for transfers between devices  46 us (47%)
  starting transfers between devices  26.5 us (27%)
  Pallas kernels  14.8 us (15%)
  other arithmetic  4.11 us (4%)
  matrix products  3.98 us (4%)
  local copies, waits for them, and re-layouts  2.2 us (2%)
    ppermute x22, waiting for transfers between devices, flip(): lax.ppermute(values, axis, [(i, i ^ bit) for i in range(lax.axis_size(axi...  46 us
    ppermute x22, starting transfers between devices, flip(): lax.ppermute(values, axis, [(i, i ^ bit) for i in range(lax.axis_size(axi...  26.5 us
    pallas_call x3, Pallas kernels, expert_rows(): pl.pallas_call(functools.partial(expert_kernel, group_count), out_shape=t...  7.34 us
    dot_general x2, matrix products, input_part(): return narrow(jnp.dot(back, gate_up.T, preferred_element_type=jnp.float32))  2.77 us
    pallas_call x1, Pallas kernels, early_terms(): pl.pallas_call(terms_kernel, out_shape=(jax.ShapeDtypeStruct((tok_cols.sh...  2.66 us
    pallas_call x1, Pallas kernels, last_rows(): pl.pallas_call(functools.partial(last_kernel, group_count), out_shape=tup...  2.59 us
    pallas_call x1, Pallas kernels, packed(): pl.pallas_call(pack_kernel, out_shape=jax.ShapeDtypeStruct((rows, 2 * wid...  2.25 us
    mul x2, other arithmetic, on_device(): grad_gate_up, grad_down = (gate_sum * factor, down_sum * factor)  2.15 us
  transfers between devices with their start and end apart: 22, of which 12 were waited for; matrix products, arithmetic and copies ran while one was open for 9% of the time, Pallas kernels for 13%

profile of v15, /device:TPU:0, one launch (start us, length us, event | category | flops | bytes accessed | tf_op | source)
XLA Modules:
  0.0 98.5 jit_solution(13849238398749719800)
XLA Ops:
  0.7 2.3 %shard_map.94.refs_0_ = bf16[128,4224]{1,0:T(8,128)(2,1)} custom-call(bf16[128,2048]{1,0:T(8,128)(2,1)} %tokens.1, bf16[128,2048]{1,0:T(8,128)(2,1)} %cotangent.1, s32[2,128]{1,0:T(2,128)} %bitcast.87, f32[2,128]{1,0:T(2,128)} %bitcast.88), custom_call_target="tpu_custom_call" | custom-call | tf_op jit(solution)/shard_map/pallas_call | solution.py:68
  3.0 3.1 %collective-permute-start.2 = (bf16[128,4224]{1,0:T(8,128)(2,1)}, bf16[128,4224]{1,0:T(8,128)(2,1)S(1)}, u32[]{:S(2)}, u32[]{:S(2)}) collective-permute-start(bf16[128,4224]{1,0:T(8,128)(2,1)} %shard_map.94.refs_0_), channel_id=1, source_target_pairs={{0,8},{4,12},{8,0},{12,4},{16,24},{20,28},{24,16},{28,20},{1,9},{5... | collective-permute-start | bytes 3244040 | tf_op jit(solution)/shard_map/ppermute | solution.py:25
  6.1 1.5 %collective-permute-start.1 = (bf16[128,4224]{1,0:T(8,128)(2,1)}, bf16[128,4224]{1,0:T(8,128)(2,1)S(1)}, u32[]{:S(2)}, u32[]{:S(2)}) collective-permute-start(bf16[128,4224]{1,0:T(8,128)(2,1)} %shard_map.94.refs_0_), channel_id=1, source_target_pairs={{0,2},{1,3},{2,0},{3,1},{4,6},{5,7},{6,4},{7,5},{8,10},{9,11},{10,... | collective-permute-start | bytes 3244040 | tf_op jit(solution)/shard_map/ppermute | solution.py:25
  7.6 1.8 %dynamic-slice_bitcast_fusion.4 = (bf16[1,1,64,2048]{3,2,1,0:T(8,128)(2,1)S(1)}, bf16[1,1,64,2048]{3,2,1,0:T(8,128)(2,1)S(1)}, bf16[1,1,64,2048]{3,2,1,0:T(8,128...) fusion(bf16[1,2,2,2,64,2048]{5,4,3,2,1,0:T(8,128)(2,1)} %bitcas, ...), kind=kLoop, calls=%fused_computation.39 | loop fusion | bytes 4194328 | tf_op jit(solution)/shard_map/stack | solution.py:254
  9.4 1.6 %collective-permute-start.3 = (bf16[1,2,64,2048]{3,2,1,0:T(8,128)(2,1)S(1)}, bf16[1,2,64,2048]{3,2,1,0:T(8,128)(2,1)S(1)}, u32[]{:S(2)}, u32[]{:S(2)}) collective-permute-start(bf16[1,2,64,2048]{3,2,1,0:T(8,128)(2,1)S(1)} %pad_maximum_fusion), channel_id=1, source_target_pairs={{0,4},{4,0},{8,12},{12,8},{16,20},{20,16},{24,28},{28,24},{1,5},{5... | collective-permute-start | bytes 1572872 | tf_op jit(solution)/shard_map/ppermute | solution.py:25
  11.1 12.8 %collective-permute-done.3 = bf16[1,2,64,2048]{3,2,1,0:T(8,128)(2,1)S(1)} collective-permute-done((bf16[1,2,64,2048]{3,2,1,0:T(8,128)(2,1)S(1)}, bf16[1,2,64,2048]{3,2,1,0:T(8,128)(2,1)S(1)}, u32[]{:S(2)}, u32[]{:S(2)}) %collective-permute-start.3) | collective-permute-done | bytes 524320 | tf_op jit(solution)/shard_map/ppermute | solution.py:25
  24.0 2.4 %shard_map.95 = (bf16[256,1024]{1,0:T(8,128)(2,1)S(1)}, bf16[256,256]{1,0:T(8,128)(2,1)S(1)}, bf16[256,2048]{1,0:T(8,128)(2,1)S(1)}, bf16[128,1024]{1,0:T(8,128)(2,1)S(1)}, bf16[128,1024]{1,0:T(8,128)(2,1)S(1)}) custom-call(s32[3]{0:T(128)S(1)} %pad_add_fusion.place, bf16[128,4224]{1,0:T(8,128)(2,1)S(1)} %copy-done.2, ...), custom_call_target="tpu_custom_call" | custom-call | tf_op jit(solution)/shard_map/pallas_call | solution.py:165
  26.5 3.7 %collective-permute-done.2.refs_1_ = bf16[128,4224]{1,0:T(8,128)(2,1)S(1)} collective-permute-done((bf16[128,4224]{1,0:T(8,128)(2,1)}, bf16[128,4224]{1,0:T(8,128)(2,1)S(1)}, u32[]{:S(2)}, u32[]{:S(2)}) %collective-permute-start.2) | collective-permute-done | bytes 1081376 | tf_op jit(solution)/shard_map/ppermute | solution.py:25
  30.1 1.5 %collective-permute-done.1.refs_0_ = bf16[128,4224]{1,0:T(8,128)(2,1)S(1)} collective-permute-done((bf16[128,4224]{1,0:T(8,128)(2,1)}, bf16[128,4224]{1,0:T(8,128)(2,1)S(1)}, u32[]{:S(2)}, u32[]{:S(2)}) %collective-permute-start.1) | collective-permute-done | bytes 1081376 | tf_op jit(solution)/shard_map/ppermute | solution.py:25
  32.2 1.6 %collective-permute-start.7 = (bf16[64,4224]{1,0:T(8,128)(2,1)S(1)}, bf16[64,4224]{1,0:T(8,128)(2,1)S(1)}, u32[]{:S(2)}, u32[]{:S(2)}) collective-permute-start(bf16[64,4224]{1,0:T(8,128)(2,1)S(1)} %slice.27), channel_id=1, source_target_pairs={{0,2},{1,3},{2,0},{3,1},{4,6},{5,7},{6,4},{7,5},{8,10},{9,11},{10,... | collective-permute-start | bytes 1622024 | tf_op jit(solution)/shard_map/ppermute | solution.py:25
  34.2 1.5 %collective-permute-start.8 = (bf16[1,2,64,2048]{3,2,1,0:T(8,128)(2,1)S(1)}, bf16[1,2,64,2048]{3,2,1,0:T(8,128)(2,1)S(1)}, u32[]{:S(2)}, u32[]{:S(2)}) collective-permute-start(bf16[1,2,64,2048]{3,2,1,0:T(8,128)(2,1)S(1)} %get-tuple-element.74), channel_id=1, source_target_pairs={{0,4},{4,0},{8,12},{12,8},{16,20},{20,16},{24,28},{28,24},{1,5},{5... | collective-permute-start | bytes 1572872 | tf_op jit(solution)/shard_map/ppermute | solution.py:25
  35.7 2.4 %shard_map.97 = (bf16[256,1024]{1,0:T(8,128)(2,1)S(1)}, bf16[256,256]{1,0:T(8,128)(2,1)S(1)}, bf16[256,2048]{1,0:T(8,128)(2,1)S(1)}, bf16[128,1024]{1,0:T(8,128)(2,1)S(1)}, bf16[128,1024]{1,0:T(8,128)(2,1)S(1)}) custom-call(s32[3]{0:T(128)S(1)} %pad_add_fusion.place, bf16[128,4224]{1,0:T(8,128)(2,1)S(1)} %get-tuple-element.56.refs_0_, ...), custom_call_target="tpu_custom_call" | custom-call | tf_op jit(solution)/shard_map/pallas_call | solution.py:165
  38.2 2.5 %shard_map.98 = (bf16[256,1024]{1,0:T(8,128)(2,1)S(1)}, bf16[256,256]{1,0:T(8,128)(2,1)S(1)}, bf16[256,2048]{1,0:T(8,128)(2,1)S(1)}, bf16[128,1024]{1,0:T(8,128)(2,1)S(1)}, bf16[128,1024]{1,0:T(8,128)(2,1)S(1)}) custom-call(s32[3]{0:T(128)S(1)} %pad_add_fusion.place, bf16[128,4224]{1,0:T(8,128)(2,1)S(1)} %get-tuple-element.65.refs_0_, ...), custom_call_target="tpu_custom_call" | custom-call | tf_op jit(solution)/shard_map/pallas_call | solution.py:165
  40.7 2.7 %shard_map.99 = (f32[1024,1024]{1,0:T(8,128)S(1)}, f32[256,2048]{1,0:T(8,128)S(1)}, bf16[256,1024]{1,0:T(8,128)(2,1)S(1)}, f32[8,128]{1,0:T(8,128)S(1)}) custom-call(bf16[256,1024]{1,0:T(8,128)(2,1)S(1)} %get-tuple-element.58.refs_0_, bf16[256,256]{1,0:T(8,128)(2,1)S(1)} %get-tuple-element.55.refs_4_.refs_1_, ...), custom_call_target="tpu_custom_call" | custom-call | tf_op jit(solution)/shard_map/pallas_call | solution.py:209
  43.3 4.2 %collective-permute-done.8.refs_3_ = bf16[1,2,64,2048]{3,2,1,0:T(8,128)(2,1)S(1)} collective-permute-done((bf16[1,2,64,2048]{3,2,1,0:T(8,128)(2,1)S(1)}, bf16[1,2,64,2048]{3,2,1,0:T(8,128)(2,1)S(1)}, u32[]{:S(2)}, u32[]{:S(2)}) %collective-permute-start.8) | collective-permute-done | bytes 524320 | tf_op jit(solution)/shard_map/ppermute | solution.py:25
  48.2 1.5 %collective-permute-start.19 = (bf16[1,2,64,2048]{3,2,1,0:T(8,128)(2,1)S(1)}, bf16[1,2,64,2048]{3,2,1,0:T(8,128)(2,1)S(1)}, u32[]{:S(2)}, u32[]{:S(2)}) collective-permute-start(bf16[1,2,64,2048]{3,2,1,0:T(8,128)(2,1)S(1)} %get-tuple-element.86), channel_id=1, source_target_pairs={{0,8},{4,12},{8,0},{12,4},{16,24},{20,28},{24,16},{28,20},{1,9},{5... | collective-permute-start | bytes 1572872 | tf_op jit(solution)/shard_map/ppermute | solution.py:25
  50.4 2.6 %shard_map.101 = (bf16[256,1024]{1,0:T(8,128)(2,1)S(1)}, bf16[256,256]{1,0:T(8,128)(2,1)S(1)}, bf16[256,2048]{1,0:T(8,128)(2,1)S(1)}, bf16[128,1024]{1,0:T(8,128...) custom-call(s32[3]{0:T(128)S(1)} %pad_add_fusion.place, ...), custom_call_target="tpu_custom_call" | custom-call | tf_op jit(solution)/shard_map/pallas_call | solution.py:149
  53.9 1.6 %collective-permute-start.15 = (bf16[1,96,1024]{2,1,0:T(8,128)(2,1)S(1)}, bf16[1,96,1024]{2,1,0:T(8,128)(2,1)S(1)}, u32[]{:S(2)}, u32[]{:S(2)}) collective-permute-start(bf16[1,96,1024]{2,1,0:T(8,128)(2,1)S(1)} %get-tuple-element.81), channel_id=1, source_target_pairs={{0,4},{4,0},{8,12},{12,8},{16,20},{20,16},{24,28},{28,24},{1,5},{5... | collective-permute-start | bytes 589832 | tf_op jit(solution)/shard_map/ppermute | solution.py:25
  56.1 1.5 %convolution_convert_fusion = bf16[256,2048]{1,0:T(8,128)(2,1)S(1)} fusion(bf16[256,1024]{1,0:T(8,128)(2,1)S(1)} %shard_map.102, bf16[1,2048,1024]{2,1,0:T(8,128)(2,1)S(1)} %copy-done), kind=kOutput, calls=%fused_computation.1 | convolution fusion | flops 1074266112 | bytes 5767168 | tf_op jit(solution)/shard_map/dot_general | solution.py:316
  58.5 3.2 %collective-permute-done.15.refs_2_ = bf16[1,96,1024]{2,1,0:T(8,128)(2,1)S(1)} collective-permute-done((bf16[1,96,1024]{2,1,0:T(8,128)(2,1)S(1)}, bf16[1,96,1024]{2,1,0:T(8,128)(2,1)S(1)}, u32[]{:S(2)}, u32[]{:S(2)}) %collective-permute-start.15) | collective-permute-done | bytes 196640 | tf_op jit(solution)/shard_map/ppermute | solution.py:25
  61.8 2.6 %collective-permute-start.16 = (bf16[1,96,1024]{2,1,0:T(8,128)(2,1)S(1)}, bf16[1,96,1024]{2,1,0:T(8,128)(2,1)S(1)}, u32[]{:S(2)}, u32[]{:S(2)}) collective-permute-start(bf16[1,96,1024]{2,1,0:T(8,128)(2,1)S(1)} %fusion.17), channel_id=1, source_target_pairs={{0,16},{4,20},{8,24},{12,28},{16,0},{20,4},{24,8},{28,12},{1,17},{... | collective-permute-start | bytes 589832 | tf_op jit(solution)/shard_map/ppermute | solution.py:25
  64.5 1.5 %collective-permute-start.20 = (bf16[1,64,2048]{2,1,0:T(8,128)(2,1)S(1)}, bf16[1,64,2048]{2,1,0:T(8,128)(2,1)S(1)}, u32[]{:S(2)}, u32[]{:S(2)}) collective-permute-start(bf16[1,64,2048]{2,1,0:T(8,128)(2,1)S(1)} %get-tuple-element.88), channel_id=1, source_target_pairs={{0,4},{4,0},{8,12},{12,8},{16,20},{20,16},{24,28},{28,24},{1,5},{5... | collective-permute-start | bytes 786440 | tf_op jit(solution)/shard_map/ppermute | solution.py:25
  66.2 1.3 %fusion.1 = f32[256,2048]{1,0:T(8,128)S(1)} fusion(bf16[256,2048]{1,0:T(8,128)(2,1)S(1)} %collective-permute-done.11, bf16[128,1024]{1,0:T(8,128)(2,1)S(1)} %get-tuple-element.57.refs_8_, bf16[128,1024]{1,0:T(8,128)(2,1)S(1)} %get-tuple-element.48.refs_3_, bf16[1,2048,1024]{2,1,0:T(8,128)(2,1)S(1)} %copy-done), kind=kOutput, calls=%fused_computation.4 | convolution fusion | flops 1076887552 | bytes 7864320 | tf_op jit(solution)/shard_map/dot_general | solution.py:316
  68.9 2.6 %collective-permute-start.17 = (bf16[1,160,1024]{2,1,0:T(8,128)(2,1)S(1)}, bf16[1,160,1024]{2,1,0:T(8,128)(2,1)S(1)}, u32[]{:S(2)}, u32[]{:S(2)}) collective-permute-start(bf16[1,160,1024]{2,1,0:T(8,128)(2,1)S(1)} %fusion.5), channel_id=1, source_target_pairs={{0,16},{4,20},{8,24},{12,28},{16,0},{20,4},{24,8},{28,12},{1,17},{... | collective-permute-start | bytes 983048 | tf_op jit(solution)/shard_map/ppermute | solution.py:25
  71.5 1.5 %collective-permute-start.14 = (bf16[1,256,1024]{2,1,0:T(8,128)(2,1)S(1)}, bf16[1,256,1024]{2,1,0:T(8,128)(2,1)S(1)}, u32[]{:S(2)}, u32[]{:S(2)}) collective-permute-start(bf16[1,256,1024]{2,1,0:T(8,128)(2,1)S(1)} %shard_map.103), channel_id=1, source_target_pairs={{0,4},{4,0},{8,12},{12,8},{16,20},{20,16},{24,28},{28,24},{1,5},{5... | collective-permute-start | bytes 1572872 | tf_op jit(solution)/shard_map/ppermute | solution.py:25
  73.0 1.4 %collective-permute-done.20 = bf16[1,64,2048]{2,1,0:T(8,128)(2,1)S(1)} collective-permute-done((bf16[1,64,2048]{2,1,0:T(8,128)(2,1)S(1)}, bf16[1,64,2048]{2,1,0:T(8,128)(2,1)S(1)}, u32[]{:S(2)}, u32[]{:S(2)}) %collective-permute-start.20) | collective-permute-done | bytes 262176 | tf_op jit(solution)/shard_map/ppermute | solution.py:25
  74.5 2.6 %collective-permute-start.21 = (bf16[1,64,2048]{2,1,0:T(8,128)(2,1)S(1)}, bf16[1,64,2048]{2,1,0:T(8,128)(2,1)S(1)}, u32[]{:S(2)}, u32[]{:S(2)}) collective-permute-start(bf16[1,64,2048]{2,1,0:T(8,128)(2,1)S(1)} %fusion.7), channel_id=1, source_target_pairs={{0,16},{4,20},{8,24},{12,28},{16,0},{20,4},{24,8},{28,12},{1,17},{... | collective-permute-start | bytes 786440 | tf_op jit(solution)/shard_map/ppermute | solution.py:25
  77.1 2.3 %collective-permute-done.12.refs_1_ = bf16[128,2048]{1,0:T(8,128)(2,1)S(1)} collective-permute-done((bf16[128,2048]{1,0:T(8,128)(2,1)S(1)}, bf16[128,2048]{1,0:T(8,128)(2,1)S(1)}, u32[]{:S(2)}, u32[]{:S(2)}) %collective-permute-start.12) | collective-permute-done | bytes 524320 | tf_op jit(solution)/shard_map/ppermute | solution.py:25
  80.8 12.2 %collective-permute-done.17.refs_0_ = bf16[1,160,1024]{2,1,0:T(8,128)(2,1)S(1)} collective-permute-done((bf16[1,160,1024]{2,1,0:T(8,128)(2,1)S(1)}, bf16[1,160,1024]{2,1,0:T(8,128)(2,1)S(1)}, u32[]{:S(2)}, u32[]{:S(2)}) %collective-permute-start.17) | collective-permute-done | bytes 327712 | tf_op jit(solution)/shard_map/ppermute | solution.py:25
  93.0 1.2 %fusion.4 = f32[1,256,1024]{2,1,0:T(8,128)} fusion(bf16[1,256,1024]{2,1,0:T(8,128)(2,1)S(1)} %collective-permute-done.14, bf16[1,160,1024]{2,1,0:T(8,128)(2,1)S(1)} %shard_map.105, bf16[1,96,1024]{2,1,0:T(8,128)(2,1)S(1)} %collective-permute-done.16, bf16[1,2,2,256,1024]{4,3,2,1,0:T(8,128)(2,1)S(1)} %bitcast.82, u32[]{:T(128)S(6)} %optimization_barrier.37, ...), kind=kLoop, calls=%fused_computation.11 | loop fusion | flops 2359296 | bytes 2621448 | tf_op jit(solution)/shard_map/mul | solution.py:340
  94.2 3.3 %collective-permute-done.21 = bf16[1,64,2048]{2,1,0:T(8,128)(2,1)S(1)} collective-permute-done((bf16[1,64,2048]{2,1,0:T(8,128)(2,1)S(1)}, bf16[1,64,2048]{2,1,0:T(8,128)(2,1)S(1)}, u32[]{:S(2)}, u32[]{:S(2)}) %collective-permute-start.21) | collective-permute-done | bytes 262176 | tf_op jit(solution)/shard_map/ppermute | solution.py:25
  97.6 0.9 fusion.10
  (56 shorter events, 8.4 us)
Async XLA Ops:
  3.0 27.2 %collective-permute-start.2 = (bf16[128,4224]{1,0:T(8,128)(2,1)}, bf16[128,4224]{1,0:T(8,128)(2,1)S(1)}, u32[]{:S(2)}, u32[]{:S(2)}) collective-permute-start(bf16[128,4224]{1,0:T(8,128)(2,1)} %shard_map.94.refs_0_), channel_id=1, source_target_pairs={{0,8},{4,12},{8,0},{12,4},{16,24},{20,28},{24,16},{28,20},{1,9},{5... | collective-permute-start | bytes 3244040 | tf_op jit(solution)/shard_map/ppermute | solution.py:25
  6.1 25.5 %collective-permute-start.1 = (bf16[128,4224]{1,0:T(8,128)(2,1)}, bf16[128,4224]{1,0:T(8,128)(2,1)S(1)}, u32[]{:S(2)}, u32[]{:S(2)}) collective-permute-start(bf16[128,4224]{1,0:T(8,128)(2,1)} %shard_map.94.refs_0_), channel_id=1, source_target_pairs={{0,2},{1,3},{2,0},{3,1},{4,6},{5,7},{6,4},{7,5},{8,10},{9,11},{10,... | collective-permute-start | bytes 3244040 | tf_op jit(solution)/shard_map/ppermute | solution.py:25
  7.6 16.4 %collective-permute-start = (bf16[128,4224]{1,0:T(8,128)(2,1)}, bf16[128,4224]{1,0:T(8,128)(2,1)S(1)}, u32[]{:S(2)}, u32[]{:S(2)}) collective-permute-start(bf16[128,4224]{1,0:T(8,128)(2,1)} %shard_map.94.refs_0_), channel_id=1, source_target_pairs={{0,1},{1,0},{2,3},{3,2},{4,5},{5,4},{6,7},{7,6},{8,9},{9,8},{10,11... | collective-permute-start | bytes 3244040 | tf_op jit(solution)/shard_map/ppermute | solution.py:25
  7.6 16.4 %copy-start = (bf16[1,2048,1024]{2,1,0:T(8,128)(2,1)S(1)}, bf16[1,2048,1024]{2,1,0:T(8,128)(2,1)}, u32[]{:S(2)}) copy-start(bf16[1,2048,1024]{2,1,0:T(8,128)(2,1)} %param.11) | copy-start | bytes 12582916
  9.4 14.6 %copy-start.1 = (bf16[1,512,2048]{2,1,0:T(8,128)(2,1)S(1)}, bf16[1,512,2048]{2,1,0:T(8,128)(2,1)}, u32[]{:S(2)}) copy-start(bf16[1,512,2048]{2,1,0:T(8,128)(2,1)} %param.12) | copy-start | bytes 6291460
  9.4 14.6 %copy-start.2 = (bf16[128,4224]{1,0:T(8,128)(2,1)S(1)}, bf16[128,4224]{1,0:T(8,128)(2,1)}, u32[]{:S(2)}) copy-start(bf16[128,4224]{1,0:T(8,128)(2,1)} %shard_map.94.refs_0_) | copy-start | bytes 3244036
  9.4 14.4 %collective-permute-start.3 = (bf16[1,2,64,2048]{3,2,1,0:T(8,128)(2,1)S(1)}, bf16[1,2,64,2048]{3,2,1,0:T(8,128)(2,1)S(1)}, u32[]{:S(2)}, u32[]{:S(2)}) collective-permute-start(bf16[1,2,64,2048]{3,2,1,0:T(8,128)(2,1)S(1)} %pad_maximum_fusion), channel_id=1, source_target_pairs={{0,4},{4,0},{8,12},{12,8},{16,20},{20,16},{24,28},{28,24},{1,5},{5... | collective-permute-start | bytes 1572872 | tf_op jit(solution)/shard_map/ppermute | solution.py:25
  31.6 4.1 %collective-permute-start.4 = (bf16[128,4224]{1,0:T(8,128)(2,1)S(1)}, bf16[128,4224]{1,0:T(8,128)(2,1)S(1)}, u32[]{:S(2)}, u32[]{:S(2)}) collective-permute-start(bf16[128,4224]{1,0:T(8,128)(2,1)S(1)} %get-tuple-element.56.refs_0_), channel_id=1, source_target_pairs={{0,1},{1,0},{2,3},{3,2},{4,5},{5,4},{6,7},{7,6},{8,9},{9,8},{10,11... | collective-permute-start | bytes 3244040 | tf_op jit(solution)/shard_map/ppermute | solution.py:25
  31.6 6.6 %collective-permute-start.5 = (bf16[128,4224]{1,0:T(8,128)(2,1)S(1)}, bf16[128,4224]{1,0:T(8,128)(2,1)S(1)}, u32[]{:S(2)}, u32[]{:S(2)}) collective-permute-start(bf16[128,4224]{1,0:T(8,128)(2,1)S(1)} %get-tuple-element.65.refs_0_), channel_id=1, source_target_pairs={{0,1},{1,0},{2,3},{3,2},{4,5},{5,4},{6,7},{7,6},{8,9},{9,8},{10,11... | collective-permute-start | bytes 3244040 | tf_op jit(solution)/shard_map/ppermute | solution.py:25
  32.2 15.3 %collective-permute-start.7 = (bf16[64,4224]{1,0:T(8,128)(2,1)S(1)}, bf16[64,4224]{1,0:T(8,128)(2,1)S(1)}, u32[]{:S(2)}, u32[]{:S(2)}) collective-permute-start(bf16[64,4224]{1,0:T(8,128)(2,1)S(1)} %slice.27), channel_id=1, source_target_pairs={{0,2},{1,3},{2,0},{3,1},{4,6},{5,7},{6,4},{7,5},{8,10},{9,11},{10,... | collective-permute-start | bytes 1622024 | tf_op jit(solution)/shard_map/ppermute | solution.py:25
  33.8 13.9 %collective-permute-start.6 = (bf16[64,4224]{1,0:T(8,128)(2,1)S(1)}, bf16[64,4224]{1,0:T(8,128)(2,1)S(1)}, u32[]{:S(2)}, u32[]{:S(2)}) collective-permute-start(bf16[64,4224]{1,0:T(8,128)(2,1)S(1)} %slice.26), channel_id=1, source_target_pairs={{0,8},{4,12},{8,0},{12,4},{16,24},{20,28},{24,16},{28,20},{1,9},{5... | collective-permute-start | bytes 1622024 | tf_op jit(solution)/shard_map/ppermute | solution.py:25
  34.2 13.3 %collective-permute-start.8 = (bf16[1,2,64,2048]{3,2,1,0:T(8,128)(2,1)S(1)}, bf16[1,2,64,2048]{3,2,1,0:T(8,128)(2,1)S(1)}, u32[]{:S(2)}, u32[]{:S(2)}) collective-permute-start(bf16[1,2,64,2048]{3,2,1,0:T(8,128)(2,1)S(1)} %get-tuple-element.74), channel_id=1, source_target_pairs={{0,4},{4,0},{8,12},{12,8},{16,20},{20,16},{24,28},{28,24},{1,5},{5... | collective-permute-start | bytes 1572872 | tf_op jit(solution)/shard_map/ppermute | solution.py:25
  47.7 2.0 %collective-permute-start.9 = (bf16[64,4224]{1,0:T(8,128)(2,1)S(1)}, bf16[64,4224]{1,0:T(8,128)(2,1)S(1)}, u32[]{:S(2)}, u32[]{:S(2)}) collective-permute-start(bf16[64,4224]{1,0:T(8,128)(2,1)S(1)} %get-tuple-element.76.refs_0_), channel_id=1, source_target_pairs={{0,1},{1,0},{2,3},{3,2},{4,5},{5,4},{6,7},{7,6},{8,9},{9,8},{10,11... | collective-permute-start | bytes 1622024 | tf_op jit(solution)/shard_map/ppermute | solution.py:25
  47.7 2.7 %collective-permute-start.10 = (bf16[64,4224]{1,0:T(8,128)(2,1)S(1)}, bf16[64,4224]{1,0:T(8,128)(2,1)S(1)}, u32[]{:S(2)}, u32[]{:S(2)}) collective-permute-start(bf16[64,4224]{1,0:T(8,128)(2,1)S(1)} %get-tuple-element.77.refs_1_), channel_id=1, source_target_pairs={{0,1},{1,0},{2,3},{3,2},{4,5},{5,4},{6,7},{7,6},{8,9},{9,8},{10,11... | collective-permute-start | bytes 1622024 | tf_op jit(solution)/shard_map/ppermute | solution.py:25
  48.2 16.3 %collective-permute-start.19 = (bf16[1,2,64,2048]{3,2,1,0:T(8,128)(2,1)S(1)}, bf16[1,2,64,2048]{3,2,1,0:T(8,128)(2,1)S(1)}, u32[]{:S(2)}, u32[]{:S(2)}) collective-permute-start(bf16[1,2,64,2048]{3,2,1,0:T(8,128)(2,1)S(1)} %get-tuple-element.86), channel_id=1, source_target_pairs={{0,8},{4,12},{8,0},{12,4},{16,24},{20,28},{24,16},{28,20},{1,9},{5... | collective-permute-start | bytes 1572872 | tf_op jit(solution)/shard_map/ppermute | solution.py:25
  53.9 7.8 %collective-permute-start.15 = (bf16[1,96,1024]{2,1,0:T(8,128)(2,1)S(1)}, bf16[1,96,1024]{2,1,0:T(8,128)(2,1)S(1)}, u32[]{:S(2)}, u32[]{:S(2)}) collective-permute-start(bf16[1,96,1024]{2,1,0:T(8,128)(2,1)S(1)} %get-tuple-element.81), channel_id=1, source_target_pairs={{0,4},{4,0},{8,12},{12,8},{16,20},{20,16},{24,28},{28,24},{1,5},{5... | collective-permute-start | bytes 589832 | tf_op jit(solution)/shard_map/ppermute | solution.py:25
  55.5 13.2 %collective-permute-start.13 = (bf16[1,160,1024]{2,1,0:T(8,128)(2,1)S(1)}, bf16[1,160,1024]{2,1,0:T(8,128)(2,1)S(1)}, u32[]{:S(2)}, u32[]{:S(2)}) collective-permute-start(bf16[1,160,1024]{2,1,0:T(8,128)(2,1)S(1)} %dynamic-slice_bitcast_fusion.1.refs_1_), channel_id=1, source_target_pairs={{0,4},{4,0},{8,12},{12,8},{16,20},{20,16},{24,28},{28,24},{1,5},{5... | collective-permute-start | bytes 983048 | tf_op jit(solution)/shard_map/ppermute | solution.py:25
  57.6 8.6 %collective-permute-start.11 = (bf16[256,2048]{1,0:T(8,128)(2,1)S(1)}, bf16[256,2048]{1,0:T(8,128)(2,1)S(1)}, u32[]{:S(2)}, u32[]{:S(2)}) collective-permute-start(bf16[256,2048]{1,0:T(8,128)(2,1)S(1)} %convolution_convert_fusion), channel_id=1, source_target_pairs={{0,1},{1,0},{2,3},{3,2},{4,5},{5,4},{6,7},{7,6},{8,9},{9,8},{10,11... | collective-permute-start | bytes 3145736 | tf_op jit(solution)/shard_map/ppermute | solution.py:25
  61.8 31.2 %collective-permute-start.16 = (bf16[1,96,1024]{2,1,0:T(8,128)(2,1)S(1)}, bf16[1,96,1024]{2,1,0:T(8,128)(2,1)S(1)}, u32[]{:S(2)}, u32[]{:S(2)}) collective-permute-start(bf16[1,96,1024]{2,1,0:T(8,128)(2,1)S(1)} %fusion.17), channel_id=1, source_target_pairs={{0,16},{4,20},{8,24},{12,28},{16,0},{20,4},{24,8},{28,12},{1,17},{... | collective-permute-start | bytes 589832 | tf_op jit(solution)/shard_map/ppermute | solution.py:25
  64.5 9.9 %collective-permute-start.20 = (bf16[1,64,2048]{2,1,0:T(8,128)(2,1)S(1)}, bf16[1,64,2048]{2,1,0:T(8,128)(2,1)S(1)}, u32[]{:S(2)}, u32[]{:S(2)}) collective-permute-start(bf16[1,64,2048]{2,1,0:T(8,128)(2,1)S(1)} %get-tuple-element.88), channel_id=1, source_target_pairs={{0,4},{4,0},{8,12},{12,8},{16,20},{20,16},{24,28},{28,24},{1,5},{5... | collective-permute-start | bytes 786440 | tf_op jit(solution)/shard_map/ppermute | solution.py:25
  67.6 11.8 %collective-permute-start.12 = (bf16[128,2048]{1,0:T(8,128)(2,1)S(1)}, bf16[128,2048]{1,0:T(8,128)(2,1)S(1)}, u32[]{:S(2)}, u32[]{:S(2)}) collective-permute-start(bf16[128,2048]{1,0:T(8,128)(2,1)S(1)} %slice.56), channel_id=1, source_target_pairs={{0,2},{1,3},{2,0},{3,1},{4,6},{5,7},{6,4},{7,5},{8,10},{9,11},{10,... | collective-permute-start | bytes 1572872 | tf_op jit(solution)/shard_map/ppermute | solution.py:25
  68.9 24.1 %collective-permute-start.17 = (bf16[1,160,1024]{2,1,0:T(8,128)(2,1)S(1)}, bf16[1,160,1024]{2,1,0:T(8,128)(2,1)S(1)}, u32[]{:S(2)}, u32[]{:S(2)}) collective-permute-start(bf16[1,160,1024]{2,1,0:T(8,128)(2,1)S(1)} %fusion.5), channel_id=1, source_target_pairs={{0,16},{4,20},{8,24},{12,28},{16,0},{20,4},{24,8},{28,12},{1,17},{... | collective-permute-start | bytes 983048 | tf_op jit(solution)/shard_map/ppermute | solution.py:25
  71.5 21.5 %collective-permute-start.14 = (bf16[1,256,1024]{2,1,0:T(8,128)(2,1)S(1)}, bf16[1,256,1024]{2,1,0:T(8,128)(2,1)S(1)}, u32[]{:S(2)}, u32[]{:S(2)}) collective-permute-start(bf16[1,256,1024]{2,1,0:T(8,128)(2,1)S(1)} %shard_map.103), channel_id=1, source_target_pairs={{0,4},{4,0},{8,12},{12,8},{16,20},{20,16},{24,28},{28,24},{1,5},{5... | collective-permute-start | bytes 1572872 | tf_op jit(solution)/shard_map/ppermute | solution.py:25
  74.5 23.1 %collective-permute-start.21 = (bf16[1,64,2048]{2,1,0:T(8,128)(2,1)S(1)}, bf16[1,64,2048]{2,1,0:T(8,128)(2,1)S(1)}, u32[]{:S(2)}, u32[]{:S(2)}) collective-permute-start(bf16[1,64,2048]{2,1,0:T(8,128)(2,1)S(1)} %fusion.7), channel_id=1, source_target_pairs={{0,16},{4,20},{8,24},{12,28},{16,0},{20,4},{24,8},{28,12},{1,17},{... | collective-permute-start | bytes 786440 | tf_op jit(solution)/shard_map/ppermute | solution.py:25
  79.4 18.2 %collective-permute-start.18 = (bf16[1,64,2048]{2,1,0:T(8,128)(2,1)S(1)}, bf16[1,64,2048]{2,1,0:T(8,128)(2,1)S(1)}, u32[]{:S(2)}, u32[]{:S(2)}) collective-permute-start(bf16[1,64,2048]{2,1,0:T(8,128)(2,1)S(1)} %shard_map.104.refs_1_), channel_id=1, source_target_pairs={{0,4},{4,0},{8,12},{12,8},{16,20},{20,16},{24,28},{28,24},{1,5},{5... | collective-permute-start | bytes 786440 | tf_op jit(solution)/shard_map/ppermute | solution.py:25

commit v16 on v15

--- a/solution.py
+++ b/solution.py
@@ -39,11 +39,18 @@
     return copies
 
 
-def pack_kernel(tokens, cotangent, ids_in, probs_in, packed, ids, probs, sems):
-    width = tokens.shape[1]
+PARTS = 4
+
+
+def pack_kernel(tokens, cotangent, ids_in, probs_in, packed, here, ids, probs, sems):
+    rows, width = tokens.shape
     small = begin([(ids_in, ids), (probs_in, probs)], sems)
-    moves = [(tokens, packed.at[:, :width]), (cotangent, packed.at[:, width : 2 * width])]
-    large = begin(moves, sems.at[2:4])
+    spans = [slice(k * rows // PARTS, (k + 1) * rows // PARTS) for k in range(PARTS)]
+    moves = []
+    for span in spans:
+        moves.append((tokens.at[span, :], here.at[span, :width]))
+        moves.append((cotangent.at[span, :], here.at[span, width : 2 * width]))
+    large = begin(moves, sems.at[2 : 2 + 2 * PARTS])
     for copy in small:
         copy.wait()
     line = lax.broadcasted_iota(jnp.int32, (LANES, tokens.shape[0]), 0)
@@ -57,8 +64,14 @@
     low = (route - high) - middle
     part = lax.rem(line, 3)
     lines = jnp.where(part == 0, high, jnp.where(part == 1, middle, low))
-    packed[:, 2 * width :] = narrow(lines.T)
-    for copy in large:
+    here[:, 2 * width :] = narrow(lines.T)
+    out = []
+    for k, span in enumerate(spans):
+        large[2 * k].wait()
+        large[2 * k + 1].wait()
+        move = (here.at[span, :], packed.at[span, :])
+        out += begin([move], sems.at[2 + 2 * PARTS + k : 3 + 2 * PARTS + k])
+    for copy in out:
         copy.wait()
 
 
@@ -69,11 +82,12 @@
         pack_kernel,
         out_shape=jax.ShapeDtypeStruct((rows, 2 * width + LANES), jnp.bfloat16),
         in_specs=[HERE] * 4,
-        out_specs=pl.BlockSpec(memory_space=pltpu.VMEM),
+        out_specs=HERE,
         scratch_shapes=[
+            pltpu.VMEM((rows, 2 * width + LANES), jnp.bfloat16),
             pltpu.VMEM((top, rows), jnp.int32),
             pltpu.VMEM((top, rows), jnp.float32),
-            pltpu.SemaphoreType.DMA((4,)),
+            pltpu.SemaphoreType.DMA((2 + 3 * PARTS,)),
         ],
         cost_estimate=FREE,
     )(tokens, cotangent, expert_ids.T, gate_probs.T)
@@ -327,7 +341,8 @@
     near_down = pair_sum(side(down_term, bit2, bit0), flip(near_sent, "dp", 1))
     crossed[-1] = hold((crossed[-1],), (near_sent,))[0]
     gate_sum = near_gate + wide(jnp.concatenate(crossed, axis=1))
-    down_sum = near_down + res_sum[:, 1] + wide(crossed_down)
+    near_down = lax.optimization_barrier(near_down + res_sum[:, 1])
+    down_sum = near_down + wide(crossed_down)
     bit = 8
     while bit < group_count:
         mine = lax.convert_element_type((group // bit) & 1, jnp.uint32)

time: 98.7 us -> 106 us (1.074)
  waiting for transfers between devices: 46 us -> 53 us
    ppermute x22, waiting for transfers between devices: 46 us -> 53 us  [flip(): lax.ppermute(values, axis, [(i, i ^ bit) for i in range(lax.axis_size(axi...]
  transfers between devices with their start and end apart: 22 -> 22, of which waited for: 12 -> 12; matrix products, arithmetic and copies ran while one was open for 9% -> 9% of each run, Pallas kernels for 13% -> 12%
where the time goes in v16:
time: 106 us; the launch traced here: 105 us
  waiting for transfers between devices  53 us (50%)
  starting transfers between devices  26.5 us (25%)
  Pallas kernels  14.7 us (14%)
  other arithmetic  4.12 us (4%)
  matrix products  3.98 us (4%)
  local copies, waits for them, and re-layouts  2.2 us (2%)
    ppermute x22, waiting for transfers between devices, flip(): lax.ppermute(values, axis, [(i, i ^ bit) for i in range(lax.axis_size(axi...  53 us
    ppermute x22, starting transfers between devices, flip(): lax.ppermute(values, axis, [(i, i ^ bit) for i in range(lax.axis_size(axi...  26.5 us
    pallas_call x3, Pallas kernels, expert_rows(): pl.pallas_call(functools.partial(expert_kernel, group_count), out_shape=t...  7.33 us
    dot_general x2, matrix products, input_part(): return narrow(jnp.dot(back, gate_up.T, preferred_element_type=jnp.float32))  2.78 us
    pallas_call x1, Pallas kernels, early_terms(): pl.pallas_call(terms_kernel, out_shape=(jax.ShapeDtypeStruct((tok_cols.sh...  2.66 us
    pallas_call x1, Pallas kernels, last_rows(): pl.pallas_call(functools.partial(last_kernel, group_count), out_shape=tup...  2.59 us
    pallas_call x1, Pallas kernels, packed(): pl.pallas_call(pack_kernel, out_shape=jax.ShapeDtypeStruct((rows, 2 * wid...  2.16 us
  transfers between devices with their start and end apart: 22, of which 12 were waited for; matrix products, arithmetic and copies ran while one was open for 9% of the time, Pallas kernels for 12%

profile of v16, /device:TPU:0, one launch (start us, length us, event | category | flops | bytes accessed | tf_op | source)
XLA Modules:
  0.0 105.4 jit_solution(4560874467735509161)
XLA Ops:
  0.7 2.2 %shard_map.94.refs_0_ = bf16[128,4224]{1,0:T(8,128)(2,1)} custom-call(bf16[128,2048]{1,0:T(8,128)(2,1)} %tokens.1, bf16[128,2048]{1,0:T(8,128)(2,1)} %cotangent.1, s32[2,128]{1,0:T(2,128)} %bitcast.82, f32[2,128]{1,0:T(2,128)} %bitcast.83), custom_call_target="tpu_custom_call" | custom-call | tf_op jit(solution)/shard_map/pallas_call | solution.py:81
  2.9 3.1 %collective-permute-start.2 = (bf16[128,4224]{1,0:T(8,128)(2,1)}, bf16[128,4224]{1,0:T(8,128)(2,1)S(1)}, u32[]{:S(2)}, u32[]{:S(2)}) collective-permute-start(bf16[128,4224]{1,0:T(8,128)(2,1)} %shard_map.94.refs_0_), channel_id=1, source_target_pairs={{0,8},{4,12},{8,0},{12,4},{16,24},{20,28},{24,16},{28,20},{1,9},{5... | collective-permute-start | bytes 3244040 | tf_op jit(solution)/shard_map/ppermute | solution.py:25
  6.0 1.5 %collective-permute-start.1 = (bf16[128,4224]{1,0:T(8,128)(2,1)}, bf16[128,4224]{1,0:T(8,128)(2,1)S(1)}, u32[]{:S(2)}, u32[]{:S(2)}) collective-permute-start(bf16[128,4224]{1,0:T(8,128)(2,1)} %shard_map.94.refs_0_), channel_id=1, source_target_pairs={{0,2},{1,3},{2,0},{3,1},{4,6},{5,7},{6,4},{7,5},{8,10},{9,11},{10,... | collective-permute-start | bytes 3244040 | tf_op jit(solution)/shard_map/ppermute | solution.py:25
  7.5 1.8 %dynamic-slice_bitcast_fusion.4 = (bf16[1,1,64,2048]{3,2,1,0:T(8,128)(2,1)S(1)}, bf16[1,1,64,2048]{3,2,1,0:T(8,128)(2,1)S(1)}, bf16[1,1,64,2048]{3,2,1,0:T(8,128...) fusion(bf16[1,2,2,2,64,2048]{5,4,3,2,1,0:T(8,128)(2,1)} %bitcas, ...), kind=kLoop, calls=%fused_computation.38 | loop fusion | bytes 4194328 | tf_op jit(solution)/shard_map/stack | solution.py:268
  9.3 1.6 %collective-permute-start.3 = (bf16[1,2,64,2048]{3,2,1,0:T(8,128)(2,1)S(1)}, bf16[1,2,64,2048]{3,2,1,0:T(8,128)(2,1)S(1)}, u32[]{:S(2)}, u32[]{:S(2)}) collective-permute-start(bf16[1,2,64,2048]{3,2,1,0:T(8,128)(2,1)S(1)} %pad_maximum_fusion), channel_id=1, source_target_pairs={{0,4},{4,0},{8,12},{12,8},{16,20},{20,16},{24,28},{28,24},{1,5},{5... | collective-permute-start | bytes 1572872 | tf_op jit(solution)/shard_map/ppermute | solution.py:25
  11.0 12.8 %collective-permute-done.3 = bf16[1,2,64,2048]{3,2,1,0:T(8,128)(2,1)S(1)} collective-permute-done((bf16[1,2,64,2048]{3,2,1,0:T(8,128)(2,1)S(1)}, bf16[1,2,64,2048]{3,2,1,0:T(8,128)(2,1)S(1)}, u32[]{:S(2)}, u32[]{:S(2)}) %collective-permute-start.3) | collective-permute-done | bytes 524320 | tf_op jit(solution)/shard_map/ppermute | solution.py:25
  23.9 2.4 %shard_map.95 = (bf16[256,1024]{1,0:T(8,128)(2,1)S(1)}, bf16[256,256]{1,0:T(8,128)(2,1)S(1)}, bf16[256,2048]{1,0:T(8,128)(2,1)S(1)}, bf16[128,1024]{1,0:T(8,128)(2,1)S(1)}, bf16[128,1024]{1,0:T(8,128)(2,1)S(1)}) custom-call(s32[3]{0:T(128)S(1)} %pad_add_fusion.place, bf16[128,4224]{1,0:T(8,128)(2,1)S(1)} %copy-done.2, ...), custom_call_target="tpu_custom_call" | custom-call | tf_op jit(solution)/shard_map/pallas_call | solution.py:179
  26.4 3.7 %collective-permute-done.2.refs_1_ = bf16[128,4224]{1,0:T(8,128)(2,1)S(1)} collective-permute-done((bf16[128,4224]{1,0:T(8,128)(2,1)}, bf16[128,4224]{1,0:T(8,128)(2,1)S(1)}, u32[]{:S(2)}, u32[]{:S(2)}) %collective-permute-start.2) | collective-permute-done | bytes 1081376 | tf_op jit(solution)/shard_map/ppermute | solution.py:25
  30.0 1.5 %collective-permute-done.1.refs_0_ = bf16[128,4224]{1,0:T(8,128)(2,1)S(1)} collective-permute-done((bf16[128,4224]{1,0:T(8,128)(2,1)}, bf16[128,4224]{1,0:T(8,128)(2,1)S(1)}, u32[]{:S(2)}, u32[]{:S(2)}) %collective-permute-start.1) | collective-permute-done | bytes 1081376 | tf_op jit(solution)/shard_map/ppermute | solution.py:25
  32.1 1.6 %collective-permute-start.7 = (bf16[64,4224]{1,0:T(8,128)(2,1)S(1)}, bf16[64,4224]{1,0:T(8,128)(2,1)S(1)}, u32[]{:S(2)}, u32[]{:S(2)}) collective-permute-start(bf16[64,4224]{1,0:T(8,128)(2,1)S(1)} %slice.27), channel_id=1, source_target_pairs={{0,2},{1,3},{2,0},{3,1},{4,6},{5,7},{6,4},{7,5},{8,10},{9,11},{10,... | collective-permute-start | bytes 1622024 | tf_op jit(solution)/shard_map/ppermute | solution.py:25
  34.1 1.5 %collective-permute-start.8 = (bf16[1,2,64,2048]{3,2,1,0:T(8,128)(2,1)S(1)}, bf16[1,2,64,2048]{3,2,1,0:T(8,128)(2,1)S(1)}, u32[]{:S(2)}, u32[]{:S(2)}) collective-permute-start(bf16[1,2,64,2048]{3,2,1,0:T(8,128)(2,1)S(1)} %get-tuple-element.74), channel_id=1, source_target_pairs={{0,4},{4,0},{8,12},{12,8},{16,20},{20,16},{24,28},{28,24},{1,5},{5... | collective-permute-start | bytes 1572872 | tf_op jit(solution)/shard_map/ppermute | solution.py:25
  35.6 2.4 %shard_map.97 = (bf16[256,1024]{1,0:T(8,128)(2,1)S(1)}, bf16[256,256]{1,0:T(8,128)(2,1)S(1)}, bf16[256,2048]{1,0:T(8,128)(2,1)S(1)}, bf16[128,1024]{1,0:T(8,128)(2,1)S(1)}, bf16[128,1024]{1,0:T(8,128)(2,1)S(1)}) custom-call(s32[3]{0:T(128)S(1)} %pad_add_fusion.place, bf16[128,4224]{1,0:T(8,128)(2,1)S(1)} %get-tuple-element.56.refs_0_, ...), custom_call_target="tpu_custom_call" | custom-call | tf_op jit(solution)/shard_map/pallas_call | solution.py:179
  38.1 2.5 %shard_map.98 = (bf16[256,1024]{1,0:T(8,128)(2,1)S(1)}, bf16[256,256]{1,0:T(8,128)(2,1)S(1)}, bf16[256,2048]{1,0:T(8,128)(2,1)S(1)}, bf16[128,1024]{1,0:T(8,128)(2,1)S(1)}, bf16[128,1024]{1,0:T(8,128)(2,1)S(1)}) custom-call(s32[3]{0:T(128)S(1)} %pad_add_fusion.place, bf16[128,4224]{1,0:T(8,128)(2,1)S(1)} %get-tuple-element.65.refs_0_, ...), custom_call_target="tpu_custom_call" | custom-call | tf_op jit(solution)/shard_map/pallas_call | solution.py:179
  40.6 2.7 %shard_map.99 = (f32[1024,1024]{1,0:T(8,128)S(1)}, f32[256,2048]{1,0:T(8,128)S(1)}, bf16[256,1024]{1,0:T(8,128)(2,1)S(1)}, f32[8,128]{1,0:T(8,128)S(1)}) custom-call(bf16[256,1024]{1,0:T(8,128)(2,1)S(1)} %get-tuple-element.58.refs_0_, bf16[256,256]{1,0:T(8,128)(2,1)S(1)} %get-tuple-element.55.refs_4_.refs_1_, ...), custom_call_target="tpu_custom_call" | custom-call | tf_op jit(solution)/shard_map/pallas_call | solution.py:223
  43.2 4.2 %collective-permute-done.8.refs_3_ = bf16[1,2,64,2048]{3,2,1,0:T(8,128)(2,1)S(1)} collective-permute-done((bf16[1,2,64,2048]{3,2,1,0:T(8,128)(2,1)S(1)}, bf16[1,2,64,2048]{3,2,1,0:T(8,128)(2,1)S(1)}, u32[]{:S(2)}, u32[]{:S(2)}) %collective-permute-start.8) | collective-permute-done | bytes 524320 | tf_op jit(solution)/shard_map/ppermute | solution.py:25
  48.1 1.5 %collective-permute-start.19 = (bf16[1,2,64,2048]{3,2,1,0:T(8,128)(2,1)S(1)}, bf16[1,2,64,2048]{3,2,1,0:T(8,128)(2,1)S(1)}, u32[]{:S(2)}, u32[]{:S(2)}) collective-permute-start(bf16[1,2,64,2048]{3,2,1,0:T(8,128)(2,1)S(1)} %get-tuple-element.86), channel_id=1, source_target_pairs={{0,8},{4,12},{8,0},{12,4},{16,24},{20,28},{24,16},{28,20},{1,9},{5... | collective-permute-start | bytes 1572872 | tf_op jit(solution)/shard_map/ppermute | solution.py:25
  50.3 2.6 %shard_map.101 = (bf16[256,1024]{1,0:T(8,128)(2,1)S(1)}, bf16[256,256]{1,0:T(8,128)(2,1)S(1)}, bf16[256,2048]{1,0:T(8,128)(2,1)S(1)}, bf16[128,1024]{1,0:T(8,128...) custom-call(s32[3]{0:T(128)S(1)} %pad_add_fusion.place, ...), custom_call_target="tpu_custom_call" | custom-call | tf_op jit(solution)/shard_map/pallas_call | solution.py:163
  53.8 1.6 %collective-permute-start.15 = (bf16[1,96,1024]{2,1,0:T(8,128)(2,1)S(1)}, bf16[1,96,1024]{2,1,0:T(8,128)(2,1)S(1)}, u32[]{:S(2)}, u32[]{:S(2)}) collective-permute-start(bf16[1,96,1024]{2,1,0:T(8,128)(2,1)S(1)} %get-tuple-element.81), channel_id=1, source_target_pairs={{0,4},{4,0},{8,12},{12,8},{16,20},{20,16},{24,28},{28,24},{1,5},{5... | collective-permute-start | bytes 589832 | tf_op jit(solution)/shard_map/ppermute | solution.py:25
  56.0 1.5 %convolution_convert_fusion = bf16[256,2048]{1,0:T(8,128)(2,1)S(1)} fusion(bf16[256,1024]{1,0:T(8,128)(2,1)S(1)} %shard_map.102, bf16[1,2048,1024]{2,1,0:T(8,128)(2,1)S(1)} %copy-done), kind=kOutput, calls=%fused_computation.1 | convolution fusion | flops 1074266112 | bytes 5767168 | tf_op jit(solution)/shard_map/dot_general | solution.py:330
  58.4 3.2 %collective-permute-done.15.refs_2_ = bf16[1,96,1024]{2,1,0:T(8,128)(2,1)S(1)} collective-permute-done((bf16[1,96,1024]{2,1,0:T(8,128)(2,1)S(1)}, bf16[1,96,1024]{2,1,0:T(8,128)(2,1)S(1)}, u32[]{:S(2)}, u32[]{:S(2)}) %collective-permute-start.15) | collective-permute-done | bytes 196640 | tf_op jit(solution)/shard_map/ppermute | solution.py:25
  61.7 2.6 %collective-permute-start.16 = (bf16[1,96,1024]{2,1,0:T(8,128)(2,1)S(1)}, bf16[1,96,1024]{2,1,0:T(8,128)(2,1)S(1)}, u32[]{:S(2)}, u32[]{:S(2)}) collective-permute-start(bf16[1,96,1024]{2,1,0:T(8,128)(2,1)S(1)} %fusion.15), channel_id=1, source_target_pairs={{0,16},{4,20},{8,24},{12,28},{16,0},{20,4},{24,8},{28,12},{1,17},{... | collective-permute-start | bytes 589832 | tf_op jit(solution)/shard_map/ppermute | solution.py:25
  64.4 1.5 %collective-permute-start.20 = (bf16[1,64,2048]{2,1,0:T(8,128)(2,1)S(1)}, bf16[1,64,2048]{2,1,0:T(8,128)(2,1)S(1)}, u32[]{:S(2)}, u32[]{:S(2)}) collective-permute-start(bf16[1,64,2048]{2,1,0:T(8,128)(2,1)S(1)} %get-tuple-element.88), channel_id=1, source_target_pairs={{0,4},{4,0},{8,12},{12,8},{16,20},{20,16},{24,28},{28,24},{1,5},{5... | collective-permute-start | bytes 786440 | tf_op jit(solution)/shard_map/ppermute | solution.py:25
  65.9 1.3 %fusion.1 = f32[256,2048]{1,0:T(8,128)S(1)} fusion(bf16[256,2048]{1,0:T(8,128)(2,1)S(1)} %collective-permute-done.11, bf16[128,1024]{1,0:T(8,128)(2,1)S(1)} %get-tuple-element.57.refs_8_, bf16[128,1024]{1,0:T(8,128)(2,1)S(1)} %get-tuple-element.48.refs_3_, bf16[1,2048,1024]{2,1,0:T(8,128)(2,1)S(1)} %copy-done), kind=kOutput, calls=%fused_computation.4 | convolution fusion | flops 1076887552 | bytes 7864320 | tf_op jit(solution)/shard_map/dot_general | solution.py:330
  68.8 2.6 %collective-permute-start.17 = (bf16[1,160,1024]{2,1,0:T(8,128)(2,1)S(1)}, bf16[1,160,1024]{2,1,0:T(8,128)(2,1)S(1)}, u32[]{:S(2)}, u32[]{:S(2)}) collective-permute-start(bf16[1,160,1024]{2,1,0:T(8,128)(2,1)S(1)} %fusion.5), channel_id=1, source_target_pairs={{0,16},{4,20},{8,24},{12,28},{16,0},{20,4},{24,8},{28,12},{1,17},{... | collective-permute-start | bytes 983048 | tf_op jit(solution)/shard_map/ppermute | solution.py:25
  71.4 1.5 %collective-permute-start.14 = (bf16[1,256,1024]{2,1,0:T(8,128)(2,1)S(1)}, bf16[1,256,1024]{2,1,0:T(8,128)(2,1)S(1)}, u32[]{:S(2)}, u32[]{:S(2)}) collective-permute-start(bf16[1,256,1024]{2,1,0:T(8,128)(2,1)S(1)} %shard_map.103), channel_id=1, source_target_pairs={{0,4},{4,0},{8,12},{12,8},{16,20},{20,16},{24,28},{28,24},{1,5},{5... | collective-permute-start | bytes 1572872 | tf_op jit(solution)/shard_map/ppermute | solution.py:25
  72.9 6.1 %collective-permute-done.12.refs_1_ = bf16[128,2048]{1,0:T(8,128)(2,1)S(1)} collective-permute-done((bf16[128,2048]{1,0:T(8,128)(2,1)S(1)}, bf16[128,2048]{1,0:T(8,128)(2,1)S(1)}, u32[]{:S(2)}, u32[]{:S(2)}) %collective-permute-start.12) | collective-permute-done | bytes 524320 | tf_op jit(solution)/shard_map/ppermute | solution.py:25
  79.6 0.9 fusion.2
  80.5 5.7 %collective-permute-done.17.refs_0_ = bf16[1,160,1024]{2,1,0:T(8,128)(2,1)S(1)} collective-permute-done((bf16[1,160,1024]{2,1,0:T(8,128)(2,1)S(1)}, bf16[1,160,1024]{2,1,0:T(8,128)(2,1)S(1)}, u32[]{:S(2)}, u32[]{:S(2)}) %collective-permute-start.17) | collective-permute-done | bytes 327712 | tf_op jit(solution)/shard_map/ppermute | solution.py:25
  86.2 4.1 %collective-permute-done.18 = bf16[1,64,2048]{2,1,0:T(8,128)(2,1)S(1)} collective-permute-done((bf16[1,64,2048]{2,1,0:T(8,128)(2,1)S(1)}, bf16[1,64,2048]{2,1,0:T(8,128)(2,1)S(1)}, u32[]{:S(2)}, u32[]{:S(2)}) %collective-permute-start.18) | collective-permute-done | bytes 262176 | tf_op jit(solution)/shard_map/ppermute | solution.py:25
  90.5 2.6 %collective-permute-start.21 = (bf16[1,64,2048]{2,1,0:T(8,128)(2,1)S(1)}, bf16[1,64,2048]{2,1,0:T(8,128)(2,1)S(1)}, u32[]{:S(2)}, u32[]{:S(2)}) collective-permute-start(bf16[1,64,2048]{2,1,0:T(8,128)(2,1)S(1)} %get-tuple-element.89), channel_id=1, source_target_pairs={{0,16},{4,20},{8,24},{12,28},{16,0},{20,4},{24,8},{28,12},{1,17},{... | collective-permute-start | bytes 786440 | tf_op jit(solution)/shard_map/ppermute | solution.py:25
  93.2 1.2 %fusion.4 = f32[1,256,1024]{2,1,0:T(8,128)} fusion(bf16[1,256,1024]{2,1,0:T(8,128)(2,1)S(1)} %collective-permute-done.14, bf16[1,160,1024]{2,1,0:T(8,128)(2,1)S(1)} %shard_map.105, bf16[1,96,1024]{2,1,0:T(8,128)(2,1)S(1)} %collective-permute-done.16, bf16[1,2,2,256,1024]{4,3,2,1,0:T(8,128)(2,1)S(1)} %bitcast.78, u32[]{:T(128)S(6)} %optimization_barrier.40, ...), kind=kLoop, calls=%fused_computation.11 | loop fusion | flops 2359296 | bytes 2621448 | tf_op jit(solution)/shard_map/mul | solution.py:355
  94.4 10.2 %collective-permute-done.21 = bf16[1,64,2048]{2,1,0:T(8,128)(2,1)S(1)} collective-permute-done((bf16[1,64,2048]{2,1,0:T(8,128)(2,1)S(1)}, bf16[1,64,2048]{2,1,0:T(8,128)(2,1)S(1)}, u32[]{:S(2)}, u32[]{:S(2)}) %collective-permute-start.21) | collective-permute-done | bytes 262176 | tf_op jit(solution)/shard_map/ppermute | solution.py:25
  (56 shorter events, 8.4 us)
Async XLA Ops:
  2.9 27.2 %collective-permute-start.2 = (bf16[128,4224]{1,0:T(8,128)(2,1)}, bf16[128,4224]{1,0:T(8,128)(2,1)S(1)}, u32[]{:S(2)}, u32[]{:S(2)}) collective-permute-start(bf16[128,4224]{1,0:T(8,128)(2,1)} %shard_map.94.refs_0_), channel_id=1, source_target_pairs={{0,8},{4,12},{8,0},{12,4},{16,24},{20,28},{24,16},{28,20},{1,9},{5... | collective-permute-start | bytes 3244040 | tf_op jit(solution)/shard_map/ppermute | solution.py:25
  6.0 25.5 %collective-permute-start.1 = (bf16[128,4224]{1,0:T(8,128)(2,1)}, bf16[128,4224]{1,0:T(8,128)(2,1)S(1)}, u32[]{:S(2)}, u32[]{:S(2)}) collective-permute-start(bf16[128,4224]{1,0:T(8,128)(2,1)} %shard_map.94.refs_0_), channel_id=1, source_target_pairs={{0,2},{1,3},{2,0},{3,1},{4,6},{5,7},{6,4},{7,5},{8,10},{9,11},{10,... | collective-permute-start | bytes 3244040 | tf_op jit(solution)/shard_map/ppermute | solution.py:25
  7.5 16.4 %collective-permute-start = (bf16[128,4224]{1,0:T(8,128)(2,1)}, bf16[128,4224]{1,0:T(8,128)(2,1)S(1)}, u32[]{:S(2)}, u32[]{:S(2)}) collective-permute-start(bf16[128,4224]{1,0:T(8,128)(2,1)} %shard_map.94.refs_0_), channel_id=1, source_target_pairs={{0,1},{1,0},{2,3},{3,2},{4,5},{5,4},{6,7},{7,6},{8,9},{9,8},{10,11... | collective-permute-start | bytes 3244040 | tf_op jit(solution)/shard_map/ppermute | solution.py:25
  7.5 16.4 %copy-start = (bf16[1,2048,1024]{2,1,0:T(8,128)(2,1)S(1)}, bf16[1,2048,1024]{2,1,0:T(8,128)(2,1)}, u32[]{:S(2)}) copy-start(bf16[1,2048,1024]{2,1,0:T(8,128)(2,1)} %param.11) | copy-start | bytes 12582916
  9.3 14.6 %copy-start.1 = (bf16[1,512,2048]{2,1,0:T(8,128)(2,1)S(1)}, bf16[1,512,2048]{2,1,0:T(8,128)(2,1)}, u32[]{:S(2)}) copy-start(bf16[1,512,2048]{2,1,0:T(8,128)(2,1)} %param.12) | copy-start | bytes 6291460
  9.3 14.6 %copy-start.2 = (bf16[128,4224]{1,0:T(8,128)(2,1)S(1)}, bf16[128,4224]{1,0:T(8,128)(2,1)}, u32[]{:S(2)}) copy-start(bf16[128,4224]{1,0:T(8,128)(2,1)} %shard_map.94.refs_0_) | copy-start | bytes 3244036
  9.3 14.4 %collective-permute-start.3 = (bf16[1,2,64,2048]{3,2,1,0:T(8,128)(2,1)S(1)}, bf16[1,2,64,2048]{3,2,1,0:T(8,128)(2,1)S(1)}, u32[]{:S(2)}, u32[]{:S(2)}) collective-permute-start(bf16[1,2,64,2048]{3,2,1,0:T(8,128)(2,1)S(1)} %pad_maximum_fusion), channel_id=1, source_target_pairs={{0,4},{4,0},{8,12},{12,8},{16,20},{20,16},{24,28},{28,24},{1,5},{5... | collective-permute-start | bytes 1572872 | tf_op jit(solution)/shard_map/ppermute | solution.py:25
  31.5 4.1 %collective-permute-start.4 = (bf16[128,4224]{1,0:T(8,128)(2,1)S(1)}, bf16[128,4224]{1,0:T(8,128)(2,1)S(1)}, u32[]{:S(2)}, u32[]{:S(2)}) collective-permute-start(bf16[128,4224]{1,0:T(8,128)(2,1)S(1)} %get-tuple-element.56.refs_0_), channel_id=1, source_target_pairs={{0,1},{1,0},{2,3},{3,2},{4,5},{5,4},{6,7},{7,6},{8,9},{9,8},{10,11... | collective-permute-start | bytes 3244040 | tf_op jit(solution)/shard_map/ppermute | solution.py:25
  31.5 6.6 %collective-permute-start.5 = (bf16[128,4224]{1,0:T(8,128)(2,1)S(1)}, bf16[128,4224]{1,0:T(8,128)(2,1)S(1)}, u32[]{:S(2)}, u32[]{:S(2)}) collective-permute-start(bf16[128,4224]{1,0:T(8,128)(2,1)S(1)} %get-tuple-element.65.refs_0_), channel_id=1, source_target_pairs={{0,1},{1,0},{2,3},{3,2},{4,5},{5,4},{6,7},{7,6},{8,9},{9,8},{10,11... | collective-permute-start | bytes 3244040 | tf_op jit(solution)/shard_map/ppermute | solution.py:25
  32.1 15.3 %collective-permute-start.7 = (bf16[64,4224]{1,0:T(8,128)(2,1)S(1)}, bf16[64,4224]{1,0:T(8,128)(2,1)S(1)}, u32[]{:S(2)}, u32[]{:S(2)}) collective-permute-start(bf16[64,4224]{1,0:T(8,128)(2,1)S(1)} %slice.27), channel_id=1, source_target_pairs={{0,2},{1,3},{2,0},{3,1},{4,6},{5,7},{6,4},{7,5},{8,10},{9,11},{10,... | collective-permute-start | bytes 1622024 | tf_op jit(solution)/shard_map/ppermute | solution.py:25
  33.7 13.9 %collective-permute-start.6 = (bf16[64,4224]{1,0:T(8,128)(2,1)S(1)}, bf16[64,4224]{1,0:T(8,128)(2,1)S(1)}, u32[]{:S(2)}, u32[]{:S(2)}) collective-permute-start(bf16[64,4224]{1,0:T(8,128)(2,1)S(1)} %slice.26), channel_id=1, source_target_pairs={{0,8},{4,12},{8,0},{12,4},{16,24},{20,28},{24,16},{28,20},{1,9},{5... | collective-permute-start | bytes 1622024 | tf_op jit(solution)/shard_map/ppermute | solution.py:25
  34.1 13.3 %collective-permute-start.8 = (bf16[1,2,64,2048]{3,2,1,0:T(8,128)(2,1)S(1)}, bf16[1,2,64,2048]{3,2,1,0:T(8,128)(2,1)S(1)}, u32[]{:S(2)}, u32[]{:S(2)}) collective-permute-start(bf16[1,2,64,2048]{3,2,1,0:T(8,128)(2,1)S(1)} %get-tuple-element.74), channel_id=1, source_target_pairs={{0,4},{4,0},{8,12},{12,8},{16,20},{20,16},{24,28},{28,24},{1,5},{5... | collective-permute-start | bytes 1572872 | tf_op jit(solution)/shard_map/ppermute | solution.py:25
  47.6 2.0 %collective-permute-start.9 = (bf16[64,4224]{1,0:T(8,128)(2,1)S(1)}, bf16[64,4224]{1,0:T(8,128)(2,1)S(1)}, u32[]{:S(2)}, u32[]{:S(2)}) collective-permute-start(bf16[64,4224]{1,0:T(8,128)(2,1)S(1)} %get-tuple-element.76.refs_0_), channel_id=1, source_target_pairs={{0,1},{1,0},{2,3},{3,2},{4,5},{5,4},{6,7},{7,6},{8,9},{9,8},{10,11... | collective-permute-start | bytes 1622024 | tf_op jit(solution)/shard_map/ppermute | solution.py:25
  47.6 2.7 %collective-permute-start.10 = (bf16[64,4224]{1,0:T(8,128)(2,1)S(1)}, bf16[64,4224]{1,0:T(8,128)(2,1)S(1)}, u32[]{:S(2)}, u32[]{:S(2)}) collective-permute-start(bf16[64,4224]{1,0:T(8,128)(2,1)S(1)} %get-tuple-element.77.refs_1_), channel_id=1, source_target_pairs={{0,1},{1,0},{2,3},{3,2},{4,5},{5,4},{6,7},{7,6},{8,9},{9,8},{10,11... | collective-permute-start | bytes 1622024 | tf_op jit(solution)/shard_map/ppermute | solution.py:25
  48.1 16.3 %collective-permute-start.19 = (bf16[1,2,64,2048]{3,2,1,0:T(8,128)(2,1)S(1)}, bf16[1,2,64,2048]{3,2,1,0:T(8,128)(2,1)S(1)}, u32[]{:S(2)}, u32[]{:S(2)}) collective-permute-start(bf16[1,2,64,2048]{3,2,1,0:T(8,128)(2,1)S(1)} %get-tuple-element.86), channel_id=1, source_target_pairs={{0,8},{4,12},{8,0},{12,4},{16,24},{20,28},{24,16},{28,20},{1,9},{5... | collective-permute-start | bytes 1572872 | tf_op jit(solution)/shard_map/ppermute | solution.py:25
  53.8 7.8 %collective-permute-start.15 = (bf16[1,96,1024]{2,1,0:T(8,128)(2,1)S(1)}, bf16[1,96,1024]{2,1,0:T(8,128)(2,1)S(1)}, u32[]{:S(2)}, u32[]{:S(2)}) collective-permute-start(bf16[1,96,1024]{2,1,0:T(8,128)(2,1)S(1)} %get-tuple-element.81), channel_id=1, source_target_pairs={{0,4},{4,0},{8,12},{12,8},{16,20},{20,16},{24,28},{28,24},{1,5},{5... | collective-permute-start | bytes 589832 | tf_op jit(solution)/shard_map/ppermute | solution.py:25
  55.4 13.2 %collective-permute-start.13 = (bf16[1,160,1024]{2,1,0:T(8,128)(2,1)S(1)}, bf16[1,160,1024]{2,1,0:T(8,128)(2,1)S(1)}, u32[]{:S(2)}, u32[]{:S(2)}) collective-permute-start(bf16[1,160,1024]{2,1,0:T(8,128)(2,1)S(1)} %dynamic-slice_bitcast_fusion.1.refs_1_), channel_id=1, source_target_pairs={{0,4},{4,0},{8,12},{12,8},{16,20},{20,16},{24,28},{28,24},{1,5},{5... | collective-permute-start | bytes 983048 | tf_op jit(solution)/shard_map/ppermute | solution.py:25
  57.5 8.4 %collective-permute-start.11 = (bf16[256,2048]{1,0:T(8,128)(2,1)S(1)}, bf16[256,2048]{1,0:T(8,128)(2,1)S(1)}, u32[]{:S(2)}, u32[]{:S(2)}) collective-permute-start(bf16[256,2048]{1,0:T(8,128)(2,1)S(1)} %convolution_convert_fusion), channel_id=1, source_target_pairs={{0,1},{1,0},{2,3},{3,2},{4,5},{5,4},{6,7},{7,6},{8,9},{9,8},{10,11... | collective-permute-start | bytes 3145736 | tf_op jit(solution)/shard_map/ppermute | solution.py:25
  61.7 31.5 %collective-permute-start.16 = (bf16[1,96,1024]{2,1,0:T(8,128)(2,1)S(1)}, bf16[1,96,1024]{2,1,0:T(8,128)(2,1)S(1)}, u32[]{:S(2)}, u32[]{:S(2)}) collective-permute-start(bf16[1,96,1024]{2,1,0:T(8,128)(2,1)S(1)} %fusion.15), channel_id=1, source_target_pairs={{0,16},{4,20},{8,24},{12,28},{16,0},{20,4},{24,8},{28,12},{1,17},{... | collective-permute-start | bytes 589832 | tf_op jit(solution)/shard_map/ppermute | solution.py:25
  64.4 21.9 %collective-permute-start.20 = (bf16[1,64,2048]{2,1,0:T(8,128)(2,1)S(1)}, bf16[1,64,2048]{2,1,0:T(8,128)(2,1)S(1)}, u32[]{:S(2)}, u32[]{:S(2)}) collective-permute-start(bf16[1,64,2048]{2,1,0:T(8,128)(2,1)S(1)} %get-tuple-element.88), channel_id=1, source_target_pairs={{0,4},{4,0},{8,12},{12,8},{16,20},{20,16},{24,28},{28,24},{1,5},{5... | collective-permute-start | bytes 786440 | tf_op jit(solution)/shard_map/ppermute | solution.py:25
  67.2 11.8 %collective-permute-start.12 = (bf16[128,2048]{1,0:T(8,128)(2,1)S(1)}, bf16[128,2048]{1,0:T(8,128)(2,1)S(1)}, u32[]{:S(2)}, u32[]{:S(2)}) collective-permute-start(bf16[128,2048]{1,0:T(8,128)(2,1)S(1)} %slice.52), channel_id=1, source_target_pairs={{0,2},{1,3},{2,0},{3,1},{4,6},{5,7},{6,4},{7,5},{8,10},{9,11},{10,... | collective-permute-start | bytes 1572872 | tf_op jit(solution)/shard_map/ppermute | solution.py:25
  68.8 17.5 %collective-permute-start.17 = (bf16[1,160,1024]{2,1,0:T(8,128)(2,1)S(1)}, bf16[1,160,1024]{2,1,0:T(8,128)(2,1)S(1)}, u32[]{:S(2)}, u32[]{:S(2)}) collective-permute-start(bf16[1,160,1024]{2,1,0:T(8,128)(2,1)S(1)} %fusion.5), channel_id=1, source_target_pairs={{0,16},{4,20},{8,24},{12,28},{16,0},{20,4},{24,8},{28,12},{1,17},{... | collective-permute-start | bytes 983048 | tf_op jit(solution)/shard_map/ppermute | solution.py:25
  71.4 21.7 %collective-permute-start.14 = (bf16[1,256,1024]{2,1,0:T(8,128)(2,1)S(1)}, bf16[1,256,1024]{2,1,0:T(8,128)(2,1)S(1)}, u32[]{:S(2)}, u32[]{:S(2)}) collective-permute-start(bf16[1,256,1024]{2,1,0:T(8,128)(2,1)S(1)} %shard_map.103), channel_id=1, source_target_pairs={{0,4},{4,0},{8,12},{12,8},{16,20},{20,16},{24,28},{28,24},{1,5},{5... | collective-permute-start | bytes 1572872 | tf_op jit(solution)/shard_map/ppermute | solution.py:25
  79.1 11.3 %collective-permute-start.18 = (bf16[1,64,2048]{2,1,0:T(8,128)(2,1)S(1)}, bf16[1,64,2048]{2,1,0:T(8,128)(2,1)S(1)}, u32[]{:S(2)}, u32[]{:S(2)}) collective-permute-start(bf16[1,64,2048]{2,1,0:T(8,128)(2,1)S(1)} %shard_map.104.refs_1_), channel_id=1, source_target_pairs={{0,4},{4,0},{8,12},{12,8},{16,20},{20,16},{24,28},{28,24},{1,5},{5... | collective-permute-start | bytes 786440 | tf_op jit(solution)/shard_map/ppermute | solution.py:25
  90.5 14.0 %collective-permute-start.21 = (bf16[1,64,2048]{2,1,0:T(8,128)(2,1)S(1)}, bf16[1,64,2048]{2,1,0:T(8,128)(2,1)S(1)}, u32[]{:S(2)}, u32[]{:S(2)}) collective-permute-start(bf16[1,64,2048]{2,1,0:T(8,128)(2,1)S(1)} %get-tuple-element.89), channel_id=1, source_target_pairs={{0,16},{4,20},{8,24},{12,28},{16,0},{20,4},{24,8},{28,12},{1,17},{... | collective-permute-start | bytes 786440 | tf_op jit(solution)/shard_map/ppermute | solution.py:25

commit v17 on v16

--- a/solution.py
+++ b/solution.py
@@ -247,7 +247,7 @@
     bits = [lax.convert_element_type((group >> k) & 1, jnp.uint32) for k in range(3)]
     bits += [1 - bit for bit in bits]
     count = model_width // group_count
-    first = max(count * 3 // 8, 16)
+    first = max(count * 5 // 16, 16)
     far_at = (2 * (1 - ((group >> 2) & 1)) + (1 - (group & 1))) * count
     place = jnp.stack([me, (group >> 1) & 1, far_at]).astype(jnp.int32)
     high_count, half = group_count // 8, tok_rows // 2
@@ -341,8 +341,7 @@
     near_down = pair_sum(side(down_term, bit2, bit0), flip(near_sent, "dp", 1))
     crossed[-1] = hold((crossed[-1],), (near_sent,))[0]
     gate_sum = near_gate + wide(jnp.concatenate(crossed, axis=1))
-    near_down = lax.optimization_barrier(near_down + res_sum[:, 1])
-    down_sum = near_down + wide(crossed_down)
+    down_sum = near_down + res_sum[:, 1] + wide(crossed_down)
     bit = 8
     while bit < group_count:
         mine = lax.convert_element_type((group // bit) & 1, jnp.uint32)

time: 106 us -> 97.7 us (0.922)
  waiting for transfers between devices: 53 us -> 45 us
    ppermute x22, waiting for transfers between devices: 53 us -> 45 us  [flip(): lax.ppermute(values, axis, [(i, i ^ bit) for i in range(lax.axis_size(axi...]
  transfers between devices with their start and end apart: 22 -> 22, of which waited for: 12 -> 12; matrix products, arithmetic and copies ran while one was open for 9% -> 10% of each run, Pallas kernels for 12% -> 13%
where the time goes in v17:
time: 97.7 us; the launch traced here: 97.5 us
  waiting for transfers between devices  45 us (46%)
  starting transfers between devices  26.5 us (27%)
  Pallas kernels  14.7 us (15%)
  other arithmetic  4.13 us (4%)
  matrix products  3.97 us (4%)
  local copies, waits for them, and re-layouts  2.22 us (2%)
    ppermute x22, waiting for transfers between devices, flip(): lax.ppermute(values, axis, [(i, i ^ bit) for i in range(lax.axis_size(axi...  45 us
    ppermute x22, starting transfers between devices, flip(): lax.ppermute(values, axis, [(i, i ^ bit) for i in range(lax.axis_size(axi...  26.5 us
    pallas_call x3, Pallas kernels, expert_rows(): pl.pallas_call(functools.partial(expert_kernel, group_count), out_shape=t...  7.34 us
    dot_general x2, matrix products, input_part(): return narrow(jnp.dot(back, gate_up.T, preferred_element_type=jnp.float32))  2.77 us
    pallas_call x1, Pallas kernels, early_terms(): pl.pallas_call(terms_kernel, out_shape=(jax.ShapeDtypeStruct((tok_cols.sh...  2.66 us
    pallas_call x1, Pallas kernels, last_rows(): pl.pallas_call(functools.partial(last_kernel, group_count), out_shape=tup...  2.58 us
    pallas_call x1, Pallas kernels, packed(): pl.pallas_call(pack_kernel, out_shape=jax.ShapeDtypeStruct((rows, 2 * wid...  2.16 us
    mul x2, other arithmetic, on_device(): grad_gate_up, grad_down = (gate_sum * factor, down_sum * factor)  2.15 us
  transfers between devices with their start and end apart: 22, of which 12 were waited for; matrix products, arithmetic and copies ran while one was open for 10% of the time, Pallas kernels for 13%

profile of v17, /device:TPU:0, one launch (start us, length us, event | category | flops | bytes accessed | tf_op | source)
XLA Modules:
  0.0 97.5 jit_solution(2625553730233132224)
XLA Ops:
  0.7 2.2 %shard_map.94.refs_0_ = bf16[128,4224]{1,0:T(8,128)(2,1)} custom-call(bf16[128,2048]{1,0:T(8,128)(2,1)} %tokens.1, bf16[128,2048]{1,0:T(8,128)(2,1)} %cotangent.1, s32[2,128]{1,0:T(2,128)} %bitcast.87, f32[2,128]{1,0:T(2,128)} %bitcast.88), custom_call_target="tpu_custom_call" | custom-call | tf_op jit(solution)/shard_map/pallas_call | solution.py:81
  2.9 3.1 %collective-permute-start.2 = (bf16[128,4224]{1,0:T(8,128)(2,1)}, bf16[128,4224]{1,0:T(8,128)(2,1)S(1)}, u32[]{:S(2)}, u32[]{:S(2)}) collective-permute-start(bf16[128,4224]{1,0:T(8,128)(2,1)} %shard_map.94.refs_0_), channel_id=1, source_target_pairs={{0,8},{4,12},{8,0},{12,4},{16,24},{20,28},{24,16},{28,20},{1,9},{5... | collective-permute-start | bytes 3244040 | tf_op jit(solution)/shard_map/ppermute | solution.py:25
  6.0 1.5 %collective-permute-start.1 = (bf16[128,4224]{1,0:T(8,128)(2,1)}, bf16[128,4224]{1,0:T(8,128)(2,1)S(1)}, u32[]{:S(2)}, u32[]{:S(2)}) collective-permute-start(bf16[128,4224]{1,0:T(8,128)(2,1)} %shard_map.94.refs_0_), channel_id=1, source_target_pairs={{0,2},{1,3},{2,0},{3,1},{4,6},{5,7},{6,4},{7,5},{8,10},{9,11},{10,... | collective-permute-start | bytes 3244040 | tf_op jit(solution)/shard_map/ppermute | solution.py:25
  7.5 1.8 %dynamic-slice_bitcast_fusion.4 = (bf16[1,1,64,2048]{3,2,1,0:T(8,128)(2,1)S(1)}, bf16[1,1,64,2048]{3,2,1,0:T(8,128)(2,1)S(1)}, bf16[1,1,64,2048]{3,2,1,0:T(8,128...) fusion(bf16[1,2,2,2,64,2048]{5,4,3,2,1,0:T(8,128)(2,1)} %bitcas, ...), kind=kLoop, calls=%fused_computation.39 | loop fusion | bytes 4194328 | tf_op jit(solution)/shard_map/stack | solution.py:268
  9.4 1.6 %collective-permute-start.3 = (bf16[1,2,64,2048]{3,2,1,0:T(8,128)(2,1)S(1)}, bf16[1,2,64,2048]{3,2,1,0:T(8,128)(2,1)S(1)}, u32[]{:S(2)}, u32[]{:S(2)}) collective-permute-start(bf16[1,2,64,2048]{3,2,1,0:T(8,128)(2,1)S(1)} %pad_maximum_fusion), channel_id=1, source_target_pairs={{0,4},{4,0},{8,12},{12,8},{16,20},{20,16},{24,28},{28,24},{1,5},{5... | collective-permute-start | bytes 1572872 | tf_op jit(solution)/shard_map/ppermute | solution.py:25
  11.0 12.8 %collective-permute-done.3 = bf16[1,2,64,2048]{3,2,1,0:T(8,128)(2,1)S(1)} collective-permute-done((bf16[1,2,64,2048]{3,2,1,0:T(8,128)(2,1)S(1)}, bf16[1,2,64,2048]{3,2,1,0:T(8,128)(2,1)S(1)}, u32[]{:S(2)}, u32[]{:S(2)}) %collective-permute-start.3) | collective-permute-done | bytes 524320 | tf_op jit(solution)/shard_map/ppermute | solution.py:25
  23.9 2.4 %shard_map.95 = (bf16[256,1024]{1,0:T(8,128)(2,1)S(1)}, bf16[256,256]{1,0:T(8,128)(2,1)S(1)}, bf16[256,2048]{1,0:T(8,128)(2,1)S(1)}, bf16[128,1024]{1,0:T(8,128)(2,1)S(1)}, bf16[128,1024]{1,0:T(8,128)(2,1)S(1)}) custom-call(s32[3]{0:T(128)S(1)} %pad_add_fusion.place, bf16[128,4224]{1,0:T(8,128)(2,1)S(1)} %copy-done.2, ...), custom_call_target="tpu_custom_call" | custom-call | tf_op jit(solution)/shard_map/pallas_call | solution.py:179
  26.4 3.7 %collective-permute-done.2.refs_1_ = bf16[128,4224]{1,0:T(8,128)(2,1)S(1)} collective-permute-done((bf16[128,4224]{1,0:T(8,128)(2,1)}, bf16[128,4224]{1,0:T(8,128)(2,1)S(1)}, u32[]{:S(2)}, u32[]{:S(2)}) %collective-permute-start.2) | collective-permute-done | bytes 1081376 | tf_op jit(solution)/shard_map/ppermute | solution.py:25
  30.1 1.5 %collective-permute-done.1.refs_0_ = bf16[128,4224]{1,0:T(8,128)(2,1)S(1)} collective-permute-done((bf16[128,4224]{1,0:T(8,128)(2,1)}, bf16[128,4224]{1,0:T(8,128)(2,1)S(1)}, u32[]{:S(2)}, u32[]{:S(2)}) %collective-permute-start.1) | collective-permute-done | bytes 1081376 | tf_op jit(solution)/shard_map/ppermute | solution.py:25
  32.1 1.6 %collective-permute-start.7 = (bf16[64,4224]{1,0:T(8,128)(2,1)S(1)}, bf16[64,4224]{1,0:T(8,128)(2,1)S(1)}, u32[]{:S(2)}, u32[]{:S(2)}) collective-permute-start(bf16[64,4224]{1,0:T(8,128)(2,1)S(1)} %slice.27), channel_id=1, source_target_pairs={{0,2},{1,3},{2,0},{3,1},{4,6},{5,7},{6,4},{7,5},{8,10},{9,11},{10,... | collective-permute-start | bytes 1622024 | tf_op jit(solution)/shard_map/ppermute | solution.py:25
  34.1 1.5 %collective-permute-start.8 = (bf16[1,2,64,2048]{3,2,1,0:T(8,128)(2,1)S(1)}, bf16[1,2,64,2048]{3,2,1,0:T(8,128)(2,1)S(1)}, u32[]{:S(2)}, u32[]{:S(2)}) collective-permute-start(bf16[1,2,64,2048]{3,2,1,0:T(8,128)(2,1)S(1)} %get-tuple-element.74), channel_id=1, source_target_pairs={{0,4},{4,0},{8,12},{12,8},{16,20},{20,16},{24,28},{28,24},{1,5},{5... | collective-permute-start | bytes 1572872 | tf_op jit(solution)/shard_map/ppermute | solution.py:25
  35.6 2.4 %shard_map.97 = (bf16[256,1024]{1,0:T(8,128)(2,1)S(1)}, bf16[256,256]{1,0:T(8,128)(2,1)S(1)}, bf16[256,2048]{1,0:T(8,128)(2,1)S(1)}, bf16[128,1024]{1,0:T(8,128)(2,1)S(1)}, bf16[128,1024]{1,0:T(8,128)(2,1)S(1)}) custom-call(s32[3]{0:T(128)S(1)} %pad_add_fusion.place, bf16[128,4224]{1,0:T(8,128)(2,1)S(1)} %get-tuple-element.56.refs_0_, ...), custom_call_target="tpu_custom_call" | custom-call | tf_op jit(solution)/shard_map/pallas_call | solution.py:179
  38.1 2.5 %shard_map.98 = (bf16[256,1024]{1,0:T(8,128)(2,1)S(1)}, bf16[256,256]{1,0:T(8,128)(2,1)S(1)}, bf16[256,2048]{1,0:T(8,128)(2,1)S(1)}, bf16[128,1024]{1,0:T(8,128)(2,1)S(1)}, bf16[128,1024]{1,0:T(8,128)(2,1)S(1)}) custom-call(s32[3]{0:T(128)S(1)} %pad_add_fusion.place, bf16[128,4224]{1,0:T(8,128)(2,1)S(1)} %get-tuple-element.65.refs_0_, ...), custom_call_target="tpu_custom_call" | custom-call | tf_op jit(solution)/shard_map/pallas_call | solution.py:179
  40.6 2.7 %shard_map.99 = (f32[1024,1024]{1,0:T(8,128)S(1)}, f32[256,2048]{1,0:T(8,128)S(1)}, bf16[256,1024]{1,0:T(8,128)(2,1)S(1)}, f32[8,128]{1,0:T(8,128)S(1)}) custom-call(bf16[256,1024]{1,0:T(8,128)(2,1)S(1)} %get-tuple-element.58.refs_0_, bf16[256,256]{1,0:T(8,128)(2,1)S(1)} %get-tuple-element.55.refs_4_.refs_1_, ...), custom_call_target="tpu_custom_call" | custom-call | tf_op jit(solution)/shard_map/pallas_call | solution.py:223
  43.2 4.2 %collective-permute-done.8.refs_3_ = bf16[1,2,64,2048]{3,2,1,0:T(8,128)(2,1)S(1)} collective-permute-done((bf16[1,2,64,2048]{3,2,1,0:T(8,128)(2,1)S(1)}, bf16[1,2,64,2048]{3,2,1,0:T(8,128)(2,1)S(1)}, u32[]{:S(2)}, u32[]{:S(2)}) %collective-permute-start.8) | collective-permute-done | bytes 524320 | tf_op jit(solution)/shard_map/ppermute | solution.py:25
  48.1 1.5 %collective-permute-start.19 = (bf16[1,2,64,2048]{3,2,1,0:T(8,128)(2,1)S(1)}, bf16[1,2,64,2048]{3,2,1,0:T(8,128)(2,1)S(1)}, u32[]{:S(2)}, u32[]{:S(2)}) collective-permute-start(bf16[1,2,64,2048]{3,2,1,0:T(8,128)(2,1)S(1)} %get-tuple-element.86), channel_id=1, source_target_pairs={{0,8},{4,12},{8,0},{12,4},{16,24},{20,28},{24,16},{28,20},{1,9},{5... | collective-permute-start | bytes 1572872 | tf_op jit(solution)/shard_map/ppermute | solution.py:25
  50.3 2.6 %shard_map.101 = (bf16[256,1024]{1,0:T(8,128)(2,1)S(1)}, bf16[256,256]{1,0:T(8,128)(2,1)S(1)}, bf16[256,2048]{1,0:T(8,128)(2,1)S(1)}, bf16[128,1024]{1,0:T(8,128...) custom-call(s32[3]{0:T(128)S(1)} %pad_add_fusion.place, ...), custom_call_target="tpu_custom_call" | custom-call | tf_op jit(solution)/shard_map/pallas_call | solution.py:163
  52.9 1.6 %collective-permute-start.15 = (bf16[1,80,1024]{2,1,0:T(8,128)(2,1)S(1)}, bf16[1,80,1024]{2,1,0:T(8,128)(2,1)S(1)}, u32[]{:S(2)}, u32[]{:S(2)}) collective-permute-start(bf16[1,80,1024]{2,1,0:T(8,128)(2,1)S(1)} %get-tuple-element.81), channel_id=1, source_target_pairs={{0,4},{4,0},{8,12},{12,8},{16,20},{20,16},{24,28},{28,24},{1,5},{5... | collective-permute-start | bytes 491528 | tf_op jit(solution)/shard_map/ppermute | solution.py:25
  55.9 1.5 %convolution_convert_fusion = bf16[256,2048]{1,0:T(8,128)(2,1)S(1)} fusion(bf16[256,1024]{1,0:T(8,128)(2,1)S(1)} %shard_map.102, bf16[1,2048,1024]{2,1,0:T(8,128)(2,1)S(1)} %copy-done), kind=kOutput, calls=%fused_computation.1 | convolution fusion | flops 1074266112 | bytes 5767168 | tf_op jit(solution)/shard_map/dot_general | solution.py:330
  58.5 1.5 %collective-permute-done.15.refs_2_ = bf16[1,80,1024]{2,1,0:T(8,128)(2,1)S(1)} collective-permute-done((bf16[1,80,1024]{2,1,0:T(8,128)(2,1)S(1)}, bf16[1,80,1024]{2,1,0:T(8,128)(2,1)S(1)}, u32[]{:S(2)}, u32[]{:S(2)}) %collective-permute-start.15) | collective-permute-done | bytes 163872 | tf_op jit(solution)/shard_map/ppermute | solution.py:25
  60.0 2.6 %collective-permute-start.16 = (bf16[1,80,1024]{2,1,0:T(8,128)(2,1)S(1)}, bf16[1,80,1024]{2,1,0:T(8,128)(2,1)S(1)}, u32[]{:S(2)}, u32[]{:S(2)}) collective-permute-start(bf16[1,80,1024]{2,1,0:T(8,128)(2,1)S(1)} %fusion.17), channel_id=1, source_target_pairs={{0,16},{4,20},{8,24},{12,28},{16,0},{20,4},{24,8},{28,12},{1,17},{... | collective-permute-start | bytes 491528 | tf_op jit(solution)/shard_map/ppermute | solution.py:25
  62.7 1.5 %collective-permute-start.20 = (bf16[1,64,2048]{2,1,0:T(8,128)(2,1)S(1)}, bf16[1,64,2048]{2,1,0:T(8,128)(2,1)S(1)}, u32[]{:S(2)}, u32[]{:S(2)}) collective-permute-start(bf16[1,64,2048]{2,1,0:T(8,128)(2,1)S(1)} %get-tuple-element.88), channel_id=1, source_target_pairs={{0,4},{4,0},{8,12},{12,8},{16,20},{20,16},{24,28},{28,24},{1,5},{5... | collective-permute-start | bytes 786440 | tf_op jit(solution)/shard_map/ppermute | solution.py:25
  64.4 1.3 %fusion.1 = f32[256,2048]{1,0:T(8,128)S(1)} fusion(bf16[256,2048]{1,0:T(8,128)(2,1)S(1)} %collective-permute-done.11, bf16[128,1024]{1,0:T(8,128)(2,1)S(1)} %get-tuple-element.57.refs_8_, bf16[128,1024]{1,0:T(8,128)(2,1)S(1)} %get-tuple-element.48.refs_3_, bf16[1,2048,1024]{2,1,0:T(8,128)(2,1)S(1)} %copy-done), kind=kOutput, calls=%fused_computation.4 | convolution fusion | flops 1076887552 | bytes 7864320 | tf_op jit(solution)/shard_map/dot_general | solution.py:330
  66.4 1.3 %collective-permute-done.13.refs_1_ = bf16[1,176,1024]{2,1,0:T(8,128)(2,1)S(1)} collective-permute-done((bf16[1,176,1024]{2,1,0:T(8,128)(2,1)S(1)}, bf16[1,176,1024]{2,1,0:T(8,128)(2,1)S(1)}, u32[]{:S(2)}, u32[]{:S(2)}) %collective-permute-start.13) | collective-permute-done | bytes 360480 | tf_op jit(solution)/shard_map/ppermute | solution.py:25
  67.8 2.6 %collective-permute-start.17 = (bf16[1,176,1024]{2,1,0:T(8,128)(2,1)S(1)}, bf16[1,176,1024]{2,1,0:T(8,128)(2,1)S(1)}, u32[]{:S(2)}, u32[]{:S(2)}) collective-permute-start(bf16[1,176,1024]{2,1,0:T(8,128)(2,1)S(1)} %fusion.5), channel_id=1, source_target_pairs={{0,16},{4,20},{8,24},{12,28},{16,0},{20,4},{24,8},{28,12},{1,17},{... | collective-permute-start | bytes 1081352 | tf_op jit(solution)/shard_map/ppermute | solution.py:25
  70.5 1.5 %collective-permute-start.14 = (bf16[1,256,1024]{2,1,0:T(8,128)(2,1)S(1)}, bf16[1,256,1024]{2,1,0:T(8,128)(2,1)S(1)}, u32[]{:S(2)}, u32[]{:S(2)}) collective-permute-start(bf16[1,256,1024]{2,1,0:T(8,128)(2,1)S(1)} %shard_map.103), channel_id=1, source_target_pairs={{0,4},{4,0},{8,12},{12,8},{16,20},{20,16},{24,28},{28,24},{1,5},{5... | collective-permute-start | bytes 1572872 | tf_op jit(solution)/shard_map/ppermute | solution.py:25
  72.0 1.3 %collective-permute-done.20 = bf16[1,64,2048]{2,1,0:T(8,128)(2,1)S(1)} collective-permute-done((bf16[1,64,2048]{2,1,0:T(8,128)(2,1)S(1)}, bf16[1,64,2048]{2,1,0:T(8,128)(2,1)S(1)}, u32[]{:S(2)}, u32[]{:S(2)}) %collective-permute-start.20) | collective-permute-done | bytes 262176 | tf_op jit(solution)/shard_map/ppermute | solution.py:25
  73.4 2.6 %collective-permute-start.21 = (bf16[1,64,2048]{2,1,0:T(8,128)(2,1)S(1)}, bf16[1,64,2048]{2,1,0:T(8,128)(2,1)S(1)}, u32[]{:S(2)}, u32[]{:S(2)}) collective-permute-start(bf16[1,64,2048]{2,1,0:T(8,128)(2,1)S(1)} %fusion.7), channel_id=1, source_target_pairs={{0,16},{4,20},{8,24},{12,28},{16,0},{20,4},{24,8},{28,12},{1,17},{... | collective-permute-start | bytes 786440 | tf_op jit(solution)/shard_map/ppermute | solution.py:25
  76.1 2.1 %collective-permute-done.12.refs_1_ = bf16[128,2048]{1,0:T(8,128)(2,1)S(1)} collective-permute-done((bf16[128,2048]{1,0:T(8,128)(2,1)S(1)}, bf16[128,2048]{1,0:T(8,128)(2,1)S(1)}, u32[]{:S(2)}, u32[]{:S(2)}) %collective-permute-start.12) | collective-permute-done | bytes 524320 | tf_op jit(solution)/shard_map/ppermute | solution.py:25
  79.5 12.5 %collective-permute-done.17.refs_0_ = bf16[1,176,1024]{2,1,0:T(8,128)(2,1)S(1)} collective-permute-done((bf16[1,176,1024]{2,1,0:T(8,128)(2,1)S(1)}, bf16[1,176,1024]{2,1,0:T(8,128)(2,1)S(1)}, u32[]{:S(2)}, u32[]{:S(2)}) %collective-permute-start.17) | collective-permute-done | bytes 360480 | tf_op jit(solution)/shard_map/ppermute | solution.py:25
  92.0 1.2 %fusion.4 = f32[1,256,1024]{2,1,0:T(8,128)} fusion(bf16[1,256,1024]{2,1,0:T(8,128)(2,1)S(1)} %collective-permute-done.14, bf16[1,176,1024]{2,1,0:T(8,128)(2,1)S(1)} %shard_map.105, bf16[1,80,1024]{2,1,0:T(8,128)(2,1)S(1)} %collective-permute-done.16, bf16[1,2,2,256,1024]{4,3,2,1,0:T(8,128)(2,1)S(1)} %bitcast.82, u32[]{:T(128)S(6)} %optimization_barrier.37, ...), kind=kLoop, calls=%fused_computation.11 | loop fusion | flops 2359296 | bytes 2621448 | tf_op jit(solution)/shard_map/mul | solution.py:354
  93.2 3.3 %collective-permute-done.21 = bf16[1,64,2048]{2,1,0:T(8,128)(2,1)S(1)} collective-permute-done((bf16[1,64,2048]{2,1,0:T(8,128)(2,1)S(1)}, bf16[1,64,2048]{2,1,0:T(8,128)(2,1)S(1)}, u32[]{:S(2)}, u32[]{:S(2)}) %collective-permute-start.21) | collective-permute-done | bytes 262176 | tf_op jit(solution)/shard_map/ppermute | solution.py:25
  (56 shorter events, 8.7 us)
Async XLA Ops:
  2.9 27.2 %collective-permute-start.2 = (bf16[128,4224]{1,0:T(8,128)(2,1)}, bf16[128,4224]{1,0:T(8,128)(2,1)S(1)}, u32[]{:S(2)}, u32[]{:S(2)}) collective-permute-start(bf16[128,4224]{1,0:T(8,128)(2,1)} %shard_map.94.refs_0_), channel_id=1, source_target_pairs={{0,8},{4,12},{8,0},{12,4},{16,24},{20,28},{24,16},{28,20},{1,9},{5... | collective-permute-start | bytes 3244040 | tf_op jit(solution)/shard_map/ppermute | solution.py:25
  6.0 25.5 %collective-permute-start.1 = (bf16[128,4224]{1,0:T(8,128)(2,1)}, bf16[128,4224]{1,0:T(8,128)(2,1)S(1)}, u32[]{:S(2)}, u32[]{:S(2)}) collective-permute-start(bf16[128,4224]{1,0:T(8,128)(2,1)} %shard_map.94.refs_0_), channel_id=1, source_target_pairs={{0,2},{1,3},{2,0},{3,1},{4,6},{5,7},{6,4},{7,5},{8,10},{9,11},{10,... | collective-permute-start | bytes 3244040 | tf_op jit(solution)/shard_map/ppermute | solution.py:25
  7.5 16.4 %collective-permute-start = (bf16[128,4224]{1,0:T(8,128)(2,1)}, bf16[128,4224]{1,0:T(8,128)(2,1)S(1)}, u32[]{:S(2)}, u32[]{:S(2)}) collective-permute-start(bf16[128,4224]{1,0:T(8,128)(2,1)} %shard_map.94.refs_0_), channel_id=1, source_target_pairs={{0,1},{1,0},{2,3},{3,2},{4,5},{5,4},{6,7},{7,6},{8,9},{9,8},{10,11... | collective-permute-start | bytes 3244040 | tf_op jit(solution)/shard_map/ppermute | solution.py:25
  7.5 16.4 %copy-start = (bf16[1,2048,1024]{2,1,0:T(8,128)(2,1)S(1)}, bf16[1,2048,1024]{2,1,0:T(8,128)(2,1)}, u32[]{:S(2)}) copy-start(bf16[1,2048,1024]{2,1,0:T(8,128)(2,1)} %param.11) | copy-start | bytes 12582916
  9.3 14.6 %copy-start.1 = (bf16[1,512,2048]{2,1,0:T(8,128)(2,1)S(1)}, bf16[1,512,2048]{2,1,0:T(8,128)(2,1)}, u32[]{:S(2)}) copy-start(bf16[1,512,2048]{2,1,0:T(8,128)(2,1)} %param.12) | copy-start | bytes 6291460
  9.3 14.6 %copy-start.2 = (bf16[128,4224]{1,0:T(8,128)(2,1)S(1)}, bf16[128,4224]{1,0:T(8,128)(2,1)}, u32[]{:S(2)}) copy-start(bf16[128,4224]{1,0:T(8,128)(2,1)} %shard_map.94.refs_0_) | copy-start | bytes 3244036
  9.4 14.4 %collective-permute-start.3 = (bf16[1,2,64,2048]{3,2,1,0:T(8,128)(2,1)S(1)}, bf16[1,2,64,2048]{3,2,1,0:T(8,128)(2,1)S(1)}, u32[]{:S(2)}, u32[]{:S(2)}) collective-permute-start(bf16[1,2,64,2048]{3,2,1,0:T(8,128)(2,1)S(1)} %pad_maximum_fusion), channel_id=1, source_target_pairs={{0,4},{4,0},{8,12},{12,8},{16,20},{20,16},{24,28},{28,24},{1,5},{5... | collective-permute-start | bytes 1572872 | tf_op jit(solution)/shard_map/ppermute | solution.py:25
  31.5 4.1 %collective-permute-start.4 = (bf16[128,4224]{1,0:T(8,128)(2,1)S(1)}, bf16[128,4224]{1,0:T(8,128)(2,1)S(1)}, u32[]{:S(2)}, u32[]{:S(2)}) collective-permute-start(bf16[128,4224]{1,0:T(8,128)(2,1)S(1)} %get-tuple-element.56.refs_0_), channel_id=1, source_target_pairs={{0,1},{1,0},{2,3},{3,2},{4,5},{5,4},{6,7},{7,6},{8,9},{9,8},{10,11... | collective-permute-start | bytes 3244040 | tf_op jit(solution)/shard_map/ppermute | solution.py:25
  31.5 6.6 %collective-permute-start.5 = (bf16[128,4224]{1,0:T(8,128)(2,1)S(1)}, bf16[128,4224]{1,0:T(8,128)(2,1)S(1)}, u32[]{:S(2)}, u32[]{:S(2)}) collective-permute-start(bf16[128,4224]{1,0:T(8,128)(2,1)S(1)} %get-tuple-element.65.refs_0_), channel_id=1, source_target_pairs={{0,1},{1,0},{2,3},{3,2},{4,5},{5,4},{6,7},{7,6},{8,9},{9,8},{10,11... | collective-permute-start | bytes 3244040 | tf_op jit(solution)/shard_map/ppermute | solution.py:25
  32.1 15.3 %collective-permute-start.7 = (bf16[64,4224]{1,0:T(8,128)(2,1)S(1)}, bf16[64,4224]{1,0:T(8,128)(2,1)S(1)}, u32[]{:S(2)}, u32[]{:S(2)}) collective-permute-start(bf16[64,4224]{1,0:T(8,128)(2,1)S(1)} %slice.27), channel_id=1, source_target_pairs={{0,2},{1,3},{2,0},{3,1},{4,6},{5,7},{6,4},{7,5},{8,10},{9,11},{10,... | collective-permute-start | bytes 1622024 | tf_op jit(solution)/shard_map/ppermute | solution.py:25
  33.7 13.9 %collective-permute-start.6 = (bf16[64,4224]{1,0:T(8,128)(2,1)S(1)}, bf16[64,4224]{1,0:T(8,128)(2,1)S(1)}, u32[]{:S(2)}, u32[]{:S(2)}) collective-permute-start(bf16[64,4224]{1,0:T(8,128)(2,1)S(1)} %slice.26), channel_id=1, source_target_pairs={{0,8},{4,12},{8,0},{12,4},{16,24},{20,28},{24,16},{28,20},{1,9},{5... | collective-permute-start | bytes 1622024 | tf_op jit(solution)/shard_map/ppermute | solution.py:25
  34.1 13.3 %collective-permute-start.8 = (bf16[1,2,64,2048]{3,2,1,0:T(8,128)(2,1)S(1)}, bf16[1,2,64,2048]{3,2,1,0:T(8,128)(2,1)S(1)}, u32[]{:S(2)}, u32[]{:S(2)}) collective-permute-start(bf16[1,2,64,2048]{3,2,1,0:T(8,128)(2,1)S(1)} %get-tuple-element.74), channel_id=1, source_target_pairs={{0,4},{4,0},{8,12},{12,8},{16,20},{20,16},{24,28},{28,24},{1,5},{5... | collective-permute-start | bytes 1572872 | tf_op jit(solution)/shard_map/ppermute | solution.py:25
  47.6 2.0 %collective-permute-start.9 = (bf16[64,4224]{1,0:T(8,128)(2,1)S(1)}, bf16[64,4224]{1,0:T(8,128)(2,1)S(1)}, u32[]{:S(2)}, u32[]{:S(2)}) collective-permute-start(bf16[64,4224]{1,0:T(8,128)(2,1)S(1)} %get-tuple-element.76.refs_0_), channel_id=1, source_target_pairs={{0,1},{1,0},{2,3},{3,2},{4,5},{5,4},{6,7},{7,6},{8,9},{9,8},{10,11... | collective-permute-start | bytes 1622024 | tf_op jit(solution)/shard_map/ppermute | solution.py:25
  47.6 2.7 %collective-permute-start.10 = (bf16[64,4224]{1,0:T(8,128)(2,1)S(1)}, bf16[64,4224]{1,0:T(8,128)(2,1)S(1)}, u32[]{:S(2)}, u32[]{:S(2)}) collective-permute-start(bf16[64,4224]{1,0:T(8,128)(2,1)S(1)} %get-tuple-element.77.refs_1_), channel_id=1, source_target_pairs={{0,1},{1,0},{2,3},{3,2},{4,5},{5,4},{6,7},{7,6},{8,9},{9,8},{10,11... | collective-permute-start | bytes 1622024 | tf_op jit(solution)/shard_map/ppermute | solution.py:25
  48.1 14.6 %collective-permute-start.19 = (bf16[1,2,64,2048]{3,2,1,0:T(8,128)(2,1)S(1)}, bf16[1,2,64,2048]{3,2,1,0:T(8,128)(2,1)S(1)}, u32[]{:S(2)}, u32[]{:S(2)}) collective-permute-start(bf16[1,2,64,2048]{3,2,1,0:T(8,128)(2,1)S(1)} %get-tuple-element.86), channel_id=1, source_target_pairs={{0,8},{4,12},{8,0},{12,4},{16,24},{20,28},{24,16},{28,20},{1,9},{5... | collective-permute-start | bytes 1572872 | tf_op jit(solution)/shard_map/ppermute | solution.py:25
  52.9 7.1 %collective-permute-start.15 = (bf16[1,80,1024]{2,1,0:T(8,128)(2,1)S(1)}, bf16[1,80,1024]{2,1,0:T(8,128)(2,1)S(1)}, u32[]{:S(2)}, u32[]{:S(2)}) collective-permute-start(bf16[1,80,1024]{2,1,0:T(8,128)(2,1)S(1)} %get-tuple-element.81), channel_id=1, source_target_pairs={{0,4},{4,0},{8,12},{12,8},{16,20},{20,16},{24,28},{28,24},{1,5},{5... | collective-permute-start | bytes 491528 | tf_op jit(solution)/shard_map/ppermute | solution.py:25
  55.4 12.4 %collective-permute-start.13 = (bf16[1,176,1024]{2,1,0:T(8,128)(2,1)S(1)}, bf16[1,176,1024]{2,1,0:T(8,128)(2,1)S(1)}, u32[]{:S(2)}, u32[]{:S(2)}) collective-permute-start(bf16[1,176,1024]{2,1,0:T(8,128)(2,1)S(1)} %dynamic-slice_bitcast_fusion.1.refs_1_), channel_id=1, source_target_pairs={{0,4},{4,0},{8,12},{12,8},{16,20},{20,16},{24,28},{28,24},{1,5},{5... | collective-permute-start | bytes 1081352 | tf_op jit(solution)/shard_map/ppermute | solution.py:25
  57.4 7.0 %collective-permute-start.11 = (bf16[256,2048]{1,0:T(8,128)(2,1)S(1)}, bf16[256,2048]{1,0:T(8,128)(2,1)S(1)}, u32[]{:S(2)}, u32[]{:S(2)}) collective-permute-start(bf16[256,2048]{1,0:T(8,128)(2,1)S(1)} %convolution_convert_fusion), channel_id=1, source_target_pairs={{0,1},{1,0},{2,3},{3,2},{4,5},{5,4},{6,7},{7,6},{8,9},{9,8},{10,11... | collective-permute-start | bytes 3145736 | tf_op jit(solution)/shard_map/ppermute | solution.py:25
  60.0 32.0 %collective-permute-start.16 = (bf16[1,80,1024]{2,1,0:T(8,128)(2,1)S(1)}, bf16[1,80,1024]{2,1,0:T(8,128)(2,1)S(1)}, u32[]{:S(2)}, u32[]{:S(2)}) collective-permute-start(bf16[1,80,1024]{2,1,0:T(8,128)(2,1)S(1)} %fusion.17), channel_id=1, source_target_pairs={{0,16},{4,20},{8,24},{12,28},{16,0},{20,4},{24,8},{28,12},{1,17},{... | collective-permute-start | bytes 491528 | tf_op jit(solution)/shard_map/ppermute | solution.py:25
  62.7 10.6 %collective-permute-start.20 = (bf16[1,64,2048]{2,1,0:T(8,128)(2,1)S(1)}, bf16[1,64,2048]{2,1,0:T(8,128)(2,1)S(1)}, u32[]{:S(2)}, u32[]{:S(2)}) collective-permute-start(bf16[1,64,2048]{2,1,0:T(8,128)(2,1)S(1)} %get-tuple-element.88), channel_id=1, source_target_pairs={{0,4},{4,0},{8,12},{12,8},{16,20},{20,16},{24,28},{28,24},{1,5},{5... | collective-permute-start | bytes 786440 | tf_op jit(solution)/shard_map/ppermute | solution.py:25
  65.8 12.3 %collective-permute-start.12 = (bf16[128,2048]{1,0:T(8,128)(2,1)S(1)}, bf16[128,2048]{1,0:T(8,128)(2,1)S(1)}, u32[]{:S(2)}, u32[]{:S(2)}) collective-permute-start(bf16[128,2048]{1,0:T(8,128)(2,1)S(1)} %slice.56), channel_id=1, source_target_pairs={{0,2},{1,3},{2,0},{3,1},{4,6},{5,7},{6,4},{7,5},{8,10},{9,11},{10,... | collective-permute-start | bytes 1572872 | tf_op jit(solution)/shard_map/ppermute | solution.py:25
  67.8 24.2 %collective-permute-start.17 = (bf16[1,176,1024]{2,1,0:T(8,128)(2,1)S(1)}, bf16[1,176,1024]{2,1,0:T(8,128)(2,1)S(1)}, u32[]{:S(2)}, u32[]{:S(2)}) collective-permute-start(bf16[1,176,1024]{2,1,0:T(8,128)(2,1)S(1)} %fusion.5), channel_id=1, source_target_pairs={{0,16},{4,20},{8,24},{12,28},{16,0},{20,4},{24,8},{28,12},{1,17},{... | collective-permute-start | bytes 1081352 | tf_op jit(solution)/shard_map/ppermute | solution.py:25
  70.5 21.5 %collective-permute-start.14 = (bf16[1,256,1024]{2,1,0:T(8,128)(2,1)S(1)}, bf16[1,256,1024]{2,1,0:T(8,128)(2,1)S(1)}, u32[]{:S(2)}, u32[]{:S(2)}) collective-permute-start(bf16[1,256,1024]{2,1,0:T(8,128)(2,1)S(1)} %shard_map.103), channel_id=1, source_target_pairs={{0,4},{4,0},{8,12},{12,8},{16,20},{20,16},{24,28},{28,24},{1,5},{5... | collective-permute-start | bytes 1572872 | tf_op jit(solution)/shard_map/ppermute | solution.py:25
  73.4 23.2 %collective-permute-start.21 = (bf16[1,64,2048]{2,1,0:T(8,128)(2,1)S(1)}, bf16[1,64,2048]{2,1,0:T(8,128)(2,1)S(1)}, u32[]{:S(2)}, u32[]{:S(2)}) collective-permute-start(bf16[1,64,2048]{2,1,0:T(8,128)(2,1)S(1)} %fusion.7), channel_id=1, source_target_pairs={{0,16},{4,20},{8,24},{12,28},{16,0},{20,4},{24,8},{28,12},{1,17},{... | collective-permute-start | bytes 786440 | tf_op jit(solution)/shard_map/ppermute | solution.py:25
  78.1 18.5 %collective-permute-start.18 = (bf16[1,64,2048]{2,1,0:T(8,128)(2,1)S(1)}, bf16[1,64,2048]{2,1,0:T(8,128)(2,1)S(1)}, u32[]{:S(2)}, u32[]{:S(2)}) collective-permute-start(bf16[1,64,2048]{2,1,0:T(8,128)(2,1)S(1)} %shard_map.104.refs_1_), channel_id=1, source_target_pairs={{0,4},{4,0},{8,12},{12,8},{16,20},{20,16},{24,28},{28,24},{1,5},{5... | collective-permute-start | bytes 786440 | tf_op jit(solution)/shard_map/ppermute | solution.py:25
